TPU v7x, 32 devices: a whole 2x2x4 slice. The times are simulated.
32 devices in a mesh: seq: 2 (over x), row: 4 (over z), col: 4 (over y, core).
Axes of the slice: x: 2, y: 2, z: 4, core: 2. Of those that a mesh axis runs over, the one named last changes fastest.
Arguments:
- alignment_input: bfloat16 [64, 256, 64], P('seq', ('row', 'col')), may hold values from -30 to 30
- pair_input: bfloat16 [256, 256, 128], P('row', 'col'), may hold values from -60 to 60
- token_valid_mask: int32 [256], replicated, may hold values from 0 to 1, as said below
- first_factor_weights: bfloat16 [64, 32], replicated, may hold values from -0.75 to 0.75
- second_factor_weights: bfloat16 [64, 32], replicated, may hold values from -0.75 to 0.75
- content_weights_grid: bfloat16 [64, 256], replicated, may hold values from -0.75 to 0.75
- sigmoid_weights_grid: bfloat16 [64, 256], replicated, may hold values from -0.75 to 0.75
- outer_matrix: float32 [1024, 128], replicated, may hold values from -0.0234375 to 0.0234375
- score_matrix: float32 [128, 8], replicated, may hold values from -20 to 20
- final_mixing_weights: bfloat16 [256, 64], replicated, may hold values from -0.375 to 0.375
- adjoint_of_rowset: bfloat16 [64, 256, 64], P('seq', ('row', 'col')), may hold values from -48 to 48
Outputs:
- alignment_output: bfloat16 [64, 256, 64], P('seq', ('row', 'col'))
- pair_output: bfloat16 [256, 256, 128], P('row', 'col')
- pair_gradient: bfloat16 [256, 256, 128], P('row', 'col')
Inputs may be any that keep to these rules, and one draw needn't show every extreme that they name: `token_valid_mask`: the mask is 1 on a first run of more than half of the 256 tokens and 0 on the rest.
All inputs are finite; a program needn't handle non-finite values.
Results may differ from a plain program's by a relative error of at most 0.028.
The roundings to bfloat16 on the way count: a program that leaves them out, or rounds other values in their place, can miss the bound.
Values may be sent and summed in bfloat16 or wider, within the bound.
No kernel may reach another device: no remote copies, remote signals or barrier semaphores. Data moves between devices by JAX's collectives and lax.ppermute only.
A program may use at most 64 MiB of HBM per device.

v0:
```python
import math

import jax
import jax.numpy as jnp
from jax import lax
from jax.sharding import PartitionSpec as P

epsilon = 1e-05
far_below = -1e30


def layer_normalize(inputs):
    center = inputs - jnp.mean(inputs, axis=-1, keepdims=True)
    inverse = lax.rsqrt(jnp.mean(center * center, axis=-1, keepdims=True) + epsilon)
    return (center * inverse, inverse)


def on_device(
    alignment_input,
    pair_input,
    token_valid_mask,
    first_factor_weights,
    second_factor_weights,
    content_weights_grid,
    sigmoid_weights_grid,
    outer_matrix,
    score_matrix,
    final_mixing_weights,
    adjoint_of_rowset,
):
    highest = lax.Precision.HIGHEST
    count_col = lax.axis_size("col")
    row_index = lax.axis_index("row")
    col_index = lax.axis_index("col")
    local_sequences = alignment_input.shape[0]
    local_tokens = alignment_input.shape[1]
    tile_i = pair_input.shape[0]
    tile_j = pair_input.shape[1]
    head_count = score_matrix.shape[1]
    proj_width = second_factor_weights.shape[1]
    own_start = (row_index * count_col + col_index) * local_tokens
    own_mask = lax.dynamic_slice_in_dim(token_valid_mask, own_start, local_tokens).astype(
        jnp.float32
    )
    col_mask = lax.dynamic_slice_in_dim(token_valid_mask, col_index * tile_j, tile_j).astype(
        jnp.float32
    )
    normalized_pair = layer_normalize(alignment_input.astype(jnp.float32))[0].astype(jnp.bfloat16)
    left_proj = (
        jnp.dot(normalized_pair, first_factor_weights, preferred_element_type=jnp.float32)
        * own_mask[None, :, None]
    ).astype(jnp.bfloat16)
    right_proj = (
        jnp.dot(normalized_pair, second_factor_weights, preferred_element_type=jnp.float32)
        * own_mask[None, :, None]
    ).astype(jnp.bfloat16)
    values = jnp.dot(
        normalized_pair, content_weights_grid, preferred_element_type=jnp.float32
    ).astype(jnp.bfloat16)
    gating = jax.nn.sigmoid(
        jnp.dot(normalized_pair, sigmoid_weights_grid, preferred_element_type=jnp.float32)
    )
    joined = jnp.concatenate([right_proj, values], axis=2)
    rows_left = lax.all_gather(left_proj, "col", axis=1, tiled=True)
    every_joined = lax.all_gather(joined, ("row", "col"), axis=1, tiled=True)
    cols_joined = lax.dynamic_slice_in_dim(every_joined, col_index * tile_j, tile_j, 1)
    cols_right = cols_joined[:, :, :proj_width]
    cols_values = cols_joined[:, :, proj_width:]

    def outer_rows(row_start, row_count):
        rows_part = lax.dynamic_slice_in_dim(rows_left, row_start, row_count, 1)
        products = jnp.einsum(
            "sic,sjd->ijcd", rows_part, cols_right, preferred_element_type=jnp.float32
        )
        return products.reshape(row_count, tile_j, -1)

    pair_float = pair_input.astype(jnp.float32)
    block_rows = math.gcd(tile_i, 8)

    def one_block(number):
        return jnp.dot(
            outer_rows(0 + number * block_rows, block_rows),
            outer_matrix,
            precision=highest,
            preferred_element_type=jnp.float32,
        )

    pieces = lax.map(one_block, jnp.arange(tile_i // block_rows, dtype=jnp.int32))
    update = lax.psum(pieces.reshape(tile_i, tile_j, outer_matrix.shape[1]), "seq")
    pair_output = (pair_float + update).astype(jnp.bfloat16)
    normal_pair, inverse_pair = layer_normalize(pair_output.astype(jnp.float32))
    logits = jnp.dot(
        normal_pair, score_matrix, precision=highest, preferred_element_type=jnp.float32
    )
    valid_cols = col_mask[None, :, None] > 0
    masked = jnp.where(valid_cols, logits, far_below)
    local_peak = jnp.max(masked, axis=1)
    row_max = lax.pmax(local_peak, "col")
    scaled = jnp.exp(masked - row_max[:, None, :]) * col_mask[None, :, None]
    row_sum = lax.psum(jnp.sum(scaled, axis=1), "col")
    probabilities = scaled / row_sum[:, None, :]
    weights = probabilities.astype(jnp.bfloat16)
    head_values = cols_values.reshape(local_sequences, tile_j, head_count, -1)
    partial_value = jnp.einsum(
        "ijh,sjhk->sihk", weights, head_values, preferred_element_type=jnp.float32
    ).reshape(local_sequences, tile_i, -1)
    averaged = lax.psum_scatter(
        partial_value.astype(jnp.bfloat16), "col", scatter_dimension=1, tiled=True
    ).astype(jnp.float32)
    gated_values = (gating * averaged).astype(jnp.bfloat16)
    alignment_output = (
        alignment_input.astype(jnp.float32)
        + jnp.dot(gated_values, final_mixing_weights, preferred_element_type=jnp.float32)
    ).astype(jnp.bfloat16)
    gated_gradient = jnp.dot(
        adjoint_of_rowset, final_mixing_weights.T, preferred_element_type=jnp.float32
    )
    grad_avg = (gated_gradient * gating).astype(jnp.bfloat16)
    rows_grad = lax.all_gather(grad_avg, "col", axis=1, tiled=True)
    weight_part = jnp.einsum(
        "sihk,sjhk->ijh",
        rows_grad.reshape(local_sequences, tile_i, head_count, -1),
        head_values,
        preferred_element_type=jnp.float32,
    )
    grad_weights = lax.psum(weight_part.astype(jnp.bfloat16), "seq").astype(jnp.float32)
    inner_sum = lax.psum(jnp.sum(probabilities * grad_weights, axis=1), "col")
    grad_logits = probabilities * (grad_weights - inner_sum[:, None, :])
    grad_normal = jnp.dot(
        grad_logits, score_matrix.T, precision=highest, preferred_element_type=jnp.float32
    )
    centered_grad = grad_normal - jnp.mean(grad_normal, axis=-1, keepdims=True)
    along = jnp.mean(grad_normal * normal_pair, axis=-1, keepdims=True)
    pair_gradient = (inverse_pair * (centered_grad - normal_pair * along)).astype(jnp.bfloat16)
    return (alignment_output, pair_output, pair_gradient)


def solution(mesh):
    in_specs = (
        P("seq", ("row", "col"), None),
        P("row", "col", None),
        P(),
        P(),
        P(),
        P(),
        P(),
        P(),
        P(),
        P(),
        P("seq", ("row", "col"), None),
    )
    out_specs = (P("seq", ("row", "col"), None), P("row", "col", None), P("row", "col", None))
    return jax.shard_map(
        on_device, mesh=mesh, in_specs=in_specs, out_specs=out_specs, check_vma=False
    )
```

profile of v0, /device:TPU:0, one launch (start us, length us, event | category | flops | bytes accessed | tf_op | source)
XLA Modules:
  0.0 308.9 jit_solution(8403152584646453797)
XLA Ops:
  7.2 1.0 convert_reduce_fusion.1
  8.3 1.1 fusion.35
  9.5 1.1 fusion.36
  10.6 1.0 convolution_convert_fusion
  11.6 0.8 dynamic-slice_convert_fusion.1
  12.3 0.9 fusion.28
  13.3 0.9 pad_maximum_fusion
  14.6 0.8 copy-done.4
  15.4 0.9 fusion.24
  16.5 8.6 %all_gather.10 = bf16[32,64,32]{2,0,1:T(8,128)(2,1)S(1)} all-gather(bf16[32,16,32]{2,0,1:T(8,128)(2,1)S(1)} %fusion.29), channel_id=1, replica_groups=mesh['seq'=2,'row'=4,'col'=4] {'col'}, dimensions={1}, use_global_device_ids=true | all-gather | bytes 163840 | tf_op jit(solution)/shard_map/all_gather | solution.py:64
  25.2 53.7 %all-gather.3.cloned.1.call-done = bf16[32,256,288]{2,1,0:T(8,128)(2,1)} async-done(((bf16[32,16,288]{2,1,0:T(8,128)(2,1)}), bf16[32,256,288]{2,1,0:T(8,128)(2,1)}) %all-gather.3.cloned.1.call-update) | async-done | bytes 4718608 | tf_op jit(solution)/shard_map/all_gather | solution.py:65
  78.9 1.1 constant_dynamic-slice_fusion.1
  80.4 94.0 %while.10 = (s32[]{:T(128)}, f32[8,8,64,128]{3,2,1,0:T(8,128)}, s32[8]{0:T(128)S(1)}, bf16[32,64,32]{2,0,1:T(8,128)(2,1)S(1)}, bf16[32,64,32]{1,0,2:T(8,128)(2,1...) while((s32[]{:T(128)}, f32[8,8,64,128]{3,2,1,0:T(8,128)}, ...), condition=%wide.region_3.4_spmd, body=%wide.region_2.3_spmd.sunk | while | flops 838860800 | bytes 9502895 | solution.py:88
  80.4 0.6 dynamic_slice.29
  81.6 0.7 convolution_bitcast_fusion.4
  82.4 2.4 copy.72
  84.8 7.4 %fusion.73 = f32[8,8,64,128]{3,2,1,0:T(8,128)} fusion(f32[8,8,64,128]{3,2,1,0:T(8,128)} %get-tuple-element.127, s32[]{:T(128)S(6)} %copy.77, f32[8,64,1024]{1,2,0:T(8,128)S(1)} %bitcast.81, f32[1024,128]{1,0:T(8,128)S(1)} %get-tuple-element.141), kind=kOutput, calls=%fused_computation.2.clone.1 | convolution fusion | flops 805306368 | bytes 2883588 | tf_op jit(solution)/shard_map/while/body/eval_jaxpr/dot_general | solution.py:81
  92.2 0.6 dynamic_slice.29
  93.4 0.7 convolution_bitcast_fusion.4
  94.1 2.4 copy.72
  96.5 7.4 %fusion.73 = f32[8,8,64,128]{3,2,1,0:T(8,128)} fusion(f32[8,8,64,128]{3,2,1,0:T(8,128)} %get-tuple-element.127, s32[]{:T(128)S(6)} %copy.77, f32[8,64,1024]{1,2,0:T(8,128)S(1)} %bitcast.81, f32[1024,128]{1,0:T(8,128)S(1)} %get-tuple-element.141), kind=kOutput, calls=%fused_computation.2.clone.1 | convolution fusion | flops 805306368 | bytes 2883588 | tf_op jit(solution)/shard_map/while/body/eval_jaxpr/dot_general | solution.py:81
  103.9 0.6 dynamic_slice.29
  105.2 0.7 convolution_bitcast_fusion.4
  105.9 2.4 copy.72
  108.3 7.4 %fusion.73 = f32[8,8,64,128]{3,2,1,0:T(8,128)} fusion(f32[8,8,64,128]{3,2,1,0:T(8,128)} %get-tuple-element.127, s32[]{:T(128)S(6)} %copy.77, f32[8,64,1024]{1,2,0:T(8,128)S(1)} %bitcast.81, f32[1024,128]{1,0:T(8,128)S(1)} %get-tuple-element.141), kind=kOutput, calls=%fused_computation.2.clone.1 | convolution fusion | flops 805306368 | bytes 2883588 | tf_op jit(solution)/shard_map/while/body/eval_jaxpr/dot_general | solution.py:81
  115.7 0.6 dynamic_slice.29
  116.9 0.7 convolution_bitcast_fusion.4
  117.7 2.4 copy.72
  120.0 7.4 %fusion.73 = f32[8,8,64,128]{3,2,1,0:T(8,128)} fusion(f32[8,8,64,128]{3,2,1,0:T(8,128)} %get-tuple-element.127, s32[]{:T(128)S(6)} %copy.77, f32[8,64,1024]{1,2,0:T(8,128)S(1)} %bitcast.81, f32[1024,128]{1,0:T(8,128)S(1)} %get-tuple-element.141), kind=kOutput, calls=%fused_computation.2.clone.1 | convolution fusion | flops 805306368 | bytes 2883588 | tf_op jit(solution)/shard_map/while/body/eval_jaxpr/dot_general | solution.py:81
  127.4 0.6 dynamic_slice.29
  128.7 0.7 convolution_bitcast_fusion.4
  129.4 2.4 copy.72
  131.8 7.4 %fusion.73 = f32[8,8,64,128]{3,2,1,0:T(8,128)} fusion(f32[8,8,64,128]{3,2,1,0:T(8,128)} %get-tuple-element.127, s32[]{:T(128)S(6)} %copy.77, f32[8,64,1024]{1,2,0:T(8,128)S(1)} %bitcast.81, f32[1024,128]{1,0:T(8,128)S(1)} %get-tuple-element.141), kind=kOutput, calls=%fused_computation.2.clone.1 | convolution fusion | flops 805306368 | bytes 2883588 | tf_op jit(solution)/shard_map/while/body/eval_jaxpr/dot_general | solution.py:81
  139.2 0.6 dynamic_slice.29
  140.4 0.7 convolution_bitcast_fusion.4
  141.1 2.4 copy.72
  143.5 7.4 %fusion.73 = f32[8,8,64,128]{3,2,1,0:T(8,128)} fusion(f32[8,8,64,128]{3,2,1,0:T(8,128)} %get-tuple-element.127, s32[]{:T(128)S(6)} %copy.77, f32[8,64,1024]{1,2,0:T(8,128)S(1)} %bitcast.81, f32[1024,128]{1,0:T(8,128)S(1)} %get-tuple-element.141), kind=kOutput, calls=%fused_computation.2.clone.1 | convolution fusion | flops 805306368 | bytes 2883588 | tf_op jit(solution)/shard_map/while/body/eval_jaxpr/dot_general | solution.py:81
  150.9 0.6 dynamic_slice.29
  152.1 0.7 convolution_bitcast_fusion.4
  152.9 2.4 copy.72
  155.3 7.4 %fusion.73 = f32[8,8,64,128]{3,2,1,0:T(8,128)} fusion(f32[8,8,64,128]{3,2,1,0:T(8,128)} %get-tuple-element.127, s32[]{:T(128)S(6)} %copy.77, f32[8,64,1024]{1,2,0:T(8,128)S(1)} %bitcast.81, f32[1024,128]{1,0:T(8,128)S(1)} %get-tuple-element.141), kind=kOutput, calls=%fused_computation.2.clone.1 | convolution fusion | flops 805306368 | bytes 2883588 | tf_op jit(solution)/shard_map/while/body/eval_jaxpr/dot_general | solution.py:81
  163.9 0.7 convolution_bitcast_fusion.4
  164.6 2.4 copy.72
  167.0 7.4 %fusion.73 = f32[8,8,64,128]{3,2,1,0:T(8,128)} fusion(f32[8,8,64,128]{3,2,1,0:T(8,128)} %get-tuple-element.127, s32[]{:T(128)S(6)} %copy.77, f32[8,64,1024]{1,2,0:T(8,128)S(1)} %bitcast.81, f32[1024,128]{1,0:T(8,128)S(1)} %get-tuple-element.141), kind=kOutput, calls=%fused_computation.2.clone.1 | convolution fusion | flops 805306368 | bytes 2883588 | tf_op jit(solution)/shard_map/while/body/eval_jaxpr/dot_general | solution.py:81
  175.2 2.8 copy.53
  177.9 2.8 constant_dynamic-slice_fusion
  180.7 1.1 copy.45
  181.8 2.4 convolution_bitcast_fusion.2
  184.2 0.8 copy.54
  185.1 50.9 %all-reduce.3.cloned.1.call-done = f32[64,64,128]{2,1,0:T(8,128)} async-done(((f32[64,64,128]{2,1,0:T(8,128)}), f32[64,64,128]{2,1,0:T(8,128)}) %all-reduce.3.cloned.1.call-update) | async-done | bytes 2097168 | tf_op jit(solution)/shard_map/psum | solution.py:89
  236.0 2.5 convert_reduce_fusion
  238.5 1.3 fusion.16
  239.8 6.0 %fusion.57 = (f32[64,8]{1,0:T(8,128)}, f32[64,64,8]{1,2,0:T(8,128)S(1)}) fusion(f32[128,8]{0,1:T(8,128)S(1)} %copy-done.15, bf16[64,64,128]{2,1,0:T(8,128)(2,1)S(1)} %get-tuple-element.71, f32[64,64]{1,0:T(8,128)S(1)} %add_rsqrt_fusion, f32[64,64]{1,0:T(8,128)S(1)} %broadcast_multiply_fusion.2, pred[64]{0:T(512)(128)(4,1)S(1)} %get-tuple-element.68), kind=kOutput, calls=%fused_computation.83 | convolution fusion | flops 51969536 | bytes 1218624 | tf_op jit(solution)/shard_map/dot_general | solution.py:92
  245.9 12.6 %pmax.7 = f32[64,8]{1,0:T(8,128)} all-reduce(f32[64,8]{1,0:T(8,128)} %get-tuple-element.74), channel_id=1, replica_groups=mesh['seq'=2,'row'=4,'col'=4] {'col'}, use_global_device_ids=true, to_apply=%region_8.9 | all-reduce | flops 512 | bytes 4096 | tf_op jit(solution)/shard_map/pmax | solution.py:98
  258.5 1.6 fusion.42
  260.1 11.6 %psum.29 = f32[64,8]{1,0:T(8,128)} all-reduce(f32[64,8]{1,0:T(8,128)} %fusion.42), channel_id=1, replica_groups=mesh['seq'=2,'row'=4,'col'=4] {'col'}, use_global_device_ids=true, to_apply=%region_10.11 | all-reduce | flops 512 | bytes 4096 | tf_op jit(solution)/shard_map/psum | solution.py:100
  271.6 1.8 fusion.37
  273.5 0.7 convert_bitcast_fusion
  274.7 1.6 copy.52
  276.4 11.0 %psum.31 = f32[64,8]{1,0:T(8,128)S(1)} all-reduce(f32[64,8]{1,0:T(8,128)} %get-tuple-element.72), channel_id=1, replica_groups=mesh['seq'=2,'row'=4,'col'=4] {'col'}, use_global_device_ids=true, to_apply=%region_14.15 | all-reduce | flops 512 | bytes 4096 | tf_op jit(solution)/shard_map/psum | solution.py:127
  287.5 7.2 %fusion.56 = (f32[64,64]{1,0:T(8,128)S(1)}, f32[64,64]{1,0:T(8,128)S(1)}, f32[64,64,128]{2,1,0:T(8,128)S(1)}) fusion(f32[64,64]{1,0:T(8,128)} %copy-done.8, f32[64,64]{1,0:T(8,128)} %copy-done.6, bf16[64,64,128]{2,1,0:T(8,128)(2,1)S(1)} %get-tuple-element.71, f32[128,8]{0,1:T(8,128)S(1)} %copy-done.15, bf16[64,64,8]{1,2,0:T(8,128)(2,1)} %all-reduce.5.cloned.1.call-done, ...), kind=kOutput, calls=%fused_computation.82 | convolution fusion | flops 53665792 | bytes 3418368 | tf_op jit(solution)/shard_map/dot_general | solution.py:129
  294.8 3.3 %fusion.15 = bf16[64,64,128]{2,1,0:T(8,128)(2,1)} fusion(bf16[64,64,128]{2,1,0:T(8,128)(2,1)S(1)} %get-tuple-element.71, f32[64,64,128]{2,1,0:T(8,128)S(1)} %get-tuple-element.76, f32[64,64]{1,0:T(8,128)S(1)} %get-tuple-element.77, f32[64,64]{1,0:T(8,128)S(1)} %get-tuple-element.78, f32[64,64]{1,0:T(8,128)S(1)} %copy-done.9, f32[64,64]{1,0:T(8,128)S(1)} %copy-done.7), kind=kLoop, calls=%fused_computation.18 | loop fusion | flops 4194304 | bytes 4259840 | tf_op jit(solution)/shard_map/convert_element_type | solution.py:134
  298.0 2.5 reduce-scatter.2.cloned.1.call-done
  300.6 1.8 fusion.30
  (57 shorter events, 3.2 us)
Async XLA Ops:
  7.2 8.2 %copy-start = (bf16[32,16,64]{2,1,0:T(8,128)(2,1)S(1)}, bf16[32,16,64]{2,1,0:T(8,128)(2,1)}, u32[]{:S(2)}) copy-start(bf16[32,16,64]{2,1,0:T(8,128)(2,1)} %param.23) | copy-start | bytes 196612
  7.2 7.1 %copy-start.14 = (bf16[64,256]{1,0:T(8,128)(2,1)S(1)}, bf16[64,256]{1,0:T(8,128)(2,1)}, u32[]{:S(2)}) copy-start(bf16[64,256]{1,0:T(8,128)(2,1)} %param.19) | copy-start | bytes 98308
  7.2 71.7 %all-gather.3.cloned.1.call-start = ((), (), s32[]{:S(2)}) async-start(), calls=%async_computation.1 | async-start | bytes 6684672 | tf_op jit(solution)/shard_map/all_gather | solution.py:65
  10.6 4.8 %copy-start.10 = (bf16[256,64]{0,1:T(8,128)(2,1)S(1)}, bf16[256,64]{0,1:T(8,128)(2,1)}, u32[]{:S(2)}) copy-start(bf16[256,64]{0,1:T(8,128)(2,1)} %param.22) | copy-start | bytes 98308
  14.2 2.2 copy-start.12
  14.2 160.9 %all-gather.5.cloned.1.call-start = ((), (), s32[]{:S(2)}) async-start(), calls=%async_computation.4 | async-start | bytes 1310720 | tf_op jit(solution)/shard_map/all_gather | solution.py:119
  14.6 0.8 copy-start.4
  15.4 65.0 %copy-start.1 = (f32[1024,128]{1,0:T(8,128)S(1)}, f32[1024,128]{1,0:T(8,128)}, u32[]{:S(2)}) copy-start(f32[1024,128]{1,0:T(8,128)} %param.20) | copy-start | bytes 1572868
  16.3 219.7 %all-reduce.3.cloned.1.call-start = ((), (), s32[]{:S(2)}) async-start(), calls=%async_computation.2 | async-start | bytes 4194304 | tf_op jit(solution)/shard_map/psum | solution.py:89
  174.4 0.7 copy-start.13
  174.4 97.2 %all-reduce.5.cloned.1.call-start = ((), (), s32[]{:S(2)}) async-start(), calls=%async_computation.5 | async-start | bytes 262144 | tf_op jit(solution)/shard_map/psum | solution.py:126
  185.0 54.8 %copy-start.15 = (f32[128,8]{0,1:T(8,128)S(1)}, f32[128,8]{0,1:T(8,128)}, u32[]{:S(2)}) copy-start(f32[128,8]{0,1:T(8,128)} %param.21) | copy-start | bytes 12292
  185.0 115.5 %reduce-scatter.2.cloned.1.call-start = ((), (), s32[]{:S(2)}) async-start(), calls=%async_computation.3 | async-start | bytes 1310720 | tf_op jit(solution)/shard_map/reduce_scatter | solution.py:107
  238.4 56.3 %copy-start.2 = (bf16[64,64,128]{2,1,0:T(8,128)(2,1)}, bf16[64,64,128]{2,1,0:T(8,128)(2,1)S(1)}, u32[]{:S(2)}) copy-start(bf16[64,64,128]{2,1,0:T(8,128)(2,1)S(1)} %get-tuple-element.71) | copy-start | bytes 3145732
  238.5 1.4 copy-start.6
  239.8 6.0 %copy-start.8 = (f32[64,64]{1,0:T(8,128)}, f32[64,64]{1,0:T(8,128)S(1)}, u32[]{:S(2)}) copy-start(f32[64,64]{1,0:T(8,128)S(1)} %add_rsqrt_fusion) | copy-start | bytes 49156
  287.4 7.3 %copy-start.7 = (f32[64,64]{1,0:T(8,128)S(1)}, f32[64,64]{1,0:T(8,128)}, u32[]{:S(2)}) copy-start(f32[64,64]{1,0:T(8,128)} %copy-done.6) | copy-start | bytes 49156
  287.4 7.3 %copy-start.9 = (f32[64,64]{1,0:T(8,128)S(1)}, f32[64,64]{1,0:T(8,128)}, u32[]{:S(2)}) copy-start(f32[64,64]{1,0:T(8,128)} %copy-done.8) | copy-start | bytes 49156
  294.7 5.8 %copy-start.3 = (bf16[32,16,64]{2,1,0:T(8,128)(2,1)S(1)}, bf16[32,16,64]{2,1,0:T(8,128)(2,1)}, u32[]{:S(2)}) copy-start(bf16[32,16,64]{2,1,0:T(8,128)(2,1)} %param.13) | copy-start | bytes 196612
  294.7 5.8 %copy-start.5 = (f32[32,16,256]{2,1,0:T(8,128)S(1)}, f32[32,16,256]{2,1,0:T(8,128)}, u32[]{:S(2)}) copy-start(f32[32,16,256]{2,1,0:T(8,128)} %copy-done.4) | copy-start | bytes 1572868
  294.7 5.8 %copy-start.11 = (bf16[256,64]{0,1:T(8,128)(2,1)S(1)}, bf16[256,64]{0,1:T(8,128)(2,1)}, u32[]{:S(2)}) copy-start(bf16[256,64]{0,1:T(8,128)(2,1)} %param.22) | copy-start | bytes 98308
Sparse Core Ops, SparseCore 0:
  14.3 64.4 all-gather.2
  81.0 15.1 all-gather.4
  174.5 61.3 all-reduce.2
  238.7 21.4 all-reduce.4
  276.5 23.9 reduce-scatter.1
where the time goes:
time: 310 us; the launch traced here: 309 us
  waiting for transfers between devices  107 us (35%)
  matrix products  86.3 us (28%)
  blocking collectives  43.9 us (14%)
  local copies, waits for them, and re-layouts  36.1 us (12%)
  other arithmetic  15.6 us (5%)
  between operations  14.2 us (5%)
  loops' own time  5.34 us (2%)
    dot_general x8, matrix products, one_block(): jnp.dot(outer_rows(0 + number * block_rows, block_rows), outer_matrix, pr...  59.2 us
    all_gather x1, waiting for transfers between devices, on_device(): every_joined = lax.all_gather(joined, ('row', 'col'), axis=1, tiled=True)  53.7 us
    psum x1, waiting for transfers between devices, on_device(): lax.psum(pieces.reshape(tile_i, tile_j, outer_matrix.shape[1]), 'seq')  50.9 us
    transpose x8, local copies, waits for them, and re-layouts, outer_rows(): jnp.einsum('sic,sjd->ijcd', rows_part, cols_right, preferred_element_type...  19 us
    pmax x1, blocking collectives, on_device(): row_max = lax.pmax(local_peak, 'col')  12.6 us
    psum x1, blocking collectives, on_device(): row_sum = lax.psum(jnp.sum(scaled, axis=1), 'col')  11.6 us
    psum x1, blocking collectives, on_device(): inner_sum = lax.psum(jnp.sum(probabilities * grad_weights, axis=1), 'col')  11 us
    all_gather x1, blocking collectives, on_device(): rows_left = lax.all_gather(left_proj, 'col', axis=1, tiled=True)  8.65 us
  transfers between devices with their start and end apart: 5, of which 3 were waited for; matrix products, arithmetic and copies ran while one was open for 40% of the time, Pallas kernels for 0%

commit v1 on v0

v1 whole, which is shorter than its diff:
```python
import functools

import jax
import jax.numpy as jnp
from jax import lax
from jax.experimental import pallas as pl
from jax.experimental.pallas import tpu as pltpu
from jax.sharding import PartitionSpec as P

epsilon = 1e-05
far_below = -1e30
vmem_bytes = 48 * 1024 * 1024
pack = 4

f32 = jnp.float32
bf16 = jnp.bfloat16


def nt_dot(a, b):
    return lax.dot_general(a, b, (((1,), (1,)), ((), ())), preferred_element_type=f32)


def nn_dot(a, b):
    return jnp.dot(a, b, preferred_element_type=f32)


def high_low(x):
    high = x.astype(bf16)
    return high, (x - high.astype(f32)).astype(bf16)


def split3(x):
    a = lax.reduce_precision(x, 8, 7)
    b = lax.reduce_precision(x - a, 8, 7)
    c = lax.reduce_precision(x - a - b, 8, 7)
    return a.astype(bf16), b.astype(bf16), c.astype(bf16)


def call(kernel, out_shape, scratch=(), smem=0, flops=0, nbytes=0):
    count = None

    def run(*args):
        specs = [pl.BlockSpec(memory_space=pltpu.SMEM)] * smem
        specs += [pl.BlockSpec(memory_space=pltpu.VMEM)] * (len(args) - smem)
        return pl.pallas_call(
            kernel,
            out_shape=out_shape,
            in_specs=specs,
            out_specs=jax.tree.map(lambda _: pl.BlockSpec(memory_space=pltpu.VMEM), out_shape),
            scratch_shapes=list(scratch),
            compiler_params=pltpu.CompilerParams(vmem_limit_bytes=vmem_bytes),
            cost_estimate=pl.CostEstimate(flops=flops, bytes_accessed=nbytes, transcendentals=0),
        )(*args)

    return run


def prepare_kernel(x_ref, xt_ref, adj_ref, w1_ref, mask_ref, norm_ref, both_ref, left_ref):
    def normalize(x):
        x = x.astype(f32)
        center = x - jnp.mean(x, axis=-1, keepdims=True)
        inverse = lax.rsqrt(jnp.mean(center * center, axis=-1, keepdims=True) + epsilon)
        return (center * inverse).astype(bf16)

    seqs, tokens, width = x_ref.shape
    normed = normalize(x_ref[...])
    norm_ref[...] = normed
    both_ref[...] = jnp.concatenate([normed, adj_ref[...]], axis=-1)
    turned = normalize(xt_ref[...]).reshape(tokens * seqs, width)
    left_ref[...] = (nt_dot(w1_ref[...], turned) * mask_ref[...]).astype(bf16)


def update_kernel(
    left_ref,
    xc_ref,
    w2_ref,
    maskj_ref,
    mt_ref,
    st_ref,
    pair_ref,
    pout_ref,
    pout_t_ref,
    logits_ref,
    rr_ref,
    lm_ref,
    oh_ref,
    ol_ref,
):
    nq, nk, fc, _ = left_ref.shape
    seqs, tokens = xc_ref.shape[2], xc_ref.shape[3]
    tile_j = nk * tokens
    width_d = w2_ref.shape[0]
    groups = pair_ref.shape[0] // (pack * tile_j)
    per_k = groups // nk
    lanes = pack * tile_j
    wk = pack * seqs
    z = pair_ref.shape[1]

    w2 = w2_ref[...]
    maskj = maskj_ref[...]

    def right_of(q, carry):
        for s in range(seqs):
            x = jnp.concatenate([xc_ref[q, k, s] for k in range(nk)], axis=0)
            res = nt_dot(w2, jnp.concatenate([x, x], axis=0)) * maskj
            rr_ref[q, :, s, :] = res
        return carry

    lax.fori_loop(0, nq, right_of, 0)

    for q in range(nq):
        for k in range(nk):
            for g in range(per_k):
                row = (k * per_k + g) * fc
                lm_ref[row : row + fc, q * wk : (q + 1) * wk] = left_ref[
                    q, k, :, g * wk : (g + 1) * wk
                ]

    first = lax.broadcasted_iota(jnp.int32, (seqs, 2 * tile_j), 1) < tile_j

    def outer_of(d, carry):
        empty = jnp.zeros((seqs, 2 * tile_j), bf16)
        rows = []
        for q in range(nq):
            both = rr_ref[q, d]
            part = (
                jnp.where(first, both, 0.0).astype(bf16),
                jnp.where(first, 0.0, both).astype(bf16),
            )
            for i in range(pack):
                pieces = [empty] * (pack // 2)
                pieces[i // 2] = part[i % 2]
                rows.append(jnp.concatenate(pieces, axis=1))
        block = jnp.concatenate(rows, axis=0)
        out = nn_dot(lm_ref[...], block)
        high, low = high_low(out)
        at = pl.ds(pl.multiple_of(d * fc, fc), fc)
        oh_ref[:, at, :] = high.reshape(groups, fc, lanes)
        ol_ref[:, at, :] = low.reshape(groups, fc, lanes)
        return carry

    lax.fori_loop(0, width_d, outer_of, 0, unroll=2)

    maskl = jnp.concatenate([maskj] * (pack // 2), axis=1) > 0

    def finish(g, carry):
        mt = mt_ref[...]
        two = nn_dot(mt, oh_ref[g])
        update = two[:z] + two[z:] + nn_dot(mt[:z], ol_ref[g])
        at = pl.ds(pl.multiple_of(g * lanes, lanes), lanes)
        before = pair_ref[at, :].astype(f32).T
        result = (before + update).astype(bf16)
        pout_t_ref[g] = result
        x = result.astype(f32)
        pout_ref[at, :] = x.T.astype(bf16)
        center = x - jnp.mean(x, axis=0, keepdims=True)
        inverse = lax.rsqrt(jnp.mean(center * center, axis=0, keepdims=True) + epsilon)
        high, low = high_low(center * inverse)
        scores = nn_dot(st_ref[...], jnp.concatenate([high, low], axis=0))
        heads = logits_ref.shape[1]
        logits = scores[:heads] + scores[heads : 2 * heads] + scores[2 * heads : 3 * heads]
        logits_ref[g] = jnp.where(maskl, logits, far_below)
        return carry

    lax.fori_loop(0, groups, finish, 0, unroll=2)


def weights_kernel(
    col_ref,
    xc_ref,
    rows_ref,
    wv_ref,
    wga_ref,
    logits_ref,
    maskj_ref,
    gw_ref,
    own_ref,
    pay1_ref,
    pay2_ref,
    pay3_ref,
    acc_ref,
):
    nq, nk, seqs, tokens, _ = xc_ref.shape
    tile = nk * tokens
    groups, heads, lanes = logits_ref.shape
    chans = wv_ref.shape[1]
    head_width = chans // heads
    wv = wv_ref[...]
    wga = wga_ref[...]
    owner = lax.broadcasted_iota(jnp.int32, (tile, chans), 1) // head_width
    step = 4

    acc_ref[...] = jnp.zeros_like(acc_ref)

    def some(n, carry):
        q = n // (seqs // step)
        s0 = (n % (seqs // step)) * step
        vs, gs = [], []
        for ds in range(step):
            x = jnp.concatenate([xc_ref[q, k, s0 + ds] for k in range(nk)], axis=0)
            v = nn_dot(x, wv).astype(bf16)
            vs.append(jnp.concatenate([v, v], axis=0))
            r = jnp.concatenate([rows_ref[q, k, s0 + ds] for k in range(nk)], axis=0)
            both = nn_dot(r, wga)
            gs.append((both[:, chans:] * jax.nn.sigmoid(both[:, :chans])).astype(bf16))
        spread = [
            jnp.concatenate(
                [jnp.where(owner == h, g, jnp.zeros_like(g)) for h in range(heads)], axis=0
            )
            for g in gs
        ]
        acc_ref[...] += nt_dot(jnp.concatenate(spread, axis=1), jnp.concatenate(vs, axis=1))
        return carry

    lax.fori_loop(0, nq * (seqs // step), some, 0)

    first = lax.broadcasted_iota(jnp.int32, (groups, 2 * tile), 1) < tile
    for h in range(heads):
        for half in range(pack // 2):
            a = acc_ref[pl.ds(h * tile + 2 * half, groups, stride=pack), :]
            b = acc_ref[pl.ds(h * tile + 2 * half + 1, groups, stride=pack), :]
            gw_ref[:, h, half * 2 * tile : (half + 1) * 2 * tile] = jnp.where(first, a, b)

    rows = groups * heads
    lane = lax.broadcasted_iota(jnp.int32, (rows, 2 * tile), 1)
    low = lane < tile
    maskj = maskj_ref[...]
    stats = jnp.zeros((rows, 2 * tile), f32)
    for half in range(pack // 2):
        cut = slice(half * 2 * tile, (half + 1) * 2 * tile)
        lg = logits_ref[:, :, cut].reshape(rows, 2 * tile)
        gw = gw_ref[:, :, cut].reshape(rows, 2 * tile)
        m0 = jnp.max(jnp.where(low, lg, far_below), axis=1, keepdims=True)
        m1 = jnp.max(jnp.where(low, far_below, lg), axis=1, keepdims=True)
        p = jnp.exp(lg - jnp.where(low, m0, m1)) * maskj
        pg = p * gw
        for e, m in ((0, m0), (1, m1)):
            mine = low if e == 0 else jnp.logical_not(low)
            i = 2 * half + e
            total = jnp.sum(jnp.where(mine, p, 0.0), axis=1, keepdims=True)
            inner = jnp.sum(jnp.where(mine, pg, 0.0), axis=1, keepdims=True)
            stats = jnp.where(lane == i, m, stats)
            stats = jnp.where(lane == pack + i, total, stats)
            stats = jnp.where(lane == 2 * pack + i, inner, stats)
    turned = stats.T[:16]
    col = col_ref[0]
    per = groups // nk
    for shift, pay in enumerate((own_ref, pay1_ref, pay2_ref, pay3_ref)):
        dest = lax.rem(col + shift, nk)
        pay[0] = turned[:8]
        pay[1] = turned[8:]
        for g in range(per):
            piece = logits_ref[dest * per + g]
            for half in range(pack // 2):
                pay[2 + g * (pack // 2) + half] = piece[:, half * 2 * tile : (half + 1) * 2 * tile]


def values_kernel(all_ref, wv_ref, norm_ref, wg_ref, v_ref, gate_ref):
    owners, seqs, tokens, width = all_ref.shape
    wv = wv_ref[...]
    for s in range(seqs):
        x = jnp.concatenate([all_ref[k, s] for k in range(owners)], axis=0)
        v_ref[s] = nn_dot(x, wv).astype(bf16)
    gate_ref[...] = jax.nn.sigmoid(
        nn_dot(norm_ref[...].reshape(seqs * tokens, width), wg_ref[...])
    )


def gradient_kernel(
    own_ref, r1_ref, r2_ref, r3_ref, logits_ref, gw_ref, pout_t_ref, sk_ref, out_ref, stat_ref
):
    groups, heads, lanes = logits_ref.shape
    rows = groups * heads
    pays = (own_ref, r1_ref, r2_ref, r3_ref)
    ms = [p[0][:pack] for p in pays]
    ls = [p[0][pack : 2 * pack] for p in pays]
    ns = [p[1][:pack] for p in pays]
    top = functools.reduce(jnp.maximum, ms)
    scales = [jnp.exp(m - top) for m in ms]
    total = sum(a * b for a, b in zip(ls, scales))
    inner = sum(a * b for a, b in zip(ns, scales)) / total
    stacked = jnp.concatenate([top, total, inner, jnp.zeros((rows - 3 * pack, rows), f32)], axis=0)
    stat_ref[...] = stacked.T

    tile = lanes // pack
    low = lax.broadcasted_iota(jnp.int32, (heads, 2 * tile), 1) < tile

    def one(g, carry):
        st = stat_ref[pl.ds(pl.multiple_of(g * heads, heads), heads), :]

        def spread(base):
            halves = [
                jnp.where(
                    low,
                    st[:, base + 2 * half : base + 2 * half + 1],
                    st[:, base + 2 * half + 1 : base + 2 * half + 2],
                )
                for half in range(pack // 2)
            ]
            return jnp.concatenate(halves, axis=1)

        prob = jnp.exp(logits_ref[g] - spread(0)) / spread(pack)
        gl = prob * (gw_ref[g] - spread(2 * pack))
        g1 = gl.astype(bf16).astype(f32)
        g2 = (gl - g1).astype(bf16).astype(f32)
        g3 = gl - g1 - g2
        stack = jnp.concatenate([g1, g2, g3, g1, g2, g1], axis=0).astype(bf16)
        grad = nn_dot(sk_ref[...], stack)
        x = pout_t_ref[g].astype(f32)
        center = x - jnp.mean(x, axis=0, keepdims=True)
        inverse = lax.rsqrt(jnp.mean(center * center, axis=0, keepdims=True) + epsilon)
        normal = center * inverse
        centered = grad - jnp.mean(grad, axis=0, keepdims=True)
        along = jnp.mean(grad * normal, axis=0, keepdims=True)
        result = inverse * (centered - normal * along)
        out_ref[pl.ds(pl.multiple_of(g * lanes, lanes), lanes), :] = result.T.astype(bf16)
        return carry

    lax.fori_loop(0, groups, one, 0, unroll=2)


def alignment_kernel(
    col_ref,
    own_ref,
    r1_ref,
    r2_ref,
    r3_ref,
    v_ref,
    gate_ref,
    x_ref,
    wf_ref,
    out_ref,
    w_ref,
    gated_ref,
):
    pays = (own_ref, r1_ref, r2_ref, r3_ref)
    nk = len(pays)
    heads = own_ref.shape[1]
    wide = own_ref.shape[2]
    tile = wide // 2
    pieces = own_ref.shape[0] - 2
    rows = pieces * heads
    seqs, all_tokens, chans = v_ref.shape
    tokens = pieces * 2
    head_width = chans // heads
    col = col_ref[0]

    low = lax.broadcasted_iota(jnp.int32, (rows, wide), 1) < tile
    lgs = [p[2:].reshape(rows, wide) for p in pays]
    peak = functools.reduce(jnp.maximum, lgs)
    m0 = jnp.max(jnp.where(low, peak, far_below), axis=1, keepdims=True)
    m1 = jnp.max(jnp.where(low, far_below, peak), axis=1, keepdims=True)
    top = jnp.where(low, m0, m1)
    ps = [jnp.exp(lg - top) for lg in lgs]
    every = sum(ps)
    t0 = jnp.sum(jnp.where(low, every, 0.0), axis=1, keepdims=True)
    t1 = jnp.sum(jnp.where(low, 0.0, every), axis=1, keepdims=True)
    total = jnp.where(low, t0, t1)
    for shift, p in enumerate(ps):
        source = lax.rem(col + nk - shift, nk)
        weight = p / total
        rolled = pltpu.roll(weight, tile, 1)
        for n in range(pieces):
            w_ref[source, :, 2 * n, :] = weight[n * heads : (n + 1) * heads]
            w_ref[source, :, 2 * n + 1, :] = rolled[n * heads : (n + 1) * heads]
    w = jnp.concatenate(
        [w_ref[k].reshape(heads * tokens, wide)[:, :tile] for k in range(nk)], axis=1
    ).astype(bf16)

    owner = lax.broadcasted_iota(jnp.int32, (tokens, chans), 1) // head_width

    def one(s, carry):
        full = nn_dot(w, v_ref[s])
        mean = jnp.zeros((tokens, chans), f32)
        for h in range(heads):
            mean = jnp.where(owner == h, full[h * tokens : (h + 1) * tokens], mean)
        at = pl.ds(pl.multiple_of(s * tokens, tokens), tokens)
        gated_ref[at, :] = (gate_ref[at, :] * mean).astype(bf16)
        return carry

    lax.fori_loop(0, seqs, one, 0, unroll=4)
    out_ref[...] = (x_ref[...].astype(f32) + nn_dot(gated_ref[...], wf_ref[...])).astype(bf16)


def on_device(
    counts,
    alignment_input,
    pair_input,
    token_valid_mask,
    first_factor_weights,
    second_factor_weights,
    content_weights_grid,
    sigmoid_weights_grid,
    outer_matrix,
    score_matrix,
    final_mixing_weights,
    adjoint_of_rowset,
):
    nq, nr, nk = counts
    row_index = lax.axis_index("row")
    col_index = lax.axis_index("col")
    seqs, tokens, width = alignment_input.shape
    tile_i, tile_j, z = pair_input.shape
    fc = first_factor_weights.shape[1]
    fd = second_factor_weights.shape[1]
    heads = score_matrix.shape[1]
    chans = content_weights_grid.shape[1]
    groups = tile_i // pack
    lanes = pack * tile_j
    sds = jax.ShapeDtypeStruct

    maskf = token_valid_mask.astype(f32)
    own_start = (row_index * nk + col_index) * tokens
    own_mask = lax.dynamic_slice_in_dim(maskf, own_start, tokens)
    own_mask = jnp.broadcast_to(own_mask[:, None], (tokens, seqs)).reshape(1, tokens * seqs)
    col_mask = lax.dynamic_slice_in_dim(maskf, col_index * tile_j, tile_j)
    col_mask = jnp.concatenate([col_mask, col_mask]).reshape(1, 2 * tile_j)
    col_scalar = col_index.astype(jnp.int32).reshape(1)

    normed, both, left = call(
        prepare_kernel,
        (
            sds((seqs, tokens, width), bf16),
            sds((seqs, tokens, 2 * width), bf16),
            sds((fc, tokens * seqs), bf16),
        ),
    )(
        alignment_input,
        jnp.swapaxes(alignment_input, 0, 1),
        adjoint_of_rowset,
        first_factor_weights.T,
        own_mask,
    )

    turn = [(r * nk + c, c * nk + r) for r in range(nr) for c in range(nk)]
    crossed = lax.ppermute(normed, ("row", "col"), turn)
    lefts = lax.all_gather(left, ("seq", "col"), axis=0).reshape(nq, nk, fc, tokens * seqs)
    cols = lax.all_gather(crossed, ("seq", "row"), axis=0).reshape(nq, nk, seqs, tokens, width)
    rows = lax.all_gather(both, ("seq", "col"), axis=0).reshape(nq, nk, seqs, tokens, 2 * width)
    every = lax.all_gather(normed, ("row", "col"), axis=0)

    m3 = outer_matrix.reshape(fc, fd, z).transpose(2, 1, 0).reshape(z, fd * fc)
    m_high = lax.reduce_precision(m3, 8, 7)
    mt = jnp.concatenate([m_high, m3 - m_high], axis=0).astype(bf16)
    s1, s2, s3 = split3(score_matrix)
    none = jnp.zeros((heads, z), bf16)
    st = jnp.concatenate(
        [
            jnp.concatenate([s1.T, s1.T], axis=1),
            jnp.concatenate([s2.T, s2.T], axis=1),
            jnp.concatenate([s3.T, none], axis=1),
            jnp.concatenate([none, none], axis=1),
        ],
        axis=0,
    )
    sk = jnp.concatenate([s1, s1, s1, s2, s2, s3], axis=1)
    blank = jnp.zeros((width, chans), bf16)
    wga = jnp.concatenate(
        [
            jnp.concatenate([sigmoid_weights_grid, blank], axis=1),
            jnp.concatenate([blank, final_mixing_weights.T], axis=1),
        ],
        axis=0,
    )

    pair_out, pair_t, logits = call(
        update_kernel,
        (
            sds((tile_i * tile_j, z), bf16),
            sds((groups, z, lanes), bf16),
            sds((groups, heads, lanes), f32),
        ),
        scratch=(
            pltpu.VMEM((nq, fd, seqs, 2 * tile_j), f32),
            pltpu.VMEM((groups * fc, nq * pack * seqs), bf16),
            pltpu.VMEM((groups, fd * fc, lanes), bf16),
            pltpu.VMEM((groups, fd * fc, lanes), bf16),
        ),
        flops=14_000_000_000,
        nbytes=5_000_000,
    )(
        lefts,
        cols,
        second_factor_weights.T,
        col_mask,
        mt,
        st,
        pair_input.reshape(tile_i * tile_j, z),
    )

    payload = sds((2 + groups // nk * (pack // 2), heads, 2 * tile_j), f32)
    gw, pay0, pay1, pay2, pay3 = call(
        weights_kernel,
        (sds((groups, heads, lanes), f32), payload, payload, payload, payload),
        scratch=(pltpu.VMEM((heads * tile_i, 2 * tile_j), f32),),
        smem=1,
        flops=6_000_000_000,
        nbytes=3_000_000,
    )(col_scalar, cols, rows, content_weights_grid, wga, logits, col_mask)

    got = [
        lax.ppermute(pay, "col", [(c, (c + shift) % nk) for c in range(nk)])
        for shift, pay in ((1, pay1), (2, pay2), (3, pay3))
    ]

    values, gating = call(
        values_kernel,
        (sds((seqs, nr * nk * tokens, chans), bf16), sds((seqs * tokens, chans), f32)),
        flops=4_000_000_000,
        nbytes=6_000_000,
    )(every, content_weights_grid, normed, sigmoid_weights_grid)

    gradient = call(
        gradient_kernel,
        sds((tile_i * tile_j, z), bf16),
        scratch=(pltpu.VMEM((groups * heads, groups * heads), f32),),
        flops=4_000_000_000,
        nbytes=3_000_000,
    )(pay0, *got, logits, gw, pair_t, sk)

    aligned = call(
        alignment_kernel,
        sds((seqs * tokens, width), bf16),
        scratch=(
            pltpu.VMEM((nk, heads, tokens, 2 * tile_j), f32),
            pltpu.VMEM((seqs * tokens, chans), bf16),
        ),
        smem=1,
        flops=3_000_000_000,
        nbytes=5_000_000,
    )(
        col_scalar,
        pay0,
        *got,
        values,
        gating,
        alignment_input.reshape(seqs * tokens, width),
        final_mixing_weights,
    )
    return (
        aligned.reshape(seqs, tokens, width),
        pair_out.reshape(tile_i, tile_j, z),
        gradient.reshape(tile_i, tile_j, z),
    )


def solution(mesh):
    counts = (mesh.shape["seq"], mesh.shape["row"], mesh.shape["col"])
    in_specs = (
        P("seq", ("row", "col"), None),
        P("row", "col", None),
        P(),
        P(),
        P(),
        P(),
        P(),
        P(),
        P(),
        P(),
        P("seq", ("row", "col"), None),
    )
    out_specs = (P("seq", ("row", "col"), None), P("row", "col", None), P("row", "col", None))
    return jax.shard_map(
        functools.partial(on_device, counts),
        mesh=mesh,
        in_specs=in_specs,
        out_specs=out_specs,
        check_vma=False,
    )
```

time: 310 us -> 129 us (0.42)
  waiting for transfers between devices: 107 us -> 1.45 us
  matrix products: 86.3 us -> 0 us
  Pallas kernels: 0 us -> 42.1 us
  local copies, waits for them, and re-layouts: 36.1 us -> 10.7 us
  other arithmetic: 15.6 us -> 3.75 us
  blocking collectives: 43.9 us -> 50.9 us
  loops' own time: 5.34 us -> 0 us
  starting transfers between devices: 0.39 us -> 4.91 us
    dot_general x26 -> x0, matrix products: 86.3 us -> none  [the longest x8 59.2 us: one_block(): jnp.dot(outer_rows(0 + number * block_rows, block_rows), outer_matrix, pr...]
    all_gather x2, waiting for transfers between devices: 53.7 us -> 0.01 us  [the longest x1 0.01 us: on_device(): lax.all_gather(both, ('seq', 'col'), axis=0)]
    psum x2 -> x0, waiting for transfers between devices: 50.9 us -> none  [the longest x1 50.9 us: on_device(): lax.psum(pieces.reshape(tile_i, tile_j, outer_matrix.shape[1]), 'seq')]
    all_gather x1 -> x2, blocking collectives: 8.65 us -> 50.9 us  [the longest x1 36.7 us: on_device(): lax.all_gather(crossed, ('seq', 'row'), axis=0)]
    pallas_call x0 -> x6, Pallas kernels: none -> 42.1 us  [run(): pl.pallas_call(kernel, out_shape=out_shape, in_specs=specs, out_specs=jax...]
    psum x2 -> x0, blocking collectives: 22.6 us -> none  [the longest x1 11.6 us: on_device(): row_sum = lax.psum(jnp.sum(scaled, axis=1), 'col')]
    transpose x8 -> x1, local copies, waits for them, and re-layouts: 19 us -> 1.35 us  [on_device(): m3 = outer_matrix.reshape(fc, fd, z).transpose(2, 1, 0).reshape(z, fd * fc)]
    pmax x1 -> x0, blocking collectives: 12.6 us -> none  [on_device(): row_max = lax.pmax(local_peak, 'col')]
  transfers between devices with their start and end apart: 5 -> 6, of which waited for: 3 -> 2; matrix products, arithmetic and copies ran while one was open for 40% -> 4% of each run, Pallas kernels for 0% -> 26%
where the time goes in v1:
time: 129 us; the launch traced here: 128 us
  blocking collectives  50.9 us (39%)
  Pallas kernels  42.1 us (33%)
  between operations  14.2 us (11%)
  local copies, waits for them, and re-layouts  10.7 us (8%)
  starting transfers between devices  4.91 us (4%)
  other arithmetic  3.75 us (3%)
  waiting for transfers between devices  1.45 us (1%)
    pallas_call x6, Pallas kernels, run(): pl.pallas_call(kernel, out_shape=out_shape, in_specs=specs, out_specs=jax...  42.1 us
    all_gather x1, blocking collectives, on_device(): lax.all_gather(crossed, ('seq', 'row'), axis=0)  36.7 us
    all_gather x1, blocking collectives, on_device(): lax.all_gather(left, ('seq', 'col'), axis=0)  14.2 us
    unnamed x30, local copies, waits for them, and re-layouts  8.6 us
    ppermute x3, starting transfers between devices, on_device(): lax.ppermute(pay, 'col', [(c, (c + shift) % nk) for c in range(nk)])  3.27 us
  transfers between devices with their start and end apart: 6, of which 2 were waited for; matrix products, arithmetic and copies ran while one was open for 4% of the time, Pallas kernels for 26%

profile of v1, /device:TPU:0, one launch (start us, length us, event | category | flops | bytes accessed | tf_op | source)
XLA Modules:
  0.0 127.9 jit_solution(6932456071182766282)
XLA Ops:
  7.2 0.0 copy-start.11
  7.2 0.0 copy-start.3
  7.2 0.0 copy-start.9
  7.2 0.0 all-gather.7.cloned.1.call-start
  7.2 0.7 convert_element_type.13
  7.9 0.1 dynamic_slice.6
  8.0 0.1 broadcast_in_dim.2
  8.1 0.1 reshape.47.mask_ref
  8.2 0.9 copy.42
  9.1 0.0 copy-start
  9.1 0.9 copy-done
  10.0 0.9 copy-done.2
  10.9 0.0 copy-start.4
  10.9 0.7 copy-done.4
  11.6 0.0 copy-start.6
  11.6 1.1 shard_map.130
  12.7 0.0 all-gather.7.cloned.1.call-update
  12.7 0.0 all-gather.9.cloned.1.call-start
  12.8 1.6 %collective-permute-start = (bf16[32,16,64]{2,1,0:T(8,128)(2,1)}, bf16[32,16,64]{2,1,0:T(8,128)(2,1)S(1)}, u32[]{:S(2)}, u32[]{:S(2)}) collective-permute-start(bf16[32,16,64]{2,1,0:T(8,128)(2,1)} %get-tuple-element.16.norm_ref), channel_id=1, source_target_pairs={{0,0},{1,4},{2,8},{3,12},{4,1},{5,5},{6,9},{7,13},{8,2},{9,6},{10,... | collective-permute-start | bytes 196616 | tf_op jit(solution)/shard_map/ppermute | solution.py:436
  14.3 0.0 all-gather.9.cloned.1.call-update
  14.4 0.7 constant_dynamic-update-slice_fusion.5
  15.1 0.7 fusion.11
  15.7 0.1 dynamic_slice.7
  15.8 1.3 %copy.36 = f32[128,32,32]{0,2,1:T(8,128)S(1)} copy(f32[128,32,32]{0,1,2:T(8,128)} %bitcast.38) | data formatting | bytes 1048576 | tf_op jit(solution)/shard_map/transpose | solution.py:442
  17.2 0.2 copy.37
  17.4 0.1 reduce-precision_convert_fusion
  17.5 0.7 constant_dynamic-update-slice_fusion.2
  18.2 0.7 constant_dynamic-update-slice_fusion.1
  18.9 0.1 pad.8.clone
  19.0 0.0 copy-done.11
  19.0 0.0 copy-done.3
  19.0 0.1 fusion.7.st_ref
  19.1 0.1 maximum_bitcast_fusion.maskj_ref
  19.2 14.2 %all-gather.2 = bf16[256,512]{1,0:T(8,128)(2,1)S(1)} all-gather(bf16[32,512]{1,0:T(8,128)(2,1)S(1)} %get-tuple-element.18), channel_id=4, replica_groups=mesh['seq'=2,'row'=4,'col'=4] {'seq','col'}, dimensions={0}, use_global_device_ids=true | all-gather | bytes 294912 | tf_op jit(solution)/shard_map/all_gather | solution.py:437
  33.4 0.0 collective-permute-done
  33.4 36.7 %all-gather = bf16[256,16,64]{2,1,0:T(8,128)(2,1)S(1)} all-gather(bf16[32,16,64]{2,1,0:T(8,128)(2,1)S(1)} %collective-permute-done), channel_id=2, replica_groups=mesh['seq'=2,'row'=4,'col'=4] {'seq','row'}, dimensions={0}, use_global_device_ids=true | all-gather | bytes 589824 | tf_op jit(solution)/shard_map/all_gather | solution.py:438
  70.1 0.0 copy-done.9
  70.1 0.0 copy-done.6
  70.1 0.0 copy-start.8
  70.1 19.1 %shard_map.131 = (bf16[4096,128]{1,0:T(8,128)(2,1)}, bf16[16,128,256]{2,1,0:T(8,128)(2,1)S(1)}, f32[16,8,256]{2,1,0:T(8,128)S(1)}) custom-call(bf16[2,4,32,512]{3,2,1,0:T(8,128)(2,1)S(1)} %bitcast.31, bf16[2,4,32,16,64]{4,3,2,1,0:T(8,128)(2,1)S(1)} %bitcast.27, bf16[32,64]{1,0:T(8,128)(2,1)S(1)} %bitcast.36, f32[1,128]{1,0:T(1,128)S(1)} %maximum_bitcast_fusion.maskj_ref, ...), custom_call_target="tpu_custom_call" | custom-call | flops 14000000000 | bytes 5000000 | tf_op jit(solution)/shard_map/pallas_call | solution.py:45
  89.2 0.0 all-gather.7.cloned.1.call-done
  89.2 0.0 copy-done.8
  89.2 0.0 copy-start.7
  89.2 1.2 copy-done.7
  90.4 0.0 copy-start.12
  90.4 10.2 %shard_map.132 = (f32[16,8,256]{2,1,0:T(8,128)S(1)}, f32[10,8,128]{2,1,0:T(8,128)S(1)}, f32[10,8,128]{2,1,0:T(8,128)S(1)}, f32[10,8,128]{2,1,0:T(8,128)S(1)}, f32[10,8,128]{2,1,0:T(8,128)S(1)}) custom-call(s32[1]{0:T(128)} %bitcast.col_ref, bf16[2,4,32,16,64]{4,3,2,1,0:T(8,128)(2,1)S(1)} %bitcast.28, bf16[2,4,32,16,128]{4,3,2,1,0:T(8,128)(2,1)S(1)} %bitcast.35, ...), custom_call_target="tpu_custom_call" | custom-call | flops 6000000000 | bytes 3000000 | tf_op jit(solution)/shard_map/pallas_call | solution.py:45
  100.6 0.0 collective-permute-start.1
  100.6 1.8 %collective-permute-start.2 = (f32[10,8,128]{2,1,0:T(8,128)S(1)}, f32[10,8,128]{2,1,0:T(8,128)S(1)}, u32[]{:S(2)}, u32[]{:S(2)}) collective-permute-start(f32[10,8,128]{2,1,0:T(8,128)S(1)} %get-tuple-element.22), channel_id=1, source_target_pairs={{0,2},{1,3},{2,0},{3,1},{4,6},{5,7},{6,4},{7,5},{8,10},{9,11},{10,... | collective-permute-start | bytes 122888 | tf_op jit(solution)/shard_map/ppermute | solution.py:502
  102.4 1.4 %collective-permute-start.3 = (f32[10,8,128]{2,1,0:T(8,128)S(1)}, f32[10,8,128]{2,1,0:T(8,128)S(1)}, u32[]{:S(2)}, u32[]{:S(2)}) collective-permute-start(f32[10,8,128]{2,1,0:T(8,128)S(1)} %get-tuple-element.23), channel_id=1, source_target_pairs={{0,3},{1,0},{2,1},{3,2},{4,7},{5,4},{6,5},{7,6},{8,11},{9,8},{10,9... | collective-permute-start | bytes 122888 | tf_op jit(solution)/shard_map/ppermute | solution.py:502
  103.8 0.0 copy-done.12
  103.9 0.1 copy.39.wf_ref
  104.0 0.1 copy.40.sk_ref
  104.1 0.0 collective-permute-done.1.r1_ref
  104.1 0.6 collective-permute-done.2.r2_ref
  104.7 0.8 collective-permute-done.3.r3_ref
  105.5 4.3 %shard_map.135 = bf16[4096,128]{1,0:T(8,128)(2,1)} custom-call(f32[10,8,128]{2,1,0:T(8,128)S(1)} %get-tuple-element.20.own_ref, f32[10,8,128]{2,1,0:T(8,128)S(1)} %collective-permute-done.1.r1_ref, f32[10,8,128]{2,1,0:T(8,128)S(1)} %collective-permute-done.2.r2_ref, f32[10,8,128]{2,1,0:T(8,128)S(1)} %collective-permute-done.3.r3_ref, ...), custom_call_target="tpu_custom_call" | custom-call | flops 4000000000 | bytes 3000000 | tf_op jit(solution)/shard_map/pallas_call | solution.py:45
  109.8 0.0 all-gather.9.cloned.1.call-done
  109.8 0.0 copy-start.5
  109.8 1.6 %copy-done.5 = bf16[512,16,64]{2,1,0:T(8,128)(2,1)S(1)} copy-done((bf16[512,16,64]{2,1,0:T(8,128)(2,1)S(1)}, bf16[512,16,64]{2,1,0:T(8,128)(2,1)}, u32[]{:S(2)}) %copy-start.5) | copy-done | bytes 1048600
  111.4 0.0 copy-start.1
  111.4 4.2 %shard_map.133 = (bf16[32,256,256]{2,1,0:T(8,128)(2,1)}, f32[512,256]{1,0:T(8,128)S(1)}) custom-call(bf16[16,32,16,64]{3,2,1,0:T(8,128)(2,1)S(1)} %bitcast.33, bf16[64,256]{1,0:T(8,128)(2,1)S(1)} %copy-done.8, bf16[32,16,64]{2,1,0:T(8,128)(2,1)} %get-tuple-element.16.norm_ref, bf16[64,256]{1,0:T(8,128)(2,1)S(1)} %copy-done.3), custom_call_target="tpu_custom_call" | custom-call | flops 4000000000 | bytes 6000000 | tf_op jit(solution)/shard_map/pallas_call | solution.py:45
  115.6 0.0 copy-done.1
  115.6 2.2 %copy-done.10 = bf16[32,256,256]{2,1,0:T(8,128)(2,1)S(1)} copy-done((bf16[32,256,256]{2,1,0:T(8,128)(2,1)S(1)}, bf16[32,256,256]{2,1,0:T(8,128)(2,1)}, u32[]{:S(2)}) %copy-start.10) | copy-done | bytes 4194328
  117.8 3.2 %shard_map.134 = bf16[512,64]{1,0:T(8,128)(2,1)} custom-call(s32[1]{0:T(128)} %bitcast.col_ref, f32[10,8,128]{2,1,0:T(8,128)S(1)} %get-tuple-element.20.own_ref, f32[10,8,128]{2,1,0:T(8,128)S(1)} %collective-permute-done.1.r1_ref, f32[10,8,128]{2,1,0:T(8,128)S(1)} %collective-permute-done.2.r2_ref, f32[10,8,128]{2,1,0:T(8,128)S(1)} %collective-permute-done.3.r3_ref, ...), custom_call_target="tpu_custom_call" | custom-call | flops 3000000000 | bytes 5000000 | tf_op jit(solution)/shard_map/pallas_call | solution.py:45
  (8 shorter events, 0.1 us)
Async XLA Ops:
  7.2 11.8 %copy-start.11 = (bf16[256,64]{0,1:T(8,128)(2,1)S(1)}, bf16[256,64]{0,1:T(8,128)(2,1)}, u32[]{:S(2)}) copy-start(bf16[256,64]{0,1:T(8,128)(2,1)} %param.20) | copy-start | bytes 98308
  7.2 11.8 %copy-start.3 = (bf16[64,256]{1,0:T(8,128)(2,1)S(1)}, bf16[64,256]{1,0:T(8,128)(2,1)}, u32[]{:S(2)}) copy-start(bf16[64,256]{1,0:T(8,128)(2,1)} %wg_ref.1) | copy-start | bytes 98308
  7.2 62.9 %copy-start.9 = (bf16[64,32]{0,1:T(8,128)(2,1)S(1)}, bf16[64,32]{0,1:T(8,128)(2,1)}, u32[]{:S(2)}) copy-start(bf16[64,32]{0,1:T(8,128)(2,1)} %param.15) | copy-start | bytes 12292
  7.2 82.0 %all-gather.7.cloned.1.call-start = ((), (), s32[]{:S(2)}) async-start(), calls=%async_computation | async-start | bytes 1179648 | tf_op jit(solution)/shard_map/all_gather | solution.py:439
  9.1 0.9 copy-start
  10.0 0.9 copy-start.2
  10.9 0.7 copy-start.4
  11.6 58.5 %copy-start.6 = (bf16[64,64,128]{2,1,0:T(8,128)(2,1)S(1)}, bf16[64,64,128]{2,1,0:T(8,128)(2,1)}, u32[]{:S(2)}) copy-start(bf16[64,64,128]{2,1,0:T(8,128)(2,1)} %param.12) | copy-start | bytes 3145732
  12.7 97.1 %all-gather.9.cloned.1.call-start = ((), (), s32[]{:S(2)}) async-start(), calls=%async_computation.1 | async-start | bytes 2228224 | tf_op jit(solution)/shard_map/all_gather | solution.py:440
  12.8 20.6 %collective-permute-start = (bf16[32,16,64]{2,1,0:T(8,128)(2,1)}, bf16[32,16,64]{2,1,0:T(8,128)(2,1)S(1)}, u32[]{:S(2)}, u32[]{:S(2)}) collective-permute-start(bf16[32,16,64]{2,1,0:T(8,128)(2,1)} %get-tuple-element.16.norm_ref), channel_id=1, source_target_pairs={{0,0},{1,4},{2,8},{3,12},{4,1},{5,5},{6,9},{7,13},{8,2},{9,6},{10,... | collective-permute-start | bytes 196616 | tf_op jit(solution)/shard_map/ppermute | solution.py:436
  70.1 19.1 %copy-start.8 = (bf16[64,256]{1,0:T(8,128)(2,1)S(1)}, bf16[64,256]{1,0:T(8,128)(2,1)}, u32[]{:S(2)}) copy-start(bf16[64,256]{1,0:T(8,128)(2,1)} %wv_ref.3) | copy-start | bytes 98308
  89.2 1.2 copy-start.7
  90.4 13.5 %copy-start.12 = (f32[128,8]{0,1:T(8,128)S(1)}, f32[128,8]{0,1:T(8,128)}, u32[]{:S(2)}) copy-start(f32[128,8]{0,1:T(8,128)} %param.19) | copy-start | bytes 12292
  100.6 3.5 %collective-permute-start.1 = (f32[10,8,128]{2,1,0:T(8,128)S(1)}, f32[10,8,128]{2,1,0:T(8,128)S(1)}, u32[]{:S(2)}, u32[]{:S(2)}) collective-permute-start(f32[10,8,128]{2,1,0:T(8,128)S(1)} %get-tuple-element.21), channel_id=1, source_target_pairs={{0,1},{1,2},{2,3},{3,0},{4,5},{5,6},{6,7},{7,4},{8,9},{9,10},{10,1... | collective-permute-start | bytes 122888 | tf_op jit(solution)/shard_map/ppermute | solution.py:502
  100.6 4.1 %collective-permute-start.2 = (f32[10,8,128]{2,1,0:T(8,128)S(1)}, f32[10,8,128]{2,1,0:T(8,128)S(1)}, u32[]{:S(2)}, u32[]{:S(2)}) collective-permute-start(f32[10,8,128]{2,1,0:T(8,128)S(1)} %get-tuple-element.22), channel_id=1, source_target_pairs={{0,2},{1,3},{2,0},{3,1},{4,6},{5,7},{6,4},{7,5},{8,10},{9,11},{10,... | collective-permute-start | bytes 122888 | tf_op jit(solution)/shard_map/ppermute | solution.py:502
  102.4 3.1 %collective-permute-start.3 = (f32[10,8,128]{2,1,0:T(8,128)S(1)}, f32[10,8,128]{2,1,0:T(8,128)S(1)}, u32[]{:S(2)}, u32[]{:S(2)}) collective-permute-start(f32[10,8,128]{2,1,0:T(8,128)S(1)} %get-tuple-element.23), channel_id=1, source_target_pairs={{0,3},{1,0},{2,1},{3,2},{4,7},{5,4},{6,5},{7,6},{8,11},{9,8},{10,9... | collective-permute-start | bytes 122888 | tf_op jit(solution)/shard_map/ppermute | solution.py:502
  109.8 1.6 %copy-start.5 = (bf16[512,16,64]{2,1,0:T(8,128)(2,1)S(1)}, bf16[512,16,64]{2,1,0:T(8,128)(2,1)}, u32[]{:S(2)}) copy-start(bf16[512,16,64]{2,1,0:T(8,128)(2,1)} %all-gather.9.cloned.1.call-done) | copy-start | bytes 3145732
  111.4 4.2 %copy-start.1 = (bf16[32,16,64]{2,1,0:T(8,128)(2,1)S(1)}, bf16[32,16,64]{2,1,0:T(8,128)(2,1)}, u32[]{:S(2)}) copy-start(bf16[32,16,64]{2,1,0:T(8,128)(2,1)} %x_ref.1) | copy-start | bytes 196612
  115.6 2.2 %copy-start.10 = (bf16[32,256,256]{2,1,0:T(8,128)(2,1)S(1)}, bf16[32,256,256]{2,1,0:T(8,128)(2,1)}, u32[]{:S(2)}) copy-start(bf16[32,256,256]{2,1,0:T(8,128)(2,1)} %get-tuple-element.24.v_ref) | copy-start | bytes 12582916
Sparse Core Ops, SparseCore 0:
  12.8 26.8 all-gather.6
  42.5 44.1 all-gather.8

commit v2 on v1

--- a/solution.py
+++ b/solution.py
@@ -29,14 +29,7 @@
     return high, (x - high.astype(f32)).astype(bf16)
 
 
-def split3(x):
-    a = lax.reduce_precision(x, 8, 7)
-    b = lax.reduce_precision(x - a, 8, 7)
-    c = lax.reduce_precision(x - a - b, 8, 7)
-    return a.astype(bf16), b.astype(bf16), c.astype(bf16)
-
-
-def call(kernel, out_shape, scratch=(), smem=0, flops=0, nbytes=0):
+def call(kernel, out_shape, scratch=(), smem=0, flops=0, nbytes=0, vmem=vmem_bytes):
     count = None
 
     def run(*args):
@@ -48,46 +41,71 @@
             in_specs=specs,
             out_specs=jax.tree.map(lambda _: pl.BlockSpec(memory_space=pltpu.VMEM), out_shape),
             scratch_shapes=list(scratch),
-            compiler_params=pltpu.CompilerParams(vmem_limit_bytes=vmem_bytes),
+            compiler_params=pltpu.CompilerParams(vmem_limit_bytes=vmem),
             cost_estimate=pl.CostEstimate(flops=flops, bytes_accessed=nbytes, transcendentals=0),
         )(*args)
 
     return run
 
 
-def prepare_kernel(x_ref, xt_ref, adj_ref, w1_ref, mask_ref, norm_ref, both_ref, left_ref):
-    def normalize(x):
-        x = x.astype(f32)
-        center = x - jnp.mean(x, axis=-1, keepdims=True)
-        inverse = lax.rsqrt(jnp.mean(center * center, axis=-1, keepdims=True) + epsilon)
-        return (center * inverse).astype(bf16)
-
+def valid_count(mask_ref):
+    return jnp.sum(mask_ref[...].astype(f32), axis=1, keepdims=True)
+
+
+def column_mask(mask_ref, col, tile, copies):
+    lane = lax.broadcasted_iota(jnp.int32, (1, copies * tile), 1)
+    token = (lax.rem(lane, tile) + col * tile).astype(f32)
+    return (token < valid_count(mask_ref)).astype(f32)
+
+
+def twice(w):
+    none = jnp.zeros_like(w)
+    return jnp.concatenate(
+        [jnp.concatenate([w, none], axis=1), jnp.concatenate([none, w], axis=1)], axis=0
+    )
+
+
+def prepare_kernel(own_ref, x_ref, adj_ref, w1_ref, mask_ref, norm_ref, both_ref, left_ref, turn_ref):
     seqs, tokens, width = x_ref.shape
-    normed = normalize(x_ref[...])
-    norm_ref[...] = normed
-    both_ref[...] = jnp.concatenate([normed, adj_ref[...]], axis=-1)
-    turned = normalize(xt_ref[...]).reshape(tokens * seqs, width)
-    left_ref[...] = (nt_dot(w1_ref[...], turned) * mask_ref[...]).astype(bf16)
+    half = seqs // 2
+    x = x_ref[...].astype(f32)
+    center = x - jnp.mean(x, axis=-1, keepdims=True)
+    inverse = lax.rsqrt(jnp.mean(center * center, axis=-1, keepdims=True) + epsilon)
+    normed = center * inverse
+    packed = jnp.concatenate([normed[:half], normed[half:]], axis=-1).astype(bf16)
+    norm_ref[...] = packed
+    both_ref[0] = packed
+    adj = adj_ref[...].astype(f32)
+    both_ref[1] = jnp.concatenate([adj[:half], adj[half:]], axis=-1).astype(bf16)
+    for s in range(seqs):
+        turn_ref[:, s, :] = normed[s]
+    token = lax.broadcasted_iota(jnp.int32, (tokens, seqs, width), 0) + own_ref[0]
+    count = valid_count(mask_ref).reshape(1, 1, 1)
+    turned = jnp.where(token.astype(f32) < count, turn_ref[...], 0.0).astype(bf16)
+    left_ref[...] = nt_dot(w1_ref[...], turned.reshape(tokens * seqs, width)).astype(bf16)
 
 
 def update_kernel(
+    col_ref,
     left_ref,
     xc_ref,
     w2_ref,
-    maskj_ref,
-    mt_ref,
-    st_ref,
+    mask_ref,
+    m_ref,
+    score_ref,
     pair_ref,
     pout_ref,
     pout_t_ref,
     logits_ref,
     rr_ref,
     lm_ref,
+    mt_ref,
     oh_ref,
     ol_ref,
 ):
     nq, nk, fc, _ = left_ref.shape
-    seqs, tokens = xc_ref.shape[2], xc_ref.shape[3]
+    half, tokens = xc_ref.shape[2], xc_ref.shape[3]
+    seqs = 2 * half
     tile_j = nk * tokens
     width_d = w2_ref.shape[0]
     groups = pair_ref.shape[0] // (pack * tile_j)
@@ -95,15 +113,17 @@
     lanes = pack * tile_j
     wk = pack * seqs
     z = pair_ref.shape[1]
-
-    w2 = w2_ref[...]
-    maskj = maskj_ref[...]
+    heads = logits_ref.shape[1]
+
+    w2 = twice(w2_ref[...])
+    maskj = column_mask(mask_ref, col_ref[0], tile_j, 2)
 
     def right_of(q, carry):
-        for s in range(seqs):
+        for s in range(half):
             x = jnp.concatenate([xc_ref[q, k, s] for k in range(nk)], axis=0)
             res = nt_dot(w2, jnp.concatenate([x, x], axis=0)) * maskj
-            rr_ref[q, :, s, :] = res
+            rr_ref[q, :, s, :] = res[:width_d]
+            rr_ref[q, :, s + half, :] = res[width_d:]
         return carry
 
     lax.fori_loop(0, nq, right_of, 0)
@@ -116,7 +136,17 @@
                     q, k, :, g * wk : (g + 1) * wk
                 ]
 
+    some = z // fc
+    for n in range(width_d // some):
+        block = jnp.concatenate(
+            [m_ref[pl.ds(n * some + e, fc, stride=width_d), :] for e in range(some)], axis=0
+        ).T
+        high, low = high_low(block)
+        mt_ref[:z, n * z : (n + 1) * z] = high
+        mt_ref[z:, n * z : (n + 1) * z] = low
+
     first = lax.broadcasted_iota(jnp.int32, (seqs, 2 * tile_j), 1) < tile_j
+    chunk = 4
 
     def outer_of(d, carry):
         empty = jnp.zeros((seqs, 2 * tile_j), bf16)
@@ -132,21 +162,33 @@
                 pieces[i // 2] = part[i % 2]
                 rows.append(jnp.concatenate(pieces, axis=1))
         block = jnp.concatenate(rows, axis=0)
-        out = nn_dot(lm_ref[...], block)
-        high, low = high_low(out)
         at = pl.ds(pl.multiple_of(d * fc, fc), fc)
-        oh_ref[:, at, :] = high.reshape(groups, fc, lanes)
-        ol_ref[:, at, :] = low.reshape(groups, fc, lanes)
+        for n in range(groups // chunk):
+            out = nn_dot(lm_ref[n * chunk * fc : (n + 1) * chunk * fc, :], block)
+            high, low = high_low(out)
+            oh_ref[n * chunk : (n + 1) * chunk, at, :] = high.reshape(chunk, fc, lanes)
+            ol_ref[n * chunk : (n + 1) * chunk, at, :] = low.reshape(chunk, fc, lanes)
         return carry
 
     lax.fori_loop(0, width_d, outer_of, 0, unroll=2)
 
     maskl = jnp.concatenate([maskj] * (pack // 2), axis=1) > 0
+    score = score_ref[...]
+    s1 = score.astype(bf16).astype(f32)
+    s2 = (score - s1).astype(bf16).astype(f32)
+    s3 = score - s1 - s2
+    none = jnp.zeros_like(s1)
+    st = jnp.concatenate(
+        [
+            jnp.concatenate([s1, s2, s3, none], axis=0),
+            jnp.concatenate([s1, s2, none, none], axis=0),
+        ],
+        axis=1,
+    ).astype(bf16)
 
     def finish(g, carry):
-        mt = mt_ref[...]
-        two = nn_dot(mt, oh_ref[g])
-        update = two[:z] + two[z:] + nn_dot(mt[:z], ol_ref[g])
+        two = nn_dot(mt_ref[...], oh_ref[g])
+        update = two[:z] + two[z:] + nn_dot(mt_ref[:z, :], ol_ref[g])
         at = pl.ds(pl.multiple_of(g * lanes, lanes), lanes)
         before = pair_ref[at, :].astype(f32).T
         result = (before + update).astype(bf16)
@@ -156,13 +198,29 @@
         center = x - jnp.mean(x, axis=0, keepdims=True)
         inverse = lax.rsqrt(jnp.mean(center * center, axis=0, keepdims=True) + epsilon)
         high, low = high_low(center * inverse)
-        scores = nn_dot(st_ref[...], jnp.concatenate([high, low], axis=0))
-        heads = logits_ref.shape[1]
+        scores = nn_dot(st, jnp.concatenate([high, low], axis=0))
         logits = scores[:heads] + scores[heads : 2 * heads] + scores[2 * heads : 3 * heads]
         logits_ref[g] = jnp.where(maskl, logits, far_below)
         return carry
 
     lax.fori_loop(0, groups, finish, 0, unroll=2)
+
+
+def by_heads(w, heads, out_ref):
+    width, chans = w.shape
+    hw = chans // heads
+    block = 4 * hw
+    slot = lax.broadcasted_iota(jnp.int32, (width, block), 1) // hw
+    w = w.astype(f32)
+    for t in range(chans // block):
+        part = w[:, t * block : (t + 1) * block]
+        turns = [part] + [pltpu.roll(part, n * hw, 1) for n in range(1, 4)]
+        for e in range(4):
+            h = t * 4 + e
+            for s in range(4):
+                out_ref[s * width : (s + 1) * width, h * block : (h + 1) * block] = jnp.where(
+                    slot == s, turns[(s - e) % 4], 0.0
+                ).astype(bf16)
 
 
 def weights_kernel(
@@ -170,64 +228,83 @@
     xc_ref,
     rows_ref,
     wv_ref,
-    wga_ref,
+    wg_ref,
+    wf_ref,
     logits_ref,
-    maskj_ref,
+    mask_ref,
     gw_ref,
     own_ref,
     pay1_ref,
     pay2_ref,
     pay3_ref,
     acc_ref,
+    bv_ref,
+    bg_ref,
+    bf_ref,
+    gs_ref,
+    vs_ref,
 ):
-    nq, nk, seqs, tokens, _ = xc_ref.shape
+    nq, nk, half, tokens, _ = xc_ref.shape
     tile = nk * tokens
     groups, heads, lanes = logits_ref.shape
-    chans = wv_ref.shape[1]
-    head_width = chans // heads
-    wv = wv_ref[...]
-    wga = wga_ref[...]
-    owner = lax.broadcasted_iota(jnp.int32, (tile, chans), 1) // head_width
-    step = 4
-
+    col = col_ref[0]
+    by_heads(wv_ref[...], heads, bv_ref)
+    by_heads(wg_ref[...], heads, bg_ref)
+    by_heads(wf_ref[...], heads, bf_ref)
     acc_ref[...] = jnp.zeros_like(acc_ref)
-
-    def some(n, carry):
-        q = n // (seqs // step)
-        s0 = (n % (seqs // step)) * step
-        vs, gs = [], []
-        for ds in range(step):
-            x = jnp.concatenate([xc_ref[q, k, s0 + ds] for k in range(nk)], axis=0)
-            v = nn_dot(x, wv).astype(bf16)
-            vs.append(jnp.concatenate([v, v], axis=0))
-            r = jnp.concatenate([rows_ref[q, k, s0 + ds] for k in range(nk)], axis=0)
-            both = nn_dot(r, wga)
-            gs.append((both[:, chans:] * jax.nn.sigmoid(both[:, :chans])).astype(bf16))
-        spread = [
-            jnp.concatenate(
-                [jnp.where(owner == h, g, jnp.zeros_like(g)) for h in range(heads)], axis=0
-            )
-            for g in gs
-        ]
-        acc_ref[...] += nt_dot(jnp.concatenate(spread, axis=1), jnp.concatenate(vs, axis=1))
+    block = bv_ref.shape[1] // heads
+
+    def four(read, n):
+        return jnp.concatenate(
+            [
+                jnp.concatenate(
+                    [
+                        jnp.concatenate([read(k, 2 * (2 * n + e) + p) for k in range(nk)], axis=0)
+                        for p in range(2)
+                    ],
+                    axis=1,
+                )
+                for e in range(2)
+            ],
+            axis=0,
+        )
+
+    def some(q, carry):
+        for hp in range(heads // 2):
+            cut = slice(hp * 2 * block, (hp + 1) * 2 * block)
+            for n in range(half // 4):
+                v = nn_dot(four(lambda k, s: xc_ref[q, k, s], n), bv_ref[:, cut]).astype(bf16)
+                gate = nn_dot(four(lambda k, s: rows_ref[q, k, 0, s], n), bg_ref[:, cut])
+                grad = nn_dot(four(lambda k, s: rows_ref[q, k, 1, s], n), bf_ref[:, cut])
+                g = (grad * jax.nn.sigmoid(gate)).astype(bf16)
+                for e in range(2):
+                    to = slice((2 * n + e) * block, (2 * n + e + 1) * block)
+                    for o in range(2):
+                        mine = slice(o * block, (o + 1) * block)
+                        ve = v[e * tile : (e + 1) * tile, mine]
+                        vs_ref[2 * hp + o, :tile, to] = ve
+                        vs_ref[2 * hp + o, tile:, to] = ve
+                        gs_ref[2 * hp + o, :, to] = g[e * tile : (e + 1) * tile, mine]
+        for h in range(heads):
+            acc_ref[h * tile : (h + 1) * tile, :] += nt_dot(gs_ref[h], vs_ref[h])
         return carry
 
-    lax.fori_loop(0, nq * (seqs // step), some, 0)
+    lax.fori_loop(0, nq, some, 0)
 
     first = lax.broadcasted_iota(jnp.int32, (groups, 2 * tile), 1) < tile
     for h in range(heads):
-        for half in range(pack // 2):
-            a = acc_ref[pl.ds(h * tile + 2 * half, groups, stride=pack), :]
-            b = acc_ref[pl.ds(h * tile + 2 * half + 1, groups, stride=pack), :]
-            gw_ref[:, h, half * 2 * tile : (half + 1) * 2 * tile] = jnp.where(first, a, b)
+        for part in range(pack // 2):
+            a = acc_ref[pl.ds(h * tile + 2 * part, groups, stride=pack), :]
+            b = acc_ref[pl.ds(h * tile + 2 * part + 1, groups, stride=pack), :]
+            gw_ref[:, h, part * 2 * tile : (part + 1) * 2 * tile] = jnp.where(first, a, b)
 
     rows = groups * heads
     lane = lax.broadcasted_iota(jnp.int32, (rows, 2 * tile), 1)
     low = lane < tile
-    maskj = maskj_ref[...]
+    maskj = column_mask(mask_ref, col, tile, 2)
     stats = jnp.zeros((rows, 2 * tile), f32)
-    for half in range(pack // 2):
-        cut = slice(half * 2 * tile, (half + 1) * 2 * tile)
+    for part in range(pack // 2):
+        cut = slice(part * 2 * tile, (part + 1) * 2 * tile)
         lg = logits_ref[:, :, cut].reshape(rows, 2 * tile)
         gw = gw_ref[:, :, cut].reshape(rows, 2 * tile)
         m0 = jnp.max(jnp.where(low, lg, far_below), axis=1, keepdims=True)
@@ -236,14 +313,13 @@
         pg = p * gw
         for e, m in ((0, m0), (1, m1)):
             mine = low if e == 0 else jnp.logical_not(low)
-            i = 2 * half + e
+            i = 2 * part + e
             total = jnp.sum(jnp.where(mine, p, 0.0), axis=1, keepdims=True)
             inner = jnp.sum(jnp.where(mine, pg, 0.0), axis=1, keepdims=True)
             stats = jnp.where(lane == i, m, stats)
             stats = jnp.where(lane == pack + i, total, stats)
             stats = jnp.where(lane == 2 * pack + i, inner, stats)
     turned = stats.T[:16]
-    col = col_ref[0]
     per = groups // nk
     for shift, pay in enumerate((own_ref, pay1_ref, pay2_ref, pay3_ref)):
         dest = lax.rem(col + shift, nk)
@@ -251,26 +327,36 @@
         pay[1] = turned[8:]
         for g in range(per):
             piece = logits_ref[dest * per + g]
-            for half in range(pack // 2):
-                pay[2 + g * (pack // 2) + half] = piece[:, half * 2 * tile : (half + 1) * 2 * tile]
+            for part in range(pack // 2):
+                pay[2 + g * (pack // 2) + part] = piece[:, part * 2 * tile : (part + 1) * 2 * tile]
 
 
 def values_kernel(all_ref, wv_ref, norm_ref, wg_ref, v_ref, gate_ref):
-    owners, seqs, tokens, width = all_ref.shape
-    wv = wv_ref[...]
-    for s in range(seqs):
+    owners, half, tokens, wide = all_ref.shape
+    chans = wv_ref.shape[1]
+    wv = twice(wv_ref[...])
+    for s in range(half):
         x = jnp.concatenate([all_ref[k, s] for k in range(owners)], axis=0)
-        v_ref[s] = nn_dot(x, wv).astype(bf16)
-    gate_ref[...] = jax.nn.sigmoid(
-        nn_dot(norm_ref[...].reshape(seqs * tokens, width), wg_ref[...])
-    )
+        v = nn_dot(x, wv).astype(bf16)
+        v_ref[s] = v[:, :chans]
+        v_ref[s + half] = v[:, chans:]
+    gate = jax.nn.sigmoid(nn_dot(norm_ref[...].reshape(half * tokens, wide), twice(wg_ref[...])))
+    gate_ref[: half * tokens] = gate[:, :chans]
+    gate_ref[half * tokens :] = gate[:, chans:]
 
 
 def gradient_kernel(
-    own_ref, r1_ref, r2_ref, r3_ref, logits_ref, gw_ref, pout_t_ref, sk_ref, out_ref, stat_ref
+    own_ref, r1_ref, r2_ref, r3_ref, logits_ref, gw_ref, pout_t_ref, score_ref, out_ref, stat_ref
 ):
     groups, heads, lanes = logits_ref.shape
     rows = groups * heads
+    score = score_ref[...]
+    z = score.shape[1]
+    s1 = score.astype(bf16).astype(f32)
+    s2 = (score - s1).astype(bf16).astype(f32)
+    s3 = score - s1 - s2
+    parts = [s1, s1, s1, s2, s2, s3, jnp.zeros((z - 6 * heads, z), f32)]
+    sk = jnp.concatenate(parts, axis=0).T[:, : 6 * heads].astype(bf16)
     pays = (own_ref, r1_ref, r2_ref, r3_ref)
     ms = [p[0][:pack] for p in pays]
     ls = [p[0][pack : 2 * pack] for p in pays]
@@ -305,7 +391,7 @@
         g2 = (gl - g1).astype(bf16).astype(f32)
         g3 = gl - g1 - g2
         stack = jnp.concatenate([g1, g2, g3, g1, g2, g1], axis=0).astype(bf16)
-        grad = nn_dot(sk_ref[...], stack)
+        grad = nn_dot(sk, stack)
         x = pout_t_ref[g].astype(f32)
         center = x - jnp.mean(x, axis=0, keepdims=True)
         inverse = lax.rsqrt(jnp.mean(center * center, axis=0, keepdims=True) + epsilon)
@@ -379,7 +465,7 @@
         return carry
 
     lax.fori_loop(0, seqs, one, 0, unroll=4)
-    out_ref[...] = (x_ref[...].astype(f32) + nn_dot(gated_ref[...], wf_ref[...])).astype(bf16)
+    out_ref[...] = (x_ref[...].astype(f32) + nt_dot(gated_ref[...], wf_ref[...])).astype(bf16)
 
 
 def on_device(
@@ -409,59 +495,34 @@
     lanes = pack * tile_j
     sds = jax.ShapeDtypeStruct
 
-    maskf = token_valid_mask.astype(f32)
-    own_start = (row_index * nk + col_index) * tokens
-    own_mask = lax.dynamic_slice_in_dim(maskf, own_start, tokens)
-    own_mask = jnp.broadcast_to(own_mask[:, None], (tokens, seqs)).reshape(1, tokens * seqs)
-    col_mask = lax.dynamic_slice_in_dim(maskf, col_index * tile_j, tile_j)
-    col_mask = jnp.concatenate([col_mask, col_mask]).reshape(1, 2 * tile_j)
+    mask = token_valid_mask.reshape(1, -1)
+    own_start = ((row_index * nk + col_index) * tokens).astype(jnp.int32).reshape(1)
     col_scalar = col_index.astype(jnp.int32).reshape(1)
+    half = seqs // 2
 
     normed, both, left = call(
         prepare_kernel,
         (
-            sds((seqs, tokens, width), bf16),
-            sds((seqs, tokens, 2 * width), bf16),
+            sds((half, tokens, 2 * width), bf16),
+            sds((2, half, tokens, 2 * width), bf16),
             sds((fc, tokens * seqs), bf16),
         ),
-    )(
-        alignment_input,
-        jnp.swapaxes(alignment_input, 0, 1),
-        adjoint_of_rowset,
-        first_factor_weights.T,
-        own_mask,
-    )
+        scratch=(pltpu.VMEM((tokens, seqs, width), f32),),
+        smem=1,
+        vmem=60 * 1024 * 1024,
+    )(own_start, alignment_input, adjoint_of_rowset, first_factor_weights.T, mask)
 
     turn = [(r * nk + c, c * nk + r) for r in range(nr) for c in range(nk)]
     crossed = lax.ppermute(normed, ("row", "col"), turn)
     lefts = lax.all_gather(left, ("seq", "col"), axis=0).reshape(nq, nk, fc, tokens * seqs)
-    cols = lax.all_gather(crossed, ("seq", "row"), axis=0).reshape(nq, nk, seqs, tokens, width)
-    rows = lax.all_gather(both, ("seq", "col"), axis=0).reshape(nq, nk, seqs, tokens, 2 * width)
-    every = lax.all_gather(normed, ("row", "col"), axis=0)
-
-    m3 = outer_matrix.reshape(fc, fd, z).transpose(2, 1, 0).reshape(z, fd * fc)
-    m_high = lax.reduce_precision(m3, 8, 7)
-    mt = jnp.concatenate([m_high, m3 - m_high], axis=0).astype(bf16)
-    s1, s2, s3 = split3(score_matrix)
-    none = jnp.zeros((heads, z), bf16)
-    st = jnp.concatenate(
-        [
-            jnp.concatenate([s1.T, s1.T], axis=1),
-            jnp.concatenate([s2.T, s2.T], axis=1),
-            jnp.concatenate([s3.T, none], axis=1),
-            jnp.concatenate([none, none], axis=1),
-        ],
-        axis=0,
-    )
-    sk = jnp.concatenate([s1, s1, s1, s2, s2, s3], axis=1)
-    blank = jnp.zeros((width, chans), bf16)
-    wga = jnp.concatenate(
-        [
-            jnp.concatenate([sigmoid_weights_grid, blank], axis=1),
-            jnp.concatenate([blank, final_mixing_weights.T], axis=1),
-        ],
-        axis=0,
-    )
+    cols = lax.all_gather(crossed, ("seq", "row"), axis=0).reshape(
+        nq, nk, half, tokens, 2 * width
+    )
+    both, after, lefts, cols = lax.optimization_barrier((both, normed, lefts, cols))
+    rows = lax.all_gather(both, ("seq", "col"), axis=0).reshape(
+        nq, nk, 2, half, tokens, 2 * width
+    )
+    every = lax.all_gather(after, ("row", "col"), axis=0)
 
     pair_out, pair_t, logits = call(
         update_kernel,
@@ -473,18 +534,21 @@
         scratch=(
             pltpu.VMEM((nq, fd, seqs, 2 * tile_j), f32),
             pltpu.VMEM((groups * fc, nq * pack * seqs), bf16),
+            pltpu.VMEM((2 * z, fd * fc), bf16),
             pltpu.VMEM((groups, fd * fc, lanes), bf16),
             pltpu.VMEM((groups, fd * fc, lanes), bf16),
         ),
+        smem=1,
         flops=14_000_000_000,
         nbytes=5_000_000,
     )(
+        col_scalar,
         lefts,
         cols,
         second_factor_weights.T,
-        col_mask,
-        mt,
-        st,
+        mask,
+        outer_matrix,
+        score_matrix.T,
         pair_input.reshape(tile_i * tile_j, z),
     )
 
@@ -492,11 +556,27 @@
     gw, pay0, pay1, pay2, pay3 = call(
         weights_kernel,
         (sds((groups, heads, lanes), f32), payload, payload, payload, payload),
-        scratch=(pltpu.VMEM((heads * tile_i, 2 * tile_j), f32),),
+        scratch=(
+            pltpu.VMEM((heads * tile_i, 2 * tile_j), f32),
+            pltpu.VMEM((4 * width, 4 * chans), bf16),
+            pltpu.VMEM((4 * width, 4 * chans), bf16),
+            pltpu.VMEM((4 * width, 4 * chans), bf16),
+            pltpu.VMEM((heads, tile_i, seqs * chans // heads), bf16),
+            pltpu.VMEM((heads, 2 * tile_j, seqs * chans // heads), bf16),
+        ),
         smem=1,
         flops=6_000_000_000,
         nbytes=3_000_000,
-    )(col_scalar, cols, rows, content_weights_grid, wga, logits, col_mask)
+    )(
+        col_scalar,
+        cols,
+        rows,
+        content_weights_grid,
+        sigmoid_weights_grid,
+        final_mixing_weights.T,
+        logits,
+        mask,
+    )
 
     got = [
         lax.ppermute(pay, "col", [(c, (c + shift) % nk) for c in range(nk)])
@@ -516,7 +596,7 @@
         scratch=(pltpu.VMEM((groups * heads, groups * heads), f32),),
         flops=4_000_000_000,
         nbytes=3_000_000,
-    )(pay0, *got, logits, gw, pair_t, sk)
+    )(pay0, *got, logits, gw, pair_t, score_matrix.T)
 
     aligned = call(
         alignment_kernel,
@@ -535,7 +615,7 @@
         values,
         gating,
         alignment_input.reshape(seqs * tokens, width),
-        final_mixing_weights,
+        final_mixing_weights.T,
     )
     return (
         aligned.reshape(seqs, tokens, width),

time: 129 us -> 132 us (1.023)
  waiting for transfers between devices: 1.45 us -> 25.8 us
  Pallas kernels: 42.1 us -> 34.2 us
  blocking collectives: 50.9 us -> 46.7 us
  local copies, waits for them, and re-layouts: 10.7 us -> 6.79 us
  other arithmetic: 3.75 us -> 0 us
    all_gather x1, waiting for transfers between devices: 0.01 us -> 23.4 us  [on_device(): every = lax.all_gather(after, ('row', 'col'), axis=0)]
    pallas_call x6, Pallas kernels: 42.1 us -> 34.2 us  [run(): pl.pallas_call(kernel, out_shape=out_shape, in_specs=specs, out_specs=jax...]
    all_gather x1, blocking collectives: 36.7 us -> 32.3 us  [on_device(): lax.all_gather(crossed, ('seq', 'row'), axis=0)]
    unnamed x3 -> x0, other arithmetic: 2.09 us -> none
    unnamed x30 -> x28, local copies, waits for them, and re-layouts: 8.6 us -> 6.79 us
    transpose x1 -> x0, local copies, waits for them, and re-layouts: 1.35 us -> none  [on_device(): m3 = outer_matrix.reshape(fc, fd, z).transpose(2, 1, 0).reshape(z, fd * fc)]
  transfers between devices with their start and end apart: 6 -> 6, of which waited for: 2 -> 4; matrix products, arithmetic and copies ran while one was open for 4% -> 0% of each run, Pallas kernels for 26% -> 21%
where the time goes in v2:
time: 132 us
  blocking collectives  46.7 us (35%)
  Pallas kernels  34.2 us (26%)
  waiting for transfers between devices  25.8 us (20%)
  between operations  14.1 us (11%)
  local copies, waits for them, and re-layouts  6.79 us (5%)
  starting transfers between devices  4.3 us (3%)
    pallas_call x6, Pallas kernels, run(): pl.pallas_call(kernel, out_shape=out_shape, in_specs=specs, out_specs=jax...  34.2 us
    all_gather x1, blocking collectives, on_device(): lax.all_gather(crossed, ('seq', 'row'), axis=0)  32.3 us
    all_gather x1, waiting for transfers between devices, on_device(): every = lax.all_gather(after, ('row', 'col'), axis=0)  23.4 us
    all_gather x1, blocking collectives, on_device(): lax.all_gather(left, ('seq', 'col'), axis=0)  14.4 us
    unnamed x28, local copies, waits for them, and re-layouts  6.79 us
    ppermute x3, starting transfers between devices, on_device(): lax.ppermute(pay, 'col', [(c, (c + shift) % nk) for c in range(nk)])  2.74 us
  transfers between devices with their start and end apart: 6, of which 4 were waited for; matrix products, arithmetic and copies ran while one was open for 0% of the time, Pallas kernels for 21%

profile of v2, /device:TPU:0, one launch (start us, length us, event | category | flops | bytes accessed | tf_op | source)
XLA Modules:
  0.0 132.0 jit_solution(4904531723964917131)
XLA Ops:
  7.2 0.0 all-gather.7.cloned.1.call-start
  7.2 2.2 %shard_map.130 = (bf16[16,16,128]{2,1,0:T(8,128)(2,1)}, bf16[2,16,16,128]{3,2,1,0:T(8,128)(2,1)}, bf16[32,512]{1,0:T(8,128)(2,1)}) custom-call(s32[1]{0:T(128)} %bitcast.1.own_ref, bf16[32,16,64]{2,1,0:T(8,128)(2,1)} %x_ref.1, bf16[32,16,64]{2,1,0:T(8,128)(2,1)} %adj_ref.1, bf16[32,64]{1,0:T(8,128)(2,1)} %bitcast.31, s32[1,256]{1,0:T(1,128)} %bitcast.20), custom_call_target="tpu_custom_call" | custom-call | tf_op jit(solution)/shard_map/pallas_call | solution.py:38
  9.4 1.5 %collective-permute-start = (bf16[16,16,128]{2,1,0:T(8,128)(2,1)}, bf16[16,16,128]{2,1,0:T(8,128)(2,1)S(1)}, u32[]{:S(2)}, u32[]{:S(2)}) collective-permute-start(bf16[16,16,128]{2,1,0:T(8,128)(2,1)} %get-tuple-element.31.norm_ref), channel_id=1, source_target_pairs={{0,0},{1,4},{2,8},{3,12},{4,1},{5,5},{6,9},{7,13},{8,2},{9,6},{10,... | collective-permute-start | bytes 196616 | tf_op jit(solution)/shard_map/ppermute | solution.py:516
  10.9 14.4 %all-gather = bf16[256,512]{1,0:T(8,128)(2,1)S(1)} all-gather(bf16[32,512]{1,0:T(8,128)(2,1)} %get-tuple-element.22), channel_id=2, replica_groups=mesh['seq'=2,'row'=4,'col'=4] {'seq','col'}, dimensions={0}, use_global_device_ids=true | all-gather | bytes 294912 | tf_op jit(solution)/shard_map/all_gather | solution.py:517
  25.2 0.0 collective-permute-done
  25.2 32.3 %all-gather.1 = bf16[128,16,128]{2,1,0:T(8,128)(2,1)S(1)} all-gather(bf16[16,16,128]{2,1,0:T(8,128)(2,1)S(1)} %collective-permute-done), channel_id=3, replica_groups=mesh['seq'=2,'row'=4,'col'=4] {'seq','row'}, dimensions={0}, use_global_device_ids=true | all-gather | bytes 589824 | tf_op jit(solution)/shard_map/all_gather | solution.py:518
  57.6 0.0 all-gather.7.cloned.1.call-update
  57.6 0.0 all-gather.9.cloned.1.call-start
  57.6 0.7 all-gather.9.cloned.1.call-update
  58.3 0.0 copy-start.2
  58.4 0.7 copy-done.2
  59.0 0.0 copy-start.4
  59.0 1.2 copy-done.4
  60.3 0.0 copy-start.7
  60.3 1.0 copy-done.7
  61.3 0.0 copy-start.11
  61.3 0.7 copy-done.11
  62.0 0.0 copy-start.12
  62.0 0.7 copy-done.12
  62.7 0.0 copy-start.3
  62.7 0.0 copy-start.8
  62.7 0.0 copy-start.9
  62.7 0.0 copy-start.10
  62.7 18.7 %shard_map.131 = (bf16[4096,128]{1,0:T(8,128)(2,1)}, bf16[16,128,256]{2,1,0:T(8,128)(2,1)S(1)}, f32[16,8,256]{2,1,0:T(8,128)S(1)}) custom-call(s32[1]{0:T(128)} %bitcast.col_ref, bf16[2,4,32,512]{3,2,1,0:T(8,128)(2,1)S(1)} %bitcast.18, bf16[2,4,16,16,128]{4,3,2,1,0:T(8,128)(2,1)S(1)} %bitcast.16, bf16[32,64]{1,0:T(8,128)(2,1)S(1)} %bitcast.28, ...), custom_call_target="tpu_custom_call" | custom-call | flops 14000000000 | bytes 5000000 | tf_op jit(solution)/shard_map/pallas_call | solution.py:38
  81.4 0.0 all-gather.7.cloned.1.call-done
  81.4 0.0 copy-done.3
  81.4 0.0 copy-done.8
  81.4 0.0 copy-done.9
  81.4 0.0 copy-done.10
  81.4 0.0 copy-start.6
  81.4 1.2 copy-done.6
  82.6 0.0 copy-start.13
  82.6 4.5 %shard_map.132 = (f32[16,8,256]{2,1,0:T(8,128)S(1)}, f32[10,8,128]{2,1,0:T(8,128)S(1)}, f32[10,8,128]{2,1,0:T(8,128)S(1)}, f32[10,8,128]{2,1,0:T(8,128)S(1)}, f32[10,8,128]{2,1,0:T(8,128)S(1)}) custom-call(s32[1]{0:T(128)} %bitcast.col_ref, bf16[2,4,16,16,128]{4,3,2,1,0:T(8,128)(2,1)S(1)} %bitcast.17, bf16[2,4,2,16,16,128]{5,4,3,2,1,0:T(8,128)(2,1)S(1)} %bitcast.25, ...), custom_call_target="tpu_custom_call" | custom-call | flops 6000000000 | bytes 3000000 | tf_op jit(solution)/shard_map/pallas_call | solution.py:38
  87.1 0.0 collective-permute-start.1
  87.2 1.3 %collective-permute-start.2 = (f32[10,8,128]{2,1,0:T(8,128)S(1)}, f32[10,8,128]{2,1,0:T(8,128)S(1)}, u32[]{:S(2)}, u32[]{:S(2)}) collective-permute-start(f32[10,8,128]{2,1,0:T(8,128)S(1)} %get-tuple-element.29), channel_id=1, source_target_pairs={{0,2},{1,3},{2,0},{3,1},{4,6},{5,7},{6,4},{7,5},{8,10},{9,11},{10,... | collective-permute-start | bytes 122888 | tf_op jit(solution)/shard_map/ppermute | solution.py:582
  88.5 1.4 %collective-permute-start.3 = (f32[10,8,128]{2,1,0:T(8,128)S(1)}, f32[10,8,128]{2,1,0:T(8,128)S(1)}, u32[]{:S(2)}, u32[]{:S(2)}) collective-permute-start(f32[10,8,128]{2,1,0:T(8,128)S(1)} %get-tuple-element.30), channel_id=1, source_target_pairs={{0,3},{1,0},{2,1},{3,2},{4,7},{5,4},{6,5},{7,6},{8,11},{9,8},{10,9... | collective-permute-start | bytes 122888 | tf_op jit(solution)/shard_map/ppermute | solution.py:582
  89.9 0.7 collective-permute-done.1.r1_ref
  90.6 0.8 collective-permute-done.2.r2_ref
  91.3 0.2 collective-permute-done.3.r3_ref
  91.5 0.0 copy-done.13
  91.5 0.0 copy-start.1
  91.5 4.4 %shard_map.135 = bf16[4096,128]{1,0:T(8,128)(2,1)} custom-call(f32[10,8,128]{2,1,0:T(8,128)S(1)} %get-tuple-element.27.own_ref, f32[10,8,128]{2,1,0:T(8,128)S(1)} %collective-permute-done.1.r1_ref, f32[10,8,128]{2,1,0:T(8,128)S(1)} %collective-permute-done.2.r2_ref, f32[10,8,128]{2,1,0:T(8,128)S(1)} %collective-permute-done.3.r3_ref, ...), custom_call_target="tpu_custom_call" | custom-call | flops 4000000000 | bytes 3000000 | tf_op jit(solution)/shard_map/pallas_call | solution.py:38
  95.9 23.4 %all-gather.9.cloned.1.call-done = bf16[256,16,128]{2,1,0:T(8,128)(2,1)} async-done(((bf16[16,16,128]{2,1,0:T(8,128)(2,1)}), bf16[256,16,128]{2,1,0:T(8,128)(2,1)}) %all-gather.9.cloned.1.call-update) | async-done | bytes 1048592 | tf_op jit(solution)/shard_map/all_gather | solution.py:525
  119.3 0.0 copy-done.1
  119.3 0.0 copy-start.5
  119.3 1.2 copy-done.5
  120.6 0.0 copy-start
  120.6 1.3 shard_map.133
  121.9 0.0 copy-done
  121.9 3.2 %shard_map.134 = bf16[512,64]{1,0:T(8,128)(2,1)} custom-call(s32[1]{0:T(128)} %bitcast.col_ref, f32[10,8,128]{2,1,0:T(8,128)S(1)} %get-tuple-element.27.own_ref, f32[10,8,128]{2,1,0:T(8,128)S(1)} %collective-permute-done.1.r1_ref, f32[10,8,128]{2,1,0:T(8,128)S(1)} %collective-permute-done.2.r2_ref, f32[10,8,128]{2,1,0:T(8,128)S(1)} %collective-permute-done.3.r3_ref, ...), custom_call_target="tpu_custom_call" | custom-call | flops 3000000000 | bytes 5000000 | tf_op jit(solution)/shard_map/pallas_call | solution.py:38
Async XLA Ops:
  7.2 74.2 %all-gather.7.cloned.1.call-start = ((), (), s32[]{:S(2)}) async-start(), calls=%async_computation | async-start | bytes 1179648 | tf_op jit(solution)/shard_map/all_gather | solution.py:522
  9.4 15.9 %collective-permute-start = (bf16[16,16,128]{2,1,0:T(8,128)(2,1)}, bf16[16,16,128]{2,1,0:T(8,128)(2,1)S(1)}, u32[]{:S(2)}, u32[]{:S(2)}) collective-permute-start(bf16[16,16,128]{2,1,0:T(8,128)(2,1)} %get-tuple-element.31.norm_ref), channel_id=1, source_target_pairs={{0,0},{1,4},{2,8},{3,12},{4,1},{5,5},{6,9},{7,13},{8,2},{9,6},{10,... | collective-permute-start | bytes 196616 | tf_op jit(solution)/shard_map/ppermute | solution.py:516
  57.6 61.7 %all-gather.9.cloned.1.call-start = ((), (), s32[]{:S(2)}) async-start(), calls=%async_computation.1 | async-start | bytes 1114112 | tf_op jit(solution)/shard_map/all_gather | solution.py:525
  58.3 0.7 copy-start.2
  59.0 1.2 copy-start.4
  60.3 1.0 copy-start.7
  61.3 0.7 copy-start.11
  62.0 0.7 copy-start.12
  62.7 18.7 %copy-start.3 = (s32[256]{0:T(256)S(1)}, s32[256]{0:T(256)}, u32[]{:S(2)}) copy-start(s32[256]{0:T(256)} %param.13) | copy-start | bytes 3076
  62.7 18.7 %copy-start.8 = (bf16[64,256]{1,0:T(8,128)(2,1)S(1)}, bf16[64,256]{1,0:T(8,128)(2,1)}, u32[]{:S(2)}) copy-start(bf16[64,256]{1,0:T(8,128)(2,1)} %wv_ref.3) | copy-start | bytes 98308
  62.7 18.7 %copy-start.9 = (bf16[64,256]{1,0:T(8,128)(2,1)S(1)}, bf16[64,256]{1,0:T(8,128)(2,1)}, u32[]{:S(2)}) copy-start(bf16[64,256]{1,0:T(8,128)(2,1)} %wg_ref.3) | copy-start | bytes 98308
  62.7 18.7 %copy-start.10 = (bf16[256,64]{0,1:T(8,128)(2,1)S(1)}, bf16[256,64]{0,1:T(8,128)(2,1)}, u32[]{:S(2)}) copy-start(bf16[256,64]{0,1:T(8,128)(2,1)} %param.20) | copy-start | bytes 98308
  81.4 1.2 copy-start.6
  82.6 8.9 %copy-start.13 = (f32[128,8]{0,1:T(8,128)S(1)}, f32[128,8]{0,1:T(8,128)}, u32[]{:S(2)}) copy-start(f32[128,8]{0,1:T(8,128)} %param.19) | copy-start | bytes 12292
  87.1 3.4 %collective-permute-start.1 = (f32[10,8,128]{2,1,0:T(8,128)S(1)}, f32[10,8,128]{2,1,0:T(8,128)S(1)}, u32[]{:S(2)}, u32[]{:S(2)}) collective-permute-start(f32[10,8,128]{2,1,0:T(8,128)S(1)} %get-tuple-element.28), channel_id=1, source_target_pairs={{0,1},{1,2},{2,3},{3,0},{4,5},{5,6},{6,7},{7,4},{8,9},{9,10},{10,1... | collective-permute-start | bytes 122888 | tf_op jit(solution)/shard_map/ppermute | solution.py:582
  87.2 4.2 %collective-permute-start.2 = (f32[10,8,128]{2,1,0:T(8,128)S(1)}, f32[10,8,128]{2,1,0:T(8,128)S(1)}, u32[]{:S(2)}, u32[]{:S(2)}) collective-permute-start(f32[10,8,128]{2,1,0:T(8,128)S(1)} %get-tuple-element.29), channel_id=1, source_target_pairs={{0,2},{1,3},{2,0},{3,1},{4,6},{5,7},{6,4},{7,5},{8,10},{9,11},{10,... | collective-permute-start | bytes 122888 | tf_op jit(solution)/shard_map/ppermute | solution.py:582
  88.5 3.1 %collective-permute-start.3 = (f32[10,8,128]{2,1,0:T(8,128)S(1)}, f32[10,8,128]{2,1,0:T(8,128)S(1)}, u32[]{:S(2)}, u32[]{:S(2)}) collective-permute-start(f32[10,8,128]{2,1,0:T(8,128)S(1)} %get-tuple-element.30), channel_id=1, source_target_pairs={{0,3},{1,0},{2,1},{3,2},{4,7},{5,4},{6,5},{7,6},{8,11},{9,8},{10,9... | collective-permute-start | bytes 122888 | tf_op jit(solution)/shard_map/ppermute | solution.py:582
  91.5 27.8 %copy-start.1 = (bf16[16,16,128]{2,1,0:T(8,128)(2,1)S(1)}, bf16[16,16,128]{2,1,0:T(8,128)(2,1)}, u32[]{:S(2)}) copy-start(bf16[16,16,128]{2,1,0:T(8,128)(2,1)} %get-tuple-element.31.norm_ref) | copy-start | bytes 196612
  119.3 1.2 copy-start.5
  120.6 1.3 %copy-start = (bf16[32,16,64]{2,1,0:T(8,128)(2,1)S(1)}, bf16[32,16,64]{2,1,0:T(8,128)(2,1)}, u32[]{:S(2)}) copy-start(bf16[32,16,64]{2,1,0:T(8,128)(2,1)} %x_ref.1) | copy-start | bytes 196612
Sparse Core Ops, SparseCore 0:
  57.7 21.3 all-gather.6
  81.3 37.9 all-gather.8

commit v3 on v2

--- a/solution.py
+++ b/solution.py
@@ -29,7 +29,7 @@
     return high, (x - high.astype(f32)).astype(bf16)
 
 
-def call(kernel, out_shape, scratch=(), smem=0, flops=0, nbytes=0, vmem=vmem_bytes):
+def call(kernel, out_shape, scratch=(), smem=0, flops=0, nbytes=0, vmem=vmem_bytes, far=(), far_out=()):
     count = None
 
     def run(*args):
@@ -38,8 +38,14 @@
         return pl.pallas_call(
             kernel,
             out_shape=out_shape,
-            in_specs=specs,
-            out_specs=jax.tree.map(lambda _: pl.BlockSpec(memory_space=pltpu.VMEM), out_shape),
+            in_specs=[
+                pl.BlockSpec(memory_space=pl.ANY) if n in far else spec
+                for n, spec in enumerate(specs)
+            ],
+            out_specs=[
+                pl.BlockSpec(memory_space=pl.ANY if n in far_out else pltpu.VMEM)
+                for n in range(len(out_shape))
+            ],
             scratch_shapes=list(scratch),
             compiler_params=pltpu.CompilerParams(vmem_limit_bytes=vmem),
             cost_estimate=pl.CostEstimate(flops=flops, bytes_accessed=nbytes, transcendentals=0),
@@ -86,25 +92,42 @@
 
 
 def update_kernel(
-    col_ref,
-    left_ref,
-    xc_ref,
+    place_ref,
+    left0_ref,
+    left1_ref,
+    left2_ref,
+    left3_ref,
+    tok0_ref,
+    tok1_ref,
+    tok2_ref,
+    tok3_ref,
     w2_ref,
     mask_ref,
+    m_hbm,
+    score_ref,
+    pair_hbm,
+    pout_hbm,
+    pout_t_ref,
+    logits_ref,
+    xc_ref,
     m_ref,
-    score_ref,
     pair_ref,
     pout_ref,
-    pout_t_ref,
-    logits_ref,
+    in_sem,
+    out_sem,
     rr_ref,
     lm_ref,
     mt_ref,
     oh_ref,
     ol_ref,
 ):
-    nq, nk, fc, _ = left_ref.shape
-    half, tokens = xc_ref.shape[2], xc_ref.shape[3]
+    fetch_m = pltpu.make_async_copy(m_hbm, m_ref, in_sem.at[0])
+    fetch_pair = pltpu.make_async_copy(pair_hbm, pair_ref, in_sem.at[1])
+    fetch_m.start()
+    fetch_pair.start()
+    nk, nq, half, tokens, _ = xc_ref.shape
+    fc = left0_ref.shape[1]
+    row, col = place_ref[0], place_ref[1]
     seqs = 2 * half
     tile_j = nk * tokens
     width_d = w2_ref.shape[0]
@@ -116,11 +139,14 @@
     heads = logits_ref.shape[1]
 
     w2 = twice(w2_ref[...])
-    maskj = column_mask(mask_ref, col_ref[0], tile_j, 2)
+    maskj = column_mask(mask_ref, col, tile_j, 2)
+
+    for t, ref in enumerate((tok0_ref, tok1_ref, tok2_ref, tok3_ref)):
+        xc_ref[lax.rem(row + nk - t, nk)] = ref[...]
 
     def right_of(q, carry):
         for s in range(half):
-            x = jnp.concatenate([xc_ref[q, k, s] for k in range(nk)], axis=0)
+            x = jnp.concatenate([xc_ref[k, q, s] for k in range(nk)], axis=0)
             res = nt_dot(w2, jnp.concatenate([x, x], axis=0)) * maskj
             rr_ref[q, :, s, :] = res[:width_d]
             rr_ref[q, :, s + half, :] = res[width_d:]
@@ -128,22 +154,12 @@
 
     lax.fori_loop(0, nq, right_of, 0)
 
-    for q in range(nq):
-        for k in range(nk):
-            for g in range(per_k):
-                row = (k * per_k + g) * fc
-                lm_ref[row : row + fc, q * wk : (q + 1) * wk] = left_ref[
-                    q, k, :, g * wk : (g + 1) * wk
-                ]
-
-    some = z // fc
-    for n in range(width_d // some):
-        block = jnp.concatenate(
-            [m_ref[pl.ds(n * some + e, fc, stride=width_d), :] for e in range(some)], axis=0
-        ).T
-        high, low = high_low(block)
-        mt_ref[:z, n * z : (n + 1) * z] = high
-        mt_ref[z:, n * z : (n + 1) * z] = low
+    for t, ref in enumerate((left0_ref, left1_ref, left2_ref, left3_ref)):
+        k = lax.rem(col + nk - t, nk)
+        for g in range(per_k):
+            at = pl.ds(pl.multiple_of((k * per_k + g) * fc, fc), fc)
+            for q in range(nq):
+                lm_ref[at, q * wk : (q + 1) * wk] = ref[q, :, g * wk : (g + 1) * wk]
 
     first = lax.broadcasted_iota(jnp.int32, (seqs, 2 * tile_j), 1) < tile_j
     chunk = 4
@@ -170,7 +186,18 @@
             ol_ref[n * chunk : (n + 1) * chunk, at, :] = low.reshape(chunk, fc, lanes)
         return carry
 
-    lax.fori_loop(0, width_d, outer_of, 0, unroll=2)
+    lax.fori_loop(0, width_d, outer_of, 0, unroll=4)
+
+    fetch_m.wait()
+    some = z // fc
+    for n in range(width_d // some):
+        block = jnp.concatenate(
+            [m_ref[pl.ds(n * some + e, fc, stride=width_d), :] for e in range(some)], axis=0
+        ).T
+        high, low = high_low(block)
+        mt_ref[:z, n * z : (n + 1) * z] = high
+        mt_ref[z:, n * z : (n + 1) * z] = low
+    fetch_pair.wait()
 
     maskl = jnp.concatenate([maskj] * (pack // 2), axis=1) > 0
     score = score_ref[...]
@@ -195,6 +222,7 @@
         pout_t_ref[g] = result
         x = result.astype(f32)
         pout_ref[at, :] = x.T.astype(bf16)
+        pltpu.make_async_copy(pout_ref.at[at], pout_hbm.at[at], out_sem.at[g]).start()
         center = x - jnp.mean(x, axis=0, keepdims=True)
         inverse = lax.rsqrt(jnp.mean(center * center, axis=0, keepdims=True) + epsilon)
         high, low = high_low(center * inverse)
@@ -203,7 +231,10 @@
         logits_ref[g] = jnp.where(maskl, logits, far_below)
         return carry
 
-    lax.fori_loop(0, groups, finish, 0, unroll=2)
+    lax.fori_loop(0, groups, finish, 0, unroll=4)
+    for g in range(groups):
+        at = pl.ds(g * lanes, lanes)
+        pltpu.make_async_copy(pout_ref.at[at], pout_hbm.at[at], out_sem.at[g]).wait()
 
 
 def by_heads(w, heads, out_ref):
@@ -244,7 +275,7 @@
     gs_ref,
     vs_ref,
 ):
-    nq, nk, half, tokens, _ = xc_ref.shape
+    nk, nq, half, tokens, _ = xc_ref.shape
     tile = nk * tokens
     groups, heads, lanes = logits_ref.shape
     col = col_ref[0]
@@ -273,7 +304,7 @@
         for hp in range(heads // 2):
             cut = slice(hp * 2 * block, (hp + 1) * 2 * block)
             for n in range(half // 4):
-                v = nn_dot(four(lambda k, s: xc_ref[q, k, s], n), bv_ref[:, cut]).astype(bf16)
+                v = nn_dot(four(lambda k, s: xc_ref[k, q, s], n), bv_ref[:, cut]).astype(bf16)
                 gate = nn_dot(four(lambda k, s: rows_ref[q, k, 0, s], n), bg_ref[:, cut])
                 grad = nn_dot(four(lambda k, s: rows_ref[q, k, 1, s], n), bf_ref[:, cut])
                 g = (grad * jax.nn.sigmoid(gate)).astype(bf16)
@@ -402,7 +433,7 @@
         out_ref[pl.ds(pl.multiple_of(g * lanes, lanes), lanes), :] = result.T.astype(bf16)
         return carry
 
-    lax.fori_loop(0, groups, one, 0, unroll=2)
+    lax.fori_loop(0, groups, one, 0, unroll=4)
 
 
 def alignment_kernel(
@@ -497,6 +528,7 @@
 
     mask = token_valid_mask.reshape(1, -1)
     own_start = ((row_index * nk + col_index) * tokens).astype(jnp.int32).reshape(1)
+    place = jnp.stack([row_index, col_index]).astype(jnp.int32)
     col_scalar = col_index.astype(jnp.int32).reshape(1)
     half = seqs // 2
 
@@ -512,26 +544,39 @@
         vmem=60 * 1024 * 1024,
     )(own_start, alignment_input, adjoint_of_rowset, first_factor_weights.T, mask)
 
-    turn = [(r * nk + c, c * nk + r) for r in range(nr) for c in range(nk)]
-    crossed = lax.ppermute(normed, ("row", "col"), turn)
-    lefts = lax.all_gather(left, ("seq", "col"), axis=0).reshape(nq, nk, fc, tokens * seqs)
-    cols = lax.all_gather(crossed, ("seq", "row"), axis=0).reshape(
-        nq, nk, half, tokens, 2 * width
-    )
-    both, after, lefts, cols = lax.optimization_barrier((both, normed, lefts, cols))
     rows = lax.all_gather(both, ("seq", "col"), axis=0).reshape(
         nq, nk, 2, half, tokens, 2 * width
     )
-    every = lax.all_gather(after, ("row", "col"), axis=0)
-
-    pair_out, pair_t, logits = call(
+    every = lax.all_gather(normed, ("row", "col"), axis=0)
+    toks = lax.all_gather(normed, "seq", axis=0)
+    lefts = lax.all_gather(left, "seq", axis=0)
+
+    all_lefts = [lefts] + [
+        lax.ppermute(lefts, "col", [(c, (c + t) % nk) for c in range(nk)]) for t in range(1, nk)
+    ]
+    all_toks = [
+        lax.ppermute(
+            toks,
+            ("row", "col"),
+            [(r * nk + c, (c + t) % nr * nk + r) for r in range(nr) for c in range(nk)],
+        )
+        for t in range(nr)
+    ]
+
+    pair_out, pair_t, logits, cols = call(
         update_kernel,
         (
             sds((tile_i * tile_j, z), bf16),
             sds((groups, z, lanes), bf16),
             sds((groups, heads, lanes), f32),
+            sds((nk, nq, half, tokens, 2 * width), bf16),
         ),
         scratch=(
+            pltpu.VMEM((fc * fd, z), f32),
+            pltpu.VMEM((tile_i * tile_j, z), bf16),
+            pltpu.VMEM((tile_i * tile_j, z), bf16),
+            pltpu.SemaphoreType.DMA((2,)),
+            pltpu.SemaphoreType.DMA((groups,)),
             pltpu.VMEM((nq, fd, seqs, 2 * tile_j), f32),
             pltpu.VMEM((groups * fc, nq * pack * seqs), bf16),
             pltpu.VMEM((2 * z, fd * fc), bf16),
@@ -541,10 +586,13 @@
         smem=1,
         flops=14_000_000_000,
         nbytes=5_000_000,
+        vmem=60 * 1024 * 1024,
+        far=(11, 13),
+        far_out=(0,),
     )(
-        col_scalar,
-        lefts,
-        cols,
+        place,
+        *all_lefts,
+        *all_toks,
         second_factor_weights.T,
         mask,
         outer_matrix,
@@ -590,17 +638,17 @@
         nbytes=6_000_000,
     )(every, content_weights_grid, normed, sigmoid_weights_grid)
 
-    gradient = call(
+    (gradient,) = call(
         gradient_kernel,
-        sds((tile_i * tile_j, z), bf16),
+        (sds((tile_i * tile_j, z), bf16),),
         scratch=(pltpu.VMEM((groups * heads, groups * heads), f32),),
         flops=4_000_000_000,
         nbytes=3_000_000,
     )(pay0, *got, logits, gw, pair_t, score_matrix.T)
 
-    aligned = call(
+    (aligned,) = call(
         alignment_kernel,
-        sds((seqs * tokens, width), bf16),
+        (sds((seqs * tokens, width), bf16),),
         scratch=(
             pltpu.VMEM((nk, heads, tokens, 2 * tile_j), f32),
             pltpu.VMEM((seqs * tokens, chans), bf16),

time: 132 us -> 94 us (0.71)
  blocking collectives: 46.7 us -> 10.9 us
  waiting for transfers between devices: 25.8 us -> 16.5 us
  starting transfers between devices: 4.3 us -> 12.6 us
  local copies, waits for them, and re-layouts: 6.79 us -> 5.16 us
    all_gather x2, blocking collectives: 46.7 us -> 10.9 us  [the longest x1 5.76 us: on_device(): lefts = lax.all_gather(left, 'seq', axis=0)]
    all_gather x1, waiting for transfers between devices: 23.4 us -> 6.69 us  [on_device(): every = lax.all_gather(normed, ('row', 'col'), axis=0)]
    ppermute x1 -> x7, waiting for transfers between devices: 0.01 us -> 7.05 us  [the longest x3 7.04 us: on_device(): lax.ppermute(lefts, 'col', [(c, (c + t) % nk) for c in range(nk)])]
    ppermute x1 -> x7, starting transfers between devices: 1.49 us -> 8.26 us  [the longest x4 4.78 us: on_device(): lax.ppermute(toks, ('row', 'col'), [(r * nk + c, (c + t) % nr * nk + r) f...]
    unnamed x28 -> x40, local copies, waits for them, and re-layouts: 6.79 us -> 5.16 us
    ppermute x3, starting transfers between devices: 2.74 us -> 4.21 us  [on_device(): lax.ppermute(pay, 'col', [(c, (c + shift) % nk) for c in range(nk)])]
  transfers between devices with their start and end apart: 6 -> 12, of which waited for: 4 -> 4; matrix products, arithmetic and copies ran while one was open for 0% -> 1% of each run, Pallas kernels for 21% -> 29%
where the time goes in v3:
time: 94 us; the launch traced here: 93.7 us
  Pallas kernels  33.7 us (36%)
  waiting for transfers between devices  16.5 us (18%)
  between operations  14.2 us (15%)
  starting transfers between devices  12.6 us (13%)
  blocking collectives  10.9 us (12%)
  local copies, waits for them, and re-layouts  5.16 us (5%)
    pallas_call x6, Pallas kernels, run(): pl.pallas_call(kernel, out_shape=out_shape, in_specs=[pl.BlockSpec(memory...  33.7 us
    ppermute x3, waiting for transfers between devices, on_device(): lax.ppermute(lefts, 'col', [(c, (c + t) % nk) for c in range(nk)])  7.04 us
    all_gather x1, waiting for transfers between devices, on_device(): every = lax.all_gather(normed, ('row', 'col'), axis=0)  6.69 us
    all_gather x1, blocking collectives, on_device(): lefts = lax.all_gather(left, 'seq', axis=0)  5.76 us
    unnamed x40, local copies, waits for them, and re-layouts  5.16 us
    all_gather x1, blocking collectives, on_device(): toks = lax.all_gather(normed, 'seq', axis=0)  5.14 us
    ppermute x4, starting transfers between devices, on_device(): lax.ppermute(toks, ('row', 'col'), [(r * nk + c, (c + t) % nr * nk + r) f...  4.78 us
    ppermute x3, starting transfers between devices, on_device(): lax.ppermute(pay, 'col', [(c, (c + shift) % nk) for c in range(nk)])  4.21 us
  transfers between devices with their start and end apart: 12, of which 4 were waited for; matrix products, arithmetic and copies ran while one was open for 1% of the time, Pallas kernels for 29%

profile of v3, /device:TPU:0, one launch (start us, length us, event | category | flops | bytes accessed | tf_op | source)
XLA Modules:
  0.0 93.7 jit_solution(14284756658354283405)
XLA Ops:
  7.2 0.0 all-gather.7.cloned.1.call-start
  7.2 2.2 %shard_map.130 = (bf16[16,16,128]{2,1,0:T(8,128)(2,1)}, bf16[2,16,16,128]{3,2,1,0:T(8,128)(2,1)}, bf16[32,512]{1,0:T(8,128)(2,1)}) custom-call(s32[1]{0:T(128)} %bitcast.2.own_ref, bf16[32,16,64]{2,1,0:T(8,128)(2,1)} %x_ref.1, bf16[32,16,64]{2,1,0:T(8,128)(2,1)} %adj_ref.1, bf16[32,64]{1,0:T(8,128)(2,1)} %bitcast.35, s32[1,256]{1,0:T(1,128)} %bitcast.18), custom_call_target="tpu_custom_call" | custom-call | tf_op jit(solution)/shard_map/pallas_call | solution.py:38
  9.4 0.0 all-gather.7.cloned.1.call-update
  9.4 0.0 all-gather.9.cloned.1.call-start
  9.4 5.8 %all-gather = bf16[64,512]{1,0:T(8,128)(2,1)S(1)} all-gather(bf16[32,512]{1,0:T(8,128)(2,1)} %get-tuple-element.17), channel_id=2, replica_groups=mesh['seq'=2,'row'=4,'col'=4] {'seq'}, dimensions={0}, use_global_device_ids=true | all-gather | bytes 98304 | tf_op jit(solution)/shard_map/all_gather | solution.py:552
  15.2 0.0 copy-start.12
  15.2 0.3 collective-permute-start.2
  15.5 1.7 %collective-permute-start.1 = (bf16[2,32,512]{2,1,0:T(8,128)(2,1)S(1)}, bf16[2,32,512]{2,1,0:T(8,128)(2,1)S(1)}, u32[]{:S(2)}, u32[]{:S(2)}) collective-permute-start(bf16[2,32,512]{2,1,0:T(8,128)(2,1)S(1)} %bitcast.32), channel_id=1, source_target_pairs={{0,2},{1,3},{2,0},{3,1},{4,6},{5,7},{6,4},{7,5},{8,10},{9,11},{10,... | collective-permute-start | bytes 196616 | tf_op jit(solution)/shard_map/ppermute | solution.py:555
  17.3 5.1 %all-gather.1 = bf16[32,16,128]{2,1,0:T(8,128)(2,1)S(1)} all-gather(bf16[16,16,128]{2,1,0:T(8,128)(2,1)} %get-tuple-element.18.norm_ref), channel_id=3, replica_groups=mesh['seq'=2,'row'=4,'col'=4] {'seq'}, dimensions={0}, use_global_device_ids=true | all-gather | bytes 196608 | tf_op jit(solution)/shard_map/all_gather | solution.py:551
  22.4 3.6 %collective-permute-start.6 = (bf16[2,16,16,128]{3,2,1,0:T(8,128)(2,1)S(1)}, bf16[2,16,16,128]{3,2,1,0:T(8,128)(2,1)S(1)}, u32[]{:S(2)}, u32[]{:S(2)}) collective-permute-start(bf16[2,16,16,128]{3,2,1,0:T(8,128)(2,1)S(1)} %bitcast.27), channel_id=1, source_target_pairs={{0,12},{1,0},{2,4},{3,8},{4,13},{5,1},{6,5},{7,9},{8,14},{9,2},{10... | collective-permute-start | bytes 393224 | tf_op jit(solution)/shard_map/ppermute | solution.py:558
  26.0 0.5 collective-permute-start.5
  26.5 0.0 collective-permute-start.4
  26.5 0.0 collective-permute-done.2.left3_ref
  26.5 0.0 copy-start.17
  26.5 0.7 collective-permute-start.3
  27.2 0.0 all-gather.9.cloned.1.call-update
  27.2 0.0 collective-permute-done.1.left2_ref
  27.2 0.0 copy-start.18
  27.2 1.4 %collective-permute-start = (bf16[2,32,512]{2,1,0:T(8,128)(2,1)S(1)}, bf16[2,32,512]{2,1,0:T(8,128)(2,1)S(1)}, u32[]{:S(2)}, u32[]{:S(2)}) collective-permute-start(bf16[2,32,512]{2,1,0:T(8,128)(2,1)S(1)} %bitcast.33), channel_id=1, source_target_pairs={{0,1},{1,2},{2,3},{3,0},{4,5},{5,6},{6,7},{7,4},{8,9},{9,10},{10,1... | collective-permute-start | bytes 196616 | tf_op jit(solution)/shard_map/ppermute | solution.py:555
  28.7 0.7 pad_add_fusion.place_ref
  29.3 7.0 %collective-permute-done.left1_ref = bf16[2,32,512]{2,1,0:T(8,128)(2,1)S(1)} collective-permute-done((bf16[2,32,512]{2,1,0:T(8,128)(2,1)S(1)}, bf16[2,32,512]{2,1,0:T(8,128)(2,1)S(1)}, u32[]{:S(2)}, u32[]{:S(2)}) %collective-permute-start) | collective-permute-done | bytes 65568 | tf_op jit(solution)/shard_map/ppermute | solution.py:555
  36.4 0.0 copy-start.19
  36.4 0.0 collective-permute-done.6.tok3_ref
  36.4 0.0 copy-start.13
  36.4 0.0 collective-permute-done.5.tok2_ref
  36.4 0.0 copy-start.14
  36.4 0.0 collective-permute-done.4.tok1_ref
  36.4 0.0 copy-start.15
  36.4 0.0 collective-permute-done.3.tok0_ref
  36.4 0.0 copy-start.16
  36.4 0.0 copy-done.12
  36.4 0.0 copy-done.17
  36.5 0.0 copy-done.18
  36.5 0.5 copy-done.19
  37.0 0.1 copy-done.13
  37.0 0.0 copy-done.14
  37.1 0.0 copy-done.15
  37.1 0.1 copy-done.16
  37.2 19.2 %shard_map.131 = (bf16[4096,128]{1,0:T(8,128)(2,1)}, bf16[16,128,256]{2,1,0:T(8,128)(2,1)}, f32[16,8,256]{2,1,0:T(8,128)}, bf16[4,2,16,16,128]{4,3,2,1,0:T(8,128)(2,1)}) custom-call(s32[2]{0:T(128)} %pad_add_fusion.place_ref, bf16[2,32,512]{2,1,0:T(8,128)(2,1)} %bitcast.34, bf16[2,32,512]{2,1,0:T(8,128)(2,1)} %copy-done.19, bf16[2,32,512]{2,1,0:T(8,128)(2,1)} %copy-done.18, ...), custom_call_target="tpu_custom_call" | custom-call | flops 14000000000 | bytes 5000000 | tf_op jit(solution)/shard_map/pallas_call | solution.py:38
  56.4 0.0 all-gather.7.cloned.1.call-done
  56.4 0.0 copy-done.2
  56.4 0.0 copy-done.5
  56.4 0.0 copy-done.6
  56.5 0.0 copy-done.7
  56.5 0.0 copy-start.3
  56.5 1.2 %copy-done.3 = bf16[16,16,16,128]{3,2,1,0:T(8,128)(2,1)S(1)} copy-done((bf16[16,16,16,128]{3,2,1,0:T(8,128)(2,1)S(1)}, bf16[16,16,16,128]{3,2,1,0:T(8,128)(2,1)}, u32[]{:S(2)}) %copy-start.3) | copy-done | bytes 1048600
  57.7 1.0 %copy-done.10 = bf16[4,2,16,16,128]{4,3,2,1,0:T(8,128)(2,1)S(1)} copy-done((bf16[4,2,16,16,128]{4,3,2,1,0:T(8,128)(2,1)S(1)}, bf16[4,2,16,16,128]{4,3,2,1,0:T(8,128)(2,1)}, u32[]{:S(2)}) %copy-start.10) | copy-done | bytes 524312
  58.7 0.9 copy-done.11
  59.6 4.5 %shard_map.132 = (f32[16,8,256]{2,1,0:T(8,128)S(1)}, f32[10,8,128]{2,1,0:T(8,128)S(1)}, f32[10,8,128]{2,1,0:T(8,128)S(1)}, f32[10,8,128]{2,1,0:T(8,128)S(1)}, f32[10,8,128]{2,1,0:T(8,128)S(1)}) custom-call(s32[1]{0:T(128)} %bitcast.col_ref, bf16[4,2,16,16,128]{4,3,2,1,0:T(8,128)(2,1)S(1)} %copy-done.10, bf16[2,4,2,16,16,128]{5,4,3,2,1,0:T(8,128)(2,1)S(1)} %bitcast.21, ...), custom_call_target="tpu_custom_call" | custom-call | flops 6000000000 | bytes 3000000 | tf_op jit(solution)/shard_map/pallas_call | solution.py:38
  64.2 0.0 collective-permute-start.7
  64.2 2.8 %collective-permute-start.8 = (f32[10,8,128]{2,1,0:T(8,128)S(1)}, f32[10,8,128]{2,1,0:T(8,128)S(1)}, u32[]{:S(2)}, u32[]{:S(2)}) collective-permute-start(f32[10,8,128]{2,1,0:T(8,128)S(1)} %get-tuple-element.24), channel_id=1, source_target_pairs={{0,2},{1,3},{2,0},{3,1},{4,6},{5,7},{6,4},{7,5},{8,10},{9,11},{10,... | collective-permute-start | bytes 122888 | tf_op jit(solution)/shard_map/ppermute | solution.py:630
  67.0 1.4 %collective-permute-start.9 = (f32[10,8,128]{2,1,0:T(8,128)S(1)}, f32[10,8,128]{2,1,0:T(8,128)S(1)}, u32[]{:S(2)}, u32[]{:S(2)}) collective-permute-start(f32[10,8,128]{2,1,0:T(8,128)S(1)} %get-tuple-element.25), channel_id=1, source_target_pairs={{0,3},{1,0},{2,1},{3,2},{4,7},{5,4},{6,5},{7,6},{8,11},{9,8},{10,9... | collective-permute-start | bytes 122888 | tf_op jit(solution)/shard_map/ppermute | solution.py:630
  68.4 0.0 collective-permute-done.7.r1_ref
  68.4 1.3 %collective-permute-done.8.r2_ref = f32[10,8,128]{2,1,0:T(8,128)S(1)} collective-permute-done((f32[10,8,128]{2,1,0:T(8,128)S(1)}, f32[10,8,128]{2,1,0:T(8,128)S(1)}, u32[]{:S(2)}, u32[]{:S(2)}) %collective-permute-start.8) | collective-permute-done | bytes 40992 | tf_op jit(solution)/shard_map/ppermute | solution.py:630
  69.7 1.4 %collective-permute-done.9.r3_ref = f32[10,8,128]{2,1,0:T(8,128)S(1)} collective-permute-done((f32[10,8,128]{2,1,0:T(8,128)S(1)}, f32[10,8,128]{2,1,0:T(8,128)S(1)}, u32[]{:S(2)}, u32[]{:S(2)}) %collective-permute-start.9) | collective-permute-done | bytes 40992 | tf_op jit(solution)/shard_map/ppermute | solution.py:630
  71.1 0.0 copy-done.8
  71.1 0.0 copy-done.9
  71.1 3.3 %shard_map.135 = bf16[4096,128]{1,0:T(8,128)(2,1)} custom-call(f32[10,8,128]{2,1,0:T(8,128)S(1)} %get-tuple-element.22.own_ref, f32[10,8,128]{2,1,0:T(8,128)S(1)} %collective-permute-done.7.r1_ref, f32[10,8,128]{2,1,0:T(8,128)S(1)} %collective-permute-done.8.r2_ref, f32[10,8,128]{2,1,0:T(8,128)S(1)} %collective-permute-done.9.r3_ref, ...), custom_call_target="tpu_custom_call" | custom-call | flops 4000000000 | bytes 3000000 | tf_op jit(solution)/shard_map/pallas_call | solution.py:38
  74.4 6.7 %all-gather.9.cloned.1.call-done = bf16[256,16,128]{2,1,0:T(8,128)(2,1)} async-done(((bf16[16,16,128]{2,1,0:T(8,128)(2,1)}), bf16[256,16,128]{2,1,0:T(8,128)(2,1)}) %all-gather.9.cloned.1.call-update) | async-done | bytes 1048592 | tf_op jit(solution)/shard_map/all_gather | solution.py:550
  81.1 0.0 copy-done
  81.1 1.2 %copy-done.4 = bf16[256,16,128]{2,1,0:T(8,128)(2,1)S(1)} copy-done((bf16[256,16,128]{2,1,0:T(8,128)(2,1)S(1)}, bf16[256,16,128]{2,1,0:T(8,128)(2,1)}, u32[]{:S(2)}) %copy-start.4) | copy-done | bytes 1048600
  82.3 1.3 %shard_map.133 = (bf16[32,256,256]{2,1,0:T(8,128)(2,1)S(1)}, f32[512,256]{1,0:T(8,128)S(1)}) custom-call(bf16[16,16,16,128]{3,2,1,0:T(8,128)(2,1)S(1)} %bitcast.22, bf16[64,256]{1,0:T(8,128)(2,1)S(1)} %copy-done.5, bf16[16,16,128]{2,1,0:T(8,128)(2,1)S(1)} %copy-done, bf16[64,256]{1,0:T(8,128)(2,1)S(1)} %copy-done.6), custom_call_target="tpu_custom_call" | custom-call | flops 4000000000 | bytes 6000000 | tf_op jit(solution)/shard_map/pallas_call | solution.py:38
  83.6 0.0 copy-done.1
  83.6 3.2 %shard_map.134 = bf16[512,64]{1,0:T(8,128)(2,1)} custom-call(s32[1]{0:T(128)} %bitcast.col_ref, f32[10,8,128]{2,1,0:T(8,128)S(1)} %get-tuple-element.22.own_ref, f32[10,8,128]{2,1,0:T(8,128)S(1)} %collective-permute-done.7.r1_ref, f32[10,8,128]{2,1,0:T(8,128)S(1)} %collective-permute-done.8.r2_ref, f32[10,8,128]{2,1,0:T(8,128)S(1)} %collective-permute-done.9.r3_ref, ...), custom_call_target="tpu_custom_call" | custom-call | flops 3000000000 | bytes 5000000 | tf_op jit(solution)/shard_map/pallas_call | solution.py:38
  (11 shorter events, 0.0 us)
Async XLA Ops:
  7.2 49.3 %all-gather.7.cloned.1.call-start = ((), (), s32[]{:S(2)}) async-start(), calls=%async_computation | async-start | bytes 1179648 | tf_op jit(solution)/shard_map/all_gather | solution.py:547
  9.4 71.7 %all-gather.9.cloned.1.call-start = ((), (), s32[]{:S(2)}) async-start(), calls=%async_computation.1 | async-start | bytes 1114112 | tf_op jit(solution)/shard_map/all_gather | solution.py:550
  15.2 21.2 %copy-start.12 = (bf16[64,512]{1,0:T(8,128)(2,1)}, bf16[64,512]{1,0:T(8,128)(2,1)S(1)}, u32[]{:S(2)}) copy-start(bf16[64,512]{1,0:T(8,128)(2,1)S(1)} %all-gather) | copy-start | bytes 196612
  15.2 11.3 %collective-permute-start.2 = (bf16[2,32,512]{2,1,0:T(8,128)(2,1)S(1)}, bf16[2,32,512]{2,1,0:T(8,128)(2,1)S(1)}, u32[]{:S(2)}, u32[]{:S(2)}) collective-permute-start(bf16[2,32,512]{2,1,0:T(8,128)(2,1)S(1)} %bitcast.31), channel_id=1, source_target_pairs={{0,3},{1,0},{2,1},{3,2},{4,7},{5,4},{6,5},{7,6},{8,11},{9,8},{10,9... | collective-permute-start | bytes 196616 | tf_op jit(solution)/shard_map/ppermute | solution.py:555
  15.5 11.7 %collective-permute-start.1 = (bf16[2,32,512]{2,1,0:T(8,128)(2,1)S(1)}, bf16[2,32,512]{2,1,0:T(8,128)(2,1)S(1)}, u32[]{:S(2)}, u32[]{:S(2)}) collective-permute-start(bf16[2,32,512]{2,1,0:T(8,128)(2,1)S(1)} %bitcast.32), channel_id=1, source_target_pairs={{0,2},{1,3},{2,0},{3,1},{4,6},{5,7},{6,4},{7,5},{8,10},{9,11},{10,... | collective-permute-start | bytes 196616 | tf_op jit(solution)/shard_map/ppermute | solution.py:555
  22.4 14.0 %collective-permute-start.6 = (bf16[2,16,16,128]{3,2,1,0:T(8,128)(2,1)S(1)}, bf16[2,16,16,128]{3,2,1,0:T(8,128)(2,1)S(1)}, u32[]{:S(2)}, u32[]{:S(2)}) collective-permute-start(bf16[2,16,16,128]{3,2,1,0:T(8,128)(2,1)S(1)} %bitcast.27), channel_id=1, source_target_pairs={{0,12},{1,0},{2,4},{3,8},{4,13},{5,1},{6,5},{7,9},{8,14},{9,2},{10... | collective-permute-start | bytes 393224 | tf_op jit(solution)/shard_map/ppermute | solution.py:558
  26.0 10.4 %collective-permute-start.5 = (bf16[2,16,16,128]{3,2,1,0:T(8,128)(2,1)S(1)}, bf16[2,16,16,128]{3,2,1,0:T(8,128)(2,1)S(1)}, u32[]{:S(2)}, u32[]{:S(2)}) collective-permute-start(bf16[2,16,16,128]{3,2,1,0:T(8,128)(2,1)S(1)} %bitcast.28), channel_id=1, source_target_pairs={{0,8},{1,12},{2,0},{3,4},{4,9},{5,13},{6,1},{7,5},{8,10},{9,14},{1... | collective-permute-start | bytes 393224 | tf_op jit(solution)/shard_map/ppermute | solution.py:558
  26.5 9.9 %collective-permute-start.4 = (bf16[2,16,16,128]{3,2,1,0:T(8,128)(2,1)S(1)}, bf16[2,16,16,128]{3,2,1,0:T(8,128)(2,1)S(1)}, u32[]{:S(2)}, u32[]{:S(2)}) collective-permute-start(bf16[2,16,16,128]{3,2,1,0:T(8,128)(2,1)S(1)} %bitcast.29), channel_id=1, source_target_pairs={{0,4},{1,8},{2,12},{3,0},{4,5},{5,9},{6,13},{7,1},{8,6},{9,10},{10... | collective-permute-start | bytes 393224 | tf_op jit(solution)/shard_map/ppermute | solution.py:558
  26.5 9.9 %copy-start.17 = (bf16[2,32,512]{2,1,0:T(8,128)(2,1)}, bf16[2,32,512]{2,1,0:T(8,128)(2,1)S(1)}, u32[]{:S(2)}) copy-start(bf16[2,32,512]{2,1,0:T(8,128)(2,1)S(1)} %collective-permute-done.2.left3_ref) | copy-start | bytes 196612
  26.5 9.9 %collective-permute-start.3 = (bf16[2,16,16,128]{3,2,1,0:T(8,128)(2,1)S(1)}, bf16[2,16,16,128]{3,2,1,0:T(8,128)(2,1)S(1)}, u32[]{:S(2)}, u32[]{:S(2)}) collective-permute-start(bf16[2,16,16,128]{3,2,1,0:T(8,128)(2,1)S(1)} %bitcast.30), channel_id=1, source_target_pairs={{0,0},{1,4},{2,8},{3,12},{4,1},{5,5},{6,9},{7,13},{8,2},{9,6},{10,... | collective-permute-start | bytes 393224 | tf_op jit(solution)/shard_map/ppermute | solution.py:558
  27.2 9.2 %copy-start.18 = (bf16[2,32,512]{2,1,0:T(8,128)(2,1)}, bf16[2,32,512]{2,1,0:T(8,128)(2,1)S(1)}, u32[]{:S(2)}) copy-start(bf16[2,32,512]{2,1,0:T(8,128)(2,1)S(1)} %collective-permute-done.1.left2_ref) | copy-start | bytes 196612
  27.2 9.1 %collective-permute-start = (bf16[2,32,512]{2,1,0:T(8,128)(2,1)S(1)}, bf16[2,32,512]{2,1,0:T(8,128)(2,1)S(1)}, u32[]{:S(2)}, u32[]{:S(2)}) collective-permute-start(bf16[2,32,512]{2,1,0:T(8,128)(2,1)S(1)} %bitcast.33), channel_id=1, source_target_pairs={{0,1},{1,2},{2,3},{3,0},{4,5},{5,6},{6,7},{7,4},{8,9},{9,10},{10,1... | collective-permute-start | bytes 196616 | tf_op jit(solution)/shard_map/ppermute | solution.py:555
  36.4 0.6 copy-start.19
  36.4 0.7 copy-start.13
  36.4 0.7 copy-start.14
  36.4 0.7 copy-start.15
  36.4 0.8 copy-start.16
  37.2 19.2 %copy-start.2 = (s32[256]{0:T(256)S(1)}, s32[256]{0:T(256)}, u32[]{:S(2)}) copy-start(s32[256]{0:T(256)} %param.13) | copy-start | bytes 3076
  37.2 19.3 %copy-start.5 = (bf16[64,256]{1,0:T(8,128)(2,1)S(1)}, bf16[64,256]{1,0:T(8,128)(2,1)}, u32[]{:S(2)}) copy-start(bf16[64,256]{1,0:T(8,128)(2,1)} %wv_ref.3) | copy-start | bytes 98308
  37.2 19.3 %copy-start.6 = (bf16[64,256]{1,0:T(8,128)(2,1)S(1)}, bf16[64,256]{1,0:T(8,128)(2,1)}, u32[]{:S(2)}) copy-start(bf16[64,256]{1,0:T(8,128)(2,1)} %wg_ref.3) | copy-start | bytes 98308
  37.2 19.3 %copy-start.7 = (bf16[256,64]{0,1:T(8,128)(2,1)S(1)}, bf16[256,64]{0,1:T(8,128)(2,1)}, u32[]{:S(2)}) copy-start(bf16[256,64]{0,1:T(8,128)(2,1)} %param.20) | copy-start | bytes 98308
  56.5 1.2 %copy-start.3 = (bf16[16,16,16,128]{3,2,1,0:T(8,128)(2,1)S(1)}, bf16[16,16,16,128]{3,2,1,0:T(8,128)(2,1)}, u32[]{:S(2)}) copy-start(bf16[16,16,16,128]{3,2,1,0:T(8,128)(2,1)} %all-gather.7.cloned.1.call-done) | copy-start | bytes 3145732
  57.7 1.0 %copy-start.10 = (bf16[4,2,16,16,128]{4,3,2,1,0:T(8,128)(2,1)S(1)}, bf16[4,2,16,16,128]{4,3,2,1,0:T(8,128)(2,1)}, u32[]{:S(2)}) copy-start(bf16[4,2,16,16,128]{4,3,2,1,0:T(8,128)(2,1)} %get-tuple-element.19.xc_ref) | copy-start | bytes 1572868
  58.7 0.9 copy-start.11
  59.6 11.4 %copy-start.8 = (f32[128,8]{0,1:T(8,128)S(1)}, f32[128,8]{0,1:T(8,128)}, u32[]{:S(2)}) copy-start(f32[128,8]{0,1:T(8,128)} %param.19) | copy-start | bytes 12292
  59.6 11.4 %copy-start.9 = (bf16[16,128,256]{2,1,0:T(8,128)(2,1)S(1)}, bf16[16,128,256]{2,1,0:T(8,128)(2,1)}, u32[]{:S(2)}) copy-start(bf16[16,128,256]{2,1,0:T(8,128)(2,1)} %get-tuple-element.30.pout_t_ref) | copy-start | bytes 3145732
  64.2 4.2 %collective-permute-start.7 = (f32[10,8,128]{2,1,0:T(8,128)S(1)}, f32[10,8,128]{2,1,0:T(8,128)S(1)}, u32[]{:S(2)}, u32[]{:S(2)}) collective-permute-start(f32[10,8,128]{2,1,0:T(8,128)S(1)} %get-tuple-element.23), channel_id=1, source_target_pairs={{0,1},{1,2},{2,3},{3,0},{4,5},{5,6},{6,7},{7,4},{8,9},{9,10},{10,1... | collective-permute-start | bytes 122888 | tf_op jit(solution)/shard_map/ppermute | solution.py:630
  64.2 5.5 %collective-permute-start.8 = (f32[10,8,128]{2,1,0:T(8,128)S(1)}, f32[10,8,128]{2,1,0:T(8,128)S(1)}, u32[]{:S(2)}, u32[]{:S(2)}) collective-permute-start(f32[10,8,128]{2,1,0:T(8,128)S(1)} %get-tuple-element.24), channel_id=1, source_target_pairs={{0,2},{1,3},{2,0},{3,1},{4,6},{5,7},{6,4},{7,5},{8,10},{9,11},{10,... | collective-permute-start | bytes 122888 | tf_op jit(solution)/shard_map/ppermute | solution.py:630
  67.0 4.1 %collective-permute-start.9 = (f32[10,8,128]{2,1,0:T(8,128)S(1)}, f32[10,8,128]{2,1,0:T(8,128)S(1)}, u32[]{:S(2)}, u32[]{:S(2)}) collective-permute-start(f32[10,8,128]{2,1,0:T(8,128)S(1)} %get-tuple-element.25), channel_id=1, source_target_pairs={{0,3},{1,0},{2,1},{3,2},{4,7},{5,4},{6,5},{7,6},{8,11},{9,8},{10,9... | collective-permute-start | bytes 122888 | tf_op jit(solution)/shard_map/ppermute | solution.py:630
  71.1 10.0 %copy-start = (bf16[16,16,128]{2,1,0:T(8,128)(2,1)S(1)}, bf16[16,16,128]{2,1,0:T(8,128)(2,1)}, u32[]{:S(2)}) copy-start(bf16[16,16,128]{2,1,0:T(8,128)(2,1)} %get-tuple-element.18.norm_ref) | copy-start | bytes 196612
  81.1 1.2 %copy-start.4 = (bf16[256,16,128]{2,1,0:T(8,128)(2,1)S(1)}, bf16[256,16,128]{2,1,0:T(8,128)(2,1)}, u32[]{:S(2)}) copy-start(bf16[256,16,128]{2,1,0:T(8,128)(2,1)} %all-gather.9.cloned.1.call-done) | copy-start | bytes 3145732
  82.3 1.3 %copy-start.1 = (bf16[32,16,64]{2,1,0:T(8,128)(2,1)S(1)}, bf16[32,16,64]{2,1,0:T(8,128)(2,1)}, u32[]{:S(2)}) copy-start(bf16[32,16,64]{2,1,0:T(8,128)(2,1)} %x_ref.1) | copy-start | bytes 196612
Sparse Core Ops, SparseCore 0:
  10.5 28.2 all-gather.6
  40.9 40.0 all-gather.8

commit v4 on v3

--- a/solution.py
+++ b/solution.py
@@ -71,24 +71,45 @@
     )
 
 
-def prepare_kernel(own_ref, x_ref, adj_ref, w1_ref, mask_ref, norm_ref, both_ref, left_ref, turn_ref):
+def prepare_kernel(
+    own_ref, x_ref, adj_ref, w1_ref, w2_ref, mask_ref, both_ref, sides_ref, turn_ref, right_ref
+):
     seqs, tokens, width = x_ref.shape
     half = seqs // 2
+    fd = w2_ref.shape[0]
     x = x_ref[...].astype(f32)
     center = x - jnp.mean(x, axis=-1, keepdims=True)
     inverse = lax.rsqrt(jnp.mean(center * center, axis=-1, keepdims=True) + epsilon)
     normed = center * inverse
-    packed = jnp.concatenate([normed[:half], normed[half:]], axis=-1).astype(bf16)
-    norm_ref[...] = packed
-    both_ref[0] = packed
+    rows = half * tokens
+    packed = jnp.concatenate([normed[:half], normed[half:]], axis=-1)
+    both_ref[:rows] = packed.reshape(rows, 2 * width).astype(bf16)
     adj = adj_ref[...].astype(f32)
-    both_ref[1] = jnp.concatenate([adj[:half], adj[half:]], axis=-1).astype(bf16)
+    packed = jnp.concatenate([adj[:half], adj[half:]], axis=-1)
+    both_ref[rows:] = packed.reshape(rows, 2 * width).astype(bf16)
+    token = lax.broadcasted_iota(jnp.int32, (seqs, tokens, width), 1) + own_ref[0]
+    count = valid_count(mask_ref).reshape(1, 1, 1)
+    real = jnp.where(token.astype(f32) < count, normed, 0.0)
     for s in range(seqs):
-        turn_ref[:, s, :] = normed[s]
-    token = lax.broadcasted_iota(jnp.int32, (tokens, seqs, width), 0) + own_ref[0]
-    count = valid_count(mask_ref).reshape(1, 1, 1)
-    turned = jnp.where(token.astype(f32) < count, turn_ref[...], 0.0).astype(bf16)
-    left_ref[...] = nt_dot(w1_ref[...], turned.reshape(tokens * seqs, width)).astype(bf16)
+        turn_ref[:, s, :] = real[s]
+    turned = turn_ref[...].astype(bf16).reshape(tokens * seqs, width)
+    left = nt_dot(w1_ref[...], turned).astype(bf16)
+    fc = w1_ref.shape[0]
+    wk = pack * seqs
+    for g in range(tokens // pack):
+        sides_ref[g * fc : (g + 1) * fc, :] = left[:, g * wk : (g + 1) * wk]
+    size = 128 // tokens
+    real = real.astype(bf16)
+    w2 = w2_ref[...]
+    d = lax.broadcasted_iota(jnp.int32, (fd, 128), 0)
+    lane = lax.broadcasted_iota(jnp.int32, (fd, 128), 1)
+    mine = lax.rem(d, size) == lane // tokens
+    for s in range(seqs):
+        res = nt_dot(w2, jnp.concatenate([real[s]] * size, axis=0))
+        res = jnp.where(mine, res, 0.0).reshape(fd // size, size, 128)
+        right_ref[:, s, :] = jnp.sum(res, axis=1)
+    base = tokens // pack * fc
+    sides_ref[base:, :] = right_ref[...].reshape(fd // size * seqs, 128).astype(bf16)
 
 
 def update_kernel(
@@ -97,11 +118,10 @@
     left1_ref,
     left2_ref,
     left3_ref,
-    tok0_ref,
-    tok1_ref,
-    tok2_ref,
-    tok3_ref,
-    w2_ref,
+    right0_ref,
+    right1_ref,
+    right2_ref,
+    right3_ref,
     mask_ref,
     m_hbm,
     score_ref,
@@ -109,13 +129,13 @@
     pout_hbm,
     pout_t_ref,
     logits_ref,
-    xc_ref,
     m_ref,
     pair_ref,
     pout_ref,
     in_sem,
     out_sem,
-    rr_ref,
+    rk_ref,
+    rab_ref,
     lm_ref,
     mt_ref,
     oh_ref,
@@ -125,54 +145,54 @@
     fetch_pair = pltpu.make_async_copy(pair_hbm, pair_ref, in_sem.at[1])
     fetch_m.start()
     fetch_pair.start()
-    nk, nq, half, tokens, _ = xc_ref.shape
-    fc = left0_ref.shape[1]
+    nk = rk_ref.shape[0]
+    width_d, pair_rows, _ = rab_ref.shape
+    nq = right0_ref.shape[0]
+    seqs = pair_rows // nq
     row, col = place_ref[0], place_ref[1]
-    seqs = 2 * half
-    tile_j = nk * tokens
-    width_d = w2_ref.shape[0]
-    groups = pair_ref.shape[0] // (pack * tile_j)
+    z = pair_ref.shape[1]
+    groups, heads, lanes = logits_ref.shape
+    tile_j = lanes // pack
+    tokens = tile_j // nk
     per_k = groups // nk
-    lanes = pack * tile_j
+    fc = lm_ref.shape[0] // groups
     wk = pack * seqs
-    z = pair_ref.shape[1]
-    heads = logits_ref.shape[1]
-
-    w2 = twice(w2_ref[...])
     maskj = column_mask(mask_ref, col, tile_j, 2)
 
-    for t, ref in enumerate((tok0_ref, tok1_ref, tok2_ref, tok3_ref)):
-        xc_ref[lax.rem(row + nk - t, nk)] = ref[...]
-
-    def right_of(q, carry):
-        for s in range(half):
-            x = jnp.concatenate([xc_ref[k, q, s] for k in range(nk)], axis=0)
-            res = nt_dot(w2, jnp.concatenate([x, x], axis=0)) * maskj
-            rr_ref[q, :, s, :] = res[:width_d]
-            rr_ref[q, :, s + half, :] = res[width_d:]
-        return carry
-
-    lax.fori_loop(0, nq, right_of, 0)
+    for t, ref in enumerate((right0_ref, right1_ref, right2_ref, right3_ref)):
+        rk_ref[lax.rem(row + nk - t, nk)] = ref[...].reshape(rk_ref.shape[1:])
+    size = 128 // tokens
+    right = jnp.concatenate([rk_ref[k] for k in range(nk)], axis=1)
+    source = lax.broadcasted_iota(jnp.int32, (nk * 128, 4 * tile_j), 0)
+    target = lax.broadcasted_iota(jnp.int32, (nk * 128, 4 * tile_j), 1)
+    used = jnp.logical_or(target < tile_j, target >= 3 * tile_j)
+    j = lax.rem(target, tile_j)
+    offset = jnp.where(used, source - (j // tokens * 128 + lax.rem(j, tokens)), -1)
+    blocks = width_d // size
+    for e in range(size):
+        pick = jnp.where(offset == e * tokens, 1.0, 0.0).astype(bf16)
+        res = nn_dot(right, pick).astype(bf16)
+        for q in range(nq):
+            for n in range(blocks):
+                at = (q * blocks + n) * seqs
+                rab_ref[n * size + e, q * seqs : (q + 1) * seqs, :] = res[at : at + seqs]
 
     for t, ref in enumerate((left0_ref, left1_ref, left2_ref, left3_ref)):
         k = lax.rem(col + nk - t, nk)
         for g in range(per_k):
             at = pl.ds(pl.multiple_of((k * per_k + g) * fc, fc), fc)
             for q in range(nq):
-                lm_ref[at, q * wk : (q + 1) * wk] = ref[q, :, g * wk : (g + 1) * wk]
-
-    first = lax.broadcasted_iota(jnp.int32, (seqs, 2 * tile_j), 1) < tile_j
+                from_row = (q * per_k + g) * fc
+                lm_ref[at, q * wk : (q + 1) * wk] = ref[from_row : from_row + fc, :]
+
     chunk = 4
 
     def outer_of(d, carry):
         empty = jnp.zeros((seqs, 2 * tile_j), bf16)
         rows = []
         for q in range(nq):
-            both = rr_ref[q, d]
-            part = (
-                jnp.where(first, both, 0.0).astype(bf16),
-                jnp.where(first, 0.0, both).astype(bf16),
-            )
+            both = rab_ref[d, q * seqs : (q + 1) * seqs, :]
+            part = both[:, : 2 * tile_j], both[:, 2 * tile_j :]
             for i in range(pack):
                 pieces = [empty] * (pack // 2)
                 pieces[i // 2] = part[i % 2]
@@ -256,33 +276,34 @@
 
 def weights_kernel(
     col_ref,
-    xc_ref,
-    rows_ref,
+    ev_ref,
+    side0_ref,
+    side1_ref,
+    side2_ref,
+    side3_ref,
     wv_ref,
     wg_ref,
     wf_ref,
-    logits_ref,
-    mask_ref,
     gw_ref,
-    own_ref,
-    pay1_ref,
-    pay2_ref,
-    pay3_ref,
     acc_ref,
     bv_ref,
     bg_ref,
     bf_ref,
+    rows_ref,
     gs_ref,
     vs_ref,
 ):
-    nk, nq, half, tokens, _ = xc_ref.shape
+    _, nk, half, tokens, _ = ev_ref.shape
     tile = nk * tokens
-    groups, heads, lanes = logits_ref.shape
+    groups, heads, lanes = gw_ref.shape
     col = col_ref[0]
+    count = rows_ref.shape[1] * rows_ref.shape[2] * tokens
+    for t, ref in enumerate((side0_ref, side1_ref, side2_ref, side3_ref)):
+        start = ref.shape[0] - count
+        rows_ref[lax.rem(col + nk - t, nk)] = ref[start:, :].reshape(rows_ref.shape[1:])
     by_heads(wv_ref[...], heads, bv_ref)
     by_heads(wg_ref[...], heads, bg_ref)
     by_heads(wf_ref[...], heads, bf_ref)
-    acc_ref[...] = jnp.zeros_like(acc_ref)
     block = bv_ref.shape[1] // heads
 
     def four(read, n):
@@ -300,27 +321,24 @@
             axis=0,
         )
 
-    def some(q, carry):
-        for hp in range(heads // 2):
-            cut = slice(hp * 2 * block, (hp + 1) * 2 * block)
-            for n in range(half // 4):
-                v = nn_dot(four(lambda k, s: xc_ref[k, q, s], n), bv_ref[:, cut]).astype(bf16)
-                gate = nn_dot(four(lambda k, s: rows_ref[q, k, 0, s], n), bg_ref[:, cut])
-                grad = nn_dot(four(lambda k, s: rows_ref[q, k, 1, s], n), bf_ref[:, cut])
-                g = (grad * jax.nn.sigmoid(gate)).astype(bf16)
-                for e in range(2):
-                    to = slice((2 * n + e) * block, (2 * n + e + 1) * block)
-                    for o in range(2):
-                        mine = slice(o * block, (o + 1) * block)
-                        ve = v[e * tile : (e + 1) * tile, mine]
-                        vs_ref[2 * hp + o, :tile, to] = ve
-                        vs_ref[2 * hp + o, tile:, to] = ve
-                        gs_ref[2 * hp + o, :, to] = g[e * tile : (e + 1) * tile, mine]
-        for h in range(heads):
-            acc_ref[h * tile : (h + 1) * tile, :] += nt_dot(gs_ref[h], vs_ref[h])
-        return carry
-
-    lax.fori_loop(0, nq, some, 0)
+    slots = [lax.rem(col + nk - k, nk) for k in range(nk)]
+    for hp in range(heads // 2):
+        cut = slice(hp * 2 * block, (hp + 1) * 2 * block)
+        for n in range(half // 4):
+            v = nn_dot(four(lambda k, s: ev_ref[col, slots[k], s], n), bv_ref[:, cut]).astype(bf16)
+            gate = nn_dot(four(lambda k, s: rows_ref[k, 0, s], n), bg_ref[:, cut])
+            grad = nn_dot(four(lambda k, s: rows_ref[k, 1, s], n), bf_ref[:, cut])
+            g = (grad * jax.nn.sigmoid(gate)).astype(bf16)
+            for e in range(2):
+                to = slice((2 * n + e) * block, (2 * n + e + 1) * block)
+                for o in range(2):
+                    mine = slice(o * block, (o + 1) * block)
+                    ve = v[e * tile : (e + 1) * tile, mine]
+                    vs_ref[2 * hp + o, :tile, to] = ve
+                    vs_ref[2 * hp + o, tile:, to] = ve
+                    gs_ref[2 * hp + o, :, to] = g[e * tile : (e + 1) * tile, mine]
+    for h in range(heads):
+        acc_ref[h * tile : (h + 1) * tile, :] = nt_dot(gs_ref[h], vs_ref[h])
 
     first = lax.broadcasted_iota(jnp.int32, (groups, 2 * tile), 1) < tile
     for h in range(heads):
@@ -329,7 +347,25 @@
             b = acc_ref[pl.ds(h * tile + 2 * part + 1, groups, stride=pack), :]
             gw_ref[:, h, part * 2 * tile : (part + 1) * 2 * tile] = jnp.where(first, a, b)
 
+
+def softmax_kernel(
+    col_ref,
+    logits_ref,
+    gwa_ref,
+    gwb_ref,
+    mask_ref,
+    gw_ref,
+    own_ref,
+    pay1_ref,
+    pay2_ref,
+    pay3_ref,
+):
+    groups, heads, lanes = logits_ref.shape
+    tile = lanes // pack
+    nk = 4
     rows = groups * heads
+    col = col_ref[0]
+    gw_ref[...] = gwa_ref[...] + gwb_ref[...]
     lane = lax.broadcasted_iota(jnp.int32, (rows, 2 * tile), 1)
     low = lane < tile
     maskj = column_mask(mask_ref, col, tile, 2)
@@ -362,16 +398,17 @@
                 pay[2 + g * (pack // 2) + part] = piece[:, part * 2 * tile : (part + 1) * 2 * tile]
 
 
-def values_kernel(all_ref, wv_ref, norm_ref, wg_ref, v_ref, gate_ref):
-    owners, half, tokens, wide = all_ref.shape
+def values_kernel(col_ref, ev_ref, wv_ref, both_ref, wg_ref, v_ref, gate_ref):
+    nr, nk, half, tokens, wide = ev_ref.shape
     chans = wv_ref.shape[1]
     wv = twice(wv_ref[...])
+    slots = [lax.rem(col_ref[0] + nk - k, nk) for k in range(nk)]
     for s in range(half):
-        x = jnp.concatenate([all_ref[k, s] for k in range(owners)], axis=0)
+        x = jnp.concatenate([ev_ref[r, slots[k], s] for r in range(nr) for k in range(nk)], axis=0)
         v = nn_dot(x, wv).astype(bf16)
         v_ref[s] = v[:, :chans]
         v_ref[s + half] = v[:, chans:]
-    gate = jax.nn.sigmoid(nn_dot(norm_ref[...].reshape(half * tokens, wide), twice(wg_ref[...])))
+    gate = jax.nn.sigmoid(nn_dot(both_ref[: half * tokens, :], twice(wg_ref[...])))
     gate_ref[: half * tokens] = gate[:, :chans]
     gate_ref[half * tokens :] = gate[:, chans:]
 
@@ -532,44 +569,50 @@
     col_scalar = col_index.astype(jnp.int32).reshape(1)
     half = seqs // 2
 
-    normed, both, left = call(
+    sides_left = tokens // pack * fc
+    sides_rows = sides_left + fd * tokens // 128 * seqs
+    both, sides = call(
         prepare_kernel,
-        (
-            sds((half, tokens, 2 * width), bf16),
-            sds((2, half, tokens, 2 * width), bf16),
-            sds((fc, tokens * seqs), bf16),
+        (sds((2 * half * tokens, 2 * width), bf16), sds((sides_rows, 128), bf16)),
+        scratch=(
+            pltpu.VMEM((tokens, seqs, width), f32),
+            pltpu.VMEM((fd * tokens // 128, seqs, 128), f32),
         ),
-        scratch=(pltpu.VMEM((tokens, seqs, width), f32),),
         smem=1,
         vmem=60 * 1024 * 1024,
-    )(own_start, alignment_input, adjoint_of_rowset, first_factor_weights.T, mask)
-
-    rows = lax.all_gather(both, ("seq", "col"), axis=0).reshape(
-        nq, nk, 2, half, tokens, 2 * width
+    )(
+        own_start,
+        alignment_input,
+        adjoint_of_rowset,
+        first_factor_weights.T,
+        second_factor_weights.T,
+        mask,
     )
-    every = lax.all_gather(normed, ("row", "col"), axis=0)
-    toks = lax.all_gather(normed, "seq", axis=0)
-    lefts = lax.all_gather(left, "seq", axis=0)
-
-    all_lefts = [lefts] + [
-        lax.ppermute(lefts, "col", [(c, (c + t) % nk) for c in range(nk)]) for t in range(1, nk)
-    ]
-    all_toks = [
+
+    sides = lax.all_gather(sides, "seq", axis=0)
+    lefts = jnp.concatenate([sides[:, :sides_left].reshape(nq * sides_left, 128), both], axis=0)
+    rights = sides[:, sides_left:]
+    all_rights = [
         lax.ppermute(
-            toks,
+            rights,
             ("row", "col"),
             [(r * nk + c, (c + t) % nr * nk + r) for r in range(nr) for c in range(nk)],
         )
         for t in range(nr)
     ]
-
-    pair_out, pair_t, logits, cols = call(
+    all_lefts = [lefts] + [
+        lax.ppermute(lefts, "col", [(c, (c + t) % nk) for c in range(nk)]) for t in range(1, nk)
+    ]
+    start = nq * sides_left
+    block_rows = jnp.stack([x[start : start + half * tokens] for x in all_lefts])
+    every = lax.all_gather(block_rows, "row", axis=0).reshape(nr, nk, half, tokens, 2 * width)
+
+    pair_out, pair_t, logits = call(
         update_kernel,
         (
             sds((tile_i * tile_j, z), bf16),
             sds((groups, z, lanes), bf16),
             sds((groups, heads, lanes), f32),
-            sds((nk, nq, half, tokens, 2 * width), bf16),
         ),
         scratch=(
             pltpu.VMEM((fc * fd, z), f32),
@@ -577,7 +620,8 @@
             pltpu.VMEM((tile_i * tile_j, z), bf16),
             pltpu.SemaphoreType.DMA((2,)),
             pltpu.SemaphoreType.DMA((groups,)),
-            pltpu.VMEM((nq, fd, seqs, 2 * tile_j), f32),
+            pltpu.VMEM((nk, nq * (sides_rows - sides_left), 128), bf16),
+            pltpu.VMEM((fd, nq * seqs, 4 * tile_j), bf16),
             pltpu.VMEM((groups * fc, nq * pack * seqs), bf16),
             pltpu.VMEM((2 * z, fd * fc), bf16),
             pltpu.VMEM((groups, fd * fc, lanes), bf16),
@@ -587,56 +631,66 @@
         flops=14_000_000_000,
         nbytes=5_000_000,
         vmem=60 * 1024 * 1024,
-        far=(11, 13),
+        far=(10, 12),
         far_out=(0,),
     )(
         place,
         *all_lefts,
-        *all_toks,
-        second_factor_weights.T,
+        *all_rights,
         mask,
         outer_matrix,
         score_matrix.T,
         pair_input.reshape(tile_i * tile_j, z),
     )
 
-    payload = sds((2 + groups // nk * (pack // 2), heads, 2 * tile_j), f32)
-    gw, pay0, pay1, pay2, pay3 = call(
+    head_lanes = seqs * chans // heads
+    (gw_own,) = call(
         weights_kernel,
-        (sds((groups, heads, lanes), f32), payload, payload, payload, payload),
+        (sds((groups, heads, lanes), f32),),
         scratch=(
             pltpu.VMEM((heads * tile_i, 2 * tile_j), f32),
             pltpu.VMEM((4 * width, 4 * chans), bf16),
             pltpu.VMEM((4 * width, 4 * chans), bf16),
             pltpu.VMEM((4 * width, 4 * chans), bf16),
-            pltpu.VMEM((heads, tile_i, seqs * chans // heads), bf16),
-            pltpu.VMEM((heads, 2 * tile_j, seqs * chans // heads), bf16),
+            pltpu.VMEM((nk, 2, half, tokens, 2 * width), bf16),
+            pltpu.VMEM((heads, tile_i, head_lanes), bf16),
+            pltpu.VMEM((heads, 2 * tile_j, head_lanes), bf16),
         ),
         smem=1,
-        flops=6_000_000_000,
+        flops=3_000_000_000,
         nbytes=3_000_000,
     )(
         col_scalar,
-        cols,
-        rows,
+        every,
+        *all_lefts,
         content_weights_grid,
         sigmoid_weights_grid,
         final_mixing_weights.T,
-        logits,
-        mask,
     )
+    if nq == 2:
+        gw_other = lax.ppermute(gw_own, "seq", [(0, 1), (1, 0)])
+    else:
+        gw_own, gw_other = lax.psum(gw_own, "seq"), jnp.zeros_like(gw_own)
+
+    values, gating = call(
+        values_kernel,
+        (sds((seqs, nr * nk * tokens, chans), bf16), sds((seqs * tokens, chans), f32)),
+        smem=1,
+        flops=4_000_000_000,
+        nbytes=6_000_000,
+    )(col_scalar, every, content_weights_grid, both, sigmoid_weights_grid)
+
+    payload = sds((2 + groups // nk * (pack // 2), heads, 2 * tile_j), f32)
+    gw, pay0, pay1, pay2, pay3 = call(
+        softmax_kernel,
+        (sds((groups, heads, lanes), f32), payload, payload, payload, payload),
+        smem=1,
+    )(col_scalar, logits, gw_own, gw_other, mask)
 
     got = [
         lax.ppermute(pay, "col", [(c, (c + shift) % nk) for c in range(nk)])
         for shift, pay in ((1, pay1), (2, pay2), (3, pay3))
     ]
-
-    values, gating = call(
-        values_kernel,
-        (sds((seqs, nr * nk * tokens, chans), bf16), sds((seqs * tokens, chans), f32)),
-        flops=4_000_000_000,
-        nbytes=6_000_000,
-    )(every, content_weights_grid, normed, sigmoid_weights_grid)
 
     (gradient,) = call(
         gradient_kernel,

time: 94 us -> 107 us (1.14)
  waiting for transfers between devices: 16.5 us -> 35.1 us
  blocking collectives: 10.9 us -> 6.1 us
  starting transfers between devices: 12.6 us -> 10.6 us
  Pallas kernels: 33.7 us -> 31.9 us
  other arithmetic: 0.65 us -> 2.32 us
    all_gather x2 -> x1, waiting for transfers between devices: 6.71 us -> 25.2 us  [on_device(): lax.all_gather(block_rows, 'row', axis=0)]
    all_gather x2 -> x1, blocking collectives: 10.9 us -> 6.1 us  [on_device(): sides = lax.all_gather(sides, 'seq', axis=0)]
    ppermute x3, starting transfers between devices: 4.21 us -> 1.79 us  [on_device(): lax.ppermute(pay, 'col', [(c, (c + shift) % nk) for c in range(nk)])]
    pallas_call x6 -> x7, Pallas kernels: 33.7 us -> 31.9 us  [run(): pl.pallas_call(kernel, out_shape=out_shape, in_specs=[pl.BlockSpec(memory...]
    ppermute x4 -> x5, starting transfers between devices: 4.78 us -> 6.5 us  [the longest x4 4.94 us: on_device(): lax.ppermute(rights, ('row', 'col'), [(r * nk + c, (c + t) % nr * nk + r)...]
    ppermute x3, waiting for transfers between devices: 7.04 us -> 8.69 us  [on_device(): lax.ppermute(lefts, 'col', [(c, (c + t) % nk) for c in range(nk)])]
    ppermute x3, waiting for transfers between devices: 2.69 us -> 1.16 us  [on_device(): lax.ppermute(pay, 'col', [(c, (c + shift) % nk) for c in range(nk)])]
    ppermute x3, starting transfers between devices: 3.48 us -> 2.3 us  [on_device(): lax.ppermute(lefts, 'col', [(c, (c + t) % nk) for c in range(nk)])]
  transfers between devices with their start and end apart: 12 -> 12, of which waited for: 4 -> 5; matrix products, arithmetic and copies ran while one was open for 1% -> 1% of each run, Pallas kernels for 29% -> 21%
where the time goes in v4:
time: 107 us; the launch traced here: 106 us
  waiting for transfers between devices  35.1 us (33%)
  Pallas kernels  31.9 us (30%)
  between operations  14.3 us (13%)
  starting transfers between devices  10.6 us (10%)
  blocking collectives  6.1 us (6%)
  local copies, waits for them, and re-layouts  5.99 us (6%)
  other arithmetic  2.32 us (2%)
    pallas_call x7, Pallas kernels, run(): pl.pallas_call(kernel, out_shape=out_shape, in_specs=[pl.BlockSpec(memory...  31.9 us
    all_gather x1, waiting for transfers between devices, on_device(): lax.all_gather(block_rows, 'row', axis=0)  25.2 us
    ppermute x3, waiting for transfers between devices, on_device(): lax.ppermute(lefts, 'col', [(c, (c + t) % nk) for c in range(nk)])  8.69 us
    all_gather x1, blocking collectives, on_device(): sides = lax.all_gather(sides, 'seq', axis=0)  6.1 us
    unnamed x46, local copies, waits for them, and re-layouts  5.12 us
    ppermute x4, starting transfers between devices, on_device(): lax.ppermute(rights, ('row', 'col'), [(r * nk + c, (c + t) % nr * nk + r)...  4.94 us
    ppermute x3, starting transfers between devices, on_device(): lax.ppermute(lefts, 'col', [(c, (c + t) % nk) for c in range(nk)])  2.3 us
  transfers between devices with their start and end apart: 12, of which 5 were waited for; matrix products, arithmetic and copies ran while one was open for 1% of the time, Pallas kernels for 21%

profile of v4, /device:TPU:0, one launch (start us, length us, event | category | flops | bytes accessed | tf_op | source)
XLA Modules:
  0.0 106.3 jit_solution(11228219018872572178)
XLA Ops:
  7.2 0.0 all-gather.4.cloned.1.call-start
  7.2 2.8 %shard_map.130 = (bf16[512,128]{1,0:T(8,128)(2,1)}, bf16[256,128]{1,0:T(8,128)(2,1)}) custom-call(s32[1]{0:T(128)} %bitcast.2.own_ref, bf16[32,16,64]{2,1,0:T(8,128)(2,1)} %x_ref.1, bf16[32,16,64]{2,1,0:T(8,128)(2,1)} %adj_ref.1, bf16[32,64]{1,0:T(8,128)(2,1)} %bitcast.36, bf16[32,64]{1,0:T(8,128)(2,1)} %bitcast.37, s32[1,256]{1,0:T(1,128)} %bitcast.25), custom_call_target="tpu_custom_call" | custom-call | tf_op jit(solution)/shard_map/pallas_call | solution.py:38
  10.0 6.1 %all-gather = bf16[512,128]{1,0:T(8,128)(2,1)S(1)} all-gather(bf16[256,128]{1,0:T(8,128)(2,1)} %get-tuple-element.15), channel_id=2, replica_groups=mesh['seq'=2,'row'=4,'col'=4] {'seq'}, dimensions={0}, use_global_device_ids=true | all-gather | bytes 196608 | tf_op jit(solution)/shard_map/all_gather | solution.py:592
  16.1 0.9 pad_maximum_fusion.1.left0_ref.side0_ref
  17.0 0.0 copy-start.1
  17.1 0.3 collective-permute-start.2
  17.4 1.8 %collective-permute-start.1 = (bf16[768,128]{1,0:T(8,128)(2,1)S(1)}, bf16[768,128]{1,0:T(8,128)(2,1)S(1)}, u32[]{:S(2)}, u32[]{:S(2)}) collective-permute-start(bf16[768,128]{1,0:T(8,128)(2,1)S(1)} %pad_maximum_fusion.1.left0_ref.side0_ref), channel_id=1, source_target_pairs={{0,2},{1,3},{2,0},{3,1},{4,6},{5,7},{6,4},{7,5},{8,10},{9,11},{10,... | collective-permute-start | bytes 589832 | tf_op jit(solution)/shard_map/ppermute | solution.py:604
  19.2 0.2 collective-permute-start
  19.4 0.8 slice_bitcast_fusion.3
  20.2 1.2 %collective-permute-done.2.left3_ref.side3_ref = bf16[768,128]{1,0:T(8,128)(2,1)S(1)} collective-permute-done((bf16[768,128]{1,0:T(8,128)(2,1)S(1)}, bf16[768,128]{1,0:T(8,128)(2,1)S(1)}, u32[]{:S(2)}, u32[]{:S(2)}) %collective-permute-start.2) | collective-permute-done | bytes 196640 | tf_op jit(solution)/shard_map/ppermute | solution.py:604
  21.4 7.5 %collective-permute-done.1.left2_ref.side2_ref = bf16[768,128]{1,0:T(8,128)(2,1)S(1)} collective-permute-done((bf16[768,128]{1,0:T(8,128)(2,1)S(1)}, bf16[768,128]{1,0:T(8,128)(2,1)S(1)}, u32[]{:S(2)}, u32[]{:S(2)}) %collective-permute-start.1) | collective-permute-done | bytes 196640 | tf_op jit(solution)/shard_map/ppermute | solution.py:604
  28.9 0.0 collective-permute-done.left1_ref.side1_ref
  28.9 0.0 copy-start.7
  28.9 0.8 pad_maximum_fusion
  29.7 0.0 all-gather.4.cloned.1.call-update
  29.8 3.8 %collective-permute-start.6 = (bf16[2,128,128]{2,1,0:T(8,128)(2,1)S(1)}, bf16[2,128,128]{2,1,0:T(8,128)(2,1)S(1)}, u32[]{:S(2)}, u32[]{:S(2)}) collective-permute-start(bf16[2,128,128]{2,1,0:T(8,128)(2,1)S(1)} %get-tuple-element.27), channel_id=1, source_target_pairs={{0,12},{1,0},{2,4},{3,8},{4,13},{5,1},{6,5},{7,9},{8,14},{9,2},{10... | collective-permute-start | bytes 196616 | tf_op jit(solution)/shard_map/ppermute | solution.py:596
  33.5 0.5 collective-permute-start.5
  34.0 0.0 collective-permute-start.4
  34.1 0.7 collective-permute-start.3
  34.7 0.6 pad_add_fusion.place_ref
  35.3 25.2 %all-gather.4.cloned.1.call-done = bf16[16,256,128]{2,1,0:T(8,128)(2,1)} async-done(((bf16[4,256,128]{2,1,0:T(8,128)(2,1)}), bf16[16,256,128]{2,1,0:T(8,128)(2,1)}) %all-gather.4.cloned.1.call-update) | async-done | bytes 1048592 | tf_op jit(solution)/shard_map/all_gather | solution.py:608
  60.5 1.2 %copy-done.9 = bf16[16,256,128]{2,1,0:T(8,128)(2,1)S(1)} copy-done((bf16[16,256,128]{2,1,0:T(8,128)(2,1)S(1)}, bf16[16,256,128]{2,1,0:T(8,128)(2,1)}, u32[]{:S(2)}) %copy-start.9) | copy-done | bytes 1048600
  61.7 0.8 copy-done.11
  62.5 0.8 copy-done.13
  63.3 0.8 copy-done.15
  64.0 2.3 %shard_map.132.gwa_ref = f32[16,8,256]{2,1,0:T(8,128)S(1)} custom-call(s32[1]{0:T(128)} %bitcast.col_ref, bf16[4,4,16,16,128]{4,3,2,1,0:T(8,128)(2,1)S(1)} %bitcast.28, bf16[768,128]{1,0:T(8,128)(2,1)S(1)} %pad_maximum_fusion.1.left0_ref.side0_ref, bf16[768,128]{1,0:T(8,128)(2,1)S(1)} %collective-permute-done.left1_ref.side1_ref, ...), custom_call_target="tpu_custom_call" | custom-call | flops 3000000000 | bytes 3000000 | tf_op jit(solution)/shard_map/pallas_call | solution.py:38
  66.3 0.0 copy-done.1
  66.3 0.0 copy-done.5
  66.3 0.0 copy-done.6
  66.3 0.0 copy-done.7
  66.3 1.6 %collective-permute-start.7 = (f32[16,8,256]{2,1,0:T(8,128)S(1)}, f32[16,8,256]{2,1,0:T(8,128)S(1)}, u32[]{:S(2)}, u32[]{:S(2)}) collective-permute-start(f32[16,8,256]{2,1,0:T(8,128)S(1)} %shard_map.132.gwa_ref), channel_id=1, source_target_pairs={{0,16},{16,0},{1,17},{17,1},{2,18},{18,2},{3,19},{19,3},{4,20},{20... | collective-permute-start | bytes 393224 | tf_op jit(solution)/shard_map/ppermute | solution.py:671
  67.9 0.0 collective-permute-done.6.right3_ref
  67.9 0.0 collective-permute-done.5.right2_ref
  67.9 0.0 copy-start.20
  67.9 0.0 collective-permute-done.4.right1_ref
  67.9 0.0 copy-start.21
  67.9 0.0 collective-permute-done.3.right0_ref
  68.0 0.0 copy-start.22
  68.0 0.6 copy-done.19
  68.5 0.0 copy-done.20
  68.6 0.0 copy-done.21
  68.6 0.0 copy-done.22
  68.6 0.0 copy-start.14
  68.6 18.5 %shard_map.131 = (bf16[4096,128]{1,0:T(8,128)(2,1)}, bf16[16,128,256]{2,1,0:T(8,128)(2,1)}, f32[16,8,256]{2,1,0:T(8,128)}) custom-call(s32[2]{0:T(128)} %pad_add_fusion.place_ref, bf16[768,128]{1,0:T(8,128)(2,1)} %copy-done.1, bf16[768,128]{1,0:T(8,128)(2,1)} %copy-done.7, bf16[768,128]{1,0:T(8,128)(2,1)} %copy-done.6, bf16[768,128]{1,0:T(8,128)(2,1)} %copy-done.5, ...), custom_call_target="tpu_custom_call" | custom-call | flops 14000000000 | bytes 5000000 | tf_op jit(solution)/shard_map/pallas_call | solution.py:38
  87.2 0.0 collective-permute-done.7.gwb_ref
  87.2 0.0 copy-done.8
  87.2 0.0 copy-start.3
  87.2 0.9 copy-done.3
  88.1 0.5 shard_map.133
  88.6 0.0 collective-permute-start.8
  88.6 0.1 collective-permute-start.9
  88.7 0.0 copy-start.17
  88.7 0.0 copy-start.18
  88.7 1.7 %collective-permute-start.10 = (f32[10,8,128]{2,1,0:T(8,128)S(1)}, f32[10,8,128]{2,1,0:T(8,128)S(1)}, u32[]{:S(2)}, u32[]{:S(2)}) collective-permute-start(f32[10,8,128]{2,1,0:T(8,128)S(1)} %get-tuple-element.21), channel_id=1, source_target_pairs={{0,3},{1,0},{2,1},{3,2},{4,7},{5,4},{6,5},{7,6},{8,11},{9,8},{10,9... | collective-permute-start | bytes 122888 | tf_op jit(solution)/shard_map/ppermute | solution.py:691
  90.4 0.0 copy-done
  90.4 1.3 %shard_map.134 = (bf16[32,256,256]{2,1,0:T(8,128)(2,1)S(1)}, f32[512,256]{1,0:T(8,128)S(1)}) custom-call(s32[1]{0:T(128)} %bitcast.col_ref, bf16[4,4,16,16,128]{4,3,2,1,0:T(8,128)(2,1)S(1)} %bitcast.29, bf16[64,256]{1,0:T(8,128)(2,1)S(1)} %copy-done.12, bf16[512,128]{1,0:T(8,128)(2,1)S(1)} %copy-done, bf16[64,256]{1,0:T(8,128)(2,1)S(1)} %copy-done.14), custom_call_target="tpu_custom_call" | custom-call | flops 4000000000 | bytes 6000000 | tf_op jit(solution)/shard_map/pallas_call | solution.py:38
  91.7 0.3 collective-permute-done.8.r1_ref
  92.0 0.9 collective-permute-done.9.r2_ref
  92.9 0.0 collective-permute-done.10.r3_ref
  92.9 0.0 copy-done.18
  92.9 0.0 copy-start.2
  92.9 0.0 copy-start.16
  92.9 3.3 %shard_map.136 = bf16[4096,128]{1,0:T(8,128)(2,1)} custom-call(f32[10,8,128]{2,1,0:T(8,128)S(1)} %get-tuple-element.18.own_ref, f32[10,8,128]{2,1,0:T(8,128)S(1)} %collective-permute-done.8.r1_ref, f32[10,8,128]{2,1,0:T(8,128)S(1)} %collective-permute-done.9.r2_ref, f32[10,8,128]{2,1,0:T(8,128)S(1)} %collective-permute-done.10.r3_ref, ...), custom_call_target="tpu_custom_call" | custom-call | flops 4000000000 | bytes 3000000 | tf_op jit(solution)/shard_map/pallas_call | solution.py:38
  96.2 3.2 %shard_map.135 = bf16[512,64]{1,0:T(8,128)(2,1)} custom-call(s32[1]{0:T(128)} %bitcast.col_ref, f32[10,8,128]{2,1,0:T(8,128)S(1)} %get-tuple-element.18.own_ref, f32[10,8,128]{2,1,0:T(8,128)S(1)} %collective-permute-done.8.r1_ref, f32[10,8,128]{2,1,0:T(8,128)S(1)} %collective-permute-done.9.r2_ref, f32[10,8,128]{2,1,0:T(8,128)S(1)} %collective-permute-done.10.r3_ref, ...), custom_call_target="tpu_custom_call" | custom-call | flops 3000000000 | bytes 5000000 | tf_op jit(solution)/shard_map/pallas_call | solution.py:38
  (23 shorter events, 0.1 us)
Async XLA Ops:
  7.2 53.4 %all-gather.4.cloned.1.call-start = ((), (), s32[]{:S(2)}) async-start(), calls=%async_computation | async-start | bytes 1310720 | tf_op jit(solution)/shard_map/all_gather | solution.py:608
  17.0 49.3 %copy-start.1 = (bf16[768,128]{1,0:T(8,128)(2,1)}, bf16[768,128]{1,0:T(8,128)(2,1)S(1)}, u32[]{:S(2)}) copy-start(bf16[768,128]{1,0:T(8,128)(2,1)S(1)} %pad_maximum_fusion.1.left0_ref.side0_ref) | copy-start | bytes 589828
  17.1 4.3 %collective-permute-start.2 = (bf16[768,128]{1,0:T(8,128)(2,1)S(1)}, bf16[768,128]{1,0:T(8,128)(2,1)S(1)}, u32[]{:S(2)}, u32[]{:S(2)}) collective-permute-start(bf16[768,128]{1,0:T(8,128)(2,1)S(1)} %pad_maximum_fusion.1.left0_ref.side0_ref), channel_id=1, source_target_pairs={{0,3},{1,0},{2,1},{3,2},{4,7},{5,4},{6,5},{7,6},{8,11},{9,8},{10,9... | collective-permute-start | bytes 589832 | tf_op jit(solution)/shard_map/ppermute | solution.py:604
  17.4 11.5 %collective-permute-start.1 = (bf16[768,128]{1,0:T(8,128)(2,1)S(1)}, bf16[768,128]{1,0:T(8,128)(2,1)S(1)}, u32[]{:S(2)}, u32[]{:S(2)}) collective-permute-start(bf16[768,128]{1,0:T(8,128)(2,1)S(1)} %pad_maximum_fusion.1.left0_ref.side0_ref), channel_id=1, source_target_pairs={{0,2},{1,3},{2,0},{3,1},{4,6},{5,7},{6,4},{7,5},{8,10},{9,11},{10,... | collective-permute-start | bytes 589832 | tf_op jit(solution)/shard_map/ppermute | solution.py:604
  19.2 9.7 %collective-permute-start = (bf16[768,128]{1,0:T(8,128)(2,1)S(1)}, bf16[768,128]{1,0:T(8,128)(2,1)S(1)}, u32[]{:S(2)}, u32[]{:S(2)}) collective-permute-start(bf16[768,128]{1,0:T(8,128)(2,1)S(1)} %pad_maximum_fusion.1.left0_ref.side0_ref), channel_id=1, source_target_pairs={{0,1},{1,2},{2,3},{3,0},{4,5},{5,6},{6,7},{7,4},{8,9},{9,10},{10,1... | collective-permute-start | bytes 589832 | tf_op jit(solution)/shard_map/ppermute | solution.py:604
  21.4 44.9 %copy-start.5 = (bf16[768,128]{1,0:T(8,128)(2,1)}, bf16[768,128]{1,0:T(8,128)(2,1)S(1)}, u32[]{:S(2)}) copy-start(bf16[768,128]{1,0:T(8,128)(2,1)S(1)} %collective-permute-done.2.left3_ref.side3_ref) | copy-start | bytes 589828
  28.9 37.4 %copy-start.6 = (bf16[768,128]{1,0:T(8,128)(2,1)}, bf16[768,128]{1,0:T(8,128)(2,1)S(1)}, u32[]{:S(2)}) copy-start(bf16[768,128]{1,0:T(8,128)(2,1)S(1)} %collective-permute-done.1.left2_ref.side2_ref) | copy-start | bytes 589828
  28.9 37.4 %copy-start.7 = (bf16[768,128]{1,0:T(8,128)(2,1)}, bf16[768,128]{1,0:T(8,128)(2,1)S(1)}, u32[]{:S(2)}) copy-start(bf16[768,128]{1,0:T(8,128)(2,1)S(1)} %collective-permute-done.left1_ref.side1_ref) | copy-start | bytes 589828
  29.8 38.1 %collective-permute-start.6 = (bf16[2,128,128]{2,1,0:T(8,128)(2,1)S(1)}, bf16[2,128,128]{2,1,0:T(8,128)(2,1)S(1)}, u32[]{:S(2)}, u32[]{:S(2)}) collective-permute-start(bf16[2,128,128]{2,1,0:T(8,128)(2,1)S(1)} %get-tuple-element.27), channel_id=1, source_target_pairs={{0,12},{1,0},{2,4},{3,8},{4,13},{5,1},{6,5},{7,9},{8,14},{9,2},{10... | collective-permute-start | bytes 196616 | tf_op jit(solution)/shard_map/ppermute | solution.py:596
  33.5 34.4 %collective-permute-start.5 = (bf16[2,128,128]{2,1,0:T(8,128)(2,1)S(1)}, bf16[2,128,128]{2,1,0:T(8,128)(2,1)S(1)}, u32[]{:S(2)}, u32[]{:S(2)}) collective-permute-start(bf16[2,128,128]{2,1,0:T(8,128)(2,1)S(1)} %get-tuple-element.27), channel_id=1, source_target_pairs={{0,8},{1,12},{2,0},{3,4},{4,9},{5,13},{6,1},{7,5},{8,10},{9,14},{1... | collective-permute-start | bytes 196616 | tf_op jit(solution)/shard_map/ppermute | solution.py:596
  34.0 33.9 %collective-permute-start.4 = (bf16[2,128,128]{2,1,0:T(8,128)(2,1)S(1)}, bf16[2,128,128]{2,1,0:T(8,128)(2,1)S(1)}, u32[]{:S(2)}, u32[]{:S(2)}) collective-permute-start(bf16[2,128,128]{2,1,0:T(8,128)(2,1)S(1)} %get-tuple-element.27), channel_id=1, source_target_pairs={{0,4},{1,8},{2,12},{3,0},{4,5},{5,9},{6,13},{7,1},{8,6},{9,10},{10... | collective-permute-start | bytes 196616 | tf_op jit(solution)/shard_map/ppermute | solution.py:596
  34.1 33.9 %collective-permute-start.3 = (bf16[2,128,128]{2,1,0:T(8,128)(2,1)S(1)}, bf16[2,128,128]{2,1,0:T(8,128)(2,1)S(1)}, u32[]{:S(2)}, u32[]{:S(2)}) collective-permute-start(bf16[2,128,128]{2,1,0:T(8,128)(2,1)S(1)} %get-tuple-element.27), channel_id=1, source_target_pairs={{0,0},{1,4},{2,8},{3,12},{4,1},{5,5},{6,9},{7,13},{8,2},{9,6},{10,... | collective-permute-start | bytes 196616 | tf_op jit(solution)/shard_map/ppermute | solution.py:596
  60.5 1.2 %copy-start.9 = (bf16[16,256,128]{2,1,0:T(8,128)(2,1)S(1)}, bf16[16,256,128]{2,1,0:T(8,128)(2,1)}, u32[]{:S(2)}) copy-start(bf16[16,256,128]{2,1,0:T(8,128)(2,1)} %all-gather.4.cloned.1.call-done) | copy-start | bytes 3145732
  61.7 0.8 copy-start.11
  62.5 0.8 copy-start.13
  63.3 0.8 copy-start.15
  66.3 20.8 %collective-permute-start.7 = (f32[16,8,256]{2,1,0:T(8,128)S(1)}, f32[16,8,256]{2,1,0:T(8,128)S(1)}, u32[]{:S(2)}, u32[]{:S(2)}) collective-permute-start(f32[16,8,256]{2,1,0:T(8,128)S(1)} %shard_map.132.gwa_ref), channel_id=1, source_target_pairs={{0,16},{16,0},{1,17},{17,1},{2,18},{18,2},{3,19},{19,3},{4,20},{20... | collective-permute-start | bytes 393224 | tf_op jit(solution)/shard_map/ppermute | solution.py:671
  67.9 0.6 copy-start.19
  67.9 0.6 copy-start.20
  67.9 0.7 copy-start.21
  68.0 0.7 copy-start.22
  68.6 18.6 %copy-start.8 = (s32[256]{0:T(256)S(1)}, s32[256]{0:T(256)}, u32[]{:S(2)}) copy-start(s32[256]{0:T(256)} %param.13) | copy-start | bytes 3076
  68.6 21.8 %copy-start = (bf16[512,128]{1,0:T(8,128)(2,1)S(1)}, bf16[512,128]{1,0:T(8,128)(2,1)}, u32[]{:S(2)}) copy-start(bf16[512,128]{1,0:T(8,128)(2,1)} %get-tuple-element.16.both_ref) | copy-start | bytes 393220
  68.6 21.8 %copy-start.10 = (bf16[16,256,128]{2,1,0:T(8,128)(2,1)S(1)}, bf16[16,256,128]{2,1,0:T(8,128)(2,1)}, u32[]{:S(2)}) copy-start(bf16[16,256,128]{2,1,0:T(8,128)(2,1)} %all-gather.4.cloned.1.call-done) | copy-start | bytes 3145732
  68.6 21.8 %copy-start.12 = (bf16[64,256]{1,0:T(8,128)(2,1)S(1)}, bf16[64,256]{1,0:T(8,128)(2,1)}, u32[]{:S(2)}) copy-start(bf16[64,256]{1,0:T(8,128)(2,1)} %wv_ref.3) | copy-start | bytes 98308
  68.6 21.8 %copy-start.14 = (bf16[64,256]{1,0:T(8,128)(2,1)S(1)}, bf16[64,256]{1,0:T(8,128)(2,1)}, u32[]{:S(2)}) copy-start(bf16[64,256]{1,0:T(8,128)(2,1)} %wg_ref.3) | copy-start | bytes 98308
  87.2 0.9 copy-start.3
  88.6 3.5 %collective-permute-start.8 = (f32[10,8,128]{2,1,0:T(8,128)S(1)}, f32[10,8,128]{2,1,0:T(8,128)S(1)}, u32[]{:S(2)}, u32[]{:S(2)}) collective-permute-start(f32[10,8,128]{2,1,0:T(8,128)S(1)} %get-tuple-element.19), channel_id=1, source_target_pairs={{0,1},{1,2},{2,3},{3,0},{4,5},{5,6},{6,7},{7,4},{8,9},{9,10},{10,1... | collective-permute-start | bytes 122888 | tf_op jit(solution)/shard_map/ppermute | solution.py:691
  88.6 4.3 %collective-permute-start.9 = (f32[10,8,128]{2,1,0:T(8,128)S(1)}, f32[10,8,128]{2,1,0:T(8,128)S(1)}, u32[]{:S(2)}, u32[]{:S(2)}) collective-permute-start(f32[10,8,128]{2,1,0:T(8,128)S(1)} %get-tuple-element.20), channel_id=1, source_target_pairs={{0,2},{1,3},{2,0},{3,1},{4,6},{5,7},{6,4},{7,5},{8,10},{9,11},{10,... | collective-permute-start | bytes 122888 | tf_op jit(solution)/shard_map/ppermute | solution.py:691
  88.7 4.2 %copy-start.4 = (f32[16,8,256]{2,1,0:T(8,128)S(1)}, f32[16,8,256]{2,1,0:T(8,128)}, u32[]{:S(2)}) copy-start(f32[16,8,256]{2,1,0:T(8,128)} %get-tuple-element.17.logits_ref) | copy-start | bytes 393220
  88.7 4.2 %copy-start.17 = (f32[128,8]{0,1:T(8,128)S(1)}, f32[128,8]{0,1:T(8,128)}, u32[]{:S(2)}) copy-start(f32[128,8]{0,1:T(8,128)} %param.19) | copy-start | bytes 12292
  88.7 4.2 %copy-start.18 = (bf16[16,128,256]{2,1,0:T(8,128)(2,1)S(1)}, bf16[16,128,256]{2,1,0:T(8,128)(2,1)}, u32[]{:S(2)}) copy-start(bf16[16,128,256]{2,1,0:T(8,128)(2,1)} %get-tuple-element.26.pout_t_ref) | copy-start | bytes 3145732
  88.7 4.2 %collective-permute-start.10 = (f32[10,8,128]{2,1,0:T(8,128)S(1)}, f32[10,8,128]{2,1,0:T(8,128)S(1)}, u32[]{:S(2)}, u32[]{:S(2)}) collective-permute-start(f32[10,8,128]{2,1,0:T(8,128)S(1)} %get-tuple-element.21), channel_id=1, source_target_pairs={{0,3},{1,0},{2,1},{3,2},{4,7},{5,4},{6,5},{7,6},{8,11},{9,8},{10,9... | collective-permute-start | bytes 122888 | tf_op jit(solution)/shard_map/ppermute | solution.py:691
  92.9 3.3 %copy-start.2 = (bf16[32,16,64]{2,1,0:T(8,128)(2,1)S(1)}, bf16[32,16,64]{2,1,0:T(8,128)(2,1)}, u32[]{:S(2)}) copy-start(bf16[32,16,64]{2,1,0:T(8,128)(2,1)} %x_ref.1) | copy-start | bytes 196612
  92.9 3.3 %copy-start.16 = (bf16[256,64]{0,1:T(8,128)(2,1)S(1)}, bf16[256,64]{0,1:T(8,128)(2,1)}, u32[]{:S(2)}) copy-start(bf16[256,64]{0,1:T(8,128)(2,1)} %param.20) | copy-start | bytes 98308
Sparse Core Ops, SparseCore 0:
  29.9 30.5 all-gather.3

commit v5 on v4

--- a/solution.py
+++ b/solution.py
@@ -72,7 +72,7 @@
 
 
 def prepare_kernel(
-    own_ref, x_ref, adj_ref, w1_ref, w2_ref, mask_ref, both_ref, sides_ref, turn_ref, right_ref
+    own_ref, x_ref, adj_ref, w1_ref, w2_ref, mask_ref, norm_ref, adj_out_ref, sides_ref, turn_ref, right_ref
 ):
     seqs, tokens, width = x_ref.shape
     half = seqs // 2
@@ -83,10 +83,10 @@
     normed = center * inverse
     rows = half * tokens
     packed = jnp.concatenate([normed[:half], normed[half:]], axis=-1)
-    both_ref[:rows] = packed.reshape(rows, 2 * width).astype(bf16)
+    norm_ref[...] = packed.reshape(rows, 2 * width).astype(bf16)
     adj = adj_ref[...].astype(f32)
     packed = jnp.concatenate([adj[:half], adj[half:]], axis=-1)
-    both_ref[rows:] = packed.reshape(rows, 2 * width).astype(bf16)
+    adj_out_ref[...] = packed.reshape(rows, 2 * width).astype(bf16)
     token = lax.broadcasted_iota(jnp.int32, (seqs, tokens, width), 1) + own_ref[0]
     count = valid_count(mask_ref).reshape(1, 1, 1)
     real = jnp.where(token.astype(f32) < count, normed, 0.0)
@@ -147,8 +147,6 @@
     fetch_pair.start()
     nk = rk_ref.shape[0]
     width_d, pair_rows, _ = rab_ref.shape
-    nq = right0_ref.shape[0]
-    seqs = pair_rows // nq
     row, col = place_ref[0], place_ref[1]
     z = pair_ref.shape[1]
     groups, heads, lanes = logits_ref.shape
@@ -156,11 +154,13 @@
     tokens = tile_j // nk
     per_k = groups // nk
     fc = lm_ref.shape[0] // groups
+    seqs = 128 // pack
+    nq = pair_rows // seqs
     wk = pack * seqs
     maskj = column_mask(mask_ref, col, tile_j, 2)
 
     for t, ref in enumerate((right0_ref, right1_ref, right2_ref, right3_ref)):
-        rk_ref[lax.rem(row + nk - t, nk)] = ref[...].reshape(rk_ref.shape[1:])
+        rk_ref[lax.rem(row + nk - t, nk)] = ref[: rk_ref.shape[1], :]
     size = 128 // tokens
     right = jnp.concatenate([rk_ref[k] for k in range(nk)], axis=1)
     source = lax.broadcasted_iota(jnp.int32, (nk * 128, 4 * tile_j), 0)
@@ -178,7 +178,7 @@
                 rab_ref[n * size + e, q * seqs : (q + 1) * seqs, :] = res[at : at + seqs]
 
     for t, ref in enumerate((left0_ref, left1_ref, left2_ref, left3_ref)):
-        k = lax.rem(col + nk - t, nk)
+        k = jnp.bitwise_xor(col, t)
         for g in range(per_k):
             at = pl.ds(pl.multiple_of((k * per_k + g) * fc, fc), fc)
             for q in range(nq):
@@ -186,9 +186,9 @@
                 lm_ref[at, q * wk : (q + 1) * wk] = ref[from_row : from_row + fc, :]
 
     chunk = 4
-
-    def outer_of(d, carry):
-        empty = jnp.zeros((seqs, 2 * tile_j), bf16)
+    empty = jnp.zeros((seqs, 2 * tile_j), bf16)
+
+    def block_of(d):
         rows = []
         for q in range(nq):
             both = rab_ref[d, q * seqs : (q + 1) * seqs, :]
@@ -197,16 +197,24 @@
                 pieces = [empty] * (pack // 2)
                 pieces[i // 2] = part[i % 2]
                 rows.append(jnp.concatenate(pieces, axis=1))
-        block = jnp.concatenate(rows, axis=0)
-        at = pl.ds(pl.multiple_of(d * fc, fc), fc)
-        for n in range(groups // chunk):
-            out = nn_dot(lm_ref[n * chunk * fc : (n + 1) * chunk * fc, :], block)
+        return jnp.concatenate(rows, axis=0)
+
+    def outer_of(n, carry):
+        block = jnp.concatenate([block_of(2 * n), block_of(2 * n + 1)], axis=1)
+        for m in range(groups // chunk):
+            out = nn_dot(lm_ref[m * chunk * fc : (m + 1) * chunk * fc, :], block)
             high, low = high_low(out)
-            oh_ref[n * chunk : (n + 1) * chunk, at, :] = high.reshape(chunk, fc, lanes)
-            ol_ref[n * chunk : (n + 1) * chunk, at, :] = low.reshape(chunk, fc, lanes)
+            for e in range(2):
+                at = pl.ds(pl.multiple_of((2 * n + e) * fc, fc), fc)
+                for g in range(chunk):
+                    group = m * chunk + g
+                    to = slice(group % 2 * lanes, (group % 2 + 1) * lanes)
+                    cut = slice(g * fc, (g + 1) * fc), slice(e * lanes, (e + 1) * lanes)
+                    oh_ref[group // 2, at, to] = high[cut]
+                    ol_ref[group // 2, at, to] = low[cut]
         return carry
 
-    lax.fori_loop(0, width_d, outer_of, 0, unroll=4)
+    lax.fori_loop(0, width_d // 2, outer_of, 0, unroll=2)
 
     fetch_m.wait()
     some = z // fc
@@ -219,7 +227,7 @@
         mt_ref[z:, n * z : (n + 1) * z] = low
     fetch_pair.wait()
 
-    maskl = jnp.concatenate([maskj] * (pack // 2), axis=1) > 0
+    maskl = jnp.concatenate([maskj] * pack, axis=1) > 0
     score = score_ref[...]
     s1 = score.astype(bf16).astype(f32)
     s2 = (score - s1).astype(bf16).astype(f32)
@@ -233,28 +241,31 @@
         axis=1,
     ).astype(bf16)
 
-    def finish(g, carry):
-        two = nn_dot(mt_ref[...], oh_ref[g])
-        update = two[:z] + two[z:] + nn_dot(mt_ref[:z, :], ol_ref[g])
-        at = pl.ds(pl.multiple_of(g * lanes, lanes), lanes)
+    def finish(n, carry):
+        two = nn_dot(mt_ref[...], oh_ref[n])
+        update = two[:z] + two[z:] + nn_dot(mt_ref[:z, :], ol_ref[n])
+        at = pl.ds(pl.multiple_of(n * 2 * lanes, 2 * lanes), 2 * lanes)
         before = pair_ref[at, :].astype(f32).T
         result = (before + update).astype(bf16)
-        pout_t_ref[g] = result
+        pout_t_ref[2 * n] = result[:, :lanes]
+        pout_t_ref[2 * n + 1] = result[:, lanes:]
         x = result.astype(f32)
         pout_ref[at, :] = x.T.astype(bf16)
-        pltpu.make_async_copy(pout_ref.at[at], pout_hbm.at[at], out_sem.at[g]).start()
+        pltpu.make_async_copy(pout_ref.at[at], pout_hbm.at[at], out_sem.at[n]).start()
         center = x - jnp.mean(x, axis=0, keepdims=True)
         inverse = lax.rsqrt(jnp.mean(center * center, axis=0, keepdims=True) + epsilon)
         high, low = high_low(center * inverse)
         scores = nn_dot(st, jnp.concatenate([high, low], axis=0))
         logits = scores[:heads] + scores[heads : 2 * heads] + scores[2 * heads : 3 * heads]
-        logits_ref[g] = jnp.where(maskl, logits, far_below)
+        logits = jnp.where(maskl, logits, far_below)
+        logits_ref[2 * n] = logits[:, :lanes]
+        logits_ref[2 * n + 1] = logits[:, lanes:]
         return carry
 
-    lax.fori_loop(0, groups, finish, 0, unroll=4)
-    for g in range(groups):
-        at = pl.ds(g * lanes, lanes)
-        pltpu.make_async_copy(pout_ref.at[at], pout_hbm.at[at], out_sem.at[g]).wait()
+    lax.fori_loop(0, groups // 2, finish, 0, unroll=2)
+    for n in range(groups // 2):
+        at = pl.ds(n * 2 * lanes, 2 * lanes)
+        pltpu.make_async_copy(pout_ref.at[at], pout_hbm.at[at], out_sem.at[n]).wait()
 
 
 def by_heads(w, heads, out_ref):
@@ -275,12 +286,15 @@
 
 
 def weights_kernel(
-    col_ref,
-    ev_ref,
+    place_ref,
     side0_ref,
     side1_ref,
     side2_ref,
     side3_ref,
+    cols0_ref,
+    cols1_ref,
+    cols2_ref,
+    cols3_ref,
     wv_ref,
     wg_ref,
     wf_ref,
@@ -290,17 +304,21 @@
     bg_ref,
     bf_ref,
     rows_ref,
+    cols_ref,
     gs_ref,
     vs_ref,
 ):
-    _, nk, half, tokens, _ = ev_ref.shape
+    nk, half, tokens, _ = cols_ref.shape
     tile = nk * tokens
     groups, heads, lanes = gw_ref.shape
-    col = col_ref[0]
-    count = rows_ref.shape[1] * rows_ref.shape[2] * tokens
+    row, col = place_ref[0], place_ref[1]
+    count = half * tokens
     for t, ref in enumerate((side0_ref, side1_ref, side2_ref, side3_ref)):
+        start = ref.shape[0] - 2 * count
+        rows_ref[jnp.bitwise_xor(col, t)] = ref[start:, :].reshape(rows_ref.shape[1:])
+    for t, ref in enumerate((cols0_ref, cols1_ref, cols2_ref, cols3_ref)):
         start = ref.shape[0] - count
-        rows_ref[lax.rem(col + nk - t, nk)] = ref[start:, :].reshape(rows_ref.shape[1:])
+        cols_ref[lax.rem(row + nk - t, nk)] = ref[start:, :].reshape(cols_ref.shape[1:])
     by_heads(wv_ref[...], heads, bv_ref)
     by_heads(wg_ref[...], heads, bg_ref)
     by_heads(wf_ref[...], heads, bf_ref)
@@ -321,11 +339,10 @@
             axis=0,
         )
 
-    slots = [lax.rem(col + nk - k, nk) for k in range(nk)]
     for hp in range(heads // 2):
         cut = slice(hp * 2 * block, (hp + 1) * 2 * block)
         for n in range(half // 4):
-            v = nn_dot(four(lambda k, s: ev_ref[col, slots[k], s], n), bv_ref[:, cut]).astype(bf16)
+            v = nn_dot(four(lambda k, s: cols_ref[k, s], n), bv_ref[:, cut]).astype(bf16)
             gate = nn_dot(four(lambda k, s: rows_ref[k, 0, s], n), bg_ref[:, cut])
             grad = nn_dot(four(lambda k, s: rows_ref[k, 1, s], n), bf_ref[:, cut])
             g = (grad * jax.nn.sigmoid(gate)).astype(bf16)
@@ -398,17 +415,16 @@
                 pay[2 + g * (pack // 2) + part] = piece[:, part * 2 * tile : (part + 1) * 2 * tile]
 
 
-def values_kernel(col_ref, ev_ref, wv_ref, both_ref, wg_ref, v_ref, gate_ref):
-    nr, nk, half, tokens, wide = ev_ref.shape
+def values_kernel(ev_ref, wv_ref, norm_ref, wg_ref, v_ref, gate_ref):
+    owners, half, tokens, wide = ev_ref.shape
     chans = wv_ref.shape[1]
     wv = twice(wv_ref[...])
-    slots = [lax.rem(col_ref[0] + nk - k, nk) for k in range(nk)]
     for s in range(half):
-        x = jnp.concatenate([ev_ref[r, slots[k], s] for r in range(nr) for k in range(nk)], axis=0)
+        x = jnp.concatenate([ev_ref[k, s] for k in range(owners)], axis=0)
         v = nn_dot(x, wv).astype(bf16)
         v_ref[s] = v[:, :chans]
         v_ref[s + half] = v[:, chans:]
-    gate = jax.nn.sigmoid(nn_dot(both_ref[: half * tokens, :], twice(wg_ref[...])))
+    gate = jax.nn.sigmoid(nn_dot(norm_ref[...], twice(wg_ref[...])))
     gate_ref[: half * tokens] = gate[:, :chans]
     gate_ref[half * tokens :] = gate[:, chans:]
 
@@ -571,9 +587,13 @@
 
     sides_left = tokens // pack * fc
     sides_rows = sides_left + fd * tokens // 128 * seqs
-    both, sides = call(
+    normed, adjoint, sides = call(
         prepare_kernel,
-        (sds((2 * half * tokens, 2 * width), bf16), sds((sides_rows, 128), bf16)),
+        (
+            sds((half * tokens, 2 * width), bf16),
+            sds((half * tokens, 2 * width), bf16),
+            sds((sides_rows, 128), bf16),
+        ),
         scratch=(
             pltpu.VMEM((tokens, seqs, width), f32),
             pltpu.VMEM((fd * tokens // 128, seqs, 128), f32),
@@ -589,9 +609,12 @@
         mask,
     )
 
+    every = lax.all_gather(normed, ("row", "col"), axis=0).reshape(
+        nr * nk, half, tokens, 2 * width
+    )
     sides = lax.all_gather(sides, "seq", axis=0)
-    lefts = jnp.concatenate([sides[:, :sides_left].reshape(nq * sides_left, 128), both], axis=0)
-    rights = sides[:, sides_left:]
+    rights = sides[:, sides_left:].reshape(nq * (sides_rows - sides_left), 128)
+    rights = jnp.concatenate([rights, normed], axis=0)
     all_rights = [
         lax.ppermute(
             rights,
@@ -600,12 +623,44 @@
         )
         for t in range(nr)
     ]
-    all_lefts = [lefts] + [
-        lax.ppermute(lefts, "col", [(c, (c + t) % nk) for c in range(nk)]) for t in range(1, nk)
-    ]
-    start = nq * sides_left
-    block_rows = jnp.stack([x[start : start + half * tokens] for x in all_lefts])
-    every = lax.all_gather(block_rows, "row", axis=0).reshape(nr, nk, half, tokens, 2 * width)
+    lefts = sides[:, :sides_left].reshape(nq * sides_left, 128)
+    lefts = jnp.concatenate([lefts, normed, adjoint], axis=0)
+
+    def exchange(x, bit):
+        return lax.ppermute(x, "col", [(c, c ^ bit) for c in range(nk)])
+
+    across = exchange(lefts, 2)
+    all_lefts = [lefts, exchange(lefts, 1), across, exchange(across, 1)]
+
+    head_lanes = seqs * chans // heads
+    (gw_own,) = call(
+        weights_kernel,
+        (sds((groups, heads, lanes), f32),),
+        scratch=(
+            pltpu.VMEM((heads * tile_i, 2 * tile_j), f32),
+            pltpu.VMEM((4 * width, 4 * chans), bf16),
+            pltpu.VMEM((4 * width, 4 * chans), bf16),
+            pltpu.VMEM((4 * width, 4 * chans), bf16),
+            pltpu.VMEM((nk, 2, half, tokens, 2 * width), bf16),
+            pltpu.VMEM((nk, half, tokens, 2 * width), bf16),
+            pltpu.VMEM((heads, tile_i, head_lanes), bf16),
+            pltpu.VMEM((heads, 2 * tile_j, head_lanes), bf16),
+        ),
+        smem=1,
+        flops=3_000_000_000,
+        nbytes=3_000_000,
+    )(
+        place,
+        *all_lefts,
+        *all_rights,
+        content_weights_grid,
+        sigmoid_weights_grid,
+        final_mixing_weights.T,
+    )
+    if nq == 2:
+        gw_other = lax.ppermute(gw_own, "seq", [(0, 1), (1, 0)])
+    else:
+        gw_own, gw_other = lax.psum(gw_own, "seq"), jnp.zeros_like(gw_own)
 
     pair_out, pair_t, logits = call(
         update_kernel,
@@ -619,13 +674,13 @@
             pltpu.VMEM((tile_i * tile_j, z), bf16),
             pltpu.VMEM((tile_i * tile_j, z), bf16),
             pltpu.SemaphoreType.DMA((2,)),
-            pltpu.SemaphoreType.DMA((groups,)),
+            pltpu.SemaphoreType.DMA((groups // 2,)),
             pltpu.VMEM((nk, nq * (sides_rows - sides_left), 128), bf16),
             pltpu.VMEM((fd, nq * seqs, 4 * tile_j), bf16),
             pltpu.VMEM((groups * fc, nq * pack * seqs), bf16),
             pltpu.VMEM((2 * z, fd * fc), bf16),
-            pltpu.VMEM((groups, fd * fc, lanes), bf16),
-            pltpu.VMEM((groups, fd * fc, lanes), bf16),
+            pltpu.VMEM((groups // 2, fd * fc, 2 * lanes), bf16),
+            pltpu.VMEM((groups // 2, fd * fc, 2 * lanes), bf16),
         ),
         smem=1,
         flops=14_000_000_000,
@@ -643,42 +698,12 @@
         pair_input.reshape(tile_i * tile_j, z),
     )
 
-    head_lanes = seqs * chans // heads
-    (gw_own,) = call(
-        weights_kernel,
-        (sds((groups, heads, lanes), f32),),
-        scratch=(
-            pltpu.VMEM((heads * tile_i, 2 * tile_j), f32),
-            pltpu.VMEM((4 * width, 4 * chans), bf16),
-            pltpu.VMEM((4 * width, 4 * chans), bf16),
-            pltpu.VMEM((4 * width, 4 * chans), bf16),
-            pltpu.VMEM((nk, 2, half, tokens, 2 * width), bf16),
-            pltpu.VMEM((heads, tile_i, head_lanes), bf16),
-            pltpu.VMEM((heads, 2 * tile_j, head_lanes), bf16),
-        ),
-        smem=1,
-        flops=3_000_000_000,
-        nbytes=3_000_000,
-    )(
-        col_scalar,
-        every,
-        *all_lefts,
-        content_weights_grid,
-        sigmoid_weights_grid,
-        final_mixing_weights.T,
-    )
-    if nq == 2:
-        gw_other = lax.ppermute(gw_own, "seq", [(0, 1), (1, 0)])
-    else:
-        gw_own, gw_other = lax.psum(gw_own, "seq"), jnp.zeros_like(gw_own)
-
     values, gating = call(
         values_kernel,
         (sds((seqs, nr * nk * tokens, chans), bf16), sds((seqs * tokens, chans), f32)),
-        smem=1,
         flops=4_000_000_000,
         nbytes=6_000_000,
-    )(col_scalar, every, content_weights_grid, both, sigmoid_weights_grid)
+    )(every, content_weights_grid, normed, sigmoid_weights_grid)
 
     payload = sds((2 + groups // nk * (pack // 2), heads, 2 * tile_j), f32)
     gw, pay0, pay1, pay2, pay3 = call(

time: 107 us -> 85.2 us (0.80)
  waiting for transfers between devices: 35.1 us -> 8.54 us
  starting transfers between devices: 10.6 us -> 19.3 us
  Pallas kernels: 31.9 us -> 27.7 us
    all_gather x1, waiting for transfers between devices: 25.2 us -> 0.01 us  [on_device(): lax.all_gather(normed, ('row', 'col'), axis=0)]
    ppermute x3, waiting for transfers between devices: 8.69 us -> 1.52 us  [exchange(): return lax.ppermute(x, 'col', [(c, c ^ bit) for c in range(nk)])]
    ppermute x3, starting transfers between devices: 1.79 us -> 8.51 us  [on_device(): lax.ppermute(pay, 'col', [(c, (c + shift) % nk) for c in range(nk)])]
    ppermute x4, waiting for transfers between devices: 0.01 us -> 5.33 us  [on_device(): lax.ppermute(rights, ('row', 'col'), [(r * nk + c, (c + t) % nr * nk + r)...]
    pallas_call x7, Pallas kernels: 31.9 us -> 27.7 us  [run(): pl.pallas_call(kernel, out_shape=out_shape, in_specs=[pl.BlockSpec(memory...]
    ppermute x4, starting transfers between devices: 4.94 us -> 7.11 us  [on_device(): lax.ppermute(rights, ('row', 'col'), [(r * nk + c, (c + t) % nr * nk + r)...]
    unnamed x46, local copies, waits for them, and re-layouts: 5.12 us -> 6.62 us
  transfers between devices with their start and end apart: 12 -> 12, of which waited for: 5 -> 5; matrix products, arithmetic and copies ran while one was open for 1% -> 1% of each run, Pallas kernels for 21% -> 24%
where the time goes in v5:
time: 85.2 us; the launch traced here: 84.4 us
  Pallas kernels  27.7 us (33%)
  starting transfers between devices  19.3 us (23%)
  between operations  14.3 us (17%)
  waiting for transfers between devices  8.54 us (10%)
  local copies, waits for them, and re-layouts  6.63 us (8%)
  blocking collectives  6.1 us (7%)
  other arithmetic  1.81 us (2%)
    pallas_call x7, Pallas kernels, run(): pl.pallas_call(kernel, out_shape=out_shape, in_specs=[pl.BlockSpec(memory...  27.7 us
    ppermute x3, starting transfers between devices, on_device(): lax.ppermute(pay, 'col', [(c, (c + shift) % nk) for c in range(nk)])  8.51 us
    ppermute x4, starting transfers between devices, on_device(): lax.ppermute(rights, ('row', 'col'), [(r * nk + c, (c + t) % nr * nk + r)...  7.11 us
    unnamed x46, local copies, waits for them, and re-layouts  6.62 us
    all_gather x1, blocking collectives, on_device(): sides = lax.all_gather(sides, 'seq', axis=0)  6.1 us
    ppermute x4, waiting for transfers between devices, on_device(): lax.ppermute(rights, ('row', 'col'), [(r * nk + c, (c + t) % nr * nk + r)...  5.33 us
    ppermute x3, starting transfers between devices, exchange(): return lax.ppermute(x, 'col', [(c, c ^ bit) for c in range(nk)])  2.08 us
  transfers between devices with their start and end apart: 12, of which 5 were waited for; matrix products, arithmetic and copies ran while one was open for 1% of the time, Pallas kernels for 24%

profile of v5, /device:TPU:0, one launch (start us, length us, event | category | flops | bytes accessed | tf_op | source)
XLA Modules:
  0.0 84.4 jit_solution(14741235067920612903)
XLA Ops:
  7.2 0.0 all-gather.4.cloned.1.call-start
  7.2 2.8 %shard_map.130 = (bf16[256,128]{1,0:T(8,128)(2,1)}, bf16[256,128]{1,0:T(8,128)(2,1)}, bf16[256,128]{1,0:T(8,128)(2,1)}) custom-call(s32[1]{0:T(128)} %bitcast.2.own_ref, bf16[32,16,64]{2,1,0:T(8,128)(2,1)} %x_ref.1, bf16[32,16,64]{2,1,0:T(8,128)(2,1)} %adj_ref.1, bf16[32,64]{1,0:T(8,128)(2,1)} %bitcast.29, bf16[32,64]{1,0:T(8,128)(2,1)} %bitcast.30, ...), custom_call_target="tpu_custom_call" | custom-call | tf_op jit(solution)/shard_map/pallas_call | solution.py:38
  10.0 6.1 %all-gather = bf16[512,128]{1,0:T(8,128)(2,1)S(1)} all-gather(bf16[256,128]{1,0:T(8,128)(2,1)} %get-tuple-element.16), channel_id=2, replica_groups=mesh['seq'=2,'row'=4,'col'=4] {'seq'}, dimensions={0}, use_global_device_ids=true | all-gather | bytes 196608 | tf_op jit(solution)/shard_map/all_gather | solution.py:615
  16.1 0.9 %pad_maximum_fusion.left0_ref.side0_ref = bf16[768,128]{1,0:T(8,128)(2,1)S(1)} fusion(bf16[256,128]{1,0:T(8,128)(2,1)} %get-tuple-element.18, bf16[256,128]{1,0:T(8,128)(2,1)} %get-tuple-element.17.norm_ref, bf16[256,128]{1,0:T(8,128)(2,1)S(1)} %bitcast.28), kind=kLoop, calls=%fused_computation | loop fusion | flops 589824 | bytes 393216 | tf_op jit(solution)/shard_map/concatenate | solution.py:627
  17.0 0.0 copy-start.1
  17.0 2.1 %collective-permute-start.1 = (bf16[768,128]{1,0:T(8,128)(2,1)S(1)}, bf16[768,128]{1,0:T(8,128)(2,1)S(1)}, u32[]{:S(2)}, u32[]{:S(2)}) collective-permute-start(bf16[768,128]{1,0:T(8,128)(2,1)S(1)} %pad_maximum_fusion.left0_ref.side0_ref), channel_id=1, source_target_pairs={{0,2},{1,3},{2,0},{3,1},{4,6},{5,7},{6,4},{7,5},{8,10},{9,11},{10,... | collective-permute-start | bytes 589832 | tf_op jit(solution)/shard_map/ppermute | solution.py:630
  19.1 0.8 %pad_maximum_fusion.1 = bf16[512,128]{1,0:T(8,128)(2,1)S(1)} fusion(bf16[256,128]{1,0:T(8,128)(2,1)} %get-tuple-element.17.norm_ref, bf16[256,128]{1,0:T(8,128)(2,1)S(1)} %bitcast.27), kind=kLoop, calls=%fused_computation.1 | loop fusion | flops 262144 | bytes 262144 | tf_op jit(solution)/shard_map/concatenate | solution.py:617
  19.9 3.7 %collective-permute-start.6 = (bf16[512,128]{1,0:T(8,128)(2,1)S(1)}, bf16[512,128]{1,0:T(8,128)(2,1)S(1)}, u32[]{:S(2)}, u32[]{:S(2)}) collective-permute-start(bf16[512,128]{1,0:T(8,128)(2,1)S(1)} %pad_maximum_fusion.1), channel_id=1, source_target_pairs={{0,12},{1,0},{2,4},{3,8},{4,13},{5,1},{6,5},{7,9},{8,14},{9,2},{10... | collective-permute-start | bytes 393224 | tf_op jit(solution)/shard_map/ppermute | solution.py:619
  23.6 0.0 collective-permute-start
  23.6 1.5 %collective-permute-done.1.left2_ref.side2_ref = bf16[768,128]{1,0:T(8,128)(2,1)S(1)} collective-permute-done((bf16[768,128]{1,0:T(8,128)(2,1)S(1)}, bf16[768,128]{1,0:T(8,128)(2,1)S(1)}, u32[]{:S(2)}, u32[]{:S(2)}) %collective-permute-start.1) | collective-permute-done | bytes 196640 | tf_op jit(solution)/shard_map/ppermute | solution.py:630
  25.1 0.0 collective-permute-start.2
  25.1 2.1 %collective-permute-start.5 = (bf16[512,128]{1,0:T(8,128)(2,1)S(1)}, bf16[512,128]{1,0:T(8,128)(2,1)S(1)}, u32[]{:S(2)}, u32[]{:S(2)}) collective-permute-start(bf16[512,128]{1,0:T(8,128)(2,1)S(1)} %pad_maximum_fusion.1), channel_id=1, source_target_pairs={{0,8},{1,12},{2,0},{3,4},{4,9},{5,13},{6,1},{7,5},{8,10},{9,14},{1... | collective-permute-start | bytes 393224 | tf_op jit(solution)/shard_map/ppermute | solution.py:619
  27.2 0.7 collective-permute-start.4
  27.9 0.0 collective-permute-done.6.right3_ref.cols3_ref
  27.9 0.7 collective-permute-start.3
  28.6 0.0 all-gather.4.cloned.1.call-update
  28.6 0.1 pad_add_fusion.place_ref
  28.7 3.9 %collective-permute-done.5.right2_ref.cols2_ref = bf16[512,128]{1,0:T(8,128)(2,1)S(1)} collective-permute-done((bf16[512,128]{1,0:T(8,128)(2,1)S(1)}, bf16[512,128]{1,0:T(8,128)(2,1)S(1)}, u32[]{:S(2)}, u32[]{:S(2)}) %collective-permute-start.5) | collective-permute-done | bytes 131104 | tf_op jit(solution)/shard_map/ppermute | solution.py:619
  32.6 1.4 %collective-permute-done.4.right1_ref.cols1_ref = bf16[512,128]{1,0:T(8,128)(2,1)S(1)} collective-permute-done((bf16[512,128]{1,0:T(8,128)(2,1)S(1)}, bf16[512,128]{1,0:T(8,128)(2,1)S(1)}, u32[]{:S(2)}, u32[]{:S(2)}) %collective-permute-start.4) | collective-permute-done | bytes 131104 | tf_op jit(solution)/shard_map/ppermute | solution.py:619
  34.0 0.0 collective-permute-done.3.right0_ref.cols0_ref
  34.0 0.0 collective-permute-done.left1_ref.side1_ref
  34.0 0.0 copy-start.8
  34.1 0.0 collective-permute-done.2.left3_ref.side3_ref
  34.1 0.0 copy-start.9
  34.1 0.0 copy-start.14
  34.1 0.8 copy-done.14
  34.9 0.8 copy-done.16
  35.6 0.8 copy-done.18
  36.4 2.8 %shard_map.132.gwa_ref = f32[16,8,256]{2,1,0:T(8,128)S(1)} custom-call(s32[2]{0:T(128)S(1)} %pad_add_fusion.place_ref, bf16[768,128]{1,0:T(8,128)(2,1)S(1)} %pad_maximum_fusion.left0_ref.side0_ref, bf16[768,128]{1,0:T(8,128)(2,1)S(1)} %collective-permute-done.left1_ref.side1_ref, bf16[768,128]{1,0:T(8,128)(2,1)S(1)} %collective-permute-done.1.left2_ref.side2_ref, ...), custom_call_target="tpu_custom_call" | custom-call | flops 3000000000 | bytes 3000000 | tf_op jit(solution)/shard_map/pallas_call | solution.py:38
  39.2 0.0 copy-done.1
  39.2 0.0 copy-done.7
  39.2 0.0 copy-done.10
  39.2 0.0 copy-done.21
  39.2 0.0 copy-done.11
  39.3 0.0 copy-done.12
  39.3 0.0 copy-done.13
  39.3 0.0 copy-done.8
  39.3 0.0 copy-done.9
  39.3 1.5 %collective-permute-start.7 = (f32[16,8,256]{2,1,0:T(8,128)S(1)}, f32[16,8,256]{2,1,0:T(8,128)S(1)}, u32[]{:S(2)}, u32[]{:S(2)}) collective-permute-start(f32[16,8,256]{2,1,0:T(8,128)S(1)} %shard_map.132.gwa_ref), channel_id=1, source_target_pairs={{0,16},{16,0},{1,17},{17,1},{2,18},{18,2},{3,19},{19,3},{4,20},{20... | collective-permute-start | bytes 393224 | tf_op jit(solution)/shard_map/ppermute | solution.py:661
  40.8 13.9 %shard_map.131 = (bf16[4096,128]{1,0:T(8,128)(2,1)}, bf16[16,128,256]{2,1,0:T(8,128)(2,1)}, f32[16,8,256]{2,1,0:T(8,128)}) custom-call(s32[2]{0:T(128)} %copy-done.21, bf16[768,128]{1,0:T(8,128)(2,1)} %copy-done.1, bf16[768,128]{1,0:T(8,128)(2,1)} %copy-done.8, bf16[768,128]{1,0:T(8,128)(2,1)} %copy-done.7, bf16[768,128]{1,0:T(8,128)(2,1)} %copy-done.9, ...), custom_call_target="tpu_custom_call" | custom-call | flops 14000000000 | bytes 5000000 | tf_op jit(solution)/shard_map/pallas_call | solution.py:38
  54.7 0.0 collective-permute-done.7.gwb_ref
  54.7 0.0 copy-done.5
  54.7 0.0 copy-start.3
  54.8 0.9 %copy-done.3 = f32[16,8,256]{2,1,0:T(8,128)S(1)} copy-done((f32[16,8,256]{2,1,0:T(8,128)S(1)}, f32[16,8,256]{2,1,0:T(8,128)}, u32[]{:S(2)}) %copy-start.3) | copy-done | bytes 131096
  55.6 0.5 shard_map.133
  56.1 3.7 %collective-permute-start.8 = (f32[10,8,128]{2,1,0:T(8,128)S(1)}, f32[10,8,128]{2,1,0:T(8,128)S(1)}, u32[]{:S(2)}, u32[]{:S(2)}) collective-permute-start(f32[10,8,128]{2,1,0:T(8,128)S(1)} %get-tuple-element.21), channel_id=1, source_target_pairs={{0,1},{1,2},{2,3},{3,0},{4,5},{5,6},{6,7},{7,4},{8,9},{9,10},{10,1... | collective-permute-start | bytes 122888 | tf_op jit(solution)/shard_map/ppermute | solution.py:716
  59.8 3.4 %collective-permute-start.9 = (f32[10,8,128]{2,1,0:T(8,128)S(1)}, f32[10,8,128]{2,1,0:T(8,128)S(1)}, u32[]{:S(2)}, u32[]{:S(2)}) collective-permute-start(f32[10,8,128]{2,1,0:T(8,128)S(1)} %get-tuple-element.22), channel_id=1, source_target_pairs={{0,2},{1,3},{2,0},{3,1},{4,6},{5,7},{6,4},{7,5},{8,10},{9,11},{10,... | collective-permute-start | bytes 122888 | tf_op jit(solution)/shard_map/ppermute | solution.py:716
  63.2 1.4 %collective-permute-start.10 = (f32[10,8,128]{2,1,0:T(8,128)S(1)}, f32[10,8,128]{2,1,0:T(8,128)S(1)}, u32[]{:S(2)}, u32[]{:S(2)}) collective-permute-start(f32[10,8,128]{2,1,0:T(8,128)S(1)} %get-tuple-element.23), channel_id=1, source_target_pairs={{0,3},{1,0},{2,1},{3,2},{4,7},{5,4},{6,5},{7,6},{8,11},{9,8},{10,9... | collective-permute-start | bytes 122888 | tf_op jit(solution)/shard_map/ppermute | solution.py:716
  64.6 0.0 collective-permute-done.8.r1_ref
  64.6 0.6 collective-permute-done.9.r2_ref
  65.2 1.1 %collective-permute-done.10.r3_ref = f32[10,8,128]{2,1,0:T(8,128)S(1)} collective-permute-done((f32[10,8,128]{2,1,0:T(8,128)S(1)}, f32[10,8,128]{2,1,0:T(8,128)S(1)}, u32[]{:S(2)}, u32[]{:S(2)}) %collective-permute-start.10) | collective-permute-done | bytes 40992 | tf_op jit(solution)/shard_map/ppermute | solution.py:716
  66.3 0.0 copy-done.20
  66.3 0.9 %copy-done.4 = f32[16,8,256]{2,1,0:T(8,128)S(1)} copy-done((f32[16,8,256]{2,1,0:T(8,128)S(1)}, f32[16,8,256]{2,1,0:T(8,128)}, u32[]{:S(2)}) %copy-start.4) | copy-done | bytes 131096
  67.2 1.2 %copy-done.22 = bf16[16,128,256]{2,1,0:T(8,128)(2,1)S(1)} copy-done((bf16[16,128,256]{2,1,0:T(8,128)(2,1)S(1)}, bf16[16,128,256]{2,1,0:T(8,128)(2,1)}, u32[]{:S(2)}) %copy-start.22) | copy-done | bytes 1048600
  68.4 3.3 %shard_map.136 = bf16[4096,128]{1,0:T(8,128)(2,1)} custom-call(f32[10,8,128]{2,1,0:T(8,128)S(1)} %get-tuple-element.20.own_ref, f32[10,8,128]{2,1,0:T(8,128)S(1)} %collective-permute-done.8.r1_ref, f32[10,8,128]{2,1,0:T(8,128)S(1)} %collective-permute-done.9.r2_ref, f32[10,8,128]{2,1,0:T(8,128)S(1)} %collective-permute-done.10.r3_ref, ...), custom_call_target="tpu_custom_call" | custom-call | flops 4000000000 | bytes 3000000 | tf_op jit(solution)/shard_map/pallas_call | solution.py:38
  71.7 0.0 copy-done
  71.7 0.0 copy-done.15
  71.7 0.0 copy-done.17
  71.7 0.0 copy-start.6
  71.7 1.2 %copy-done.6 = bf16[4096,128]{1,0:T(8,128)(2,1)S(1)} copy-done((bf16[4096,128]{1,0:T(8,128)(2,1)S(1)}, bf16[4096,128]{1,0:T(8,128)(2,1)}, u32[]{:S(2)}) %copy-start.6) | copy-done | bytes 1048600
  73.0 1.3 %shard_map.134 = (bf16[32,256,256]{2,1,0:T(8,128)(2,1)S(1)}, f32[512,256]{1,0:T(8,128)S(1)}) custom-call(bf16[16,16,16,128]{3,2,1,0:T(8,128)(2,1)S(1)} %bitcast.21, bf16[64,256]{1,0:T(8,128)(2,1)S(1)} %copy-done.15, bf16[256,128]{1,0:T(8,128)(2,1)S(1)} %copy-done, bf16[64,256]{1,0:T(8,128)(2,1)S(1)} %copy-done.17), custom_call_target="tpu_custom_call" | custom-call | flops 4000000000 | bytes 6000000 | tf_op jit(solution)/shard_map/pallas_call | solution.py:38
  74.3 0.0 copy-done.2
  74.3 0.0 copy-done.19
  74.3 3.2 %shard_map.135 = bf16[512,64]{1,0:T(8,128)(2,1)} custom-call(s32[1]{0:T(128)} %bitcast.col_ref, f32[10,8,128]{2,1,0:T(8,128)S(1)} %get-tuple-element.20.own_ref, f32[10,8,128]{2,1,0:T(8,128)S(1)} %collective-permute-done.8.r1_ref, f32[10,8,128]{2,1,0:T(8,128)S(1)} %collective-permute-done.9.r2_ref, f32[10,8,128]{2,1,0:T(8,128)S(1)} %collective-permute-done.10.r3_ref, ...), custom_call_target="tpu_custom_call" | custom-call | flops 3000000000 | bytes 5000000 | tf_op jit(solution)/shard_map/pallas_call | solution.py:38
  (19 shorter events, 0.0 us)
Async XLA Ops:
  7.2 64.6 %all-gather.4.cloned.1.call-start = ((), (), s32[]{:S(2)}) async-start(), calls=%async_computation | async-start | bytes 1114112 | tf_op jit(solution)/shard_map/all_gather | solution.py:612
  17.0 22.2 %copy-start.1 = (bf16[768,128]{1,0:T(8,128)(2,1)}, bf16[768,128]{1,0:T(8,128)(2,1)S(1)}, u32[]{:S(2)}) copy-start(bf16[768,128]{1,0:T(8,128)(2,1)S(1)} %pad_maximum_fusion.left0_ref.side0_ref) | copy-start | bytes 589828
  17.0 8.1 %collective-permute-start.1 = (bf16[768,128]{1,0:T(8,128)(2,1)S(1)}, bf16[768,128]{1,0:T(8,128)(2,1)S(1)}, u32[]{:S(2)}, u32[]{:S(2)}) collective-permute-start(bf16[768,128]{1,0:T(8,128)(2,1)S(1)} %pad_maximum_fusion.left0_ref.side0_ref), channel_id=1, source_target_pairs={{0,2},{1,3},{2,0},{3,1},{4,6},{5,7},{6,4},{7,5},{8,10},{9,11},{10,... | collective-permute-start | bytes 589832 | tf_op jit(solution)/shard_map/ppermute | solution.py:630
  19.9 8.0 %collective-permute-start.6 = (bf16[512,128]{1,0:T(8,128)(2,1)S(1)}, bf16[512,128]{1,0:T(8,128)(2,1)S(1)}, u32[]{:S(2)}, u32[]{:S(2)}) collective-permute-start(bf16[512,128]{1,0:T(8,128)(2,1)S(1)} %pad_maximum_fusion.1), channel_id=1, source_target_pairs={{0,12},{1,0},{2,4},{3,8},{4,13},{5,1},{6,5},{7,9},{8,14},{9,2},{10... | collective-permute-start | bytes 393224 | tf_op jit(solution)/shard_map/ppermute | solution.py:619
  23.6 10.4 %collective-permute-start = (bf16[768,128]{1,0:T(8,128)(2,1)S(1)}, bf16[768,128]{1,0:T(8,128)(2,1)S(1)}, u32[]{:S(2)}, u32[]{:S(2)}) collective-permute-start(bf16[768,128]{1,0:T(8,128)(2,1)S(1)} %pad_maximum_fusion.left0_ref.side0_ref), channel_id=1, source_target_pairs={{0,1},{1,0},{2,3},{3,2},{4,5},{5,4},{6,7},{7,6},{8,9},{9,8},{10,11... | collective-permute-start | bytes 589832 | tf_op jit(solution)/shard_map/ppermute | solution.py:630
  25.1 14.1 %copy-start.7 = (bf16[768,128]{1,0:T(8,128)(2,1)}, bf16[768,128]{1,0:T(8,128)(2,1)S(1)}, u32[]{:S(2)}) copy-start(bf16[768,128]{1,0:T(8,128)(2,1)S(1)} %collective-permute-done.1.left2_ref.side2_ref) | copy-start | bytes 589828
  25.1 8.9 %collective-permute-start.2 = (bf16[768,128]{1,0:T(8,128)(2,1)S(1)}, bf16[768,128]{1,0:T(8,128)(2,1)S(1)}, u32[]{:S(2)}, u32[]{:S(2)}) collective-permute-start(bf16[768,128]{1,0:T(8,128)(2,1)S(1)} %collective-permute-done.1.left2_ref.side2_ref), channel_id=1, source_target_pairs={{0,1},{1,0},{2,3},{3,2},{4,5},{5,4},{6,7},{7,6},{8,9},{9,8},{10,11... | collective-permute-start | bytes 589832 | tf_op jit(solution)/shard_map/ppermute | solution.py:630
  25.1 7.5 %collective-permute-start.5 = (bf16[512,128]{1,0:T(8,128)(2,1)S(1)}, bf16[512,128]{1,0:T(8,128)(2,1)S(1)}, u32[]{:S(2)}, u32[]{:S(2)}) collective-permute-start(bf16[512,128]{1,0:T(8,128)(2,1)S(1)} %pad_maximum_fusion.1), channel_id=1, source_target_pairs={{0,8},{1,12},{2,0},{3,4},{4,9},{5,13},{6,1},{7,5},{8,10},{9,14},{1... | collective-permute-start | bytes 393224 | tf_op jit(solution)/shard_map/ppermute | solution.py:619
  27.2 6.8 %collective-permute-start.4 = (bf16[512,128]{1,0:T(8,128)(2,1)S(1)}, bf16[512,128]{1,0:T(8,128)(2,1)S(1)}, u32[]{:S(2)}, u32[]{:S(2)}) collective-permute-start(bf16[512,128]{1,0:T(8,128)(2,1)S(1)} %pad_maximum_fusion.1), channel_id=1, source_target_pairs={{0,4},{1,8},{2,12},{3,0},{4,5},{5,9},{6,13},{7,1},{8,6},{9,10},{10... | collective-permute-start | bytes 393224 | tf_op jit(solution)/shard_map/ppermute | solution.py:619
  27.9 11.3 %copy-start.10 = (bf16[512,128]{1,0:T(8,128)(2,1)}, bf16[512,128]{1,0:T(8,128)(2,1)S(1)}, u32[]{:S(2)}) copy-start(bf16[512,128]{1,0:T(8,128)(2,1)S(1)} %collective-permute-done.6.right3_ref.cols3_ref) | copy-start | bytes 393220
  27.9 6.1 %collective-permute-start.3 = (bf16[512,128]{1,0:T(8,128)(2,1)S(1)}, bf16[512,128]{1,0:T(8,128)(2,1)S(1)}, u32[]{:S(2)}, u32[]{:S(2)}) collective-permute-start(bf16[512,128]{1,0:T(8,128)(2,1)S(1)} %pad_maximum_fusion.1), channel_id=1, source_target_pairs={{0,0},{1,4},{2,8},{3,12},{4,1},{5,5},{6,9},{7,13},{8,2},{9,6},{10,... | collective-permute-start | bytes 393224 | tf_op jit(solution)/shard_map/ppermute | solution.py:619
  28.7 10.5 %copy-start.21 = (s32[2]{0:T(128)}, s32[2]{0:T(128)S(1)}, u32[]{:S(2)}) copy-start(s32[2]{0:T(128)S(1)} %pad_add_fusion.place_ref) | copy-start | bytes 28
  32.6 6.6 %copy-start.11 = (bf16[512,128]{1,0:T(8,128)(2,1)}, bf16[512,128]{1,0:T(8,128)(2,1)S(1)}, u32[]{:S(2)}) copy-start(bf16[512,128]{1,0:T(8,128)(2,1)S(1)} %collective-permute-done.5.right2_ref.cols2_ref) | copy-start | bytes 393220
  34.0 5.2 %copy-start.12 = (bf16[512,128]{1,0:T(8,128)(2,1)}, bf16[512,128]{1,0:T(8,128)(2,1)S(1)}, u32[]{:S(2)}) copy-start(bf16[512,128]{1,0:T(8,128)(2,1)S(1)} %collective-permute-done.4.right1_ref.cols1_ref) | copy-start | bytes 393220
  34.0 5.2 %copy-start.13 = (bf16[512,128]{1,0:T(8,128)(2,1)}, bf16[512,128]{1,0:T(8,128)(2,1)S(1)}, u32[]{:S(2)}) copy-start(bf16[512,128]{1,0:T(8,128)(2,1)S(1)} %collective-permute-done.3.right0_ref.cols0_ref) | copy-start | bytes 393220
  34.0 5.2 %copy-start.8 = (bf16[768,128]{1,0:T(8,128)(2,1)}, bf16[768,128]{1,0:T(8,128)(2,1)S(1)}, u32[]{:S(2)}) copy-start(bf16[768,128]{1,0:T(8,128)(2,1)S(1)} %collective-permute-done.left1_ref.side1_ref) | copy-start | bytes 589828
  34.1 5.2 %copy-start.9 = (bf16[768,128]{1,0:T(8,128)(2,1)}, bf16[768,128]{1,0:T(8,128)(2,1)S(1)}, u32[]{:S(2)}) copy-start(bf16[768,128]{1,0:T(8,128)(2,1)S(1)} %collective-permute-done.2.left3_ref.side3_ref) | copy-start | bytes 589828
  34.1 0.8 copy-start.14
  34.9 0.8 copy-start.16
  35.6 0.8 copy-start.18
  39.3 15.4 %collective-permute-start.7 = (f32[16,8,256]{2,1,0:T(8,128)S(1)}, f32[16,8,256]{2,1,0:T(8,128)S(1)}, u32[]{:S(2)}, u32[]{:S(2)}) collective-permute-start(f32[16,8,256]{2,1,0:T(8,128)S(1)} %shard_map.132.gwa_ref), channel_id=1, source_target_pairs={{0,16},{16,0},{1,17},{17,1},{2,18},{18,2},{3,19},{19,3},{4,20},{20... | collective-permute-start | bytes 393224 | tf_op jit(solution)/shard_map/ppermute | solution.py:661
  40.8 13.9 %copy-start.5 = (s32[256]{0:T(256)S(1)}, s32[256]{0:T(256)}, u32[]{:S(2)}) copy-start(s32[256]{0:T(256)} %param.13) | copy-start | bytes 3076
  40.8 25.5 %copy-start.20 = (f32[128,8]{0,1:T(8,128)S(1)}, f32[128,8]{0,1:T(8,128)}, u32[]{:S(2)}) copy-start(f32[128,8]{0,1:T(8,128)} %param.19) | copy-start | bytes 12292
  54.7 0.9 %copy-start.3 = (f32[16,8,256]{2,1,0:T(8,128)S(1)}, f32[16,8,256]{2,1,0:T(8,128)}, u32[]{:S(2)}) copy-start(f32[16,8,256]{2,1,0:T(8,128)} %get-tuple-element.19.logits_ref) | copy-start | bytes 393220
  56.1 8.5 %collective-permute-start.8 = (f32[10,8,128]{2,1,0:T(8,128)S(1)}, f32[10,8,128]{2,1,0:T(8,128)S(1)}, u32[]{:S(2)}, u32[]{:S(2)}) collective-permute-start(f32[10,8,128]{2,1,0:T(8,128)S(1)} %get-tuple-element.21), channel_id=1, source_target_pairs={{0,1},{1,2},{2,3},{3,0},{4,5},{5,6},{6,7},{7,4},{8,9},{9,10},{10,1... | collective-permute-start | bytes 122888 | tf_op jit(solution)/shard_map/ppermute | solution.py:716
  59.8 5.4 %collective-permute-start.9 = (f32[10,8,128]{2,1,0:T(8,128)S(1)}, f32[10,8,128]{2,1,0:T(8,128)S(1)}, u32[]{:S(2)}, u32[]{:S(2)}) collective-permute-start(f32[10,8,128]{2,1,0:T(8,128)S(1)} %get-tuple-element.22), channel_id=1, source_target_pairs={{0,2},{1,3},{2,0},{3,1},{4,6},{5,7},{6,4},{7,5},{8,10},{9,11},{10,... | collective-permute-start | bytes 122888 | tf_op jit(solution)/shard_map/ppermute | solution.py:716
  63.2 3.1 %collective-permute-start.10 = (f32[10,8,128]{2,1,0:T(8,128)S(1)}, f32[10,8,128]{2,1,0:T(8,128)S(1)}, u32[]{:S(2)}, u32[]{:S(2)}) collective-permute-start(f32[10,8,128]{2,1,0:T(8,128)S(1)} %get-tuple-element.23), channel_id=1, source_target_pairs={{0,3},{1,0},{2,1},{3,2},{4,7},{5,4},{6,5},{7,6},{8,11},{9,8},{10,9... | collective-permute-start | bytes 122888 | tf_op jit(solution)/shard_map/ppermute | solution.py:716
  66.3 0.9 %copy-start.4 = (f32[16,8,256]{2,1,0:T(8,128)S(1)}, f32[16,8,256]{2,1,0:T(8,128)}, u32[]{:S(2)}) copy-start(f32[16,8,256]{2,1,0:T(8,128)} %get-tuple-element.19.logits_ref) | copy-start | bytes 393220
  67.2 1.2 %copy-start.22 = (bf16[16,128,256]{2,1,0:T(8,128)(2,1)S(1)}, bf16[16,128,256]{2,1,0:T(8,128)(2,1)}, u32[]{:S(2)}) copy-start(bf16[16,128,256]{2,1,0:T(8,128)(2,1)} %get-tuple-element.28.pout_t_ref) | copy-start | bytes 3145732
  68.4 3.3 %copy-start = (bf16[256,128]{1,0:T(8,128)(2,1)S(1)}, bf16[256,128]{1,0:T(8,128)(2,1)}, u32[]{:S(2)}) copy-start(bf16[256,128]{1,0:T(8,128)(2,1)} %get-tuple-element.17.norm_ref) | copy-start | bytes 196612
  68.4 3.3 %copy-start.15 = (bf16[64,256]{1,0:T(8,128)(2,1)S(1)}, bf16[64,256]{1,0:T(8,128)(2,1)}, u32[]{:S(2)}) copy-start(bf16[64,256]{1,0:T(8,128)(2,1)} %wv_ref.3) | copy-start | bytes 98308
  68.4 3.3 %copy-start.17 = (bf16[64,256]{1,0:T(8,128)(2,1)S(1)}, bf16[64,256]{1,0:T(8,128)(2,1)}, u32[]{:S(2)}) copy-start(bf16[64,256]{1,0:T(8,128)(2,1)} %wg_ref.3) | copy-start | bytes 98308
  71.7 1.2 %copy-start.6 = (bf16[4096,128]{1,0:T(8,128)(2,1)S(1)}, bf16[4096,128]{1,0:T(8,128)(2,1)}, u32[]{:S(2)}) copy-start(bf16[4096,128]{1,0:T(8,128)(2,1)} %all-gather.4.cloned.1.call-done) | copy-start | bytes 3145732
  73.0 1.3 %copy-start.2 = (bf16[32,16,64]{2,1,0:T(8,128)(2,1)S(1)}, bf16[32,16,64]{2,1,0:T(8,128)(2,1)}, u32[]{:S(2)}) copy-start(bf16[32,16,64]{2,1,0:T(8,128)(2,1)} %x_ref.1) | copy-start | bytes 196612
  73.0 1.3 %copy-start.19 = (bf16[256,64]{0,1:T(8,128)(2,1)S(1)}, bf16[256,64]{0,1:T(8,128)(2,1)}, u32[]{:S(2)}) copy-start(bf16[256,64]{0,1:T(8,128)(2,1)} %param.20) | copy-start | bytes 98308
Sparse Core Ops, SparseCore 0:
  28.7 40.1 all-gather.3

commit v6 on v5

--- a/solution.py
+++ b/solution.py
@@ -9,7 +9,7 @@
 
 epsilon = 1e-05
 far_below = -1e30
-vmem_bytes = 48 * 1024 * 1024
+vmem_bytes = 32 * 1024 * 1024
 pack = 4
 
 f32 = jnp.float32
@@ -29,24 +29,45 @@
     return high, (x - high.astype(f32)).astype(bf16)
 
 
-def call(kernel, out_shape, scratch=(), smem=0, flops=0, nbytes=0, vmem=vmem_bytes, far=(), far_out=()):
-    count = None
-
+def call(
+    kernel, out_shape, scratch=(), smem=0, flops=0, nbytes=0, vmem=vmem_bytes, far=(), far_out=()
+):
     def run(*args):
-        specs = [pl.BlockSpec(memory_space=pltpu.SMEM)] * smem
-        specs += [pl.BlockSpec(memory_space=pltpu.VMEM)] * (len(args) - smem)
+        count = len(args)
+        in_specs = [
+            pl.BlockSpec(memory_space=pltpu.SMEM if n < smem else pltpu.VMEM) for n in range(count)
+        ]
+        for n in far:
+            in_specs[n] = pl.BlockSpec(memory_space=pltpu.HBM)
+        landing = [pltpu.VMEM(args[n].shape, args[n].dtype) for n in far]
+        if far:
+            landing.append(pltpu.SemaphoreType.DMA((len(far),)))
+
+        def body(*refs):
+            inputs = list(refs[:count])
+            extra = refs[len(refs) - len(landing) :]
+            rest = refs[count : len(refs) - len(landing)]
+            copies = []
+            for i, n in enumerate(far):
+                copies.append(pltpu.make_async_copy(inputs[n], extra[i], extra[-1].at[i]))
+                copies[-1].start()
+                inputs[n] = extra[i]
+
+            def ready():
+                for copy in copies:
+                    copy.wait()
+
+            kernel(ready, *inputs, *rest)
+
         return pl.pallas_call(
-            kernel,
+            body,
             out_shape=out_shape,
-            in_specs=[
-                pl.BlockSpec(memory_space=pl.ANY) if n in far else spec
-                for n, spec in enumerate(specs)
-            ],
+            in_specs=in_specs,
             out_specs=[
-                pl.BlockSpec(memory_space=pl.ANY if n in far_out else pltpu.VMEM)
+                pl.BlockSpec(memory_space=pltpu.HBM if n in far_out else pltpu.VMEM)
                 for n in range(len(out_shape))
             ],
-            scratch_shapes=list(scratch),
+            scratch_shapes=list(scratch) + landing,
             compiler_params=pltpu.CompilerParams(vmem_limit_bytes=vmem),
             cost_estimate=pl.CostEstimate(flops=flops, bytes_accessed=nbytes, transcendentals=0),
         )(*args)
@@ -72,7 +93,20 @@
 
 
 def prepare_kernel(
-    own_ref, x_ref, adj_ref, w1_ref, w2_ref, mask_ref, norm_ref, adj_out_ref, sides_ref, turn_ref, right_ref
+    ready,
+    own_ref,
+    x_ref,
+    adj_ref,
+    w1_ref,
+    w2_ref,
+    mask_ref,
+    rows_ref,
+    cols_ref,
+    left_ref,
+    right_ref,
+    norm_ref,
+    turn_ref,
+    place_ref,
 ):
     seqs, tokens, width = x_ref.shape
     half = seqs // 2
@@ -82,11 +116,17 @@
     inverse = lax.rsqrt(jnp.mean(center * center, axis=-1, keepdims=True) + epsilon)
     normed = center * inverse
     rows = half * tokens
-    packed = jnp.concatenate([normed[:half], normed[half:]], axis=-1)
-    norm_ref[...] = packed.reshape(rows, 2 * width).astype(bf16)
     adj = adj_ref[...].astype(f32)
-    packed = jnp.concatenate([adj[:half], adj[half:]], axis=-1)
-    adj_out_ref[...] = packed.reshape(rows, 2 * width).astype(bf16)
+
+    def two(x):
+        x = jnp.concatenate([x[:half], x[half:]], axis=-1)
+        return x.reshape(rows, 2 * width).astype(bf16)
+
+    packed = two(normed)
+    norm_ref[...] = packed
+    rows_ref[-2 * rows : -rows, :] = packed
+    rows_ref[-rows:, :] = two(adj)
+    cols_ref[-rows:, :] = packed
     token = lax.broadcasted_iota(jnp.int32, (seqs, tokens, width), 1) + own_ref[0]
     count = valid_count(mask_ref).reshape(1, 1, 1)
     real = jnp.where(token.astype(f32) < count, normed, 0.0)
@@ -97,7 +137,8 @@
     fc = w1_ref.shape[0]
     wk = pack * seqs
     for g in range(tokens // pack):
-        sides_ref[g * fc : (g + 1) * fc, :] = left[:, g * wk : (g + 1) * wk]
+        left_ref[g * fc : (g + 1) * fc, :] = left[:, g * wk : (g + 1) * wk]
+    rows_ref[: -2 * rows, :] = left_ref[...]
     size = 128 // tokens
     real = real.astype(bf16)
     w2 = w2_ref[...]
@@ -107,12 +148,14 @@
     for s in range(seqs):
         res = nt_dot(w2, jnp.concatenate([real[s]] * size, axis=0))
         res = jnp.where(mine, res, 0.0).reshape(fd // size, size, 128)
-        right_ref[:, s, :] = jnp.sum(res, axis=1)
-    base = tokens // pack * fc
-    sides_ref[base:, :] = right_ref[...].reshape(fd // size * seqs, 128).astype(bf16)
+        place_ref[:, s, :] = jnp.sum(res, axis=1)
+    right = place_ref[...].reshape(fd // size * seqs, 128).astype(bf16)
+    right_ref[...] = right
+    cols_ref[:-rows, :] = right
 
 
 def update_kernel(
+    ready,
     place_ref,
     left0_ref,
     left1_ref,
@@ -122,17 +165,22 @@
     right1_ref,
     right2_ref,
     right3_ref,
+    far_left0_ref,
+    far_left1_ref,
+    far_left2_ref,
+    far_left3_ref,
+    far_right0_ref,
+    far_right1_ref,
+    far_right2_ref,
+    far_right3_ref,
     mask_ref,
-    m_hbm,
+    m_ref,
     score_ref,
-    pair_hbm,
+    pair_ref,
     pout_hbm,
     pout_t_ref,
     logits_ref,
-    m_ref,
-    pair_ref,
     pout_ref,
-    in_sem,
     out_sem,
     rk_ref,
     rab_ref,
@@ -141,13 +189,9 @@
     oh_ref,
     ol_ref,
 ):
-    fetch_m = pltpu.make_async_copy(m_hbm, m_ref, in_sem.at[0])
-    fetch_pair = pltpu.make_async_copy(pair_hbm, pair_ref, in_sem.at[1])
-    fetch_m.start()
-    fetch_pair.start()
     nk = rk_ref.shape[0]
     width_d, pair_rows, _ = rab_ref.shape
-    row, col = place_ref[0], place_ref[1]
+    row, col, seq = place_ref[0], place_ref[1], place_ref[2]
     z = pair_ref.shape[1]
     groups, heads, lanes = logits_ref.shape
     tile_j = lanes // pack
@@ -157,10 +201,29 @@
     seqs = 128 // pack
     nq = pair_rows // seqs
     wk = pack * seqs
-    maskj = column_mask(mask_ref, col, tile_j, 2)
-
-    for t, ref in enumerate((right0_ref, right1_ref, right2_ref, right3_ref)):
-        rk_ref[lax.rem(row + nk - t, nk)] = ref[: rk_ref.shape[1], :]
+
+    rights = (right0_ref, right1_ref, right2_ref, right3_ref)
+    far_rights = (far_right0_ref, far_right1_ref, far_right2_ref, far_right3_ref)
+    lefts = (left0_ref, left1_ref, left2_ref, left3_ref)
+    far_lefts = (far_left0_ref, far_left1_ref, far_left2_ref, far_left3_ref)
+    r_rows = rk_ref.shape[1] // nq
+    l_rows = per_k * fc
+    if nq == 2:
+        sources = ((seq, 0, rights, lefts), (1 - seq, 0, far_rights, far_lefts))
+    else:
+        sources = tuple((q, q, far_rights, far_lefts) for q in range(nq))
+    for q, slot, from_rights, from_lefts in sources:
+        for t in range(nk):
+            at = pl.ds(pl.multiple_of(q * r_rows, r_rows), r_rows)
+            part = from_rights[t][slot * r_rows : (slot + 1) * r_rows, :]
+            rk_ref[lax.rem(row + nk - t, nk), at, :] = part
+            k = jnp.bitwise_xor(col, t)
+            at = pl.ds(pl.multiple_of(k * l_rows, l_rows), l_rows)
+            for g in range(per_k):
+                from_row = slot * l_rows + g * fc
+                at = pl.ds(pl.multiple_of((k * per_k + g) * fc, fc), fc)
+                to = pl.ds(pl.multiple_of(q * wk, wk), wk)
+                lm_ref[at, to] = from_lefts[t][from_row : from_row + fc, :]
     size = 128 // tokens
     right = jnp.concatenate([rk_ref[k] for k in range(nk)], axis=1)
     source = lax.broadcasted_iota(jnp.int32, (nk * 128, 4 * tile_j), 0)
@@ -177,15 +240,8 @@
                 at = (q * blocks + n) * seqs
                 rab_ref[n * size + e, q * seqs : (q + 1) * seqs, :] = res[at : at + seqs]
 
-    for t, ref in enumerate((left0_ref, left1_ref, left2_ref, left3_ref)):
-        k = jnp.bitwise_xor(col, t)
-        for g in range(per_k):
-            at = pl.ds(pl.multiple_of((k * per_k + g) * fc, fc), fc)
-            for q in range(nq):
-                from_row = (q * per_k + g) * fc
-                lm_ref[at, q * wk : (q + 1) * wk] = ref[from_row : from_row + fc, :]
-
     chunk = 4
+    many = 4
     empty = jnp.zeros((seqs, 2 * tile_j), bf16)
 
     def block_of(d):
@@ -200,12 +256,12 @@
         return jnp.concatenate(rows, axis=0)
 
     def outer_of(n, carry):
-        block = jnp.concatenate([block_of(2 * n), block_of(2 * n + 1)], axis=1)
+        block = jnp.concatenate([block_of(many * n + e) for e in range(many)], axis=1)
         for m in range(groups // chunk):
             out = nn_dot(lm_ref[m * chunk * fc : (m + 1) * chunk * fc, :], block)
             high, low = high_low(out)
-            for e in range(2):
-                at = pl.ds(pl.multiple_of((2 * n + e) * fc, fc), fc)
+            for e in range(many):
+                at = pl.ds(pl.multiple_of((many * n + e) * fc, fc), fc)
                 for g in range(chunk):
                     group = m * chunk + g
                     to = slice(group % 2 * lanes, (group % 2 + 1) * lanes)
@@ -214,9 +270,9 @@
                     ol_ref[group // 2, at, to] = low[cut]
         return carry
 
-    lax.fori_loop(0, width_d // 2, outer_of, 0, unroll=2)
-
-    fetch_m.wait()
+    lax.fori_loop(0, width_d // many, outer_of, 0)
+
+    ready()
     some = z // fc
     for n in range(width_d // some):
         block = jnp.concatenate(
@@ -225,7 +281,7 @@
         high, low = high_low(block)
         mt_ref[:z, n * z : (n + 1) * z] = high
         mt_ref[z:, n * z : (n + 1) * z] = low
-    fetch_pair.wait()
+    maskj = column_mask(mask_ref, col, tile_j, 2)
 
     maskl = jnp.concatenate([maskj] * pack, axis=1) > 0
     score = score_ref[...]
@@ -286,6 +342,7 @@
 
 
 def weights_kernel(
+    ready,
     place_ref,
     side0_ref,
     side1_ref,
@@ -319,6 +376,7 @@
     for t, ref in enumerate((cols0_ref, cols1_ref, cols2_ref, cols3_ref)):
         start = ref.shape[0] - count
         cols_ref[lax.rem(row + nk - t, nk)] = ref[start:, :].reshape(cols_ref.shape[1:])
+    ready()
     by_heads(wv_ref[...], heads, bv_ref)
     by_heads(wg_ref[...], heads, bg_ref)
     by_heads(wf_ref[...], heads, bf_ref)
@@ -366,6 +424,7 @@
 
 
 def softmax_kernel(
+    ready,
     col_ref,
     logits_ref,
     gwa_ref,
@@ -415,21 +474,23 @@
                 pay[2 + g * (pack // 2) + part] = piece[:, part * 2 * tile : (part + 1) * 2 * tile]
 
 
-def values_kernel(ev_ref, wv_ref, norm_ref, wg_ref, v_ref, gate_ref):
+def values_kernel(ready, ev_ref, wv_ref, norm_ref, wg_ref, v_ref, gate_ref):
     owners, half, tokens, wide = ev_ref.shape
     chans = wv_ref.shape[1]
+    gate = jax.nn.sigmoid(nn_dot(norm_ref[...], twice(wg_ref[...])))
+    gate_ref[: half * tokens] = gate[:, :chans]
+    gate_ref[half * tokens :] = gate[:, chans:]
     wv = twice(wv_ref[...])
+    ready()
     for s in range(half):
         x = jnp.concatenate([ev_ref[k, s] for k in range(owners)], axis=0)
         v = nn_dot(x, wv).astype(bf16)
         v_ref[s] = v[:, :chans]
         v_ref[s + half] = v[:, chans:]
-    gate = jax.nn.sigmoid(nn_dot(norm_ref[...], twice(wg_ref[...])))
-    gate_ref[: half * tokens] = gate[:, :chans]
-    gate_ref[half * tokens :] = gate[:, chans:]
 
 
 def gradient_kernel(
+    ready,
     own_ref, r1_ref, r2_ref, r3_ref, logits_ref, gw_ref, pout_t_ref, score_ref, out_ref, stat_ref
 ):
     groups, heads, lanes = logits_ref.shape
@@ -490,6 +551,7 @@
 
 
 def alignment_kernel(
+    ready,
     col_ref,
     own_ref,
     r1_ref,
@@ -581,18 +643,22 @@
 
     mask = token_valid_mask.reshape(1, -1)
     own_start = ((row_index * nk + col_index) * tokens).astype(jnp.int32).reshape(1)
-    place = jnp.stack([row_index, col_index]).astype(jnp.int32)
+    seq_index = lax.axis_index("seq")
+    place = jnp.stack([row_index, col_index, seq_index]).astype(jnp.int32)
     col_scalar = col_index.astype(jnp.int32).reshape(1)
     half = seqs // 2
 
-    sides_left = tokens // pack * fc
-    sides_rows = sides_left + fd * tokens // 128 * seqs
-    normed, adjoint, sides = call(
+    l_rows = tokens // pack * fc
+    r_rows = fd * tokens // 128 * seqs
+    n_rows = half * tokens
+    rows, cols, left, right, normed = call(
         prepare_kernel,
         (
-            sds((half * tokens, 2 * width), bf16),
-            sds((half * tokens, 2 * width), bf16),
-            sds((sides_rows, 128), bf16),
+            sds((l_rows + 2 * n_rows, 128), bf16),
+            sds((r_rows + n_rows, 128), bf16),
+            sds((l_rows, 128), bf16),
+            sds((r_rows, 128), bf16),
+            sds((n_rows, 128), bf16),
         ),
         scratch=(
             pltpu.VMEM((tokens, seqs, width), f32),
@@ -612,25 +678,35 @@
     every = lax.all_gather(normed, ("row", "col"), axis=0).reshape(
         nr * nk, half, tokens, 2 * width
     )
-    sides = lax.all_gather(sides, "seq", axis=0)
-    rights = sides[:, sides_left:].reshape(nq * (sides_rows - sides_left), 128)
-    rights = jnp.concatenate([rights, normed], axis=0)
-    all_rights = [
-        lax.ppermute(
-            rights,
-            ("row", "col"),
-            [(r * nk + c, (c + t) % nr * nk + r) for r in range(nr) for c in range(nk)],
-        )
-        for t in range(nr)
-    ]
-    lefts = sides[:, :sides_left].reshape(nq * sides_left, 128)
-    lefts = jnp.concatenate([lefts, normed, adjoint], axis=0)
-
-    def exchange(x, bit):
-        return lax.ppermute(x, "col", [(c, c ^ bit) for c in range(nk)])
-
-    across = exchange(lefts, 2)
-    all_lefts = [lefts, exchange(lefts, 1), across, exchange(across, 1)]
+    def to_columns(x, t, flip):
+        pairs = [
+            ((s * nr + r) * nk + c, ((s ^ flip) * nr + (c + t) % nr) * nk + r)
+            for s in range(nq)
+            for r in range(nr)
+            for c in range(nk)
+        ]
+        return lax.ppermute(x, ("seq", "row", "col"), pairs)
+
+    def to_rows(x, t, flip):
+        pairs = [
+            ((s * nr + r) * nk + c, ((s ^ flip) * nr + r) * nk + (c ^ t))
+            for s in range(nq)
+            for r in range(nr)
+            for c in range(nk)
+        ]
+        return lax.ppermute(x, ("seq", "row", "col"), pairs)
+
+    all_cols = [to_columns(cols, t, 0) for t in range(nr)]
+    across = to_rows(rows, 2, 0)
+    all_rows = [rows, to_rows(rows, 1, 0), across, to_rows(across, 1, 0)]
+    if nq == 2:
+        far_rights = [to_columns(right, t, 1) for t in range(nr)]
+        far_lefts = [to_rows(left, t, 1) for t in range(nk)]
+    else:
+        right = lax.all_gather(right, "seq", axis=0, tiled=True)
+        left = lax.all_gather(left, "seq", axis=0, tiled=True)
+        far_rights = [to_columns(right, t, 0) for t in range(nr)]
+        far_lefts = [left] + [to_rows(left, t, 0) for t in range(1, nk)]
 
     head_lanes = seqs * chans // heads
     (gw_own,) = call(
@@ -649,10 +725,11 @@
         smem=1,
         flops=3_000_000_000,
         nbytes=3_000_000,
+        far=(9, 10, 11),
     )(
         place,
-        *all_lefts,
-        *all_rights,
+        *all_rows,
+        *all_cols,
         content_weights_grid,
         sigmoid_weights_grid,
         final_mixing_weights.T,
@@ -670,12 +747,9 @@
             sds((groups, heads, lanes), f32),
         ),
         scratch=(
-            pltpu.VMEM((fc * fd, z), f32),
             pltpu.VMEM((tile_i * tile_j, z), bf16),
-            pltpu.VMEM((tile_i * tile_j, z), bf16),
-            pltpu.SemaphoreType.DMA((2,)),
             pltpu.SemaphoreType.DMA((groups // 2,)),
-            pltpu.VMEM((nk, nq * (sides_rows - sides_left), 128), bf16),
+            pltpu.VMEM((nk, nq * r_rows, 128), bf16),
             pltpu.VMEM((fd, nq * seqs, 4 * tile_j), bf16),
             pltpu.VMEM((groups * fc, nq * pack * seqs), bf16),
             pltpu.VMEM((2 * z, fd * fc), bf16),
@@ -685,13 +759,15 @@
         smem=1,
         flops=14_000_000_000,
         nbytes=5_000_000,
-        vmem=60 * 1024 * 1024,
-        far=(10, 12),
+        vmem=44 * 1024 * 1024,
+        far=(17, 18, 19, 20),
         far_out=(0,),
     )(
         place,
-        *all_lefts,
-        *all_rights,
+        *all_rows,
+        *all_cols,
+        *far_lefts,
+        *far_rights,
         mask,
         outer_matrix,
         score_matrix.T,
@@ -703,6 +779,7 @@
         (sds((seqs, nr * nk * tokens, chans), bf16), sds((seqs * tokens, chans), f32)),
         flops=4_000_000_000,
         nbytes=6_000_000,
+        far=(0,),
     )(every, content_weights_grid, normed, sigmoid_weights_grid)
 
     payload = sds((2 + groups // nk * (pack // 2), heads, 2 * tile_j), f32)
@@ -716,6 +793,8 @@
         lax.ppermute(pay, "col", [(c, (c + shift) % nk) for c in range(nk)])
         for shift, pay in ((1, pay1), (2, pay2), (3, pay3))
     ]
+
+    got, values, gating = lax.optimization_barrier((got, values, gating))
 
     (gradient,) = call(
         gradient_kernel,

time: 85.2 us -> 82 us (0.962)
  starting transfers between devices: 19.3 us -> 29.5 us
  blocking collectives: 6.1 us -> 0 us
  local copies, waits for them, and re-layouts: 6.63 us -> 4.46 us
  waiting for transfers between devices: 8.54 us -> 6.49 us
  other arithmetic: 1.81 us -> 0.08 us
  Pallas kernels: 27.7 us -> 26.6 us
    ppermute x7 -> x15, starting transfers between devices: 9.19 us -> 26.5 us  [the longest x8 16.8 us: to_columns(): return lax.ppermute(x, ('seq', 'row', 'col'), pairs)]
    all_gather x1 -> x0, blocking collectives: 6.1 us -> none  [on_device(): sides = lax.all_gather(sides, 'seq', axis=0)]
    ppermute x3, starting transfers between devices: 8.51 us -> 2.61 us  [on_device(): lax.ppermute(pay, 'col', [(c, (c + shift) % nk) for c in range(nk)])]
    unnamed x46 -> x30, local copies, waits for them, and re-layouts: 6.62 us -> 4.46 us
    concatenate x2 -> x0, other arithmetic: 1.74 us -> none  [the longest x1 0.89 us: on_device(): lefts = jnp.concatenate([lefts, normed, adjoint], axis=0)]
    ppermute x3, waiting for transfers between devices: 1.67 us -> 0.01 us  [on_device(): lax.ppermute(pay, 'col', [(c, (c + shift) % nk) for c in range(nk)])]
    ppermute x1, starting transfers between devices: 1.54 us -> 0.37 us  [on_device(): gw_other = lax.ppermute(gw_own, 'seq', [(0, 1), (1, 0)])]
    pallas_call x7, Pallas kernels: 27.7 us -> 26.6 us  [run(): pl.pallas_call(body, out_shape=out_shape, in_specs=in_specs, out_specs=[p...]
  transfers between devices with their start and end apart: 12 -> 20, of which waited for: 5 -> 4; matrix products, arithmetic and copies ran while one was open for 1% -> 0% of each run, Pallas kernels for 24% -> 21%
where the time goes in v6:
time: 82 us; the launch traced here: 81.4 us
  starting transfers between devices  29.5 us (36%)
  Pallas kernels  26.6 us (32%)
  between operations  14.2 us (17%)
  waiting for transfers between devices  6.49 us (8%)
  local copies, waits for them, and re-layouts  4.46 us (5%)
    pallas_call x7, Pallas kernels, run(): pl.pallas_call(body, out_shape=out_shape, in_specs=in_specs, out_specs=[p...  26.6 us
    ppermute x8, starting transfers between devices, to_columns(): return lax.ppermute(x, ('seq', 'row', 'col'), pairs)  16.8 us
    ppermute x7, starting transfers between devices, to_rows(): return lax.ppermute(x, ('seq', 'row', 'col'), pairs)  9.68 us
    unnamed x30, local copies, waits for them, and re-layouts  4.46 us
    ppermute x7, waiting for transfers between devices, to_rows(): return lax.ppermute(x, ('seq', 'row', 'col'), pairs)  3.67 us
    ppermute x8, waiting for transfers between devices, to_columns(): return lax.ppermute(x, ('seq', 'row', 'col'), pairs)  2.79 us
    ppermute x3, starting transfers between devices, on_device(): lax.ppermute(pay, 'col', [(c, (c + shift) % nk) for c in range(nk)])  2.61 us
  transfers between devices with their start and end apart: 20, of which 4 were waited for; matrix products, arithmetic and copies ran while one was open for 0% of the time, Pallas kernels for 21%

profile of v6, /device:TPU:0, one launch (start us, length us, event | category | flops | bytes accessed | tf_op | source)
XLA Modules:
  0.0 81.4 jit_solution(2477850930360738760)
XLA Ops:
  7.2 0.0 all-gather.3.cloned.1.call-start
  7.2 2.8 %shard_map.130 = (bf16[640,128]{1,0:T(8,128)(2,1)}, bf16[384,128]{1,0:T(8,128)(2,1)}, bf16[128,128]{1,0:T(8,128)(2,1)}, bf16[128,128]{1,0:T(8,128)(2,1)}, bf16[256,128]{1,0:T(8,128)(2,1)}) custom-call(s32[1]{0:T(128)} %bitcast.3.refs_0_, bf16[32,16,64]{2,1,0:T(8,128)(2,1)} %refs_1_.2, bf16[32,16,64]{2,1,0:T(8,128)(2,1)} %refs_2_.1, bf16[32,64]{1,0:T(8,128)(2,1)} %bitcast.25, ...), custom_call_target="tpu_custom_call" | custom-call | tf_op jit(solution)/shard_map/pallas_call | solution.py:62
  10.1 0.0 all-gather.3.cloned.1.call-update
  10.1 3.0 %collective-permute-start.1 = (bf16[640,128]{1,0:T(8,128)(2,1)}, bf16[640,128]{1,0:T(8,128)(2,1)S(1)}, u32[]{:S(2)}, u32[]{:S(2)}) collective-permute-start(bf16[640,128]{1,0:T(8,128)(2,1)} %get-tuple-element.23.refs_1_), channel_id=1, source_target_pairs={{0,2},{1,3},{2,0},{3,1},{4,6},{5,7},{6,4},{7,5},{8,10},{9,11},{10,... | collective-permute-start | bytes 491528 | tf_op jit(solution)/shard_map/ppermute | solution.py:697
  13.1 3.6 %collective-permute-start.6 = (bf16[384,128]{1,0:T(8,128)(2,1)}, bf16[384,128]{1,0:T(8,128)(2,1)S(1)}, u32[]{:S(2)}, u32[]{:S(2)}) collective-permute-start(bf16[384,128]{1,0:T(8,128)(2,1)} %get-tuple-element.24), channel_id=1, source_target_pairs={{0,12},{1,0},{2,4},{3,8},{4,13},{5,1},{6,5},{7,9},{8,14},{9,2},{10... | collective-permute-start | bytes 294920 | tf_op jit(solution)/shard_map/ppermute | solution.py:688
  16.7 1.1 %collective-permute-start.10 = (bf16[128,128]{1,0:T(8,128)(2,1)}, bf16[128,128]{1,0:T(8,128)(2,1)S(1)}, u32[]{:S(2)}, u32[]{:S(2)}) collective-permute-start(bf16[128,128]{1,0:T(8,128)(2,1)} %get-tuple-element.25), channel_id=1, source_target_pairs={{0,19},{1,18},{2,17},{3,16},{4,23},{5,22},{6,21},{7,20},{8,27},{9,... | collective-permute-start | bytes 98312 | tf_op jit(solution)/shard_map/ppermute | solution.py:697
  17.8 0.0 collective-permute-start
  17.8 1.6 %collective-permute-done.1.refs_3_ = bf16[640,128]{1,0:T(8,128)(2,1)S(1)} collective-permute-done((bf16[640,128]{1,0:T(8,128)(2,1)}, bf16[640,128]{1,0:T(8,128)(2,1)S(1)}, u32[]{:S(2)}, u32[]{:S(2)}) %collective-permute-start.1) | collective-permute-done | bytes 163872 | tf_op jit(solution)/shard_map/ppermute | solution.py:697
  19.4 0.0 collective-permute-start.2
  19.4 3.6 %collective-permute-start.9 = (bf16[128,128]{1,0:T(8,128)(2,1)}, bf16[128,128]{1,0:T(8,128)(2,1)S(1)}, u32[]{:S(2)}, u32[]{:S(2)}) collective-permute-start(bf16[128,128]{1,0:T(8,128)(2,1)} %get-tuple-element.25), channel_id=1, source_target_pairs={{0,18},{1,19},{2,16},{3,17},{4,22},{5,23},{6,20},{7,21},{8,26},{9,... | collective-permute-start | bytes 98312 | tf_op jit(solution)/shard_map/ppermute | solution.py:697
  23.0 0.0 collective-permute-done.10.refs_12_
  23.0 0.4 collective-permute-start.8
  23.4 2.1 %collective-permute-done.9.refs_11_ = bf16[128,128]{1,0:T(8,128)(2,1)S(1)} collective-permute-done((bf16[128,128]{1,0:T(8,128)(2,1)}, bf16[128,128]{1,0:T(8,128)(2,1)S(1)}, u32[]{:S(2)}, u32[]{:S(2)}) %collective-permute-start.9) | collective-permute-done | bytes 32800 | tf_op jit(solution)/shard_map/ppermute | solution.py:697
  25.5 2.7 %collective-permute-start.5 = (bf16[384,128]{1,0:T(8,128)(2,1)}, bf16[384,128]{1,0:T(8,128)(2,1)S(1)}, u32[]{:S(2)}, u32[]{:S(2)}) collective-permute-start(bf16[384,128]{1,0:T(8,128)(2,1)} %get-tuple-element.24), channel_id=1, source_target_pairs={{0,8},{1,12},{2,0},{3,4},{4,9},{5,13},{6,1},{7,5},{8,10},{9,14},{1... | collective-permute-start | bytes 294920 | tf_op jit(solution)/shard_map/ppermute | solution.py:688
  28.2 0.0 collective-permute-done.8.refs_10_
  28.2 0.0 collective-permute-start.4
  28.2 0.0 collective-permute-done.6.refs_8_
  28.2 1.6 %collective-permute-start.3 = (bf16[384,128]{1,0:T(8,128)(2,1)}, bf16[384,128]{1,0:T(8,128)(2,1)S(1)}, u32[]{:S(2)}, u32[]{:S(2)}) collective-permute-start(bf16[384,128]{1,0:T(8,128)(2,1)} %get-tuple-element.24), channel_id=1, source_target_pairs={{0,0},{1,4},{2,8},{3,12},{4,1},{5,5},{6,9},{7,13},{8,2},{9,6},{10,... | collective-permute-start | bytes 294920 | tf_op jit(solution)/shard_map/ppermute | solution.py:688
  29.7 0.1 pad_add_fusion.refs_0_
  29.8 2.3 %collective-permute-done.5.refs_7_ = bf16[384,128]{1,0:T(8,128)(2,1)S(1)} collective-permute-done((bf16[384,128]{1,0:T(8,128)(2,1)}, bf16[384,128]{1,0:T(8,128)(2,1)S(1)}, u32[]{:S(2)}, u32[]{:S(2)}) %collective-permute-start.5) | collective-permute-done | bytes 98336 | tf_op jit(solution)/shard_map/ppermute | solution.py:688
  32.1 1.6 %collective-permute-start.7 = (bf16[128,128]{1,0:T(8,128)(2,1)}, bf16[128,128]{1,0:T(8,128)(2,1)S(1)}, u32[]{:S(2)}, u32[]{:S(2)}) collective-permute-start(bf16[128,128]{1,0:T(8,128)(2,1)} %get-tuple-element.25), channel_id=1, source_target_pairs={{0,16},{1,17},{2,18},{3,19},{4,20},{5,21},{6,22},{7,23},{8,24},{9,... | collective-permute-start | bytes 98312 | tf_op jit(solution)/shard_map/ppermute | solution.py:697
  33.6 0.5 collective-permute-done.4.refs_6_
  34.2 3.0 %collective-permute-start.14 = (bf16[128,128]{1,0:T(8,128)(2,1)}, bf16[128,128]{1,0:T(8,128)(2,1)S(1)}, u32[]{:S(2)}, u32[]{:S(2)}) collective-permute-start(bf16[128,128]{1,0:T(8,128)(2,1)} %get-tuple-element.26), channel_id=1, source_target_pairs={{0,28},{1,16},{2,20},{3,24},{4,29},{5,17},{6,21},{7,25},{8,30},{9,... | collective-permute-start | bytes 98312 | tf_op jit(solution)/shard_map/ppermute | solution.py:688
  37.1 0.0 collective-permute-done.3.refs_5_
  37.1 2.7 %collective-permute-start.13 = (bf16[128,128]{1,0:T(8,128)(2,1)}, bf16[128,128]{1,0:T(8,128)(2,1)S(1)}, u32[]{:S(2)}, u32[]{:S(2)}) collective-permute-start(bf16[128,128]{1,0:T(8,128)(2,1)} %get-tuple-element.26), channel_id=1, source_target_pairs={{0,24},{1,28},{2,16},{3,20},{4,25},{5,29},{6,17},{7,21},{8,26},{9,... | collective-permute-start | bytes 98312 | tf_op jit(solution)/shard_map/ppermute | solution.py:688
  39.9 0.0 collective-permute-done.refs_2_
  39.9 1.5 %collective-permute-start.12 = (bf16[128,128]{1,0:T(8,128)(2,1)}, bf16[128,128]{1,0:T(8,128)(2,1)S(1)}, u32[]{:S(2)}, u32[]{:S(2)}) collective-permute-start(bf16[128,128]{1,0:T(8,128)(2,1)} %get-tuple-element.26), channel_id=1, source_target_pairs={{0,20},{1,24},{2,28},{3,16},{4,21},{5,25},{6,29},{7,17},{8,22},{9,... | collective-permute-start | bytes 98312 | tf_op jit(solution)/shard_map/ppermute | solution.py:688
  41.4 0.0 collective-permute-done.2.refs_4_
  41.4 1.7 %collective-permute-start.11 = (bf16[128,128]{1,0:T(8,128)(2,1)}, bf16[128,128]{1,0:T(8,128)(2,1)S(1)}, u32[]{:S(2)}, u32[]{:S(2)}) collective-permute-start(bf16[128,128]{1,0:T(8,128)(2,1)} %get-tuple-element.26), channel_id=1, source_target_pairs={{0,16},{1,20},{2,24},{3,28},{4,17},{5,21},{6,25},{7,29},{8,18},{9,... | collective-permute-start | bytes 98312 | tf_op jit(solution)/shard_map/ppermute | solution.py:688
  43.1 0.9 %copy-done.6 = bf16[640,128]{1,0:T(8,128)(2,1)S(1)} copy-done((bf16[640,128]{1,0:T(8,128)(2,1)S(1)}, bf16[640,128]{1,0:T(8,128)(2,1)}, u32[]{:S(2)}) %copy-start.6) | copy-done | bytes 163864
  44.0 0.8 copy-done.8
  44.8 0.8 copy-done.10
  45.5 0.8 copy-done.12
  46.3 0.0 copy-start.14
  46.3 3.0 %shard_map.132.refs_2_ = f32[16,8,256]{2,1,0:T(8,128)S(1)} custom-call(s32[3]{0:T(128)S(1)} %pad_add_fusion.refs_0_, bf16[640,128]{1,0:T(8,128)(2,1)S(1)} %copy-done.6, bf16[640,128]{1,0:T(8,128)(2,1)S(1)} %collective-permute-done.refs_2_, bf16[640,128]{1,0:T(8,128)(2,1)S(1)} %collective-permute-done.1.refs_3_, ...), custom_call_target="tpu_custom_call" | custom-call | flops 3000000000 | bytes 3000000 | tf_op jit(solution)/shard_map/pallas_call | solution.py:62
  49.3 0.0 collective-permute-done.7.refs_9_
  49.3 0.4 collective-permute-start.15
  49.7 0.0 collective-permute-done.14.refs_16_
  49.7 0.0 collective-permute-done.13.refs_15_
  49.7 0.0 collective-permute-done.12.refs_14_
  49.7 0.0 collective-permute-done.11.refs_13_
  49.7 0.0 copy-done.2
  49.7 0.0 copy-done.3
  49.7 0.0 copy-done.5
  49.7 0.0 copy-done.7
  49.7 0.0 copy-done.14
  49.8 0.0 copy-start.9
  49.8 0.0 copy-start.11
  49.8 12.3 %shard_map.131 = (bf16[4096,128]{1,0:T(8,128)(2,1)}, bf16[16,128,256]{2,1,0:T(8,128)(2,1)S(1)}, f32[16,8,256]{2,1,0:T(8,128)S(1)}) custom-call(s32[3]{0:T(128)S(1)} %pad_add_fusion.refs_0_, bf16[640,128]{1,0:T(8,128)(2,1)S(1)} %copy-done.7, bf16[640,128]{1,0:T(8,128)(2,1)S(1)} %collective-permute-done.refs_2_, ...), custom_call_target="tpu_custom_call" | custom-call | flops 14000000000 | bytes 5000000 | tf_op jit(solution)/shard_map/pallas_call | solution.py:62
  62.1 0.0 collective-permute-done.15.refs_3_
  62.1 0.5 shard_map.133
  62.6 0.0 collective-permute-start.16
  62.6 2.6 %collective-permute-start.17 = (f32[10,8,128]{2,1,0:T(8,128)S(1)}, f32[10,8,128]{2,1,0:T(8,128)S(1)}, u32[]{:S(2)}, u32[]{:S(2)}) collective-permute-start(f32[10,8,128]{2,1,0:T(8,128)S(1)} %get-tuple-element.30), channel_id=1, source_target_pairs={{0,2},{1,3},{2,0},{3,1},{4,6},{5,7},{6,4},{7,5},{8,10},{9,11},{10,... | collective-permute-start | bytes 122888 | tf_op jit(solution)/shard_map/ppermute | solution.py:793
  65.2 0.0 collective-permute-start.18
  65.2 0.0 copy-done.1
  65.2 1.2 %copy-done.4 = bf16[4096,128]{1,0:T(8,128)(2,1)S(1)} copy-done((bf16[4096,128]{1,0:T(8,128)(2,1)S(1)}, bf16[4096,128]{1,0:T(8,128)(2,1)}, u32[]{:S(2)}) %copy-start.4) | copy-done | bytes 1048600
  66.4 1.5 %shard_map.134 = (bf16[32,256,256]{2,1,0:T(8,128)(2,1)S(1)}, f32[512,256]{1,0:T(8,128)S(1)}) custom-call(bf16[16,16,16,128]{3,2,1,0:T(8,128)(2,1)S(1)} %bitcast.20, bf16[64,256]{1,0:T(8,128)(2,1)S(1)} %copy-done.9, bf16[256,128]{1,0:T(8,128)(2,1)S(1)} %copy-done.1, bf16[64,256]{1,0:T(8,128)(2,1)S(1)} %copy-done.11), custom_call_target="tpu_custom_call" | custom-call | flops 4000000000 | bytes 6000000 | tf_op jit(solution)/shard_map/pallas_call | solution.py:62
  68.0 0.0 collective-permute-done.16.refs_2_.refs_1_
  68.0 0.0 collective-permute-done.17.refs_3_.refs_2_
  68.0 0.0 collective-permute-done.18.refs_4_.refs_3_
  68.0 0.0 copy-start
  68.0 0.0 copy-start.13
  68.0 3.3 %shard_map.136 = bf16[4096,128]{1,0:T(8,128)(2,1)} custom-call(f32[10,8,128]{2,1,0:T(8,128)S(1)} %get-tuple-element.28.refs_1_.refs_0_, f32[10,8,128]{2,1,0:T(8,128)S(1)} %collective-permute-done.16.refs_2_.refs_1_, f32[10,8,128]{2,1,0:T(8,128)S(1)} %collective-permute-done.17.refs_3_.refs_2_, f32[10,8,128]{2,1,0:T(8,128)S(1)} %collective-permute-done.18.refs_4_.refs_3_, ...), custom_call_target="tpu_custom_call" | custom-call | flops 4000000000 | bytes 3000000 | tf_op jit(solution)/shard_map/pallas_call | solution.py:62
  71.3 3.2 %shard_map.135 = bf16[512,64]{1,0:T(8,128)(2,1)} custom-call(s32[1]{0:T(128)} %bitcast.refs_0_, f32[10,8,128]{2,1,0:T(8,128)S(1)} %get-tuple-element.28.refs_1_.refs_0_, f32[10,8,128]{2,1,0:T(8,128)S(1)} %collective-permute-done.16.refs_2_.refs_1_, f32[10,8,128]{2,1,0:T(8,128)S(1)} %collective-permute-done.17.refs_3_.refs_2_, ...), custom_call_target="tpu_custom_call" | custom-call | flops 3000000000 | bytes 5000000 | tf_op jit(solution)/shard_map/pallas_call | solution.py:62
  (15 shorter events, 0.0 us)
Async XLA Ops:
  7.2 58.0 %all-gather.3.cloned.1.call-start = ((), (), s32[]{:S(2)}) async-start(), calls=%async_computation | async-start | bytes 1114112 | tf_op jit(solution)/shard_map/all_gather | solution.py:678
  10.1 9.3 %collective-permute-start.1 = (bf16[640,128]{1,0:T(8,128)(2,1)}, bf16[640,128]{1,0:T(8,128)(2,1)S(1)}, u32[]{:S(2)}, u32[]{:S(2)}) collective-permute-start(bf16[640,128]{1,0:T(8,128)(2,1)} %get-tuple-element.23.refs_1_), channel_id=1, source_target_pairs={{0,2},{1,3},{2,0},{3,1},{4,6},{5,7},{6,4},{7,5},{8,10},{9,11},{10,... | collective-permute-start | bytes 491528 | tf_op jit(solution)/shard_map/ppermute | solution.py:697
  13.1 15.1 %collective-permute-start.6 = (bf16[384,128]{1,0:T(8,128)(2,1)}, bf16[384,128]{1,0:T(8,128)(2,1)S(1)}, u32[]{:S(2)}, u32[]{:S(2)}) collective-permute-start(bf16[384,128]{1,0:T(8,128)(2,1)} %get-tuple-element.24), channel_id=1, source_target_pairs={{0,12},{1,0},{2,4},{3,8},{4,13},{5,1},{6,5},{7,9},{8,14},{9,2},{10... | collective-permute-start | bytes 294920 | tf_op jit(solution)/shard_map/ppermute | solution.py:688
  16.7 6.3 %collective-permute-start.10 = (bf16[128,128]{1,0:T(8,128)(2,1)}, bf16[128,128]{1,0:T(8,128)(2,1)S(1)}, u32[]{:S(2)}, u32[]{:S(2)}) collective-permute-start(bf16[128,128]{1,0:T(8,128)(2,1)} %get-tuple-element.25), channel_id=1, source_target_pairs={{0,19},{1,18},{2,17},{3,16},{4,23},{5,22},{6,21},{7,20},{8,27},{9,... | collective-permute-start | bytes 98312 | tf_op jit(solution)/shard_map/ppermute | solution.py:697
  17.8 22.1 %collective-permute-start = (bf16[640,128]{1,0:T(8,128)(2,1)}, bf16[640,128]{1,0:T(8,128)(2,1)S(1)}, u32[]{:S(2)}, u32[]{:S(2)}) collective-permute-start(bf16[640,128]{1,0:T(8,128)(2,1)} %get-tuple-element.23.refs_1_), channel_id=1, source_target_pairs={{0,1},{1,0},{2,3},{3,2},{4,5},{5,4},{6,7},{7,6},{8,9},{9,8},{10,11... | collective-permute-start | bytes 491528 | tf_op jit(solution)/shard_map/ppermute | solution.py:697
  19.4 22.0 %collective-permute-start.2 = (bf16[640,128]{1,0:T(8,128)(2,1)S(1)}, bf16[640,128]{1,0:T(8,128)(2,1)S(1)}, u32[]{:S(2)}, u32[]{:S(2)}) collective-permute-start(bf16[640,128]{1,0:T(8,128)(2,1)S(1)} %collective-permute-done.1.refs_3_), channel_id=1, source_target_pairs={{0,1},{1,0},{2,3},{3,2},{4,5},{5,4},{6,7},{7,6},{8,9},{9,8},{10,11... | collective-permute-start | bytes 491528 | tf_op jit(solution)/shard_map/ppermute | solution.py:697
  19.4 6.1 %collective-permute-start.9 = (bf16[128,128]{1,0:T(8,128)(2,1)}, bf16[128,128]{1,0:T(8,128)(2,1)S(1)}, u32[]{:S(2)}, u32[]{:S(2)}) collective-permute-start(bf16[128,128]{1,0:T(8,128)(2,1)} %get-tuple-element.25), channel_id=1, source_target_pairs={{0,18},{1,19},{2,16},{3,17},{4,22},{5,23},{6,20},{7,21},{8,26},{9,... | collective-permute-start | bytes 98312 | tf_op jit(solution)/shard_map/ppermute | solution.py:697
  23.0 5.2 %collective-permute-start.8 = (bf16[128,128]{1,0:T(8,128)(2,1)}, bf16[128,128]{1,0:T(8,128)(2,1)S(1)}, u32[]{:S(2)}, u32[]{:S(2)}) collective-permute-start(bf16[128,128]{1,0:T(8,128)(2,1)} %get-tuple-element.25), channel_id=1, source_target_pairs={{0,17},{1,16},{2,19},{3,18},{4,21},{5,20},{6,23},{7,22},{8,25},{9,... | collective-permute-start | bytes 98312 | tf_op jit(solution)/shard_map/ppermute | solution.py:697
  25.5 6.6 %collective-permute-start.5 = (bf16[384,128]{1,0:T(8,128)(2,1)}, bf16[384,128]{1,0:T(8,128)(2,1)S(1)}, u32[]{:S(2)}, u32[]{:S(2)}) collective-permute-start(bf16[384,128]{1,0:T(8,128)(2,1)} %get-tuple-element.24), channel_id=1, source_target_pairs={{0,8},{1,12},{2,0},{3,4},{4,9},{5,13},{6,1},{7,5},{8,10},{9,14},{1... | collective-permute-start | bytes 294920 | tf_op jit(solution)/shard_map/ppermute | solution.py:688
  28.2 6.0 %collective-permute-start.4 = (bf16[384,128]{1,0:T(8,128)(2,1)}, bf16[384,128]{1,0:T(8,128)(2,1)S(1)}, u32[]{:S(2)}, u32[]{:S(2)}) collective-permute-start(bf16[384,128]{1,0:T(8,128)(2,1)} %get-tuple-element.24), channel_id=1, source_target_pairs={{0,4},{1,8},{2,12},{3,0},{4,5},{5,9},{6,13},{7,1},{8,6},{9,10},{10... | collective-permute-start | bytes 294920 | tf_op jit(solution)/shard_map/ppermute | solution.py:688
  28.2 8.9 %collective-permute-start.3 = (bf16[384,128]{1,0:T(8,128)(2,1)}, bf16[384,128]{1,0:T(8,128)(2,1)S(1)}, u32[]{:S(2)}, u32[]{:S(2)}) collective-permute-start(bf16[384,128]{1,0:T(8,128)(2,1)} %get-tuple-element.24), channel_id=1, source_target_pairs={{0,0},{1,4},{2,8},{3,12},{4,1},{5,5},{6,9},{7,13},{8,2},{9,6},{10,... | collective-permute-start | bytes 294920 | tf_op jit(solution)/shard_map/ppermute | solution.py:688
  32.1 17.2 %collective-permute-start.7 = (bf16[128,128]{1,0:T(8,128)(2,1)}, bf16[128,128]{1,0:T(8,128)(2,1)S(1)}, u32[]{:S(2)}, u32[]{:S(2)}) collective-permute-start(bf16[128,128]{1,0:T(8,128)(2,1)} %get-tuple-element.25), channel_id=1, source_target_pairs={{0,16},{1,17},{2,18},{3,19},{4,20},{5,21},{6,22},{7,23},{8,24},{9,... | collective-permute-start | bytes 98312 | tf_op jit(solution)/shard_map/ppermute | solution.py:697
  34.2 15.5 %collective-permute-start.14 = (bf16[128,128]{1,0:T(8,128)(2,1)}, bf16[128,128]{1,0:T(8,128)(2,1)S(1)}, u32[]{:S(2)}, u32[]{:S(2)}) collective-permute-start(bf16[128,128]{1,0:T(8,128)(2,1)} %get-tuple-element.26), channel_id=1, source_target_pairs={{0,28},{1,16},{2,20},{3,24},{4,29},{5,17},{6,21},{7,25},{8,30},{9,... | collective-permute-start | bytes 98312 | tf_op jit(solution)/shard_map/ppermute | solution.py:688
  37.1 12.6 %collective-permute-start.13 = (bf16[128,128]{1,0:T(8,128)(2,1)}, bf16[128,128]{1,0:T(8,128)(2,1)S(1)}, u32[]{:S(2)}, u32[]{:S(2)}) collective-permute-start(bf16[128,128]{1,0:T(8,128)(2,1)} %get-tuple-element.26), channel_id=1, source_target_pairs={{0,24},{1,28},{2,16},{3,20},{4,25},{5,29},{6,17},{7,21},{8,26},{9,... | collective-permute-start | bytes 98312 | tf_op jit(solution)/shard_map/ppermute | solution.py:688
  39.9 9.8 %collective-permute-start.12 = (bf16[128,128]{1,0:T(8,128)(2,1)}, bf16[128,128]{1,0:T(8,128)(2,1)S(1)}, u32[]{:S(2)}, u32[]{:S(2)}) collective-permute-start(bf16[128,128]{1,0:T(8,128)(2,1)} %get-tuple-element.26), channel_id=1, source_target_pairs={{0,20},{1,24},{2,28},{3,16},{4,21},{5,25},{6,29},{7,17},{8,22},{9,... | collective-permute-start | bytes 98312 | tf_op jit(solution)/shard_map/ppermute | solution.py:688
  41.4 8.3 %collective-permute-start.11 = (bf16[128,128]{1,0:T(8,128)(2,1)}, bf16[128,128]{1,0:T(8,128)(2,1)S(1)}, u32[]{:S(2)}, u32[]{:S(2)}) collective-permute-start(bf16[128,128]{1,0:T(8,128)(2,1)} %get-tuple-element.26), channel_id=1, source_target_pairs={{0,16},{1,20},{2,24},{3,28},{4,17},{5,21},{6,25},{7,29},{8,18},{9,... | collective-permute-start | bytes 98312 | tf_op jit(solution)/shard_map/ppermute | solution.py:688
  43.1 0.9 %copy-start.6 = (bf16[640,128]{1,0:T(8,128)(2,1)S(1)}, bf16[640,128]{1,0:T(8,128)(2,1)}, u32[]{:S(2)}) copy-start(bf16[640,128]{1,0:T(8,128)(2,1)} %get-tuple-element.23.refs_1_) | copy-start | bytes 491524
  44.0 0.8 copy-start.8
  44.8 0.8 copy-start.10
  45.5 0.8 copy-start.12
  46.3 3.4 %copy-start.2 = (s32[256]{0:T(256)S(1)}, s32[256]{0:T(256)}, u32[]{:S(2)}) copy-start(s32[256]{0:T(256)} %param.13) | copy-start | bytes 3076
  46.3 3.4 %copy-start.3 = (bf16[64,64,128]{2,1,0:T(8,128)(2,1)S(1)}, bf16[64,64,128]{2,1,0:T(8,128)(2,1)}, u32[]{:S(2)}) copy-start(bf16[64,64,128]{2,1,0:T(8,128)(2,1)} %param.12) | copy-start | bytes 3145732
  46.3 3.4 %copy-start.5 = (f32[1024,128]{1,0:T(8,128)S(1)}, f32[1024,128]{1,0:T(8,128)}, u32[]{:S(2)}) copy-start(f32[1024,128]{1,0:T(8,128)} %refs_18_.1) | copy-start | bytes 1572868
  46.3 3.4 %copy-start.7 = (bf16[640,128]{1,0:T(8,128)(2,1)S(1)}, bf16[640,128]{1,0:T(8,128)(2,1)}, u32[]{:S(2)}) copy-start(bf16[640,128]{1,0:T(8,128)(2,1)} %get-tuple-element.23.refs_1_) | copy-start | bytes 491524
  46.3 3.4 %copy-start.14 = (f32[128,8]{0,1:T(8,128)S(1)}, f32[128,8]{0,1:T(8,128)}, u32[]{:S(2)}) copy-start(f32[128,8]{0,1:T(8,128)} %param.19) | copy-start | bytes 12292
  49.3 12.8 %collective-permute-start.15 = (f32[16,8,256]{2,1,0:T(8,128)S(1)}, f32[16,8,256]{2,1,0:T(8,128)S(1)}, u32[]{:S(2)}, u32[]{:S(2)}) collective-permute-start(f32[16,8,256]{2,1,0:T(8,128)S(1)} %shard_map.132.refs_2_), channel_id=1, source_target_pairs={{0,16},{16,0},{1,17},{17,1},{2,18},{18,2},{3,19},{19,3},{4,20},{20... | collective-permute-start | bytes 393224 | tf_op jit(solution)/shard_map/ppermute | solution.py:738
  49.8 15.4 %copy-start.1 = (bf16[256,128]{1,0:T(8,128)(2,1)S(1)}, bf16[256,128]{1,0:T(8,128)(2,1)}, u32[]{:S(2)}) copy-start(bf16[256,128]{1,0:T(8,128)(2,1)} %get-tuple-element.32.refs_2_) | copy-start | bytes 196612
  49.8 15.4 %copy-start.9 = (bf16[64,256]{1,0:T(8,128)(2,1)S(1)}, bf16[64,256]{1,0:T(8,128)(2,1)}, u32[]{:S(2)}) copy-start(bf16[64,256]{1,0:T(8,128)(2,1)} %refs_1_.3) | copy-start | bytes 98308
  49.8 15.4 %copy-start.11 = (bf16[64,256]{1,0:T(8,128)(2,1)S(1)}, bf16[64,256]{1,0:T(8,128)(2,1)}, u32[]{:S(2)}) copy-start(bf16[64,256]{1,0:T(8,128)(2,1)} %refs_3_.1) | copy-start | bytes 98308
  62.6 5.4 %collective-permute-start.16 = (f32[10,8,128]{2,1,0:T(8,128)S(1)}, f32[10,8,128]{2,1,0:T(8,128)S(1)}, u32[]{:S(2)}, u32[]{:S(2)}) collective-permute-start(f32[10,8,128]{2,1,0:T(8,128)S(1)} %get-tuple-element.29), channel_id=1, source_target_pairs={{0,1},{1,2},{2,3},{3,0},{4,5},{5,6},{6,7},{7,4},{8,9},{9,10},{10,1... | collective-permute-start | bytes 122888 | tf_op jit(solution)/shard_map/ppermute | solution.py:793
  62.6 5.4 %collective-permute-start.17 = (f32[10,8,128]{2,1,0:T(8,128)S(1)}, f32[10,8,128]{2,1,0:T(8,128)S(1)}, u32[]{:S(2)}, u32[]{:S(2)}) collective-permute-start(f32[10,8,128]{2,1,0:T(8,128)S(1)} %get-tuple-element.30), channel_id=1, source_target_pairs={{0,2},{1,3},{2,0},{3,1},{4,6},{5,7},{6,4},{7,5},{8,10},{9,11},{10,... | collective-permute-start | bytes 122888 | tf_op jit(solution)/shard_map/ppermute | solution.py:793
  65.2 2.8 %collective-permute-start.18 = (f32[10,8,128]{2,1,0:T(8,128)S(1)}, f32[10,8,128]{2,1,0:T(8,128)S(1)}, u32[]{:S(2)}, u32[]{:S(2)}) collective-permute-start(f32[10,8,128]{2,1,0:T(8,128)S(1)} %get-tuple-element.31), channel_id=1, source_target_pairs={{0,3},{1,0},{2,1},{3,2},{4,7},{5,4},{6,5},{7,6},{8,11},{9,8},{10,9... | collective-permute-start | bytes 122888 | tf_op jit(solution)/shard_map/ppermute | solution.py:793
  65.2 1.2 %copy-start.4 = (bf16[4096,128]{1,0:T(8,128)(2,1)S(1)}, bf16[4096,128]{1,0:T(8,128)(2,1)}, u32[]{:S(2)}) copy-start(bf16[4096,128]{1,0:T(8,128)(2,1)} %all-gather.3.cloned.1.call-done) | copy-start | bytes 3145732
  68.0 3.3 %copy-start = (bf16[32,16,64]{2,1,0:T(8,128)(2,1)S(1)}, bf16[32,16,64]{2,1,0:T(8,128)(2,1)}, u32[]{:S(2)}) copy-start(bf16[32,16,64]{2,1,0:T(8,128)(2,1)} %refs_1_.2) | copy-start | bytes 196612
  68.0 3.3 %copy-start.13 = (bf16[256,64]{0,1:T(8,128)(2,1)S(1)}, bf16[256,64]{0,1:T(8,128)(2,1)}, u32[]{:S(2)}) copy-start(bf16[256,64]{0,1:T(8,128)(2,1)} %param.20) | copy-start | bytes 98308
Sparse Core Ops, SparseCore 0:
  10.2 43.8 all-gather.2

commit v7 on v6

--- a/solution.py
+++ b/solution.py
@@ -102,8 +102,6 @@
     mask_ref,
     rows_ref,
     cols_ref,
-    left_ref,
-    right_ref,
     norm_ref,
     turn_ref,
     place_ref,
@@ -137,8 +135,7 @@
     fc = w1_ref.shape[0]
     wk = pack * seqs
     for g in range(tokens // pack):
-        left_ref[g * fc : (g + 1) * fc, :] = left[:, g * wk : (g + 1) * wk]
-    rows_ref[: -2 * rows, :] = left_ref[...]
+        rows_ref[g * fc : (g + 1) * fc, :] = left[:, g * wk : (g + 1) * wk]
     size = 128 // tokens
     real = real.astype(bf16)
     w2 = w2_ref[...]
@@ -149,30 +146,39 @@
         res = nt_dot(w2, jnp.concatenate([real[s]] * size, axis=0))
         res = jnp.where(mine, res, 0.0).reshape(fd // size, size, 128)
         place_ref[:, s, :] = jnp.sum(res, axis=1)
-    right = place_ref[...].reshape(fd // size * seqs, 128).astype(bf16)
-    right_ref[...] = right
-    cols_ref[:-rows, :] = right
+    cols_ref[:-rows, :] = place_ref[...].reshape(fd // size * seqs, 128).astype(bf16)
+
+
+def join_kernel(
+    ready,
+    place_ref,
+    rows0_ref,
+    rows1_ref,
+    rows2_ref,
+    rows3_ref,
+    cols0_ref,
+    cols1_ref,
+    cols2_ref,
+    cols3_ref,
+    out_ref,
+):
+    nk = 4
+    row, col = place_ref[0], place_ref[1]
+    r_rows = l_rows = out_ref.shape[0] // (2 * nk)
+    for t, ref in enumerate((cols0_ref, cols1_ref, cols2_ref, cols3_ref)):
+        at = pl.ds(pl.multiple_of(lax.rem(row + nk - t, nk) * r_rows, r_rows), r_rows)
+        out_ref[at, :] = ref[:r_rows, :]
+    for t, ref in enumerate((rows0_ref, rows1_ref, rows2_ref, rows3_ref)):
+        start = nk * r_rows + jnp.bitwise_xor(col, t) * l_rows
+        at = pl.ds(pl.multiple_of(start, l_rows), l_rows)
+        out_ref[at, :] = ref[:l_rows, :]
 
 
 def update_kernel(
     ready,
     place_ref,
-    left0_ref,
-    left1_ref,
-    left2_ref,
-    left3_ref,
-    right0_ref,
-    right1_ref,
-    right2_ref,
-    right3_ref,
-    far_left0_ref,
-    far_left1_ref,
-    far_left2_ref,
-    far_left3_ref,
-    far_right0_ref,
-    far_right1_ref,
-    far_right2_ref,
-    far_right3_ref,
+    sides_ref,
+    far_sides_ref,
     mask_ref,
     m_ref,
     score_ref,
@@ -188,42 +194,34 @@
     mt_ref,
     oh_ref,
     ol_ref,
+    update_ref,
 ):
     nk = rk_ref.shape[0]
     width_d, pair_rows, _ = rab_ref.shape
-    row, col, seq = place_ref[0], place_ref[1], place_ref[2]
+    col, seq = place_ref[1], place_ref[2]
     z = pair_ref.shape[1]
     groups, heads, lanes = logits_ref.shape
     tile_j = lanes // pack
     tokens = tile_j // nk
-    per_k = groups // nk
     fc = lm_ref.shape[0] // groups
     seqs = 128 // pack
     nq = pair_rows // seqs
     wk = pack * seqs
 
-    rights = (right0_ref, right1_ref, right2_ref, right3_ref)
-    far_rights = (far_right0_ref, far_right1_ref, far_right2_ref, far_right3_ref)
-    lefts = (left0_ref, left1_ref, left2_ref, left3_ref)
-    far_lefts = (far_left0_ref, far_left1_ref, far_left2_ref, far_left3_ref)
     r_rows = rk_ref.shape[1] // nq
-    l_rows = per_k * fc
+    l_rows = groups * fc
     if nq == 2:
-        sources = ((seq, 0, rights, lefts), (1 - seq, 0, far_rights, far_lefts))
+        sources = ((seq, 0, sides_ref), (1 - seq, 0, far_sides_ref))
     else:
-        sources = tuple((q, q, far_rights, far_lefts) for q in range(nq))
-    for q, slot, from_rights, from_lefts in sources:
-        for t in range(nk):
-            at = pl.ds(pl.multiple_of(q * r_rows, r_rows), r_rows)
-            part = from_rights[t][slot * r_rows : (slot + 1) * r_rows, :]
-            rk_ref[lax.rem(row + nk - t, nk), at, :] = part
-            k = jnp.bitwise_xor(col, t)
-            at = pl.ds(pl.multiple_of(k * l_rows, l_rows), l_rows)
-            for g in range(per_k):
-                from_row = slot * l_rows + g * fc
-                at = pl.ds(pl.multiple_of((k * per_k + g) * fc, fc), fc)
-                to = pl.ds(pl.multiple_of(q * wk, wk), wk)
-                lm_ref[at, to] = from_lefts[t][from_row : from_row + fc, :]
+        sources = tuple((q, q, far_sides_ref) for q in range(nq))
+    for q, slot, ref in sources:
+        base = slot * (nk * r_rows + l_rows)
+        at = pl.ds(pl.multiple_of(q * r_rows, r_rows), r_rows)
+        for k in range(nk):
+            rk_ref[k, at, :] = ref[base + k * r_rows : base + (k + 1) * r_rows, :]
+        base = base + nk * r_rows
+        to = pl.ds(pl.multiple_of(q * wk, wk), wk)
+        lm_ref[:, to] = ref[base : base + l_rows, :]
     size = 128 // tokens
     right = jnp.concatenate([rk_ref[k] for k in range(nk)], axis=1)
     source = lax.broadcasted_iota(jnp.int32, (nk * 128, 4 * tile_j), 0)
@@ -242,6 +240,7 @@
 
     chunk = 4
     many = 4
+    wide = oh_ref.shape[2] // lanes
     empty = jnp.zeros((seqs, 2 * tile_j), bf16)
 
     def block_of(d):
@@ -264,10 +263,10 @@
                 at = pl.ds(pl.multiple_of((many * n + e) * fc, fc), fc)
                 for g in range(chunk):
                     group = m * chunk + g
-                    to = slice(group % 2 * lanes, (group % 2 + 1) * lanes)
+                    to = slice(group % wide * lanes, (group % wide + 1) * lanes)
                     cut = slice(g * fc, (g + 1) * fc), slice(e * lanes, (e + 1) * lanes)
-                    oh_ref[group // 2, at, to] = high[cut]
-                    ol_ref[group // 2, at, to] = low[cut]
+                    oh_ref[group // wide, at, to] = high[cut]
+                    ol_ref[group // wide, at, to] = low[cut]
         return carry
 
     lax.fori_loop(0, width_d // many, outer_of, 0)
@@ -283,7 +282,7 @@
         mt_ref[z:, n * z : (n + 1) * z] = low
     maskj = column_mask(mask_ref, col, tile_j, 2)
 
-    maskl = jnp.concatenate([maskj] * pack, axis=1) > 0
+    maskl = jnp.concatenate([maskj] * (pack // 2), axis=1) > 0
     score = score_ref[...]
     s1 = score.astype(bf16).astype(f32)
     s2 = (score - s1).astype(bf16).astype(f32)
@@ -299,28 +298,28 @@
 
     def finish(n, carry):
         two = nn_dot(mt_ref[...], oh_ref[n])
-        update = two[:z] + two[z:] + nn_dot(mt_ref[:z, :], ol_ref[n])
-        at = pl.ds(pl.multiple_of(n * 2 * lanes, 2 * lanes), 2 * lanes)
-        before = pair_ref[at, :].astype(f32).T
-        result = (before + update).astype(bf16)
-        pout_t_ref[2 * n] = result[:, :lanes]
-        pout_t_ref[2 * n + 1] = result[:, lanes:]
-        x = result.astype(f32)
-        pout_ref[at, :] = x.T.astype(bf16)
+        update_ref[...] = two[:z] + two[z:] + nn_dot(mt_ref[:z, :], ol_ref[n])
+        for e in range(wide):
+            g = n * wide + e
+            at = pl.ds(pl.multiple_of(g * lanes, lanes), lanes)
+            before = pair_ref[at, :].astype(f32).T
+            result = (before + update_ref[:, e * lanes : (e + 1) * lanes]).astype(bf16)
+            pout_t_ref[g] = result
+            x = result.astype(f32)
+            pout_ref[at, :] = x.T.astype(bf16)
+            center = x - jnp.mean(x, axis=0, keepdims=True)
+            inverse = lax.rsqrt(jnp.mean(center * center, axis=0, keepdims=True) + epsilon)
+            high, low = high_low(center * inverse)
+            scores = nn_dot(st, jnp.concatenate([high, low], axis=0))
+            logits = scores[:heads] + scores[heads : 2 * heads] + scores[2 * heads : 3 * heads]
+            logits_ref[g] = jnp.where(maskl, logits, far_below)
+        at = pl.ds(pl.multiple_of(n * wide * lanes, wide * lanes), wide * lanes)
         pltpu.make_async_copy(pout_ref.at[at], pout_hbm.at[at], out_sem.at[n]).start()
-        center = x - jnp.mean(x, axis=0, keepdims=True)
-        inverse = lax.rsqrt(jnp.mean(center * center, axis=0, keepdims=True) + epsilon)
-        high, low = high_low(center * inverse)
-        scores = nn_dot(st, jnp.concatenate([high, low], axis=0))
-        logits = scores[:heads] + scores[heads : 2 * heads] + scores[2 * heads : 3 * heads]
-        logits = jnp.where(maskl, logits, far_below)
-        logits_ref[2 * n] = logits[:, :lanes]
-        logits_ref[2 * n + 1] = logits[:, lanes:]
         return carry
 
-    lax.fori_loop(0, groups // 2, finish, 0, unroll=2)
-    for n in range(groups // 2):
-        at = pl.ds(n * 2 * lanes, 2 * lanes)
+    lax.fori_loop(0, groups // wide, finish, 0)
+    for n in range(groups // wide):
+        at = pl.ds(n * wide * lanes, wide * lanes)
         pltpu.make_async_copy(pout_ref.at[at], pout_hbm.at[at], out_sem.at[n]).wait()
 
 
@@ -484,14 +483,12 @@
     ready()
     for s in range(half):
         x = jnp.concatenate([ev_ref[k, s] for k in range(owners)], axis=0)
-        v = nn_dot(x, wv).astype(bf16)
-        v_ref[s] = v[:, :chans]
-        v_ref[s + half] = v[:, chans:]
+        v_ref[s] = nn_dot(x, wv).astype(bf16)
 
 
 def gradient_kernel(
     ready,
-    own_ref, r1_ref, r2_ref, r3_ref, logits_ref, gw_ref, pout_t_ref, score_ref, out_ref, stat_ref
+    own_ref, r1_ref, r2_ref, r3_ref, logits_ref, gw_ref, pout_t_ref, score_ref, out_hbm, stat_ref, out_ref, out_sem
 ):
     groups, heads, lanes = logits_ref.shape
     rows = groups * heads
@@ -516,7 +513,7 @@
     tile = lanes // pack
     low = lax.broadcasted_iota(jnp.int32, (heads, 2 * tile), 1) < tile
 
-    def one(g, carry):
+    def one(g):
         st = stat_ref[pl.ds(pl.multiple_of(g * heads, heads), heads), :]
 
         def spread(base):
@@ -545,9 +542,20 @@
         along = jnp.mean(grad * normal, axis=0, keepdims=True)
         result = inverse * (centered - normal * along)
         out_ref[pl.ds(pl.multiple_of(g * lanes, lanes), lanes), :] = result.T.astype(bf16)
+
+    many = 4
+
+    def some(n, carry):
+        for e in range(many):
+            one(n * many + e)
+        at = pl.ds(pl.multiple_of(n * many * lanes, many * lanes), many * lanes)
+        pltpu.make_async_copy(out_ref.at[at], out_hbm.at[at], out_sem.at[n]).start()
         return carry
 
-    lax.fori_loop(0, groups, one, 0, unroll=4)
+    lax.fori_loop(0, groups // many, some, 0)
+    for n in range(groups // many):
+        at = pl.ds(n * many * lanes, many * lanes)
+        pltpu.make_async_copy(out_ref.at[at], out_hbm.at[at], out_sem.at[n]).wait()
 
 
 def alignment_kernel(
@@ -572,7 +580,8 @@
     tile = wide // 2
     pieces = own_ref.shape[0] - 2
     rows = pieces * heads
-    seqs, all_tokens, chans = v_ref.shape
+    half, all_tokens, chans = v_ref.shape
+    chans = chans // 2
     tokens = pieces * 2
     head_width = chans // heads
     col = col_ref[0]
@@ -603,14 +612,16 @@
 
     def one(s, carry):
         full = nn_dot(w, v_ref[s])
-        mean = jnp.zeros((tokens, chans), f32)
-        for h in range(heads):
-            mean = jnp.where(owner == h, full[h * tokens : (h + 1) * tokens], mean)
-        at = pl.ds(pl.multiple_of(s * tokens, tokens), tokens)
-        gated_ref[at, :] = (gate_ref[at, :] * mean).astype(bf16)
+        for e in range(2):
+            cut = slice(e * chans, (e + 1) * chans)
+            mean = jnp.zeros((tokens, chans), f32)
+            for h in range(heads):
+                mean = jnp.where(owner == h, full[h * tokens : (h + 1) * tokens, cut], mean)
+            at = pl.ds(pl.multiple_of((e * half + s) * tokens, tokens), tokens)
+            gated_ref[at, :] = (gate_ref[at, :] * mean).astype(bf16)
         return carry
 
-    lax.fori_loop(0, seqs, one, 0, unroll=4)
+    lax.fori_loop(0, half, one, 0, unroll=4)
     out_ref[...] = (x_ref[...].astype(f32) + nt_dot(gated_ref[...], wf_ref[...])).astype(bf16)
 
 
@@ -651,13 +662,11 @@
     l_rows = tokens // pack * fc
     r_rows = fd * tokens // 128 * seqs
     n_rows = half * tokens
-    rows, cols, left, right, normed = call(
+    rows, cols, normed = call(
         prepare_kernel,
         (
             sds((l_rows + 2 * n_rows, 128), bf16),
             sds((r_rows + n_rows, 128), bf16),
-            sds((l_rows, 128), bf16),
-            sds((r_rows, 128), bf16),
             sds((n_rows, 128), bf16),
         ),
         scratch=(
@@ -678,35 +687,30 @@
     every = lax.all_gather(normed, ("row", "col"), axis=0).reshape(
         nr * nk, half, tokens, 2 * width
     )
-    def to_columns(x, t, flip):
-        pairs = [
-            ((s * nr + r) * nk + c, ((s ^ flip) * nr + (c + t) % nr) * nk + r)
-            for s in range(nq)
-            for r in range(nr)
-            for c in range(nk)
-        ]
-        return lax.ppermute(x, ("seq", "row", "col"), pairs)
-
-    def to_rows(x, t, flip):
-        pairs = [
-            ((s * nr + r) * nk + c, ((s ^ flip) * nr + r) * nk + (c ^ t))
-            for s in range(nq)
-            for r in range(nr)
-            for c in range(nk)
-        ]
-        return lax.ppermute(x, ("seq", "row", "col"), pairs)
-
-    all_cols = [to_columns(cols, t, 0) for t in range(nr)]
-    across = to_rows(rows, 2, 0)
-    all_rows = [rows, to_rows(rows, 1, 0), across, to_rows(across, 1, 0)]
+    all_cols = [
+        lax.ppermute(
+            cols,
+            ("row", "col"),
+            [(r * nk + c, (c + t) % nr * nk + r) for r in range(nr) for c in range(nk)],
+        )
+        for t in range(nr)
+    ]
+
+    def exchange(x, bit):
+        return lax.ppermute(x, "col", [(c, c ^ bit) for c in range(nk)])
+
+    across = exchange(rows, 2)
+    all_rows = [rows, exchange(rows, 1), across, exchange(across, 1)]
+
+    (sides,) = call(
+        join_kernel,
+        (sds((nk * (r_rows + l_rows), 128), bf16),),
+        smem=1,
+    )(place, *all_rows, *all_cols)
     if nq == 2:
-        far_rights = [to_columns(right, t, 1) for t in range(nr)]
-        far_lefts = [to_rows(left, t, 1) for t in range(nk)]
+        far_sides = lax.ppermute(sides, "seq", [(0, 1), (1, 0)])
     else:
-        right = lax.all_gather(right, "seq", axis=0, tiled=True)
-        left = lax.all_gather(left, "seq", axis=0, tiled=True)
-        far_rights = [to_columns(right, t, 0) for t in range(nr)]
-        far_lefts = [left] + [to_rows(left, t, 0) for t in range(1, nk)]
+        far_sides = lax.all_gather(sides, "seq", axis=0, tiled=True)
 
     head_lanes = seqs * chans // heads
     (gw_own,) = call(
@@ -748,26 +752,25 @@
         ),
         scratch=(
             pltpu.VMEM((tile_i * tile_j, z), bf16),
-            pltpu.SemaphoreType.DMA((groups // 2,)),
+            pltpu.SemaphoreType.DMA((groups // 4,)),
             pltpu.VMEM((nk, nq * r_rows, 128), bf16),
             pltpu.VMEM((fd, nq * seqs, 4 * tile_j), bf16),
             pltpu.VMEM((groups * fc, nq * pack * seqs), bf16),
             pltpu.VMEM((2 * z, fd * fc), bf16),
-            pltpu.VMEM((groups // 2, fd * fc, 2 * lanes), bf16),
-            pltpu.VMEM((groups // 2, fd * fc, 2 * lanes), bf16),
+            pltpu.VMEM((groups // 4, fd * fc, 4 * lanes), bf16),
+            pltpu.VMEM((groups // 4, fd * fc, 4 * lanes), bf16),
+            pltpu.VMEM((z, 4 * lanes), f32),
         ),
         smem=1,
         flops=14_000_000_000,
         nbytes=5_000_000,
         vmem=44 * 1024 * 1024,
-        far=(17, 18, 19, 20),
+        far=(3, 4, 5, 6),
         far_out=(0,),
     )(
         place,
-        *all_rows,
-        *all_cols,
-        *far_lefts,
-        *far_rights,
+        sides,
+        far_sides,
         mask,
         outer_matrix,
         score_matrix.T,
@@ -776,7 +779,7 @@
 
     values, gating = call(
         values_kernel,
-        (sds((seqs, nr * nk * tokens, chans), bf16), sds((seqs * tokens, chans), f32)),
+        (sds((half, nr * nk * tokens, 2 * chans), bf16), sds((seqs * tokens, chans), f32)),
         flops=4_000_000_000,
         nbytes=6_000_000,
         far=(0,),
@@ -799,7 +802,12 @@
     (gradient,) = call(
         gradient_kernel,
         (sds((tile_i * tile_j, z), bf16),),
-        scratch=(pltpu.VMEM((groups * heads, groups * heads), f32),),
+        scratch=(
+            pltpu.VMEM((groups * heads, groups * heads), f32),
+            pltpu.VMEM((tile_i * tile_j, z), bf16),
+            pltpu.SemaphoreType.DMA((groups // 4,)),
+        ),
+        far_out=(0,),
         flops=4_000_000_000,
         nbytes=3_000_000,
     )(pay0, *got, logits, gw, pair_t, score_matrix.T)

time: 82 us -> 73.3 us (0.89)
  starting transfers between devices: 29.5 us -> 23.5 us
  Pallas kernels: 26.6 us -> 25.2 us
  waiting for transfers between devices: 6.49 us -> 5.47 us
    ppermute x15 -> x8, starting transfers between devices: 26.5 us -> 14.3 us  [the longest x4 9.26 us: on_device(): lax.ppermute(cols, ('row', 'col'), [(r * nk + c, (c + t) % nr * nk + r) f...]
    ppermute x3, starting transfers between devices: 2.61 us -> 8.99 us  [on_device(): lax.ppermute(pay, 'col', [(c, (c + shift) % nk) for c in range(nk)])]
    pallas_call x7 -> x8, Pallas kernels: 26.6 us -> 25.2 us  [run(): pl.pallas_call(body, out_shape=out_shape, in_specs=in_specs, out_specs=[p...]
    ppermute x15 -> x8, waiting for transfers between devices: 6.47 us -> 5.44 us  [the longest x4 3.16 us: on_device(): lax.ppermute(cols, ('row', 'col'), [(r * nk + c, (c + t) % nr * nk + r) f...]
    unnamed x30 -> x28, local copies, waits for them, and re-layouts: 4.46 us -> 4.45 us
  transfers between devices with their start and end apart: 20 -> 13, of which waited for: 4 -> 3; matrix products, arithmetic and copies ran while one was open for 0% -> 0% of each run, Pallas kernels for 21% -> 23%
where the time goes in v7:
time: 73.3 us; the launch traced here: 72.9 us
  Pallas kernels  25.2 us (34%)
  starting transfers between devices  23.5 us (32%)
  between operations  14.2 us (19%)
  waiting for transfers between devices  5.47 us (7%)
  local copies, waits for them, and re-layouts  4.45 us (6%)
    pallas_call x8, Pallas kernels, run(): pl.pallas_call(body, out_shape=out_shape, in_specs=in_specs, out_specs=[p...  25.2 us
    ppermute x4, starting transfers between devices, on_device(): lax.ppermute(cols, ('row', 'col'), [(r * nk + c, (c + t) % nr * nk + r) f...  9.26 us
    ppermute x3, starting transfers between devices, on_device(): lax.ppermute(pay, 'col', [(c, (c + shift) % nk) for c in range(nk)])  8.99 us
    unnamed x28, local copies, waits for them, and re-layouts  4.45 us
    ppermute x4, waiting for transfers between devices, on_device(): lax.ppermute(cols, ('row', 'col'), [(r * nk + c, (c + t) % nr * nk + r) f...  3.16 us
    ppermute x3, starting transfers between devices, exchange(): return lax.ppermute(x, 'col', [(c, c ^ bit) for c in range(nk)])  3.04 us
    ppermute x3, waiting for transfers between devices, exchange(): return lax.ppermute(x, 'col', [(c, c ^ bit) for c in range(nk)])  2.28 us
    ppermute x1, starting transfers between devices, on_device(): far_sides = lax.ppermute(sides, 'seq', [(0, 1), (1, 0)])  2.03 us
  transfers between devices with their start and end apart: 13, of which 3 were waited for; matrix products, arithmetic and copies ran while one was open for 0% of the time, Pallas kernels for 23%

profile of v7, /device:TPU:0, one launch (start us, length us, event | category | flops | bytes accessed | tf_op | source)
XLA Modules:
  0.0 72.9 jit_solution(3359295120010333781)
XLA Ops:
  7.2 0.0 all-gather.3.cloned.1.call-start
  7.2 2.8 %shard_map.130 = (bf16[640,128]{1,0:T(8,128)(2,1)}, bf16[384,128]{1,0:T(8,128)(2,1)}, bf16[256,128]{1,0:T(8,128)(2,1)}) custom-call(s32[1]{0:T(128)} %bitcast.3.refs_0_, bf16[32,16,64]{2,1,0:T(8,128)(2,1)} %refs_1_.2, bf16[32,16,64]{2,1,0:T(8,128)(2,1)} %refs_2_.1, bf16[32,64]{1,0:T(8,128)(2,1)} %bitcast.25, bf16[32,64]{1,0:T(8,128)(2,1)} %bitcast.26, ...), custom_call_target="tpu_custom_call" | custom-call | tf_op jit(solution)/shard_map/pallas_call | solution.py:62
  10.0 0.0 all-gather.3.cloned.1.call-update
  10.1 3.0 %collective-permute-start.1 = (bf16[640,128]{1,0:T(8,128)(2,1)}, bf16[640,128]{1,0:T(8,128)(2,1)S(1)}, u32[]{:S(2)}, u32[]{:S(2)}) collective-permute-start(bf16[640,128]{1,0:T(8,128)(2,1)} %get-tuple-element.21.refs_1_), channel_id=1, source_target_pairs={{0,2},{1,3},{2,0},{3,1},{4,6},{5,7},{6,4},{7,5},{8,10},{9,11},{10,... | collective-permute-start | bytes 491528 | tf_op jit(solution)/shard_map/ppermute | solution.py:700
  13.1 3.6 %collective-permute-start.6 = (bf16[384,128]{1,0:T(8,128)(2,1)}, bf16[384,128]{1,0:T(8,128)(2,1)S(1)}, u32[]{:S(2)}, u32[]{:S(2)}) collective-permute-start(bf16[384,128]{1,0:T(8,128)(2,1)} %get-tuple-element.22), channel_id=1, source_target_pairs={{0,12},{1,0},{2,4},{3,8},{4,13},{5,1},{6,5},{7,9},{8,14},{9,2},{10... | collective-permute-start | bytes 294920 | tf_op jit(solution)/shard_map/ppermute | solution.py:691
  16.7 0.0 collective-permute-start
  16.7 2.3 %collective-permute-done.1.refs_3_ = bf16[640,128]{1,0:T(8,128)(2,1)S(1)} collective-permute-done((bf16[640,128]{1,0:T(8,128)(2,1)}, bf16[640,128]{1,0:T(8,128)(2,1)S(1)}, u32[]{:S(2)}, u32[]{:S(2)}) %collective-permute-start.1) | collective-permute-done | bytes 163872 | tf_op jit(solution)/shard_map/ppermute | solution.py:700
  19.0 0.0 collective-permute-start.2
  19.0 3.4 %collective-permute-start.5 = (bf16[384,128]{1,0:T(8,128)(2,1)}, bf16[384,128]{1,0:T(8,128)(2,1)S(1)}, u32[]{:S(2)}, u32[]{:S(2)}) collective-permute-start(bf16[384,128]{1,0:T(8,128)(2,1)} %get-tuple-element.22), channel_id=1, source_target_pairs={{0,8},{1,12},{2,0},{3,4},{4,9},{5,13},{6,1},{7,5},{8,10},{9,14},{1... | collective-permute-start | bytes 294920 | tf_op jit(solution)/shard_map/ppermute | solution.py:691
  22.4 0.7 collective-permute-start.4
  23.1 0.0 collective-permute-done.6.refs_8_
  23.1 1.5 %collective-permute-start.3 = (bf16[384,128]{1,0:T(8,128)(2,1)}, bf16[384,128]{1,0:T(8,128)(2,1)S(1)}, u32[]{:S(2)}, u32[]{:S(2)}) collective-permute-start(bf16[384,128]{1,0:T(8,128)(2,1)} %get-tuple-element.22), channel_id=1, source_target_pairs={{0,0},{1,4},{2,8},{3,12},{4,1},{5,5},{6,9},{7,13},{8,2},{9,6},{10,... | collective-permute-start | bytes 294920 | tf_op jit(solution)/shard_map/ppermute | solution.py:691
  24.6 0.1 pad_add_fusion.refs_0_
  24.7 1.6 %collective-permute-done.5.refs_7_ = bf16[384,128]{1,0:T(8,128)(2,1)S(1)} collective-permute-done((bf16[384,128]{1,0:T(8,128)(2,1)}, bf16[384,128]{1,0:T(8,128)(2,1)S(1)}, u32[]{:S(2)}, u32[]{:S(2)}) %collective-permute-start.5) | collective-permute-done | bytes 98336 | tf_op jit(solution)/shard_map/ppermute | solution.py:691
  26.3 1.6 %collective-permute-done.4.refs_6_ = bf16[384,128]{1,0:T(8,128)(2,1)S(1)} collective-permute-done((bf16[384,128]{1,0:T(8,128)(2,1)}, bf16[384,128]{1,0:T(8,128)(2,1)S(1)}, u32[]{:S(2)}, u32[]{:S(2)}) %collective-permute-start.4) | collective-permute-done | bytes 98336 | tf_op jit(solution)/shard_map/ppermute | solution.py:691
  27.9 0.0 collective-permute-done.3.refs_5_
  27.9 0.0 collective-permute-done.refs_2_
  27.9 0.0 collective-permute-done.2.refs_4_
  27.9 0.0 copy-start
  27.9 0.9 %copy-done = bf16[640,128]{1,0:T(8,128)(2,1)S(1)} copy-done((bf16[640,128]{1,0:T(8,128)(2,1)S(1)}, bf16[640,128]{1,0:T(8,128)(2,1)}, u32[]{:S(2)}) %copy-start) | copy-done | bytes 163864
  28.8 0.6 shard_map.131.refs_1_
  29.4 2.0 %collective-permute-start.7 = (bf16[1024,128]{1,0:T(8,128)(2,1)S(1)}, bf16[1024,128]{1,0:T(8,128)(2,1)S(1)}, u32[]{:S(2)}, u32[]{:S(2)}) collective-permute-start(bf16[1024,128]{1,0:T(8,128)(2,1)S(1)} %shard_map.131.refs_1_), channel_id=1, source_target_pairs={{0,16},{16,0},{1,17},{17,1},{2,18},{18,2},{3,19},{19,3},{4,20},{20... | collective-permute-start | bytes 786440 | tf_op jit(solution)/shard_map/ppermute | solution.py:711
  31.4 0.0 copy-start.7
  31.4 0.8 %copy-done.7 = bf16[64,256]{1,0:T(8,128)(2,1)S(1)} copy-done((bf16[64,256]{1,0:T(8,128)(2,1)S(1)}, bf16[64,256]{1,0:T(8,128)(2,1)}, u32[]{:S(2)}) %copy-start.7) | copy-done | bytes 32792
  32.2 0.0 copy-start.9
  32.2 0.8 %copy-done.9 = bf16[64,256]{1,0:T(8,128)(2,1)S(1)} copy-done((bf16[64,256]{1,0:T(8,128)(2,1)S(1)}, bf16[64,256]{1,0:T(8,128)(2,1)}, u32[]{:S(2)}) %copy-start.9) | copy-done | bytes 32792
  32.9 0.0 copy-start.11
  32.9 0.8 %copy-done.11 = bf16[256,64]{0,1:T(8,128)(2,1)S(1)} copy-done((bf16[256,64]{0,1:T(8,128)(2,1)S(1)}, bf16[256,64]{0,1:T(8,128)(2,1)}, u32[]{:S(2)}) %copy-start.11) | copy-done | bytes 32792
  33.7 0.0 copy-start.3
  33.7 0.0 copy-start.4
  33.7 0.0 copy-start.6
  33.7 0.0 copy-start.13
  33.7 3.0 %shard_map.133.refs_2_ = f32[16,8,256]{2,1,0:T(8,128)S(1)} custom-call(s32[3]{0:T(128)S(1)} %pad_add_fusion.refs_0_, bf16[640,128]{1,0:T(8,128)(2,1)S(1)} %copy-done, bf16[640,128]{1,0:T(8,128)(2,1)S(1)} %collective-permute-done.refs_2_, bf16[640,128]{1,0:T(8,128)(2,1)S(1)} %collective-permute-done.1.refs_3_, ...), custom_call_target="tpu_custom_call" | custom-call | flops 3000000000 | bytes 3000000 | tf_op jit(solution)/shard_map/pallas_call | solution.py:62
  36.7 0.1 collective-permute-start.8
  36.8 0.0 collective-permute-done.7.refs_2_
  36.8 0.0 copy-done.3
  36.8 0.0 copy-done.4
  36.8 0.0 copy-done.6
  36.8 0.0 copy-done.13
  36.8 0.0 copy-start.2
  36.8 0.0 copy-start.8
  36.9 0.0 copy-start.10
  36.9 11.2 %shard_map.132 = (bf16[4096,128]{1,0:T(8,128)(2,1)}, bf16[16,128,256]{2,1,0:T(8,128)(2,1)S(1)}, f32[16,8,256]{2,1,0:T(8,128)S(1)}) custom-call(s32[3]{0:T(128)S(1)} %pad_add_fusion.refs_0_, bf16[1024,128]{1,0:T(8,128)(2,1)S(1)} %shard_map.131.refs_1_, bf16[1024,128]{1,0:T(8,128)(2,1)S(1)} %collective-permute-done.7.refs_2_, s32[1,256]{1,0:T(1,128)S(1)} %bitcast.17, ...), custom_call_target="tpu_custom_call" | custom-call | flops 14000000000 | bytes 5000000 | tf_op jit(solution)/shard_map/pallas_call | solution.py:62
  48.1 0.0 collective-permute-done.8.refs_3_
  48.1 0.5 shard_map.134
  48.6 3.6 %collective-permute-start.9 = (f32[10,8,128]{2,1,0:T(8,128)S(1)}, f32[10,8,128]{2,1,0:T(8,128)S(1)}, u32[]{:S(2)}, u32[]{:S(2)}) collective-permute-start(f32[10,8,128]{2,1,0:T(8,128)S(1)} %get-tuple-element.25), channel_id=1, source_target_pairs={{0,1},{1,2},{2,3},{3,0},{4,5},{5,6},{6,7},{7,4},{8,9},{9,10},{10,1... | collective-permute-start | bytes 122888 | tf_op jit(solution)/shard_map/ppermute | solution.py:796
  52.2 4.0 %collective-permute-start.10 = (f32[10,8,128]{2,1,0:T(8,128)S(1)}, f32[10,8,128]{2,1,0:T(8,128)S(1)}, u32[]{:S(2)}, u32[]{:S(2)}) collective-permute-start(f32[10,8,128]{2,1,0:T(8,128)S(1)} %get-tuple-element.26), channel_id=1, source_target_pairs={{0,2},{1,3},{2,0},{3,1},{4,6},{5,7},{6,4},{7,5},{8,10},{9,11},{10,... | collective-permute-start | bytes 122888 | tf_op jit(solution)/shard_map/ppermute | solution.py:796
  56.2 1.4 %collective-permute-start.11 = (f32[10,8,128]{2,1,0:T(8,128)S(1)}, f32[10,8,128]{2,1,0:T(8,128)S(1)}, u32[]{:S(2)}, u32[]{:S(2)}) collective-permute-start(f32[10,8,128]{2,1,0:T(8,128)S(1)} %get-tuple-element.27), channel_id=1, source_target_pairs={{0,3},{1,0},{2,1},{3,2},{4,7},{5,4},{6,5},{7,6},{8,11},{9,8},{10,9... | collective-permute-start | bytes 122888 | tf_op jit(solution)/shard_map/ppermute | solution.py:796
  57.6 0.0 all-gather.3.cloned.1.call-done
  57.6 0.0 copy-done.2
  57.6 0.0 copy-done.8
  57.6 0.0 copy-done.10
  57.6 0.0 copy-start.5
  57.6 1.2 %copy-done.5 = bf16[4096,128]{1,0:T(8,128)(2,1)S(1)} copy-done((bf16[4096,128]{1,0:T(8,128)(2,1)S(1)}, bf16[4096,128]{1,0:T(8,128)(2,1)}, u32[]{:S(2)}) %copy-start.5) | copy-done | bytes 1048600
  58.8 1.5 %shard_map.135 = (bf16[16,256,512]{2,1,0:T(8,128)(2,1)S(1)}, f32[512,256]{1,0:T(8,128)S(1)}) custom-call(bf16[16,16,16,128]{3,2,1,0:T(8,128)(2,1)S(1)} %bitcast.20, bf16[64,256]{1,0:T(8,128)(2,1)S(1)} %copy-done.8, bf16[256,128]{1,0:T(8,128)(2,1)S(1)} %copy-done.2, bf16[64,256]{1,0:T(8,128)(2,1)S(1)} %copy-done.10), custom_call_target="tpu_custom_call" | custom-call | flops 4000000000 | bytes 6000000 | tf_op jit(solution)/shard_map/pallas_call | solution.py:62
  60.3 0.0 collective-permute-done.9.refs_2_.refs_1_
  60.3 0.0 collective-permute-done.10.refs_3_.refs_2_
  60.4 0.0 collective-permute-done.11.refs_4_.refs_3_
  60.4 0.0 copy-start.1
  60.4 0.0 copy-start.12
  60.4 3.1 %shard_map.137 = bf16[4096,128]{1,0:T(8,128)(2,1)} custom-call(f32[10,8,128]{2,1,0:T(8,128)S(1)} %get-tuple-element.24.refs_1_.refs_0_, f32[10,8,128]{2,1,0:T(8,128)S(1)} %collective-permute-done.9.refs_2_.refs_1_, f32[10,8,128]{2,1,0:T(8,128)S(1)} %collective-permute-done.10.refs_3_.refs_2_, f32[10,8,128]{2,1,0:T(8,128)S(1)} %collective-permute-done.11.refs_4_.refs_3_, ...), custom_call_target="tpu_custom_call" | custom-call | flops 4000000000 | bytes 3000000 | tf_op jit(solution)/shard_map/pallas_call | solution.py:62
  63.5 0.0 copy-done.1
  63.5 0.0 copy-done.12
  63.5 2.6 %shard_map.136 = bf16[512,64]{1,0:T(8,128)(2,1)} custom-call(s32[1]{0:T(128)} %bitcast.refs_0_, f32[10,8,128]{2,1,0:T(8,128)S(1)} %get-tuple-element.24.refs_1_.refs_0_, f32[10,8,128]{2,1,0:T(8,128)S(1)} %collective-permute-done.9.refs_2_.refs_1_, f32[10,8,128]{2,1,0:T(8,128)S(1)} %collective-permute-done.10.refs_3_.refs_2_, ...), custom_call_target="tpu_custom_call" | custom-call | flops 3000000000 | bytes 5000000 | tf_op jit(solution)/shard_map/pallas_call | solution.py:62
Async XLA Ops:
  7.2 50.4 %all-gather.3.cloned.1.call-start = ((), (), s32[]{:S(2)}) async-start(), calls=%async_computation | async-start | bytes 1114112 | tf_op jit(solution)/shard_map/all_gather | solution.py:687
  10.1 8.9 %collective-permute-start.1 = (bf16[640,128]{1,0:T(8,128)(2,1)}, bf16[640,128]{1,0:T(8,128)(2,1)S(1)}, u32[]{:S(2)}, u32[]{:S(2)}) collective-permute-start(bf16[640,128]{1,0:T(8,128)(2,1)} %get-tuple-element.21.refs_1_), channel_id=1, source_target_pairs={{0,2},{1,3},{2,0},{3,1},{4,6},{5,7},{6,4},{7,5},{8,10},{9,11},{10,... | collective-permute-start | bytes 491528 | tf_op jit(solution)/shard_map/ppermute | solution.py:700
  13.1 10.0 %collective-permute-start.6 = (bf16[384,128]{1,0:T(8,128)(2,1)}, bf16[384,128]{1,0:T(8,128)(2,1)S(1)}, u32[]{:S(2)}, u32[]{:S(2)}) collective-permute-start(bf16[384,128]{1,0:T(8,128)(2,1)} %get-tuple-element.22), channel_id=1, source_target_pairs={{0,12},{1,0},{2,4},{3,8},{4,13},{5,1},{6,5},{7,9},{8,14},{9,2},{10... | collective-permute-start | bytes 294920 | tf_op jit(solution)/shard_map/ppermute | solution.py:691
  16.7 11.2 %collective-permute-start = (bf16[640,128]{1,0:T(8,128)(2,1)}, bf16[640,128]{1,0:T(8,128)(2,1)S(1)}, u32[]{:S(2)}, u32[]{:S(2)}) collective-permute-start(bf16[640,128]{1,0:T(8,128)(2,1)} %get-tuple-element.21.refs_1_), channel_id=1, source_target_pairs={{0,1},{1,0},{2,3},{3,2},{4,5},{5,4},{6,7},{7,6},{8,9},{9,8},{10,11... | collective-permute-start | bytes 491528 | tf_op jit(solution)/shard_map/ppermute | solution.py:700
  19.0 8.9 %collective-permute-start.2 = (bf16[640,128]{1,0:T(8,128)(2,1)S(1)}, bf16[640,128]{1,0:T(8,128)(2,1)S(1)}, u32[]{:S(2)}, u32[]{:S(2)}) collective-permute-start(bf16[640,128]{1,0:T(8,128)(2,1)S(1)} %collective-permute-done.1.refs_3_), channel_id=1, source_target_pairs={{0,1},{1,0},{2,3},{3,2},{4,5},{5,4},{6,7},{7,6},{8,9},{9,8},{10,11... | collective-permute-start | bytes 491528 | tf_op jit(solution)/shard_map/ppermute | solution.py:700
  19.0 7.3 %collective-permute-start.5 = (bf16[384,128]{1,0:T(8,128)(2,1)}, bf16[384,128]{1,0:T(8,128)(2,1)S(1)}, u32[]{:S(2)}, u32[]{:S(2)}) collective-permute-start(bf16[384,128]{1,0:T(8,128)(2,1)} %get-tuple-element.22), channel_id=1, source_target_pairs={{0,8},{1,12},{2,0},{3,4},{4,9},{5,13},{6,1},{7,5},{8,10},{9,14},{1... | collective-permute-start | bytes 294920 | tf_op jit(solution)/shard_map/ppermute | solution.py:691
  22.4 5.5 %collective-permute-start.4 = (bf16[384,128]{1,0:T(8,128)(2,1)}, bf16[384,128]{1,0:T(8,128)(2,1)S(1)}, u32[]{:S(2)}, u32[]{:S(2)}) collective-permute-start(bf16[384,128]{1,0:T(8,128)(2,1)} %get-tuple-element.22), channel_id=1, source_target_pairs={{0,4},{1,8},{2,12},{3,0},{4,5},{5,9},{6,13},{7,1},{8,6},{9,10},{10... | collective-permute-start | bytes 294920 | tf_op jit(solution)/shard_map/ppermute | solution.py:691
  23.1 4.8 %collective-permute-start.3 = (bf16[384,128]{1,0:T(8,128)(2,1)}, bf16[384,128]{1,0:T(8,128)(2,1)S(1)}, u32[]{:S(2)}, u32[]{:S(2)}) collective-permute-start(bf16[384,128]{1,0:T(8,128)(2,1)} %get-tuple-element.22), channel_id=1, source_target_pairs={{0,0},{1,4},{2,8},{3,12},{4,1},{5,5},{6,9},{7,13},{8,2},{9,6},{10,... | collective-permute-start | bytes 294920 | tf_op jit(solution)/shard_map/ppermute | solution.py:691
  27.9 0.9 %copy-start = (bf16[640,128]{1,0:T(8,128)(2,1)S(1)}, bf16[640,128]{1,0:T(8,128)(2,1)}, u32[]{:S(2)}) copy-start(bf16[640,128]{1,0:T(8,128)(2,1)} %get-tuple-element.21.refs_1_) | copy-start | bytes 491524
  29.4 7.4 %collective-permute-start.7 = (bf16[1024,128]{1,0:T(8,128)(2,1)S(1)}, bf16[1024,128]{1,0:T(8,128)(2,1)S(1)}, u32[]{:S(2)}, u32[]{:S(2)}) collective-permute-start(bf16[1024,128]{1,0:T(8,128)(2,1)S(1)} %shard_map.131.refs_1_), channel_id=1, source_target_pairs={{0,16},{16,0},{1,17},{17,1},{2,18},{18,2},{3,19},{19,3},{4,20},{20... | collective-permute-start | bytes 786440 | tf_op jit(solution)/shard_map/ppermute | solution.py:711
  31.4 0.8 %copy-start.7 = (bf16[64,256]{1,0:T(8,128)(2,1)S(1)}, bf16[64,256]{1,0:T(8,128)(2,1)}, u32[]{:S(2)}) copy-start(bf16[64,256]{1,0:T(8,128)(2,1)} %refs_1_.3) | copy-start | bytes 98308
  32.2 0.8 %copy-start.9 = (bf16[64,256]{1,0:T(8,128)(2,1)S(1)}, bf16[64,256]{1,0:T(8,128)(2,1)}, u32[]{:S(2)}) copy-start(bf16[64,256]{1,0:T(8,128)(2,1)} %refs_3_.1) | copy-start | bytes 98308
  32.9 0.8 %copy-start.11 = (bf16[256,64]{0,1:T(8,128)(2,1)S(1)}, bf16[256,64]{0,1:T(8,128)(2,1)}, u32[]{:S(2)}) copy-start(bf16[256,64]{0,1:T(8,128)(2,1)} %param.20) | copy-start | bytes 98308
  33.7 3.1 %copy-start.3 = (s32[256]{0:T(256)S(1)}, s32[256]{0:T(256)}, u32[]{:S(2)}) copy-start(s32[256]{0:T(256)} %param.13) | copy-start | bytes 3076
  33.7 3.1 %copy-start.4 = (bf16[64,64,128]{2,1,0:T(8,128)(2,1)S(1)}, bf16[64,64,128]{2,1,0:T(8,128)(2,1)}, u32[]{:S(2)}) copy-start(bf16[64,64,128]{2,1,0:T(8,128)(2,1)} %param.12) | copy-start | bytes 3145732
  33.7 3.1 %copy-start.6 = (f32[1024,128]{1,0:T(8,128)S(1)}, f32[1024,128]{1,0:T(8,128)}, u32[]{:S(2)}) copy-start(f32[1024,128]{1,0:T(8,128)} %refs_4_.1) | copy-start | bytes 1572868
  33.7 3.1 %copy-start.13 = (f32[128,8]{0,1:T(8,128)S(1)}, f32[128,8]{0,1:T(8,128)}, u32[]{:S(2)}) copy-start(f32[128,8]{0,1:T(8,128)} %param.19) | copy-start | bytes 12292
  36.7 11.4 %collective-permute-start.8 = (f32[16,8,256]{2,1,0:T(8,128)S(1)}, f32[16,8,256]{2,1,0:T(8,128)S(1)}, u32[]{:S(2)}, u32[]{:S(2)}) collective-permute-start(f32[16,8,256]{2,1,0:T(8,128)S(1)} %shard_map.133.refs_2_), channel_id=1, source_target_pairs={{0,16},{16,0},{1,17},{17,1},{2,18},{18,2},{3,19},{19,3},{4,20},{20... | collective-permute-start | bytes 393224 | tf_op jit(solution)/shard_map/ppermute | solution.py:742
  36.8 20.7 %copy-start.2 = (bf16[256,128]{1,0:T(8,128)(2,1)S(1)}, bf16[256,128]{1,0:T(8,128)(2,1)}, u32[]{:S(2)}) copy-start(bf16[256,128]{1,0:T(8,128)(2,1)} %get-tuple-element.28.refs_2_) | copy-start | bytes 196612
  36.8 20.7 %copy-start.8 = (bf16[64,256]{1,0:T(8,128)(2,1)S(1)}, bf16[64,256]{1,0:T(8,128)(2,1)}, u32[]{:S(2)}) copy-start(bf16[64,256]{1,0:T(8,128)(2,1)} %refs_1_.3) | copy-start | bytes 98308
  36.9 20.7 %copy-start.10 = (bf16[64,256]{1,0:T(8,128)(2,1)S(1)}, bf16[64,256]{1,0:T(8,128)(2,1)}, u32[]{:S(2)}) copy-start(bf16[64,256]{1,0:T(8,128)(2,1)} %refs_3_.1) | copy-start | bytes 98308
  48.6 11.8 %collective-permute-start.9 = (f32[10,8,128]{2,1,0:T(8,128)S(1)}, f32[10,8,128]{2,1,0:T(8,128)S(1)}, u32[]{:S(2)}, u32[]{:S(2)}) collective-permute-start(f32[10,8,128]{2,1,0:T(8,128)S(1)} %get-tuple-element.25), channel_id=1, source_target_pairs={{0,1},{1,2},{2,3},{3,0},{4,5},{5,6},{6,7},{7,4},{8,9},{9,10},{10,1... | collective-permute-start | bytes 122888 | tf_op jit(solution)/shard_map/ppermute | solution.py:796
  52.2 8.2 %collective-permute-start.10 = (f32[10,8,128]{2,1,0:T(8,128)S(1)}, f32[10,8,128]{2,1,0:T(8,128)S(1)}, u32[]{:S(2)}, u32[]{:S(2)}) collective-permute-start(f32[10,8,128]{2,1,0:T(8,128)S(1)} %get-tuple-element.26), channel_id=1, source_target_pairs={{0,2},{1,3},{2,0},{3,1},{4,6},{5,7},{6,4},{7,5},{8,10},{9,11},{10,... | collective-permute-start | bytes 122888 | tf_op jit(solution)/shard_map/ppermute | solution.py:796
  56.2 4.2 %collective-permute-start.11 = (f32[10,8,128]{2,1,0:T(8,128)S(1)}, f32[10,8,128]{2,1,0:T(8,128)S(1)}, u32[]{:S(2)}, u32[]{:S(2)}) collective-permute-start(f32[10,8,128]{2,1,0:T(8,128)S(1)} %get-tuple-element.27), channel_id=1, source_target_pairs={{0,3},{1,0},{2,1},{3,2},{4,7},{5,4},{6,5},{7,6},{8,11},{9,8},{10,9... | collective-permute-start | bytes 122888 | tf_op jit(solution)/shard_map/ppermute | solution.py:796
  57.6 1.2 %copy-start.5 = (bf16[4096,128]{1,0:T(8,128)(2,1)S(1)}, bf16[4096,128]{1,0:T(8,128)(2,1)}, u32[]{:S(2)}) copy-start(bf16[4096,128]{1,0:T(8,128)(2,1)} %all-gather.3.cloned.1.call-done) | copy-start | bytes 3145732
  60.4 3.1 %copy-start.1 = (bf16[32,16,64]{2,1,0:T(8,128)(2,1)S(1)}, bf16[32,16,64]{2,1,0:T(8,128)(2,1)}, u32[]{:S(2)}) copy-start(bf16[32,16,64]{2,1,0:T(8,128)(2,1)} %refs_1_.2) | copy-start | bytes 196612
  60.4 3.1 %copy-start.12 = (bf16[256,64]{0,1:T(8,128)(2,1)S(1)}, bf16[256,64]{0,1:T(8,128)(2,1)}, u32[]{:S(2)}) copy-start(bf16[256,64]{0,1:T(8,128)(2,1)} %param.20) | copy-start | bytes 98308
Sparse Core Ops, SparseCore 0:
  10.2 43.0 all-gather.2

commit v8 on v7

--- a/solution.py
+++ b/solution.py
@@ -161,6 +161,7 @@
     cols2_ref,
     cols3_ref,
     out_ref,
+    norm_ref,
 ):
     nk = 4
     row, col = place_ref[0], place_ref[1]
@@ -172,6 +173,10 @@
         start = nk * r_rows + jnp.bitwise_xor(col, t) * l_rows
         at = pl.ds(pl.multiple_of(start, l_rows), l_rows)
         out_ref[at, :] = ref[:l_rows, :]
+        half, tokens, _ = norm_ref.shape[1:]
+        count = half * tokens
+        start = ref.shape[0] - 2 * count
+        norm_ref[jnp.bitwise_xor(col, t)] = ref[start : start + count, :].reshape(norm_ref.shape[1:])
 
 
 def update_kernel(
@@ -238,7 +243,7 @@
                 at = (q * blocks + n) * seqs
                 rab_ref[n * size + e, q * seqs : (q + 1) * seqs, :] = res[at : at + seqs]
 
-    chunk = 4
+    chunk = 8
     many = 4
     wide = oh_ref.shape[2] // lanes
     empty = jnp.zeros((seqs, 2 * tile_j), bf16)
@@ -473,16 +478,18 @@
                 pay[2 + g * (pack // 2) + part] = piece[:, part * 2 * tile : (part + 1) * 2 * tile]
 
 
-def values_kernel(ready, ev_ref, wv_ref, norm_ref, wg_ref, v_ref, gate_ref):
-    owners, half, tokens, wide = ev_ref.shape
+def values_kernel(
+    ready, ev0_ref, ev1_ref, ev2_ref, ev3_ref, wv_ref, norm_ref, wg_ref, v_ref, gate_ref
+):
+    evs = (ev0_ref, ev1_ref, ev2_ref, ev3_ref)
+    nk, half, tokens, wide = ev0_ref.shape
     chans = wv_ref.shape[1]
     gate = jax.nn.sigmoid(nn_dot(norm_ref[...], twice(wg_ref[...])))
     gate_ref[: half * tokens] = gate[:, :chans]
     gate_ref[half * tokens :] = gate[:, chans:]
     wv = twice(wv_ref[...])
-    ready()
     for s in range(half):
-        x = jnp.concatenate([ev_ref[k, s] for k in range(owners)], axis=0)
+        x = jnp.concatenate([ev[k, s] for ev in evs for k in range(nk)], axis=0)
         v_ref[s] = nn_dot(x, wv).astype(bf16)
 
 
@@ -560,7 +567,7 @@
 
 def alignment_kernel(
     ready,
-    col_ref,
+    place_ref,
     own_ref,
     r1_ref,
     r2_ref,
@@ -584,7 +591,7 @@
     chans = chans // 2
     tokens = pieces * 2
     head_width = chans // heads
-    col = col_ref[0]
+    row, col = place_ref[0], place_ref[1]
 
     low = lax.broadcasted_iota(jnp.int32, (rows, wide), 1) < tile
     lgs = [p[2:].reshape(rows, wide) for p in pays]
@@ -605,7 +612,11 @@
             w_ref[source, :, 2 * n, :] = weight[n * heads : (n + 1) * heads]
             w_ref[source, :, 2 * n + 1, :] = rolled[n * heads : (n + 1) * heads]
     w = jnp.concatenate(
-        [w_ref[k].reshape(heads * tokens, wide)[:, :tile] for k in range(nk)], axis=1
+        [
+            w_ref[jnp.bitwise_xor(row, t)].reshape(heads * tokens, wide)[:, :tile]
+            for t in range(nk)
+        ],
+        axis=1,
     ).astype(bf16)
 
     owner = lax.broadcasted_iota(jnp.int32, (tokens, chans), 1) // head_width
@@ -684,9 +695,6 @@
         mask,
     )
 
-    every = lax.all_gather(normed, ("row", "col"), axis=0).reshape(
-        nr * nk, half, tokens, 2 * width
-    )
     all_cols = [
         lax.ppermute(
             cols,
@@ -702,15 +710,24 @@
     across = exchange(rows, 2)
     all_rows = [rows, exchange(rows, 1), across, exchange(across, 1)]
 
-    (sides,) = call(
+    sides, block = call(
         join_kernel,
-        (sds((nk * (r_rows + l_rows), 128), bf16),),
+        (
+            sds((nk * (r_rows + l_rows), 128), bf16),
+            sds((nk, half, tokens, 2 * width), bf16),
+        ),
         smem=1,
     )(place, *all_rows, *all_cols)
     if nq == 2:
         far_sides = lax.ppermute(sides, "seq", [(0, 1), (1, 0)])
     else:
         far_sides = lax.all_gather(sides, "seq", axis=0, tiled=True)
+
+    def exchange_rows(x, bit):
+        return lax.ppermute(x, "row", [(r, r ^ bit) for r in range(nr)])
+
+    beyond = exchange_rows(block, 2)
+    every = [block, exchange_rows(block, 1), beyond, exchange_rows(beyond, 1)]
 
     head_lanes = seqs * chans // heads
     (gw_own,) = call(
@@ -782,8 +799,7 @@
         (sds((half, nr * nk * tokens, 2 * chans), bf16), sds((seqs * tokens, chans), f32)),
         flops=4_000_000_000,
         nbytes=6_000_000,
-        far=(0,),
-    )(every, content_weights_grid, normed, sigmoid_weights_grid)
+    )(*every, content_weights_grid, normed, sigmoid_weights_grid)
 
     payload = sds((2 + groups // nk * (pack // 2), heads, 2 * tile_j), f32)
     gw, pay0, pay1, pay2, pay3 = call(
@@ -823,7 +839,7 @@
         flops=3_000_000_000,
         nbytes=5_000_000,
     )(
-        col_scalar,
+        place,
         pay0,
         *got,
         values,

time: 73.3 us -> 64 us (0.87)
  between operations: 14.2 us -> 0.82 us
  waiting for transfers between devices: 5.47 us -> 10.1 us
  local copies, waits for them, and re-layouts: 4.45 us -> 3.22 us
    ppermute x3, starting transfers between devices: 8.99 us -> 2.23 us  [on_device(): lax.ppermute(pay, 'col', [(c, (c + shift) % nk) for c in range(nk)])]
    ppermute x0 -> x3, starting transfers between devices: none -> 6.59 us  [exchange_rows(): return lax.ppermute(x, 'row', [(r, r ^ bit) for r in range(nr)])]
    ppermute x0 -> x3, waiting for transfers between devices: none -> 4.71 us  [exchange_rows(): return lax.ppermute(x, 'row', [(r, r ^ bit) for r in range(nr)])]
    unnamed x28 -> x26, local copies, waits for them, and re-layouts: 4.45 us -> 3.22 us
    ppermute x4, waiting for transfers between devices: 3.16 us -> 2.29 us  [on_device(): lax.ppermute(cols, ('row', 'col'), [(r * nk + c, (c + t) % nr * nk + r) f...]
    ppermute x3, waiting for transfers between devices: 0.01 us -> 0.77 us  [on_device(): lax.ppermute(pay, 'col', [(c, (c + shift) % nk) for c in range(nk)])]
  transfers between devices with their start and end apart: 13 -> 15, of which waited for: 3 -> 5; matrix products, arithmetic and copies ran while one was open for 0% -> 0% of each run, Pallas kernels for 23% -> 26%
where the time goes in v8:
time: 64 us; the launch traced here: 63.1 us
  Pallas kernels  25.8 us (40%)
  starting transfers between devices  23.1 us (36%)
  waiting for transfers between devices  10.1 us (16%)
  local copies, waits for them, and re-layouts  3.22 us (5%)
  between operations  0.82 us (1%)
    pallas_call x8, Pallas kernels, run(): pl.pallas_call(body, out_shape=out_shape, in_specs=in_specs, out_specs=[p...  25.8 us
    ppermute x4, starting transfers between devices, on_device(): lax.ppermute(cols, ('row', 'col'), [(r * nk + c, (c + t) % nr * nk + r) f...  9.27 us
    ppermute x3, starting transfers between devices, exchange_rows(): return lax.ppermute(x, 'row', [(r, r ^ bit) for r in range(nr)])  6.59 us
    ppermute x3, waiting for transfers between devices, exchange_rows(): return lax.ppermute(x, 'row', [(r, r ^ bit) for r in range(nr)])  4.71 us
    unnamed x26, local copies, waits for them, and re-layouts  3.22 us
    ppermute x3, starting transfers between devices, exchange(): return lax.ppermute(x, 'col', [(c, c ^ bit) for c in range(nk)])  2.97 us
    ppermute x4, waiting for transfers between devices, on_device(): lax.ppermute(cols, ('row', 'col'), [(r * nk + c, (c + t) % nr * nk + r) f...  2.29 us
    ppermute x3, waiting for transfers between devices, exchange(): return lax.ppermute(x, 'col', [(c, c ^ bit) for c in range(nk)])  2.28 us
  transfers between devices with their start and end apart: 15, of which 5 were waited for; matrix products, arithmetic and copies ran while one was open for 0% of the time, Pallas kernels for 26%

profile of v8, /device:TPU:0, one launch (start us, length us, event | category | flops | bytes accessed | tf_op | source)
XLA Modules:
  0.0 63.1 jit_solution(16221735666476938410)
XLA Ops:
  0.6 2.8 %shard_map.130 = (bf16[640,128]{1,0:T(8,128)(2,1)}, bf16[384,128]{1,0:T(8,128)(2,1)}, bf16[256,128]{1,0:T(8,128)(2,1)}) custom-call(s32[1]{0:T(128)} %bitcast.3.refs_0_, bf16[32,16,64]{2,1,0:T(8,128)(2,1)} %refs_1_.1, bf16[32,16,64]{2,1,0:T(8,128)(2,1)} %refs_2_.1, bf16[32,64]{1,0:T(8,128)(2,1)} %bitcast.23, bf16[32,64]{1,0:T(8,128)(2,1)} %bitcast.24, ...), custom_call_target="tpu_custom_call" | custom-call | tf_op jit(solution)/shard_map/pallas_call | solution.py:62
  3.5 3.0 %collective-permute-start.1 = (bf16[640,128]{1,0:T(8,128)(2,1)}, bf16[640,128]{1,0:T(8,128)(2,1)S(1)}, u32[]{:S(2)}, u32[]{:S(2)}) collective-permute-start(bf16[640,128]{1,0:T(8,128)(2,1)} %get-tuple-element.23.refs_1_), channel_id=1, source_target_pairs={{0,2},{1,3},{2,0},{3,1},{4,6},{5,7},{6,4},{7,5},{8,10},{9,11},{10,... | collective-permute-start | bytes 491528 | tf_op jit(solution)/shard_map/ppermute | solution.py:708
  6.4 3.6 %collective-permute-start.6 = (bf16[384,128]{1,0:T(8,128)(2,1)}, bf16[384,128]{1,0:T(8,128)(2,1)S(1)}, u32[]{:S(2)}, u32[]{:S(2)}) collective-permute-start(bf16[384,128]{1,0:T(8,128)(2,1)} %get-tuple-element.24), channel_id=1, source_target_pairs={{0,12},{1,0},{2,4},{3,8},{4,13},{5,1},{6,5},{7,9},{8,14},{9,2},{10... | collective-permute-start | bytes 294920 | tf_op jit(solution)/shard_map/ppermute | solution.py:699
  10.0 0.0 collective-permute-start
  10.0 2.3 %collective-permute-done.1.refs_3_ = bf16[640,128]{1,0:T(8,128)(2,1)S(1)} collective-permute-done((bf16[640,128]{1,0:T(8,128)(2,1)}, bf16[640,128]{1,0:T(8,128)(2,1)S(1)}, u32[]{:S(2)}, u32[]{:S(2)}) %collective-permute-start.1) | collective-permute-done | bytes 163872 | tf_op jit(solution)/shard_map/ppermute | solution.py:708
  12.3 0.0 collective-permute-start.2
  12.3 3.4 %collective-permute-start.5 = (bf16[384,128]{1,0:T(8,128)(2,1)}, bf16[384,128]{1,0:T(8,128)(2,1)S(1)}, u32[]{:S(2)}, u32[]{:S(2)}) collective-permute-start(bf16[384,128]{1,0:T(8,128)(2,1)} %get-tuple-element.24), channel_id=1, source_target_pairs={{0,8},{1,12},{2,0},{3,4},{4,9},{5,13},{6,1},{7,5},{8,10},{9,14},{1... | collective-permute-start | bytes 294920 | tf_op jit(solution)/shard_map/ppermute | solution.py:699
  15.8 0.7 %collective-permute-start.4 = (bf16[384,128]{1,0:T(8,128)(2,1)}, bf16[384,128]{1,0:T(8,128)(2,1)S(1)}, u32[]{:S(2)}, u32[]{:S(2)}) collective-permute-start(bf16[384,128]{1,0:T(8,128)(2,1)} %get-tuple-element.24), channel_id=1, source_target_pairs={{0,4},{1,8},{2,12},{3,0},{4,5},{5,9},{6,13},{7,1},{8,6},{9,10},{10... | collective-permute-start | bytes 294920 | tf_op jit(solution)/shard_map/ppermute | solution.py:699
  16.4 0.0 collective-permute-done.6.refs_8_
  16.4 1.5 %collective-permute-start.3 = (bf16[384,128]{1,0:T(8,128)(2,1)}, bf16[384,128]{1,0:T(8,128)(2,1)S(1)}, u32[]{:S(2)}, u32[]{:S(2)}) collective-permute-start(bf16[384,128]{1,0:T(8,128)(2,1)} %get-tuple-element.24), channel_id=1, source_target_pairs={{0,0},{1,4},{2,8},{3,12},{4,1},{5,5},{6,9},{7,13},{8,2},{9,6},{10,... | collective-permute-start | bytes 294920 | tf_op jit(solution)/shard_map/ppermute | solution.py:699
  18.0 0.1 pad_add_fusion.refs_0_
  18.1 0.7 %collective-permute-done.5.refs_7_ = bf16[384,128]{1,0:T(8,128)(2,1)S(1)} collective-permute-done((bf16[384,128]{1,0:T(8,128)(2,1)}, bf16[384,128]{1,0:T(8,128)(2,1)S(1)}, u32[]{:S(2)}, u32[]{:S(2)}) %collective-permute-start.5) | collective-permute-done | bytes 98336 | tf_op jit(solution)/shard_map/ppermute | solution.py:699
  18.7 1.6 %collective-permute-done.4.refs_6_ = bf16[384,128]{1,0:T(8,128)(2,1)S(1)} collective-permute-done((bf16[384,128]{1,0:T(8,128)(2,1)}, bf16[384,128]{1,0:T(8,128)(2,1)S(1)}, u32[]{:S(2)}, u32[]{:S(2)}) %collective-permute-start.4) | collective-permute-done | bytes 98336 | tf_op jit(solution)/shard_map/ppermute | solution.py:699
  20.4 0.0 collective-permute-done.3.refs_5_
  20.4 0.0 collective-permute-done.refs_2_
  20.4 0.0 collective-permute-done.2.refs_4_
  20.4 0.0 copy-start
  20.4 0.9 %copy-done = bf16[640,128]{1,0:T(8,128)(2,1)S(1)} copy-done((bf16[640,128]{1,0:T(8,128)(2,1)S(1)}, bf16[640,128]{1,0:T(8,128)(2,1)}, u32[]{:S(2)}) %copy-start) | copy-done | bytes 163864
  21.3 0.6 shard_map.131
  21.9 5.8 %collective-permute-start.13 = (bf16[4,16,16,128]{3,2,1,0:T(8,128)(2,1)S(1)}, bf16[4,16,16,128]{3,2,1,0:T(8,128)(2,1)S(1)}, u32[]{:S(2)}, u32[]{:S(2)}) collective-permute-start(bf16[4,16,16,128]{3,2,1,0:T(8,128)(2,1)S(1)} %get-tuple-element.31.refs_0_), channel_id=1, source_target_pairs={{0,8},{4,12},{8,0},{12,4},{1,9},{5,13},{9,1},{13,5},{2,10},{6,14},... | collective-permute-start | bytes 786440 | tf_op jit(solution)/shard_map/ppermute | solution.py:727
  27.7 0.6 %collective-permute-start.12 = (bf16[4,16,16,128]{3,2,1,0:T(8,128)(2,1)S(1)}, bf16[4,16,16,128]{3,2,1,0:T(8,128)(2,1)S(1)}, u32[]{:S(2)}, u32[]{:S(2)}) collective-permute-start(bf16[4,16,16,128]{3,2,1,0:T(8,128)(2,1)S(1)} %get-tuple-element.31.refs_0_), channel_id=1, source_target_pairs={{0,4},{4,0},{8,12},{12,8},{1,5},{5,1},{9,13},{13,9},{2,6},{6,2},{1... | collective-permute-start | bytes 786440 | tf_op jit(solution)/shard_map/ppermute | solution.py:727
  28.3 1.5 %collective-permute-start.7 = (bf16[1024,128]{1,0:T(8,128)(2,1)S(1)}, bf16[1024,128]{1,0:T(8,128)(2,1)S(1)}, u32[]{:S(2)}, u32[]{:S(2)}) collective-permute-start(bf16[1024,128]{1,0:T(8,128)(2,1)S(1)} %get-tuple-element.25.refs_1_), channel_id=1, source_target_pairs={{0,16},{16,0},{1,17},{17,1},{2,18},{18,2},{3,19},{19,3},{4,20},{20... | collective-permute-start | bytes 786440 | tf_op jit(solution)/shard_map/ppermute | solution.py:722
  29.8 0.0 copy-start.6
  29.8 0.8 %copy-done.6 = bf16[64,256]{1,0:T(8,128)(2,1)S(1)} copy-done((bf16[64,256]{1,0:T(8,128)(2,1)S(1)}, bf16[64,256]{1,0:T(8,128)(2,1)}, u32[]{:S(2)}) %copy-start.6) | copy-done | bytes 32792
  30.5 0.0 copy-start.8
  30.5 0.8 %copy-done.8 = bf16[64,256]{1,0:T(8,128)(2,1)S(1)} copy-done((bf16[64,256]{1,0:T(8,128)(2,1)S(1)}, bf16[64,256]{1,0:T(8,128)(2,1)}, u32[]{:S(2)}) %copy-start.8) | copy-done | bytes 32792
  31.3 0.0 copy-start.10
  31.3 0.8 %copy-done.10 = bf16[256,64]{0,1:T(8,128)(2,1)S(1)} copy-done((bf16[256,64]{0,1:T(8,128)(2,1)S(1)}, bf16[256,64]{0,1:T(8,128)(2,1)}, u32[]{:S(2)}) %copy-start.10) | copy-done | bytes 32792
  32.0 0.0 copy-start.2
  32.0 0.0 copy-start.3
  32.0 0.0 copy-start.4
  32.1 0.0 copy-start.12
  32.1 3.0 %shard_map.133.refs_2_ = f32[16,8,256]{2,1,0:T(8,128)S(1)} custom-call(s32[3]{0:T(128)S(1)} %pad_add_fusion.refs_0_, bf16[640,128]{1,0:T(8,128)(2,1)S(1)} %copy-done, bf16[640,128]{1,0:T(8,128)(2,1)S(1)} %collective-permute-done.refs_2_, bf16[640,128]{1,0:T(8,128)(2,1)S(1)} %collective-permute-done.1.refs_3_, ...), custom_call_target="tpu_custom_call" | custom-call | flops 3000000000 | bytes 3000000 | tf_op jit(solution)/shard_map/pallas_call | solution.py:62
  35.0 0.6 collective-permute-start.8
  35.7 4.7 %collective-permute-done.13.refs_2_ = bf16[4,16,16,128]{3,2,1,0:T(8,128)(2,1)S(1)} collective-permute-done((bf16[4,16,16,128]{3,2,1,0:T(8,128)(2,1)S(1)}, bf16[4,16,16,128]{3,2,1,0:T(8,128)(2,1)S(1)}, u32[]{:S(2)}, u32[]{:S(2)}) %collective-permute-start.13) | collective-permute-done | bytes 262176 | tf_op jit(solution)/shard_map/ppermute | solution.py:727
  40.4 0.1 collective-permute-start.14
  40.5 0.0 collective-permute-done.7.refs_2_
  40.5 0.0 copy-done.2
  40.5 0.0 copy-done.3
  40.5 0.0 copy-done.4
  40.5 0.0 copy-done.12
  40.6 0.0 copy-start.5
  40.6 0.0 copy-start.7
  40.6 0.0 copy-start.9
  40.6 11.5 %shard_map.132 = (bf16[4096,128]{1,0:T(8,128)(2,1)}, bf16[16,128,256]{2,1,0:T(8,128)(2,1)S(1)}, f32[16,8,256]{2,1,0:T(8,128)S(1)}) custom-call(s32[3]{0:T(128)S(1)} %pad_add_fusion.refs_0_, bf16[1024,128]{1,0:T(8,128)(2,1)S(1)} %get-tuple-element.25.refs_1_, bf16[1024,128]{1,0:T(8,128)(2,1)S(1)} %collective-permute-done.7.refs_2_, s32[1,256]{1,0:T(1,128)S(1)} %bitcast.16, ...), custom_call_target="tpu_custom_call" | custom-call | flops 14000000000 | bytes 5000000 | tf_op jit(solution)/shard_map/pallas_call | solution.py:62
  52.1 0.0 collective-permute-done.8.refs_3_
  52.1 0.5 shard_map.134
  52.6 0.0 collective-permute-start.9
  52.6 0.8 %collective-permute-start.10 = (f32[10,8,128]{2,1,0:T(8,128)S(1)}, f32[10,8,128]{2,1,0:T(8,128)S(1)}, u32[]{:S(2)}, u32[]{:S(2)}) collective-permute-start(f32[10,8,128]{2,1,0:T(8,128)S(1)} %get-tuple-element.29), channel_id=1, source_target_pairs={{0,2},{1,3},{2,0},{3,1},{4,6},{5,7},{6,4},{7,5},{8,10},{9,11},{10,... | collective-permute-start | bytes 122888 | tf_op jit(solution)/shard_map/ppermute | solution.py:812
  53.4 1.4 %collective-permute-start.11 = (f32[10,8,128]{2,1,0:T(8,128)S(1)}, f32[10,8,128]{2,1,0:T(8,128)S(1)}, u32[]{:S(2)}, u32[]{:S(2)}) collective-permute-start(f32[10,8,128]{2,1,0:T(8,128)S(1)} %get-tuple-element.30), channel_id=1, source_target_pairs={{0,3},{1,0},{2,1},{3,2},{4,7},{5,4},{6,5},{7,6},{8,11},{9,8},{10,9... | collective-permute-start | bytes 122888 | tf_op jit(solution)/shard_map/ppermute | solution.py:812
  54.8 0.0 collective-permute-done.12.refs_1_
  54.8 0.0 collective-permute-done.14.refs_3_
  54.8 0.0 copy-done.5
  54.8 0.0 copy-done.7
  54.8 0.0 copy-done.9
  54.8 1.3 %shard_map.135 = (bf16[16,256,512]{2,1,0:T(8,128)(2,1)S(1)}, f32[512,256]{1,0:T(8,128)S(1)}) custom-call(bf16[4,16,16,128]{3,2,1,0:T(8,128)(2,1)S(1)} %get-tuple-element.31.refs_0_, bf16[4,16,16,128]{3,2,1,0:T(8,128)(2,1)S(1)} %collective-permute-done.12.refs_1_, bf16[4,16,16,128]{3,2,1,0:T(8,128)(2,1)S(1)} %collective-permute-done.13.refs_2_, ...), custom_call_target="tpu_custom_call" | custom-call | flops 4000000000 | bytes 6000000 | tf_op jit(solution)/shard_map/pallas_call | solution.py:62
  56.2 0.0 collective-permute-done.9.refs_2_.refs_1_
  56.2 0.8 %collective-permute-done.10.refs_3_.refs_2_ = f32[10,8,128]{2,1,0:T(8,128)S(1)} collective-permute-done((f32[10,8,128]{2,1,0:T(8,128)S(1)}, f32[10,8,128]{2,1,0:T(8,128)S(1)}, u32[]{:S(2)}, u32[]{:S(2)}) %collective-permute-start.10) | collective-permute-done | bytes 40992 | tf_op jit(solution)/shard_map/ppermute | solution.py:812
  56.9 0.0 collective-permute-done.11.refs_4_.refs_3_
  56.9 0.0 copy-start.1
  56.9 3.1 %shard_map.137 = bf16[4096,128]{1,0:T(8,128)(2,1)} custom-call(f32[10,8,128]{2,1,0:T(8,128)S(1)} %get-tuple-element.27.refs_1_.refs_0_, f32[10,8,128]{2,1,0:T(8,128)S(1)} %collective-permute-done.9.refs_2_.refs_1_, f32[10,8,128]{2,1,0:T(8,128)S(1)} %collective-permute-done.10.refs_3_.refs_2_, f32[10,8,128]{2,1,0:T(8,128)S(1)} %collective-permute-done.11.refs_4_.refs_3_, ...), custom_call_target="tpu_custom_call" | custom-call | flops 4000000000 | bytes 3000000 | tf_op jit(solution)/shard_map/pallas_call | solution.py:62
  60.0 0.0 copy-done.1
  60.0 0.0 copy-done.11
  60.0 3.1 %shard_map.136 = bf16[512,64]{1,0:T(8,128)(2,1)} custom-call(s32[3]{0:T(128)S(1)} %pad_add_fusion.refs_0_, f32[10,8,128]{2,1,0:T(8,128)S(1)} %get-tuple-element.27.refs_1_.refs_0_, f32[10,8,128]{2,1,0:T(8,128)S(1)} %collective-permute-done.9.refs_2_.refs_1_, f32[10,8,128]{2,1,0:T(8,128)S(1)} %collective-permute-done.10.refs_3_.refs_2_, ...), custom_call_target="tpu_custom_call" | custom-call | flops 3000000000 | bytes 5000000 | tf_op jit(solution)/shard_map/pallas_call | solution.py:62
  (1 shorter events, 0.0 us)
Async XLA Ops:
  3.5 8.8 %collective-permute-start.1 = (bf16[640,128]{1,0:T(8,128)(2,1)}, bf16[640,128]{1,0:T(8,128)(2,1)S(1)}, u32[]{:S(2)}, u32[]{:S(2)}) collective-permute-start(bf16[640,128]{1,0:T(8,128)(2,1)} %get-tuple-element.23.refs_1_), channel_id=1, source_target_pairs={{0,2},{1,3},{2,0},{3,1},{4,6},{5,7},{6,4},{7,5},{8,10},{9,11},{10,... | collective-permute-start | bytes 491528 | tf_op jit(solution)/shard_map/ppermute | solution.py:708
  6.4 10.0 %collective-permute-start.6 = (bf16[384,128]{1,0:T(8,128)(2,1)}, bf16[384,128]{1,0:T(8,128)(2,1)S(1)}, u32[]{:S(2)}, u32[]{:S(2)}) collective-permute-start(bf16[384,128]{1,0:T(8,128)(2,1)} %get-tuple-element.24), channel_id=1, source_target_pairs={{0,12},{1,0},{2,4},{3,8},{4,13},{5,1},{6,5},{7,9},{8,14},{9,2},{10... | collective-permute-start | bytes 294920 | tf_op jit(solution)/shard_map/ppermute | solution.py:699
  10.0 10.3 %collective-permute-start = (bf16[640,128]{1,0:T(8,128)(2,1)}, bf16[640,128]{1,0:T(8,128)(2,1)S(1)}, u32[]{:S(2)}, u32[]{:S(2)}) collective-permute-start(bf16[640,128]{1,0:T(8,128)(2,1)} %get-tuple-element.23.refs_1_), channel_id=1, source_target_pairs={{0,1},{1,0},{2,3},{3,2},{4,5},{5,4},{6,7},{7,6},{8,9},{9,8},{10,11... | collective-permute-start | bytes 491528 | tf_op jit(solution)/shard_map/ppermute | solution.py:708
  12.3 8.0 %collective-permute-start.2 = (bf16[640,128]{1,0:T(8,128)(2,1)S(1)}, bf16[640,128]{1,0:T(8,128)(2,1)S(1)}, u32[]{:S(2)}, u32[]{:S(2)}) collective-permute-start(bf16[640,128]{1,0:T(8,128)(2,1)S(1)} %collective-permute-done.1.refs_3_), channel_id=1, source_target_pairs={{0,1},{1,0},{2,3},{3,2},{4,5},{5,4},{6,7},{7,6},{8,9},{9,8},{10,11... | collective-permute-start | bytes 491528 | tf_op jit(solution)/shard_map/ppermute | solution.py:708
  12.3 6.4 %collective-permute-start.5 = (bf16[384,128]{1,0:T(8,128)(2,1)}, bf16[384,128]{1,0:T(8,128)(2,1)S(1)}, u32[]{:S(2)}, u32[]{:S(2)}) collective-permute-start(bf16[384,128]{1,0:T(8,128)(2,1)} %get-tuple-element.24), channel_id=1, source_target_pairs={{0,8},{1,12},{2,0},{3,4},{4,9},{5,13},{6,1},{7,5},{8,10},{9,14},{1... | collective-permute-start | bytes 294920 | tf_op jit(solution)/shard_map/ppermute | solution.py:699
  15.8 4.6 %collective-permute-start.4 = (bf16[384,128]{1,0:T(8,128)(2,1)}, bf16[384,128]{1,0:T(8,128)(2,1)S(1)}, u32[]{:S(2)}, u32[]{:S(2)}) collective-permute-start(bf16[384,128]{1,0:T(8,128)(2,1)} %get-tuple-element.24), channel_id=1, source_target_pairs={{0,4},{1,8},{2,12},{3,0},{4,5},{5,9},{6,13},{7,1},{8,6},{9,10},{10... | collective-permute-start | bytes 294920 | tf_op jit(solution)/shard_map/ppermute | solution.py:699
  16.4 3.9 %collective-permute-start.3 = (bf16[384,128]{1,0:T(8,128)(2,1)}, bf16[384,128]{1,0:T(8,128)(2,1)S(1)}, u32[]{:S(2)}, u32[]{:S(2)}) collective-permute-start(bf16[384,128]{1,0:T(8,128)(2,1)} %get-tuple-element.24), channel_id=1, source_target_pairs={{0,0},{1,4},{2,8},{3,12},{4,1},{5,5},{6,9},{7,13},{8,2},{9,6},{10,... | collective-permute-start | bytes 294920 | tf_op jit(solution)/shard_map/ppermute | solution.py:699
  20.4 0.9 %copy-start = (bf16[640,128]{1,0:T(8,128)(2,1)S(1)}, bf16[640,128]{1,0:T(8,128)(2,1)}, u32[]{:S(2)}) copy-start(bf16[640,128]{1,0:T(8,128)(2,1)} %get-tuple-element.23.refs_1_) | copy-start | bytes 491524
  21.9 18.5 %collective-permute-start.13 = (bf16[4,16,16,128]{3,2,1,0:T(8,128)(2,1)S(1)}, bf16[4,16,16,128]{3,2,1,0:T(8,128)(2,1)S(1)}, u32[]{:S(2)}, u32[]{:S(2)}) collective-permute-start(bf16[4,16,16,128]{3,2,1,0:T(8,128)(2,1)S(1)} %get-tuple-element.31.refs_0_), channel_id=1, source_target_pairs={{0,8},{4,12},{8,0},{12,4},{1,9},{5,13},{9,1},{13,5},{2,10},{6,14},... | collective-permute-start | bytes 786440 | tf_op jit(solution)/shard_map/ppermute | solution.py:727
  27.7 27.1 %collective-permute-start.12 = (bf16[4,16,16,128]{3,2,1,0:T(8,128)(2,1)S(1)}, bf16[4,16,16,128]{3,2,1,0:T(8,128)(2,1)S(1)}, u32[]{:S(2)}, u32[]{:S(2)}) collective-permute-start(bf16[4,16,16,128]{3,2,1,0:T(8,128)(2,1)S(1)} %get-tuple-element.31.refs_0_), channel_id=1, source_target_pairs={{0,4},{4,0},{8,12},{12,8},{1,5},{5,1},{9,13},{13,9},{2,6},{6,2},{1... | collective-permute-start | bytes 786440 | tf_op jit(solution)/shard_map/ppermute | solution.py:727
  28.3 12.2 %collective-permute-start.7 = (bf16[1024,128]{1,0:T(8,128)(2,1)S(1)}, bf16[1024,128]{1,0:T(8,128)(2,1)S(1)}, u32[]{:S(2)}, u32[]{:S(2)}) collective-permute-start(bf16[1024,128]{1,0:T(8,128)(2,1)S(1)} %get-tuple-element.25.refs_1_), channel_id=1, source_target_pairs={{0,16},{16,0},{1,17},{17,1},{2,18},{18,2},{3,19},{19,3},{4,20},{20... | collective-permute-start | bytes 786440 | tf_op jit(solution)/shard_map/ppermute | solution.py:722
  29.8 0.8 %copy-start.6 = (bf16[64,256]{1,0:T(8,128)(2,1)S(1)}, bf16[64,256]{1,0:T(8,128)(2,1)}, u32[]{:S(2)}) copy-start(bf16[64,256]{1,0:T(8,128)(2,1)} %refs_4_.3) | copy-start | bytes 98308
  30.5 0.8 %copy-start.8 = (bf16[64,256]{1,0:T(8,128)(2,1)S(1)}, bf16[64,256]{1,0:T(8,128)(2,1)}, u32[]{:S(2)}) copy-start(bf16[64,256]{1,0:T(8,128)(2,1)} %refs_6_.1) | copy-start | bytes 98308
  31.3 0.8 %copy-start.10 = (bf16[256,64]{0,1:T(8,128)(2,1)S(1)}, bf16[256,64]{0,1:T(8,128)(2,1)}, u32[]{:S(2)}) copy-start(bf16[256,64]{0,1:T(8,128)(2,1)} %param.20) | copy-start | bytes 98308
  32.0 8.5 %copy-start.2 = (s32[256]{0:T(256)S(1)}, s32[256]{0:T(256)}, u32[]{:S(2)}) copy-start(s32[256]{0:T(256)} %param.13) | copy-start | bytes 3076
  32.0 8.5 %copy-start.3 = (bf16[64,64,128]{2,1,0:T(8,128)(2,1)S(1)}, bf16[64,64,128]{2,1,0:T(8,128)(2,1)}, u32[]{:S(2)}) copy-start(bf16[64,64,128]{2,1,0:T(8,128)(2,1)} %param.12) | copy-start | bytes 3145732
  32.0 8.5 %copy-start.4 = (f32[1024,128]{1,0:T(8,128)S(1)}, f32[1024,128]{1,0:T(8,128)}, u32[]{:S(2)}) copy-start(f32[1024,128]{1,0:T(8,128)} %refs_4_.2) | copy-start | bytes 1572868
  32.1 8.5 %copy-start.12 = (f32[128,8]{0,1:T(8,128)S(1)}, f32[128,8]{0,1:T(8,128)}, u32[]{:S(2)}) copy-start(f32[128,8]{0,1:T(8,128)} %param.19) | copy-start | bytes 12292
  35.0 17.1 %collective-permute-start.8 = (f32[16,8,256]{2,1,0:T(8,128)S(1)}, f32[16,8,256]{2,1,0:T(8,128)S(1)}, u32[]{:S(2)}, u32[]{:S(2)}) collective-permute-start(f32[16,8,256]{2,1,0:T(8,128)S(1)} %shard_map.133.refs_2_), channel_id=1, source_target_pairs={{0,16},{16,0},{1,17},{17,1},{2,18},{18,2},{3,19},{19,3},{4,20},{20... | collective-permute-start | bytes 393224 | tf_op jit(solution)/shard_map/ppermute | solution.py:759
  40.4 14.4 %collective-permute-start.14 = (bf16[4,16,16,128]{3,2,1,0:T(8,128)(2,1)S(1)}, bf16[4,16,16,128]{3,2,1,0:T(8,128)(2,1)S(1)}, u32[]{:S(2)}, u32[]{:S(2)}) collective-permute-start(bf16[4,16,16,128]{3,2,1,0:T(8,128)(2,1)S(1)} %collective-permute-done.13.refs_2_), channel_id=1, source_target_pairs={{0,4},{4,0},{8,12},{12,8},{1,5},{5,1},{9,13},{13,9},{2,6},{6,2},{1... | collective-permute-start | bytes 786440 | tf_op jit(solution)/shard_map/ppermute | solution.py:727
  40.6 14.3 %copy-start.5 = (bf16[256,128]{1,0:T(8,128)(2,1)S(1)}, bf16[256,128]{1,0:T(8,128)(2,1)}, u32[]{:S(2)}) copy-start(bf16[256,128]{1,0:T(8,128)(2,1)} %get-tuple-element.32.refs_5_) | copy-start | bytes 196612
  40.6 14.3 %copy-start.7 = (bf16[64,256]{1,0:T(8,128)(2,1)S(1)}, bf16[64,256]{1,0:T(8,128)(2,1)}, u32[]{:S(2)}) copy-start(bf16[64,256]{1,0:T(8,128)(2,1)} %refs_4_.3) | copy-start | bytes 98308
  40.6 14.3 %copy-start.9 = (bf16[64,256]{1,0:T(8,128)(2,1)S(1)}, bf16[64,256]{1,0:T(8,128)(2,1)}, u32[]{:S(2)}) copy-start(bf16[64,256]{1,0:T(8,128)(2,1)} %refs_6_.1) | copy-start | bytes 98308
  52.6 3.6 %collective-permute-start.9 = (f32[10,8,128]{2,1,0:T(8,128)S(1)}, f32[10,8,128]{2,1,0:T(8,128)S(1)}, u32[]{:S(2)}, u32[]{:S(2)}) collective-permute-start(f32[10,8,128]{2,1,0:T(8,128)S(1)} %get-tuple-element.28), channel_id=1, source_target_pairs={{0,1},{1,2},{2,3},{3,0},{4,5},{5,6},{6,7},{7,4},{8,9},{9,10},{10,1... | collective-permute-start | bytes 122888 | tf_op jit(solution)/shard_map/ppermute | solution.py:812
  52.6 4.3 %collective-permute-start.10 = (f32[10,8,128]{2,1,0:T(8,128)S(1)}, f32[10,8,128]{2,1,0:T(8,128)S(1)}, u32[]{:S(2)}, u32[]{:S(2)}) collective-permute-start(f32[10,8,128]{2,1,0:T(8,128)S(1)} %get-tuple-element.29), channel_id=1, source_target_pairs={{0,2},{1,3},{2,0},{3,1},{4,6},{5,7},{6,4},{7,5},{8,10},{9,11},{10,... | collective-permute-start | bytes 122888 | tf_op jit(solution)/shard_map/ppermute | solution.py:812
  53.4 3.5 %collective-permute-start.11 = (f32[10,8,128]{2,1,0:T(8,128)S(1)}, f32[10,8,128]{2,1,0:T(8,128)S(1)}, u32[]{:S(2)}, u32[]{:S(2)}) collective-permute-start(f32[10,8,128]{2,1,0:T(8,128)S(1)} %get-tuple-element.30), channel_id=1, source_target_pairs={{0,3},{1,0},{2,1},{3,2},{4,7},{5,4},{6,5},{7,6},{8,11},{9,8},{10,9... | collective-permute-start | bytes 122888 | tf_op jit(solution)/shard_map/ppermute | solution.py:812
  56.9 3.1 %copy-start.1 = (bf16[32,16,64]{2,1,0:T(8,128)(2,1)S(1)}, bf16[32,16,64]{2,1,0:T(8,128)(2,1)}, u32[]{:S(2)}) copy-start(bf16[32,16,64]{2,1,0:T(8,128)(2,1)} %refs_1_.1) | copy-start | bytes 196612
  56.9 3.1 %copy-start.11 = (bf16[256,64]{0,1:T(8,128)(2,1)S(1)}, bf16[256,64]{0,1:T(8,128)(2,1)}, u32[]{:S(2)}) copy-start(bf16[256,64]{0,1:T(8,128)(2,1)} %param.20) | copy-start | bytes 98308

commit v9 on v8

--- a/solution.py
+++ b/solution.py
@@ -100,12 +100,20 @@
     w1_ref,
     w2_ref,
     mask_ref,
+    wv_ref,
+    wg_ref,
+    wf_ref,
     rows_ref,
     cols_ref,
     norm_ref,
+    weights_ref,
     turn_ref,
     place_ref,
 ):
+    chans = wv_ref.shape[1]
+    weights_ref[:, :chans] = wv_ref[...]
+    weights_ref[:, chans : 2 * chans] = wg_ref[...]
+    weights_ref[:, 2 * chans :] = wf_ref[...]
     seqs, tokens, width = x_ref.shape
     half = seqs // 2
     fd = w2_ref.shape[0]
@@ -151,7 +159,8 @@
 
 def join_kernel(
     ready,
-    place_ref,
+    row_ref,
+    col_ref,
     rows0_ref,
     rows1_ref,
     rows2_ref,
@@ -164,7 +173,7 @@
     norm_ref,
 ):
     nk = 4
-    row, col = place_ref[0], place_ref[1]
+    row, col = row_ref[0], col_ref[0]
     r_rows = l_rows = out_ref.shape[0] // (2 * nk)
     for t, ref in enumerate((cols0_ref, cols1_ref, cols2_ref, cols3_ref)):
         at = pl.ds(pl.multiple_of(lax.rem(row + nk - t, nk) * r_rows, r_rows), r_rows)
@@ -181,7 +190,8 @@
 
 def update_kernel(
     ready,
-    place_ref,
+    col_ref,
+    seq_ref,
     sides_ref,
     far_sides_ref,
     mask_ref,
@@ -203,7 +213,7 @@
 ):
     nk = rk_ref.shape[0]
     width_d, pair_rows, _ = rab_ref.shape
-    col, seq = place_ref[1], place_ref[2]
+    col, seq = col_ref[0], seq_ref[0]
     z = pair_ref.shape[1]
     groups, heads, lanes = logits_ref.shape
     tile_j = lanes // pack
@@ -307,11 +317,11 @@
         for e in range(wide):
             g = n * wide + e
             at = pl.ds(pl.multiple_of(g * lanes, lanes), lanes)
-            before = pair_ref[at, :].astype(f32).T
+            before = pair_ref[at, :].T.astype(f32)
             result = (before + update_ref[:, e * lanes : (e + 1) * lanes]).astype(bf16)
             pout_t_ref[g] = result
             x = result.astype(f32)
-            pout_ref[at, :] = x.T.astype(bf16)
+            pout_ref[at, :] = result.T
             center = x - jnp.mean(x, axis=0, keepdims=True)
             inverse = lax.rsqrt(jnp.mean(center * center, axis=0, keepdims=True) + epsilon)
             high, low = high_low(center * inverse)
@@ -347,7 +357,8 @@
 
 def weights_kernel(
     ready,
-    place_ref,
+    row_ref,
+    col_ref,
     side0_ref,
     side1_ref,
     side2_ref,
@@ -356,9 +367,7 @@
     cols1_ref,
     cols2_ref,
     cols3_ref,
-    wv_ref,
-    wg_ref,
-    wf_ref,
+    weights_ref,
     gw_ref,
     acc_ref,
     bv_ref,
@@ -372,7 +381,7 @@
     nk, half, tokens, _ = cols_ref.shape
     tile = nk * tokens
     groups, heads, lanes = gw_ref.shape
-    row, col = place_ref[0], place_ref[1]
+    row, col = row_ref[0], col_ref[0]
     count = half * tokens
     for t, ref in enumerate((side0_ref, side1_ref, side2_ref, side3_ref)):
         start = ref.shape[0] - 2 * count
@@ -380,10 +389,10 @@
     for t, ref in enumerate((cols0_ref, cols1_ref, cols2_ref, cols3_ref)):
         start = ref.shape[0] - count
         cols_ref[lax.rem(row + nk - t, nk)] = ref[start:, :].reshape(cols_ref.shape[1:])
-    ready()
-    by_heads(wv_ref[...], heads, bv_ref)
-    by_heads(wg_ref[...], heads, bg_ref)
-    by_heads(wf_ref[...], heads, bf_ref)
+    chans = weights_ref.shape[1] // 3
+    by_heads(weights_ref[:, :chans], heads, bv_ref)
+    by_heads(weights_ref[:, chans : 2 * chans], heads, bg_ref)
+    by_heads(weights_ref[:, 2 * chans :], heads, bf_ref)
     block = bv_ref.shape[1] // heads
 
     def four(read, n):
@@ -548,7 +557,7 @@
         centered = grad - jnp.mean(grad, axis=0, keepdims=True)
         along = jnp.mean(grad * normal, axis=0, keepdims=True)
         result = inverse * (centered - normal * along)
-        out_ref[pl.ds(pl.multiple_of(g * lanes, lanes), lanes), :] = result.T.astype(bf16)
+        out_ref[pl.ds(pl.multiple_of(g * lanes, lanes), lanes), :] = result.astype(bf16).T
 
     many = 4
 
@@ -567,7 +576,8 @@
 
 def alignment_kernel(
     ready,
-    place_ref,
+    row_ref,
+    col_ref,
     own_ref,
     r1_ref,
     r2_ref,
@@ -591,7 +601,7 @@
     chans = chans // 2
     tokens = pieces * 2
     head_width = chans // heads
-    row, col = place_ref[0], place_ref[1]
+    row, col = row_ref[0], col_ref[0]
 
     low = lax.broadcasted_iota(jnp.int32, (rows, wide), 1) < tile
     lgs = [p[2:].reshape(rows, wide) for p in pays]
@@ -666,19 +676,20 @@
     mask = token_valid_mask.reshape(1, -1)
     own_start = ((row_index * nk + col_index) * tokens).astype(jnp.int32).reshape(1)
     seq_index = lax.axis_index("seq")
-    place = jnp.stack([row_index, col_index, seq_index]).astype(jnp.int32)
+    place = tuple(x.astype(jnp.int32).reshape(1) for x in (row_index, col_index, seq_index))
     col_scalar = col_index.astype(jnp.int32).reshape(1)
     half = seqs // 2
 
     l_rows = tokens // pack * fc
     r_rows = fd * tokens // 128 * seqs
     n_rows = half * tokens
-    rows, cols, normed = call(
+    rows, cols, normed, weights = call(
         prepare_kernel,
         (
             sds((l_rows + 2 * n_rows, 128), bf16),
             sds((r_rows + n_rows, 128), bf16),
             sds((n_rows, 128), bf16),
+            sds((width, 3 * chans), bf16),
         ),
         scratch=(
             pltpu.VMEM((tokens, seqs, width), f32),
@@ -693,6 +704,9 @@
         first_factor_weights.T,
         second_factor_weights.T,
         mask,
+        content_weights_grid,
+        sigmoid_weights_grid,
+        final_mixing_weights.T,
     )
 
     all_cols = [
@@ -716,18 +730,12 @@
             sds((nk * (r_rows + l_rows), 128), bf16),
             sds((nk, half, tokens, 2 * width), bf16),
         ),
-        smem=1,
-    )(place, *all_rows, *all_cols)
+        smem=2,
+    )(*place[:2], *all_rows, *all_cols)
     if nq == 2:
         far_sides = lax.ppermute(sides, "seq", [(0, 1), (1, 0)])
     else:
         far_sides = lax.all_gather(sides, "seq", axis=0, tiled=True)
-
-    def exchange_rows(x, bit):
-        return lax.ppermute(x, "row", [(r, r ^ bit) for r in range(nr)])
-
-    beyond = exchange_rows(block, 2)
-    every = [block, exchange_rows(block, 1), beyond, exchange_rows(beyond, 1)]
 
     head_lanes = seqs * chans // heads
     (gw_own,) = call(
@@ -743,22 +751,20 @@
             pltpu.VMEM((heads, tile_i, head_lanes), bf16),
             pltpu.VMEM((heads, 2 * tile_j, head_lanes), bf16),
         ),
-        smem=1,
+        smem=2,
         flops=3_000_000_000,
         nbytes=3_000_000,
-        far=(9, 10, 11),
-    )(
-        place,
-        *all_rows,
-        *all_cols,
-        content_weights_grid,
-        sigmoid_weights_grid,
-        final_mixing_weights.T,
-    )
+    )(*place[:2], *all_rows, *all_cols, weights)
     if nq == 2:
         gw_other = lax.ppermute(gw_own, "seq", [(0, 1), (1, 0)])
     else:
         gw_own, gw_other = lax.psum(gw_own, "seq"), jnp.zeros_like(gw_own)
+
+    def exchange_rows(x, bit):
+        return lax.ppermute(x, "row", [(r, r ^ bit) for r in range(nr)])
+
+    block, gw_own = lax.optimization_barrier((block, gw_own))
+    near, beyond = exchange_rows(block, 1), exchange_rows(block, 2)
 
     pair_out, pair_t, logits = call(
         update_kernel,
@@ -778,14 +784,14 @@
             pltpu.VMEM((groups // 4, fd * fc, 4 * lanes), bf16),
             pltpu.VMEM((z, 4 * lanes), f32),
         ),
-        smem=1,
+        smem=2,
         flops=14_000_000_000,
         nbytes=5_000_000,
         vmem=44 * 1024 * 1024,
-        far=(3, 4, 5, 6),
+        far=(4, 5, 6, 7),
         far_out=(0,),
     )(
-        place,
+        *place[1:],
         sides,
         far_sides,
         mask,
@@ -794,6 +800,8 @@
         pair_input.reshape(tile_i * tile_j, z),
     )
 
+    beyond, logits = lax.optimization_barrier((beyond, logits))
+    every = [block, near, beyond, exchange_rows(beyond, 1)]
     values, gating = call(
         values_kernel,
         (sds((half, nr * nk * tokens, 2 * chans), bf16), sds((seqs * tokens, chans), f32)),
@@ -835,11 +843,11 @@
             pltpu.VMEM((nk, heads, tokens, 2 * tile_j), f32),
             pltpu.VMEM((seqs * tokens, chans), bf16),
         ),
-        smem=1,
+        smem=2,
         flops=3_000_000_000,
         nbytes=5_000_000,
     )(
-        place,
+        *place[:2],
         pay0,
         *got,
         values,

time: 64 us -> 60.1 us (0.939)
  Pallas kernels: 25.8 us -> 23.5 us
  starting transfers between devices: 23.1 us -> 25.4 us
  waiting for transfers between devices: 10.1 us -> 8.01 us
  local copies, waits for them, and re-layouts: 3.22 us -> 1.85 us
    ppermute x3, waiting for transfers between devices: 4.71 us -> 0.01 us  [exchange_rows(): return lax.ppermute(x, 'row', [(r, r ^ bit) for r in range(nr)])]
    ppermute x1, waiting for transfers between devices: 0.01 us -> 4.4 us  [on_device(): gw_other = lax.ppermute(gw_own, 'seq', [(0, 1), (1, 0)])]
    pallas_call x8, Pallas kernels: 25.8 us -> 23.5 us  [run(): pl.pallas_call(body, out_shape=out_shape, in_specs=in_specs, out_specs=[p...]
    ppermute x3, starting transfers between devices: 2.97 us -> 5.09 us  [exchange(): return lax.ppermute(x, 'col', [(c, c ^ bit) for c in range(nk)])]
    ppermute x3, starting transfers between devices: 6.59 us -> 4.89 us  [exchange_rows(): return lax.ppermute(x, 'row', [(r, r ^ bit) for r in range(nr)])]
    ppermute x3, waiting for transfers between devices: 2.28 us -> 0.75 us  [exchange(): return lax.ppermute(x, 'col', [(c, c ^ bit) for c in range(nk)])]
    unnamed x26 -> x22, local copies, waits for them, and re-layouts: 3.22 us -> 1.85 us
    ppermute x4, starting transfers between devices: 9.27 us -> 10.3 us  [on_device(): lax.ppermute(cols, ('row', 'col'), [(r * nk + c, (c + t) % nr * nk + r) f...]
  transfers between devices with their start and end apart: 15 -> 15, of which waited for: 5 -> 4; matrix products, arithmetic and copies ran while one was open for 0% -> 0% of each run, Pallas kernels for 26% -> 25%
where the time goes in v9:
time: 60.1 us; the launch traced here: 59.5 us
  starting transfers between devices  25.4 us (42%)
  Pallas kernels  23.5 us (39%)
  waiting for transfers between devices  8.01 us (13%)
  local copies, waits for them, and re-layouts  1.85 us (3%)
  between operations  0.81 us (1%)
    pallas_call x8, Pallas kernels, run(): pl.pallas_call(body, out_shape=out_shape, in_specs=in_specs, out_specs=[p...  23.5 us
    ppermute x4, starting transfers between devices, on_device(): lax.ppermute(cols, ('row', 'col'), [(r * nk + c, (c + t) % nr * nk + r) f...  10.3 us
    ppermute x3, starting transfers between devices, exchange(): return lax.ppermute(x, 'col', [(c, c ^ bit) for c in range(nk)])  5.09 us
    ppermute x3, starting transfers between devices, exchange_rows(): return lax.ppermute(x, 'row', [(r, r ^ bit) for r in range(nr)])  4.89 us
    ppermute x1, waiting for transfers between devices, on_device(): gw_other = lax.ppermute(gw_own, 'seq', [(0, 1), (1, 0)])  4.4 us
    ppermute x3, starting transfers between devices, on_device(): lax.ppermute(pay, 'col', [(c, (c + shift) % nk) for c in range(nk)])  2.95 us
    ppermute x4, waiting for transfers between devices, on_device(): lax.ppermute(cols, ('row', 'col'), [(r * nk + c, (c + t) % nr * nk + r) f...  2.53 us
    unnamed x22, local copies, waits for them, and re-layouts  1.85 us
  transfers between devices with their start and end apart: 15, of which 4 were waited for; matrix products, arithmetic and copies ran while one was open for 0% of the time, Pallas kernels for 25%

profile of v9, /device:TPU:0, one launch (start us, length us, event | category | flops | bytes accessed | tf_op | source)
XLA Modules:
  0.0 59.5 jit_solution(10909671556471691764)
XLA Ops:
  0.6 2.9 %shard_map.130 = (bf16[640,128]{1,0:T(8,128)(2,1)}, bf16[384,128]{1,0:T(8,128)(2,1)}, bf16[256,128]{1,0:T(8,128)(2,1)}, bf16[64,768]{1,0:T(8,128)(2,1)}) custom-call(s32[1]{0:T(128)} %bitcast.2.refs_0_, bf16[32,16,64]{2,1,0:T(8,128)(2,1)} %refs_1_.1, bf16[32,16,64]{2,1,0:T(8,128)(2,1)} %refs_2_.1, bf16[32,64]{1,0:T(8,128)(2,1)} %bitcast.23, ...), custom_call_target="tpu_custom_call" | custom-call | tf_op jit(solution)/shard_map/pallas_call | solution.py:62
  3.5 3.0 %collective-permute-start.1 = (bf16[640,128]{1,0:T(8,128)(2,1)}, bf16[640,128]{1,0:T(8,128)(2,1)S(1)}, u32[]{:S(2)}, u32[]{:S(2)}) collective-permute-start(bf16[640,128]{1,0:T(8,128)(2,1)} %get-tuple-element.28.refs_2_), channel_id=1, source_target_pairs={{0,2},{1,3},{2,0},{3,1},{4,6},{5,7},{6,4},{7,5},{8,10},{9,11},{10,... | collective-permute-start | bytes 491528 | tf_op jit(solution)/shard_map/ppermute | solution.py:722
  6.5 1.5 %collective-permute-start.3 = (bf16[384,128]{1,0:T(8,128)(2,1)}, bf16[384,128]{1,0:T(8,128)(2,1)S(1)}, u32[]{:S(2)}, u32[]{:S(2)}) collective-permute-start(bf16[384,128]{1,0:T(8,128)(2,1)} %get-tuple-element.29), channel_id=1, source_target_pairs={{0,0},{1,4},{2,8},{3,12},{4,1},{5,5},{6,9},{7,13},{8,2},{9,6},{10,... | collective-permute-start | bytes 294920 | tf_op jit(solution)/shard_map/ppermute | solution.py:713
  8.0 2.1 %collective-permute-start = (bf16[640,128]{1,0:T(8,128)(2,1)}, bf16[640,128]{1,0:T(8,128)(2,1)S(1)}, u32[]{:S(2)}, u32[]{:S(2)}) collective-permute-start(bf16[640,128]{1,0:T(8,128)(2,1)} %get-tuple-element.28.refs_2_), channel_id=1, source_target_pairs={{0,1},{1,0},{2,3},{3,2},{4,5},{5,4},{6,7},{7,6},{8,9},{9,8},{10,11... | collective-permute-start | bytes 491528 | tf_op jit(solution)/shard_map/ppermute | solution.py:722
  10.1 0.7 %collective-permute-done.1.refs_4_ = bf16[640,128]{1,0:T(8,128)(2,1)S(1)} collective-permute-done((bf16[640,128]{1,0:T(8,128)(2,1)}, bf16[640,128]{1,0:T(8,128)(2,1)S(1)}, u32[]{:S(2)}, u32[]{:S(2)}) %collective-permute-start.1) | collective-permute-done | bytes 163872 | tf_op jit(solution)/shard_map/ppermute | solution.py:722
  10.9 0.0 collective-permute-start.2
  10.9 1.8 %collective-permute-start.4 = (bf16[384,128]{1,0:T(8,128)(2,1)}, bf16[384,128]{1,0:T(8,128)(2,1)S(1)}, u32[]{:S(2)}, u32[]{:S(2)}) collective-permute-start(bf16[384,128]{1,0:T(8,128)(2,1)} %get-tuple-element.29), channel_id=1, source_target_pairs={{0,4},{1,8},{2,12},{3,0},{4,5},{5,9},{6,13},{7,1},{8,6},{9,10},{10... | collective-permute-start | bytes 294920 | tf_op jit(solution)/shard_map/ppermute | solution.py:713
  12.7 2.4 %collective-permute-start.5 = (bf16[384,128]{1,0:T(8,128)(2,1)}, bf16[384,128]{1,0:T(8,128)(2,1)S(1)}, u32[]{:S(2)}, u32[]{:S(2)}) collective-permute-start(bf16[384,128]{1,0:T(8,128)(2,1)} %get-tuple-element.29), channel_id=1, source_target_pairs={{0,8},{1,12},{2,0},{3,4},{4,9},{5,13},{6,1},{7,5},{8,10},{9,14},{1... | collective-permute-start | bytes 294920 | tf_op jit(solution)/shard_map/ppermute | solution.py:713
  15.1 0.0 collective-permute-done.3.refs_6_
  15.1 4.5 %collective-permute-start.6 = (bf16[384,128]{1,0:T(8,128)(2,1)}, bf16[384,128]{1,0:T(8,128)(2,1)S(1)}, u32[]{:S(2)}, u32[]{:S(2)}) collective-permute-start(bf16[384,128]{1,0:T(8,128)(2,1)} %get-tuple-element.29), channel_id=1, source_target_pairs={{0,12},{1,0},{2,4},{3,8},{4,13},{5,1},{6,5},{7,9},{8,14},{9,2},{10... | collective-permute-start | bytes 294920 | tf_op jit(solution)/shard_map/ppermute | solution.py:713
  19.6 0.0 collective-permute-done.4.refs_7_
  19.6 0.0 collective-permute-done.5.refs_8_
  19.6 2.5 %collective-permute-done.6.refs_9_ = bf16[384,128]{1,0:T(8,128)(2,1)S(1)} collective-permute-done((bf16[384,128]{1,0:T(8,128)(2,1)}, bf16[384,128]{1,0:T(8,128)(2,1)S(1)}, u32[]{:S(2)}, u32[]{:S(2)}) %collective-permute-start.6) | collective-permute-done | bytes 98336 | tf_op jit(solution)/shard_map/ppermute | solution.py:713
  22.2 0.0 collective-permute-done.refs_3_
  22.2 0.0 collective-permute-done.2.refs_5_
  22.2 0.0 copy-start
  22.2 0.9 %copy-done = bf16[640,128]{1,0:T(8,128)(2,1)S(1)} copy-done((bf16[640,128]{1,0:T(8,128)(2,1)S(1)}, bf16[640,128]{1,0:T(8,128)(2,1)}, u32[]{:S(2)}) %copy-start) | copy-done | bytes 163864
  23.1 1.6 %collective-permute-start.8 = (bf16[1024,128]{1,0:T(8,128)(2,1)S(1)}, bf16[1024,128]{1,0:T(8,128)(2,1)S(1)}, u32[]{:S(2)}, u32[]{:S(2)}) collective-permute-start(bf16[1024,128]{1,0:T(8,128)(2,1)S(1)} %get-tuple-element.33.refs_2_), channel_id=1, source_target_pairs={{0,16},{16,0},{1,17},{17,1},{2,18},{18,2},{3,19},{19,3},{4,20},{20... | collective-permute-start | bytes 786440 | tf_op jit(solution)/shard_map/ppermute | solution.py:736
  24.7 0.0 copy-start.8
  24.7 0.9 %copy-done.8 = bf16[64,768]{1,0:T(8,128)(2,1)S(1)} copy-done((bf16[64,768]{1,0:T(8,128)(2,1)S(1)}, bf16[64,768]{1,0:T(8,128)(2,1)}, u32[]{:S(2)}) %copy-start.8) | copy-done | bytes 98328
  25.6 0.0 copy-start.5
  25.6 0.0 copy-start.6
  25.6 0.0 copy-start.7
  25.6 0.0 copy-start.10
  25.6 2.3 %shard_map.132.refs_2_ = f32[16,8,256]{2,1,0:T(8,128)S(1)} custom-call(s32[1]{0:T(128)} %bitcast.refs_0_, s32[1]{0:T(128)} %bitcast.1.refs_1_.refs_0_, bf16[640,128]{1,0:T(8,128)(2,1)S(1)} %copy-done, bf16[640,128]{1,0:T(8,128)(2,1)S(1)} %collective-permute-done.refs_3_, bf16[640,128]{1,0:T(8,128)(2,1)S(1)} %collective-permute-done.1.refs_4_, ...), custom_call_target="tpu_custom_call" | custom-call | flops 3000000000 | bytes 3000000 | tf_op jit(solution)/shard_map/pallas_call | solution.py:62
  27.9 2.3 %collective-permute-start.7 = (bf16[4,16,16,128]{3,2,1,0:T(8,128)(2,1)S(1)}, bf16[4,16,16,128]{3,2,1,0:T(8,128)(2,1)S(1)}, u32[]{:S(2)}, u32[]{:S(2)}) collective-permute-start(bf16[4,16,16,128]{3,2,1,0:T(8,128)(2,1)S(1)} %get-tuple-element.32.refs_0_), channel_id=1, source_target_pairs={{0,8},{4,12},{8,0},{12,4},{1,9},{5,13},{9,1},{13,5},{2,10},{6,14},... | collective-permute-start | bytes 786440 | tf_op jit(solution)/shard_map/ppermute | solution.py:764
  30.2 2.5 %collective-permute-start.13 = (bf16[4,16,16,128]{3,2,1,0:T(8,128)(2,1)S(1)}, bf16[4,16,16,128]{3,2,1,0:T(8,128)(2,1)S(1)}, u32[]{:S(2)}, u32[]{:S(2)}) collective-permute-start(bf16[4,16,16,128]{3,2,1,0:T(8,128)(2,1)S(1)} %get-tuple-element.32.refs_0_), channel_id=1, source_target_pairs={{0,4},{4,0},{8,12},{12,8},{1,5},{5,1},{9,13},{13,9},{2,6},{6,2},{1... | collective-permute-start | bytes 786440 | tf_op jit(solution)/shard_map/ppermute | solution.py:764
  32.7 0.0 collective-permute-done.8.refs_3_
  32.7 0.0 copy-done.5
  32.7 0.0 copy-done.6
  32.7 0.0 copy-done.7
  32.7 0.0 copy-done.10
  32.7 0.0 copy-start.2
  32.7 0.0 copy-start.3
  32.8 0.0 copy-start.9
  32.8 11.0 %shard_map.133 = (bf16[4096,128]{1,0:T(8,128)(2,1)}, bf16[16,128,256]{2,1,0:T(8,128)(2,1)S(1)}, f32[16,8,256]{2,1,0:T(8,128)S(1)}) custom-call(s32[1]{0:T(128)} %bitcast.1.refs_1_.refs_0_, s32[1]{0:T(128)} %bitcast.7.refs_1_, bf16[1024,128]{1,0:T(8,128)(2,1)S(1)} %get-tuple-element.33.refs_2_, bf16[1024,128]{1,0:T(8,128)(2,1)S(1)} %collective-permute-done.8.refs_3_, ...), custom_call_target="tpu_custom_call" | custom-call | flops 14000000000 | bytes 5000000 | tf_op jit(solution)/shard_map/pallas_call | solution.py:62
  43.8 0.0 collective-permute-done.7.refs_2_
  43.8 0.1 collective-permute-start.14
  43.9 0.6 %collective-permute-start.9 = (f32[16,8,256]{2,1,0:T(8,128)S(1)}, f32[16,8,256]{2,1,0:T(8,128)S(1)}, u32[]{:S(2)}, u32[]{:S(2)}) collective-permute-start(f32[16,8,256]{2,1,0:T(8,128)S(1)} %shard_map.132.refs_2_), channel_id=1, source_target_pairs={{0,16},{16,0},{1,17},{17,1},{2,18},{18,2},{3,19},{19,3},{4,20},{20... | collective-permute-start | bytes 393224 | tf_op jit(solution)/shard_map/ppermute | solution.py:759
  44.5 4.4 %collective-permute-done.9.refs_3_ = f32[16,8,256]{2,1,0:T(8,128)S(1)} collective-permute-done((f32[16,8,256]{2,1,0:T(8,128)S(1)}, f32[16,8,256]{2,1,0:T(8,128)S(1)}, u32[]{:S(2)}, u32[]{:S(2)}) %collective-permute-start.9) | collective-permute-done | bytes 131104 | tf_op jit(solution)/shard_map/ppermute | solution.py:759
  48.9 0.5 shard_map.134
  49.4 0.0 collective-permute-start.10
  49.4 1.5 %collective-permute-start.11 = (f32[10,8,128]{2,1,0:T(8,128)S(1)}, f32[10,8,128]{2,1,0:T(8,128)S(1)}, u32[]{:S(2)}, u32[]{:S(2)}) collective-permute-start(f32[10,8,128]{2,1,0:T(8,128)S(1)} %get-tuple-element.39), channel_id=1, source_target_pairs={{0,2},{1,3},{2,0},{3,1},{4,6},{5,7},{6,4},{7,5},{8,10},{9,11},{10,... | collective-permute-start | bytes 122888 | tf_op jit(solution)/shard_map/ppermute | solution.py:820
  50.9 1.4 %collective-permute-start.12 = (f32[10,8,128]{2,1,0:T(8,128)S(1)}, f32[10,8,128]{2,1,0:T(8,128)S(1)}, u32[]{:S(2)}, u32[]{:S(2)}) collective-permute-start(f32[10,8,128]{2,1,0:T(8,128)S(1)} %get-tuple-element.40), channel_id=1, source_target_pairs={{0,3},{1,0},{2,1},{3,2},{4,7},{5,4},{6,5},{7,6},{8,11},{9,8},{10,9... | collective-permute-start | bytes 122888 | tf_op jit(solution)/shard_map/ppermute | solution.py:820
  52.3 0.0 collective-permute-done.13.refs_1_
  52.3 0.0 collective-permute-done.14.refs_3_
  52.3 0.0 copy-done.2
  52.3 0.0 copy-done.3
  52.4 0.0 copy-done.9
  52.4 1.3 %shard_map.135 = (bf16[16,256,512]{2,1,0:T(8,128)(2,1)S(1)}, f32[512,256]{1,0:T(8,128)S(1)}) custom-call(bf16[4,16,16,128]{3,2,1,0:T(8,128)(2,1)S(1)} %get-tuple-element.32.refs_0_, bf16[4,16,16,128]{3,2,1,0:T(8,128)(2,1)S(1)} %collective-permute-done.13.refs_1_, bf16[4,16,16,128]{3,2,1,0:T(8,128)(2,1)S(1)} %collective-permute-done.7.refs_2_, ...), custom_call_target="tpu_custom_call" | custom-call | flops 4000000000 | bytes 6000000 | tf_op jit(solution)/shard_map/pallas_call | solution.py:62
  53.7 0.0 collective-permute-done.10.refs_3_.refs_1_
  53.7 0.0 collective-permute-done.11.refs_4_.refs_2_
  53.7 0.3 collective-permute-done.12.refs_5_.refs_3_
  54.0 0.0 copy-start.1
  54.0 0.0 copy-start.4
  54.0 3.0 %shard_map.137 = bf16[4096,128]{1,0:T(8,128)(2,1)} custom-call(f32[10,8,128]{2,1,0:T(8,128)S(1)} %get-tuple-element.37.refs_2_.refs_0_, f32[10,8,128]{2,1,0:T(8,128)S(1)} %collective-permute-done.10.refs_3_.refs_1_, f32[10,8,128]{2,1,0:T(8,128)S(1)} %collective-permute-done.11.refs_4_.refs_2_, f32[10,8,128]{2,1,0:T(8,128)S(1)} %collective-permute-done.12.refs_5_.refs_3_, ...), custom_call_target="tpu_custom_call" | custom-call | flops 4000000000 | bytes 3000000 | tf_op jit(solution)/shard_map/pallas_call | solution.py:62
  57.0 0.0 copy-done.1
  57.0 0.0 copy-done.4
  57.0 2.6 %shard_map.136 = bf16[512,64]{1,0:T(8,128)(2,1)} custom-call(s32[1]{0:T(128)} %bitcast.refs_0_, s32[1]{0:T(128)} %bitcast.1.refs_1_.refs_0_, f32[10,8,128]{2,1,0:T(8,128)S(1)} %get-tuple-element.37.refs_2_.refs_0_, f32[10,8,128]{2,1,0:T(8,128)S(1)} %collective-permute-done.10.refs_3_.refs_1_, f32[10,8,128]{2,1,0:T(8,128)S(1)} %collective-permute-done.11.refs_4_.refs_2_, ...), custom_call_target="tpu_custom_call" | custom-call | flops 3000000000 | bytes 5000000 | tf_op jit(solution)/shard_map/pallas_call | solution.py:62
  (1 shorter events, 0.0 us)
Async XLA Ops:
  3.5 7.4 %collective-permute-start.1 = (bf16[640,128]{1,0:T(8,128)(2,1)}, bf16[640,128]{1,0:T(8,128)(2,1)S(1)}, u32[]{:S(2)}, u32[]{:S(2)}) collective-permute-start(bf16[640,128]{1,0:T(8,128)(2,1)} %get-tuple-element.28.refs_2_), channel_id=1, source_target_pairs={{0,2},{1,3},{2,0},{3,1},{4,6},{5,7},{6,4},{7,5},{8,10},{9,11},{10,... | collective-permute-start | bytes 491528 | tf_op jit(solution)/shard_map/ppermute | solution.py:722
  6.5 8.6 %collective-permute-start.3 = (bf16[384,128]{1,0:T(8,128)(2,1)}, bf16[384,128]{1,0:T(8,128)(2,1)S(1)}, u32[]{:S(2)}, u32[]{:S(2)}) collective-permute-start(bf16[384,128]{1,0:T(8,128)(2,1)} %get-tuple-element.29), channel_id=1, source_target_pairs={{0,0},{1,4},{2,8},{3,12},{4,1},{5,5},{6,9},{7,13},{8,2},{9,6},{10,... | collective-permute-start | bytes 294920 | tf_op jit(solution)/shard_map/ppermute | solution.py:713
  8.0 14.2 %collective-permute-start = (bf16[640,128]{1,0:T(8,128)(2,1)}, bf16[640,128]{1,0:T(8,128)(2,1)S(1)}, u32[]{:S(2)}, u32[]{:S(2)}) collective-permute-start(bf16[640,128]{1,0:T(8,128)(2,1)} %get-tuple-element.28.refs_2_), channel_id=1, source_target_pairs={{0,1},{1,0},{2,3},{3,2},{4,5},{5,4},{6,7},{7,6},{8,9},{9,8},{10,11... | collective-permute-start | bytes 491528 | tf_op jit(solution)/shard_map/ppermute | solution.py:722
  10.9 11.3 %collective-permute-start.2 = (bf16[640,128]{1,0:T(8,128)(2,1)S(1)}, bf16[640,128]{1,0:T(8,128)(2,1)S(1)}, u32[]{:S(2)}, u32[]{:S(2)}) collective-permute-start(bf16[640,128]{1,0:T(8,128)(2,1)S(1)} %collective-permute-done.1.refs_4_), channel_id=1, source_target_pairs={{0,1},{1,0},{2,3},{3,2},{4,5},{5,4},{6,7},{7,6},{8,9},{9,8},{10,11... | collective-permute-start | bytes 491528 | tf_op jit(solution)/shard_map/ppermute | solution.py:722
  10.9 8.8 %collective-permute-start.4 = (bf16[384,128]{1,0:T(8,128)(2,1)}, bf16[384,128]{1,0:T(8,128)(2,1)S(1)}, u32[]{:S(2)}, u32[]{:S(2)}) collective-permute-start(bf16[384,128]{1,0:T(8,128)(2,1)} %get-tuple-element.29), channel_id=1, source_target_pairs={{0,4},{1,8},{2,12},{3,0},{4,5},{5,9},{6,13},{7,1},{8,6},{9,10},{10... | collective-permute-start | bytes 294920 | tf_op jit(solution)/shard_map/ppermute | solution.py:713
  12.7 7.0 %collective-permute-start.5 = (bf16[384,128]{1,0:T(8,128)(2,1)}, bf16[384,128]{1,0:T(8,128)(2,1)S(1)}, u32[]{:S(2)}, u32[]{:S(2)}) collective-permute-start(bf16[384,128]{1,0:T(8,128)(2,1)} %get-tuple-element.29), channel_id=1, source_target_pairs={{0,8},{1,12},{2,0},{3,4},{4,9},{5,13},{6,1},{7,5},{8,10},{9,14},{1... | collective-permute-start | bytes 294920 | tf_op jit(solution)/shard_map/ppermute | solution.py:713
  15.1 7.1 %collective-permute-start.6 = (bf16[384,128]{1,0:T(8,128)(2,1)}, bf16[384,128]{1,0:T(8,128)(2,1)S(1)}, u32[]{:S(2)}, u32[]{:S(2)}) collective-permute-start(bf16[384,128]{1,0:T(8,128)(2,1)} %get-tuple-element.29), channel_id=1, source_target_pairs={{0,12},{1,0},{2,4},{3,8},{4,13},{5,1},{6,5},{7,9},{8,14},{9,2},{10... | collective-permute-start | bytes 294920 | tf_op jit(solution)/shard_map/ppermute | solution.py:713
  22.2 0.9 %copy-start = (bf16[640,128]{1,0:T(8,128)(2,1)S(1)}, bf16[640,128]{1,0:T(8,128)(2,1)}, u32[]{:S(2)}) copy-start(bf16[640,128]{1,0:T(8,128)(2,1)} %get-tuple-element.28.refs_2_) | copy-start | bytes 491524
  23.1 9.6 %collective-permute-start.8 = (bf16[1024,128]{1,0:T(8,128)(2,1)S(1)}, bf16[1024,128]{1,0:T(8,128)(2,1)S(1)}, u32[]{:S(2)}, u32[]{:S(2)}) collective-permute-start(bf16[1024,128]{1,0:T(8,128)(2,1)S(1)} %get-tuple-element.33.refs_2_), channel_id=1, source_target_pairs={{0,16},{16,0},{1,17},{17,1},{2,18},{18,2},{3,19},{19,3},{4,20},{20... | collective-permute-start | bytes 786440 | tf_op jit(solution)/shard_map/ppermute | solution.py:736
  24.7 0.9 %copy-start.8 = (bf16[64,768]{1,0:T(8,128)(2,1)S(1)}, bf16[64,768]{1,0:T(8,128)(2,1)}, u32[]{:S(2)}) copy-start(bf16[64,768]{1,0:T(8,128)(2,1)} %get-tuple-element.31.refs_10_) | copy-start | bytes 294916
  25.6 7.1 %copy-start.5 = (s32[256]{0:T(256)S(1)}, s32[256]{0:T(256)}, u32[]{:S(2)}) copy-start(s32[256]{0:T(256)} %param.13) | copy-start | bytes 3076
  25.6 7.1 %copy-start.6 = (bf16[64,64,128]{2,1,0:T(8,128)(2,1)S(1)}, bf16[64,64,128]{2,1,0:T(8,128)(2,1)}, u32[]{:S(2)}) copy-start(bf16[64,64,128]{2,1,0:T(8,128)(2,1)} %param.12) | copy-start | bytes 3145732
  25.6 7.1 %copy-start.7 = (f32[1024,128]{1,0:T(8,128)S(1)}, f32[1024,128]{1,0:T(8,128)}, u32[]{:S(2)}) copy-start(f32[1024,128]{1,0:T(8,128)} %refs_5_.1) | copy-start | bytes 1572868
  25.6 7.1 %copy-start.10 = (f32[128,8]{0,1:T(8,128)S(1)}, f32[128,8]{0,1:T(8,128)}, u32[]{:S(2)}) copy-start(f32[128,8]{0,1:T(8,128)} %param.19) | copy-start | bytes 12292
  27.9 15.9 %collective-permute-start.7 = (bf16[4,16,16,128]{3,2,1,0:T(8,128)(2,1)S(1)}, bf16[4,16,16,128]{3,2,1,0:T(8,128)(2,1)S(1)}, u32[]{:S(2)}, u32[]{:S(2)}) collective-permute-start(bf16[4,16,16,128]{3,2,1,0:T(8,128)(2,1)S(1)} %get-tuple-element.32.refs_0_), channel_id=1, source_target_pairs={{0,8},{4,12},{8,0},{12,4},{1,9},{5,13},{9,1},{13,5},{2,10},{6,14},... | collective-permute-start | bytes 786440 | tf_op jit(solution)/shard_map/ppermute | solution.py:764
  30.2 22.1 %collective-permute-start.13 = (bf16[4,16,16,128]{3,2,1,0:T(8,128)(2,1)S(1)}, bf16[4,16,16,128]{3,2,1,0:T(8,128)(2,1)S(1)}, u32[]{:S(2)}, u32[]{:S(2)}) collective-permute-start(bf16[4,16,16,128]{3,2,1,0:T(8,128)(2,1)S(1)} %get-tuple-element.32.refs_0_), channel_id=1, source_target_pairs={{0,4},{4,0},{8,12},{12,8},{1,5},{5,1},{9,13},{13,9},{2,6},{6,2},{1... | collective-permute-start | bytes 786440 | tf_op jit(solution)/shard_map/ppermute | solution.py:764
  32.7 19.6 %copy-start.2 = (bf16[64,256]{1,0:T(8,128)(2,1)S(1)}, bf16[64,256]{1,0:T(8,128)(2,1)}, u32[]{:S(2)}) copy-start(bf16[64,256]{1,0:T(8,128)(2,1)} %refs_4_.1) | copy-start | bytes 98308
  32.7 19.6 %copy-start.3 = (bf16[64,256]{1,0:T(8,128)(2,1)S(1)}, bf16[64,256]{1,0:T(8,128)(2,1)}, u32[]{:S(2)}) copy-start(bf16[64,256]{1,0:T(8,128)(2,1)} %refs_6_.3) | copy-start | bytes 98308
  32.8 19.6 %copy-start.9 = (bf16[256,128]{1,0:T(8,128)(2,1)S(1)}, bf16[256,128]{1,0:T(8,128)(2,1)}, u32[]{:S(2)}) copy-start(bf16[256,128]{1,0:T(8,128)(2,1)} %get-tuple-element.42.refs_5_) | copy-start | bytes 196612
  43.8 8.5 %collective-permute-start.14 = (bf16[4,16,16,128]{3,2,1,0:T(8,128)(2,1)S(1)}, bf16[4,16,16,128]{3,2,1,0:T(8,128)(2,1)S(1)}, u32[]{:S(2)}, u32[]{:S(2)}) collective-permute-start(bf16[4,16,16,128]{3,2,1,0:T(8,128)(2,1)S(1)} %collective-permute-done.7.refs_2_), channel_id=1, source_target_pairs={{0,4},{4,0},{8,12},{12,8},{1,5},{5,1},{9,13},{13,9},{2,6},{6,2},{1... | collective-permute-start | bytes 786440 | tf_op jit(solution)/shard_map/ppermute | solution.py:764
  43.9 5.0 %collective-permute-start.9 = (f32[16,8,256]{2,1,0:T(8,128)S(1)}, f32[16,8,256]{2,1,0:T(8,128)S(1)}, u32[]{:S(2)}, u32[]{:S(2)}) collective-permute-start(f32[16,8,256]{2,1,0:T(8,128)S(1)} %shard_map.132.refs_2_), channel_id=1, source_target_pairs={{0,16},{16,0},{1,17},{17,1},{2,18},{18,2},{3,19},{19,3},{4,20},{20... | collective-permute-start | bytes 393224 | tf_op jit(solution)/shard_map/ppermute | solution.py:759
  49.4 4.3 %collective-permute-start.10 = (f32[10,8,128]{2,1,0:T(8,128)S(1)}, f32[10,8,128]{2,1,0:T(8,128)S(1)}, u32[]{:S(2)}, u32[]{:S(2)}) collective-permute-start(f32[10,8,128]{2,1,0:T(8,128)S(1)} %get-tuple-element.38), channel_id=1, source_target_pairs={{0,1},{1,2},{2,3},{3,0},{4,5},{5,6},{6,7},{7,4},{8,9},{9,10},{10,1... | collective-permute-start | bytes 122888 | tf_op jit(solution)/shard_map/ppermute | solution.py:820
  49.4 4.3 %collective-permute-start.11 = (f32[10,8,128]{2,1,0:T(8,128)S(1)}, f32[10,8,128]{2,1,0:T(8,128)S(1)}, u32[]{:S(2)}, u32[]{:S(2)}) collective-permute-start(f32[10,8,128]{2,1,0:T(8,128)S(1)} %get-tuple-element.39), channel_id=1, source_target_pairs={{0,2},{1,3},{2,0},{3,1},{4,6},{5,7},{6,4},{7,5},{8,10},{9,11},{10,... | collective-permute-start | bytes 122888 | tf_op jit(solution)/shard_map/ppermute | solution.py:820
  50.9 3.1 %collective-permute-start.12 = (f32[10,8,128]{2,1,0:T(8,128)S(1)}, f32[10,8,128]{2,1,0:T(8,128)S(1)}, u32[]{:S(2)}, u32[]{:S(2)}) collective-permute-start(f32[10,8,128]{2,1,0:T(8,128)S(1)} %get-tuple-element.40), channel_id=1, source_target_pairs={{0,3},{1,0},{2,1},{3,2},{4,7},{5,4},{6,5},{7,6},{8,11},{9,8},{10,9... | collective-permute-start | bytes 122888 | tf_op jit(solution)/shard_map/ppermute | solution.py:820
  54.0 3.0 %copy-start.1 = (bf16[32,16,64]{2,1,0:T(8,128)(2,1)S(1)}, bf16[32,16,64]{2,1,0:T(8,128)(2,1)}, u32[]{:S(2)}) copy-start(bf16[32,16,64]{2,1,0:T(8,128)(2,1)} %refs_1_.1) | copy-start | bytes 196612
  54.0 3.0 %copy-start.4 = (bf16[256,64]{0,1:T(8,128)(2,1)S(1)}, bf16[256,64]{0,1:T(8,128)(2,1)}, u32[]{:S(2)}) copy-start(bf16[256,64]{0,1:T(8,128)(2,1)} %param.20) | copy-start | bytes 98308

commit v10 on v9

--- a/solution.py
+++ b/solution.py
@@ -130,9 +130,12 @@
 
     packed = two(normed)
     norm_ref[...] = packed
-    rows_ref[-2 * rows : -rows, :] = packed
-    rows_ref[-rows:, :] = two(adj)
-    cols_ref[-rows:, :] = packed
+    adj = two(adj)
+    copies = rows_ref.shape[0]
+    for n in range(copies):
+        rows_ref[n, -2 * rows : -rows, :] = packed
+        rows_ref[n, -rows:, :] = adj
+        cols_ref[n, -rows:, :] = packed
     token = lax.broadcasted_iota(jnp.int32, (seqs, tokens, width), 1) + own_ref[0]
     count = valid_count(mask_ref).reshape(1, 1, 1)
     real = jnp.where(token.astype(f32) < count, normed, 0.0)
@@ -143,7 +146,8 @@
     fc = w1_ref.shape[0]
     wk = pack * seqs
     for g in range(tokens // pack):
-        rows_ref[g * fc : (g + 1) * fc, :] = left[:, g * wk : (g + 1) * wk]
+        for n in range(copies):
+            rows_ref[n, g * fc : (g + 1) * fc, :] = left[:, g * wk : (g + 1) * wk]
     size = 128 // tokens
     real = real.astype(bf16)
     w2 = w2_ref[...]
@@ -154,38 +158,20 @@
         res = nt_dot(w2, jnp.concatenate([real[s]] * size, axis=0))
         res = jnp.where(mine, res, 0.0).reshape(fd // size, size, 128)
         place_ref[:, s, :] = jnp.sum(res, axis=1)
-    cols_ref[:-rows, :] = place_ref[...].reshape(fd // size * seqs, 128).astype(bf16)
-
-
-def join_kernel(
-    ready,
-    row_ref,
-    col_ref,
-    rows0_ref,
-    rows1_ref,
-    rows2_ref,
-    rows3_ref,
-    cols0_ref,
-    cols1_ref,
-    cols2_ref,
-    cols3_ref,
-    out_ref,
-    norm_ref,
-):
-    nk = 4
-    row, col = row_ref[0], col_ref[0]
-    r_rows = l_rows = out_ref.shape[0] // (2 * nk)
-    for t, ref in enumerate((cols0_ref, cols1_ref, cols2_ref, cols3_ref)):
-        at = pl.ds(pl.multiple_of(lax.rem(row + nk - t, nk) * r_rows, r_rows), r_rows)
-        out_ref[at, :] = ref[:r_rows, :]
-    for t, ref in enumerate((rows0_ref, rows1_ref, rows2_ref, rows3_ref)):
-        start = nk * r_rows + jnp.bitwise_xor(col, t) * l_rows
-        at = pl.ds(pl.multiple_of(start, l_rows), l_rows)
-        out_ref[at, :] = ref[:l_rows, :]
-        half, tokens, _ = norm_ref.shape[1:]
-        count = half * tokens
-        start = ref.shape[0] - 2 * count
-        norm_ref[jnp.bitwise_xor(col, t)] = ref[start : start + count, :].reshape(norm_ref.shape[1:])
+    right = place_ref[...].reshape(fd // size * seqs, 128).astype(bf16)
+    for n in range(copies):
+        cols_ref[n, :-rows, :] = right
+
+
+def join_kernel(ready, rows_ref, cols_ref, parts_ref, out_ref, norm_ref):
+    nk = rows_ref.shape[0]
+    size = out_ref.shape[0] // (2 * nk)
+    count = norm_ref.shape[1]
+    for k in range(nk):
+        out_ref[k * size : (k + 1) * size, :] = cols_ref[k, :size, :]
+        out_ref[(nk + k) * size : (nk + k + 1) * size, :] = rows_ref[k, :size, :]
+    for r in range(parts_ref.shape[0]):
+        norm_ref[r] = parts_ref[r, parts_ref.shape[1] - count :, :]
 
 
 def update_kernel(
@@ -357,38 +343,28 @@
 
 def weights_kernel(
     ready,
-    row_ref,
-    col_ref,
-    side0_ref,
-    side1_ref,
-    side2_ref,
-    side3_ref,
-    cols0_ref,
-    cols1_ref,
-    cols2_ref,
-    cols3_ref,
+    rows_ref,
+    cols_ref,
     weights_ref,
     gw_ref,
     acc_ref,
     bv_ref,
     bg_ref,
     bf_ref,
-    rows_ref,
-    cols_ref,
     gs_ref,
     vs_ref,
 ):
-    nk, half, tokens, _ = cols_ref.shape
-    tile = nk * tokens
     groups, heads, lanes = gw_ref.shape
-    row, col = row_ref[0], col_ref[0]
+    tile = lanes // pack
+    nk = rows_ref.shape[0]
+    tokens = tile // nk
+    half = gs_ref.shape[2] // bv_ref.shape[1] * heads * 2
     count = half * tokens
-    for t, ref in enumerate((side0_ref, side1_ref, side2_ref, side3_ref)):
-        start = ref.shape[0] - 2 * count
-        rows_ref[jnp.bitwise_xor(col, t)] = ref[start:, :].reshape(rows_ref.shape[1:])
-    for t, ref in enumerate((cols0_ref, cols1_ref, cols2_ref, cols3_ref)):
-        start = ref.shape[0] - count
-        cols_ref[lax.rem(row + nk - t, nk)] = ref[start:, :].reshape(cols_ref.shape[1:])
+
+    def part(ref, k, which, s):
+        start = ref.shape[1] - which * count + s * tokens
+        return ref[k, start : start + tokens, :]
+
     chans = weights_ref.shape[1] // 3
     by_heads(weights_ref[:, :chans], heads, bv_ref)
     by_heads(weights_ref[:, chans : 2 * chans], heads, bg_ref)
@@ -413,9 +389,9 @@
     for hp in range(heads // 2):
         cut = slice(hp * 2 * block, (hp + 1) * 2 * block)
         for n in range(half // 4):
-            v = nn_dot(four(lambda k, s: cols_ref[k, s], n), bv_ref[:, cut]).astype(bf16)
-            gate = nn_dot(four(lambda k, s: rows_ref[k, 0, s], n), bg_ref[:, cut])
-            grad = nn_dot(four(lambda k, s: rows_ref[k, 1, s], n), bf_ref[:, cut])
+            v = nn_dot(four(lambda k, s: part(cols_ref, k, 1, s), n), bv_ref[:, cut]).astype(bf16)
+            gate = nn_dot(four(lambda k, s: part(rows_ref, k, 2, s), n), bg_ref[:, cut])
+            grad = nn_dot(four(lambda k, s: part(rows_ref, k, 1, s), n), bf_ref[:, cut])
             g = (grad * jax.nn.sigmoid(gate)).astype(bf16)
             for e in range(2):
                 to = slice((2 * n + e) * block, (2 * n + e + 1) * block)
@@ -444,14 +420,11 @@
     gwb_ref,
     mask_ref,
     gw_ref,
-    own_ref,
-    pay1_ref,
-    pay2_ref,
-    pay3_ref,
+    pay_ref,
 ):
     groups, heads, lanes = logits_ref.shape
     tile = lanes // pack
-    nk = 4
+    nk = pay_ref.shape[0]
     rows = groups * heads
     col = col_ref[0]
     gw_ref[...] = gwa_ref[...] + gwb_ref[...]
@@ -477,34 +450,38 @@
             stats = jnp.where(lane == 2 * pack + i, inner, stats)
     turned = stats.T[:16]
     per = groups // nk
-    for shift, pay in enumerate((own_ref, pay1_ref, pay2_ref, pay3_ref)):
-        dest = lax.rem(col + shift, nk)
-        pay[0] = turned[:8]
-        pay[1] = turned[8:]
+    for dest in range(nk):
+        pay_ref[dest, 0] = turned[:8]
+        pay_ref[dest, 1] = turned[8:]
         for g in range(per):
             piece = logits_ref[dest * per + g]
             for part in range(pack // 2):
-                pay[2 + g * (pack // 2) + part] = piece[:, part * 2 * tile : (part + 1) * 2 * tile]
+                cut = slice(part * 2 * tile, (part + 1) * 2 * tile)
+                pay_ref[dest, 2 + g * (pack // 2) + part] = piece[:, cut]
 
 
 def values_kernel(
-    ready, ev0_ref, ev1_ref, ev2_ref, ev3_ref, wv_ref, norm_ref, wg_ref, v_ref, gate_ref
+    ready, col_ref, ev0_ref, ev1_ref, ev2_ref, ev3_ref, wv_ref, norm_ref, wg_ref, v_ref, gate_ref, ev_ref
 ):
-    evs = (ev0_ref, ev1_ref, ev2_ref, ev3_ref)
-    nk, half, tokens, wide = ev0_ref.shape
+    nk, nr, count, wide = ev_ref.shape
+    half = v_ref.shape[0]
+    tokens = count // half
     chans = wv_ref.shape[1]
+    for t, ref in enumerate((ev0_ref, ev1_ref, ev2_ref, ev3_ref)):
+        ev_ref[jnp.bitwise_xor(col_ref[0], t)] = ref[...]
     gate = jax.nn.sigmoid(nn_dot(norm_ref[...], twice(wg_ref[...])))
     gate_ref[: half * tokens] = gate[:, :chans]
     gate_ref[half * tokens :] = gate[:, chans:]
     wv = twice(wv_ref[...])
     for s in range(half):
-        x = jnp.concatenate([ev[k, s] for ev in evs for k in range(nk)], axis=0)
+        at = slice(s * tokens, (s + 1) * tokens)
+        x = jnp.concatenate([ev_ref[k, r, at, :] for r in range(nr) for k in range(nk)], axis=0)
         v_ref[s] = nn_dot(x, wv).astype(bf16)
 
 
 def gradient_kernel(
     ready,
-    own_ref, r1_ref, r2_ref, r3_ref, logits_ref, gw_ref, pout_t_ref, score_ref, out_hbm, stat_ref, out_ref, out_sem
+    pay_ref, logits_ref, gw_ref, pout_t_ref, score_ref, out_hbm, stat_ref, out_ref, out_sem
 ):
     groups, heads, lanes = logits_ref.shape
     rows = groups * heads
@@ -515,7 +492,7 @@
     s3 = score - s1 - s2
     parts = [s1, s1, s1, s2, s2, s3, jnp.zeros((z - 6 * heads, z), f32)]
     sk = jnp.concatenate(parts, axis=0).T[:, : 6 * heads].astype(bf16)
-    pays = (own_ref, r1_ref, r2_ref, r3_ref)
+    pays = [pay_ref.at[k] for k in range(pay_ref.shape[0])]
     ms = [p[0][:pack] for p in pays]
     ls = [p[0][pack : 2 * pack] for p in pays]
     ns = [p[1][:pack] for p in pays]
@@ -574,37 +551,17 @@
         pltpu.make_async_copy(out_ref.at[at], out_hbm.at[at], out_sem.at[n]).wait()
 
 
-def alignment_kernel(
-    ready,
-    row_ref,
-    col_ref,
-    own_ref,
-    r1_ref,
-    r2_ref,
-    r3_ref,
-    v_ref,
-    gate_ref,
-    x_ref,
-    wf_ref,
-    out_ref,
-    w_ref,
-    gated_ref,
-):
-    pays = (own_ref, r1_ref, r2_ref, r3_ref)
-    nk = len(pays)
-    heads = own_ref.shape[1]
-    wide = own_ref.shape[2]
+def alignment_kernel(ready, pay_ref, v_ref, gate_ref, x_ref, wf_ref, out_ref, w_ref, gated_ref):
+    nk, count, heads, wide = pay_ref.shape
     tile = wide // 2
-    pieces = own_ref.shape[0] - 2
+    pieces = count - 2
     rows = pieces * heads
     half, all_tokens, chans = v_ref.shape
     chans = chans // 2
     tokens = pieces * 2
     head_width = chans // heads
-    row, col = row_ref[0], col_ref[0]
-
     low = lax.broadcasted_iota(jnp.int32, (rows, wide), 1) < tile
-    lgs = [p[2:].reshape(rows, wide) for p in pays]
+    lgs = [pay_ref[k, 2:].reshape(rows, wide) for k in range(nk)]
     peak = functools.reduce(jnp.maximum, lgs)
     m0 = jnp.max(jnp.where(low, peak, far_below), axis=1, keepdims=True)
     m1 = jnp.max(jnp.where(low, far_below, peak), axis=1, keepdims=True)
@@ -614,8 +571,7 @@
     t0 = jnp.sum(jnp.where(low, every, 0.0), axis=1, keepdims=True)
     t1 = jnp.sum(jnp.where(low, 0.0, every), axis=1, keepdims=True)
     total = jnp.where(low, t0, t1)
-    for shift, p in enumerate(ps):
-        source = lax.rem(col + nk - shift, nk)
+    for source, p in enumerate(ps):
         weight = p / total
         rolled = pltpu.roll(weight, tile, 1)
         for n in range(pieces):
@@ -623,8 +579,8 @@
             w_ref[source, :, 2 * n + 1, :] = rolled[n * heads : (n + 1) * heads]
     w = jnp.concatenate(
         [
-            w_ref[jnp.bitwise_xor(row, t)].reshape(heads * tokens, wide)[:, :tile]
-            for t in range(nk)
+            w_ref[k].reshape(heads * tokens, wide)[:, :tile]
+            for k in range(nk)
         ],
         axis=1,
     ).astype(bf16)
@@ -686,8 +642,8 @@
     rows, cols, normed, weights = call(
         prepare_kernel,
         (
-            sds((l_rows + 2 * n_rows, 128), bf16),
-            sds((r_rows + n_rows, 128), bf16),
+            sds((nk, l_rows + 2 * n_rows, 128), bf16),
+            sds((nr, r_rows + n_rows, 128), bf16),
             sds((n_rows, 128), bf16),
             sds((width, 3 * chans), bf16),
         ),
@@ -709,29 +665,17 @@
         final_mixing_weights.T,
     )
 
-    all_cols = [
-        lax.ppermute(
-            cols,
-            ("row", "col"),
-            [(r * nk + c, (c + t) % nr * nk + r) for r in range(nr) for c in range(nk)],
-        )
-        for t in range(nr)
-    ]
-
-    def exchange(x, bit):
-        return lax.ppermute(x, "col", [(c, c ^ bit) for c in range(nk)])
-
-    across = exchange(rows, 2)
-    all_rows = [rows, exchange(rows, 1), across, exchange(across, 1)]
+    parts = lax.all_to_all(cols, "row", 0, 0)
+    all_rows = lax.all_to_all(rows, "col", 0, 0)
+    all_cols = lax.all_to_all(parts, "col", 0, 0)
 
     sides, block = call(
         join_kernel,
         (
             sds((nk * (r_rows + l_rows), 128), bf16),
-            sds((nk, half, tokens, 2 * width), bf16),
+            sds((nr, n_rows, 2 * width), bf16),
         ),
-        smem=2,
-    )(*place[:2], *all_rows, *all_cols)
+    )(all_rows, all_cols, parts)
     if nq == 2:
         far_sides = lax.ppermute(sides, "seq", [(0, 1), (1, 0)])
     else:
@@ -746,25 +690,22 @@
             pltpu.VMEM((4 * width, 4 * chans), bf16),
             pltpu.VMEM((4 * width, 4 * chans), bf16),
             pltpu.VMEM((4 * width, 4 * chans), bf16),
-            pltpu.VMEM((nk, 2, half, tokens, 2 * width), bf16),
-            pltpu.VMEM((nk, half, tokens, 2 * width), bf16),
             pltpu.VMEM((heads, tile_i, head_lanes), bf16),
             pltpu.VMEM((heads, 2 * tile_j, head_lanes), bf16),
         ),
-        smem=2,
         flops=3_000_000_000,
         nbytes=3_000_000,
-    )(*place[:2], *all_rows, *all_cols, weights)
+    )(all_rows, all_cols, weights)
     if nq == 2:
         gw_other = lax.ppermute(gw_own, "seq", [(0, 1), (1, 0)])
     else:
         gw_own, gw_other = lax.psum(gw_own, "seq"), jnp.zeros_like(gw_own)
 
-    def exchange_rows(x, bit):
-        return lax.ppermute(x, "row", [(r, r ^ bit) for r in range(nr)])
-
     block, gw_own = lax.optimization_barrier((block, gw_own))
-    near, beyond = exchange_rows(block, 1), exchange_rows(block, 2)
+    every = [block] + [
+        lax.ppermute(block, "col", [(c, c ^ t) for c in range(nk)]) for t in range(1, nk)
+    ]
+    sides, far_sides, gw_other = lax.optimization_barrier((sides, far_sides, gw_other))
 
     pair_out, pair_t, logits = call(
         update_kernel,
@@ -800,27 +741,23 @@
         pair_input.reshape(tile_i * tile_j, z),
     )
 
-    beyond, logits = lax.optimization_barrier((beyond, logits))
-    every = [block, near, beyond, exchange_rows(beyond, 1)]
     values, gating = call(
         values_kernel,
         (sds((half, nr * nk * tokens, 2 * chans), bf16), sds((seqs * tokens, chans), f32)),
+        scratch=(pltpu.VMEM((nk, nr, n_rows, 2 * width), bf16),),
+        smem=1,
         flops=4_000_000_000,
         nbytes=6_000_000,
-    )(*every, content_weights_grid, normed, sigmoid_weights_grid)
-
-    payload = sds((2 + groups // nk * (pack // 2), heads, 2 * tile_j), f32)
-    gw, pay0, pay1, pay2, pay3 = call(
+    )(col_scalar, *every, content_weights_grid, normed, sigmoid_weights_grid)
+
+    payload = sds((nk, 2 + groups // nk * (pack // 2), heads, 2 * tile_j), f32)
+    gw, pay = call(
         softmax_kernel,
-        (sds((groups, heads, lanes), f32), payload, payload, payload, payload),
+        (sds((groups, heads, lanes), f32), payload),
         smem=1,
     )(col_scalar, logits, gw_own, gw_other, mask)
 
-    got = [
-        lax.ppermute(pay, "col", [(c, (c + shift) % nk) for c in range(nk)])
-        for shift, pay in ((1, pay1), (2, pay2), (3, pay3))
-    ]
-
+    got = lax.all_to_all(pay, "col", 0, 0)
     got, values, gating = lax.optimization_barrier((got, values, gating))
 
     (gradient,) = call(
@@ -834,7 +771,7 @@
         far_out=(0,),
         flops=4_000_000_000,
         nbytes=3_000_000,
-    )(pay0, *got, logits, gw, pair_t, score_matrix.T)
+    )(got, logits, gw, pair_t, score_matrix.T)
 
     (aligned,) = call(
         alignment_kernel,
@@ -843,13 +780,10 @@
             pltpu.VMEM((nk, heads, tokens, 2 * tile_j), f32),
             pltpu.VMEM((seqs * tokens, chans), bf16),
         ),
-        smem=2,
         flops=3_000_000_000,
         nbytes=5_000_000,
     )(
-        *place[:2],
-        pay0,
-        *got,
+        got,
         values,
         gating,
         alignment_input.reshape(seqs * tokens, width),

time: 60.1 us -> 84.1 us (1.40)
  blocking collectives: 0 us -> 41.3 us
  starting transfers between devices: 25.4 us -> 7.37 us
  waiting for transfers between devices: 8.01 us -> 5.89 us
  Pallas kernels: 23.5 us -> 25.3 us
  local copies, waits for them, and re-layouts: 1.85 us -> 2.95 us
    all_to_all x0 -> x3, blocking collectives: none -> 41.3 us  [the longest x1 16.8 us: on_device(): parts = lax.all_to_all(cols, 'row', 0, 0)]
    ppermute x13 -> x3, starting transfers between devices: 23.2 us -> 1.86 us  [on_device(): lax.ppermute(block, 'col', [(c, c ^ t) for c in range(nk)])]
    ppermute x13 -> x3, waiting for transfers between devices: 3.61 us -> 0.01 us  [on_device(): lax.ppermute(block, 'col', [(c, c ^ t) for c in range(nk)])]
    all_to_all x0 -> x1, starting transfers between devices: none -> 3.34 us  [on_device(): got = lax.all_to_all(pay, 'col', 0, 0)]
    pallas_call x8, Pallas kernels: 23.5 us -> 25.3 us  [run(): pl.pallas_call(body, out_shape=out_shape, in_specs=in_specs, out_specs=[p...]
    all_to_all x0 -> x1, waiting for transfers between devices: none -> 1.61 us  [on_device(): got = lax.all_to_all(pay, 'col', 0, 0)]
    unnamed x22 -> x28, local copies, waits for them, and re-layouts: 1.85 us -> 2.95 us
  transfers between devices with their start and end apart: 15 -> 6, of which waited for: 4 -> 2; matrix products, arithmetic and copies ran while one was open for 0% -> 0% of each run, Pallas kernels for 25% -> 20%
where the time goes in v10:
time: 84.1 us; the launch traced here: 83.7 us
  blocking collectives  41.3 us (49%)
  Pallas kernels  25.3 us (30%)
  starting transfers between devices  7.37 us (9%)
  waiting for transfers between devices  5.89 us (7%)
  local copies, waits for them, and re-layouts  2.95 us (4%)
  between operations  0.85 us (1%)
    pallas_call x8, Pallas kernels, run(): pl.pallas_call(body, out_shape=out_shape, in_specs=in_specs, out_specs=[p...  25.3 us
    all_to_all x1, blocking collectives, on_device(): parts = lax.all_to_all(cols, 'row', 0, 0)  16.8 us
    all_to_all x1, blocking collectives, on_device(): all_rows = lax.all_to_all(rows, 'col', 0, 0)  14.6 us
    all_to_all x1, blocking collectives, on_device(): all_cols = lax.all_to_all(parts, 'col', 0, 0)  9.82 us
    ppermute x1, waiting for transfers between devices, on_device(): gw_other = lax.ppermute(gw_own, 'seq', [(0, 1), (1, 0)])  4.27 us
    all_to_all x1, starting transfers between devices, on_device(): got = lax.all_to_all(pay, 'col', 0, 0)  3.34 us
    unnamed x28, local copies, waits for them, and re-layouts  2.95 us
    ppermute x3, starting transfers between devices, on_device(): lax.ppermute(block, 'col', [(c, c ^ t) for c in range(nk)])  1.86 us
  transfers between devices with their start and end apart: 6, of which 2 were waited for; matrix products, arithmetic and copies ran while one was open for 0% of the time, Pallas kernels for 20%

profile of v10, /device:TPU:0, one launch (start us, length us, event | category | flops | bytes accessed | tf_op | source)
XLA Modules:
  0.0 83.7 jit_solution(4103906518826239186)
XLA Ops:
  0.6 3.1 %shard_map.130 = (bf16[4,640,128]{2,1,0:T(8,128)(2,1)}, bf16[4,384,128]{2,1,0:T(8,128)(2,1)}, bf16[256,128]{1,0:T(8,128)(2,1)}, bf16[64,768]{1,0:T(8,128)(2,1)}) custom-call(s32[1]{0:T(128)} %bitcast.2.refs_0_, bf16[32,16,64]{2,1,0:T(8,128)(2,1)} %refs_1_.1, bf16[32,16,64]{2,1,0:T(8,128)(2,1)} %refs_2_.1, bf16[32,64]{1,0:T(8,128)(2,1)} %bitcast.22, ...), custom_call_target="tpu_custom_call" | custom-call | tf_op jit(solution)/shard_map/pallas_call | solution.py:62
  3.8 0.0 copy-start.7
  3.8 14.6 %all_to_all.20.refs_0_ = bf16[4,640,128]{2,1,0:T(8,128)(2,1)S(1)} all-to-all(bf16[4,640,128]{2,1,0:T(8,128)(2,1)} %get-tuple-element.24), channel_id=1, replica_groups=mesh['seq'=2,'row'=4,'col'=4] {'col'}, dimensions={0} | all-to-all | bytes 1310720 | tf_op jit(solution)/shard_map/all_to_all | solution.py:669
  18.4 16.8 %all_to_all.21.refs_2_ = bf16[4,384,128]{2,1,0:T(8,128)(2,1)S(1)} all-to-all(bf16[4,384,128]{2,1,0:T(8,128)(2,1)} %get-tuple-element.25), channel_id=1, replica_groups=mesh['seq'=2,'row'=4,'col'=4] {'row'}, dimensions={0} | all-to-all | bytes 786432 | tf_op jit(solution)/shard_map/all_to_all | solution.py:668
  35.2 9.8 %all_to_all.22.refs_1_ = bf16[4,384,128]{2,1,0:T(8,128)(2,1)S(1)} all-to-all(bf16[4,384,128]{2,1,0:T(8,128)(2,1)S(1)} %all_to_all.21.refs_2_), channel_id=1, replica_groups=mesh['seq'=2,'row'=4,'col'=4] {'col'}, dimensions={0} | all-to-all | bytes 786432 | tf_op jit(solution)/shard_map/all_to_all | solution.py:670
  45.1 1.6 %collective-permute-start = (bf16[1024,128]{1,0:T(8,128)(2,1)S(1)}, bf16[1024,128]{1,0:T(8,128)(2,1)}, u32[]{:S(2)}, u32[]{:S(2)}) collective-permute-start(bf16[1024,128]{1,0:T(8,128)(2,1)S(1)} %get-tuple-element.28.refs_2_), channel_id=1, source_target_pairs={{0,16},{16,0},{1,17},{17,1},{2,18},{18,2},{3,19},{19,3},{4,20},{20... | collective-permute-start | bytes 786440 | tf_op jit(solution)/shard_map/ppermute | solution.py:680
  46.6 0.0 copy-done.7
  46.7 0.0 copy-start.4
  46.7 0.0 copy-start.5
  46.7 0.0 copy-start.6
  46.7 0.0 copy-start.9
  46.7 2.2 %shard_map.132.refs_2_ = f32[16,8,256]{2,1,0:T(8,128)S(1)} custom-call(bf16[4,640,128]{2,1,0:T(8,128)(2,1)S(1)} %all_to_all.20.refs_0_, bf16[4,384,128]{2,1,0:T(8,128)(2,1)S(1)} %all_to_all.22.refs_1_, bf16[64,768]{1,0:T(8,128)(2,1)S(1)} %copy-done.7), custom_call_target="tpu_custom_call" | custom-call | flops 3000000000 | bytes 3000000 | tf_op jit(solution)/shard_map/pallas_call | solution.py:62
  48.9 0.6 collective-permute-start.1
  49.5 0.0 collective-permute-start.2
  49.5 0.3 collective-permute-start.3
  49.9 1.5 %collective-permute-start.4 = (bf16[4,256,128]{2,1,0:T(8,128)(2,1)S(1)}, bf16[4,256,128]{2,1,0:T(8,128)(2,1)S(1)}, u32[]{:S(2)}, u32[]{:S(2)}) collective-permute-start(bf16[4,256,128]{2,1,0:T(8,128)(2,1)S(1)} %get-tuple-element.35.refs_1_), channel_id=1, source_target_pairs={{0,3},{1,2},{2,1},{3,0},{4,7},{5,6},{6,5},{7,4},{8,11},{9,10},{10,... | collective-permute-start | bytes 786440 | tf_op jit(solution)/shard_map/ppermute | solution.py:706
  51.4 4.3 %collective-permute-done.1.refs_3_ = f32[16,8,256]{2,1,0:T(8,128)S(1)} collective-permute-done((f32[16,8,256]{2,1,0:T(8,128)S(1)}, f32[16,8,256]{2,1,0:T(8,128)S(1)}, u32[]{:S(2)}, u32[]{:S(2)}) %collective-permute-start.1) | collective-permute-done | bytes 131104 | tf_op jit(solution)/shard_map/ppermute | solution.py:700
  55.6 0.0 collective-permute-done.refs_3_
  55.6 0.0 copy-done.4
  55.7 0.0 copy-done.5
  55.7 0.0 copy-done.6
  55.7 0.0 copy-done.9
  55.7 0.0 copy-start.1
  55.7 0.0 copy-start.2
  55.7 0.0 copy-start.8
  55.7 12.0 %shard_map.133 = (bf16[4096,128]{1,0:T(8,128)(2,1)}, bf16[16,128,256]{2,1,0:T(8,128)(2,1)S(1)}, f32[16,8,256]{2,1,0:T(8,128)S(1)}) custom-call(s32[1]{0:T(128)} %bitcast.refs_0_, s32[1]{0:T(128)} %bitcast.1.refs_1_, bf16[1024,128]{1,0:T(8,128)(2,1)S(1)} %get-tuple-element.28.refs_2_, bf16[1024,128]{1,0:T(8,128)(2,1)} %collective-permute-done.refs_3_, ...), custom_call_target="tpu_custom_call" | custom-call | flops 14000000000 | bytes 5000000 | tf_op jit(solution)/shard_map/pallas_call | solution.py:62
  67.7 0.0 copy-start.12
  67.7 1.0 %copy-done.12 = bf16[16,128,256]{2,1,0:T(8,128)(2,1)} copy-done((bf16[16,128,256]{2,1,0:T(8,128)(2,1)}, bf16[16,128,256]{2,1,0:T(8,128)(2,1)S(1)}, u32[]{:S(2)}) %copy-start.12) | copy-done | bytes 1048600
  68.7 1.1 %shard_map.134 = (f32[16,8,256]{2,1,0:T(8,128)S(1)}, f32[4,10,8,128]{3,2,1,0:T(8,128)}) custom-call(s32[1]{0:T(128)} %bitcast.refs_0_, f32[16,8,256]{2,1,0:T(8,128)S(1)} %get-tuple-element.30.refs_1_, f32[16,8,256]{2,1,0:T(8,128)S(1)} %shard_map.132.refs_2_, f32[16,8,256]{2,1,0:T(8,128)S(1)} %collective-permute-done.1.refs_3_, s32[1,256]{1,0:T(1,128)S(1)} %bitcast.18), custom_call_target="tpu_custom_call" | custom-call | tf_op jit(solution)/shard_map/pallas_call | solution.py:62
  69.8 3.3 %all-to-all-start.3 = ((f32[4,10,8,128]{3,2,1,0:T(8,128)}), f32[4,10,8,128]{3,2,1,0:T(8,128)S(1)}, u32[]{:S(2)}, u32[]{:S(2)}) async-start(f32[4,10,8,128]{3,2,1,0:T(8,128)} %get-tuple-element.34), calls=%async_computation.3 | async-start | bytes 327680 | tf_op jit(solution)/shard_map/all_to_all | solution.py:760
  73.2 0.0 collective-permute-done.2.refs_2_
  73.2 0.0 collective-permute-done.3.refs_3_
  73.2 0.0 collective-permute-done.4.refs_4_
  73.2 0.0 copy-done.1
  73.2 0.0 copy-done.2
  73.2 0.0 copy-done.8
  73.2 0.0 copy-start.13
  73.2 1.3 %shard_map.135 = (bf16[16,256,512]{2,1,0:T(8,128)(2,1)S(1)}, f32[512,256]{1,0:T(8,128)S(1)}) custom-call(s32[1]{0:T(128)} %bitcast.refs_0_, bf16[4,256,128]{2,1,0:T(8,128)(2,1)S(1)} %get-tuple-element.35.refs_1_, bf16[4,256,128]{2,1,0:T(8,128)(2,1)S(1)} %collective-permute-done.2.refs_2_, bf16[4,256,128]{2,1,0:T(8,128)(2,1)S(1)} %collective-permute-done.3.refs_3_, ...), custom_call_target="tpu_custom_call" | custom-call | flops 4000000000 | bytes 6000000 | tf_op jit(solution)/shard_map/pallas_call | solution.py:62
  74.6 0.0 copy-start.10
  74.6 1.9 %copy-done.10 = bf16[16,256,512]{2,1,0:T(8,128)(2,1)} copy-done((bf16[16,256,512]{2,1,0:T(8,128)(2,1)}, bf16[16,256,512]{2,1,0:T(8,128)(2,1)S(1)}, u32[]{:S(2)}) %copy-start.10) | copy-done | bytes 4194328
  76.5 1.6 %all-to-all-done.3.refs_0_ = f32[4,10,8,128]{3,2,1,0:T(8,128)S(1)} async-done(((f32[4,10,8,128]{3,2,1,0:T(8,128)}), f32[4,10,8,128]{3,2,1,0:T(8,128)S(1)}, u32[]{:S(2)}, u32[]{:S(2)}) %all-to-all-start.3) | async-done | bytes 163872 | tf_op jit(solution)/shard_map/all_to_all | solution.py:760
  78.1 0.0 copy-done.13
  78.1 0.0 copy-start
  78.1 0.0 copy-start.3
  78.1 0.0 copy-start.11
  78.1 3.0 %shard_map.137 = bf16[4096,128]{1,0:T(8,128)(2,1)} custom-call(f32[4,10,8,128]{3,2,1,0:T(8,128)S(1)} %all-to-all-done.3.refs_0_, f32[16,8,256]{2,1,0:T(8,128)S(1)} %get-tuple-element.30.refs_1_, f32[16,8,256]{2,1,0:T(8,128)S(1)} %get-tuple-element.43.refs_2_, bf16[16,128,256]{2,1,0:T(8,128)(2,1)S(1)} %copy-done.13, f32[8,128]{1,0:T(8,128)S(1)} %bitcast.21), custom_call_target="tpu_custom_call" | custom-call | flops 4000000000 | bytes 3000000 | tf_op jit(solution)/shard_map/pallas_call | solution.py:62
  81.1 0.0 copy-done
  81.1 0.0 copy-done.3
  81.1 0.0 copy-done.11
  81.1 2.5 %shard_map.136 = bf16[512,64]{1,0:T(8,128)(2,1)} custom-call(f32[4,10,8,128]{3,2,1,0:T(8,128)S(1)} %all-to-all-done.3.refs_0_, bf16[16,256,512]{2,1,0:T(8,128)(2,1)S(1)} %copy-done.11, f32[512,256]{1,0:T(8,128)S(1)} %get-tuple-element.41.refs_2_, bf16[512,64]{1,0:T(8,128)(2,1)S(1)} %bitcast.13, bf16[64,256]{1,0:T(8,128)(2,1)S(1)} %bitcast.15), custom_call_target="tpu_custom_call" | custom-call | flops 3000000000 | bytes 5000000 | tf_op jit(solution)/shard_map/pallas_call | solution.py:62
  (1 shorter events, 0.0 us)
Async XLA Ops:
  3.8 42.9 %copy-start.7 = (bf16[64,768]{1,0:T(8,128)(2,1)S(1)}, bf16[64,768]{1,0:T(8,128)(2,1)}, u32[]{:S(2)}) copy-start(bf16[64,768]{1,0:T(8,128)(2,1)} %get-tuple-element.27.refs_2_) | copy-start | bytes 294916
  45.1 10.6 %collective-permute-start = (bf16[1024,128]{1,0:T(8,128)(2,1)S(1)}, bf16[1024,128]{1,0:T(8,128)(2,1)}, u32[]{:S(2)}, u32[]{:S(2)}) collective-permute-start(bf16[1024,128]{1,0:T(8,128)(2,1)S(1)} %get-tuple-element.28.refs_2_), channel_id=1, source_target_pairs={{0,16},{16,0},{1,17},{17,1},{2,18},{18,2},{3,19},{19,3},{4,20},{20... | collective-permute-start | bytes 786440 | tf_op jit(solution)/shard_map/ppermute | solution.py:680
  46.7 9.0 %copy-start.4 = (s32[256]{0:T(256)S(1)}, s32[256]{0:T(256)}, u32[]{:S(2)}) copy-start(s32[256]{0:T(256)} %param.13) | copy-start | bytes 3076
  46.7 9.0 %copy-start.5 = (bf16[64,64,128]{2,1,0:T(8,128)(2,1)S(1)}, bf16[64,64,128]{2,1,0:T(8,128)(2,1)}, u32[]{:S(2)}) copy-start(bf16[64,64,128]{2,1,0:T(8,128)(2,1)} %param.12) | copy-start | bytes 3145732
  46.7 9.0 %copy-start.6 = (f32[1024,128]{1,0:T(8,128)S(1)}, f32[1024,128]{1,0:T(8,128)}, u32[]{:S(2)}) copy-start(f32[1024,128]{1,0:T(8,128)} %refs_5_.2) | copy-start | bytes 1572868
  46.7 9.0 %copy-start.9 = (f32[128,8]{0,1:T(8,128)S(1)}, f32[128,8]{0,1:T(8,128)}, u32[]{:S(2)}) copy-start(f32[128,8]{0,1:T(8,128)} %param.19) | copy-start | bytes 12292
  48.9 6.7 %collective-permute-start.1 = (f32[16,8,256]{2,1,0:T(8,128)S(1)}, f32[16,8,256]{2,1,0:T(8,128)S(1)}, u32[]{:S(2)}, u32[]{:S(2)}) collective-permute-start(f32[16,8,256]{2,1,0:T(8,128)S(1)} %shard_map.132.refs_2_), channel_id=1, source_target_pairs={{0,16},{16,0},{1,17},{17,1},{2,18},{18,2},{3,19},{19,3},{4,20},{20... | collective-permute-start | bytes 393224 | tf_op jit(solution)/shard_map/ppermute | solution.py:700
  49.5 23.7 %collective-permute-start.2 = (bf16[4,256,128]{2,1,0:T(8,128)(2,1)S(1)}, bf16[4,256,128]{2,1,0:T(8,128)(2,1)S(1)}, u32[]{:S(2)}, u32[]{:S(2)}) collective-permute-start(bf16[4,256,128]{2,1,0:T(8,128)(2,1)S(1)} %get-tuple-element.35.refs_1_), channel_id=1, source_target_pairs={{0,1},{1,0},{2,3},{3,2},{4,5},{5,4},{6,7},{7,6},{8,9},{9,8},{10,11... | collective-permute-start | bytes 786440 | tf_op jit(solution)/shard_map/ppermute | solution.py:706
  49.5 23.7 %collective-permute-start.3 = (bf16[4,256,128]{2,1,0:T(8,128)(2,1)S(1)}, bf16[4,256,128]{2,1,0:T(8,128)(2,1)S(1)}, u32[]{:S(2)}, u32[]{:S(2)}) collective-permute-start(bf16[4,256,128]{2,1,0:T(8,128)(2,1)S(1)} %get-tuple-element.35.refs_1_), channel_id=1, source_target_pairs={{0,2},{1,3},{2,0},{3,1},{4,6},{5,7},{6,4},{7,5},{8,10},{9,11},{10,... | collective-permute-start | bytes 786440 | tf_op jit(solution)/shard_map/ppermute | solution.py:706
  49.9 23.3 %collective-permute-start.4 = (bf16[4,256,128]{2,1,0:T(8,128)(2,1)S(1)}, bf16[4,256,128]{2,1,0:T(8,128)(2,1)S(1)}, u32[]{:S(2)}, u32[]{:S(2)}) collective-permute-start(bf16[4,256,128]{2,1,0:T(8,128)(2,1)S(1)} %get-tuple-element.35.refs_1_), channel_id=1, source_target_pairs={{0,3},{1,2},{2,1},{3,0},{4,7},{5,6},{6,5},{7,4},{8,11},{9,10},{10,... | collective-permute-start | bytes 786440 | tf_op jit(solution)/shard_map/ppermute | solution.py:706
  55.7 17.5 %copy-start.1 = (bf16[64,256]{1,0:T(8,128)(2,1)S(1)}, bf16[64,256]{1,0:T(8,128)(2,1)}, u32[]{:S(2)}) copy-start(bf16[64,256]{1,0:T(8,128)(2,1)} %refs_5_.3) | copy-start | bytes 98308
  55.7 17.5 %copy-start.2 = (bf16[64,256]{1,0:T(8,128)(2,1)S(1)}, bf16[64,256]{1,0:T(8,128)(2,1)}, u32[]{:S(2)}) copy-start(bf16[64,256]{1,0:T(8,128)(2,1)} %refs_7_.3) | copy-start | bytes 98308
  55.7 17.5 %copy-start.8 = (bf16[256,128]{1,0:T(8,128)(2,1)S(1)}, bf16[256,128]{1,0:T(8,128)(2,1)}, u32[]{:S(2)}) copy-start(bf16[256,128]{1,0:T(8,128)(2,1)} %get-tuple-element.36.refs_6_) | copy-start | bytes 196612
  67.7 1.0 %copy-start.12 = (bf16[16,128,256]{2,1,0:T(8,128)(2,1)}, bf16[16,128,256]{2,1,0:T(8,128)(2,1)S(1)}, u32[]{:S(2)}) copy-start(bf16[16,128,256]{2,1,0:T(8,128)(2,1)S(1)} %get-tuple-element.44.refs_3_) | copy-start | bytes 3145732
  69.8 8.3 %all-to-all-start.3 = ((f32[4,10,8,128]{3,2,1,0:T(8,128)}), f32[4,10,8,128]{3,2,1,0:T(8,128)S(1)}, u32[]{:S(2)}, u32[]{:S(2)}) async-start(f32[4,10,8,128]{3,2,1,0:T(8,128)} %get-tuple-element.34), calls=%async_computation.3 | async-start | bytes 327680 | tf_op jit(solution)/shard_map/all_to_all | solution.py:760
  73.2 4.9 %copy-start.13 = (bf16[16,128,256]{2,1,0:T(8,128)(2,1)S(1)}, bf16[16,128,256]{2,1,0:T(8,128)(2,1)}, u32[]{:S(2)}) copy-start(bf16[16,128,256]{2,1,0:T(8,128)(2,1)} %copy-done.12) | copy-start | bytes 3145732
  74.6 1.9 %copy-start.10 = (bf16[16,256,512]{2,1,0:T(8,128)(2,1)}, bf16[16,256,512]{2,1,0:T(8,128)(2,1)S(1)}, u32[]{:S(2)}) copy-start(bf16[16,256,512]{2,1,0:T(8,128)(2,1)S(1)} %get-tuple-element.40.refs_1_) | copy-start | bytes 12582916
  78.1 3.0 %copy-start = (bf16[32,16,64]{2,1,0:T(8,128)(2,1)S(1)}, bf16[32,16,64]{2,1,0:T(8,128)(2,1)}, u32[]{:S(2)}) copy-start(bf16[32,16,64]{2,1,0:T(8,128)(2,1)} %refs_1_.1) | copy-start | bytes 196612
  78.1 3.0 %copy-start.3 = (bf16[256,64]{0,1:T(8,128)(2,1)S(1)}, bf16[256,64]{0,1:T(8,128)(2,1)}, u32[]{:S(2)}) copy-start(bf16[256,64]{0,1:T(8,128)(2,1)} %param.20) | copy-start | bytes 98308
  78.1 3.0 %copy-start.11 = (bf16[16,256,512]{2,1,0:T(8,128)(2,1)S(1)}, bf16[16,256,512]{2,1,0:T(8,128)(2,1)}, u32[]{:S(2)}) copy-start(bf16[16,256,512]{2,1,0:T(8,128)(2,1)} %copy-done.10) | copy-start | bytes 12582916

commit v11 on v9

--- a/solution.py
+++ b/solution.py
@@ -103,8 +103,7 @@
     wv_ref,
     wg_ref,
     wf_ref,
-    rows_ref,
-    cols_ref,
+    shard_ref,
     norm_ref,
     weights_ref,
     turn_ref,
@@ -130,9 +129,9 @@
 
     packed = two(normed)
     norm_ref[...] = packed
-    rows_ref[-2 * rows : -rows, :] = packed
-    rows_ref[-rows:, :] = two(adj)
-    cols_ref[-rows:, :] = packed
+    base = tokens // pack * w1_ref.shape[0]
+    shard_ref[base : base + rows, :] = two(adj)
+    shard_ref[base + rows : base + 2 * rows, :] = packed
     token = lax.broadcasted_iota(jnp.int32, (seqs, tokens, width), 1) + own_ref[0]
     count = valid_count(mask_ref).reshape(1, 1, 1)
     real = jnp.where(token.astype(f32) < count, normed, 0.0)
@@ -143,7 +142,7 @@
     fc = w1_ref.shape[0]
     wk = pack * seqs
     for g in range(tokens // pack):
-        rows_ref[g * fc : (g + 1) * fc, :] = left[:, g * wk : (g + 1) * wk]
+        shard_ref[g * fc : (g + 1) * fc, :] = left[:, g * wk : (g + 1) * wk]
     size = 128 // tokens
     real = real.astype(bf16)
     w2 = w2_ref[...]
@@ -154,38 +153,38 @@
         res = nt_dot(w2, jnp.concatenate([real[s]] * size, axis=0))
         res = jnp.where(mine, res, 0.0).reshape(fd // size, size, 128)
         place_ref[:, s, :] = jnp.sum(res, axis=1)
-    cols_ref[:-rows, :] = place_ref[...].reshape(fd // size * seqs, 128).astype(bf16)
+    right = place_ref[...].reshape(fd // size * seqs, 128).astype(bf16)
+    shard_ref[base + 2 * rows :, :] = right
 
 
 def join_kernel(
     ready,
     row_ref,
     col_ref,
-    rows0_ref,
-    rows1_ref,
-    rows2_ref,
-    rows3_ref,
+    shard0_ref,
+    shard1_ref,
+    shard2_ref,
+    shard3_ref,
     cols0_ref,
     cols1_ref,
-    cols2_ref,
-    cols3_ref,
     out_ref,
     norm_ref,
 ):
     nk = 4
     row, col = row_ref[0], col_ref[0]
-    r_rows = l_rows = out_ref.shape[0] // (2 * nk)
-    for t, ref in enumerate((cols0_ref, cols1_ref, cols2_ref, cols3_ref)):
-        at = pl.ds(pl.multiple_of(lax.rem(row + nk - t, nk) * r_rows, r_rows), r_rows)
-        out_ref[at, :] = ref[:r_rows, :]
-    for t, ref in enumerate((rows0_ref, rows1_ref, rows2_ref, rows3_ref)):
-        start = nk * r_rows + jnp.bitwise_xor(col, t) * l_rows
-        at = pl.ds(pl.multiple_of(start, l_rows), l_rows)
-        out_ref[at, :] = ref[:l_rows, :]
-        half, tokens, _ = norm_ref.shape[1:]
-        count = half * tokens
-        start = ref.shape[0] - 2 * count
-        norm_ref[jnp.bitwise_xor(col, t)] = ref[start : start + count, :].reshape(norm_ref.shape[1:])
+    size = out_ref.shape[0] // (2 * nk)
+    half, tokens, _ = norm_ref.shape[1:]
+    count = half * tokens
+    for t in range(nk):
+        ref = (cols0_ref, cols1_ref)[t // 2]
+        at = pl.ds(pl.multiple_of(jnp.bitwise_xor(row, t) * size, size), size)
+        end = ref.shape[0] // 2 * (t % 2 + 1)
+        out_ref[at, :] = ref[end - size : end, :]
+    for t, ref in enumerate((shard0_ref, shard1_ref, shard2_ref, shard3_ref)):
+        k = jnp.bitwise_xor(col, t)
+        at = pl.ds(pl.multiple_of((nk + k) * size, size), size)
+        out_ref[at, :] = ref[:size, :]
+        norm_ref[k] = ref[size + count : size + 2 * count, :].reshape(norm_ref.shape[1:])
 
 
 def update_kernel(
@@ -199,7 +198,8 @@
     score_ref,
     pair_ref,
     pout_hbm,
-    pout_t_ref,
+    normal_ref,
+    inverse_ref,
     logits_ref,
     pout_ref,
     out_sem,
@@ -319,12 +319,14 @@
             at = pl.ds(pl.multiple_of(g * lanes, lanes), lanes)
             before = pair_ref[at, :].T.astype(f32)
             result = (before + update_ref[:, e * lanes : (e + 1) * lanes]).astype(bf16)
-            pout_t_ref[g] = result
             x = result.astype(f32)
             pout_ref[at, :] = result.T
             center = x - jnp.mean(x, axis=0, keepdims=True)
             inverse = lax.rsqrt(jnp.mean(center * center, axis=0, keepdims=True) + epsilon)
-            high, low = high_low(center * inverse)
+            normal = center * inverse
+            normal_ref[g] = normal
+            inverse_ref[g] = jnp.broadcast_to(inverse, inverse_ref.shape[1:])
+            high, low = high_low(normal)
             scores = nn_dot(st, jnp.concatenate([high, low], axis=0))
             logits = scores[:heads] + scores[heads : 2 * heads] + scores[2 * heads : 3 * heads]
             logits_ref[g] = jnp.where(maskl, logits, far_below)
@@ -365,8 +367,6 @@
     side3_ref,
     cols0_ref,
     cols1_ref,
-    cols2_ref,
-    cols3_ref,
     weights_ref,
     gw_ref,
     acc_ref,
@@ -383,12 +383,15 @@
     groups, heads, lanes = gw_ref.shape
     row, col = row_ref[0], col_ref[0]
     count = half * tokens
+    size = side0_ref.shape[0] - 2 * count - cols0_ref.shape[0] // 2 + count
     for t, ref in enumerate((side0_ref, side1_ref, side2_ref, side3_ref)):
-        start = ref.shape[0] - 2 * count
-        rows_ref[jnp.bitwise_xor(col, t)] = ref[start:, :].reshape(rows_ref.shape[1:])
-    for t, ref in enumerate((cols0_ref, cols1_ref, cols2_ref, cols3_ref)):
-        start = ref.shape[0] - count
-        cols_ref[lax.rem(row + nk - t, nk)] = ref[start:, :].reshape(cols_ref.shape[1:])
+        k = jnp.bitwise_xor(col, t)
+        rows_ref[k] = ref[size : size + 2 * count, :].reshape(rows_ref.shape[1:])
+    for t in range(nk):
+        ref = (cols0_ref, cols1_ref)[t // 2]
+        start = ref.shape[0] // 2 * (t % 2)
+        part = ref[start : start + count, :]
+        cols_ref[jnp.bitwise_xor(row, t)] = part.reshape(cols_ref.shape[1:])
     chans = weights_ref.shape[1] // 3
     by_heads(weights_ref[:, :chans], heads, bv_ref)
     by_heads(weights_ref[:, chans : 2 * chans], heads, bg_ref)
@@ -414,8 +417,8 @@
         cut = slice(hp * 2 * block, (hp + 1) * 2 * block)
         for n in range(half // 4):
             v = nn_dot(four(lambda k, s: cols_ref[k, s], n), bv_ref[:, cut]).astype(bf16)
-            gate = nn_dot(four(lambda k, s: rows_ref[k, 0, s], n), bg_ref[:, cut])
-            grad = nn_dot(four(lambda k, s: rows_ref[k, 1, s], n), bf_ref[:, cut])
+            gate = nn_dot(four(lambda k, s: rows_ref[k, 1, s], n), bg_ref[:, cut])
+            grad = nn_dot(four(lambda k, s: rows_ref[k, 0, s], n), bf_ref[:, cut])
             g = (grad * jax.nn.sigmoid(gate)).astype(bf16)
             for e in range(2):
                 to = slice((2 * n + e) * block, (2 * n + e + 1) * block)
@@ -504,7 +507,7 @@
 
 def gradient_kernel(
     ready,
-    own_ref, r1_ref, r2_ref, r3_ref, logits_ref, gw_ref, pout_t_ref, score_ref, out_hbm, stat_ref, out_ref, out_sem
+    own_ref, r1_ref, r2_ref, r3_ref, logits_ref, gw_ref, normal_ref, inverse_ref, score_ref, out_hbm, stat_ref, out_ref, out_sem
 ):
     groups, heads, lanes = logits_ref.shape
     rows = groups * heads
@@ -550,10 +553,8 @@
         g3 = gl - g1 - g2
         stack = jnp.concatenate([g1, g2, g3, g1, g2, g1], axis=0).astype(bf16)
         grad = nn_dot(sk, stack)
-        x = pout_t_ref[g].astype(f32)
-        center = x - jnp.mean(x, axis=0, keepdims=True)
-        inverse = lax.rsqrt(jnp.mean(center * center, axis=0, keepdims=True) + epsilon)
-        normal = center * inverse
+        normal = normal_ref[g]
+        inverse = inverse_ref[g][:1]
         centered = grad - jnp.mean(grad, axis=0, keepdims=True)
         along = jnp.mean(grad * normal, axis=0, keepdims=True)
         result = inverse * (centered - normal * along)
@@ -683,11 +684,10 @@
     l_rows = tokens // pack * fc
     r_rows = fd * tokens // 128 * seqs
     n_rows = half * tokens
-    rows, cols, normed, weights = call(
+    shard, normed, weights = call(
         prepare_kernel,
         (
-            sds((l_rows + 2 * n_rows, 128), bf16),
-            sds((r_rows + n_rows, 128), bf16),
+            sds((l_rows + 2 * n_rows + r_rows, 128), bf16),
             sds((n_rows, 128), bf16),
             sds((width, 3 * chans), bf16),
         ),
@@ -709,20 +709,21 @@
         final_mixing_weights.T,
     )
 
+    def exchange(x, bit):
+        return lax.ppermute(x, "col", [(c, c ^ bit) for c in range(nk)])
+
+    other = exchange(shard, 1)
+    across = exchange(shard, 2)
+    all_rows = [shard, other, across, exchange(across, 1)]
+    pair = jnp.concatenate([x[l_rows + n_rows :] for x in (shard, other)], axis=0)
     all_cols = [
         lax.ppermute(
-            cols,
+            pair,
             ("row", "col"),
-            [(r * nk + c, (c + t) % nr * nk + r) for r in range(nr) for c in range(nk)],
+            [(r * nk + c, (c ^ flip) * nk + r) for r in range(nr) for c in range(nk)],
         )
-        for t in range(nr)
+        for flip in (0, 2)
     ]
-
-    def exchange(x, bit):
-        return lax.ppermute(x, "col", [(c, c ^ bit) for c in range(nk)])
-
-    across = exchange(rows, 2)
-    all_rows = [rows, exchange(rows, 1), across, exchange(across, 1)]
 
     sides, block = call(
         join_kernel,
@@ -763,14 +764,15 @@
     def exchange_rows(x, bit):
         return lax.ppermute(x, "row", [(r, r ^ bit) for r in range(nr)])
 
-    block, gw_own = lax.optimization_barrier((block, gw_own))
+    block, _ = lax.optimization_barrier((block, gw_own))
     near, beyond = exchange_rows(block, 1), exchange_rows(block, 2)
 
-    pair_out, pair_t, logits = call(
+    pair_out, normal, inverse, logits = call(
         update_kernel,
         (
             sds((tile_i * tile_j, z), bf16),
-            sds((groups, z, lanes), bf16),
+            sds((groups, z, lanes), f32),
+            sds((groups, 8, lanes), f32),
             sds((groups, heads, lanes), f32),
         ),
         scratch=(
@@ -800,15 +802,6 @@
         pair_input.reshape(tile_i * tile_j, z),
     )
 
-    beyond, logits = lax.optimization_barrier((beyond, logits))
-    every = [block, near, beyond, exchange_rows(beyond, 1)]
-    values, gating = call(
-        values_kernel,
-        (sds((half, nr * nk * tokens, 2 * chans), bf16), sds((seqs * tokens, chans), f32)),
-        flops=4_000_000_000,
-        nbytes=6_000_000,
-    )(*every, content_weights_grid, normed, sigmoid_weights_grid)
-
     payload = sds((2 + groups // nk * (pack // 2), heads, 2 * tile_j), f32)
     gw, pay0, pay1, pay2, pay3 = call(
         softmax_kernel,
@@ -821,7 +814,8 @@
         for shift, pay in ((1, pay1), (2, pay2), (3, pay3))
     ]
 
-    got, values, gating = lax.optimization_barrier((got, values, gating))
+    near, beyond, pay0 = lax.optimization_barrier((near, beyond, pay0))
+    every = [block, near, beyond, exchange_rows(beyond, 1)]
 
     (gradient,) = call(
         gradient_kernel,
@@ -834,7 +828,14 @@
         far_out=(0,),
         flops=4_000_000_000,
         nbytes=3_000_000,
-    )(pay0, *got, logits, gw, pair_t, score_matrix.T)
+    )(pay0, *got, logits, gw, normal, inverse, score_matrix.T)
+
+    values, gating = call(
+        values_kernel,
+        (sds((half, nr * nk * tokens, 2 * chans), bf16), sds((seqs * tokens, chans), f32)),
+        flops=4_000_000_000,
+        nbytes=6_000_000,
+    )(*every, content_weights_grid, normed, sigmoid_weights_grid)
 
     (aligned,) = call(
         alignment_kernel,

time: 60.1 us -> 63.1 us (1.050)
  waiting for transfers between devices: 8.01 us -> 11.9 us
  starting transfers between devices: 25.4 us -> 24 us
  local copies, waits for them, and re-layouts: 1.85 us -> 2.8 us
    ppermute x4 -> x2, starting transfers between devices: 10.3 us -> 3.47 us  [on_device(): lax.ppermute(pair, ('row', 'col'), [(r * nk + c, (c ^ flip) * nk + r) for...]
    ppermute x3, starting transfers between devices: 4.89 us -> 11.4 us  [exchange_rows(): return lax.ppermute(x, 'row', [(r, r ^ bit) for r in range(nr)])]
    ppermute x1, waiting for transfers between devices: 4.4 us -> 0.01 us  [on_device(): gw_other = lax.ppermute(gw_own, 'seq', [(0, 1), (1, 0)])]
    ppermute x3, waiting for transfers between devices: 0.75 us -> 4.81 us  [exchange(): return lax.ppermute(x, 'col', [(c, c ^ bit) for c in range(nk)])]
    ppermute x3, waiting for transfers between devices: 0.01 us -> 2.52 us  [exchange_rows(): return lax.ppermute(x, 'row', [(r, r ^ bit) for r in range(nr)])]
    ppermute x3, starting transfers between devices: 5.09 us -> 2.97 us  [exchange(): return lax.ppermute(x, 'col', [(c, c ^ bit) for c in range(nk)])]
    ppermute x4 -> x2, waiting for transfers between devices: 2.53 us -> 4.3 us  [on_device(): lax.ppermute(pair, ('row', 'col'), [(r * nk + c, (c ^ flip) * nk + r) for...]
    ppermute x3, starting transfers between devices: 2.95 us -> 3.97 us  [on_device(): lax.ppermute(pay, 'col', [(c, (c + shift) % nk) for c in range(nk)])]
  transfers between devices with their start and end apart: 15 -> 13, of which waited for: 4 -> 4; matrix products, arithmetic and copies ran while one was open for 0% -> 2% of each run, Pallas kernels for 25% -> 26%
where the time goes in v11:
time: 63.1 us; the launch traced here: 62.9 us
  starting transfers between devices  24 us (38%)
  Pallas kernels  23.4 us (37%)
  waiting for transfers between devices  11.9 us (19%)
  local copies, waits for them, and re-layouts  2.8 us (4%)
  between operations  0.8 us (1%)
    pallas_call x8, Pallas kernels, run(): pl.pallas_call(body, out_shape=out_shape, in_specs=in_specs, out_specs=[p...  23.4 us
    ppermute x3, starting transfers between devices, exchange_rows(): return lax.ppermute(x, 'row', [(r, r ^ bit) for r in range(nr)])  11.4 us
    ppermute x3, waiting for transfers between devices, exchange(): return lax.ppermute(x, 'col', [(c, c ^ bit) for c in range(nk)])  4.81 us
    ppermute x2, waiting for transfers between devices, on_device(): lax.ppermute(pair, ('row', 'col'), [(r * nk + c, (c ^ flip) * nk + r) for...  4.3 us
    ppermute x3, starting transfers between devices, on_device(): lax.ppermute(pay, 'col', [(c, (c + shift) % nk) for c in range(nk)])  3.97 us
    ppermute x2, starting transfers between devices, on_device(): lax.ppermute(pair, ('row', 'col'), [(r * nk + c, (c ^ flip) * nk + r) for...  3.47 us
    ppermute x3, starting transfers between devices, exchange(): return lax.ppermute(x, 'col', [(c, c ^ bit) for c in range(nk)])  2.97 us
    ppermute x3, waiting for transfers between devices, exchange_rows(): return lax.ppermute(x, 'row', [(r, r ^ bit) for r in range(nr)])  2.52 us
  transfers between devices with their start and end apart: 13, of which 4 were waited for; matrix products, arithmetic and copies ran while one was open for 2% of the time, Pallas kernels for 26%

profile of v11, /device:TPU:0, one launch (start us, length us, event | category | flops | bytes accessed | tf_op | source)
XLA Modules:
  0.0 62.9 jit_solution(14279488038215362703)
XLA Ops:
  0.6 2.9 %shard_map.130 = (bf16[768,128]{1,0:T(8,128)(2,1)}, bf16[256,128]{1,0:T(8,128)(2,1)}, bf16[64,768]{1,0:T(8,128)(2,1)}) custom-call(s32[1]{0:T(128)} %bitcast.2.refs_0_, bf16[32,16,64]{2,1,0:T(8,128)(2,1)} %refs_1_.1, bf16[32,16,64]{2,1,0:T(8,128)(2,1)} %refs_2_.1, bf16[32,64]{1,0:T(8,128)(2,1)} %bitcast.23, bf16[32,64]{1,0:T(8,128)(2,1)} %bitcast.24, ...), custom_call_target="tpu_custom_call" | custom-call | tf_op jit(solution)/shard_map/pallas_call | solution.py:62
  3.5 0.5 collective-permute-start
  4.0 2.5 %collective-permute-start.1 = (bf16[768,128]{1,0:T(8,128)(2,1)}, bf16[768,128]{1,0:T(8,128)(2,1)S(1)}, u32[]{:S(2)}, u32[]{:S(2)}) collective-permute-start(bf16[768,128]{1,0:T(8,128)(2,1)} %get-tuple-element.23.refs_2_), channel_id=1, source_target_pairs={{0,2},{1,3},{2,0},{3,1},{4,6},{5,7},{6,4},{7,5},{8,10},{9,11},{10,... | collective-permute-start | bytes 589832 | tf_op jit(solution)/shard_map/ppermute | solution.py:713
  6.5 0.9 %slice.6 = bf16[384,128]{1,0:T(8,128)(2,1)S(1)} slice(bf16[768,128]{1,0:T(8,128)(2,1)} %get-tuple-element.23.refs_2_), slice={[384:768], [0:128]} | slice | bytes 196608 | tf_op jit(solution)/shard_map/slice | solution.py:718
  7.4 0.0 collective-permute-done.refs_3_
  7.5 4.8 %collective-permute-done.1.refs_4_ = bf16[768,128]{1,0:T(8,128)(2,1)S(1)} collective-permute-done((bf16[768,128]{1,0:T(8,128)(2,1)}, bf16[768,128]{1,0:T(8,128)(2,1)S(1)}, u32[]{:S(2)}, u32[]{:S(2)}) %collective-permute-start.1) | collective-permute-done | bytes 196640 | tf_op jit(solution)/shard_map/ppermute | solution.py:713
  12.3 0.0 collective-permute-start.2
  12.3 2.8 %collective-permute-start.4 = (bf16[768,128]{1,0:T(8,128)(2,1)S(1)}, bf16[768,128]{1,0:T(8,128)(2,1)S(1)}, u32[]{:S(2)}, u32[]{:S(2)}) collective-permute-start(bf16[768,128]{1,0:T(8,128)(2,1)S(1)} %pad_maximum_fusion), channel_id=1, source_target_pairs={{0,8},{1,12},{2,0},{3,4},{4,9},{5,13},{6,1},{7,5},{8,10},{9,14},{1... | collective-permute-start | bytes 589832 | tf_op jit(solution)/shard_map/ppermute | solution.py:720
  15.1 0.7 %collective-permute-start.3 = (bf16[768,128]{1,0:T(8,128)(2,1)S(1)}, bf16[768,128]{1,0:T(8,128)(2,1)S(1)}, u32[]{:S(2)}, u32[]{:S(2)}) collective-permute-start(bf16[768,128]{1,0:T(8,128)(2,1)S(1)} %pad_maximum_fusion), channel_id=1, source_target_pairs={{0,0},{1,4},{2,8},{3,12},{4,1},{5,5},{6,9},{7,13},{8,2},{9,6},{10,... | collective-permute-start | bytes 589832 | tf_op jit(solution)/shard_map/ppermute | solution.py:720
  15.7 0.0 collective-permute-done.2.refs_5_
  15.8 4.3 %collective-permute-done.4.refs_7_ = bf16[768,128]{1,0:T(8,128)(2,1)S(1)} collective-permute-done((bf16[768,128]{1,0:T(8,128)(2,1)S(1)}, bf16[768,128]{1,0:T(8,128)(2,1)S(1)}, u32[]{:S(2)}, u32[]{:S(2)}) %collective-permute-start.4) | collective-permute-done | bytes 196640 | tf_op jit(solution)/shard_map/ppermute | solution.py:720
  20.1 0.0 collective-permute-done.3.refs_6_
  20.1 0.0 copy-start
  20.1 0.9 %copy-done = bf16[768,128]{1,0:T(8,128)(2,1)S(1)} copy-done((bf16[768,128]{1,0:T(8,128)(2,1)S(1)}, bf16[768,128]{1,0:T(8,128)(2,1)}, u32[]{:S(2)}) %copy-start) | copy-done | bytes 196632
  21.0 1.8 %collective-permute-start.7 = (bf16[1024,128]{1,0:T(8,128)(2,1)S(1)}, bf16[1024,128]{1,0:T(8,128)(2,1)S(1)}, u32[]{:S(2)}, u32[]{:S(2)}) collective-permute-start(bf16[1024,128]{1,0:T(8,128)(2,1)S(1)} %get-tuple-element.27.refs_2_), channel_id=1, source_target_pairs={{0,16},{16,0},{1,17},{17,1},{2,18},{18,2},{3,19},{19,3},{4,20},{20... | collective-permute-start | bytes 786440 | tf_op jit(solution)/shard_map/ppermute | solution.py:737
  22.8 0.0 copy-start.8
  22.8 0.9 %copy-done.8 = bf16[64,768]{1,0:T(8,128)(2,1)S(1)} copy-done((bf16[64,768]{1,0:T(8,128)(2,1)S(1)}, bf16[64,768]{1,0:T(8,128)(2,1)}, u32[]{:S(2)}) %copy-start.8) | copy-done | bytes 98328
  23.7 0.0 copy-start.5
  23.7 0.0 copy-start.6
  23.7 0.0 copy-start.7
  23.7 0.0 copy-start.10
  23.7 2.3 %shard_map.132.refs_2_ = f32[16,8,256]{2,1,0:T(8,128)S(1)} custom-call(s32[1]{0:T(128)} %bitcast.refs_0_, s32[1]{0:T(128)} %bitcast.1.refs_1_.refs_0_, bf16[768,128]{1,0:T(8,128)(2,1)S(1)} %copy-done, bf16[768,128]{1,0:T(8,128)(2,1)S(1)} %collective-permute-done.refs_3_, bf16[768,128]{1,0:T(8,128)(2,1)S(1)} %collective-permute-done.1.refs_4_, ...), custom_call_target="tpu_custom_call" | custom-call | flops 3000000000 | bytes 3000000 | tf_op jit(solution)/shard_map/pallas_call | solution.py:62
  26.0 0.4 collective-permute-start.8
  26.4 7.7 %collective-permute-start.6 = (bf16[4,16,16,128]{3,2,1,0:T(8,128)(2,1)S(1)}, bf16[4,16,16,128]{3,2,1,0:T(8,128)(2,1)S(1)}, u32[]{:S(2)}, u32[]{:S(2)}) collective-permute-start(bf16[4,16,16,128]{3,2,1,0:T(8,128)(2,1)S(1)} %get-tuple-element.26.refs_0_), channel_id=1, source_target_pairs={{0,8},{4,12},{8,0},{12,4},{1,9},{5,13},{9,1},{13,5},{2,10},{6,14},... | collective-permute-start | bytes 786440 | tf_op jit(solution)/shard_map/ppermute | solution.py:765
  34.1 1.8 %collective-permute-start.5 = (bf16[4,16,16,128]{3,2,1,0:T(8,128)(2,1)S(1)}, bf16[4,16,16,128]{3,2,1,0:T(8,128)(2,1)S(1)}, u32[]{:S(2)}, u32[]{:S(2)}) collective-permute-start(bf16[4,16,16,128]{3,2,1,0:T(8,128)(2,1)S(1)} %get-tuple-element.26.refs_0_), channel_id=1, source_target_pairs={{0,4},{4,0},{8,12},{12,8},{1,5},{5,1},{9,13},{13,9},{2,6},{6,2},{1... | collective-permute-start | bytes 786440 | tf_op jit(solution)/shard_map/ppermute | solution.py:765
  35.9 0.0 collective-permute-done.7.refs_3_
  35.9 0.0 copy-done.5
  35.9 0.0 copy-done.6
  36.0 0.0 copy-done.7
  36.0 0.0 copy-done.10
  36.0 11.0 %shard_map.133 = (bf16[4096,128]{1,0:T(8,128)(2,1)}, f32[16,128,256]{2,1,0:T(8,128)S(1)}, f32[16,8,256]{2,1,0:T(8,128)S(1)}, f32[16,8,256]{2,1,0:T(8,128)S(1)}) custom-call(s32[1]{0:T(128)} %bitcast.1.refs_1_.refs_0_, s32[1]{0:T(128)} %bitcast.7.refs_1_, bf16[1024,128]{1,0:T(8,128)(2,1)S(1)} %get-tuple-element.27.refs_2_, ...), custom_call_target="tpu_custom_call" | custom-call | flops 14000000000 | bytes 5000000 | tf_op jit(solution)/shard_map/pallas_call | solution.py:62
  47.0 0.0 collective-permute-done.8.refs_3_
  47.0 0.5 shard_map.134
  47.5 1.8 %collective-permute-start.9 = (f32[10,8,128]{2,1,0:T(8,128)S(1)}, f32[10,8,128]{2,1,0:T(8,128)S(1)}, u32[]{:S(2)}, u32[]{:S(2)}) collective-permute-start(f32[10,8,128]{2,1,0:T(8,128)S(1)} %get-tuple-element.31), channel_id=1, source_target_pairs={{0,1},{1,2},{2,3},{3,0},{4,5},{5,6},{6,7},{7,4},{8,9},{9,10},{10,1... | collective-permute-start | bytes 122888 | tf_op jit(solution)/shard_map/ppermute | solution.py:813
  49.3 0.8 %collective-permute-start.10 = (f32[10,8,128]{2,1,0:T(8,128)S(1)}, f32[10,8,128]{2,1,0:T(8,128)S(1)}, u32[]{:S(2)}, u32[]{:S(2)}) collective-permute-start(f32[10,8,128]{2,1,0:T(8,128)S(1)} %get-tuple-element.32), channel_id=1, source_target_pairs={{0,2},{1,3},{2,0},{3,1},{4,6},{5,7},{6,4},{7,5},{8,10},{9,11},{10,... | collective-permute-start | bytes 122888 | tf_op jit(solution)/shard_map/ppermute | solution.py:813
  50.1 1.4 %collective-permute-start.11 = (f32[10,8,128]{2,1,0:T(8,128)S(1)}, f32[10,8,128]{2,1,0:T(8,128)S(1)}, u32[]{:S(2)}, u32[]{:S(2)}) collective-permute-start(f32[10,8,128]{2,1,0:T(8,128)S(1)} %get-tuple-element.33), channel_id=1, source_target_pairs={{0,3},{1,0},{2,1},{3,2},{4,7},{5,4},{6,5},{7,6},{8,11},{9,8},{10,9... | collective-permute-start | bytes 122888 | tf_op jit(solution)/shard_map/ppermute | solution.py:813
  51.5 0.0 collective-permute-done.6.refs_2_
  51.5 0.0 collective-permute-done.5.refs_1_
  51.5 1.9 %collective-permute-start.12 = (bf16[4,16,16,128]{3,2,1,0:T(8,128)(2,1)S(1)}, bf16[4,16,16,128]{3,2,1,0:T(8,128)(2,1)S(1)}, u32[]{:S(2)}, u32[]{:S(2)}) collective-permute-start(bf16[4,16,16,128]{3,2,1,0:T(8,128)(2,1)S(1)} %collective-permute-done.6.refs_2_), channel_id=1, source_target_pairs={{0,4},{4,0},{8,12},{12,8},{1,5},{5,1},{9,13},{13,9},{2,6},{6,2},{1... | collective-permute-start | bytes 786440 | tf_op jit(solution)/shard_map/ppermute | solution.py:765
  53.4 0.0 collective-permute-done.9.refs_3_.refs_1_
  53.4 0.2 collective-permute-done.10.refs_4_.refs_2_
  53.6 0.0 collective-permute-done.11.refs_5_.refs_3_
  53.6 0.0 copy-start.2
  53.6 0.0 copy-start.3
  53.6 0.0 copy-start.9
  53.6 2.8 %shard_map.137 = bf16[4096,128]{1,0:T(8,128)(2,1)} custom-call(f32[10,8,128]{2,1,0:T(8,128)S(1)} %get-tuple-element.30.refs_2_.refs_0_, f32[10,8,128]{2,1,0:T(8,128)S(1)} %collective-permute-done.9.refs_3_.refs_1_, f32[10,8,128]{2,1,0:T(8,128)S(1)} %collective-permute-done.10.refs_4_.refs_2_, f32[10,8,128]{2,1,0:T(8,128)S(1)} %collective-permute-done.11.refs_5_.refs_3_, ...), custom_call_target="tpu_custom_call" | custom-call | flops 4000000000 | bytes 3000000 | tf_op jit(solution)/shard_map/pallas_call | solution.py:62
  56.4 2.5 %collective-permute-done.12.refs_3_ = bf16[4,16,16,128]{3,2,1,0:T(8,128)(2,1)S(1)} collective-permute-done((bf16[4,16,16,128]{3,2,1,0:T(8,128)(2,1)S(1)}, bf16[4,16,16,128]{3,2,1,0:T(8,128)(2,1)S(1)}, u32[]{:S(2)}, u32[]{:S(2)}) %collective-permute-start.12) | collective-permute-done | bytes 262176 | tf_op jit(solution)/shard_map/ppermute | solution.py:765
  58.9 0.0 copy-done.2
  58.9 0.0 copy-done.3
  58.9 0.0 copy-done.9
  59.0 0.0 copy-start.1
  59.0 0.0 copy-start.4
  59.0 1.3 %shard_map.135 = (bf16[16,256,512]{2,1,0:T(8,128)(2,1)S(1)}, f32[512,256]{1,0:T(8,128)S(1)}) custom-call(bf16[4,16,16,128]{3,2,1,0:T(8,128)(2,1)S(1)} %get-tuple-element.26.refs_0_, bf16[4,16,16,128]{3,2,1,0:T(8,128)(2,1)S(1)} %collective-permute-done.5.refs_1_, bf16[4,16,16,128]{3,2,1,0:T(8,128)(2,1)S(1)} %collective-permute-done.6.refs_2_, ...), custom_call_target="tpu_custom_call" | custom-call | flops 4000000000 | bytes 6000000 | tf_op jit(solution)/shard_map/pallas_call | solution.py:62
  60.3 0.0 copy-done.1
  60.3 0.0 copy-done.4
  60.3 2.6 %shard_map.136 = bf16[512,64]{1,0:T(8,128)(2,1)} custom-call(s32[1]{0:T(128)} %bitcast.refs_0_, s32[1]{0:T(128)} %bitcast.1.refs_1_.refs_0_, f32[10,8,128]{2,1,0:T(8,128)S(1)} %get-tuple-element.30.refs_2_.refs_0_, f32[10,8,128]{2,1,0:T(8,128)S(1)} %collective-permute-done.9.refs_3_.refs_1_, f32[10,8,128]{2,1,0:T(8,128)S(1)} %collective-permute-done.10.refs_4_.refs_2_, ...), custom_call_target="tpu_custom_call" | custom-call | flops 3000000000 | bytes 5000000 | tf_op jit(solution)/shard_map/pallas_call | solution.py:62
  (3 shorter events, 0.1 us)
Async XLA Ops:
  3.5 3.9 %collective-permute-start = (bf16[768,128]{1,0:T(8,128)(2,1)}, bf16[768,128]{1,0:T(8,128)(2,1)S(1)}, u32[]{:S(2)}, u32[]{:S(2)}) collective-permute-start(bf16[768,128]{1,0:T(8,128)(2,1)} %get-tuple-element.23.refs_2_), channel_id=1, source_target_pairs={{0,1},{1,0},{2,3},{3,2},{4,5},{5,4},{6,7},{7,6},{8,9},{9,8},{10,11... | collective-permute-start | bytes 589832 | tf_op jit(solution)/shard_map/ppermute | solution.py:713
  4.0 8.3 %collective-permute-start.1 = (bf16[768,128]{1,0:T(8,128)(2,1)}, bf16[768,128]{1,0:T(8,128)(2,1)S(1)}, u32[]{:S(2)}, u32[]{:S(2)}) collective-permute-start(bf16[768,128]{1,0:T(8,128)(2,1)} %get-tuple-element.23.refs_2_), channel_id=1, source_target_pairs={{0,2},{1,3},{2,0},{3,1},{4,6},{5,7},{6,4},{7,5},{8,10},{9,11},{10,... | collective-permute-start | bytes 589832 | tf_op jit(solution)/shard_map/ppermute | solution.py:713
  12.3 3.5 %collective-permute-start.2 = (bf16[768,128]{1,0:T(8,128)(2,1)S(1)}, bf16[768,128]{1,0:T(8,128)(2,1)S(1)}, u32[]{:S(2)}, u32[]{:S(2)}) collective-permute-start(bf16[768,128]{1,0:T(8,128)(2,1)S(1)} %collective-permute-done.1.refs_4_), channel_id=1, source_target_pairs={{0,1},{1,0},{2,3},{3,2},{4,5},{5,4},{6,7},{7,6},{8,9},{9,8},{10,11... | collective-permute-start | bytes 589832 | tf_op jit(solution)/shard_map/ppermute | solution.py:713
  12.3 7.8 %collective-permute-start.4 = (bf16[768,128]{1,0:T(8,128)(2,1)S(1)}, bf16[768,128]{1,0:T(8,128)(2,1)S(1)}, u32[]{:S(2)}, u32[]{:S(2)}) collective-permute-start(bf16[768,128]{1,0:T(8,128)(2,1)S(1)} %pad_maximum_fusion), channel_id=1, source_target_pairs={{0,8},{1,12},{2,0},{3,4},{4,9},{5,13},{6,1},{7,5},{8,10},{9,14},{1... | collective-permute-start | bytes 589832 | tf_op jit(solution)/shard_map/ppermute | solution.py:720
  15.1 5.0 %collective-permute-start.3 = (bf16[768,128]{1,0:T(8,128)(2,1)S(1)}, bf16[768,128]{1,0:T(8,128)(2,1)S(1)}, u32[]{:S(2)}, u32[]{:S(2)}) collective-permute-start(bf16[768,128]{1,0:T(8,128)(2,1)S(1)} %pad_maximum_fusion), channel_id=1, source_target_pairs={{0,0},{1,4},{2,8},{3,12},{4,1},{5,5},{6,9},{7,13},{8,2},{9,6},{10,... | collective-permute-start | bytes 589832 | tf_op jit(solution)/shard_map/ppermute | solution.py:720
  20.1 0.9 %copy-start = (bf16[768,128]{1,0:T(8,128)(2,1)S(1)}, bf16[768,128]{1,0:T(8,128)(2,1)}, u32[]{:S(2)}) copy-start(bf16[768,128]{1,0:T(8,128)(2,1)} %get-tuple-element.23.refs_2_) | copy-start | bytes 589828
  21.0 14.9 %collective-permute-start.7 = (bf16[1024,128]{1,0:T(8,128)(2,1)S(1)}, bf16[1024,128]{1,0:T(8,128)(2,1)S(1)}, u32[]{:S(2)}, u32[]{:S(2)}) collective-permute-start(bf16[1024,128]{1,0:T(8,128)(2,1)S(1)} %get-tuple-element.27.refs_2_), channel_id=1, source_target_pairs={{0,16},{16,0},{1,17},{17,1},{2,18},{18,2},{3,19},{19,3},{4,20},{20... | collective-permute-start | bytes 786440 | tf_op jit(solution)/shard_map/ppermute | solution.py:737
  22.8 0.9 %copy-start.8 = (bf16[64,768]{1,0:T(8,128)(2,1)S(1)}, bf16[64,768]{1,0:T(8,128)(2,1)}, u32[]{:S(2)}) copy-start(bf16[64,768]{1,0:T(8,128)(2,1)} %get-tuple-element.25.refs_8_) | copy-start | bytes 294916
  23.7 12.3 %copy-start.5 = (s32[256]{0:T(256)S(1)}, s32[256]{0:T(256)}, u32[]{:S(2)}) copy-start(s32[256]{0:T(256)} %param.13) | copy-start | bytes 3076
  23.7 12.3 %copy-start.6 = (bf16[64,64,128]{2,1,0:T(8,128)(2,1)S(1)}, bf16[64,64,128]{2,1,0:T(8,128)(2,1)}, u32[]{:S(2)}) copy-start(bf16[64,64,128]{2,1,0:T(8,128)(2,1)} %param.12) | copy-start | bytes 3145732
  23.7 12.3 %copy-start.7 = (f32[1024,128]{1,0:T(8,128)S(1)}, f32[1024,128]{1,0:T(8,128)}, u32[]{:S(2)}) copy-start(f32[1024,128]{1,0:T(8,128)} %refs_5_.1) | copy-start | bytes 1572868
  23.7 12.3 %copy-start.10 = (f32[128,8]{0,1:T(8,128)S(1)}, f32[128,8]{0,1:T(8,128)}, u32[]{:S(2)}) copy-start(f32[128,8]{0,1:T(8,128)} %param.19) | copy-start | bytes 12292
  26.0 21.0 %collective-permute-start.8 = (f32[16,8,256]{2,1,0:T(8,128)S(1)}, f32[16,8,256]{2,1,0:T(8,128)S(1)}, u32[]{:S(2)}, u32[]{:S(2)}) collective-permute-start(f32[16,8,256]{2,1,0:T(8,128)S(1)} %shard_map.132.refs_2_), channel_id=1, source_target_pairs={{0,16},{16,0},{1,17},{17,1},{2,18},{18,2},{3,19},{19,3},{4,20},{20... | collective-permute-start | bytes 393224 | tf_op jit(solution)/shard_map/ppermute | solution.py:760
  26.4 25.1 %collective-permute-start.6 = (bf16[4,16,16,128]{3,2,1,0:T(8,128)(2,1)S(1)}, bf16[4,16,16,128]{3,2,1,0:T(8,128)(2,1)S(1)}, u32[]{:S(2)}, u32[]{:S(2)}) collective-permute-start(bf16[4,16,16,128]{3,2,1,0:T(8,128)(2,1)S(1)} %get-tuple-element.26.refs_0_), channel_id=1, source_target_pairs={{0,8},{4,12},{8,0},{12,4},{1,9},{5,13},{9,1},{13,5},{2,10},{6,14},... | collective-permute-start | bytes 786440 | tf_op jit(solution)/shard_map/ppermute | solution.py:765
  34.1 17.4 %collective-permute-start.5 = (bf16[4,16,16,128]{3,2,1,0:T(8,128)(2,1)S(1)}, bf16[4,16,16,128]{3,2,1,0:T(8,128)(2,1)S(1)}, u32[]{:S(2)}, u32[]{:S(2)}) collective-permute-start(bf16[4,16,16,128]{3,2,1,0:T(8,128)(2,1)S(1)} %get-tuple-element.26.refs_0_), channel_id=1, source_target_pairs={{0,4},{4,0},{8,12},{12,8},{1,5},{5,1},{9,13},{13,9},{2,6},{6,2},{1... | collective-permute-start | bytes 786440 | tf_op jit(solution)/shard_map/ppermute | solution.py:765
  47.5 5.9 %collective-permute-start.9 = (f32[10,8,128]{2,1,0:T(8,128)S(1)}, f32[10,8,128]{2,1,0:T(8,128)S(1)}, u32[]{:S(2)}, u32[]{:S(2)}) collective-permute-start(f32[10,8,128]{2,1,0:T(8,128)S(1)} %get-tuple-element.31), channel_id=1, source_target_pairs={{0,1},{1,2},{2,3},{3,0},{4,5},{5,6},{6,7},{7,4},{8,9},{9,10},{10,1... | collective-permute-start | bytes 122888 | tf_op jit(solution)/shard_map/ppermute | solution.py:813
  49.3 4.3 %collective-permute-start.10 = (f32[10,8,128]{2,1,0:T(8,128)S(1)}, f32[10,8,128]{2,1,0:T(8,128)S(1)}, u32[]{:S(2)}, u32[]{:S(2)}) collective-permute-start(f32[10,8,128]{2,1,0:T(8,128)S(1)} %get-tuple-element.32), channel_id=1, source_target_pairs={{0,2},{1,3},{2,0},{3,1},{4,6},{5,7},{6,4},{7,5},{8,10},{9,11},{10,... | collective-permute-start | bytes 122888 | tf_op jit(solution)/shard_map/ppermute | solution.py:813
  50.1 3.5 %collective-permute-start.11 = (f32[10,8,128]{2,1,0:T(8,128)S(1)}, f32[10,8,128]{2,1,0:T(8,128)S(1)}, u32[]{:S(2)}, u32[]{:S(2)}) collective-permute-start(f32[10,8,128]{2,1,0:T(8,128)S(1)} %get-tuple-element.33), channel_id=1, source_target_pairs={{0,3},{1,0},{2,1},{3,2},{4,7},{5,4},{6,5},{7,6},{8,11},{9,8},{10,9... | collective-permute-start | bytes 122888 | tf_op jit(solution)/shard_map/ppermute | solution.py:813
  51.5 7.5 %collective-permute-start.12 = (bf16[4,16,16,128]{3,2,1,0:T(8,128)(2,1)S(1)}, bf16[4,16,16,128]{3,2,1,0:T(8,128)(2,1)S(1)}, u32[]{:S(2)}, u32[]{:S(2)}) collective-permute-start(bf16[4,16,16,128]{3,2,1,0:T(8,128)(2,1)S(1)} %collective-permute-done.6.refs_2_), channel_id=1, source_target_pairs={{0,4},{4,0},{8,12},{12,8},{1,5},{5,1},{9,13},{13,9},{2,6},{6,2},{1... | collective-permute-start | bytes 786440 | tf_op jit(solution)/shard_map/ppermute | solution.py:765
  53.6 5.4 %copy-start.2 = (bf16[64,256]{1,0:T(8,128)(2,1)S(1)}, bf16[64,256]{1,0:T(8,128)(2,1)}, u32[]{:S(2)}) copy-start(bf16[64,256]{1,0:T(8,128)(2,1)} %refs_4_.1) | copy-start | bytes 98308
  53.6 5.4 %copy-start.3 = (bf16[64,256]{1,0:T(8,128)(2,1)S(1)}, bf16[64,256]{1,0:T(8,128)(2,1)}, u32[]{:S(2)}) copy-start(bf16[64,256]{1,0:T(8,128)(2,1)} %refs_6_.3) | copy-start | bytes 98308
  53.6 5.4 %copy-start.9 = (bf16[256,128]{1,0:T(8,128)(2,1)S(1)}, bf16[256,128]{1,0:T(8,128)(2,1)}, u32[]{:S(2)}) copy-start(bf16[256,128]{1,0:T(8,128)(2,1)} %get-tuple-element.36.refs_5_) | copy-start | bytes 196612
  59.0 1.3 %copy-start.1 = (bf16[32,16,64]{2,1,0:T(8,128)(2,1)S(1)}, bf16[32,16,64]{2,1,0:T(8,128)(2,1)}, u32[]{:S(2)}) copy-start(bf16[32,16,64]{2,1,0:T(8,128)(2,1)} %refs_1_.1) | copy-start | bytes 196612
  59.0 1.3 %copy-start.4 = (bf16[256,64]{0,1:T(8,128)(2,1)S(1)}, bf16[256,64]{0,1:T(8,128)(2,1)}, u32[]{:S(2)}) copy-start(bf16[256,64]{0,1:T(8,128)(2,1)} %param.20) | copy-start | bytes 98308

commit v12 on v11

--- a/solution.py
+++ b/solution.py
@@ -104,6 +104,7 @@
     wg_ref,
     wf_ref,
     shard_ref,
+    right_ref,
     norm_ref,
     weights_ref,
     turn_ref,
@@ -153,8 +154,7 @@
         res = nt_dot(w2, jnp.concatenate([real[s]] * size, axis=0))
         res = jnp.where(mine, res, 0.0).reshape(fd // size, size, 128)
         place_ref[:, s, :] = jnp.sum(res, axis=1)
-    right = place_ref[...].reshape(fd // size * seqs, 128).astype(bf16)
-    shard_ref[base + 2 * rows :, :] = right
+    right_ref[...] = place_ref[...].reshape(fd // size * seqs, 128).astype(bf16)
 
 
 def join_kernel(
@@ -165,26 +165,34 @@
     shard1_ref,
     shard2_ref,
     shard3_ref,
+    right0_ref,
+    right1_ref,
+    right2_ref,
+    right3_ref,
+    norm0_ref,
+    norm1_ref,
+    norm2_ref,
+    norm3_ref,
+    sides_ref,
+    parts_ref,
     cols0_ref,
     cols1_ref,
-    out_ref,
-    norm_ref,
+    cols2_ref,
+    cols3_ref,
 ):
     nk = 4
     row, col = row_ref[0], col_ref[0]
-    size = out_ref.shape[0] // (2 * nk)
-    half, tokens, _ = norm_ref.shape[1:]
-    count = half * tokens
-    for t in range(nk):
-        ref = (cols0_ref, cols1_ref)[t // 2]
-        at = pl.ds(pl.multiple_of(jnp.bitwise_xor(row, t) * size, size), size)
-        end = ref.shape[0] // 2 * (t % 2 + 1)
-        out_ref[at, :] = ref[end - size : end, :]
+    size = right0_ref.shape[0]
+    for t, ref in enumerate((right0_ref, right1_ref, right2_ref, right3_ref)):
+        at = pl.ds(pl.multiple_of(lax.rem(row + nk - t, nk) * size, size), size)
+        sides_ref[at, :] = ref[...]
     for t, ref in enumerate((shard0_ref, shard1_ref, shard2_ref, shard3_ref)):
-        k = jnp.bitwise_xor(col, t)
-        at = pl.ds(pl.multiple_of((nk + k) * size, size), size)
-        out_ref[at, :] = ref[:size, :]
-        norm_ref[k] = ref[size + count : size + 2 * count, :].reshape(norm_ref.shape[1:])
+        at = pl.ds(pl.multiple_of((nk + jnp.bitwise_xor(col, t)) * size, size), size)
+        sides_ref[at, :] = ref[:size, :]
+    for t, ref in enumerate((norm0_ref, norm1_ref, norm2_ref, norm3_ref)):
+        parts_ref[jnp.bitwise_xor(row, t)] = ref[...]
+    for t, ref in enumerate((cols0_ref, cols1_ref, cols2_ref, cols3_ref)):
+        ref[...] = parts_ref[jnp.bitwise_xor(col, t)]
 
 
 def update_kernel(
@@ -359,7 +367,6 @@
 
 def weights_kernel(
     ready,
-    row_ref,
     col_ref,
     side0_ref,
     side1_ref,
@@ -367,6 +374,8 @@
     side3_ref,
     cols0_ref,
     cols1_ref,
+    cols2_ref,
+    cols3_ref,
     weights_ref,
     gw_ref,
     acc_ref,
@@ -381,17 +390,13 @@
     nk, half, tokens, _ = cols_ref.shape
     tile = nk * tokens
     groups, heads, lanes = gw_ref.shape
-    row, col = row_ref[0], col_ref[0]
+    col = col_ref[0]
     count = half * tokens
-    size = side0_ref.shape[0] - 2 * count - cols0_ref.shape[0] // 2 + count
+    start = side0_ref.shape[0] - 2 * count
     for t, ref in enumerate((side0_ref, side1_ref, side2_ref, side3_ref)):
-        k = jnp.bitwise_xor(col, t)
-        rows_ref[k] = ref[size : size + 2 * count, :].reshape(rows_ref.shape[1:])
-    for t in range(nk):
-        ref = (cols0_ref, cols1_ref)[t // 2]
-        start = ref.shape[0] // 2 * (t % 2)
-        part = ref[start : start + count, :]
-        cols_ref[jnp.bitwise_xor(row, t)] = part.reshape(cols_ref.shape[1:])
+        rows_ref[jnp.bitwise_xor(col, t)] = ref[start:, :].reshape(rows_ref.shape[1:])
+    for t, ref in enumerate((cols0_ref, cols1_ref, cols2_ref, cols3_ref)):
+        cols_ref[jnp.bitwise_xor(col, t)] = ref[...].reshape(cols_ref.shape[1:])
     chans = weights_ref.shape[1] // 3
     by_heads(weights_ref[:, :chans], heads, bv_ref)
     by_heads(weights_ref[:, chans : 2 * chans], heads, bg_ref)
@@ -491,17 +496,21 @@
 
 
 def values_kernel(
-    ready, ev0_ref, ev1_ref, ev2_ref, ev3_ref, wv_ref, norm_ref, wg_ref, v_ref, gate_ref
+    ready, col_ref, ev0_ref, ev1_ref, ev2_ref, ev3_ref, wv_ref, norm_ref, wg_ref, v_ref, gate_ref, ev_ref
 ):
-    evs = (ev0_ref, ev1_ref, ev2_ref, ev3_ref)
-    nk, half, tokens, wide = ev0_ref.shape
+    nk, nr, count, wide = ev_ref.shape
+    half = v_ref.shape[0]
+    tokens = count // half
     chans = wv_ref.shape[1]
+    for t, ref in enumerate((ev0_ref, ev1_ref, ev2_ref, ev3_ref)):
+        ev_ref[jnp.bitwise_xor(col_ref[0], t)] = ref[...]
     gate = jax.nn.sigmoid(nn_dot(norm_ref[...], twice(wg_ref[...])))
     gate_ref[: half * tokens] = gate[:, :chans]
     gate_ref[half * tokens :] = gate[:, chans:]
     wv = twice(wv_ref[...])
     for s in range(half):
-        x = jnp.concatenate([ev[k, s] for ev in evs for k in range(nk)], axis=0)
+        at = slice(s * tokens, (s + 1) * tokens)
+        x = jnp.concatenate([ev_ref[k, r, at, :] for r in range(nr) for k in range(nk)], axis=0)
         v_ref[s] = nn_dot(x, wv).astype(bf16)
 
 
@@ -577,7 +586,6 @@
 
 def alignment_kernel(
     ready,
-    row_ref,
     col_ref,
     own_ref,
     r1_ref,
@@ -602,7 +610,7 @@
     chans = chans // 2
     tokens = pieces * 2
     head_width = chans // heads
-    row, col = row_ref[0], col_ref[0]
+    col = col_ref[0]
 
     low = lax.broadcasted_iota(jnp.int32, (rows, wide), 1) < tile
     lgs = [p[2:].reshape(rows, wide) for p in pays]
@@ -624,8 +632,8 @@
             w_ref[source, :, 2 * n + 1, :] = rolled[n * heads : (n + 1) * heads]
     w = jnp.concatenate(
         [
-            w_ref[jnp.bitwise_xor(row, t)].reshape(heads * tokens, wide)[:, :tile]
-            for t in range(nk)
+            w_ref[k].reshape(heads * tokens, wide)[:, :tile]
+            for k in range(nk)
         ],
         axis=1,
     ).astype(bf16)
@@ -684,10 +692,11 @@
     l_rows = tokens // pack * fc
     r_rows = fd * tokens // 128 * seqs
     n_rows = half * tokens
-    shard, normed, weights = call(
+    shard, right, normed, weights = call(
         prepare_kernel,
         (
-            sds((l_rows + 2 * n_rows + r_rows, 128), bf16),
+            sds((l_rows + 2 * n_rows, 128), bf16),
+            sds((r_rows, 128), bf16),
             sds((n_rows, 128), bf16),
             sds((width, 3 * chans), bf16),
         ),
@@ -712,27 +721,32 @@
     def exchange(x, bit):
         return lax.ppermute(x, "col", [(c, c ^ bit) for c in range(nk)])
 
-    other = exchange(shard, 1)
-    across = exchange(shard, 2)
-    all_rows = [shard, other, across, exchange(across, 1)]
-    pair = jnp.concatenate([x[l_rows + n_rows :] for x in (shard, other)], axis=0)
-    all_cols = [
+    def exchange_rows(x, bit):
+        return lax.ppermute(x, "row", [(r, r ^ bit) for r in range(nr)])
+
+    rights = [
         lax.ppermute(
-            pair,
+            right,
             ("row", "col"),
-            [(r * nk + c, (c ^ flip) * nk + r) for r in range(nr) for c in range(nk)],
+            [(r * nk + c, (c + t) % nr * nk + r) for r in range(nr) for c in range(nk)],
         )
-        for flip in (0, 2)
+        for t in range(nr)
     ]
-
-    sides, block = call(
+    across, beyond = exchange(shard, 2), exchange_rows(normed, 2)
+    across, beyond, *rights = lax.optimization_barrier((across, beyond, *rights))
+    all_rows = [shard, exchange(shard, 1), across, exchange(across, 1)]
+    norms = [normed, exchange_rows(normed, 1), beyond, exchange_rows(beyond, 1)]
+
+    sides, block, *all_cols = call(
         join_kernel,
         (
             sds((nk * (r_rows + l_rows), 128), bf16),
-            sds((nk, half, tokens, 2 * width), bf16),
-        ),
+            sds((nr, n_rows, 2 * width), bf16),
+        )
+        + (sds((n_rows, 2 * width), bf16),) * nk,
         smem=2,
-    )(*place[:2], *all_rows, *all_cols)
+    )(*place[:2], *all_rows, *rights, *norms)
+    all_cols = all_cols[:1] + [exchange(all_cols[t], t) for t in range(1, nk)]
     if nq == 2:
         far_sides = lax.ppermute(sides, "seq", [(0, 1), (1, 0)])
     else:
@@ -752,20 +766,17 @@
             pltpu.VMEM((heads, tile_i, head_lanes), bf16),
             pltpu.VMEM((heads, 2 * tile_j, head_lanes), bf16),
         ),
-        smem=2,
+        smem=1,
         flops=3_000_000_000,
         nbytes=3_000_000,
-    )(*place[:2], *all_rows, *all_cols, weights)
+    )(col_scalar, *all_rows, *all_cols, weights)
     if nq == 2:
         gw_other = lax.ppermute(gw_own, "seq", [(0, 1), (1, 0)])
     else:
         gw_own, gw_other = lax.psum(gw_own, "seq"), jnp.zeros_like(gw_own)
 
-    def exchange_rows(x, bit):
-        return lax.ppermute(x, "row", [(r, r ^ bit) for r in range(nr)])
-
     block, _ = lax.optimization_barrier((block, gw_own))
-    near, beyond = exchange_rows(block, 1), exchange_rows(block, 2)
+    close, remote = exchange(block, 1), exchange(block, 2)
 
     pair_out, normal, inverse, logits = call(
         update_kernel,
@@ -814,8 +825,19 @@
         for shift, pay in ((1, pay1), (2, pay2), (3, pay3))
     ]
 
-    near, beyond, pay0 = lax.optimization_barrier((near, beyond, pay0))
-    every = [block, near, beyond, exchange_rows(beyond, 1)]
+
+    close, remote, pay0 = lax.optimization_barrier((close, remote, pay0))
+    every = [block, close, remote, exchange(remote, 1)]
+    values, gating = call(
+        values_kernel,
+        (sds((half, nr * nk * tokens, 2 * chans), bf16), sds((seqs * tokens, chans), f32)),
+        scratch=(pltpu.VMEM((nk, nr, n_rows, 2 * width), bf16),),
+        smem=1,
+        flops=4_000_000_000,
+        nbytes=6_000_000,
+    )(col_scalar, *every, content_weights_grid, normed, sigmoid_weights_grid)
+
+    got, values, gating = lax.optimization_barrier((got, values, gating))
 
     (gradient,) = call(
         gradient_kernel,
@@ -830,13 +852,6 @@
         nbytes=3_000_000,
     )(pay0, *got, logits, gw, normal, inverse, score_matrix.T)
 
-    values, gating = call(
-        values_kernel,
-        (sds((half, nr * nk * tokens, 2 * chans), bf16), sds((seqs * tokens, chans), f32)),
-        flops=4_000_000_000,
-        nbytes=6_000_000,
-    )(*every, content_weights_grid, normed, sigmoid_weights_grid)
-
     (aligned,) = call(
         alignment_kernel,
         (sds((seqs * tokens, width), bf16),),
@@ -844,11 +859,11 @@
             pltpu.VMEM((nk, heads, tokens, 2 * tile_j), f32),
             pltpu.VMEM((seqs * tokens, chans), bf16),
         ),
-        smem=2,
+        smem=1,
         flops=3_000_000_000,
         nbytes=5_000_000,
     )(
-        *place[:2],
+        col_scalar,
         pay0,
         *got,
         values,

time: 63.1 us -> 65 us (1.030); the launches traced: 62.9 us -> 64.1 us
  starting transfers between devices: 24 us -> 27 us
  waiting for transfers between devices: 11.9 us -> 9.29 us
  local copies, waits for them, and re-layouts: 2.8 us -> 3.6 us
    ppermute x3 -> x9, starting transfers between devices: 2.97 us -> 11.9 us  [exchange(): return lax.ppermute(x, 'col', [(c, c ^ bit) for c in range(nk)])]
    ppermute x3, starting transfers between devices: 11.4 us -> 2.53 us  [exchange_rows(): return lax.ppermute(x, 'row', [(r, r ^ bit) for r in range(nr)])]
    ppermute x2 -> x4, starting transfers between devices: 3.47 us -> 7.43 us  [on_device(): lax.ppermute(right, ('row', 'col'), [(r * nk + c, (c + t) % nr * nk + r)...]
    ppermute x2 -> x4, waiting for transfers between devices: 4.3 us -> 1.82 us  [on_device(): lax.ppermute(right, ('row', 'col'), [(r * nk + c, (c + t) % nr * nk + r)...]
    ppermute x3 -> x9, waiting for transfers between devices: 4.81 us -> 2.5 us  [exchange(): return lax.ppermute(x, 'col', [(c, c ^ bit) for c in range(nk)])]
    ppermute x3, starting transfers between devices: 3.97 us -> 2.13 us  [on_device(): lax.ppermute(pay, 'col', [(c, (c + shift) % nk) for c in range(nk)])]
    unnamed x22 -> x26, local copies, waits for them, and re-layouts: 1.86 us -> 3.6 us
    ppermute x3, waiting for transfers between devices: 2.52 us -> 4.14 us  [exchange_rows(): return lax.ppermute(x, 'row', [(r, r ^ bit) for r in range(nr)])]
  transfers between devices with their start and end apart: 13 -> 21, of which waited for: 4 -> 7; matrix products, arithmetic and copies ran while one was open for 2% -> 0% of each run, Pallas kernels for 26% -> 24%
where the time goes in v12:
time: 65 us; the launch traced here: 64.1 us
  starting transfers between devices  27 us (42%)
  Pallas kernels  23.4 us (36%)
  waiting for transfers between devices  9.29 us (14%)
  local copies, waits for them, and re-layouts  3.6 us (6%)
  between operations  0.81 us (1%)
    pallas_call x8, Pallas kernels, run(): pl.pallas_call(body, out_shape=out_shape, in_specs=in_specs, out_specs=[p...  23.4 us
    ppermute x9, starting transfers between devices, exchange(): return lax.ppermute(x, 'col', [(c, c ^ bit) for c in range(nk)])  11.9 us
    ppermute x4, starting transfers between devices, on_device(): lax.ppermute(right, ('row', 'col'), [(r * nk + c, (c + t) % nr * nk + r)...  7.43 us
    ppermute x3, waiting for transfers between devices, exchange_rows(): return lax.ppermute(x, 'row', [(r, r ^ bit) for r in range(nr)])  4.14 us
    unnamed x26, local copies, waits for them, and re-layouts  3.6 us
    ppermute x3, starting transfers between devices, exchange_rows(): return lax.ppermute(x, 'row', [(r, r ^ bit) for r in range(nr)])  2.53 us
    ppermute x9, waiting for transfers between devices, exchange(): return lax.ppermute(x, 'col', [(c, c ^ bit) for c in range(nk)])  2.5 us
    ppermute x3, starting transfers between devices, on_device(): lax.ppermute(pay, 'col', [(c, (c + shift) % nk) for c in range(nk)])  2.13 us
  transfers between devices with their start and end apart: 21, of which 7 were waited for; matrix products, arithmetic and copies ran while one was open for 0% of the time, Pallas kernels for 24%

profile of v12, /device:TPU:0, one launch (start us, length us, event | category | flops | bytes accessed | tf_op | source)
XLA Modules:
  0.0 64.1 jit_solution(14290746184031446011)
XLA Ops:
  0.6 2.8 %shard_map.130 = (bf16[640,128]{1,0:T(8,128)(2,1)}, bf16[128,128]{1,0:T(8,128)(2,1)}, bf16[256,128]{1,0:T(8,128)(2,1)}, bf16[64,768]{1,0:T(8,128)(2,1)}) custom-call(s32[1]{0:T(128)} %bitcast.2.refs_0_, bf16[32,16,64]{2,1,0:T(8,128)(2,1)} %refs_1_.1, bf16[32,16,64]{2,1,0:T(8,128)(2,1)} %refs_2_.1, bf16[32,64]{1,0:T(8,128)(2,1)} %bitcast.23, ...), custom_call_target="tpu_custom_call" | custom-call | tf_op jit(solution)/shard_map/pallas_call | solution.py:62
  3.5 3.0 %collective-permute-start.1 = (bf16[640,128]{1,0:T(8,128)(2,1)}, bf16[640,128]{1,0:T(8,128)(2,1)S(1)}, u32[]{:S(2)}, u32[]{:S(2)}) collective-permute-start(bf16[640,128]{1,0:T(8,128)(2,1)} %get-tuple-element.39.refs_2_.refs_1_), channel_id=1, source_target_pairs={{0,2},{1,3},{2,0},{3,1},{4,6},{5,7},{6,4},{7,5},{8,10},{9,11},{10,... | collective-permute-start | bytes 491528 | tf_op jit(solution)/shard_map/ppermute | solution.py:722
  6.4 3.6 %collective-permute-start.6 = (bf16[128,128]{1,0:T(8,128)(2,1)}, bf16[128,128]{1,0:T(8,128)(2,1)S(1)}, u32[]{:S(2)}, u32[]{:S(2)}) collective-permute-start(bf16[128,128]{1,0:T(8,128)(2,1)} %get-tuple-element.41), channel_id=1, source_target_pairs={{0,12},{1,0},{2,4},{3,8},{4,13},{5,1},{6,5},{7,9},{8,14},{9,2},{10... | collective-permute-start | bytes 98312 | tf_op jit(solution)/shard_map/ppermute | solution.py:728
  10.0 0.5 collective-permute-start.2
  10.6 2.4 %collective-permute-start.5 = (bf16[128,128]{1,0:T(8,128)(2,1)}, bf16[128,128]{1,0:T(8,128)(2,1)S(1)}, u32[]{:S(2)}, u32[]{:S(2)}) collective-permute-start(bf16[128,128]{1,0:T(8,128)(2,1)} %get-tuple-element.41), channel_id=1, source_target_pairs={{0,8},{1,12},{2,0},{3,4},{4,9},{5,13},{6,1},{7,5},{8,10},{9,14},{1... | collective-permute-start | bytes 98312 | tf_op jit(solution)/shard_map/ppermute | solution.py:728
  13.0 0.0 collective-permute-start.4
  13.0 0.0 collective-permute-done.6.refs_9_
  13.0 1.4 %collective-permute-start.3 = (bf16[128,128]{1,0:T(8,128)(2,1)}, bf16[128,128]{1,0:T(8,128)(2,1)S(1)}, u32[]{:S(2)}, u32[]{:S(2)}) collective-permute-start(bf16[128,128]{1,0:T(8,128)(2,1)} %get-tuple-element.41), channel_id=1, source_target_pairs={{0,0},{1,4},{2,8},{3,12},{4,1},{5,5},{6,9},{7,13},{8,2},{9,6},{10,... | collective-permute-start | bytes 98312 | tf_op jit(solution)/shard_map/ppermute | solution.py:728
  14.4 0.5 collective-permute-done.5.refs_8_
  14.9 0.4 collective-permute-start
  15.3 1.3 %collective-permute-done.4.refs_7_ = bf16[128,128]{1,0:T(8,128)(2,1)S(1)} collective-permute-done((bf16[128,128]{1,0:T(8,128)(2,1)}, bf16[128,128]{1,0:T(8,128)(2,1)S(1)}, u32[]{:S(2)}, u32[]{:S(2)}) %collective-permute-start.4) | collective-permute-done | bytes 32800 | tf_op jit(solution)/shard_map/ppermute | solution.py:728
  16.6 0.0 collective-permute-done.3.refs_6_
  16.6 0.0 collective-permute-done.2.refs_12_
  16.6 0.0 collective-permute-done.1.refs_4_.refs_3_
  16.6 2.0 %collective-permute-start.7 = (bf16[640,128]{1,0:T(8,128)(2,1)S(1)}, bf16[640,128]{1,0:T(8,128)(2,1)S(1)}, u32[]{:S(2)}, u32[]{:S(2)}) collective-permute-start(bf16[640,128]{1,0:T(8,128)(2,1)S(1)} %collective-permute-done.1.refs_4_.refs_3_), channel_id=1, source_target_pairs={{0,1},{1,0},{2,3},{3,2},{4,5},{5,4},{6,7},{7,6},{8,9},{9,8},{10,11... | collective-permute-start | bytes 491528 | tf_op jit(solution)/shard_map/ppermute | solution.py:722
  18.6 0.1 collective-permute-start.8
  18.7 1.9 %collective-permute-start.9 = (bf16[256,128]{1,0:T(8,128)(2,1)S(1)}, bf16[256,128]{1,0:T(8,128)(2,1)S(1)}, u32[]{:S(2)}, u32[]{:S(2)}) collective-permute-start(bf16[256,128]{1,0:T(8,128)(2,1)S(1)} %collective-permute-done.2.refs_12_), channel_id=1, source_target_pairs={{0,4},{4,0},{8,12},{12,8},{1,5},{5,1},{9,13},{13,9},{2,6},{6,2},{1... | collective-permute-start | bytes 196616 | tf_op jit(solution)/shard_map/ppermute | solution.py:725
  20.6 3.1 %collective-permute-done.8.refs_11_ = bf16[256,128]{1,0:T(8,128)(2,1)S(1)} collective-permute-done((bf16[256,128]{1,0:T(8,128)(2,1)}, bf16[256,128]{1,0:T(8,128)(2,1)S(1)}, u32[]{:S(2)}, u32[]{:S(2)}) %collective-permute-start.8) | collective-permute-done | bytes 65568 | tf_op jit(solution)/shard_map/ppermute | solution.py:725
  23.7 0.0 collective-permute-done.refs_3_.refs_2_
  23.7 1.0 %collective-permute-done.9.refs_13_ = bf16[256,128]{1,0:T(8,128)(2,1)S(1)} collective-permute-done((bf16[256,128]{1,0:T(8,128)(2,1)S(1)}, bf16[256,128]{1,0:T(8,128)(2,1)S(1)}, u32[]{:S(2)}, u32[]{:S(2)}) %collective-permute-start.9) | collective-permute-done | bytes 65568 | tf_op jit(solution)/shard_map/ppermute | solution.py:725
  24.7 0.0 collective-permute-done.7.refs_5_.refs_4_
  24.7 0.9 %copy-done = bf16[640,128]{1,0:T(8,128)(2,1)S(1)} copy-done((bf16[640,128]{1,0:T(8,128)(2,1)S(1)}, bf16[640,128]{1,0:T(8,128)(2,1)}, u32[]{:S(2)}) %copy-start) | copy-done | bytes 163864
  25.7 0.8 %copy-done.3 = bf16[256,128]{1,0:T(8,128)(2,1)S(1)} copy-done((bf16[256,128]{1,0:T(8,128)(2,1)S(1)}, bf16[256,128]{1,0:T(8,128)(2,1)}, u32[]{:S(2)}) %copy-start.3) | copy-done | bytes 65560
  26.5 0.1 shard_map.131
  26.6 0.1 collective-permute-start.10
  26.6 4.5 %collective-permute-start.11 = (bf16[256,128]{1,0:T(8,128)(2,1)S(1)}, bf16[256,128]{1,0:T(8,128)(2,1)S(1)}, u32[]{:S(2)}, u32[]{:S(2)}) collective-permute-start(bf16[256,128]{1,0:T(8,128)(2,1)S(1)} %get-tuple-element.51), channel_id=1, source_target_pairs={{0,2},{1,3},{2,0},{3,1},{4,6},{5,7},{6,4},{7,5},{8,10},{9,11},{10,... | collective-permute-start | bytes 196616 | tf_op jit(solution)/shard_map/ppermute | solution.py:722
  31.2 0.1 collective-permute-start.12
  31.2 1.5 %collective-permute-start.15 = (bf16[1024,128]{1,0:T(8,128)(2,1)S(1)}, bf16[1024,128]{1,0:T(8,128)(2,1)S(1)}, u32[]{:S(2)}, u32[]{:S(2)}) collective-permute-start(bf16[1024,128]{1,0:T(8,128)(2,1)S(1)} %get-tuple-element.55.refs_2_), channel_id=1, source_target_pairs={{0,16},{16,0},{1,17},{17,1},{2,18},{18,2},{3,19},{19,3},{4,20},{20... | collective-permute-start | bytes 786440 | tf_op jit(solution)/shard_map/ppermute | solution.py:751
  32.7 0.0 collective-permute-done.10.refs_6_
  32.7 1.1 %collective-permute-done.11.refs_7_ = bf16[256,128]{1,0:T(8,128)(2,1)S(1)} collective-permute-done((bf16[256,128]{1,0:T(8,128)(2,1)S(1)}, bf16[256,128]{1,0:T(8,128)(2,1)S(1)}, u32[]{:S(2)}, u32[]{:S(2)}) %collective-permute-start.11) | collective-permute-done | bytes 65568 | tf_op jit(solution)/shard_map/ppermute | solution.py:722
  33.8 1.4 %collective-permute-done.12.refs_8_ = bf16[256,128]{1,0:T(8,128)(2,1)S(1)} collective-permute-done((bf16[256,128]{1,0:T(8,128)(2,1)S(1)}, bf16[256,128]{1,0:T(8,128)(2,1)S(1)}, u32[]{:S(2)}, u32[]{:S(2)}) %collective-permute-start.12) | collective-permute-done | bytes 65568 | tf_op jit(solution)/shard_map/ppermute | solution.py:722
  35.2 0.9 %copy-done.1 = bf16[640,128]{1,0:T(8,128)(2,1)S(1)} copy-done((bf16[640,128]{1,0:T(8,128)(2,1)S(1)}, bf16[640,128]{1,0:T(8,128)(2,1)}, u32[]{:S(2)}) %copy-start.1) | copy-done | bytes 163864
  36.1 0.9 %copy-done.11 = bf16[64,768]{1,0:T(8,128)(2,1)S(1)} copy-done((bf16[64,768]{1,0:T(8,128)(2,1)S(1)}, bf16[64,768]{1,0:T(8,128)(2,1)}, u32[]{:S(2)}) %copy-start.11) | copy-done | bytes 98328
  37.0 2.3 %shard_map.132.refs_2_ = f32[16,8,256]{2,1,0:T(8,128)S(1)} custom-call(s32[1]{0:T(128)} %bitcast.refs_1_.refs_0_, bf16[640,128]{1,0:T(8,128)(2,1)S(1)} %copy-done.1, bf16[640,128]{1,0:T(8,128)(2,1)S(1)} %collective-permute-done.refs_3_.refs_2_, bf16[640,128]{1,0:T(8,128)(2,1)S(1)} %collective-permute-done.1.refs_4_.refs_3_, ...), custom_call_target="tpu_custom_call" | custom-call | flops 3000000000 | bytes 3000000 | tf_op jit(solution)/shard_map/pallas_call | solution.py:62
  39.3 1.6 %collective-permute-start.16 = (f32[16,8,256]{2,1,0:T(8,128)S(1)}, f32[16,8,256]{2,1,0:T(8,128)S(1)}, u32[]{:S(2)}, u32[]{:S(2)}) collective-permute-start(f32[16,8,256]{2,1,0:T(8,128)S(1)} %shard_map.132.refs_2_), channel_id=1, source_target_pairs={{0,16},{16,0},{1,17},{17,1},{2,18},{18,2},{3,19},{19,3},{4,20},{20... | collective-permute-start | bytes 393224 | tf_op jit(solution)/shard_map/ppermute | solution.py:774
  40.9 1.4 %collective-permute-start.14 = (bf16[4,256,128]{2,1,0:T(8,128)(2,1)S(1)}, bf16[4,256,128]{2,1,0:T(8,128)(2,1)S(1)}, u32[]{:S(2)}, u32[]{:S(2)}) collective-permute-start(bf16[4,256,128]{2,1,0:T(8,128)(2,1)S(1)} %get-tuple-element.54.refs_1_), channel_id=1, source_target_pairs={{0,2},{1,3},{2,0},{3,1},{4,6},{5,7},{6,4},{7,5},{8,10},{9,11},{10,... | collective-permute-start | bytes 786440 | tf_op jit(solution)/shard_map/ppermute | solution.py:722
  42.2 0.0 collective-permute-start.13
  42.2 0.0 collective-permute-done.15.refs_3_
  42.2 0.0 copy-done.8
  42.2 0.0 copy-done.9
  42.2 0.0 copy-done.10
  42.2 0.0 copy-done.12
  42.3 0.0 copy-start.4
  42.3 0.0 copy-start.5
  42.3 0.0 copy-start.6
  42.3 11.0 %shard_map.133 = (bf16[4096,128]{1,0:T(8,128)(2,1)}, f32[16,128,256]{2,1,0:T(8,128)S(1)}, f32[16,8,256]{2,1,0:T(8,128)S(1)}, f32[16,8,256]{2,1,0:T(8,128)S(1)}) custom-call(s32[1]{0:T(128)} %bitcast.refs_1_.refs_0_, s32[1]{0:T(128)} %bitcast.7.refs_1_, bf16[1024,128]{1,0:T(8,128)(2,1)S(1)} %get-tuple-element.55.refs_2_, ...), custom_call_target="tpu_custom_call" | custom-call | flops 14000000000 | bytes 5000000 | tf_op jit(solution)/shard_map/pallas_call | solution.py:62
  53.3 0.0 collective-permute-done.16.refs_3_
  53.4 0.5 shard_map.134
  53.8 0.0 collective-permute-done.14.refs_3_
  53.8 0.0 collective-permute-done.13.refs_2_
  53.8 0.6 collective-permute-start.20
  54.4 0.1 collective-permute-start.17
  54.5 0.7 %collective-permute-start.18 = (f32[10,8,128]{2,1,0:T(8,128)S(1)}, f32[10,8,128]{2,1,0:T(8,128)S(1)}, u32[]{:S(2)}, u32[]{:S(2)}) collective-permute-start(f32[10,8,128]{2,1,0:T(8,128)S(1)} %get-tuple-element.60), channel_id=1, source_target_pairs={{0,2},{1,3},{2,0},{3,1},{4,6},{5,7},{6,4},{7,5},{8,10},{9,11},{10,... | collective-permute-start | bytes 122888 | tf_op jit(solution)/shard_map/ppermute | solution.py:824
  55.1 1.4 %collective-permute-start.19 = (f32[10,8,128]{2,1,0:T(8,128)S(1)}, f32[10,8,128]{2,1,0:T(8,128)S(1)}, u32[]{:S(2)}, u32[]{:S(2)}) collective-permute-start(f32[10,8,128]{2,1,0:T(8,128)S(1)} %get-tuple-element.61), channel_id=1, source_target_pairs={{0,3},{1,0},{2,1},{3,2},{4,7},{5,4},{6,5},{7,6},{8,11},{9,8},{10,9... | collective-permute-start | bytes 122888 | tf_op jit(solution)/shard_map/ppermute | solution.py:824
  56.5 0.0 collective-permute-done.20.refs_4_
  56.5 0.0 copy-done.5
  56.5 1.3 %shard_map.135 = (bf16[16,256,512]{2,1,0:T(8,128)(2,1)S(1)}, f32[512,256]{1,0:T(8,128)S(1)}) custom-call(s32[1]{0:T(128)} %bitcast.refs_1_.refs_0_, bf16[4,256,128]{2,1,0:T(8,128)(2,1)S(1)} %get-tuple-element.54.refs_1_, bf16[4,256,128]{2,1,0:T(8,128)(2,1)S(1)} %collective-permute-done.13.refs_2_, bf16[4,256,128]{2,1,0:T(8,128)(2,1)S(1)} %collective-permute-done.14.refs_3_, ...), custom_call_target="tpu_custom_call" | custom-call | flops 4000000000 | bytes 6000000 | tf_op jit(solution)/shard_map/pallas_call | solution.py:62
  57.9 0.0 collective-permute-done.17.refs_2_.refs_1_
  57.9 0.8 %collective-permute-done.18.refs_3_.refs_2_ = f32[10,8,128]{2,1,0:T(8,128)S(1)} collective-permute-done((f32[10,8,128]{2,1,0:T(8,128)S(1)}, f32[10,8,128]{2,1,0:T(8,128)S(1)}, u32[]{:S(2)}, u32[]{:S(2)}) %collective-permute-start.18) | collective-permute-done | bytes 40992 | tf_op jit(solution)/shard_map/ppermute | solution.py:824
  58.7 0.0 collective-permute-done.19.refs_4_.refs_3_
  58.7 2.8 %shard_map.137 = bf16[4096,128]{1,0:T(8,128)(2,1)} custom-call(f32[10,8,128]{2,1,0:T(8,128)S(1)} %get-tuple-element.58.refs_1_.refs_0_, f32[10,8,128]{2,1,0:T(8,128)S(1)} %collective-permute-done.17.refs_2_.refs_1_, f32[10,8,128]{2,1,0:T(8,128)S(1)} %collective-permute-done.18.refs_3_.refs_2_, f32[10,8,128]{2,1,0:T(8,128)S(1)} %collective-permute-done.19.refs_4_.refs_3_, ...), custom_call_target="tpu_custom_call" | custom-call | flops 4000000000 | bytes 3000000 | tf_op jit(solution)/shard_map/pallas_call | solution.py:62
  61.5 0.0 copy-done.2
  61.5 0.0 copy-done.7
  61.5 2.6 %shard_map.136 = bf16[512,64]{1,0:T(8,128)(2,1)} custom-call(s32[1]{0:T(128)} %bitcast.refs_1_.refs_0_, f32[10,8,128]{2,1,0:T(8,128)S(1)} %get-tuple-element.58.refs_1_.refs_0_, f32[10,8,128]{2,1,0:T(8,128)S(1)} %collective-permute-done.17.refs_2_.refs_1_, f32[10,8,128]{2,1,0:T(8,128)S(1)} %collective-permute-done.18.refs_3_.refs_2_, ...), custom_call_target="tpu_custom_call" | custom-call | flops 3000000000 | bytes 5000000 | tf_op jit(solution)/shard_map/pallas_call | solution.py:62
  (12 shorter events, 0.0 us)
Async XLA Ops:
  3.5 13.1 %collective-permute-start.1 = (bf16[640,128]{1,0:T(8,128)(2,1)}, bf16[640,128]{1,0:T(8,128)(2,1)S(1)}, u32[]{:S(2)}, u32[]{:S(2)}) collective-permute-start(bf16[640,128]{1,0:T(8,128)(2,1)} %get-tuple-element.39.refs_2_.refs_1_), channel_id=1, source_target_pairs={{0,2},{1,3},{2,0},{3,1},{4,6},{5,7},{6,4},{7,5},{8,10},{9,11},{10,... | collective-permute-start | bytes 491528 | tf_op jit(solution)/shard_map/ppermute | solution.py:722
  6.4 6.5 %collective-permute-start.6 = (bf16[128,128]{1,0:T(8,128)(2,1)}, bf16[128,128]{1,0:T(8,128)(2,1)S(1)}, u32[]{:S(2)}, u32[]{:S(2)}) collective-permute-start(bf16[128,128]{1,0:T(8,128)(2,1)} %get-tuple-element.41), channel_id=1, source_target_pairs={{0,12},{1,0},{2,4},{3,8},{4,13},{5,1},{6,5},{7,9},{8,14},{9,2},{10... | collective-permute-start | bytes 98312 | tf_op jit(solution)/shard_map/ppermute | solution.py:728
  10.0 6.5 %collective-permute-start.2 = (bf16[256,128]{1,0:T(8,128)(2,1)}, bf16[256,128]{1,0:T(8,128)(2,1)S(1)}, u32[]{:S(2)}, u32[]{:S(2)}) collective-permute-start(bf16[256,128]{1,0:T(8,128)(2,1)} %get-tuple-element.40.refs_10_.refs_6_), channel_id=1, source_target_pairs={{0,8},{4,12},{8,0},{12,4},{1,9},{5,13},{9,1},{13,5},{2,10},{6,14},... | collective-permute-start | bytes 196616 | tf_op jit(solution)/shard_map/ppermute | solution.py:725
  10.6 4.3 %collective-permute-start.5 = (bf16[128,128]{1,0:T(8,128)(2,1)}, bf16[128,128]{1,0:T(8,128)(2,1)S(1)}, u32[]{:S(2)}, u32[]{:S(2)}) collective-permute-start(bf16[128,128]{1,0:T(8,128)(2,1)} %get-tuple-element.41), channel_id=1, source_target_pairs={{0,8},{1,12},{2,0},{3,4},{4,9},{5,13},{6,1},{7,5},{8,10},{9,14},{1... | collective-permute-start | bytes 98312 | tf_op jit(solution)/shard_map/ppermute | solution.py:728
  13.0 3.6 %collective-permute-start.4 = (bf16[128,128]{1,0:T(8,128)(2,1)}, bf16[128,128]{1,0:T(8,128)(2,1)S(1)}, u32[]{:S(2)}, u32[]{:S(2)}) collective-permute-start(bf16[128,128]{1,0:T(8,128)(2,1)} %get-tuple-element.41), channel_id=1, source_target_pairs={{0,4},{1,8},{2,12},{3,0},{4,5},{5,9},{6,13},{7,1},{8,6},{9,10},{10... | collective-permute-start | bytes 98312 | tf_op jit(solution)/shard_map/ppermute | solution.py:728
  13.0 3.6 %collective-permute-start.3 = (bf16[128,128]{1,0:T(8,128)(2,1)}, bf16[128,128]{1,0:T(8,128)(2,1)S(1)}, u32[]{:S(2)}, u32[]{:S(2)}) collective-permute-start(bf16[128,128]{1,0:T(8,128)(2,1)} %get-tuple-element.41), channel_id=1, source_target_pairs={{0,0},{1,4},{2,8},{3,12},{4,1},{5,5},{6,9},{7,13},{8,2},{9,6},{10,... | collective-permute-start | bytes 98312 | tf_op jit(solution)/shard_map/ppermute | solution.py:728
  14.9 8.8 %collective-permute-start = (bf16[640,128]{1,0:T(8,128)(2,1)}, bf16[640,128]{1,0:T(8,128)(2,1)S(1)}, u32[]{:S(2)}, u32[]{:S(2)}) collective-permute-start(bf16[640,128]{1,0:T(8,128)(2,1)} %get-tuple-element.39.refs_2_.refs_1_), channel_id=1, source_target_pairs={{0,1},{1,0},{2,3},{3,2},{4,5},{5,4},{6,7},{7,6},{8,9},{9,8},{10,11... | collective-permute-start | bytes 491528 | tf_op jit(solution)/shard_map/ppermute | solution.py:722
  16.6 8.2 %collective-permute-start.7 = (bf16[640,128]{1,0:T(8,128)(2,1)S(1)}, bf16[640,128]{1,0:T(8,128)(2,1)S(1)}, u32[]{:S(2)}, u32[]{:S(2)}) collective-permute-start(bf16[640,128]{1,0:T(8,128)(2,1)S(1)} %collective-permute-done.1.refs_4_.refs_3_), channel_id=1, source_target_pairs={{0,1},{1,0},{2,3},{3,2},{4,5},{5,4},{6,7},{7,6},{8,9},{9,8},{10,11... | collective-permute-start | bytes 491528 | tf_op jit(solution)/shard_map/ppermute | solution.py:722
  18.6 5.2 %collective-permute-start.8 = (bf16[256,128]{1,0:T(8,128)(2,1)}, bf16[256,128]{1,0:T(8,128)(2,1)S(1)}, u32[]{:S(2)}, u32[]{:S(2)}) collective-permute-start(bf16[256,128]{1,0:T(8,128)(2,1)} %get-tuple-element.40.refs_10_.refs_6_), channel_id=1, source_target_pairs={{0,4},{4,0},{8,12},{12,8},{1,5},{5,1},{9,13},{13,9},{2,6},{6,2},{1... | collective-permute-start | bytes 196616 | tf_op jit(solution)/shard_map/ppermute | solution.py:725
  18.7 6.1 %collective-permute-start.9 = (bf16[256,128]{1,0:T(8,128)(2,1)S(1)}, bf16[256,128]{1,0:T(8,128)(2,1)S(1)}, u32[]{:S(2)}, u32[]{:S(2)}) collective-permute-start(bf16[256,128]{1,0:T(8,128)(2,1)S(1)} %collective-permute-done.2.refs_12_), channel_id=1, source_target_pairs={{0,4},{4,0},{8,12},{12,8},{1,5},{5,1},{9,13},{13,9},{2,6},{6,2},{1... | collective-permute-start | bytes 196616 | tf_op jit(solution)/shard_map/ppermute | solution.py:725
  24.7 0.9 %copy-start = (bf16[640,128]{1,0:T(8,128)(2,1)S(1)}, bf16[640,128]{1,0:T(8,128)(2,1)}, u32[]{:S(2)}) copy-start(bf16[640,128]{1,0:T(8,128)(2,1)} %get-tuple-element.39.refs_2_.refs_1_) | copy-start | bytes 491524
  25.7 0.8 %copy-start.3 = (bf16[256,128]{1,0:T(8,128)(2,1)S(1)}, bf16[256,128]{1,0:T(8,128)(2,1)}, u32[]{:S(2)}) copy-start(bf16[256,128]{1,0:T(8,128)(2,1)} %get-tuple-element.40.refs_10_.refs_6_) | copy-start | bytes 196612
  26.6 6.2 %collective-permute-start.10 = (bf16[256,128]{1,0:T(8,128)(2,1)S(1)}, bf16[256,128]{1,0:T(8,128)(2,1)S(1)}, u32[]{:S(2)}, u32[]{:S(2)}) collective-permute-start(bf16[256,128]{1,0:T(8,128)(2,1)S(1)} %get-tuple-element.50), channel_id=1, source_target_pairs={{0,1},{1,0},{2,3},{3,2},{4,5},{5,4},{6,7},{7,6},{8,9},{9,8},{10,11... | collective-permute-start | bytes 196616 | tf_op jit(solution)/shard_map/ppermute | solution.py:722
  26.6 7.2 %collective-permute-start.11 = (bf16[256,128]{1,0:T(8,128)(2,1)S(1)}, bf16[256,128]{1,0:T(8,128)(2,1)S(1)}, u32[]{:S(2)}, u32[]{:S(2)}) collective-permute-start(bf16[256,128]{1,0:T(8,128)(2,1)S(1)} %get-tuple-element.51), channel_id=1, source_target_pairs={{0,2},{1,3},{2,0},{3,1},{4,6},{5,7},{6,4},{7,5},{8,10},{9,11},{10,... | collective-permute-start | bytes 196616 | tf_op jit(solution)/shard_map/ppermute | solution.py:722
  31.2 4.0 %collective-permute-start.12 = (bf16[256,128]{1,0:T(8,128)(2,1)S(1)}, bf16[256,128]{1,0:T(8,128)(2,1)S(1)}, u32[]{:S(2)}, u32[]{:S(2)}) collective-permute-start(bf16[256,128]{1,0:T(8,128)(2,1)S(1)} %get-tuple-element.52), channel_id=1, source_target_pairs={{0,3},{1,2},{2,1},{3,0},{4,7},{5,6},{6,5},{7,4},{8,11},{9,10},{10,... | collective-permute-start | bytes 196616 | tf_op jit(solution)/shard_map/ppermute | solution.py:722
  31.2 11.0 %collective-permute-start.15 = (bf16[1024,128]{1,0:T(8,128)(2,1)S(1)}, bf16[1024,128]{1,0:T(8,128)(2,1)S(1)}, u32[]{:S(2)}, u32[]{:S(2)}) collective-permute-start(bf16[1024,128]{1,0:T(8,128)(2,1)S(1)} %get-tuple-element.55.refs_2_), channel_id=1, source_target_pairs={{0,16},{16,0},{1,17},{17,1},{2,18},{18,2},{3,19},{19,3},{4,20},{20... | collective-permute-start | bytes 786440 | tf_op jit(solution)/shard_map/ppermute | solution.py:751
  35.2 0.9 %copy-start.1 = (bf16[640,128]{1,0:T(8,128)(2,1)S(1)}, bf16[640,128]{1,0:T(8,128)(2,1)}, u32[]{:S(2)}) copy-start(bf16[640,128]{1,0:T(8,128)(2,1)} %get-tuple-element.39.refs_2_.refs_1_) | copy-start | bytes 491524
  36.1 0.9 %copy-start.11 = (bf16[64,768]{1,0:T(8,128)(2,1)S(1)}, bf16[64,768]{1,0:T(8,128)(2,1)}, u32[]{:S(2)}) copy-start(bf16[64,768]{1,0:T(8,128)(2,1)} %get-tuple-element.53.refs_9_) | copy-start | bytes 294916
  37.0 5.2 %copy-start.8 = (s32[256]{0:T(256)S(1)}, s32[256]{0:T(256)}, u32[]{:S(2)}) copy-start(s32[256]{0:T(256)} %param.13) | copy-start | bytes 3076
  37.0 5.2 %copy-start.9 = (bf16[64,64,128]{2,1,0:T(8,128)(2,1)S(1)}, bf16[64,64,128]{2,1,0:T(8,128)(2,1)}, u32[]{:S(2)}) copy-start(bf16[64,64,128]{2,1,0:T(8,128)(2,1)} %param.12) | copy-start | bytes 3145732
  37.0 5.2 %copy-start.10 = (f32[1024,128]{1,0:T(8,128)S(1)}, f32[1024,128]{1,0:T(8,128)}, u32[]{:S(2)}) copy-start(f32[1024,128]{1,0:T(8,128)} %refs_5_.2) | copy-start | bytes 1572868
  37.0 5.2 %copy-start.12 = (f32[128,8]{0,1:T(8,128)S(1)}, f32[128,8]{0,1:T(8,128)}, u32[]{:S(2)}) copy-start(f32[128,8]{0,1:T(8,128)} %param.19) | copy-start | bytes 12292
  39.3 14.0 %collective-permute-start.16 = (f32[16,8,256]{2,1,0:T(8,128)S(1)}, f32[16,8,256]{2,1,0:T(8,128)S(1)}, u32[]{:S(2)}, u32[]{:S(2)}) collective-permute-start(f32[16,8,256]{2,1,0:T(8,128)S(1)} %shard_map.132.refs_2_), channel_id=1, source_target_pairs={{0,16},{16,0},{1,17},{17,1},{2,18},{18,2},{3,19},{19,3},{4,20},{20... | collective-permute-start | bytes 393224 | tf_op jit(solution)/shard_map/ppermute | solution.py:774
  40.9 13.0 %collective-permute-start.14 = (bf16[4,256,128]{2,1,0:T(8,128)(2,1)S(1)}, bf16[4,256,128]{2,1,0:T(8,128)(2,1)S(1)}, u32[]{:S(2)}, u32[]{:S(2)}) collective-permute-start(bf16[4,256,128]{2,1,0:T(8,128)(2,1)S(1)} %get-tuple-element.54.refs_1_), channel_id=1, source_target_pairs={{0,2},{1,3},{2,0},{3,1},{4,6},{5,7},{6,4},{7,5},{8,10},{9,11},{10,... | collective-permute-start | bytes 786440 | tf_op jit(solution)/shard_map/ppermute | solution.py:722
  42.2 11.6 %collective-permute-start.13 = (bf16[4,256,128]{2,1,0:T(8,128)(2,1)S(1)}, bf16[4,256,128]{2,1,0:T(8,128)(2,1)S(1)}, u32[]{:S(2)}, u32[]{:S(2)}) collective-permute-start(bf16[4,256,128]{2,1,0:T(8,128)(2,1)S(1)} %get-tuple-element.54.refs_1_), channel_id=1, source_target_pairs={{0,1},{1,0},{2,3},{3,2},{4,5},{5,4},{6,7},{7,6},{8,9},{9,8},{10,11... | collective-permute-start | bytes 786440 | tf_op jit(solution)/shard_map/ppermute | solution.py:722
  42.3 14.3 %copy-start.4 = (bf16[256,128]{1,0:T(8,128)(2,1)S(1)}, bf16[256,128]{1,0:T(8,128)(2,1)}, u32[]{:S(2)}) copy-start(bf16[256,128]{1,0:T(8,128)(2,1)} %get-tuple-element.40.refs_10_.refs_6_) | copy-start | bytes 196612
  42.3 14.3 %copy-start.5 = (bf16[64,256]{1,0:T(8,128)(2,1)S(1)}, bf16[64,256]{1,0:T(8,128)(2,1)}, u32[]{:S(2)}) copy-start(bf16[64,256]{1,0:T(8,128)(2,1)} %refs_5_.3) | copy-start | bytes 98308
  42.3 14.3 %copy-start.6 = (bf16[64,256]{1,0:T(8,128)(2,1)S(1)}, bf16[64,256]{1,0:T(8,128)(2,1)}, u32[]{:S(2)}) copy-start(bf16[64,256]{1,0:T(8,128)(2,1)} %refs_7_.3) | copy-start | bytes 98308
  53.8 2.7 %collective-permute-start.20 = (bf16[4,256,128]{2,1,0:T(8,128)(2,1)S(1)}, bf16[4,256,128]{2,1,0:T(8,128)(2,1)S(1)}, u32[]{:S(2)}, u32[]{:S(2)}) collective-permute-start(bf16[4,256,128]{2,1,0:T(8,128)(2,1)S(1)} %collective-permute-done.14.refs_3_), channel_id=1, source_target_pairs={{0,1},{1,0},{2,3},{3,2},{4,5},{5,4},{6,7},{7,6},{8,9},{9,8},{10,11... | collective-permute-start | bytes 786440 | tf_op jit(solution)/shard_map/ppermute | solution.py:722
  54.4 3.5 %collective-permute-start.17 = (f32[10,8,128]{2,1,0:T(8,128)S(1)}, f32[10,8,128]{2,1,0:T(8,128)S(1)}, u32[]{:S(2)}, u32[]{:S(2)}) collective-permute-start(f32[10,8,128]{2,1,0:T(8,128)S(1)} %get-tuple-element.59), channel_id=1, source_target_pairs={{0,1},{1,2},{2,3},{3,0},{4,5},{5,6},{6,7},{7,4},{8,9},{9,10},{10,1... | collective-permute-start | bytes 122888 | tf_op jit(solution)/shard_map/ppermute | solution.py:824
  54.5 4.2 %collective-permute-start.18 = (f32[10,8,128]{2,1,0:T(8,128)S(1)}, f32[10,8,128]{2,1,0:T(8,128)S(1)}, u32[]{:S(2)}, u32[]{:S(2)}) collective-permute-start(f32[10,8,128]{2,1,0:T(8,128)S(1)} %get-tuple-element.60), channel_id=1, source_target_pairs={{0,2},{1,3},{2,0},{3,1},{4,6},{5,7},{6,4},{7,5},{8,10},{9,11},{10,... | collective-permute-start | bytes 122888 | tf_op jit(solution)/shard_map/ppermute | solution.py:824
  55.1 3.6 %collective-permute-start.19 = (f32[10,8,128]{2,1,0:T(8,128)S(1)}, f32[10,8,128]{2,1,0:T(8,128)S(1)}, u32[]{:S(2)}, u32[]{:S(2)}) collective-permute-start(f32[10,8,128]{2,1,0:T(8,128)S(1)} %get-tuple-element.61), channel_id=1, source_target_pairs={{0,3},{1,0},{2,1},{3,2},{4,7},{5,4},{6,5},{7,6},{8,11},{9,8},{10,9... | collective-permute-start | bytes 122888 | tf_op jit(solution)/shard_map/ppermute | solution.py:824
  58.7 2.8 %copy-start.2 = (bf16[32,16,64]{2,1,0:T(8,128)(2,1)S(1)}, bf16[32,16,64]{2,1,0:T(8,128)(2,1)}, u32[]{:S(2)}) copy-start(bf16[32,16,64]{2,1,0:T(8,128)(2,1)} %refs_1_.1) | copy-start | bytes 196612
  58.7 2.8 %copy-start.7 = (bf16[256,64]{0,1:T(8,128)(2,1)S(1)}, bf16[256,64]{0,1:T(8,128)(2,1)}, u32[]{:S(2)}) copy-start(bf16[256,64]{0,1:T(8,128)(2,1)} %param.20) | copy-start | bytes 98308

commit v13 on v11

--- a/solution.py
+++ b/solution.py
@@ -165,26 +165,20 @@
     shard1_ref,
     shard2_ref,
     shard3_ref,
-    cols0_ref,
-    cols1_ref,
+    right0_ref,
+    right1_ref,
     out_ref,
-    norm_ref,
 ):
     nk = 4
     row, col = row_ref[0], col_ref[0]
     size = out_ref.shape[0] // (2 * nk)
-    half, tokens, _ = norm_ref.shape[1:]
-    count = half * tokens
     for t in range(nk):
-        ref = (cols0_ref, cols1_ref)[t // 2]
+        ref = (right0_ref, right1_ref)[t // 2]
         at = pl.ds(pl.multiple_of(jnp.bitwise_xor(row, t) * size, size), size)
-        end = ref.shape[0] // 2 * (t % 2 + 1)
-        out_ref[at, :] = ref[end - size : end, :]
+        out_ref[at, :] = ref[t % 2 * size : (t % 2 + 1) * size, :]
     for t, ref in enumerate((shard0_ref, shard1_ref, shard2_ref, shard3_ref)):
-        k = jnp.bitwise_xor(col, t)
-        at = pl.ds(pl.multiple_of((nk + k) * size, size), size)
+        at = pl.ds(pl.multiple_of((nk + jnp.bitwise_xor(col, t)) * size, size), size)
         out_ref[at, :] = ref[:size, :]
-        norm_ref[k] = ref[size + count : size + 2 * count, :].reshape(norm_ref.shape[1:])
 
 
 def update_kernel(
@@ -369,12 +363,12 @@
     cols1_ref,
     weights_ref,
     gw_ref,
+    cols_ref,
     acc_ref,
     bv_ref,
     bg_ref,
     bf_ref,
     rows_ref,
-    cols_ref,
     gs_ref,
     vs_ref,
 ):
@@ -383,14 +377,13 @@
     groups, heads, lanes = gw_ref.shape
     row, col = row_ref[0], col_ref[0]
     count = half * tokens
-    size = side0_ref.shape[0] - 2 * count - cols0_ref.shape[0] // 2 + count
+    size = (side0_ref.shape[0] - 2 * count) // 2
     for t, ref in enumerate((side0_ref, side1_ref, side2_ref, side3_ref)):
         k = jnp.bitwise_xor(col, t)
         rows_ref[k] = ref[size : size + 2 * count, :].reshape(rows_ref.shape[1:])
     for t in range(nk):
         ref = (cols0_ref, cols1_ref)[t // 2]
-        start = ref.shape[0] // 2 * (t % 2)
-        part = ref[start : start + count, :]
+        part = ref[t % 2 * count : (t % 2 + 1) * count, :]
         cols_ref[jnp.bitwise_xor(row, t)] = part.reshape(cols_ref.shape[1:])
     chans = weights_ref.shape[1] // 3
     by_heads(weights_ref[:, :chans], heads, bv_ref)
@@ -491,17 +484,18 @@
 
 
 def values_kernel(
-    ready, ev0_ref, ev1_ref, ev2_ref, ev3_ref, wv_ref, norm_ref, wg_ref, v_ref, gate_ref
-):
-    evs = (ev0_ref, ev1_ref, ev2_ref, ev3_ref)
-    nk, half, tokens, wide = ev0_ref.shape
+    ready, col_ref, ev0_ref, ev1_ref, ev2_ref, ev3_ref, wv_ref, norm_ref, wg_ref, v_ref, gate_ref, ev_ref
+):
+    nr, nk, half, tokens, wide = ev_ref.shape
     chans = wv_ref.shape[1]
+    for t, ref in enumerate((ev0_ref, ev1_ref, ev2_ref, ev3_ref)):
+        ev_ref[jnp.bitwise_xor(col_ref[0], t)] = ref[...]
     gate = jax.nn.sigmoid(nn_dot(norm_ref[...], twice(wg_ref[...])))
     gate_ref[: half * tokens] = gate[:, :chans]
     gate_ref[half * tokens :] = gate[:, chans:]
     wv = twice(wv_ref[...])
     for s in range(half):
-        x = jnp.concatenate([ev[k, s] for ev in evs for k in range(nk)], axis=0)
+        x = jnp.concatenate([ev_ref[r, k, s] for r in range(nr) for k in range(nk)], axis=0)
         v_ref[s] = nn_dot(x, wv).astype(bf16)
 
 
@@ -577,7 +571,6 @@
 
 def alignment_kernel(
     ready,
-    row_ref,
     col_ref,
     own_ref,
     r1_ref,
@@ -602,7 +595,7 @@
     chans = chans // 2
     tokens = pieces * 2
     head_width = chans // heads
-    row, col = row_ref[0], col_ref[0]
+    col = col_ref[0]
 
     low = lax.broadcasted_iota(jnp.int32, (rows, wide), 1) < tile
     lgs = [p[2:].reshape(rows, wide) for p in pays]
@@ -624,8 +617,8 @@
             w_ref[source, :, 2 * n + 1, :] = rolled[n * heads : (n + 1) * heads]
     w = jnp.concatenate(
         [
-            w_ref[jnp.bitwise_xor(row, t)].reshape(heads * tokens, wide)[:, :tile]
-            for t in range(nk)
+            w_ref[k].reshape(heads * tokens, wide)[:, :tile]
+            for k in range(nk)
         ],
         axis=1,
     ).astype(bf16)
@@ -712,43 +705,46 @@
     def exchange(x, bit):
         return lax.ppermute(x, "col", [(c, c ^ bit) for c in range(nk)])
 
-    other = exchange(shard, 1)
-    across = exchange(shard, 2)
+    def to_columns(start, size):
+        pair = jnp.concatenate([x[start : start + size] for x in (shard, other)], axis=0)
+        return [
+            lax.ppermute(
+                pair,
+                ("row", "col"),
+                [(r * nk + c, (c ^ flip) * nk + r) for r in range(nr) for c in range(nk)],
+            )
+            for flip in (0, 2)
+        ]
+
+    other, across = exchange(shard, 1), exchange(shard, 2)
+    rights = to_columns(l_rows + 2 * n_rows, r_rows)
+    across, *rights = lax.optimization_barrier((across, *rights))
     all_rows = [shard, other, across, exchange(across, 1)]
-    pair = jnp.concatenate([x[l_rows + n_rows :] for x in (shard, other)], axis=0)
-    all_cols = [
-        lax.ppermute(
-            pair,
-            ("row", "col"),
-            [(r * nk + c, (c ^ flip) * nk + r) for r in range(nr) for c in range(nk)],
-        )
-        for flip in (0, 2)
-    ]
-
-    sides, block = call(
+    all_cols = to_columns(l_rows + n_rows, n_rows)
+
+    (sides,) = call(
         join_kernel,
-        (
-            sds((nk * (r_rows + l_rows), 128), bf16),
-            sds((nk, half, tokens, 2 * width), bf16),
-        ),
+        (sds((nk * (r_rows + l_rows), 128), bf16),),
         smem=2,
-    )(*place[:2], *all_rows, *all_cols)
+    )(*place[:2], *all_rows, *rights)
     if nq == 2:
         far_sides = lax.ppermute(sides, "seq", [(0, 1), (1, 0)])
     else:
         far_sides = lax.all_gather(sides, "seq", axis=0, tiled=True)
 
     head_lanes = seqs * chans // heads
-    (gw_own,) = call(
+    gw_own, block = call(
         weights_kernel,
-        (sds((groups, heads, lanes), f32),),
+        (
+            sds((groups, heads, lanes), f32),
+            sds((nk, half, tokens, 2 * width), bf16),
+        ),
         scratch=(
             pltpu.VMEM((heads * tile_i, 2 * tile_j), f32),
             pltpu.VMEM((4 * width, 4 * chans), bf16),
             pltpu.VMEM((4 * width, 4 * chans), bf16),
             pltpu.VMEM((4 * width, 4 * chans), bf16),
             pltpu.VMEM((nk, 2, half, tokens, 2 * width), bf16),
-            pltpu.VMEM((nk, half, tokens, 2 * width), bf16),
             pltpu.VMEM((heads, tile_i, head_lanes), bf16),
             pltpu.VMEM((heads, 2 * tile_j, head_lanes), bf16),
         ),
@@ -761,11 +757,7 @@
     else:
         gw_own, gw_other = lax.psum(gw_own, "seq"), jnp.zeros_like(gw_own)
 
-    def exchange_rows(x, bit):
-        return lax.ppermute(x, "row", [(r, r ^ bit) for r in range(nr)])
-
-    block, _ = lax.optimization_barrier((block, gw_own))
-    near, beyond = exchange_rows(block, 1), exchange_rows(block, 2)
+    close, remote = exchange(block, 1), exchange(block, 2)
 
     pair_out, normal, inverse, logits = call(
         update_kernel,
@@ -814,8 +806,19 @@
         for shift, pay in ((1, pay1), (2, pay2), (3, pay3))
     ]
 
-    near, beyond, pay0 = lax.optimization_barrier((near, beyond, pay0))
-    every = [block, near, beyond, exchange_rows(beyond, 1)]
+
+    close, remote, pay0 = lax.optimization_barrier((close, remote, pay0))
+    every = [block, close, remote, exchange(remote, 1)]
+    values, gating = call(
+        values_kernel,
+        (sds((half, nr * nk * tokens, 2 * chans), bf16), sds((seqs * tokens, chans), f32)),
+        scratch=(pltpu.VMEM((nr, nk, half, tokens, 2 * width), bf16),),
+        smem=1,
+        flops=4_000_000_000,
+        nbytes=6_000_000,
+    )(col_scalar, *every, content_weights_grid, normed, sigmoid_weights_grid)
+
+    got, values, gating = lax.optimization_barrier((got, values, gating))
 
     (gradient,) = call(
         gradient_kernel,
@@ -830,13 +833,6 @@
         nbytes=3_000_000,
     )(pay0, *got, logits, gw, normal, inverse, score_matrix.T)
 
-    values, gating = call(
-        values_kernel,
-        (sds((half, nr * nk * tokens, 2 * chans), bf16), sds((seqs * tokens, chans), f32)),
-        flops=4_000_000_000,
-        nbytes=6_000_000,
-    )(*every, content_weights_grid, normed, sigmoid_weights_grid)
-
     (aligned,) = call(
         alignment_kernel,
         (sds((seqs * tokens, width), bf16),),
@@ -844,11 +840,11 @@
             pltpu.VMEM((nk, heads, tokens, 2 * tile_j), f32),
             pltpu.VMEM((seqs * tokens, chans), bf16),
         ),
-        smem=2,
+        smem=1,
         flops=3_000_000_000,
         nbytes=5_000_000,
     )(
-        *place[:2],
+        col_scalar,
         pay0,
         *got,
         values,

time: 63.1 us -> 58.5 us (0.927)
  waiting for transfers between devices: 11.9 us -> 4.56 us
  starting transfers between devices: 24 us -> 25.4 us
  local copies, waits for them, and re-layouts: 2.8 us -> 3.5 us
    ppermute x3 -> x6, starting transfers between devices: 2.97 us -> 14.7 us  [exchange(): return lax.ppermute(x, 'col', [(c, c ^ bit) for c in range(nk)])]
    ppermute x5 -> x4, starting transfers between devices: 14.9 us -> 5.92 us  [to_columns(): lax.ppermute(pair, ('row', 'col'), [(r * nk + c, (c ^ flip) * nk + r) for...]
    ppermute x5 -> x4, waiting for transfers between devices: 6.82 us -> 1.86 us  [to_columns(): lax.ppermute(pair, ('row', 'col'), [(r * nk + c, (c ^ flip) * nk + r) for...]
    ppermute x3 -> x6, waiting for transfers between devices: 4.81 us -> 1.52 us  [exchange(): return lax.ppermute(x, 'col', [(c, c ^ bit) for c in range(nk)])]
    ppermute x3, starting transfers between devices: 3.97 us -> 1.78 us  [on_device(): lax.ppermute(pay, 'col', [(c, (c + shift) % nk) for c in range(nk)])]
    ppermute x1, starting transfers between devices: 0.39 us -> 1.48 us  [on_device(): gw_other = lax.ppermute(gw_own, 'seq', [(0, 1), (1, 0)])]
    ppermute x3, waiting for transfers between devices: 0.24 us -> 1.17 us  [on_device(): lax.ppermute(pay, 'col', [(c, (c + shift) % nk) for c in range(nk)])]
    slice x2 -> x4, local copies, waits for them, and re-layouts: 0.94 us -> 1.65 us  [to_columns(): x[start:start + size]]
  transfers between devices with their start and end apart: 13 -> 15, of which waited for: 4 -> 5; matrix products, arithmetic and copies ran while one was open for 2% -> 3% of each run, Pallas kernels for 26% -> 26%
where the time goes in v13:
time: 58.5 us; the launch traced here: 57.7 us
  starting transfers between devices  25.4 us (43%)
  Pallas kernels  23.3 us (40%)
  waiting for transfers between devices  4.56 us (8%)
  local copies, waits for them, and re-layouts  3.5 us (6%)
  between operations  0.83 us (1%)
    pallas_call x8, Pallas kernels, run(): pl.pallas_call(body, out_shape=out_shape, in_specs=in_specs, out_specs=[p...  23.3 us
    ppermute x6, starting transfers between devices, exchange(): return lax.ppermute(x, 'col', [(c, c ^ bit) for c in range(nk)])  14.7 us
    ppermute x4, starting transfers between devices, to_columns(): lax.ppermute(pair, ('row', 'col'), [(r * nk + c, (c ^ flip) * nk + r) for...  5.92 us
    ppermute x4, waiting for transfers between devices, to_columns(): lax.ppermute(pair, ('row', 'col'), [(r * nk + c, (c ^ flip) * nk + r) for...  1.86 us
    unnamed x22, local copies, waits for them, and re-layouts  1.85 us
    ppermute x3, starting transfers between devices, on_device(): lax.ppermute(pay, 'col', [(c, (c + shift) % nk) for c in range(nk)])  1.78 us
    slice x4, local copies, waits for them, and re-layouts, to_columns(): x[start:start + size]  1.65 us
    ppermute x1, starting transfers between devices, on_device(): far_sides = lax.ppermute(sides, 'seq', [(0, 1), (1, 0)])  1.56 us
  transfers between devices with their start and end apart: 15, of which 5 were waited for; matrix products, arithmetic and copies ran while one was open for 3% of the time, Pallas kernels for 26%

profile of v13, /device:TPU:0, one launch (start us, length us, event | category | flops | bytes accessed | tf_op | source)
XLA Modules:
  0.0 57.7 jit_solution(5074555099205118854)
XLA Ops:
  0.6 2.9 %shard_map.130 = (bf16[768,128]{1,0:T(8,128)(2,1)}, bf16[256,128]{1,0:T(8,128)(2,1)}, bf16[64,768]{1,0:T(8,128)(2,1)}) custom-call(s32[1]{0:T(128)} %bitcast.2.refs_0_, bf16[32,16,64]{2,1,0:T(8,128)(2,1)} %refs_1_.1, bf16[32,16,64]{2,1,0:T(8,128)(2,1)} %refs_2_.1, bf16[32,64]{1,0:T(8,128)(2,1)} %bitcast.23, bf16[32,64]{1,0:T(8,128)(2,1)} %bitcast.24, ...), custom_call_target="tpu_custom_call" | custom-call | tf_op jit(solution)/shard_map/pallas_call | solution.py:62
  3.5 0.5 collective-permute-start
  4.0 2.5 %collective-permute-start.1 = (bf16[768,128]{1,0:T(8,128)(2,1)}, bf16[768,128]{1,0:T(8,128)(2,1)S(1)}, u32[]{:S(2)}, u32[]{:S(2)}) collective-permute-start(bf16[768,128]{1,0:T(8,128)(2,1)} %get-tuple-element.30.refs_2_), channel_id=1, source_target_pairs={{0,2},{1,3},{2,0},{3,1},{4,6},{5,7},{6,4},{7,5},{8,10},{9,11},{10,... | collective-permute-start | bytes 589832 | tf_op jit(solution)/shard_map/ppermute | solution.py:706
  6.5 0.8 %slice.12 = bf16[128,128]{1,0:T(8,128)(2,1)S(1)} slice(bf16[768,128]{1,0:T(8,128)(2,1)} %get-tuple-element.30.refs_2_), slice={[640:768], [0:128]} | slice | bytes 65536 | tf_op jit(solution)/shard_map/slice | solution.py:709
  7.3 0.0 collective-permute-done.refs_3_
  7.3 2.6 %collective-permute-start.3 = (bf16[256,128]{1,0:T(8,128)(2,1)S(1)}, bf16[256,128]{1,0:T(8,128)(2,1)S(1)}, u32[]{:S(2)}, u32[]{:S(2)}) collective-permute-start(bf16[256,128]{1,0:T(8,128)(2,1)S(1)} %pad_maximum_fusion.1), channel_id=1, source_target_pairs={{0,8},{1,12},{2,0},{3,4},{4,9},{5,13},{6,1},{7,5},{8,10},{9,14},{1... | collective-permute-start | bytes 196616 | tf_op jit(solution)/shard_map/ppermute | solution.py:711
  9.9 0.7 %collective-permute-start.2 = (bf16[256,128]{1,0:T(8,128)(2,1)S(1)}, bf16[256,128]{1,0:T(8,128)(2,1)S(1)}, u32[]{:S(2)}, u32[]{:S(2)}) collective-permute-start(bf16[256,128]{1,0:T(8,128)(2,1)S(1)} %pad_maximum_fusion.1), channel_id=1, source_target_pairs={{0,0},{1,4},{2,8},{3,12},{4,1},{5,5},{6,9},{7,13},{8,2},{9,6},{10,... | collective-permute-start | bytes 196616 | tf_op jit(solution)/shard_map/ppermute | solution.py:711
  10.6 0.8 %slice.14 = bf16[256,128]{1,0:T(8,128)(2,1)S(1)} slice(bf16[768,128]{1,0:T(8,128)(2,1)} %get-tuple-element.30.refs_2_), slice={[384:640], [0:128]} | slice | bytes 131072 | tf_op jit(solution)/shard_map/slice | solution.py:709
  11.5 1.5 %collective-permute-done.1.refs_4_ = bf16[768,128]{1,0:T(8,128)(2,1)S(1)} collective-permute-done((bf16[768,128]{1,0:T(8,128)(2,1)}, bf16[768,128]{1,0:T(8,128)(2,1)S(1)}, u32[]{:S(2)}, u32[]{:S(2)}) %collective-permute-start.1) | collective-permute-done | bytes 196640 | tf_op jit(solution)/shard_map/ppermute | solution.py:706
  13.0 0.7 %collective-permute-done.3.refs_7_ = bf16[256,128]{1,0:T(8,128)(2,1)S(1)} collective-permute-done((bf16[256,128]{1,0:T(8,128)(2,1)S(1)}, bf16[256,128]{1,0:T(8,128)(2,1)S(1)}, u32[]{:S(2)}, u32[]{:S(2)}) %collective-permute-start.3) | collective-permute-done | bytes 65568 | tf_op jit(solution)/shard_map/ppermute | solution.py:711
  13.7 0.0 collective-permute-done.2.refs_6_
  13.7 4.2 %collective-permute-start.4 = (bf16[768,128]{1,0:T(8,128)(2,1)S(1)}, bf16[768,128]{1,0:T(8,128)(2,1)S(1)}, u32[]{:S(2)}, u32[]{:S(2)}) collective-permute-start(bf16[768,128]{1,0:T(8,128)(2,1)S(1)} %collective-permute-done.1.refs_4_), channel_id=1, source_target_pairs={{0,1},{1,0},{2,3},{3,2},{4,5},{5,4},{6,7},{7,6},{8,9},{9,8},{10,11... | collective-permute-start | bytes 589832 | tf_op jit(solution)/shard_map/ppermute | solution.py:706
  17.9 2.0 %collective-permute-start.6 = (bf16[512,128]{1,0:T(8,128)(2,1)S(1)}, bf16[512,128]{1,0:T(8,128)(2,1)S(1)}, u32[]{:S(2)}, u32[]{:S(2)}) collective-permute-start(bf16[512,128]{1,0:T(8,128)(2,1)S(1)} %pad_maximum_fusion), channel_id=1, source_target_pairs={{0,8},{1,12},{2,0},{3,4},{4,9},{5,13},{6,1},{7,5},{8,10},{9,14},{1... | collective-permute-start | bytes 393224 | tf_op jit(solution)/shard_map/ppermute | solution.py:711
  19.8 0.7 %collective-permute-start.5 = (bf16[512,128]{1,0:T(8,128)(2,1)S(1)}, bf16[512,128]{1,0:T(8,128)(2,1)S(1)}, u32[]{:S(2)}, u32[]{:S(2)}) collective-permute-start(bf16[512,128]{1,0:T(8,128)(2,1)S(1)} %pad_maximum_fusion), channel_id=1, source_target_pairs={{0,0},{1,4},{2,8},{3,12},{4,1},{5,5},{6,9},{7,13},{8,2},{9,6},{10,... | collective-permute-start | bytes 393224 | tf_op jit(solution)/shard_map/ppermute | solution.py:711
  20.5 0.0 collective-permute-done.4.refs_5_
  20.5 0.0 copy-start
  20.5 0.9 %copy-done = bf16[768,128]{1,0:T(8,128)(2,1)S(1)} copy-done((bf16[768,128]{1,0:T(8,128)(2,1)S(1)}, bf16[768,128]{1,0:T(8,128)(2,1)}, u32[]{:S(2)}) %copy-start) | copy-done | bytes 196632
  21.5 1.6 %collective-permute-start.9 = (bf16[1024,128]{1,0:T(8,128)(2,1)S(1)}, bf16[1024,128]{1,0:T(8,128)(2,1)S(1)}, u32[]{:S(2)}, u32[]{:S(2)}) collective-permute-start(bf16[1024,128]{1,0:T(8,128)(2,1)S(1)} %shard_map.132.refs_2_), channel_id=1, source_target_pairs={{0,16},{16,0},{1,17},{17,1},{2,18},{18,2},{3,19},{19,3},{4,20},{20... | collective-permute-start | bytes 786440 | tf_op jit(solution)/shard_map/ppermute | solution.py:731
  23.0 1.2 %collective-permute-done.6.refs_7_ = bf16[512,128]{1,0:T(8,128)(2,1)S(1)} collective-permute-done((bf16[512,128]{1,0:T(8,128)(2,1)S(1)}, bf16[512,128]{1,0:T(8,128)(2,1)S(1)}, u32[]{:S(2)}, u32[]{:S(2)}) %collective-permute-start.6) | collective-permute-done | bytes 131104 | tf_op jit(solution)/shard_map/ppermute | solution.py:711
  24.2 0.0 collective-permute-done.5.refs_6_
  24.2 0.0 copy-start.8
  24.2 0.9 %copy-done.8 = bf16[64,768]{1,0:T(8,128)(2,1)S(1)} copy-done((bf16[64,768]{1,0:T(8,128)(2,1)S(1)}, bf16[64,768]{1,0:T(8,128)(2,1)}, u32[]{:S(2)}) %copy-start.8) | copy-done | bytes 98328
  25.1 0.0 copy-start.5
  25.1 0.0 copy-start.6
  25.1 0.0 copy-start.7
  25.1 0.0 copy-start.10
  25.1 2.3 %shard_map.131 = (f32[16,8,256]{2,1,0:T(8,128)S(1)}, bf16[4,16,16,128]{3,2,1,0:T(8,128)(2,1)S(1)}) custom-call(s32[1]{0:T(128)} %bitcast.1.refs_0_, s32[1]{0:T(128)} %bitcast.refs_1_.refs_0_, bf16[768,128]{1,0:T(8,128)(2,1)S(1)} %copy-done, bf16[768,128]{1,0:T(8,128)(2,1)S(1)} %collective-permute-done.refs_3_, ...), custom_call_target="tpu_custom_call" | custom-call | flops 3000000000 | bytes 3000000 | tf_op jit(solution)/shard_map/pallas_call | solution.py:62
  27.4 7.2 %collective-permute-start.8 = (bf16[4,16,16,128]{3,2,1,0:T(8,128)(2,1)S(1)}, bf16[4,16,16,128]{3,2,1,0:T(8,128)(2,1)S(1)}, u32[]{:S(2)}, u32[]{:S(2)}) collective-permute-start(bf16[4,16,16,128]{3,2,1,0:T(8,128)(2,1)S(1)} %get-tuple-element.33.refs_1_), channel_id=1, source_target_pairs={{0,2},{1,3},{2,0},{3,1},{4,6},{5,7},{6,4},{7,5},{8,10},{9,11},{10,... | collective-permute-start | bytes 786440 | tf_op jit(solution)/shard_map/ppermute | solution.py:706
  34.6 0.0 collective-permute-start.7
  34.6 1.5 %collective-permute-start.10 = (f32[16,8,256]{2,1,0:T(8,128)S(1)}, f32[16,8,256]{2,1,0:T(8,128)S(1)}, u32[]{:S(2)}, u32[]{:S(2)}) collective-permute-start(f32[16,8,256]{2,1,0:T(8,128)S(1)} %get-tuple-element.37.refs_2_), channel_id=1, source_target_pairs={{0,16},{16,0},{1,17},{17,1},{2,18},{18,2},{3,19},{19,3},{4,20},{20... | collective-permute-start | bytes 393224 | tf_op jit(solution)/shard_map/ppermute | solution.py:756
  36.1 0.0 collective-permute-done.9.refs_3_
  36.1 0.0 copy-done.5
  36.1 0.0 copy-done.6
  36.1 0.0 copy-done.7
  36.1 0.0 copy-done.10
  36.1 0.0 copy-start.2
  36.1 0.0 copy-start.3
  36.1 0.0 copy-start.9
  36.1 11.0 %shard_map.133 = (bf16[4096,128]{1,0:T(8,128)(2,1)}, f32[16,128,256]{2,1,0:T(8,128)S(1)}, f32[16,8,256]{2,1,0:T(8,128)S(1)}, f32[16,8,256]{2,1,0:T(8,128)S(1)}) custom-call(s32[1]{0:T(128)} %bitcast.refs_1_.refs_0_, s32[1]{0:T(128)} %bitcast.7.refs_1_, bf16[1024,128]{1,0:T(8,128)(2,1)S(1)} %shard_map.132.refs_2_, ...), custom_call_target="tpu_custom_call" | custom-call | flops 14000000000 | bytes 5000000 | tf_op jit(solution)/shard_map/pallas_call | solution.py:62
  47.2 0.0 collective-permute-done.10.refs_3_
  47.2 0.5 shard_map.134
  47.6 0.0 collective-permute-done.8.refs_3_
  47.6 0.0 collective-permute-done.7.refs_2_
  47.6 0.3 collective-permute-start.14
  47.9 0.3 collective-permute-start.11
  48.2 0.2 collective-permute-start.12
  48.4 1.3 %collective-permute-start.13 = (f32[10,8,128]{2,1,0:T(8,128)S(1)}, f32[10,8,128]{2,1,0:T(8,128)S(1)}, u32[]{:S(2)}, u32[]{:S(2)}) collective-permute-start(f32[10,8,128]{2,1,0:T(8,128)S(1)} %get-tuple-element.42), channel_id=1, source_target_pairs={{0,3},{1,0},{2,1},{3,2},{4,7},{5,4},{6,5},{7,6},{8,11},{9,8},{10,9... | collective-permute-start | bytes 122888 | tf_op jit(solution)/shard_map/ppermute | solution.py:805
  49.7 0.0 collective-permute-done.14.refs_4_
  49.7 0.0 copy-done.2
  49.7 0.0 copy-done.3
  49.7 0.0 copy-done.9
  49.7 1.3 %shard_map.135 = (bf16[16,256,512]{2,1,0:T(8,128)(2,1)S(1)}, f32[512,256]{1,0:T(8,128)S(1)}) custom-call(s32[1]{0:T(128)} %bitcast.refs_1_.refs_0_, bf16[4,16,16,128]{3,2,1,0:T(8,128)(2,1)S(1)} %get-tuple-element.33.refs_1_, bf16[4,16,16,128]{3,2,1,0:T(8,128)(2,1)S(1)} %collective-permute-done.7.refs_2_, ...), custom_call_target="tpu_custom_call" | custom-call | flops 4000000000 | bytes 6000000 | tf_op jit(solution)/shard_map/pallas_call | solution.py:62
  51.1 0.3 collective-permute-done.11.refs_2_.refs_1_
  51.4 0.9 %collective-permute-done.12.refs_3_.refs_2_ = f32[10,8,128]{2,1,0:T(8,128)S(1)} collective-permute-done((f32[10,8,128]{2,1,0:T(8,128)S(1)}, f32[10,8,128]{2,1,0:T(8,128)S(1)}, u32[]{:S(2)}, u32[]{:S(2)}) %collective-permute-start.12) | collective-permute-done | bytes 40992 | tf_op jit(solution)/shard_map/ppermute | solution.py:805
  52.2 0.0 collective-permute-done.13.refs_4_.refs_3_
  52.2 0.0 copy-start.1
  52.2 0.0 copy-start.4
  52.2 2.8 %shard_map.137 = bf16[4096,128]{1,0:T(8,128)(2,1)} custom-call(f32[10,8,128]{2,1,0:T(8,128)S(1)} %get-tuple-element.39.refs_1_.refs_0_, f32[10,8,128]{2,1,0:T(8,128)S(1)} %collective-permute-done.11.refs_2_.refs_1_, f32[10,8,128]{2,1,0:T(8,128)S(1)} %collective-permute-done.12.refs_3_.refs_2_, f32[10,8,128]{2,1,0:T(8,128)S(1)} %collective-permute-done.13.refs_4_.refs_3_, ...), custom_call_target="tpu_custom_call" | custom-call | flops 4000000000 | bytes 3000000 | tf_op jit(solution)/shard_map/pallas_call | solution.py:62
  55.1 0.0 copy-done.1
  55.1 0.0 copy-done.4
  55.1 2.6 %shard_map.136 = bf16[512,64]{1,0:T(8,128)(2,1)} custom-call(s32[1]{0:T(128)} %bitcast.refs_1_.refs_0_, f32[10,8,128]{2,1,0:T(8,128)S(1)} %get-tuple-element.39.refs_1_.refs_0_, f32[10,8,128]{2,1,0:T(8,128)S(1)} %collective-permute-done.11.refs_2_.refs_1_, f32[10,8,128]{2,1,0:T(8,128)S(1)} %collective-permute-done.12.refs_3_.refs_2_, ...), custom_call_target="tpu_custom_call" | custom-call | flops 3000000000 | bytes 5000000 | tf_op jit(solution)/shard_map/pallas_call | solution.py:62
  (5 shorter events, 0.0 us)
Async XLA Ops:
  3.5 3.8 %collective-permute-start = (bf16[768,128]{1,0:T(8,128)(2,1)}, bf16[768,128]{1,0:T(8,128)(2,1)S(1)}, u32[]{:S(2)}, u32[]{:S(2)}) collective-permute-start(bf16[768,128]{1,0:T(8,128)(2,1)} %get-tuple-element.30.refs_2_), channel_id=1, source_target_pairs={{0,1},{1,0},{2,3},{3,2},{4,5},{5,4},{6,7},{7,6},{8,9},{9,8},{10,11... | collective-permute-start | bytes 589832 | tf_op jit(solution)/shard_map/ppermute | solution.py:706
  4.0 9.0 %collective-permute-start.1 = (bf16[768,128]{1,0:T(8,128)(2,1)}, bf16[768,128]{1,0:T(8,128)(2,1)S(1)}, u32[]{:S(2)}, u32[]{:S(2)}) collective-permute-start(bf16[768,128]{1,0:T(8,128)(2,1)} %get-tuple-element.30.refs_2_), channel_id=1, source_target_pairs={{0,2},{1,3},{2,0},{3,1},{4,6},{5,7},{6,4},{7,5},{8,10},{9,11},{10,... | collective-permute-start | bytes 589832 | tf_op jit(solution)/shard_map/ppermute | solution.py:706
  7.3 6.4 %collective-permute-start.3 = (bf16[256,128]{1,0:T(8,128)(2,1)S(1)}, bf16[256,128]{1,0:T(8,128)(2,1)S(1)}, u32[]{:S(2)}, u32[]{:S(2)}) collective-permute-start(bf16[256,128]{1,0:T(8,128)(2,1)S(1)} %pad_maximum_fusion.1), channel_id=1, source_target_pairs={{0,8},{1,12},{2,0},{3,4},{4,9},{5,13},{6,1},{7,5},{8,10},{9,14},{1... | collective-permute-start | bytes 196616 | tf_op jit(solution)/shard_map/ppermute | solution.py:711
  9.9 3.7 %collective-permute-start.2 = (bf16[256,128]{1,0:T(8,128)(2,1)S(1)}, bf16[256,128]{1,0:T(8,128)(2,1)S(1)}, u32[]{:S(2)}, u32[]{:S(2)}) collective-permute-start(bf16[256,128]{1,0:T(8,128)(2,1)S(1)} %pad_maximum_fusion.1), channel_id=1, source_target_pairs={{0,0},{1,4},{2,8},{3,12},{4,1},{5,5},{6,9},{7,13},{8,2},{9,6},{10,... | collective-permute-start | bytes 196616 | tf_op jit(solution)/shard_map/ppermute | solution.py:711
  13.7 6.9 %collective-permute-start.4 = (bf16[768,128]{1,0:T(8,128)(2,1)S(1)}, bf16[768,128]{1,0:T(8,128)(2,1)S(1)}, u32[]{:S(2)}, u32[]{:S(2)}) collective-permute-start(bf16[768,128]{1,0:T(8,128)(2,1)S(1)} %collective-permute-done.1.refs_4_), channel_id=1, source_target_pairs={{0,1},{1,0},{2,3},{3,2},{4,5},{5,4},{6,7},{7,6},{8,9},{9,8},{10,11... | collective-permute-start | bytes 589832 | tf_op jit(solution)/shard_map/ppermute | solution.py:706
  17.9 6.3 %collective-permute-start.6 = (bf16[512,128]{1,0:T(8,128)(2,1)S(1)}, bf16[512,128]{1,0:T(8,128)(2,1)S(1)}, u32[]{:S(2)}, u32[]{:S(2)}) collective-permute-start(bf16[512,128]{1,0:T(8,128)(2,1)S(1)} %pad_maximum_fusion), channel_id=1, source_target_pairs={{0,8},{1,12},{2,0},{3,4},{4,9},{5,13},{6,1},{7,5},{8,10},{9,14},{1... | collective-permute-start | bytes 393224 | tf_op jit(solution)/shard_map/ppermute | solution.py:711
  19.8 4.3 %collective-permute-start.5 = (bf16[512,128]{1,0:T(8,128)(2,1)S(1)}, bf16[512,128]{1,0:T(8,128)(2,1)S(1)}, u32[]{:S(2)}, u32[]{:S(2)}) collective-permute-start(bf16[512,128]{1,0:T(8,128)(2,1)S(1)} %pad_maximum_fusion), channel_id=1, source_target_pairs={{0,0},{1,4},{2,8},{3,12},{4,1},{5,5},{6,9},{7,13},{8,2},{9,6},{10,... | collective-permute-start | bytes 393224 | tf_op jit(solution)/shard_map/ppermute | solution.py:711
  20.5 0.9 %copy-start = (bf16[768,128]{1,0:T(8,128)(2,1)S(1)}, bf16[768,128]{1,0:T(8,128)(2,1)}, u32[]{:S(2)}) copy-start(bf16[768,128]{1,0:T(8,128)(2,1)} %get-tuple-element.30.refs_2_) | copy-start | bytes 589828
  21.5 14.6 %collective-permute-start.9 = (bf16[1024,128]{1,0:T(8,128)(2,1)S(1)}, bf16[1024,128]{1,0:T(8,128)(2,1)S(1)}, u32[]{:S(2)}, u32[]{:S(2)}) collective-permute-start(bf16[1024,128]{1,0:T(8,128)(2,1)S(1)} %shard_map.132.refs_2_), channel_id=1, source_target_pairs={{0,16},{16,0},{1,17},{17,1},{2,18},{18,2},{3,19},{19,3},{4,20},{20... | collective-permute-start | bytes 786440 | tf_op jit(solution)/shard_map/ppermute | solution.py:731
  24.2 0.9 %copy-start.8 = (bf16[64,768]{1,0:T(8,128)(2,1)S(1)}, bf16[64,768]{1,0:T(8,128)(2,1)}, u32[]{:S(2)}) copy-start(bf16[64,768]{1,0:T(8,128)(2,1)} %get-tuple-element.32.refs_8_) | copy-start | bytes 294916
  25.1 11.0 %copy-start.5 = (s32[256]{0:T(256)S(1)}, s32[256]{0:T(256)}, u32[]{:S(2)}) copy-start(s32[256]{0:T(256)} %param.13) | copy-start | bytes 3076
  25.1 11.0 %copy-start.6 = (bf16[64,64,128]{2,1,0:T(8,128)(2,1)S(1)}, bf16[64,64,128]{2,1,0:T(8,128)(2,1)}, u32[]{:S(2)}) copy-start(bf16[64,64,128]{2,1,0:T(8,128)(2,1)} %param.12) | copy-start | bytes 3145732
  25.1 11.0 %copy-start.7 = (f32[1024,128]{1,0:T(8,128)S(1)}, f32[1024,128]{1,0:T(8,128)}, u32[]{:S(2)}) copy-start(f32[1024,128]{1,0:T(8,128)} %refs_5_.2) | copy-start | bytes 1572868
  25.1 11.0 %copy-start.10 = (f32[128,8]{0,1:T(8,128)S(1)}, f32[128,8]{0,1:T(8,128)}, u32[]{:S(2)}) copy-start(f32[128,8]{0,1:T(8,128)} %param.19) | copy-start | bytes 12292
  27.4 20.3 %collective-permute-start.8 = (bf16[4,16,16,128]{3,2,1,0:T(8,128)(2,1)S(1)}, bf16[4,16,16,128]{3,2,1,0:T(8,128)(2,1)S(1)}, u32[]{:S(2)}, u32[]{:S(2)}) collective-permute-start(bf16[4,16,16,128]{3,2,1,0:T(8,128)(2,1)S(1)} %get-tuple-element.33.refs_1_), channel_id=1, source_target_pairs={{0,2},{1,3},{2,0},{3,1},{4,6},{5,7},{6,4},{7,5},{8,10},{9,11},{10,... | collective-permute-start | bytes 786440 | tf_op jit(solution)/shard_map/ppermute | solution.py:706
  34.6 13.1 %collective-permute-start.7 = (bf16[4,16,16,128]{3,2,1,0:T(8,128)(2,1)S(1)}, bf16[4,16,16,128]{3,2,1,0:T(8,128)(2,1)S(1)}, u32[]{:S(2)}, u32[]{:S(2)}) collective-permute-start(bf16[4,16,16,128]{3,2,1,0:T(8,128)(2,1)S(1)} %get-tuple-element.33.refs_1_), channel_id=1, source_target_pairs={{0,1},{1,0},{2,3},{3,2},{4,5},{5,4},{6,7},{7,6},{8,9},{9,8},{10,11... | collective-permute-start | bytes 786440 | tf_op jit(solution)/shard_map/ppermute | solution.py:706
  34.6 12.6 %collective-permute-start.10 = (f32[16,8,256]{2,1,0:T(8,128)S(1)}, f32[16,8,256]{2,1,0:T(8,128)S(1)}, u32[]{:S(2)}, u32[]{:S(2)}) collective-permute-start(f32[16,8,256]{2,1,0:T(8,128)S(1)} %get-tuple-element.37.refs_2_), channel_id=1, source_target_pairs={{0,16},{16,0},{1,17},{17,1},{2,18},{18,2},{3,19},{19,3},{4,20},{20... | collective-permute-start | bytes 393224 | tf_op jit(solution)/shard_map/ppermute | solution.py:756
  36.1 13.6 %copy-start.2 = (bf16[64,256]{1,0:T(8,128)(2,1)S(1)}, bf16[64,256]{1,0:T(8,128)(2,1)}, u32[]{:S(2)}) copy-start(bf16[64,256]{1,0:T(8,128)(2,1)} %refs_5_.3) | copy-start | bytes 98308
  36.1 13.6 %copy-start.3 = (bf16[64,256]{1,0:T(8,128)(2,1)S(1)}, bf16[64,256]{1,0:T(8,128)(2,1)}, u32[]{:S(2)}) copy-start(bf16[64,256]{1,0:T(8,128)(2,1)} %refs_7_.3) | copy-start | bytes 98308
  36.1 13.6 %copy-start.9 = (bf16[256,128]{1,0:T(8,128)(2,1)S(1)}, bf16[256,128]{1,0:T(8,128)(2,1)}, u32[]{:S(2)}) copy-start(bf16[256,128]{1,0:T(8,128)(2,1)} %get-tuple-element.45.refs_6_) | copy-start | bytes 196612
  47.6 2.1 %collective-permute-start.14 = (bf16[4,16,16,128]{3,2,1,0:T(8,128)(2,1)S(1)}, bf16[4,16,16,128]{3,2,1,0:T(8,128)(2,1)S(1)}, u32[]{:S(2)}, u32[]{:S(2)}) collective-permute-start(bf16[4,16,16,128]{3,2,1,0:T(8,128)(2,1)S(1)} %collective-permute-done.8.refs_3_), channel_id=1, source_target_pairs={{0,1},{1,0},{2,3},{3,2},{4,5},{5,4},{6,7},{7,6},{8,9},{9,8},{10,11... | collective-permute-start | bytes 786440 | tf_op jit(solution)/shard_map/ppermute | solution.py:706
  47.9 3.4 %collective-permute-start.11 = (f32[10,8,128]{2,1,0:T(8,128)S(1)}, f32[10,8,128]{2,1,0:T(8,128)S(1)}, u32[]{:S(2)}, u32[]{:S(2)}) collective-permute-start(f32[10,8,128]{2,1,0:T(8,128)S(1)} %get-tuple-element.40), channel_id=1, source_target_pairs={{0,1},{1,2},{2,3},{3,0},{4,5},{5,6},{6,7},{7,4},{8,9},{9,10},{10,1... | collective-permute-start | bytes 122888 | tf_op jit(solution)/shard_map/ppermute | solution.py:805
  48.2 4.0 %collective-permute-start.12 = (f32[10,8,128]{2,1,0:T(8,128)S(1)}, f32[10,8,128]{2,1,0:T(8,128)S(1)}, u32[]{:S(2)}, u32[]{:S(2)}) collective-permute-start(f32[10,8,128]{2,1,0:T(8,128)S(1)} %get-tuple-element.41), channel_id=1, source_target_pairs={{0,2},{1,3},{2,0},{3,1},{4,6},{5,7},{6,4},{7,5},{8,10},{9,11},{10,... | collective-permute-start | bytes 122888 | tf_op jit(solution)/shard_map/ppermute | solution.py:805
  48.4 3.8 %collective-permute-start.13 = (f32[10,8,128]{2,1,0:T(8,128)S(1)}, f32[10,8,128]{2,1,0:T(8,128)S(1)}, u32[]{:S(2)}, u32[]{:S(2)}) collective-permute-start(f32[10,8,128]{2,1,0:T(8,128)S(1)} %get-tuple-element.42), channel_id=1, source_target_pairs={{0,3},{1,0},{2,1},{3,2},{4,7},{5,4},{6,5},{7,6},{8,11},{9,8},{10,9... | collective-permute-start | bytes 122888 | tf_op jit(solution)/shard_map/ppermute | solution.py:805
  52.2 2.8 %copy-start.1 = (bf16[32,16,64]{2,1,0:T(8,128)(2,1)S(1)}, bf16[32,16,64]{2,1,0:T(8,128)(2,1)}, u32[]{:S(2)}) copy-start(bf16[32,16,64]{2,1,0:T(8,128)(2,1)} %refs_1_.1) | copy-start | bytes 196612
  52.2 2.8 %copy-start.4 = (bf16[256,64]{0,1:T(8,128)(2,1)S(1)}, bf16[256,64]{0,1:T(8,128)(2,1)}, u32[]{:S(2)}) copy-start(bf16[256,64]{0,1:T(8,128)(2,1)} %param.20) | copy-start | bytes 98308

commit v14 on v13

--- a/solution.py
+++ b/solution.py
@@ -104,6 +104,7 @@
     wg_ref,
     wf_ref,
     shard_ref,
+    rows_ref,
     norm_ref,
     weights_ref,
     turn_ref,
@@ -154,39 +155,34 @@
         res = jnp.where(mine, res, 0.0).reshape(fd // size, size, 128)
         place_ref[:, s, :] = jnp.sum(res, axis=1)
     right = place_ref[...].reshape(fd // size * seqs, 128).astype(bf16)
+    rows_ref[...] = shard_ref[: base + 2 * rows, :]
     shard_ref[base + 2 * rows :, :] = right
 
 
-def join_kernel(
-    ready,
-    row_ref,
-    col_ref,
-    shard0_ref,
-    shard1_ref,
-    shard2_ref,
-    shard3_ref,
-    right0_ref,
-    right1_ref,
-    out_ref,
-):
-    nk = 4
-    row, col = row_ref[0], col_ref[0]
-    size = out_ref.shape[0] // (2 * nk)
-    for t in range(nk):
-        ref = (right0_ref, right1_ref)[t // 2]
-        at = pl.ds(pl.multiple_of(jnp.bitwise_xor(row, t) * size, size), size)
-        out_ref[at, :] = ref[t % 2 * size : (t % 2 + 1) * size, :]
-    for t, ref in enumerate((shard0_ref, shard1_ref, shard2_ref, shard3_ref)):
-        at = pl.ds(pl.multiple_of((nk + jnp.bitwise_xor(col, t)) * size, size), size)
+def join_left_kernel(ready, col_ref, rows0_ref, rows1_ref, rows2_ref, rows3_ref, out_ref):
+    size = out_ref.shape[0] // 4
+    for t, ref in enumerate((rows0_ref, rows1_ref, rows2_ref, rows3_ref)):
+        at = pl.ds(pl.multiple_of(jnp.bitwise_xor(col_ref[0], t) * size, size), size)
         out_ref[at, :] = ref[:size, :]
+
+
+def join_right_kernel(ready, row_ref, pair0_ref, pair1_ref, out_ref):
+    size = out_ref.shape[0] // 4
+    for t in range(4):
+        ref = (pair0_ref, pair1_ref)[t // 2]
+        at = pl.ds(pl.multiple_of(jnp.bitwise_xor(row_ref[0], t) * size, size), size)
+        end = ref.shape[0] // 2 * (t % 2 + 1)
+        out_ref[at, :] = ref[end - size : end, :]
 
 
 def update_kernel(
     ready,
     col_ref,
     seq_ref,
-    sides_ref,
-    far_sides_ref,
+    left_ref,
+    right_ref,
+    far_left_ref,
+    far_right_ref,
     mask_ref,
     m_ref,
     score_ref,
@@ -220,17 +216,16 @@
     r_rows = rk_ref.shape[1] // nq
     l_rows = groups * fc
     if nq == 2:
-        sources = ((seq, 0, sides_ref), (1 - seq, 0, far_sides_ref))
+        sources = ((seq, 0, left_ref, right_ref), (1 - seq, 0, far_left_ref, far_right_ref))
     else:
-        sources = tuple((q, q, far_sides_ref) for q in range(nq))
-    for q, slot, ref in sources:
-        base = slot * (nk * r_rows + l_rows)
+        sources = tuple((q, q, far_left_ref, far_right_ref) for q in range(nq))
+    for q, slot, from_left, from_right in sources:
         at = pl.ds(pl.multiple_of(q * r_rows, r_rows), r_rows)
         for k in range(nk):
-            rk_ref[k, at, :] = ref[base + k * r_rows : base + (k + 1) * r_rows, :]
-        base = base + nk * r_rows
+            first = (slot * nk + k) * r_rows
+            rk_ref[k, at, :] = from_right[first : first + r_rows, :]
         to = pl.ds(pl.multiple_of(q * wk, wk), wk)
-        lm_ref[:, to] = ref[base : base + l_rows, :]
+        lm_ref[:, to] = from_left[slot * l_rows : (slot + 1) * l_rows, :]
     size = 128 // tokens
     right = jnp.concatenate([rk_ref[k] for k in range(nk)], axis=1)
     source = lax.broadcasted_iota(jnp.int32, (nk * 128, 4 * tile_j), 0)
@@ -377,13 +372,14 @@
     groups, heads, lanes = gw_ref.shape
     row, col = row_ref[0], col_ref[0]
     count = half * tokens
-    size = (side0_ref.shape[0] - 2 * count) // 2
+    size = side0_ref.shape[0] - 2 * count
     for t, ref in enumerate((side0_ref, side1_ref, side2_ref, side3_ref)):
         k = jnp.bitwise_xor(col, t)
         rows_ref[k] = ref[size : size + 2 * count, :].reshape(rows_ref.shape[1:])
     for t in range(nk):
         ref = (cols0_ref, cols1_ref)[t // 2]
-        part = ref[t % 2 * count : (t % 2 + 1) * count, :]
+        start = ref.shape[0] // 2 * (t % 2)
+        part = ref[start : start + count, :]
         cols_ref[jnp.bitwise_xor(row, t)] = part.reshape(cols_ref.shape[1:])
     chans = weights_ref.shape[1] // 3
     by_heads(weights_ref[:, :chans], heads, bv_ref)
@@ -677,10 +673,11 @@
     l_rows = tokens // pack * fc
     r_rows = fd * tokens // 128 * seqs
     n_rows = half * tokens
-    shard, normed, weights = call(
+    shard, rows, normed, weights = call(
         prepare_kernel,
         (
             sds((l_rows + 2 * n_rows + r_rows, 128), bf16),
+            sds((l_rows + 2 * n_rows, 128), bf16),
             sds((n_rows, 128), bf16),
             sds((width, 3 * chans), bf16),
         ),
@@ -705,32 +702,28 @@
     def exchange(x, bit):
         return lax.ppermute(x, "col", [(c, c ^ bit) for c in range(nk)])
 
-    def to_columns(start, size):
-        pair = jnp.concatenate([x[start : start + size] for x in (shard, other)], axis=0)
-        return [
-            lax.ppermute(
-                pair,
-                ("row", "col"),
-                [(r * nk + c, (c ^ flip) * nk + r) for r in range(nr) for c in range(nk)],
-            )
-            for flip in (0, 2)
-        ]
-
-    other, across = exchange(shard, 1), exchange(shard, 2)
-    rights = to_columns(l_rows + 2 * n_rows, r_rows)
-    across, *rights = lax.optimization_barrier((across, *rights))
-    all_rows = [shard, other, across, exchange(across, 1)]
-    all_cols = to_columns(l_rows + n_rows, n_rows)
-
-    (sides,) = call(
-        join_kernel,
-        (sds((nk * (r_rows + l_rows), 128), bf16),),
-        smem=2,
-    )(*place[:2], *all_rows, *rights)
-    if nq == 2:
-        far_sides = lax.ppermute(sides, "seq", [(0, 1), (1, 0)])
-    else:
-        far_sides = lax.all_gather(sides, "seq", axis=0, tiled=True)
+    other = exchange(shard, 1)
+    all_rows = [rows, other, exchange(rows, 2), exchange(rows, 3)]
+    pair = jnp.concatenate([x[l_rows + n_rows :] for x in (shard, other)], axis=0)
+    all_cols = [
+        lax.ppermute(
+            pair,
+            ("row", "col"),
+            [(r * nk + c, (c ^ flip) * nk + r) for r in range(nr) for c in range(nk)],
+        )
+        for flip in (0, 2)
+    ]
+
+    def over_seq(x):
+        if nq == 2:
+            return lax.ppermute(x, "seq", [(0, 1), (1, 0)])
+        return lax.all_gather(x, "seq", axis=0, tiled=True)
+
+    (left,) = call(join_left_kernel, (sds((nk * l_rows, 128), bf16),), smem=1)(place[1], *all_rows)
+    (right,) = call(join_right_kernel, (sds((nk * r_rows, 128), bf16),), smem=1)(
+        place[0], *all_cols
+    )
+    far_left, far_right = over_seq(left), over_seq(right)
 
     head_lanes = seqs * chans // heads
     gw_own, block = call(
@@ -782,12 +775,14 @@
         flops=14_000_000_000,
         nbytes=5_000_000,
         vmem=44 * 1024 * 1024,
-        far=(4, 5, 6, 7),
+        far=(6, 7, 8, 9),
         far_out=(0,),
     )(
         *place[1:],
-        sides,
-        far_sides,
+        left,
+        right,
+        far_left,
+        far_right,
         mask,
         outer_matrix,
         score_matrix.T,

time: 58.5 us -> 59.5 us (1.017)
  waiting for transfers between devices: 4.56 us -> 12.6 us
  starting transfers between devices: 25.4 us -> 18.2 us
    ppermute x6, waiting for transfers between devices: 1.52 us -> 11.4 us  [exchange(): return lax.ppermute(x, 'col', [(c, c ^ bit) for c in range(nk)])]
    ppermute x6, starting transfers between devices: 14.7 us -> 7.82 us  [exchange(): return lax.ppermute(x, 'col', [(c, c ^ bit) for c in range(nk)])]
    ppermute x5 -> x4, waiting for transfers between devices: 1.86 us -> 0.01 us  [the longest x2 0.01 us: on_device(): lax.ppermute(pair, ('row', 'col'), [(r * nk + c, (c ^ flip) * nk + r) for...]
    unnamed x22 -> x24, local copies, waits for them, and re-layouts: 1.85 us -> 2.76 us
    slice x4 -> x2, local copies, waits for them, and re-layouts: 1.65 us -> 0.91 us  [on_device(): x[l_rows + n_rows:]]
    ppermute x5 -> x4, starting transfers between devices: 7.47 us -> 6.83 us  [the longest x2 4.68 us: on_device(): lax.ppermute(pair, ('row', 'col'), [(r * nk + c, (c ^ flip) * nk + r) for...]
    pallas_call x8 -> x9, Pallas kernels: 23.3 us -> 23.4 us  [run(): pl.pallas_call(body, out_shape=out_shape, in_specs=in_specs, out_specs=[p...]
  transfers between devices with their start and end apart: 15 -> 14, of which waited for: 5 -> 5; matrix products, arithmetic and copies ran while one was open for 3% -> 2% of each run, Pallas kernels for 26% -> 26%
where the time goes in v14:
time: 59.5 us; the launch traced here: 58.7 us
  Pallas kernels  23.4 us (39%)
  starting transfers between devices  18.2 us (31%)
  waiting for transfers between devices  12.6 us (21%)
  local copies, waits for them, and re-layouts  3.67 us (6%)
  between operations  0.8 us (1%)
    pallas_call x9, Pallas kernels, run(): pl.pallas_call(body, out_shape=out_shape, in_specs=in_specs, out_specs=[p...  23.4 us
    ppermute x6, waiting for transfers between devices, exchange(): return lax.ppermute(x, 'col', [(c, c ^ bit) for c in range(nk)])  11.4 us
    ppermute x6, starting transfers between devices, exchange(): return lax.ppermute(x, 'col', [(c, c ^ bit) for c in range(nk)])  7.82 us
    ppermute x2, starting transfers between devices, on_device(): lax.ppermute(pair, ('row', 'col'), [(r * nk + c, (c ^ flip) * nk + r) for...  4.68 us
    unnamed x24, local copies, waits for them, and re-layouts  2.76 us
    ppermute x2, starting transfers between devices, over_seq(): return lax.ppermute(x, 'seq', [(0, 1), (1, 0)])  2.16 us
    ppermute x3, starting transfers between devices, on_device(): lax.ppermute(pay, 'col', [(c, (c + shift) % nk) for c in range(nk)])  1.78 us
    ppermute x1, starting transfers between devices, on_device(): gw_other = lax.ppermute(gw_own, 'seq', [(0, 1), (1, 0)])  1.74 us
  transfers between devices with their start and end apart: 14, of which 5 were waited for; matrix products, arithmetic and copies ran while one was open for 2% of the time, Pallas kernels for 26%

profile of v14, /device:TPU:0, one launch (start us, length us, event | category | flops | bytes accessed | tf_op | source)
XLA Modules:
  0.0 58.7 jit_solution(12013434422589645649)
XLA Ops:
  0.6 2.9 %shard_map.130 = (bf16[768,128]{1,0:T(8,128)(2,1)}, bf16[640,128]{1,0:T(8,128)(2,1)}, bf16[256,128]{1,0:T(8,128)(2,1)}, bf16[64,768]{1,0:T(8,128)(2,1)}) custom-call(s32[1]{0:T(128)} %bitcast.2.refs_0_, bf16[32,16,64]{2,1,0:T(8,128)(2,1)} %refs_1_.1, bf16[32,16,64]{2,1,0:T(8,128)(2,1)} %refs_2_.1, bf16[32,64]{1,0:T(8,128)(2,1)} %bitcast.23, ...), custom_call_target="tpu_custom_call" | custom-call | tf_op jit(solution)/shard_map/pallas_call | solution.py:62
  3.6 0.5 collective-permute-start
  4.0 0.9 %slice.6 = bf16[384,128]{1,0:T(8,128)(2,1)S(1)} slice(bf16[768,128]{1,0:T(8,128)(2,1)} %get-tuple-element.29), slice={[384:768], [0:128]} | slice | bytes 196608 | tf_op jit(solution)/shard_map/slice | solution.py:707
  4.9 0.4 collective-permute-done.refs_3_.refs_2_
  5.3 4.0 %collective-permute-start.4 = (bf16[768,128]{1,0:T(8,128)(2,1)S(1)}, bf16[768,128]{1,0:T(8,128)(2,1)S(1)}, u32[]{:S(2)}, u32[]{:S(2)}) collective-permute-start(bf16[768,128]{1,0:T(8,128)(2,1)S(1)} %pad_maximum_fusion), channel_id=1, source_target_pairs={{0,8},{1,12},{2,0},{3,4},{4,9},{5,13},{6,1},{7,5},{8,10},{9,14},{1... | collective-permute-start | bytes 589832 | tf_op jit(solution)/shard_map/ppermute | solution.py:709
  9.3 0.7 %collective-permute-start.3 = (bf16[768,128]{1,0:T(8,128)(2,1)S(1)}, bf16[768,128]{1,0:T(8,128)(2,1)S(1)}, u32[]{:S(2)}, u32[]{:S(2)}) collective-permute-start(bf16[768,128]{1,0:T(8,128)(2,1)S(1)} %pad_maximum_fusion), channel_id=1, source_target_pairs={{0,0},{1,4},{2,8},{3,12},{4,1},{5,5},{6,9},{7,13},{8,2},{9,6},{10,... | collective-permute-start | bytes 589832 | tf_op jit(solution)/shard_map/ppermute | solution.py:709
  10.0 4.6 %collective-permute-start.2 = (bf16[640,128]{1,0:T(8,128)(2,1)}, bf16[640,128]{1,0:T(8,128)(2,1)S(1)}, u32[]{:S(2)}, u32[]{:S(2)}) collective-permute-start(bf16[640,128]{1,0:T(8,128)(2,1)} %get-tuple-element.28.refs_2_.refs_1_), channel_id=1, source_target_pairs={{0,3},{1,2},{2,1},{3,0},{4,7},{5,6},{6,5},{7,4},{8,11},{9,10},{10,... | collective-permute-start | bytes 491528 | tf_op jit(solution)/shard_map/ppermute | solution.py:703
  14.6 0.0 collective-permute-start.1
  14.6 8.1 %collective-permute-done.2.refs_5_.refs_4_ = bf16[640,128]{1,0:T(8,128)(2,1)S(1)} collective-permute-done((bf16[640,128]{1,0:T(8,128)(2,1)}, bf16[640,128]{1,0:T(8,128)(2,1)S(1)}, u32[]{:S(2)}, u32[]{:S(2)}) %collective-permute-start.2) | collective-permute-done | bytes 163872 | tf_op jit(solution)/shard_map/ppermute | solution.py:703
  22.8 2.9 %collective-permute-done.1.refs_4_.refs_3_ = bf16[640,128]{1,0:T(8,128)(2,1)S(1)} collective-permute-done((bf16[640,128]{1,0:T(8,128)(2,1)}, bf16[640,128]{1,0:T(8,128)(2,1)S(1)}, u32[]{:S(2)}, u32[]{:S(2)}) %collective-permute-start.1) | collective-permute-done | bytes 163872 | tf_op jit(solution)/shard_map/ppermute | solution.py:703
  25.7 0.0 copy-start
  25.7 0.9 %copy-done = bf16[640,128]{1,0:T(8,128)(2,1)S(1)} copy-done((bf16[640,128]{1,0:T(8,128)(2,1)S(1)}, bf16[640,128]{1,0:T(8,128)(2,1)}, u32[]{:S(2)}) %copy-start) | copy-done | bytes 163864
  26.6 1.8 %collective-permute-start.7 = (bf16[512,128]{1,0:T(8,128)(2,1)S(1)}, bf16[512,128]{1,0:T(8,128)(2,1)S(1)}, u32[]{:S(2)}, u32[]{:S(2)}) collective-permute-start(bf16[512,128]{1,0:T(8,128)(2,1)S(1)} %shard_map.132.refs_2_), channel_id=1, source_target_pairs={{0,16},{16,0},{1,17},{17,1},{2,18},{18,2},{3,19},{19,3},{4,20},{20... | collective-permute-start | bytes 393224 | tf_op jit(solution)/shard_map/ppermute | solution.py:719
  28.4 0.0 collective-permute-done.4.refs_7_.refs_2_
  28.4 0.0 collective-permute-done.3.refs_6_.refs_1_
  28.4 0.4 collective-permute-start.8
  28.8 0.0 copy-start.1
  28.8 0.9 %copy-done.1 = bf16[640,128]{1,0:T(8,128)(2,1)S(1)} copy-done((bf16[640,128]{1,0:T(8,128)(2,1)S(1)}, bf16[640,128]{1,0:T(8,128)(2,1)}, u32[]{:S(2)}) %copy-start.1) | copy-done | bytes 163864
  29.7 0.0 copy-start.9
  29.7 0.9 %copy-done.9 = bf16[64,768]{1,0:T(8,128)(2,1)S(1)} copy-done((bf16[64,768]{1,0:T(8,128)(2,1)S(1)}, bf16[64,768]{1,0:T(8,128)(2,1)}, u32[]{:S(2)}) %copy-start.9) | copy-done | bytes 98328
  30.6 0.0 copy-start.6
  30.6 0.0 copy-start.7
  30.6 0.0 copy-start.8
  30.6 0.0 copy-start.11
  30.6 2.3 %shard_map.131 = (f32[16,8,256]{2,1,0:T(8,128)S(1)}, bf16[4,16,16,128]{3,2,1,0:T(8,128)(2,1)S(1)}) custom-call(s32[1]{0:T(128)} %bitcast.1.refs_0_, s32[1]{0:T(128)} %bitcast.refs_1_.refs_0_, bf16[640,128]{1,0:T(8,128)(2,1)S(1)} %copy-done.1, bf16[768,128]{1,0:T(8,128)(2,1)S(1)} %collective-permute-done.refs_3_.refs_2_, ...), custom_call_target="tpu_custom_call" | custom-call | flops 3000000000 | bytes 3000000 | tf_op jit(solution)/shard_map/pallas_call | solution.py:62
  32.9 2.4 %collective-permute-start.6 = (bf16[4,16,16,128]{3,2,1,0:T(8,128)(2,1)S(1)}, bf16[4,16,16,128]{3,2,1,0:T(8,128)(2,1)S(1)}, u32[]{:S(2)}, u32[]{:S(2)}) collective-permute-start(bf16[4,16,16,128]{3,2,1,0:T(8,128)(2,1)S(1)} %get-tuple-element.31.refs_1_), channel_id=1, source_target_pairs={{0,2},{1,3},{2,0},{3,1},{4,6},{5,7},{6,4},{7,5},{8,10},{9,11},{10,... | collective-permute-start | bytes 786440 | tf_op jit(solution)/shard_map/ppermute | solution.py:703
  35.3 0.0 collective-permute-start.5
  35.3 1.7 %collective-permute-start.9 = (f32[16,8,256]{2,1,0:T(8,128)S(1)}, f32[16,8,256]{2,1,0:T(8,128)S(1)}, u32[]{:S(2)}, u32[]{:S(2)}) collective-permute-start(f32[16,8,256]{2,1,0:T(8,128)S(1)} %get-tuple-element.33.refs_2_), channel_id=1, source_target_pairs={{0,16},{16,0},{1,17},{17,1},{2,18},{18,2},{3,19},{19,3},{4,20},{20... | collective-permute-start | bytes 393224 | tf_op jit(solution)/shard_map/ppermute | solution.py:749
  37.1 0.0 collective-permute-done.7.refs_4_
  37.1 0.0 collective-permute-done.8.refs_5_
  37.1 0.0 copy-done.6
  37.1 0.0 copy-done.7
  37.1 0.0 copy-done.8
  37.1 0.0 copy-done.11
  37.1 0.0 copy-start.3
  37.1 0.0 copy-start.4
  37.1 0.0 copy-start.10
  37.2 11.0 %shard_map.134 = (bf16[4096,128]{1,0:T(8,128)(2,1)}, f32[16,128,256]{2,1,0:T(8,128)S(1)}, f32[16,8,256]{2,1,0:T(8,128)S(1)}, f32[16,8,256]{2,1,0:T(8,128)S(1)}) custom-call(s32[1]{0:T(128)} %bitcast.refs_1_.refs_0_, s32[1]{0:T(128)} %bitcast.7.refs_1_, bf16[512,128]{1,0:T(8,128)(2,1)S(1)} %shard_map.132.refs_2_, bf16[512,128]{1,0:T(8,128)(2,1)S(1)} %shard_map.133.refs_3_, ...), custom_call_target="tpu_custom_call" | custom-call | flops 14000000000 | bytes 5000000 | tf_op jit(solution)/shard_map/pallas_call | solution.py:62
  48.2 0.0 collective-permute-done.9.refs_3_
  48.2 0.5 shard_map.135
  48.7 0.0 collective-permute-done.6.refs_3_
  48.7 0.0 collective-permute-done.5.refs_2_
  48.7 0.3 collective-permute-start.13
  49.0 0.3 collective-permute-start.10
  49.2 0.2 collective-permute-start.11
  49.4 1.3 %collective-permute-start.12 = (f32[10,8,128]{2,1,0:T(8,128)S(1)}, f32[10,8,128]{2,1,0:T(8,128)S(1)}, u32[]{:S(2)}, u32[]{:S(2)}) collective-permute-start(f32[10,8,128]{2,1,0:T(8,128)S(1)} %get-tuple-element.38), channel_id=1, source_target_pairs={{0,3},{1,0},{2,1},{3,2},{4,7},{5,4},{6,5},{7,6},{8,11},{9,8},{10,9... | collective-permute-start | bytes 122888 | tf_op jit(solution)/shard_map/ppermute | solution.py:800
  50.7 0.0 collective-permute-done.13.refs_4_
  50.7 0.0 copy-done.3
  50.7 0.0 copy-done.4
  50.8 0.0 copy-done.10
  50.8 1.3 %shard_map.136 = (bf16[16,256,512]{2,1,0:T(8,128)(2,1)S(1)}, f32[512,256]{1,0:T(8,128)S(1)}) custom-call(s32[1]{0:T(128)} %bitcast.refs_1_.refs_0_, bf16[4,16,16,128]{3,2,1,0:T(8,128)(2,1)S(1)} %get-tuple-element.31.refs_1_, bf16[4,16,16,128]{3,2,1,0:T(8,128)(2,1)S(1)} %collective-permute-done.5.refs_2_, ...), custom_call_target="tpu_custom_call" | custom-call | flops 4000000000 | bytes 6000000 | tf_op jit(solution)/shard_map/pallas_call | solution.py:62
  52.1 0.3 collective-permute-done.10.refs_2_.refs_1_
  52.4 0.9 %collective-permute-done.11.refs_3_.refs_2_ = f32[10,8,128]{2,1,0:T(8,128)S(1)} collective-permute-done((f32[10,8,128]{2,1,0:T(8,128)S(1)}, f32[10,8,128]{2,1,0:T(8,128)S(1)}, u32[]{:S(2)}, u32[]{:S(2)}) %collective-permute-start.11) | collective-permute-done | bytes 40992 | tf_op jit(solution)/shard_map/ppermute | solution.py:800
  53.3 0.0 collective-permute-done.12.refs_4_.refs_3_
  53.3 0.0 copy-start.2
  53.3 0.0 copy-start.5
  53.3 2.8 %shard_map.138 = bf16[4096,128]{1,0:T(8,128)(2,1)} custom-call(f32[10,8,128]{2,1,0:T(8,128)S(1)} %get-tuple-element.35.refs_1_.refs_0_, f32[10,8,128]{2,1,0:T(8,128)S(1)} %collective-permute-done.10.refs_2_.refs_1_, f32[10,8,128]{2,1,0:T(8,128)S(1)} %collective-permute-done.11.refs_3_.refs_2_, f32[10,8,128]{2,1,0:T(8,128)S(1)} %collective-permute-done.12.refs_4_.refs_3_, ...), custom_call_target="tpu_custom_call" | custom-call | flops 4000000000 | bytes 3000000 | tf_op jit(solution)/shard_map/pallas_call | solution.py:62
  56.1 0.0 copy-done.2
  56.1 0.0 copy-done.5
  56.1 2.6 %shard_map.137 = bf16[512,64]{1,0:T(8,128)(2,1)} custom-call(s32[1]{0:T(128)} %bitcast.refs_1_.refs_0_, f32[10,8,128]{2,1,0:T(8,128)S(1)} %get-tuple-element.35.refs_1_.refs_0_, f32[10,8,128]{2,1,0:T(8,128)S(1)} %collective-permute-done.10.refs_2_.refs_1_, f32[10,8,128]{2,1,0:T(8,128)S(1)} %collective-permute-done.11.refs_3_.refs_2_, ...), custom_call_target="tpu_custom_call" | custom-call | flops 3000000000 | bytes 5000000 | tf_op jit(solution)/shard_map/pallas_call | solution.py:62
  (4 shorter events, 0.0 us)
Async XLA Ops:
  3.6 1.7 %collective-permute-start = (bf16[768,128]{1,0:T(8,128)(2,1)}, bf16[768,128]{1,0:T(8,128)(2,1)S(1)}, u32[]{:S(2)}, u32[]{:S(2)}) collective-permute-start(bf16[768,128]{1,0:T(8,128)(2,1)} %get-tuple-element.29), channel_id=1, source_target_pairs={{0,1},{1,0},{2,3},{3,2},{4,5},{5,4},{6,7},{7,6},{8,9},{9,8},{10,11... | collective-permute-start | bytes 589832 | tf_op jit(solution)/shard_map/ppermute | solution.py:703
  5.3 23.1 %collective-permute-start.4 = (bf16[768,128]{1,0:T(8,128)(2,1)S(1)}, bf16[768,128]{1,0:T(8,128)(2,1)S(1)}, u32[]{:S(2)}, u32[]{:S(2)}) collective-permute-start(bf16[768,128]{1,0:T(8,128)(2,1)S(1)} %pad_maximum_fusion), channel_id=1, source_target_pairs={{0,8},{1,12},{2,0},{3,4},{4,9},{5,13},{6,1},{7,5},{8,10},{9,14},{1... | collective-permute-start | bytes 589832 | tf_op jit(solution)/shard_map/ppermute | solution.py:709
  9.3 19.1 %collective-permute-start.3 = (bf16[768,128]{1,0:T(8,128)(2,1)S(1)}, bf16[768,128]{1,0:T(8,128)(2,1)S(1)}, u32[]{:S(2)}, u32[]{:S(2)}) collective-permute-start(bf16[768,128]{1,0:T(8,128)(2,1)S(1)} %pad_maximum_fusion), channel_id=1, source_target_pairs={{0,0},{1,4},{2,8},{3,12},{4,1},{5,5},{6,9},{7,13},{8,2},{9,6},{10,... | collective-permute-start | bytes 589832 | tf_op jit(solution)/shard_map/ppermute | solution.py:709
  10.0 12.8 %collective-permute-start.2 = (bf16[640,128]{1,0:T(8,128)(2,1)}, bf16[640,128]{1,0:T(8,128)(2,1)S(1)}, u32[]{:S(2)}, u32[]{:S(2)}) collective-permute-start(bf16[640,128]{1,0:T(8,128)(2,1)} %get-tuple-element.28.refs_2_.refs_1_), channel_id=1, source_target_pairs={{0,3},{1,2},{2,1},{3,0},{4,7},{5,6},{6,5},{7,4},{8,11},{9,10},{10,... | collective-permute-start | bytes 491528 | tf_op jit(solution)/shard_map/ppermute | solution.py:703
  14.6 11.0 %collective-permute-start.1 = (bf16[640,128]{1,0:T(8,128)(2,1)}, bf16[640,128]{1,0:T(8,128)(2,1)S(1)}, u32[]{:S(2)}, u32[]{:S(2)}) collective-permute-start(bf16[640,128]{1,0:T(8,128)(2,1)} %get-tuple-element.28.refs_2_.refs_1_), channel_id=1, source_target_pairs={{0,2},{1,3},{2,0},{3,1},{4,6},{5,7},{6,4},{7,5},{8,10},{9,11},{10,... | collective-permute-start | bytes 491528 | tf_op jit(solution)/shard_map/ppermute | solution.py:703
  25.7 0.9 %copy-start = (bf16[640,128]{1,0:T(8,128)(2,1)S(1)}, bf16[640,128]{1,0:T(8,128)(2,1)}, u32[]{:S(2)}) copy-start(bf16[640,128]{1,0:T(8,128)(2,1)} %get-tuple-element.28.refs_2_.refs_1_) | copy-start | bytes 491524
  26.6 10.5 %collective-permute-start.7 = (bf16[512,128]{1,0:T(8,128)(2,1)S(1)}, bf16[512,128]{1,0:T(8,128)(2,1)S(1)}, u32[]{:S(2)}, u32[]{:S(2)}) collective-permute-start(bf16[512,128]{1,0:T(8,128)(2,1)S(1)} %shard_map.132.refs_2_), channel_id=1, source_target_pairs={{0,16},{16,0},{1,17},{17,1},{2,18},{18,2},{3,19},{19,3},{4,20},{20... | collective-permute-start | bytes 393224 | tf_op jit(solution)/shard_map/ppermute | solution.py:719
  28.4 8.6 %collective-permute-start.8 = (bf16[512,128]{1,0:T(8,128)(2,1)S(1)}, bf16[512,128]{1,0:T(8,128)(2,1)S(1)}, u32[]{:S(2)}, u32[]{:S(2)}) collective-permute-start(bf16[512,128]{1,0:T(8,128)(2,1)S(1)} %shard_map.133.refs_3_), channel_id=1, source_target_pairs={{0,16},{16,0},{1,17},{17,1},{2,18},{18,2},{3,19},{19,3},{4,20},{20... | collective-permute-start | bytes 393224 | tf_op jit(solution)/shard_map/ppermute | solution.py:719
  28.8 0.9 %copy-start.1 = (bf16[640,128]{1,0:T(8,128)(2,1)S(1)}, bf16[640,128]{1,0:T(8,128)(2,1)}, u32[]{:S(2)}) copy-start(bf16[640,128]{1,0:T(8,128)(2,1)} %get-tuple-element.28.refs_2_.refs_1_) | copy-start | bytes 491524
  29.7 0.9 %copy-start.9 = (bf16[64,768]{1,0:T(8,128)(2,1)S(1)}, bf16[64,768]{1,0:T(8,128)(2,1)}, u32[]{:S(2)}) copy-start(bf16[64,768]{1,0:T(8,128)(2,1)} %get-tuple-element.30.refs_8_) | copy-start | bytes 294916
  30.6 6.5 %copy-start.6 = (s32[256]{0:T(256)S(1)}, s32[256]{0:T(256)}, u32[]{:S(2)}) copy-start(s32[256]{0:T(256)} %param.13) | copy-start | bytes 3076
  30.6 6.5 %copy-start.7 = (bf16[64,64,128]{2,1,0:T(8,128)(2,1)S(1)}, bf16[64,64,128]{2,1,0:T(8,128)(2,1)}, u32[]{:S(2)}) copy-start(bf16[64,64,128]{2,1,0:T(8,128)(2,1)} %param.12) | copy-start | bytes 3145732
  30.6 6.5 %copy-start.8 = (f32[1024,128]{1,0:T(8,128)S(1)}, f32[1024,128]{1,0:T(8,128)}, u32[]{:S(2)}) copy-start(f32[1024,128]{1,0:T(8,128)} %refs_7_.4) | copy-start | bytes 1572868
  30.6 6.5 %copy-start.11 = (f32[128,8]{0,1:T(8,128)S(1)}, f32[128,8]{0,1:T(8,128)}, u32[]{:S(2)}) copy-start(f32[128,8]{0,1:T(8,128)} %param.19) | copy-start | bytes 12292
  32.9 15.8 %collective-permute-start.6 = (bf16[4,16,16,128]{3,2,1,0:T(8,128)(2,1)S(1)}, bf16[4,16,16,128]{3,2,1,0:T(8,128)(2,1)S(1)}, u32[]{:S(2)}, u32[]{:S(2)}) collective-permute-start(bf16[4,16,16,128]{3,2,1,0:T(8,128)(2,1)S(1)} %get-tuple-element.31.refs_1_), channel_id=1, source_target_pairs={{0,2},{1,3},{2,0},{3,1},{4,6},{5,7},{6,4},{7,5},{8,10},{9,11},{10,... | collective-permute-start | bytes 786440 | tf_op jit(solution)/shard_map/ppermute | solution.py:703
  35.3 13.3 %collective-permute-start.5 = (bf16[4,16,16,128]{3,2,1,0:T(8,128)(2,1)S(1)}, bf16[4,16,16,128]{3,2,1,0:T(8,128)(2,1)S(1)}, u32[]{:S(2)}, u32[]{:S(2)}) collective-permute-start(bf16[4,16,16,128]{3,2,1,0:T(8,128)(2,1)S(1)} %get-tuple-element.31.refs_1_), channel_id=1, source_target_pairs={{0,1},{1,0},{2,3},{3,2},{4,5},{5,4},{6,7},{7,6},{8,9},{9,8},{10,11... | collective-permute-start | bytes 786440 | tf_op jit(solution)/shard_map/ppermute | solution.py:703
  35.3 12.9 %collective-permute-start.9 = (f32[16,8,256]{2,1,0:T(8,128)S(1)}, f32[16,8,256]{2,1,0:T(8,128)S(1)}, u32[]{:S(2)}, u32[]{:S(2)}) collective-permute-start(f32[16,8,256]{2,1,0:T(8,128)S(1)} %get-tuple-element.33.refs_2_), channel_id=1, source_target_pairs={{0,16},{16,0},{1,17},{17,1},{2,18},{18,2},{3,19},{19,3},{4,20},{20... | collective-permute-start | bytes 393224 | tf_op jit(solution)/shard_map/ppermute | solution.py:749
  37.1 13.6 %copy-start.3 = (bf16[64,256]{1,0:T(8,128)(2,1)S(1)}, bf16[64,256]{1,0:T(8,128)(2,1)}, u32[]{:S(2)}) copy-start(bf16[64,256]{1,0:T(8,128)(2,1)} %refs_5_.1) | copy-start | bytes 98308
  37.1 13.6 %copy-start.4 = (bf16[64,256]{1,0:T(8,128)(2,1)S(1)}, bf16[64,256]{1,0:T(8,128)(2,1)}, u32[]{:S(2)}) copy-start(bf16[64,256]{1,0:T(8,128)(2,1)} %refs_7_.5) | copy-start | bytes 98308
  37.1 13.6 %copy-start.10 = (bf16[256,128]{1,0:T(8,128)(2,1)S(1)}, bf16[256,128]{1,0:T(8,128)(2,1)}, u32[]{:S(2)}) copy-start(bf16[256,128]{1,0:T(8,128)(2,1)} %get-tuple-element.41.refs_6_) | copy-start | bytes 196612
  48.7 2.1 %collective-permute-start.13 = (bf16[4,16,16,128]{3,2,1,0:T(8,128)(2,1)S(1)}, bf16[4,16,16,128]{3,2,1,0:T(8,128)(2,1)S(1)}, u32[]{:S(2)}, u32[]{:S(2)}) collective-permute-start(bf16[4,16,16,128]{3,2,1,0:T(8,128)(2,1)S(1)} %collective-permute-done.6.refs_3_), channel_id=1, source_target_pairs={{0,1},{1,0},{2,3},{3,2},{4,5},{5,4},{6,7},{7,6},{8,9},{9,8},{10,11... | collective-permute-start | bytes 786440 | tf_op jit(solution)/shard_map/ppermute | solution.py:703
  49.0 3.4 %collective-permute-start.10 = (f32[10,8,128]{2,1,0:T(8,128)S(1)}, f32[10,8,128]{2,1,0:T(8,128)S(1)}, u32[]{:S(2)}, u32[]{:S(2)}) collective-permute-start(f32[10,8,128]{2,1,0:T(8,128)S(1)} %get-tuple-element.36), channel_id=1, source_target_pairs={{0,1},{1,2},{2,3},{3,0},{4,5},{5,6},{6,7},{7,4},{8,9},{9,10},{10,1... | collective-permute-start | bytes 122888 | tf_op jit(solution)/shard_map/ppermute | solution.py:800
  49.2 4.0 %collective-permute-start.11 = (f32[10,8,128]{2,1,0:T(8,128)S(1)}, f32[10,8,128]{2,1,0:T(8,128)S(1)}, u32[]{:S(2)}, u32[]{:S(2)}) collective-permute-start(f32[10,8,128]{2,1,0:T(8,128)S(1)} %get-tuple-element.37), channel_id=1, source_target_pairs={{0,2},{1,3},{2,0},{3,1},{4,6},{5,7},{6,4},{7,5},{8,10},{9,11},{10,... | collective-permute-start | bytes 122888 | tf_op jit(solution)/shard_map/ppermute | solution.py:800
  49.4 3.9 %collective-permute-start.12 = (f32[10,8,128]{2,1,0:T(8,128)S(1)}, f32[10,8,128]{2,1,0:T(8,128)S(1)}, u32[]{:S(2)}, u32[]{:S(2)}) collective-permute-start(f32[10,8,128]{2,1,0:T(8,128)S(1)} %get-tuple-element.38), channel_id=1, source_target_pairs={{0,3},{1,0},{2,1},{3,2},{4,7},{5,4},{6,5},{7,6},{8,11},{9,8},{10,9... | collective-permute-start | bytes 122888 | tf_op jit(solution)/shard_map/ppermute | solution.py:800
  53.3 2.8 %copy-start.2 = (bf16[32,16,64]{2,1,0:T(8,128)(2,1)S(1)}, bf16[32,16,64]{2,1,0:T(8,128)(2,1)}, u32[]{:S(2)}) copy-start(bf16[32,16,64]{2,1,0:T(8,128)(2,1)} %refs_1_.1) | copy-start | bytes 196612
  53.3 2.8 %copy-start.5 = (bf16[256,64]{0,1:T(8,128)(2,1)S(1)}, bf16[256,64]{0,1:T(8,128)(2,1)}, u32[]{:S(2)}) copy-start(bf16[256,64]{0,1:T(8,128)(2,1)} %param.20) | copy-start | bytes 98308

commit v15 on v14

--- a/solution.py
+++ b/solution.py
@@ -703,7 +703,7 @@
         return lax.ppermute(x, "col", [(c, c ^ bit) for c in range(nk)])
 
     other = exchange(shard, 1)
-    all_rows = [rows, other, exchange(rows, 2), exchange(rows, 3)]
+    across = exchange(rows, 2)
     pair = jnp.concatenate([x[l_rows + n_rows :] for x in (shard, other)], axis=0)
     all_cols = [
         lax.ppermute(
@@ -713,6 +713,9 @@
         )
         for flip in (0, 2)
     ]
+
+    across, *all_cols = lax.optimization_barrier((across, *all_cols))
+    all_rows = [rows, other, across, exchange(across, 1)]
 
     def over_seq(x):
         if nq == 2:

time: 59.5 us -> 55.4 us (0.931)
  waiting for transfers between devices: 12.6 us -> 9.59 us
  local copies, waits for them, and re-layouts: 3.67 us -> 2.75 us
    ppermute x6, waiting for transfers between devices: 11.4 us -> 8.62 us  [exchange(): return lax.ppermute(x, 'col', [(c, c ^ bit) for c in range(nk)])]
    ppermute x2, starting transfers between devices: 2.16 us -> 3.16 us  [over_seq(): return lax.ppermute(x, 'seq', [(0, 1), (1, 0)])]
    ppermute x1, starting transfers between devices: 1.74 us -> 0.73 us  [on_device(): gw_other = lax.ppermute(gw_own, 'seq', [(0, 1), (1, 0)])]
    unnamed x24 -> x22, local copies, waits for them, and re-layouts: 2.76 us -> 1.85 us
  transfers between devices with their start and end apart: 14 -> 14, of which waited for: 5 -> 4; matrix products, arithmetic and copies ran while one was open for 2% -> 2% of each run, Pallas kernels for 26% -> 28%
where the time goes in v15:
time: 55.4 us; the launch traced here: 54.6 us
  Pallas kernels  23.4 us (42%)
  starting transfers between devices  18 us (32%)
  waiting for transfers between devices  9.59 us (17%)
  local copies, waits for them, and re-layouts  2.75 us (5%)
  between operations  0.81 us (1%)
    pallas_call x9, Pallas kernels, run(): pl.pallas_call(body, out_shape=out_shape, in_specs=in_specs, out_specs=[p...  23.4 us
    ppermute x6, waiting for transfers between devices, exchange(): return lax.ppermute(x, 'col', [(c, c ^ bit) for c in range(nk)])  8.62 us
    ppermute x6, starting transfers between devices, exchange(): return lax.ppermute(x, 'col', [(c, c ^ bit) for c in range(nk)])  7.47 us
    ppermute x2, starting transfers between devices, on_device(): lax.ppermute(pair, ('row', 'col'), [(r * nk + c, (c ^ flip) * nk + r) for...  4.68 us
    ppermute x2, starting transfers between devices, over_seq(): return lax.ppermute(x, 'seq', [(0, 1), (1, 0)])  3.16 us
    ppermute x3, starting transfers between devices, on_device(): lax.ppermute(pay, 'col', [(c, (c + shift) % nk) for c in range(nk)])  2 us
    unnamed x22, local copies, waits for them, and re-layouts  1.85 us
  transfers between devices with their start and end apart: 14, of which 4 were waited for; matrix products, arithmetic and copies ran while one was open for 2% of the time, Pallas kernels for 28%

profile of v15, /device:TPU:0, one launch (start us, length us, event | category | flops | bytes accessed | tf_op | source)
XLA Modules:
  0.0 54.6 jit_solution(3543665343403716519)
XLA Ops:
  0.6 2.9 %shard_map.130 = (bf16[768,128]{1,0:T(8,128)(2,1)}, bf16[640,128]{1,0:T(8,128)(2,1)}, bf16[256,128]{1,0:T(8,128)(2,1)}, bf16[64,768]{1,0:T(8,128)(2,1)}) custom-call(s32[1]{0:T(128)} %bitcast.2.refs_0_, bf16[32,16,64]{2,1,0:T(8,128)(2,1)} %refs_1_.1, bf16[32,16,64]{2,1,0:T(8,128)(2,1)} %refs_2_.1, bf16[32,64]{1,0:T(8,128)(2,1)} %bitcast.23, ...), custom_call_target="tpu_custom_call" | custom-call | tf_op jit(solution)/shard_map/pallas_call | solution.py:62
  3.6 0.5 collective-permute-start
  4.0 0.9 %slice.6 = bf16[384,128]{1,0:T(8,128)(2,1)S(1)} slice(bf16[768,128]{1,0:T(8,128)(2,1)} %get-tuple-element.32), slice={[384:768], [0:128]} | slice | bytes 196608 | tf_op jit(solution)/shard_map/slice | solution.py:707
  4.9 0.4 collective-permute-done.refs_3_.refs_2_
  5.3 4.0 %collective-permute-start.3 = (bf16[768,128]{1,0:T(8,128)(2,1)S(1)}, bf16[768,128]{1,0:T(8,128)(2,1)S(1)}, u32[]{:S(2)}, u32[]{:S(2)}) collective-permute-start(bf16[768,128]{1,0:T(8,128)(2,1)S(1)} %pad_maximum_fusion), channel_id=1, source_target_pairs={{0,8},{1,12},{2,0},{3,4},{4,9},{5,13},{6,1},{7,5},{8,10},{9,14},{1... | collective-permute-start | bytes 589832 | tf_op jit(solution)/shard_map/ppermute | solution.py:709
  9.3 0.7 %collective-permute-start.2 = (bf16[768,128]{1,0:T(8,128)(2,1)S(1)}, bf16[768,128]{1,0:T(8,128)(2,1)S(1)}, u32[]{:S(2)}, u32[]{:S(2)}) collective-permute-start(bf16[768,128]{1,0:T(8,128)(2,1)S(1)} %pad_maximum_fusion), channel_id=1, source_target_pairs={{0,0},{1,4},{2,8},{3,12},{4,1},{5,5},{6,9},{7,13},{8,2},{9,6},{10,... | collective-permute-start | bytes 589832 | tf_op jit(solution)/shard_map/ppermute | solution.py:709
  10.0 4.3 %collective-permute-start.1 = (bf16[640,128]{1,0:T(8,128)(2,1)}, bf16[640,128]{1,0:T(8,128)(2,1)S(1)}, u32[]{:S(2)}, u32[]{:S(2)}) collective-permute-start(bf16[640,128]{1,0:T(8,128)(2,1)} %get-tuple-element.31.refs_2_.refs_1_), channel_id=1, source_target_pairs={{0,2},{1,3},{2,0},{3,1},{4,6},{5,7},{6,4},{7,5},{8,10},{9,11},{10,... | collective-permute-start | bytes 491528 | tf_op jit(solution)/shard_map/ppermute | solution.py:703
  14.3 8.2 %collective-permute-done.1.refs_4_.refs_3_ = bf16[640,128]{1,0:T(8,128)(2,1)S(1)} collective-permute-done((bf16[640,128]{1,0:T(8,128)(2,1)}, bf16[640,128]{1,0:T(8,128)(2,1)S(1)}, u32[]{:S(2)}, u32[]{:S(2)}) %collective-permute-start.1) | collective-permute-done | bytes 163872 | tf_op jit(solution)/shard_map/ppermute | solution.py:703
  22.5 0.0 collective-permute-done.3.refs_7_.refs_2_
  22.5 0.0 collective-permute-done.2.refs_6_.refs_1_
  22.5 0.0 collective-permute-start.4
  22.6 1.8 %collective-permute-start.8 = (bf16[512,128]{1,0:T(8,128)(2,1)S(1)}, bf16[512,128]{1,0:T(8,128)(2,1)S(1)}, u32[]{:S(2)}, u32[]{:S(2)}) collective-permute-start(bf16[512,128]{1,0:T(8,128)(2,1)S(1)} %shard_map.133.refs_3_), channel_id=1, source_target_pairs={{0,16},{16,0},{1,17},{17,1},{2,18},{18,2},{3,19},{19,3},{4,20},{20... | collective-permute-start | bytes 393224 | tf_op jit(solution)/shard_map/ppermute | solution.py:722
  24.4 0.0 collective-permute-done.4.refs_5_.refs_4_
  24.4 0.0 copy-start
  24.4 0.9 %copy-done = bf16[640,128]{1,0:T(8,128)(2,1)S(1)} copy-done((bf16[640,128]{1,0:T(8,128)(2,1)S(1)}, bf16[640,128]{1,0:T(8,128)(2,1)}, u32[]{:S(2)}) %copy-start) | copy-done | bytes 163864
  25.3 1.4 %collective-permute-start.7 = (bf16[512,128]{1,0:T(8,128)(2,1)S(1)}, bf16[512,128]{1,0:T(8,128)(2,1)S(1)}, u32[]{:S(2)}, u32[]{:S(2)}) collective-permute-start(bf16[512,128]{1,0:T(8,128)(2,1)S(1)} %shard_map.132.refs_2_), channel_id=1, source_target_pairs={{0,16},{16,0},{1,17},{17,1},{2,18},{18,2},{3,19},{19,3},{4,20},{20... | collective-permute-start | bytes 393224 | tf_op jit(solution)/shard_map/ppermute | solution.py:722
  26.7 0.0 copy-start.8
  26.7 0.9 %copy-done.8 = bf16[64,768]{1,0:T(8,128)(2,1)S(1)} copy-done((bf16[64,768]{1,0:T(8,128)(2,1)S(1)}, bf16[64,768]{1,0:T(8,128)(2,1)}, u32[]{:S(2)}) %copy-start.8) | copy-done | bytes 98328
  27.5 0.0 copy-start.5
  27.6 0.0 copy-start.6
  27.6 0.0 copy-start.7
  27.6 0.0 copy-start.10
  27.6 2.3 %shard_map.131 = (f32[16,8,256]{2,1,0:T(8,128)S(1)}, bf16[4,16,16,128]{3,2,1,0:T(8,128)(2,1)S(1)}) custom-call(s32[1]{0:T(128)} %bitcast.1.refs_0_, s32[1]{0:T(128)} %bitcast.refs_1_.refs_0_, bf16[640,128]{1,0:T(8,128)(2,1)S(1)} %copy-done, bf16[768,128]{1,0:T(8,128)(2,1)S(1)} %collective-permute-done.refs_3_.refs_2_, ...), custom_call_target="tpu_custom_call" | custom-call | flops 3000000000 | bytes 3000000 | tf_op jit(solution)/shard_map/pallas_call | solution.py:62
  29.8 2.4 %collective-permute-start.6 = (bf16[4,16,16,128]{3,2,1,0:T(8,128)(2,1)S(1)}, bf16[4,16,16,128]{3,2,1,0:T(8,128)(2,1)S(1)}, u32[]{:S(2)}, u32[]{:S(2)}) collective-permute-start(bf16[4,16,16,128]{3,2,1,0:T(8,128)(2,1)S(1)} %get-tuple-element.37.refs_1_), channel_id=1, source_target_pairs={{0,2},{1,3},{2,0},{3,1},{4,6},{5,7},{6,4},{7,5},{8,10},{9,11},{10,... | collective-permute-start | bytes 786440 | tf_op jit(solution)/shard_map/ppermute | solution.py:703
  32.3 0.0 collective-permute-start.5
  32.3 0.7 %collective-permute-start.9 = (f32[16,8,256]{2,1,0:T(8,128)S(1)}, f32[16,8,256]{2,1,0:T(8,128)S(1)}, u32[]{:S(2)}, u32[]{:S(2)}) collective-permute-start(f32[16,8,256]{2,1,0:T(8,128)S(1)} %get-tuple-element.39.refs_2_), channel_id=1, source_target_pairs={{0,16},{16,0},{1,17},{17,1},{2,18},{18,2},{3,19},{19,3},{4,20},{20... | collective-permute-start | bytes 393224 | tf_op jit(solution)/shard_map/ppermute | solution.py:752
  33.0 0.0 collective-permute-done.8.refs_5_
  33.0 0.0 collective-permute-done.7.refs_4_
  33.0 0.0 copy-done.5
  33.0 0.0 copy-done.6
  33.0 0.0 copy-done.7
  33.0 0.0 copy-done.10
  33.1 0.0 copy-start.2
  33.1 0.0 copy-start.3
  33.1 0.0 copy-start.9
  33.1 11.0 %shard_map.134 = (bf16[4096,128]{1,0:T(8,128)(2,1)}, f32[16,128,256]{2,1,0:T(8,128)S(1)}, f32[16,8,256]{2,1,0:T(8,128)S(1)}, f32[16,8,256]{2,1,0:T(8,128)S(1)}) custom-call(s32[1]{0:T(128)} %bitcast.refs_1_.refs_0_, s32[1]{0:T(128)} %bitcast.7.refs_1_, bf16[512,128]{1,0:T(8,128)(2,1)S(1)} %shard_map.132.refs_2_, bf16[512,128]{1,0:T(8,128)(2,1)S(1)} %shard_map.133.refs_3_, ...), custom_call_target="tpu_custom_call" | custom-call | flops 14000000000 | bytes 5000000 | tf_op jit(solution)/shard_map/pallas_call | solution.py:62
  44.1 0.0 collective-permute-done.9.refs_3_
  44.1 0.5 shard_map.135
  44.6 0.0 collective-permute-done.6.refs_3_
  44.6 0.0 collective-permute-done.5.refs_2_
  44.6 0.3 collective-permute-start.13
  44.9 0.3 collective-permute-start.10
  45.2 0.7 %collective-permute-start.11 = (f32[10,8,128]{2,1,0:T(8,128)S(1)}, f32[10,8,128]{2,1,0:T(8,128)S(1)}, u32[]{:S(2)}, u32[]{:S(2)}) collective-permute-start(f32[10,8,128]{2,1,0:T(8,128)S(1)} %get-tuple-element.43), channel_id=1, source_target_pairs={{0,2},{1,3},{2,0},{3,1},{4,6},{5,7},{6,4},{7,5},{8,10},{9,11},{10,... | collective-permute-start | bytes 122888 | tf_op jit(solution)/shard_map/ppermute | solution.py:803
  45.9 1.0 %collective-permute-start.12 = (f32[10,8,128]{2,1,0:T(8,128)S(1)}, f32[10,8,128]{2,1,0:T(8,128)S(1)}, u32[]{:S(2)}, u32[]{:S(2)}) collective-permute-start(f32[10,8,128]{2,1,0:T(8,128)S(1)} %get-tuple-element.44), channel_id=1, source_target_pairs={{0,3},{1,0},{2,1},{3,2},{4,7},{5,4},{6,5},{7,6},{8,11},{9,8},{10,9... | collective-permute-start | bytes 122888 | tf_op jit(solution)/shard_map/ppermute | solution.py:803
  46.9 0.0 collective-permute-done.13.refs_4_
  46.9 0.0 copy-done.2
  46.9 0.0 copy-done.3
  46.9 0.0 copy-done.9
  46.9 1.3 %shard_map.136 = (bf16[16,256,512]{2,1,0:T(8,128)(2,1)S(1)}, f32[512,256]{1,0:T(8,128)S(1)}) custom-call(s32[1]{0:T(128)} %bitcast.refs_1_.refs_0_, bf16[4,16,16,128]{3,2,1,0:T(8,128)(2,1)S(1)} %get-tuple-element.37.refs_1_, bf16[4,16,16,128]{3,2,1,0:T(8,128)(2,1)S(1)} %collective-permute-done.5.refs_2_, ...), custom_call_target="tpu_custom_call" | custom-call | flops 4000000000 | bytes 6000000 | tf_op jit(solution)/shard_map/pallas_call | solution.py:62
  48.2 0.1 collective-permute-done.10.refs_2_.refs_1_
  48.3 0.9 %collective-permute-done.11.refs_3_.refs_2_ = f32[10,8,128]{2,1,0:T(8,128)S(1)} collective-permute-done((f32[10,8,128]{2,1,0:T(8,128)S(1)}, f32[10,8,128]{2,1,0:T(8,128)S(1)}, u32[]{:S(2)}, u32[]{:S(2)}) %collective-permute-start.11) | collective-permute-done | bytes 40992 | tf_op jit(solution)/shard_map/ppermute | solution.py:803
  49.2 0.0 collective-permute-done.12.refs_4_.refs_3_
  49.2 0.0 copy-start.1
  49.2 0.0 copy-start.4
  49.2 2.8 %shard_map.138 = bf16[4096,128]{1,0:T(8,128)(2,1)} custom-call(f32[10,8,128]{2,1,0:T(8,128)S(1)} %get-tuple-element.41.refs_1_.refs_0_, f32[10,8,128]{2,1,0:T(8,128)S(1)} %collective-permute-done.10.refs_2_.refs_1_, f32[10,8,128]{2,1,0:T(8,128)S(1)} %collective-permute-done.11.refs_3_.refs_2_, f32[10,8,128]{2,1,0:T(8,128)S(1)} %collective-permute-done.12.refs_4_.refs_3_, ...), custom_call_target="tpu_custom_call" | custom-call | flops 4000000000 | bytes 3000000 | tf_op jit(solution)/shard_map/pallas_call | solution.py:62
  52.0 0.0 copy-done.1
  52.0 0.0 copy-done.4
  52.1 2.6 %shard_map.137 = bf16[512,64]{1,0:T(8,128)(2,1)} custom-call(s32[1]{0:T(128)} %bitcast.refs_1_.refs_0_, f32[10,8,128]{2,1,0:T(8,128)S(1)} %get-tuple-element.41.refs_1_.refs_0_, f32[10,8,128]{2,1,0:T(8,128)S(1)} %collective-permute-done.10.refs_2_.refs_1_, f32[10,8,128]{2,1,0:T(8,128)S(1)} %collective-permute-done.11.refs_3_.refs_2_, ...), custom_call_target="tpu_custom_call" | custom-call | flops 3000000000 | bytes 5000000 | tf_op jit(solution)/shard_map/pallas_call | solution.py:62
  (4 shorter events, 0.0 us)
Async XLA Ops:
  3.6 1.7 %collective-permute-start = (bf16[768,128]{1,0:T(8,128)(2,1)}, bf16[768,128]{1,0:T(8,128)(2,1)S(1)}, u32[]{:S(2)}, u32[]{:S(2)}) collective-permute-start(bf16[768,128]{1,0:T(8,128)(2,1)} %get-tuple-element.32), channel_id=1, source_target_pairs={{0,1},{1,0},{2,3},{3,2},{4,5},{5,4},{6,7},{7,6},{8,9},{9,8},{10,11... | collective-permute-start | bytes 589832 | tf_op jit(solution)/shard_map/ppermute | solution.py:703
  5.3 17.2 %collective-permute-start.3 = (bf16[768,128]{1,0:T(8,128)(2,1)S(1)}, bf16[768,128]{1,0:T(8,128)(2,1)S(1)}, u32[]{:S(2)}, u32[]{:S(2)}) collective-permute-start(bf16[768,128]{1,0:T(8,128)(2,1)S(1)} %pad_maximum_fusion), channel_id=1, source_target_pairs={{0,8},{1,12},{2,0},{3,4},{4,9},{5,13},{6,1},{7,5},{8,10},{9,14},{1... | collective-permute-start | bytes 589832 | tf_op jit(solution)/shard_map/ppermute | solution.py:709
  9.3 13.2 %collective-permute-start.2 = (bf16[768,128]{1,0:T(8,128)(2,1)S(1)}, bf16[768,128]{1,0:T(8,128)(2,1)S(1)}, u32[]{:S(2)}, u32[]{:S(2)}) collective-permute-start(bf16[768,128]{1,0:T(8,128)(2,1)S(1)} %pad_maximum_fusion), channel_id=1, source_target_pairs={{0,0},{1,4},{2,8},{3,12},{4,1},{5,5},{6,9},{7,13},{8,2},{9,6},{10,... | collective-permute-start | bytes 589832 | tf_op jit(solution)/shard_map/ppermute | solution.py:709
  10.0 12.5 %collective-permute-start.1 = (bf16[640,128]{1,0:T(8,128)(2,1)}, bf16[640,128]{1,0:T(8,128)(2,1)S(1)}, u32[]{:S(2)}, u32[]{:S(2)}) collective-permute-start(bf16[640,128]{1,0:T(8,128)(2,1)} %get-tuple-element.31.refs_2_.refs_1_), channel_id=1, source_target_pairs={{0,2},{1,3},{2,0},{3,1},{4,6},{5,7},{6,4},{7,5},{8,10},{9,11},{10,... | collective-permute-start | bytes 491528 | tf_op jit(solution)/shard_map/ppermute | solution.py:703
  22.5 1.8 %collective-permute-start.4 = (bf16[640,128]{1,0:T(8,128)(2,1)S(1)}, bf16[640,128]{1,0:T(8,128)(2,1)S(1)}, u32[]{:S(2)}, u32[]{:S(2)}) collective-permute-start(bf16[640,128]{1,0:T(8,128)(2,1)S(1)} %collective-permute-done.1.refs_4_.refs_3_), channel_id=1, source_target_pairs={{0,1},{1,0},{2,3},{3,2},{4,5},{5,4},{6,7},{7,6},{8,9},{9,8},{10,11... | collective-permute-start | bytes 491528 | tf_op jit(solution)/shard_map/ppermute | solution.py:703
  22.6 10.5 %collective-permute-start.8 = (bf16[512,128]{1,0:T(8,128)(2,1)S(1)}, bf16[512,128]{1,0:T(8,128)(2,1)S(1)}, u32[]{:S(2)}, u32[]{:S(2)}) collective-permute-start(bf16[512,128]{1,0:T(8,128)(2,1)S(1)} %shard_map.133.refs_3_), channel_id=1, source_target_pairs={{0,16},{16,0},{1,17},{17,1},{2,18},{18,2},{3,19},{19,3},{4,20},{20... | collective-permute-start | bytes 393224 | tf_op jit(solution)/shard_map/ppermute | solution.py:722
  24.4 0.9 %copy-start = (bf16[640,128]{1,0:T(8,128)(2,1)S(1)}, bf16[640,128]{1,0:T(8,128)(2,1)}, u32[]{:S(2)}) copy-start(bf16[640,128]{1,0:T(8,128)(2,1)} %get-tuple-element.31.refs_2_.refs_1_) | copy-start | bytes 491524
  25.3 7.7 %collective-permute-start.7 = (bf16[512,128]{1,0:T(8,128)(2,1)S(1)}, bf16[512,128]{1,0:T(8,128)(2,1)S(1)}, u32[]{:S(2)}, u32[]{:S(2)}) collective-permute-start(bf16[512,128]{1,0:T(8,128)(2,1)S(1)} %shard_map.132.refs_2_), channel_id=1, source_target_pairs={{0,16},{16,0},{1,17},{17,1},{2,18},{18,2},{3,19},{19,3},{4,20},{20... | collective-permute-start | bytes 393224 | tf_op jit(solution)/shard_map/ppermute | solution.py:722
  26.7 0.9 %copy-start.8 = (bf16[64,768]{1,0:T(8,128)(2,1)S(1)}, bf16[64,768]{1,0:T(8,128)(2,1)}, u32[]{:S(2)}) copy-start(bf16[64,768]{1,0:T(8,128)(2,1)} %get-tuple-element.36.refs_8_) | copy-start | bytes 294916
  27.5 5.5 %copy-start.5 = (s32[256]{0:T(256)S(1)}, s32[256]{0:T(256)}, u32[]{:S(2)}) copy-start(s32[256]{0:T(256)} %param.13) | copy-start | bytes 3076
  27.6 5.5 %copy-start.6 = (bf16[64,64,128]{2,1,0:T(8,128)(2,1)S(1)}, bf16[64,64,128]{2,1,0:T(8,128)(2,1)}, u32[]{:S(2)}) copy-start(bf16[64,64,128]{2,1,0:T(8,128)(2,1)} %param.12) | copy-start | bytes 3145732
  27.6 5.5 %copy-start.7 = (f32[1024,128]{1,0:T(8,128)S(1)}, f32[1024,128]{1,0:T(8,128)}, u32[]{:S(2)}) copy-start(f32[1024,128]{1,0:T(8,128)} %refs_7_.4) | copy-start | bytes 1572868
  27.6 5.5 %copy-start.10 = (f32[128,8]{0,1:T(8,128)S(1)}, f32[128,8]{0,1:T(8,128)}, u32[]{:S(2)}) copy-start(f32[128,8]{0,1:T(8,128)} %param.19) | copy-start | bytes 12292
  29.8 14.8 %collective-permute-start.6 = (bf16[4,16,16,128]{3,2,1,0:T(8,128)(2,1)S(1)}, bf16[4,16,16,128]{3,2,1,0:T(8,128)(2,1)S(1)}, u32[]{:S(2)}, u32[]{:S(2)}) collective-permute-start(bf16[4,16,16,128]{3,2,1,0:T(8,128)(2,1)S(1)} %get-tuple-element.37.refs_1_), channel_id=1, source_target_pairs={{0,2},{1,3},{2,0},{3,1},{4,6},{5,7},{6,4},{7,5},{8,10},{9,11},{10,... | collective-permute-start | bytes 786440 | tf_op jit(solution)/shard_map/ppermute | solution.py:703
  32.3 12.3 %collective-permute-start.5 = (bf16[4,16,16,128]{3,2,1,0:T(8,128)(2,1)S(1)}, bf16[4,16,16,128]{3,2,1,0:T(8,128)(2,1)S(1)}, u32[]{:S(2)}, u32[]{:S(2)}) collective-permute-start(bf16[4,16,16,128]{3,2,1,0:T(8,128)(2,1)S(1)} %get-tuple-element.37.refs_1_), channel_id=1, source_target_pairs={{0,1},{1,0},{2,3},{3,2},{4,5},{5,4},{6,7},{7,6},{8,9},{9,8},{10,11... | collective-permute-start | bytes 786440 | tf_op jit(solution)/shard_map/ppermute | solution.py:703
  32.3 11.9 %collective-permute-start.9 = (f32[16,8,256]{2,1,0:T(8,128)S(1)}, f32[16,8,256]{2,1,0:T(8,128)S(1)}, u32[]{:S(2)}, u32[]{:S(2)}) collective-permute-start(f32[16,8,256]{2,1,0:T(8,128)S(1)} %get-tuple-element.39.refs_2_), channel_id=1, source_target_pairs={{0,16},{16,0},{1,17},{17,1},{2,18},{18,2},{3,19},{19,3},{4,20},{20... | collective-permute-start | bytes 393224 | tf_op jit(solution)/shard_map/ppermute | solution.py:752
  33.1 13.8 %copy-start.2 = (bf16[64,256]{1,0:T(8,128)(2,1)S(1)}, bf16[64,256]{1,0:T(8,128)(2,1)}, u32[]{:S(2)}) copy-start(bf16[64,256]{1,0:T(8,128)(2,1)} %refs_5_.1) | copy-start | bytes 98308
  33.1 13.8 %copy-start.3 = (bf16[64,256]{1,0:T(8,128)(2,1)S(1)}, bf16[64,256]{1,0:T(8,128)(2,1)}, u32[]{:S(2)}) copy-start(bf16[64,256]{1,0:T(8,128)(2,1)} %refs_7_.5) | copy-start | bytes 98308
  33.1 13.8 %copy-start.9 = (bf16[256,128]{1,0:T(8,128)(2,1)S(1)}, bf16[256,128]{1,0:T(8,128)(2,1)}, u32[]{:S(2)}) copy-start(bf16[256,128]{1,0:T(8,128)(2,1)} %get-tuple-element.47.refs_6_) | copy-start | bytes 196612
  44.6 2.3 %collective-permute-start.13 = (bf16[4,16,16,128]{3,2,1,0:T(8,128)(2,1)S(1)}, bf16[4,16,16,128]{3,2,1,0:T(8,128)(2,1)S(1)}, u32[]{:S(2)}, u32[]{:S(2)}) collective-permute-start(bf16[4,16,16,128]{3,2,1,0:T(8,128)(2,1)S(1)} %collective-permute-done.6.refs_3_), channel_id=1, source_target_pairs={{0,1},{1,0},{2,3},{3,2},{4,5},{5,4},{6,7},{7,6},{8,9},{9,8},{10,11... | collective-permute-start | bytes 786440 | tf_op jit(solution)/shard_map/ppermute | solution.py:703
  44.9 3.4 %collective-permute-start.10 = (f32[10,8,128]{2,1,0:T(8,128)S(1)}, f32[10,8,128]{2,1,0:T(8,128)S(1)}, u32[]{:S(2)}, u32[]{:S(2)}) collective-permute-start(f32[10,8,128]{2,1,0:T(8,128)S(1)} %get-tuple-element.42), channel_id=1, source_target_pairs={{0,1},{1,2},{2,3},{3,0},{4,5},{5,6},{6,7},{7,4},{8,9},{9,10},{10,1... | collective-permute-start | bytes 122888 | tf_op jit(solution)/shard_map/ppermute | solution.py:803
  45.2 4.0 %collective-permute-start.11 = (f32[10,8,128]{2,1,0:T(8,128)S(1)}, f32[10,8,128]{2,1,0:T(8,128)S(1)}, u32[]{:S(2)}, u32[]{:S(2)}) collective-permute-start(f32[10,8,128]{2,1,0:T(8,128)S(1)} %get-tuple-element.43), channel_id=1, source_target_pairs={{0,2},{1,3},{2,0},{3,1},{4,6},{5,7},{6,4},{7,5},{8,10},{9,11},{10,... | collective-permute-start | bytes 122888 | tf_op jit(solution)/shard_map/ppermute | solution.py:803
  45.9 3.3 %collective-permute-start.12 = (f32[10,8,128]{2,1,0:T(8,128)S(1)}, f32[10,8,128]{2,1,0:T(8,128)S(1)}, u32[]{:S(2)}, u32[]{:S(2)}) collective-permute-start(f32[10,8,128]{2,1,0:T(8,128)S(1)} %get-tuple-element.44), channel_id=1, source_target_pairs={{0,3},{1,0},{2,1},{3,2},{4,7},{5,4},{6,5},{7,6},{8,11},{9,8},{10,9... | collective-permute-start | bytes 122888 | tf_op jit(solution)/shard_map/ppermute | solution.py:803
  49.2 2.8 %copy-start.1 = (bf16[32,16,64]{2,1,0:T(8,128)(2,1)S(1)}, bf16[32,16,64]{2,1,0:T(8,128)(2,1)}, u32[]{:S(2)}) copy-start(bf16[32,16,64]{2,1,0:T(8,128)(2,1)} %refs_1_.1) | copy-start | bytes 196612
  49.2 2.8 %copy-start.4 = (bf16[256,64]{0,1:T(8,128)(2,1)S(1)}, bf16[256,64]{0,1:T(8,128)(2,1)}, u32[]{:S(2)}) copy-start(bf16[256,64]{0,1:T(8,128)(2,1)} %param.20) | copy-start | bytes 98308

commit v16 on v15

--- a/solution.py
+++ b/solution.py
@@ -105,6 +105,7 @@
     wf_ref,
     shard_ref,
     rows_ref,
+    left_ref,
     norm_ref,
     weights_ref,
     turn_ref,
@@ -156,6 +157,7 @@
         place_ref[:, s, :] = jnp.sum(res, axis=1)
     right = place_ref[...].reshape(fd // size * seqs, 128).astype(bf16)
     rows_ref[...] = shard_ref[: base + 2 * rows, :]
+    left_ref[...] = shard_ref[:base, :]
     shard_ref[base + 2 * rows :, :] = right
 
 
@@ -199,7 +201,8 @@
     mt_ref,
     oh_ref,
     ol_ref,
-    update_ref,
+    update0_ref,
+    update1_ref,
 ):
     nk = rk_ref.shape[0]
     width_d, pair_rows, _ = rab_ref.shape
@@ -273,7 +276,7 @@
                     ol_ref[group // wide, at, to] = low[cut]
         return carry
 
-    lax.fori_loop(0, width_d // many, outer_of, 0)
+    lax.fori_loop(0, width_d // many, outer_of, 0, unroll=2)
 
     ready()
     some = z // fc
@@ -300,14 +303,17 @@
         axis=1,
     ).astype(bf16)
 
-    def finish(n, carry):
+    def product(n):
         two = nn_dot(mt_ref[...], oh_ref[n])
-        update_ref[...] = two[:z] + two[z:] + nn_dot(mt_ref[:z, :], ol_ref[n])
+        update_refs[n % 2][...] = two[:z] + two[z:] + nn_dot(mt_ref[:z, :], ol_ref[n])
+
+    def finish(n):
         for e in range(wide):
             g = n * wide + e
-            at = pl.ds(pl.multiple_of(g * lanes, lanes), lanes)
+            at = slice(g * lanes, (g + 1) * lanes)
             before = pair_ref[at, :].T.astype(f32)
-            result = (before + update_ref[:, e * lanes : (e + 1) * lanes]).astype(bf16)
+            update = update_refs[n % 2][:, e * lanes : (e + 1) * lanes]
+            result = (before + update).astype(bf16)
             x = result.astype(f32)
             pout_ref[at, :] = result.T
             center = x - jnp.mean(x, axis=0, keepdims=True)
@@ -319,14 +325,21 @@
             scores = nn_dot(st, jnp.concatenate([high, low], axis=0))
             logits = scores[:heads] + scores[heads : 2 * heads] + scores[2 * heads : 3 * heads]
             logits_ref[g] = jnp.where(maskl, logits, far_below)
-        at = pl.ds(pl.multiple_of(n * wide * lanes, wide * lanes), wide * lanes)
-        pltpu.make_async_copy(pout_ref.at[at], pout_hbm.at[at], out_sem.at[n]).start()
-        return carry
-
-    lax.fori_loop(0, groups // wide, finish, 0)
-    for n in range(groups // wide):
+
+    steps = groups // wide
+    update_refs = (update0_ref, update1_ref)
+    product(0)
+    for n in range(1, steps):
+        product(n)
+        finish(n - 1)
+    finish(steps - 1)
+    copies = []
+    for n in range(steps):
         at = pl.ds(n * wide * lanes, wide * lanes)
-        pltpu.make_async_copy(pout_ref.at[at], pout_hbm.at[at], out_sem.at[n]).wait()
+        copies.append(pltpu.make_async_copy(pout_ref.at[at], pout_hbm.at[at], out_sem.at[n]))
+        copies[-1].start()
+    for copy in copies:
+        copy.wait()
 
 
 def by_heads(w, heads, out_ref):
@@ -673,11 +686,12 @@
     l_rows = tokens // pack * fc
     r_rows = fd * tokens // 128 * seqs
     n_rows = half * tokens
-    shard, rows, normed, weights = call(
+    shard, rows, own_left, normed, weights = call(
         prepare_kernel,
         (
             sds((l_rows + 2 * n_rows + r_rows, 128), bf16),
             sds((l_rows + 2 * n_rows, 128), bf16),
+            sds((l_rows, 128), bf16),
             sds((n_rows, 128), bf16),
             sds((width, 3 * chans), bf16),
         ),
@@ -714,19 +728,21 @@
         for flip in (0, 2)
     ]
 
-    across, *all_cols = lax.optimization_barrier((across, *all_cols))
-    all_rows = [rows, other, across, exchange(across, 1)]
-
     def over_seq(x):
         if nq == 2:
             return lax.ppermute(x, "seq", [(0, 1), (1, 0)])
         return lax.all_gather(x, "seq", axis=0, tiled=True)
 
-    (left,) = call(join_left_kernel, (sds((nk * l_rows, 128), bf16),), smem=1)(place[1], *all_rows)
+    lefts = [own_left, other, across, exchange(own_left, 3)]
+    (left,) = call(join_left_kernel, (sds((nk * l_rows, 128), bf16),), smem=1)(place[1], *lefts)
+    far_left = over_seq(left)
+    across, far_left, *all_cols = lax.optimization_barrier((across, far_left, *all_cols))
+    all_rows = [rows, other, across, exchange(across, 1)]
+
     (right,) = call(join_right_kernel, (sds((nk * r_rows, 128), bf16),), smem=1)(
         place[0], *all_cols
     )
-    far_left, far_right = over_seq(left), over_seq(right)
+    far_right = over_seq(right)
 
     head_lanes = seqs * chans // heads
     gw_own, block = call(
@@ -773,6 +789,7 @@
             pltpu.VMEM((groups // 4, fd * fc, 4 * lanes), bf16),
             pltpu.VMEM((groups // 4, fd * fc, 4 * lanes), bf16),
             pltpu.VMEM((z, 4 * lanes), f32),
+            pltpu.VMEM((z, 4 * lanes), f32),
         ),
         smem=2,
         flops=14_000_000_000,

time: 55.4 us -> 53.3 us (0.962)
  waiting for transfers between devices: 9.59 us -> 7.31 us
  Pallas kernels: 23.4 us -> 22.4 us
  local copies, waits for them, and re-layouts: 2.75 us -> 3.51 us
    ppermute x6 -> x7, waiting for transfers between devices: 8.62 us -> 1.93 us  [exchange(): return lax.ppermute(x, 'col', [(c, c ^ bit) for c in range(nk)])]
    ppermute x2, waiting for transfers between devices: 0.01 us -> 4.2 us  [over_seq(): return lax.ppermute(x, 'seq', [(0, 1), (1, 0)])]
    ppermute x6 -> x7, starting transfers between devices: 7.47 us -> 9.05 us  [exchange(): return lax.ppermute(x, 'col', [(c, c ^ bit) for c in range(nk)])]
    ppermute x2, starting transfers between devices: 4.68 us -> 3.3 us  [on_device(): lax.ppermute(pair, ('row', 'col'), [(r * nk + c, (c ^ flip) * nk + r) for...]
    pallas_call x9, Pallas kernels: 23.4 us -> 22.4 us  [run(): pl.pallas_call(body, out_shape=out_shape, in_specs=in_specs, out_specs=[p...]
    unnamed x22 -> x24, local copies, waits for them, and re-layouts: 1.85 us -> 2.61 us
  transfers between devices with their start and end apart: 14 -> 15, of which waited for: 4 -> 4; matrix products, arithmetic and copies ran while one was open for 2% -> 2% of each run, Pallas kernels for 28% -> 27%
where the time goes in v16:
time: 53.3 us; the launch traced here: 52.5 us
  Pallas kernels  22.4 us (42%)
  starting transfers between devices  18.4 us (35%)
  waiting for transfers between devices  7.31 us (14%)
  local copies, waits for them, and re-layouts  3.51 us (7%)
  between operations  0.83 us (2%)
    pallas_call x9, Pallas kernels, run(): pl.pallas_call(body, out_shape=out_shape, in_specs=in_specs, out_specs=[p...  22.4 us
    ppermute x7, starting transfers between devices, exchange(): return lax.ppermute(x, 'col', [(c, c ^ bit) for c in range(nk)])  9.05 us
    ppermute x2, waiting for transfers between devices, over_seq(): return lax.ppermute(x, 'seq', [(0, 1), (1, 0)])  4.2 us
    ppermute x2, starting transfers between devices, on_device(): lax.ppermute(pair, ('row', 'col'), [(r * nk + c, (c ^ flip) * nk + r) for...  3.3 us
    ppermute x2, starting transfers between devices, over_seq(): return lax.ppermute(x, 'seq', [(0, 1), (1, 0)])  3.11 us
    unnamed x24, local copies, waits for them, and re-layouts  2.61 us
    ppermute x7, waiting for transfers between devices, exchange(): return lax.ppermute(x, 'col', [(c, c ^ bit) for c in range(nk)])  1.93 us
    ppermute x3, starting transfers between devices, on_device(): lax.ppermute(pay, 'col', [(c, (c + shift) % nk) for c in range(nk)])  1.79 us
  transfers between devices with their start and end apart: 15, of which 4 were waited for; matrix products, arithmetic and copies ran while one was open for 2% of the time, Pallas kernels for 27%

profile of v16, /device:TPU:0, one launch (start us, length us, event | category | flops | bytes accessed | tf_op | source)
XLA Modules:
  0.0 52.5 jit_solution(4783605150194997752)
XLA Ops:
  0.6 2.9 %shard_map.130 = (bf16[768,128]{1,0:T(8,128)(2,1)}, bf16[640,128]{1,0:T(8,128)(2,1)}, bf16[128,128]{1,0:T(8,128)(2,1)}, bf16[256,128]{1,0:T(8,128)(2,1)}, bf16[64,768]{1,0:T(8,128)(2,1)}) custom-call(s32[1]{0:T(128)} %bitcast.2.refs_0_, bf16[32,16,64]{2,1,0:T(8,128)(2,1)} %refs_1_.1, bf16[32,16,64]{2,1,0:T(8,128)(2,1)} %refs_2_.1, bf16[32,64]{1,0:T(8,128)(2,1)} %bitcast.23, ...), custom_call_target="tpu_custom_call" | custom-call | tf_op jit(solution)/shard_map/pallas_call | solution.py:62
  3.6 0.5 collective-permute-start
  4.0 2.6 %collective-permute-start.1 = (bf16[640,128]{1,0:T(8,128)(2,1)}, bf16[640,128]{1,0:T(8,128)(2,1)S(1)}, u32[]{:S(2)}, u32[]{:S(2)}) collective-permute-start(bf16[640,128]{1,0:T(8,128)(2,1)} %get-tuple-element.33.refs_2_), channel_id=1, source_target_pairs={{0,2},{1,3},{2,0},{3,1},{4,6},{5,7},{6,4},{7,5},{8,10},{9,11},{10,... | collective-permute-start | bytes 491528 | tf_op jit(solution)/shard_map/ppermute | solution.py:717
  6.6 0.9 %slice.6 = bf16[384,128]{1,0:T(8,128)(2,1)S(1)} slice(bf16[768,128]{1,0:T(8,128)(2,1)} %get-tuple-element.34), slice={[384:768], [0:128]} | slice | bytes 196608 | tf_op jit(solution)/shard_map/slice | solution.py:721
  7.5 0.0 collective-permute-done.refs_2_.refs_3_
  7.5 2.6 %collective-permute-start.5 = (bf16[768,128]{1,0:T(8,128)(2,1)S(1)}, bf16[768,128]{1,0:T(8,128)(2,1)S(1)}, u32[]{:S(2)}, u32[]{:S(2)}) collective-permute-start(bf16[768,128]{1,0:T(8,128)(2,1)S(1)} %pad_maximum_fusion), channel_id=1, source_target_pairs={{0,8},{1,12},{2,0},{3,4},{4,9},{5,13},{6,1},{7,5},{8,10},{9,14},{1... | collective-permute-start | bytes 589832 | tf_op jit(solution)/shard_map/ppermute | solution.py:723
  10.2 0.7 %collective-permute-start.4 = (bf16[768,128]{1,0:T(8,128)(2,1)S(1)}, bf16[768,128]{1,0:T(8,128)(2,1)S(1)}, u32[]{:S(2)}, u32[]{:S(2)}) collective-permute-start(bf16[768,128]{1,0:T(8,128)(2,1)S(1)} %pad_maximum_fusion), channel_id=1, source_target_pairs={{0,0},{1,4},{2,8},{3,12},{4,1},{5,5},{6,9},{7,13},{8,2},{9,6},{10,... | collective-permute-start | bytes 589832 | tf_op jit(solution)/shard_map/ppermute | solution.py:723
  10.8 3.8 %collective-permute-start.2 = (bf16[128,128]{1,0:T(8,128)(2,1)}, bf16[128,128]{1,0:T(8,128)(2,1)S(1)}, u32[]{:S(2)}, u32[]{:S(2)}) collective-permute-start(bf16[128,128]{1,0:T(8,128)(2,1)} %get-tuple-element.35.refs_1_), channel_id=1, source_target_pairs={{0,3},{1,2},{2,1},{3,0},{4,7},{5,6},{6,5},{7,4},{8,11},{9,10},{10,... | collective-permute-start | bytes 98312 | tf_op jit(solution)/shard_map/ppermute | solution.py:717
  14.6 1.9 %collective-permute-done.2.refs_4_ = bf16[128,128]{1,0:T(8,128)(2,1)S(1)} collective-permute-done((bf16[128,128]{1,0:T(8,128)(2,1)}, bf16[128,128]{1,0:T(8,128)(2,1)S(1)}, u32[]{:S(2)}, u32[]{:S(2)}) %collective-permute-start.2) | collective-permute-done | bytes 32800 | tf_op jit(solution)/shard_map/ppermute | solution.py:717
  16.5 0.0 collective-permute-done.1.refs_3_.refs_4_
  16.6 0.0 copy-start.4
  16.6 0.8 %copy-done.4 = bf16[128,128]{1,0:T(8,128)(2,1)S(1)} copy-done((bf16[128,128]{1,0:T(8,128)(2,1)S(1)}, bf16[128,128]{1,0:T(8,128)(2,1)}, u32[]{:S(2)}) %copy-start.4) | copy-done | bytes 32792
  17.3 1.6 %collective-permute-start.3 = (bf16[512,128]{1,0:T(8,128)(2,1)S(1)}, bf16[512,128]{1,0:T(8,128)(2,1)S(1)}, u32[]{:S(2)}, u32[]{:S(2)}) collective-permute-start(bf16[512,128]{1,0:T(8,128)(2,1)S(1)} %shard_map.131.refs_2_), channel_id=1, source_target_pairs={{0,16},{16,0},{1,17},{17,1},{2,18},{18,2},{3,19},{19,3},{4,20},{20... | collective-permute-start | bytes 393224 | tf_op jit(solution)/shard_map/ppermute | solution.py:733
  18.9 4.2 %collective-permute-done.3.refs_4_ = bf16[512,128]{1,0:T(8,128)(2,1)S(1)} collective-permute-done((bf16[512,128]{1,0:T(8,128)(2,1)S(1)}, bf16[512,128]{1,0:T(8,128)(2,1)S(1)}, u32[]{:S(2)}, u32[]{:S(2)}) %collective-permute-start.3) | collective-permute-done | bytes 131104 | tf_op jit(solution)/shard_map/ppermute | solution.py:733
  23.1 0.0 collective-permute-done.5.refs_7_.refs_2_
  23.1 0.0 collective-permute-done.4.refs_6_.refs_1_
  23.1 0.0 collective-permute-start.6
  23.1 1.6 %collective-permute-start.9 = (bf16[512,128]{1,0:T(8,128)(2,1)S(1)}, bf16[512,128]{1,0:T(8,128)(2,1)S(1)}, u32[]{:S(2)}, u32[]{:S(2)}) collective-permute-start(bf16[512,128]{1,0:T(8,128)(2,1)S(1)} %shard_map.133.refs_3_), channel_id=1, source_target_pairs={{0,16},{16,0},{1,17},{17,1},{2,18},{18,2},{3,19},{19,3},{4,20},{20... | collective-permute-start | bytes 393224 | tf_op jit(solution)/shard_map/ppermute | solution.py:733
  24.7 0.0 collective-permute-done.6.refs_5_
  24.7 0.0 copy-start.8
  24.7 0.9 %copy-done.8 = bf16[640,128]{1,0:T(8,128)(2,1)S(1)} copy-done((bf16[640,128]{1,0:T(8,128)(2,1)S(1)}, bf16[640,128]{1,0:T(8,128)(2,1)}, u32[]{:S(2)}) %copy-start.8) | copy-done | bytes 163864
  25.6 0.0 copy-start.9
  25.6 0.9 %copy-done.9 = bf16[64,768]{1,0:T(8,128)(2,1)S(1)} copy-done((bf16[64,768]{1,0:T(8,128)(2,1)S(1)}, bf16[64,768]{1,0:T(8,128)(2,1)}, u32[]{:S(2)}) %copy-start.9) | copy-done | bytes 98328
  26.5 0.0 copy-start.5
  26.5 0.0 copy-start.6
  26.5 0.0 copy-start.7
  26.5 0.0 copy-start.11
  26.5 2.3 %shard_map.132 = (f32[16,8,256]{2,1,0:T(8,128)S(1)}, bf16[4,16,16,128]{3,2,1,0:T(8,128)(2,1)S(1)}) custom-call(s32[1]{0:T(128)} %bitcast.1.refs_0_, s32[1]{0:T(128)} %bitcast.refs_0_.refs_1_, bf16[640,128]{1,0:T(8,128)(2,1)S(1)} %copy-done.8, bf16[768,128]{1,0:T(8,128)(2,1)S(1)} %collective-permute-done.refs_2_.refs_3_, ...), custom_call_target="tpu_custom_call" | custom-call | flops 3000000000 | bytes 3000000 | tf_op jit(solution)/shard_map/pallas_call | solution.py:62
  28.8 1.9 %collective-permute-start.8 = (bf16[4,16,16,128]{3,2,1,0:T(8,128)(2,1)S(1)}, bf16[4,16,16,128]{3,2,1,0:T(8,128)(2,1)S(1)}, u32[]{:S(2)}, u32[]{:S(2)}) collective-permute-start(bf16[4,16,16,128]{3,2,1,0:T(8,128)(2,1)S(1)} %get-tuple-element.40.refs_1_), channel_id=1, source_target_pairs={{0,2},{1,3},{2,0},{3,1},{4,6},{5,7},{6,4},{7,5},{8,10},{9,11},{10,... | collective-permute-start | bytes 786440 | tf_op jit(solution)/shard_map/ppermute | solution.py:717
  30.7 0.0 collective-permute-start.7
  30.7 1.2 %collective-permute-start.10 = (f32[16,8,256]{2,1,0:T(8,128)S(1)}, f32[16,8,256]{2,1,0:T(8,128)S(1)}, u32[]{:S(2)}, u32[]{:S(2)}) collective-permute-start(f32[16,8,256]{2,1,0:T(8,128)S(1)} %get-tuple-element.43.refs_2_), channel_id=1, source_target_pairs={{0,16},{16,0},{1,17},{17,1},{2,18},{18,2},{3,19},{19,3},{4,20},{20... | collective-permute-start | bytes 393224 | tf_op jit(solution)/shard_map/ppermute | solution.py:768
  31.9 0.0 collective-permute-done.9.refs_5_
  31.9 0.0 copy-done.5
  31.9 0.0 copy-done.6
  31.9 0.0 copy-done.7
  31.9 0.0 copy-done.11
  31.9 0.0 copy-start.1
  32.0 0.0 copy-start.2
  32.0 0.0 copy-start.10
  32.0 10.1 %shard_map.134 = (bf16[4096,128]{1,0:T(8,128)(2,1)}, f32[16,128,256]{2,1,0:T(8,128)S(1)}, f32[16,8,256]{2,1,0:T(8,128)S(1)}, f32[16,8,256]{2,1,0:T(8,128)S(1)}) custom-call(s32[1]{0:T(128)} %bitcast.refs_0_.refs_1_, s32[1]{0:T(128)} %bitcast.7.refs_1_, bf16[512,128]{1,0:T(8,128)(2,1)S(1)} %shard_map.131.refs_2_, bf16[512,128]{1,0:T(8,128)(2,1)S(1)} %shard_map.133.refs_3_, ...), custom_call_target="tpu_custom_call" | custom-call | flops 14000000000 | bytes 5000000 | tf_op jit(solution)/shard_map/pallas_call | solution.py:62
  42.0 0.0 collective-permute-done.10.refs_3_
  42.0 0.5 shard_map.135
  42.5 0.0 collective-permute-done.8.refs_3_
  42.5 0.0 collective-permute-done.7.refs_2_
  42.5 0.3 collective-permute-start.14
  42.8 0.3 collective-permute-start.11
  43.1 0.3 collective-permute-start.12
  43.4 1.2 %collective-permute-start.13 = (f32[10,8,128]{2,1,0:T(8,128)S(1)}, f32[10,8,128]{2,1,0:T(8,128)S(1)}, u32[]{:S(2)}, u32[]{:S(2)}) collective-permute-start(f32[10,8,128]{2,1,0:T(8,128)S(1)} %get-tuple-element.48), channel_id=1, source_target_pairs={{0,3},{1,0},{2,1},{3,2},{4,7},{5,4},{6,5},{7,6},{8,11},{9,8},{10,9... | collective-permute-start | bytes 122888 | tf_op jit(solution)/shard_map/ppermute | solution.py:820
  44.6 0.0 collective-permute-done.14.refs_4_
  44.6 0.0 copy-done.1
  44.6 0.0 copy-done.2
  44.6 0.0 copy-done.10
  44.6 1.3 %shard_map.136 = (bf16[16,256,512]{2,1,0:T(8,128)(2,1)S(1)}, f32[512,256]{1,0:T(8,128)S(1)}) custom-call(s32[1]{0:T(128)} %bitcast.refs_0_.refs_1_, bf16[4,16,16,128]{3,2,1,0:T(8,128)(2,1)S(1)} %get-tuple-element.40.refs_1_, bf16[4,16,16,128]{3,2,1,0:T(8,128)(2,1)S(1)} %collective-permute-done.7.refs_2_, ...), custom_call_target="tpu_custom_call" | custom-call | flops 4000000000 | bytes 6000000 | tf_op jit(solution)/shard_map/pallas_call | solution.py:62
  45.9 0.3 collective-permute-done.11.refs_2_.refs_1_
  46.2 0.9 %collective-permute-done.12.refs_3_.refs_2_ = f32[10,8,128]{2,1,0:T(8,128)S(1)} collective-permute-done((f32[10,8,128]{2,1,0:T(8,128)S(1)}, f32[10,8,128]{2,1,0:T(8,128)S(1)}, u32[]{:S(2)}, u32[]{:S(2)}) %collective-permute-start.12) | collective-permute-done | bytes 40992 | tf_op jit(solution)/shard_map/ppermute | solution.py:820
  47.1 0.0 collective-permute-done.13.refs_4_.refs_3_
  47.1 0.0 copy-start
  47.1 0.0 copy-start.3
  47.1 2.8 %shard_map.138 = bf16[4096,128]{1,0:T(8,128)(2,1)} custom-call(f32[10,8,128]{2,1,0:T(8,128)S(1)} %get-tuple-element.45.refs_1_.refs_0_, f32[10,8,128]{2,1,0:T(8,128)S(1)} %collective-permute-done.11.refs_2_.refs_1_, f32[10,8,128]{2,1,0:T(8,128)S(1)} %collective-permute-done.12.refs_3_.refs_2_, f32[10,8,128]{2,1,0:T(8,128)S(1)} %collective-permute-done.13.refs_4_.refs_3_, ...), custom_call_target="tpu_custom_call" | custom-call | flops 4000000000 | bytes 3000000 | tf_op jit(solution)/shard_map/pallas_call | solution.py:62
  49.9 0.0 copy-done
  49.9 0.0 copy-done.3
  49.9 2.6 %shard_map.137 = bf16[512,64]{1,0:T(8,128)(2,1)} custom-call(s32[1]{0:T(128)} %bitcast.refs_0_.refs_1_, f32[10,8,128]{2,1,0:T(8,128)S(1)} %get-tuple-element.45.refs_1_.refs_0_, f32[10,8,128]{2,1,0:T(8,128)S(1)} %collective-permute-done.11.refs_2_.refs_1_, f32[10,8,128]{2,1,0:T(8,128)S(1)} %collective-permute-done.12.refs_3_.refs_2_, ...), custom_call_target="tpu_custom_call" | custom-call | flops 3000000000 | bytes 5000000 | tf_op jit(solution)/shard_map/pallas_call | solution.py:62
  (4 shorter events, 0.0 us)
Async XLA Ops:
  3.6 3.9 %collective-permute-start = (bf16[768,128]{1,0:T(8,128)(2,1)}, bf16[768,128]{1,0:T(8,128)(2,1)S(1)}, u32[]{:S(2)}, u32[]{:S(2)}) collective-permute-start(bf16[768,128]{1,0:T(8,128)(2,1)} %get-tuple-element.34), channel_id=1, source_target_pairs={{0,1},{1,0},{2,3},{3,2},{4,5},{5,4},{6,7},{7,6},{8,9},{9,8},{10,11... | collective-permute-start | bytes 589832 | tf_op jit(solution)/shard_map/ppermute | solution.py:717
  4.0 12.5 %collective-permute-start.1 = (bf16[640,128]{1,0:T(8,128)(2,1)}, bf16[640,128]{1,0:T(8,128)(2,1)S(1)}, u32[]{:S(2)}, u32[]{:S(2)}) collective-permute-start(bf16[640,128]{1,0:T(8,128)(2,1)} %get-tuple-element.33.refs_2_), channel_id=1, source_target_pairs={{0,2},{1,3},{2,0},{3,1},{4,6},{5,7},{6,4},{7,5},{8,10},{9,11},{10,... | collective-permute-start | bytes 491528 | tf_op jit(solution)/shard_map/ppermute | solution.py:717
  7.5 15.6 %collective-permute-start.5 = (bf16[768,128]{1,0:T(8,128)(2,1)S(1)}, bf16[768,128]{1,0:T(8,128)(2,1)S(1)}, u32[]{:S(2)}, u32[]{:S(2)}) collective-permute-start(bf16[768,128]{1,0:T(8,128)(2,1)S(1)} %pad_maximum_fusion), channel_id=1, source_target_pairs={{0,8},{1,12},{2,0},{3,4},{4,9},{5,13},{6,1},{7,5},{8,10},{9,14},{1... | collective-permute-start | bytes 589832 | tf_op jit(solution)/shard_map/ppermute | solution.py:723
  10.2 12.9 %collective-permute-start.4 = (bf16[768,128]{1,0:T(8,128)(2,1)S(1)}, bf16[768,128]{1,0:T(8,128)(2,1)S(1)}, u32[]{:S(2)}, u32[]{:S(2)}) collective-permute-start(bf16[768,128]{1,0:T(8,128)(2,1)S(1)} %pad_maximum_fusion), channel_id=1, source_target_pairs={{0,0},{1,4},{2,8},{3,12},{4,1},{5,5},{6,9},{7,13},{8,2},{9,6},{10,... | collective-permute-start | bytes 589832 | tf_op jit(solution)/shard_map/ppermute | solution.py:723
  10.8 5.7 %collective-permute-start.2 = (bf16[128,128]{1,0:T(8,128)(2,1)}, bf16[128,128]{1,0:T(8,128)(2,1)S(1)}, u32[]{:S(2)}, u32[]{:S(2)}) collective-permute-start(bf16[128,128]{1,0:T(8,128)(2,1)} %get-tuple-element.35.refs_1_), channel_id=1, source_target_pairs={{0,3},{1,2},{2,1},{3,0},{4,7},{5,6},{6,5},{7,4},{8,11},{9,10},{10,... | collective-permute-start | bytes 98312 | tf_op jit(solution)/shard_map/ppermute | solution.py:717
  16.6 0.8 %copy-start.4 = (bf16[128,128]{1,0:T(8,128)(2,1)S(1)}, bf16[128,128]{1,0:T(8,128)(2,1)}, u32[]{:S(2)}) copy-start(bf16[128,128]{1,0:T(8,128)(2,1)} %get-tuple-element.35.refs_1_) | copy-start | bytes 98308
  17.3 5.8 %collective-permute-start.3 = (bf16[512,128]{1,0:T(8,128)(2,1)S(1)}, bf16[512,128]{1,0:T(8,128)(2,1)S(1)}, u32[]{:S(2)}, u32[]{:S(2)}) collective-permute-start(bf16[512,128]{1,0:T(8,128)(2,1)S(1)} %shard_map.131.refs_2_), channel_id=1, source_target_pairs={{0,16},{16,0},{1,17},{17,1},{2,18},{18,2},{3,19},{19,3},{4,20},{20... | collective-permute-start | bytes 393224 | tf_op jit(solution)/shard_map/ppermute | solution.py:733
  23.1 1.6 %collective-permute-start.6 = (bf16[640,128]{1,0:T(8,128)(2,1)S(1)}, bf16[640,128]{1,0:T(8,128)(2,1)S(1)}, u32[]{:S(2)}, u32[]{:S(2)}) collective-permute-start(bf16[640,128]{1,0:T(8,128)(2,1)S(1)} %collective-permute-done.1.refs_3_.refs_4_), channel_id=1, source_target_pairs={{0,1},{1,0},{2,3},{3,2},{4,5},{5,4},{6,7},{7,6},{8,9},{9,8},{10,11... | collective-permute-start | bytes 491528 | tf_op jit(solution)/shard_map/ppermute | solution.py:717
  23.1 8.8 %collective-permute-start.9 = (bf16[512,128]{1,0:T(8,128)(2,1)S(1)}, bf16[512,128]{1,0:T(8,128)(2,1)S(1)}, u32[]{:S(2)}, u32[]{:S(2)}) collective-permute-start(bf16[512,128]{1,0:T(8,128)(2,1)S(1)} %shard_map.133.refs_3_), channel_id=1, source_target_pairs={{0,16},{16,0},{1,17},{17,1},{2,18},{18,2},{3,19},{19,3},{4,20},{20... | collective-permute-start | bytes 393224 | tf_op jit(solution)/shard_map/ppermute | solution.py:733
  24.7 0.9 %copy-start.8 = (bf16[640,128]{1,0:T(8,128)(2,1)S(1)}, bf16[640,128]{1,0:T(8,128)(2,1)}, u32[]{:S(2)}) copy-start(bf16[640,128]{1,0:T(8,128)(2,1)} %get-tuple-element.33.refs_2_) | copy-start | bytes 491524
  25.6 0.9 %copy-start.9 = (bf16[64,768]{1,0:T(8,128)(2,1)S(1)}, bf16[64,768]{1,0:T(8,128)(2,1)}, u32[]{:S(2)}) copy-start(bf16[64,768]{1,0:T(8,128)(2,1)} %get-tuple-element.39.refs_8_) | copy-start | bytes 294916
  26.5 5.4 %copy-start.5 = (s32[256]{0:T(256)S(1)}, s32[256]{0:T(256)}, u32[]{:S(2)}) copy-start(s32[256]{0:T(256)} %param.13) | copy-start | bytes 3076
  26.5 5.4 %copy-start.6 = (bf16[64,64,128]{2,1,0:T(8,128)(2,1)S(1)}, bf16[64,64,128]{2,1,0:T(8,128)(2,1)}, u32[]{:S(2)}) copy-start(bf16[64,64,128]{2,1,0:T(8,128)(2,1)} %param.12) | copy-start | bytes 3145732
  26.5 5.4 %copy-start.7 = (f32[1024,128]{1,0:T(8,128)S(1)}, f32[1024,128]{1,0:T(8,128)}, u32[]{:S(2)}) copy-start(f32[1024,128]{1,0:T(8,128)} %refs_7_.4) | copy-start | bytes 1572868
  26.5 5.4 %copy-start.11 = (f32[128,8]{0,1:T(8,128)S(1)}, f32[128,8]{0,1:T(8,128)}, u32[]{:S(2)}) copy-start(f32[128,8]{0,1:T(8,128)} %param.19) | copy-start | bytes 12292
  28.8 13.7 %collective-permute-start.8 = (bf16[4,16,16,128]{3,2,1,0:T(8,128)(2,1)S(1)}, bf16[4,16,16,128]{3,2,1,0:T(8,128)(2,1)S(1)}, u32[]{:S(2)}, u32[]{:S(2)}) collective-permute-start(bf16[4,16,16,128]{3,2,1,0:T(8,128)(2,1)S(1)} %get-tuple-element.40.refs_1_), channel_id=1, source_target_pairs={{0,2},{1,3},{2,0},{3,1},{4,6},{5,7},{6,4},{7,5},{8,10},{9,11},{10,... | collective-permute-start | bytes 786440 | tf_op jit(solution)/shard_map/ppermute | solution.py:717
  30.7 11.8 %collective-permute-start.7 = (bf16[4,16,16,128]{3,2,1,0:T(8,128)(2,1)S(1)}, bf16[4,16,16,128]{3,2,1,0:T(8,128)(2,1)S(1)}, u32[]{:S(2)}, u32[]{:S(2)}) collective-permute-start(bf16[4,16,16,128]{3,2,1,0:T(8,128)(2,1)S(1)} %get-tuple-element.40.refs_1_), channel_id=1, source_target_pairs={{0,1},{1,0},{2,3},{3,2},{4,5},{5,4},{6,7},{7,6},{8,9},{9,8},{10,11... | collective-permute-start | bytes 786440 | tf_op jit(solution)/shard_map/ppermute | solution.py:717
  30.7 11.3 %collective-permute-start.10 = (f32[16,8,256]{2,1,0:T(8,128)S(1)}, f32[16,8,256]{2,1,0:T(8,128)S(1)}, u32[]{:S(2)}, u32[]{:S(2)}) collective-permute-start(f32[16,8,256]{2,1,0:T(8,128)S(1)} %get-tuple-element.43.refs_2_), channel_id=1, source_target_pairs={{0,16},{16,0},{1,17},{17,1},{2,18},{18,2},{3,19},{19,3},{4,20},{20... | collective-permute-start | bytes 393224 | tf_op jit(solution)/shard_map/ppermute | solution.py:768
  31.9 12.6 %copy-start.1 = (bf16[64,256]{1,0:T(8,128)(2,1)S(1)}, bf16[64,256]{1,0:T(8,128)(2,1)}, u32[]{:S(2)}) copy-start(bf16[64,256]{1,0:T(8,128)(2,1)} %refs_5_.1) | copy-start | bytes 98308
  32.0 12.6 %copy-start.2 = (bf16[64,256]{1,0:T(8,128)(2,1)S(1)}, bf16[64,256]{1,0:T(8,128)(2,1)}, u32[]{:S(2)}) copy-start(bf16[64,256]{1,0:T(8,128)(2,1)} %refs_7_.5) | copy-start | bytes 98308
  32.0 12.6 %copy-start.10 = (bf16[256,128]{1,0:T(8,128)(2,1)S(1)}, bf16[256,128]{1,0:T(8,128)(2,1)}, u32[]{:S(2)}) copy-start(bf16[256,128]{1,0:T(8,128)(2,1)} %get-tuple-element.51.refs_6_) | copy-start | bytes 196612
  42.5 2.1 %collective-permute-start.14 = (bf16[4,16,16,128]{3,2,1,0:T(8,128)(2,1)S(1)}, bf16[4,16,16,128]{3,2,1,0:T(8,128)(2,1)S(1)}, u32[]{:S(2)}, u32[]{:S(2)}) collective-permute-start(bf16[4,16,16,128]{3,2,1,0:T(8,128)(2,1)S(1)} %collective-permute-done.8.refs_3_), channel_id=1, source_target_pairs={{0,1},{1,0},{2,3},{3,2},{4,5},{5,4},{6,7},{7,6},{8,9},{9,8},{10,11... | collective-permute-start | bytes 786440 | tf_op jit(solution)/shard_map/ppermute | solution.py:717
  42.8 3.4 %collective-permute-start.11 = (f32[10,8,128]{2,1,0:T(8,128)S(1)}, f32[10,8,128]{2,1,0:T(8,128)S(1)}, u32[]{:S(2)}, u32[]{:S(2)}) collective-permute-start(f32[10,8,128]{2,1,0:T(8,128)S(1)} %get-tuple-element.46), channel_id=1, source_target_pairs={{0,1},{1,2},{2,3},{3,0},{4,5},{5,6},{6,7},{7,4},{8,9},{9,10},{10,1... | collective-permute-start | bytes 122888 | tf_op jit(solution)/shard_map/ppermute | solution.py:820
  43.1 4.0 %collective-permute-start.12 = (f32[10,8,128]{2,1,0:T(8,128)S(1)}, f32[10,8,128]{2,1,0:T(8,128)S(1)}, u32[]{:S(2)}, u32[]{:S(2)}) collective-permute-start(f32[10,8,128]{2,1,0:T(8,128)S(1)} %get-tuple-element.47), channel_id=1, source_target_pairs={{0,2},{1,3},{2,0},{3,1},{4,6},{5,7},{6,4},{7,5},{8,10},{9,11},{10,... | collective-permute-start | bytes 122888 | tf_op jit(solution)/shard_map/ppermute | solution.py:820
  43.4 3.7 %collective-permute-start.13 = (f32[10,8,128]{2,1,0:T(8,128)S(1)}, f32[10,8,128]{2,1,0:T(8,128)S(1)}, u32[]{:S(2)}, u32[]{:S(2)}) collective-permute-start(f32[10,8,128]{2,1,0:T(8,128)S(1)} %get-tuple-element.48), channel_id=1, source_target_pairs={{0,3},{1,0},{2,1},{3,2},{4,7},{5,4},{6,5},{7,6},{8,11},{9,8},{10,9... | collective-permute-start | bytes 122888 | tf_op jit(solution)/shard_map/ppermute | solution.py:820
  47.1 2.8 %copy-start = (bf16[32,16,64]{2,1,0:T(8,128)(2,1)S(1)}, bf16[32,16,64]{2,1,0:T(8,128)(2,1)}, u32[]{:S(2)}) copy-start(bf16[32,16,64]{2,1,0:T(8,128)(2,1)} %refs_1_.1) | copy-start | bytes 196612
  47.1 2.8 %copy-start.3 = (bf16[256,64]{0,1:T(8,128)(2,1)S(1)}, bf16[256,64]{0,1:T(8,128)(2,1)}, u32[]{:S(2)}) copy-start(bf16[256,64]{0,1:T(8,128)(2,1)} %param.20) | copy-start | bytes 98308

commit v17 on v16

--- a/solution.py
+++ b/solution.py
@@ -328,16 +328,16 @@
 
     steps = groups // wide
     update_refs = (update0_ref, update1_ref)
-    product(0)
-    for n in range(1, steps):
-        product(n)
-        finish(n - 1)
-    finish(steps - 1)
     copies = []
-    for n in range(steps):
-        at = pl.ds(n * wide * lanes, wide * lanes)
-        copies.append(pltpu.make_async_copy(pout_ref.at[at], pout_hbm.at[at], out_sem.at[n]))
-        copies[-1].start()
+    for n in range(steps + 1):
+        if n < steps:
+            product(n)
+        if n > 0:
+            finish(n - 1)
+            at = pl.ds((n - 1) * wide * lanes, wide * lanes)
+            part = pltpu.make_async_copy(pout_ref.at[at], pout_hbm.at[at], out_sem.at[n - 1])
+            part.start()
+            copies.append(part)
     for copy in copies:
         copy.wait()
 
@@ -536,7 +536,7 @@
     low = lax.broadcasted_iota(jnp.int32, (heads, 2 * tile), 1) < tile
 
     def one(g):
-        st = stat_ref[pl.ds(pl.multiple_of(g * heads, heads), heads), :]
+        st = stat_ref[g * heads : (g + 1) * heads, :]
 
         def spread(base):
             halves = [
@@ -561,21 +561,20 @@
         centered = grad - jnp.mean(grad, axis=0, keepdims=True)
         along = jnp.mean(grad * normal, axis=0, keepdims=True)
         result = inverse * (centered - normal * along)
-        out_ref[pl.ds(pl.multiple_of(g * lanes, lanes), lanes), :] = result.astype(bf16).T
+        out_ref[g * lanes : (g + 1) * lanes, :] = result.astype(bf16).T
 
     many = 4
 
-    def some(n, carry):
+    copies = []
+    for n in range(groups // many):
         for e in range(many):
             one(n * many + e)
-        at = pl.ds(pl.multiple_of(n * many * lanes, many * lanes), many * lanes)
-        pltpu.make_async_copy(out_ref.at[at], out_hbm.at[at], out_sem.at[n]).start()
-        return carry
-
-    lax.fori_loop(0, groups // many, some, 0)
-    for n in range(groups // many):
         at = pl.ds(n * many * lanes, many * lanes)
-        pltpu.make_async_copy(out_ref.at[at], out_hbm.at[at], out_sem.at[n]).wait()
+        part = pltpu.make_async_copy(out_ref.at[at], out_hbm.at[at], out_sem.at[n])
+        part.start()
+        copies.append(part)
+    for copy in copies:
+        copy.wait()
 
 
 def alignment_kernel(
@@ -645,7 +644,7 @@
             gated_ref[at, :] = (gate_ref[at, :] * mean).astype(bf16)
         return carry
 
-    lax.fori_loop(0, half, one, 0, unroll=4)
+    lax.fori_loop(0, half, one, 0, unroll=8)
     out_ref[...] = (x_ref[...].astype(f32) + nt_dot(gated_ref[...], wf_ref[...])).astype(bf16)
 
 

time: 53.3 us -> 52.6 us (0.987)
  Pallas kernels: 22.4 us -> 21.7 us
    pallas_call x9, Pallas kernels: 22.4 us -> 21.7 us  [run(): pl.pallas_call(body, out_shape=out_shape, in_specs=in_specs, out_specs=[p...]
where the time goes in v17:
time: 52.6 us; the launch traced here: 51.8 us
  Pallas kernels  21.7 us (41%)
  starting transfers between devices  18.4 us (35%)
  waiting for transfers between devices  7.31 us (14%)
  local copies, waits for them, and re-layouts  3.51 us (7%)
  between operations  0.83 us (2%)
    pallas_call x9, Pallas kernels, run(): pl.pallas_call(body, out_shape=out_shape, in_specs=in_specs, out_specs=[p...  21.7 us
    ppermute x7, starting transfers between devices, exchange(): return lax.ppermute(x, 'col', [(c, c ^ bit) for c in range(nk)])  9.05 us
    ppermute x2, waiting for transfers between devices, over_seq(): return lax.ppermute(x, 'seq', [(0, 1), (1, 0)])  4.2 us
    ppermute x2, starting transfers between devices, on_device(): lax.ppermute(pair, ('row', 'col'), [(r * nk + c, (c ^ flip) * nk + r) for...  3.3 us
    ppermute x2, starting transfers between devices, over_seq(): return lax.ppermute(x, 'seq', [(0, 1), (1, 0)])  3.11 us
    unnamed x24, local copies, waits for them, and re-layouts  2.61 us
    ppermute x7, waiting for transfers between devices, exchange(): return lax.ppermute(x, 'col', [(c, c ^ bit) for c in range(nk)])  1.93 us
    ppermute x3, starting transfers between devices, on_device(): lax.ppermute(pay, 'col', [(c, (c + shift) % nk) for c in range(nk)])  1.79 us
  transfers between devices with their start and end apart: 15, of which 4 were waited for; matrix products, arithmetic and copies ran while one was open for 2% of the time, Pallas kernels for 27%

profile of v17, /device:TPU:0, one launch (start us, length us, event | category | flops | bytes accessed | tf_op | source)
XLA Modules:
  0.0 51.8 jit_solution(2955232868669841707)
XLA Ops:
  0.6 2.9 %shard_map.130 = (bf16[768,128]{1,0:T(8,128)(2,1)}, bf16[640,128]{1,0:T(8,128)(2,1)}, bf16[128,128]{1,0:T(8,128)(2,1)}, bf16[256,128]{1,0:T(8,128)(2,1)}, bf16[64,768]{1,0:T(8,128)(2,1)}) custom-call(s32[1]{0:T(128)} %bitcast.2.refs_0_, bf16[32,16,64]{2,1,0:T(8,128)(2,1)} %refs_1_.1, bf16[32,16,64]{2,1,0:T(8,128)(2,1)} %refs_2_.1, bf16[32,64]{1,0:T(8,128)(2,1)} %bitcast.23, ...), custom_call_target="tpu_custom_call" | custom-call | tf_op jit(solution)/shard_map/pallas_call | solution.py:62
  3.6 0.5 collective-permute-start
  4.0 2.6 %collective-permute-start.1 = (bf16[640,128]{1,0:T(8,128)(2,1)}, bf16[640,128]{1,0:T(8,128)(2,1)S(1)}, u32[]{:S(2)}, u32[]{:S(2)}) collective-permute-start(bf16[640,128]{1,0:T(8,128)(2,1)} %get-tuple-element.33.refs_2_), channel_id=1, source_target_pairs={{0,2},{1,3},{2,0},{3,1},{4,6},{5,7},{6,4},{7,5},{8,10},{9,11},{10,... | collective-permute-start | bytes 491528 | tf_op jit(solution)/shard_map/ppermute | solution.py:716
  6.6 0.9 %slice.6 = bf16[384,128]{1,0:T(8,128)(2,1)S(1)} slice(bf16[768,128]{1,0:T(8,128)(2,1)} %get-tuple-element.34), slice={[384:768], [0:128]} | slice | bytes 196608 | tf_op jit(solution)/shard_map/slice | solution.py:720
  7.5 0.0 collective-permute-done.refs_2_.refs_3_
  7.5 2.6 %collective-permute-start.5 = (bf16[768,128]{1,0:T(8,128)(2,1)S(1)}, bf16[768,128]{1,0:T(8,128)(2,1)S(1)}, u32[]{:S(2)}, u32[]{:S(2)}) collective-permute-start(bf16[768,128]{1,0:T(8,128)(2,1)S(1)} %pad_maximum_fusion), channel_id=1, source_target_pairs={{0,8},{1,12},{2,0},{3,4},{4,9},{5,13},{6,1},{7,5},{8,10},{9,14},{1... | collective-permute-start | bytes 589832 | tf_op jit(solution)/shard_map/ppermute | solution.py:722
  10.2 0.7 %collective-permute-start.4 = (bf16[768,128]{1,0:T(8,128)(2,1)S(1)}, bf16[768,128]{1,0:T(8,128)(2,1)S(1)}, u32[]{:S(2)}, u32[]{:S(2)}) collective-permute-start(bf16[768,128]{1,0:T(8,128)(2,1)S(1)} %pad_maximum_fusion), channel_id=1, source_target_pairs={{0,0},{1,4},{2,8},{3,12},{4,1},{5,5},{6,9},{7,13},{8,2},{9,6},{10,... | collective-permute-start | bytes 589832 | tf_op jit(solution)/shard_map/ppermute | solution.py:722
  10.8 3.8 %collective-permute-start.2 = (bf16[128,128]{1,0:T(8,128)(2,1)}, bf16[128,128]{1,0:T(8,128)(2,1)S(1)}, u32[]{:S(2)}, u32[]{:S(2)}) collective-permute-start(bf16[128,128]{1,0:T(8,128)(2,1)} %get-tuple-element.35.refs_1_), channel_id=1, source_target_pairs={{0,3},{1,2},{2,1},{3,0},{4,7},{5,6},{6,5},{7,4},{8,11},{9,10},{10,... | collective-permute-start | bytes 98312 | tf_op jit(solution)/shard_map/ppermute | solution.py:716
  14.6 1.9 %collective-permute-done.2.refs_4_ = bf16[128,128]{1,0:T(8,128)(2,1)S(1)} collective-permute-done((bf16[128,128]{1,0:T(8,128)(2,1)}, bf16[128,128]{1,0:T(8,128)(2,1)S(1)}, u32[]{:S(2)}, u32[]{:S(2)}) %collective-permute-start.2) | collective-permute-done | bytes 32800 | tf_op jit(solution)/shard_map/ppermute | solution.py:716
  16.5 0.0 collective-permute-done.1.refs_3_.refs_4_
  16.6 0.0 copy-start.4
  16.6 0.8 %copy-done.4 = bf16[128,128]{1,0:T(8,128)(2,1)S(1)} copy-done((bf16[128,128]{1,0:T(8,128)(2,1)S(1)}, bf16[128,128]{1,0:T(8,128)(2,1)}, u32[]{:S(2)}) %copy-start.4) | copy-done | bytes 32792
  17.3 1.6 %collective-permute-start.3 = (bf16[512,128]{1,0:T(8,128)(2,1)S(1)}, bf16[512,128]{1,0:T(8,128)(2,1)S(1)}, u32[]{:S(2)}, u32[]{:S(2)}) collective-permute-start(bf16[512,128]{1,0:T(8,128)(2,1)S(1)} %shard_map.131.refs_2_), channel_id=1, source_target_pairs={{0,16},{16,0},{1,17},{17,1},{2,18},{18,2},{3,19},{19,3},{4,20},{20... | collective-permute-start | bytes 393224 | tf_op jit(solution)/shard_map/ppermute | solution.py:732
  18.9 4.2 %collective-permute-done.3.refs_4_ = bf16[512,128]{1,0:T(8,128)(2,1)S(1)} collective-permute-done((bf16[512,128]{1,0:T(8,128)(2,1)S(1)}, bf16[512,128]{1,0:T(8,128)(2,1)S(1)}, u32[]{:S(2)}, u32[]{:S(2)}) %collective-permute-start.3) | collective-permute-done | bytes 131104 | tf_op jit(solution)/shard_map/ppermute | solution.py:732
  23.1 0.0 collective-permute-done.5.refs_7_.refs_2_
  23.1 0.0 collective-permute-done.4.refs_6_.refs_1_
  23.1 0.0 collective-permute-start.6
  23.1 1.6 %collective-permute-start.9 = (bf16[512,128]{1,0:T(8,128)(2,1)S(1)}, bf16[512,128]{1,0:T(8,128)(2,1)S(1)}, u32[]{:S(2)}, u32[]{:S(2)}) collective-permute-start(bf16[512,128]{1,0:T(8,128)(2,1)S(1)} %shard_map.133.refs_3_), channel_id=1, source_target_pairs={{0,16},{16,0},{1,17},{17,1},{2,18},{18,2},{3,19},{19,3},{4,20},{20... | collective-permute-start | bytes 393224 | tf_op jit(solution)/shard_map/ppermute | solution.py:732
  24.7 0.0 collective-permute-done.6.refs_5_
  24.7 0.0 copy-start.8
  24.7 0.9 %copy-done.8 = bf16[640,128]{1,0:T(8,128)(2,1)S(1)} copy-done((bf16[640,128]{1,0:T(8,128)(2,1)S(1)}, bf16[640,128]{1,0:T(8,128)(2,1)}, u32[]{:S(2)}) %copy-start.8) | copy-done | bytes 163864
  25.6 0.0 copy-start.9
  25.6 0.9 %copy-done.9 = bf16[64,768]{1,0:T(8,128)(2,1)S(1)} copy-done((bf16[64,768]{1,0:T(8,128)(2,1)S(1)}, bf16[64,768]{1,0:T(8,128)(2,1)}, u32[]{:S(2)}) %copy-start.9) | copy-done | bytes 98328
  26.5 0.0 copy-start.5
  26.5 0.0 copy-start.6
  26.5 0.0 copy-start.7
  26.5 0.0 copy-start.11
  26.5 2.3 %shard_map.132 = (f32[16,8,256]{2,1,0:T(8,128)S(1)}, bf16[4,16,16,128]{3,2,1,0:T(8,128)(2,1)S(1)}) custom-call(s32[1]{0:T(128)} %bitcast.1.refs_0_, s32[1]{0:T(128)} %bitcast.refs_0_.refs_1_, bf16[640,128]{1,0:T(8,128)(2,1)S(1)} %copy-done.8, bf16[768,128]{1,0:T(8,128)(2,1)S(1)} %collective-permute-done.refs_2_.refs_3_, ...), custom_call_target="tpu_custom_call" | custom-call | flops 3000000000 | bytes 3000000 | tf_op jit(solution)/shard_map/pallas_call | solution.py:62
  28.8 1.9 %collective-permute-start.8 = (bf16[4,16,16,128]{3,2,1,0:T(8,128)(2,1)S(1)}, bf16[4,16,16,128]{3,2,1,0:T(8,128)(2,1)S(1)}, u32[]{:S(2)}, u32[]{:S(2)}) collective-permute-start(bf16[4,16,16,128]{3,2,1,0:T(8,128)(2,1)S(1)} %get-tuple-element.40.refs_1_), channel_id=1, source_target_pairs={{0,2},{1,3},{2,0},{3,1},{4,6},{5,7},{6,4},{7,5},{8,10},{9,11},{10,... | collective-permute-start | bytes 786440 | tf_op jit(solution)/shard_map/ppermute | solution.py:716
  30.7 0.0 collective-permute-start.7
  30.7 1.2 %collective-permute-start.10 = (f32[16,8,256]{2,1,0:T(8,128)S(1)}, f32[16,8,256]{2,1,0:T(8,128)S(1)}, u32[]{:S(2)}, u32[]{:S(2)}) collective-permute-start(f32[16,8,256]{2,1,0:T(8,128)S(1)} %get-tuple-element.43.refs_2_), channel_id=1, source_target_pairs={{0,16},{16,0},{1,17},{17,1},{2,18},{18,2},{3,19},{19,3},{4,20},{20... | collective-permute-start | bytes 393224 | tf_op jit(solution)/shard_map/ppermute | solution.py:767
  31.9 0.0 collective-permute-done.9.refs_5_
  31.9 0.0 copy-done.5
  31.9 0.0 copy-done.6
  31.9 0.0 copy-done.7
  31.9 0.0 copy-done.11
  31.9 0.0 copy-start.1
  32.0 0.0 copy-start.2
  32.0 0.0 copy-start.10
  32.0 9.9 %shard_map.134 = (bf16[4096,128]{1,0:T(8,128)(2,1)}, f32[16,128,256]{2,1,0:T(8,128)S(1)}, f32[16,8,256]{2,1,0:T(8,128)S(1)}, f32[16,8,256]{2,1,0:T(8,128)S(1)}) custom-call(s32[1]{0:T(128)} %bitcast.refs_0_.refs_1_, s32[1]{0:T(128)} %bitcast.7.refs_1_, bf16[512,128]{1,0:T(8,128)(2,1)S(1)} %shard_map.131.refs_2_, bf16[512,128]{1,0:T(8,128)(2,1)S(1)} %shard_map.133.refs_3_, ...), custom_call_target="tpu_custom_call" | custom-call | flops 14000000000 | bytes 5000000 | tf_op jit(solution)/shard_map/pallas_call | solution.py:62
  41.8 0.0 collective-permute-done.10.refs_3_
  41.8 0.5 shard_map.135
  42.3 0.0 collective-permute-done.8.refs_3_
  42.3 0.0 collective-permute-done.7.refs_2_
  42.3 0.3 collective-permute-start.14
  42.6 0.3 collective-permute-start.11
  42.9 0.3 collective-permute-start.12
  43.2 1.2 %collective-permute-start.13 = (f32[10,8,128]{2,1,0:T(8,128)S(1)}, f32[10,8,128]{2,1,0:T(8,128)S(1)}, u32[]{:S(2)}, u32[]{:S(2)}) collective-permute-start(f32[10,8,128]{2,1,0:T(8,128)S(1)} %get-tuple-element.48), channel_id=1, source_target_pairs={{0,3},{1,0},{2,1},{3,2},{4,7},{5,4},{6,5},{7,6},{8,11},{9,8},{10,9... | collective-permute-start | bytes 122888 | tf_op jit(solution)/shard_map/ppermute | solution.py:819
  44.4 0.0 collective-permute-done.14.refs_4_
  44.4 0.0 copy-done.1
  44.4 0.0 copy-done.2
  44.4 0.0 copy-done.10
  44.4 1.3 %shard_map.136 = (bf16[16,256,512]{2,1,0:T(8,128)(2,1)S(1)}, f32[512,256]{1,0:T(8,128)S(1)}) custom-call(s32[1]{0:T(128)} %bitcast.refs_0_.refs_1_, bf16[4,16,16,128]{3,2,1,0:T(8,128)(2,1)S(1)} %get-tuple-element.40.refs_1_, bf16[4,16,16,128]{3,2,1,0:T(8,128)(2,1)S(1)} %collective-permute-done.7.refs_2_, ...), custom_call_target="tpu_custom_call" | custom-call | flops 4000000000 | bytes 6000000 | tf_op jit(solution)/shard_map/pallas_call | solution.py:62
  45.7 0.3 collective-permute-done.11.refs_2_.refs_1_
  46.0 0.9 %collective-permute-done.12.refs_3_.refs_2_ = f32[10,8,128]{2,1,0:T(8,128)S(1)} collective-permute-done((f32[10,8,128]{2,1,0:T(8,128)S(1)}, f32[10,8,128]{2,1,0:T(8,128)S(1)}, u32[]{:S(2)}, u32[]{:S(2)}) %collective-permute-start.12) | collective-permute-done | bytes 40992 | tf_op jit(solution)/shard_map/ppermute | solution.py:819
  46.9 0.0 collective-permute-done.13.refs_4_.refs_3_
  46.9 0.0 copy-start
  46.9 0.0 copy-start.3
  46.9 2.6 %shard_map.138 = bf16[4096,128]{1,0:T(8,128)(2,1)} custom-call(f32[10,8,128]{2,1,0:T(8,128)S(1)} %get-tuple-element.45.refs_1_.refs_0_, f32[10,8,128]{2,1,0:T(8,128)S(1)} %collective-permute-done.11.refs_2_.refs_1_, f32[10,8,128]{2,1,0:T(8,128)S(1)} %collective-permute-done.12.refs_3_.refs_2_, f32[10,8,128]{2,1,0:T(8,128)S(1)} %collective-permute-done.13.refs_4_.refs_3_, ...), custom_call_target="tpu_custom_call" | custom-call | flops 4000000000 | bytes 3000000 | tf_op jit(solution)/shard_map/pallas_call | solution.py:62
  49.5 0.0 copy-done
  49.5 0.0 copy-done.3
  49.5 2.2 %shard_map.137 = bf16[512,64]{1,0:T(8,128)(2,1)} custom-call(s32[1]{0:T(128)} %bitcast.refs_0_.refs_1_, f32[10,8,128]{2,1,0:T(8,128)S(1)} %get-tuple-element.45.refs_1_.refs_0_, f32[10,8,128]{2,1,0:T(8,128)S(1)} %collective-permute-done.11.refs_2_.refs_1_, f32[10,8,128]{2,1,0:T(8,128)S(1)} %collective-permute-done.12.refs_3_.refs_2_, ...), custom_call_target="tpu_custom_call" | custom-call | flops 3000000000 | bytes 5000000 | tf_op jit(solution)/shard_map/pallas_call | solution.py:62
  (4 shorter events, 0.0 us)
Async XLA Ops:
  3.6 3.9 %collective-permute-start = (bf16[768,128]{1,0:T(8,128)(2,1)}, bf16[768,128]{1,0:T(8,128)(2,1)S(1)}, u32[]{:S(2)}, u32[]{:S(2)}) collective-permute-start(bf16[768,128]{1,0:T(8,128)(2,1)} %get-tuple-element.34), channel_id=1, source_target_pairs={{0,1},{1,0},{2,3},{3,2},{4,5},{5,4},{6,7},{7,6},{8,9},{9,8},{10,11... | collective-permute-start | bytes 589832 | tf_op jit(solution)/shard_map/ppermute | solution.py:716
  4.0 12.5 %collective-permute-start.1 = (bf16[640,128]{1,0:T(8,128)(2,1)}, bf16[640,128]{1,0:T(8,128)(2,1)S(1)}, u32[]{:S(2)}, u32[]{:S(2)}) collective-permute-start(bf16[640,128]{1,0:T(8,128)(2,1)} %get-tuple-element.33.refs_2_), channel_id=1, source_target_pairs={{0,2},{1,3},{2,0},{3,1},{4,6},{5,7},{6,4},{7,5},{8,10},{9,11},{10,... | collective-permute-start | bytes 491528 | tf_op jit(solution)/shard_map/ppermute | solution.py:716
  7.5 15.6 %collective-permute-start.5 = (bf16[768,128]{1,0:T(8,128)(2,1)S(1)}, bf16[768,128]{1,0:T(8,128)(2,1)S(1)}, u32[]{:S(2)}, u32[]{:S(2)}) collective-permute-start(bf16[768,128]{1,0:T(8,128)(2,1)S(1)} %pad_maximum_fusion), channel_id=1, source_target_pairs={{0,8},{1,12},{2,0},{3,4},{4,9},{5,13},{6,1},{7,5},{8,10},{9,14},{1... | collective-permute-start | bytes 589832 | tf_op jit(solution)/shard_map/ppermute | solution.py:722
  10.2 12.9 %collective-permute-start.4 = (bf16[768,128]{1,0:T(8,128)(2,1)S(1)}, bf16[768,128]{1,0:T(8,128)(2,1)S(1)}, u32[]{:S(2)}, u32[]{:S(2)}) collective-permute-start(bf16[768,128]{1,0:T(8,128)(2,1)S(1)} %pad_maximum_fusion), channel_id=1, source_target_pairs={{0,0},{1,4},{2,8},{3,12},{4,1},{5,5},{6,9},{7,13},{8,2},{9,6},{10,... | collective-permute-start | bytes 589832 | tf_op jit(solution)/shard_map/ppermute | solution.py:722
  10.8 5.7 %collective-permute-start.2 = (bf16[128,128]{1,0:T(8,128)(2,1)}, bf16[128,128]{1,0:T(8,128)(2,1)S(1)}, u32[]{:S(2)}, u32[]{:S(2)}) collective-permute-start(bf16[128,128]{1,0:T(8,128)(2,1)} %get-tuple-element.35.refs_1_), channel_id=1, source_target_pairs={{0,3},{1,2},{2,1},{3,0},{4,7},{5,6},{6,5},{7,4},{8,11},{9,10},{10,... | collective-permute-start | bytes 98312 | tf_op jit(solution)/shard_map/ppermute | solution.py:716
  16.6 0.8 %copy-start.4 = (bf16[128,128]{1,0:T(8,128)(2,1)S(1)}, bf16[128,128]{1,0:T(8,128)(2,1)}, u32[]{:S(2)}) copy-start(bf16[128,128]{1,0:T(8,128)(2,1)} %get-tuple-element.35.refs_1_) | copy-start | bytes 98308
  17.3 5.8 %collective-permute-start.3 = (bf16[512,128]{1,0:T(8,128)(2,1)S(1)}, bf16[512,128]{1,0:T(8,128)(2,1)S(1)}, u32[]{:S(2)}, u32[]{:S(2)}) collective-permute-start(bf16[512,128]{1,0:T(8,128)(2,1)S(1)} %shard_map.131.refs_2_), channel_id=1, source_target_pairs={{0,16},{16,0},{1,17},{17,1},{2,18},{18,2},{3,19},{19,3},{4,20},{20... | collective-permute-start | bytes 393224 | tf_op jit(solution)/shard_map/ppermute | solution.py:732
  23.1 1.6 %collective-permute-start.6 = (bf16[640,128]{1,0:T(8,128)(2,1)S(1)}, bf16[640,128]{1,0:T(8,128)(2,1)S(1)}, u32[]{:S(2)}, u32[]{:S(2)}) collective-permute-start(bf16[640,128]{1,0:T(8,128)(2,1)S(1)} %collective-permute-done.1.refs_3_.refs_4_), channel_id=1, source_target_pairs={{0,1},{1,0},{2,3},{3,2},{4,5},{5,4},{6,7},{7,6},{8,9},{9,8},{10,11... | collective-permute-start | bytes 491528 | tf_op jit(solution)/shard_map/ppermute | solution.py:716
  23.1 8.8 %collective-permute-start.9 = (bf16[512,128]{1,0:T(8,128)(2,1)S(1)}, bf16[512,128]{1,0:T(8,128)(2,1)S(1)}, u32[]{:S(2)}, u32[]{:S(2)}) collective-permute-start(bf16[512,128]{1,0:T(8,128)(2,1)S(1)} %shard_map.133.refs_3_), channel_id=1, source_target_pairs={{0,16},{16,0},{1,17},{17,1},{2,18},{18,2},{3,19},{19,3},{4,20},{20... | collective-permute-start | bytes 393224 | tf_op jit(solution)/shard_map/ppermute | solution.py:732
  24.7 0.9 %copy-start.8 = (bf16[640,128]{1,0:T(8,128)(2,1)S(1)}, bf16[640,128]{1,0:T(8,128)(2,1)}, u32[]{:S(2)}) copy-start(bf16[640,128]{1,0:T(8,128)(2,1)} %get-tuple-element.33.refs_2_) | copy-start | bytes 491524
  25.6 0.9 %copy-start.9 = (bf16[64,768]{1,0:T(8,128)(2,1)S(1)}, bf16[64,768]{1,0:T(8,128)(2,1)}, u32[]{:S(2)}) copy-start(bf16[64,768]{1,0:T(8,128)(2,1)} %get-tuple-element.39.refs_8_) | copy-start | bytes 294916
  26.5 5.4 %copy-start.5 = (s32[256]{0:T(256)S(1)}, s32[256]{0:T(256)}, u32[]{:S(2)}) copy-start(s32[256]{0:T(256)} %param.13) | copy-start | bytes 3076
  26.5 5.4 %copy-start.6 = (bf16[64,64,128]{2,1,0:T(8,128)(2,1)S(1)}, bf16[64,64,128]{2,1,0:T(8,128)(2,1)}, u32[]{:S(2)}) copy-start(bf16[64,64,128]{2,1,0:T(8,128)(2,1)} %param.12) | copy-start | bytes 3145732
  26.5 5.4 %copy-start.7 = (f32[1024,128]{1,0:T(8,128)S(1)}, f32[1024,128]{1,0:T(8,128)}, u32[]{:S(2)}) copy-start(f32[1024,128]{1,0:T(8,128)} %refs_7_.4) | copy-start | bytes 1572868
  26.5 5.4 %copy-start.11 = (f32[128,8]{0,1:T(8,128)S(1)}, f32[128,8]{0,1:T(8,128)}, u32[]{:S(2)}) copy-start(f32[128,8]{0,1:T(8,128)} %param.19) | copy-start | bytes 12292
  28.8 13.5 %collective-permute-start.8 = (bf16[4,16,16,128]{3,2,1,0:T(8,128)(2,1)S(1)}, bf16[4,16,16,128]{3,2,1,0:T(8,128)(2,1)S(1)}, u32[]{:S(2)}, u32[]{:S(2)}) collective-permute-start(bf16[4,16,16,128]{3,2,1,0:T(8,128)(2,1)S(1)} %get-tuple-element.40.refs_1_), channel_id=1, source_target_pairs={{0,2},{1,3},{2,0},{3,1},{4,6},{5,7},{6,4},{7,5},{8,10},{9,11},{10,... | collective-permute-start | bytes 786440 | tf_op jit(solution)/shard_map/ppermute | solution.py:716
  30.7 11.6 %collective-permute-start.7 = (bf16[4,16,16,128]{3,2,1,0:T(8,128)(2,1)S(1)}, bf16[4,16,16,128]{3,2,1,0:T(8,128)(2,1)S(1)}, u32[]{:S(2)}, u32[]{:S(2)}) collective-permute-start(bf16[4,16,16,128]{3,2,1,0:T(8,128)(2,1)S(1)} %get-tuple-element.40.refs_1_), channel_id=1, source_target_pairs={{0,1},{1,0},{2,3},{3,2},{4,5},{5,4},{6,7},{7,6},{8,9},{9,8},{10,11... | collective-permute-start | bytes 786440 | tf_op jit(solution)/shard_map/ppermute | solution.py:716
  30.7 11.1 %collective-permute-start.10 = (f32[16,8,256]{2,1,0:T(8,128)S(1)}, f32[16,8,256]{2,1,0:T(8,128)S(1)}, u32[]{:S(2)}, u32[]{:S(2)}) collective-permute-start(f32[16,8,256]{2,1,0:T(8,128)S(1)} %get-tuple-element.43.refs_2_), channel_id=1, source_target_pairs={{0,16},{16,0},{1,17},{17,1},{2,18},{18,2},{3,19},{19,3},{4,20},{20... | collective-permute-start | bytes 393224 | tf_op jit(solution)/shard_map/ppermute | solution.py:767
  31.9 12.4 %copy-start.1 = (bf16[64,256]{1,0:T(8,128)(2,1)S(1)}, bf16[64,256]{1,0:T(8,128)(2,1)}, u32[]{:S(2)}) copy-start(bf16[64,256]{1,0:T(8,128)(2,1)} %refs_5_.1) | copy-start | bytes 98308
  32.0 12.4 %copy-start.2 = (bf16[64,256]{1,0:T(8,128)(2,1)S(1)}, bf16[64,256]{1,0:T(8,128)(2,1)}, u32[]{:S(2)}) copy-start(bf16[64,256]{1,0:T(8,128)(2,1)} %refs_7_.5) | copy-start | bytes 98308
  32.0 12.4 %copy-start.10 = (bf16[256,128]{1,0:T(8,128)(2,1)S(1)}, bf16[256,128]{1,0:T(8,128)(2,1)}, u32[]{:S(2)}) copy-start(bf16[256,128]{1,0:T(8,128)(2,1)} %get-tuple-element.51.refs_6_) | copy-start | bytes 196612
  42.3 2.1 %collective-permute-start.14 = (bf16[4,16,16,128]{3,2,1,0:T(8,128)(2,1)S(1)}, bf16[4,16,16,128]{3,2,1,0:T(8,128)(2,1)S(1)}, u32[]{:S(2)}, u32[]{:S(2)}) collective-permute-start(bf16[4,16,16,128]{3,2,1,0:T(8,128)(2,1)S(1)} %collective-permute-done.8.refs_3_), channel_id=1, source_target_pairs={{0,1},{1,0},{2,3},{3,2},{4,5},{5,4},{6,7},{7,6},{8,9},{9,8},{10,11... | collective-permute-start | bytes 786440 | tf_op jit(solution)/shard_map/ppermute | solution.py:716
  42.6 3.4 %collective-permute-start.11 = (f32[10,8,128]{2,1,0:T(8,128)S(1)}, f32[10,8,128]{2,1,0:T(8,128)S(1)}, u32[]{:S(2)}, u32[]{:S(2)}) collective-permute-start(f32[10,8,128]{2,1,0:T(8,128)S(1)} %get-tuple-element.46), channel_id=1, source_target_pairs={{0,1},{1,2},{2,3},{3,0},{4,5},{5,6},{6,7},{7,4},{8,9},{9,10},{10,1... | collective-permute-start | bytes 122888 | tf_op jit(solution)/shard_map/ppermute | solution.py:819
  42.9 4.0 %collective-permute-start.12 = (f32[10,8,128]{2,1,0:T(8,128)S(1)}, f32[10,8,128]{2,1,0:T(8,128)S(1)}, u32[]{:S(2)}, u32[]{:S(2)}) collective-permute-start(f32[10,8,128]{2,1,0:T(8,128)S(1)} %get-tuple-element.47), channel_id=1, source_target_pairs={{0,2},{1,3},{2,0},{3,1},{4,6},{5,7},{6,4},{7,5},{8,10},{9,11},{10,... | collective-permute-start | bytes 122888 | tf_op jit(solution)/shard_map/ppermute | solution.py:819
  43.2 3.7 %collective-permute-start.13 = (f32[10,8,128]{2,1,0:T(8,128)S(1)}, f32[10,8,128]{2,1,0:T(8,128)S(1)}, u32[]{:S(2)}, u32[]{:S(2)}) collective-permute-start(f32[10,8,128]{2,1,0:T(8,128)S(1)} %get-tuple-element.48), channel_id=1, source_target_pairs={{0,3},{1,0},{2,1},{3,2},{4,7},{5,4},{6,5},{7,6},{8,11},{9,8},{10,9... | collective-permute-start | bytes 122888 | tf_op jit(solution)/shard_map/ppermute | solution.py:819
  46.9 2.6 %copy-start = (bf16[32,16,64]{2,1,0:T(8,128)(2,1)S(1)}, bf16[32,16,64]{2,1,0:T(8,128)(2,1)}, u32[]{:S(2)}) copy-start(bf16[32,16,64]{2,1,0:T(8,128)(2,1)} %refs_1_.1) | copy-start | bytes 196612
  46.9 2.6 %copy-start.3 = (bf16[256,64]{0,1:T(8,128)(2,1)S(1)}, bf16[256,64]{0,1:T(8,128)(2,1)}, u32[]{:S(2)}) copy-start(bf16[256,64]{0,1:T(8,128)(2,1)} %param.20) | copy-start | bytes 98308

commit v18 on v17

--- a/solution.py
+++ b/solution.py
@@ -166,6 +166,11 @@
     for t, ref in enumerate((rows0_ref, rows1_ref, rows2_ref, rows3_ref)):
         at = pl.ds(pl.multiple_of(jnp.bitwise_xor(col_ref[0], t) * size, size), size)
         out_ref[at, :] = ref[:size, :]
+
+
+def hand_on_kernel(ready, weights_ref, rows_ref, weights_out_ref, rows_out_ref):
+    weights_out_ref[...] = weights_ref[...]
+    rows_out_ref[...] = rows_ref[...]
 
 
 def join_right_kernel(ready, row_ref, pair0_ref, pair1_ref, out_ref):
@@ -735,8 +740,13 @@
     lefts = [own_left, other, across, exchange(own_left, 3)]
     (left,) = call(join_left_kernel, (sds((nk * l_rows, 128), bf16),), smem=1)(place[1], *lefts)
     far_left = over_seq(left)
-    across, far_left, *all_cols = lax.optimization_barrier((across, far_left, *all_cols))
-    all_rows = [rows, other, across, exchange(across, 1)]
+    weights, own = call(hand_on_kernel, (sds(weights.shape, bf16), sds(rows.shape, bf16)))(
+        weights, rows
+    )
+    across, far_left, weights, own, *all_cols = lax.optimization_barrier(
+        (across, far_left, weights, own, *all_cols)
+    )
+    all_rows = [own, other, across, exchange(across, 1)]
 
     (right,) = call(join_right_kernel, (sds((nk * r_rows, 128), bf16),), smem=1)(
         place[0], *all_cols

time: 52.6 us -> 50.7 us (0.964)
  waiting for transfers between devices: 7.31 us -> 5.14 us
    ppermute x2, waiting for transfers between devices: 4.2 us -> 2.37 us  [over_seq(): return lax.ppermute(x, 'seq', [(0, 1), (1, 0)])]
    pallas_call x9 -> x10, Pallas kernels: 21.7 us -> 21.7 us  [run(): pl.pallas_call(body, out_shape=out_shape, in_specs=in_specs, out_specs=[p...]
  transfers between devices with their start and end apart: 15 -> 15, of which waited for: 4 -> 3; matrix products, arithmetic and copies ran while one was open for 2% -> 2% of each run, Pallas kernels for 27% -> 28%
where the time goes in v18:
time: 50.7 us; the launch traced here: 49.9 us
  Pallas kernels  21.7 us (43%)
  starting transfers between devices  18.7 us (37%)
  waiting for transfers between devices  5.14 us (10%)
  local copies, waits for them, and re-layouts  3.52 us (7%)
  between operations  0.86 us (2%)
    pallas_call x10, Pallas kernels, run(): pl.pallas_call(body, out_shape=out_shape, in_specs=in_specs, out_specs=[p...  21.7 us
    ppermute x7, starting transfers between devices, exchange(): return lax.ppermute(x, 'col', [(c, c ^ bit) for c in range(nk)])  9.07 us
    ppermute x2, starting transfers between devices, on_device(): lax.ppermute(pair, ('row', 'col'), [(r * nk + c, (c ^ flip) * nk + r) for...  3.3 us
    ppermute x2, starting transfers between devices, over_seq(): return lax.ppermute(x, 'seq', [(0, 1), (1, 0)])  3.11 us
    unnamed x24, local copies, waits for them, and re-layouts  2.62 us
    ppermute x2, waiting for transfers between devices, over_seq(): return lax.ppermute(x, 'seq', [(0, 1), (1, 0)])  2.37 us
    ppermute x3, starting transfers between devices, on_device(): lax.ppermute(pay, 'col', [(c, (c + shift) % nk) for c in range(nk)])  2.12 us
    ppermute x7, waiting for transfers between devices, exchange(): return lax.ppermute(x, 'col', [(c, c ^ bit) for c in range(nk)])  1.93 us
  transfers between devices with their start and end apart: 15, of which 3 were waited for; matrix products, arithmetic and copies ran while one was open for 2% of the time, Pallas kernels for 28%

profile of v18, /device:TPU:0, one launch (start us, length us, event | category | flops | bytes accessed | tf_op | source)
XLA Modules:
  0.0 49.9 jit_solution(13791615966851472569)
XLA Ops:
  0.6 2.9 %shard_map.130 = (bf16[768,128]{1,0:T(8,128)(2,1)}, bf16[640,128]{1,0:T(8,128)(2,1)}, bf16[128,128]{1,0:T(8,128)(2,1)}, bf16[256,128]{1,0:T(8,128)(2,1)}, bf16[64,768]{1,0:T(8,128)(2,1)}) custom-call(s32[1]{0:T(128)} %bitcast.2.refs_0_, bf16[32,16,64]{2,1,0:T(8,128)(2,1)} %refs_1_.1, bf16[32,16,64]{2,1,0:T(8,128)(2,1)} %refs_2_.1, bf16[32,64]{1,0:T(8,128)(2,1)} %bitcast.23, ...), custom_call_target="tpu_custom_call" | custom-call | tf_op jit(solution)/shard_map/pallas_call | solution.py:62
  3.6 0.5 collective-permute-start.1
  4.0 2.6 %collective-permute-start = (bf16[640,128]{1,0:T(8,128)(2,1)}, bf16[640,128]{1,0:T(8,128)(2,1)S(1)}, u32[]{:S(2)}, u32[]{:S(2)}) collective-permute-start(bf16[640,128]{1,0:T(8,128)(2,1)} %get-tuple-element.37.refs_1_), channel_id=1, source_target_pairs={{0,2},{1,3},{2,0},{3,1},{4,6},{5,7},{6,4},{7,5},{8,10},{9,11},{10,... | collective-permute-start | bytes 491528 | tf_op jit(solution)/shard_map/ppermute | solution.py:721
  6.6 0.9 %slice.6 = bf16[384,128]{1,0:T(8,128)(2,1)S(1)} slice(bf16[768,128]{1,0:T(8,128)(2,1)} %get-tuple-element.39), slice={[384:768], [0:128]} | slice | bytes 196608 | tf_op jit(solution)/shard_map/slice | solution.py:725
  7.5 0.0 collective-permute-done.1.refs_2_.refs_3_
  7.5 2.6 %collective-permute-start.5 = (bf16[768,128]{1,0:T(8,128)(2,1)S(1)}, bf16[768,128]{1,0:T(8,128)(2,1)S(1)}, u32[]{:S(2)}, u32[]{:S(2)}) collective-permute-start(bf16[768,128]{1,0:T(8,128)(2,1)S(1)} %pad_maximum_fusion), channel_id=1, source_target_pairs={{0,8},{1,12},{2,0},{3,4},{4,9},{5,13},{6,1},{7,5},{8,10},{9,14},{1... | collective-permute-start | bytes 589832 | tf_op jit(solution)/shard_map/ppermute | solution.py:727
  10.2 0.7 %collective-permute-start.4 = (bf16[768,128]{1,0:T(8,128)(2,1)S(1)}, bf16[768,128]{1,0:T(8,128)(2,1)S(1)}, u32[]{:S(2)}, u32[]{:S(2)}) collective-permute-start(bf16[768,128]{1,0:T(8,128)(2,1)S(1)} %pad_maximum_fusion), channel_id=1, source_target_pairs={{0,0},{1,4},{2,8},{3,12},{4,1},{5,5},{6,9},{7,13},{8,2},{9,6},{10,... | collective-permute-start | bytes 589832 | tf_op jit(solution)/shard_map/ppermute | solution.py:727
  10.8 3.8 %collective-permute-start.2 = (bf16[128,128]{1,0:T(8,128)(2,1)}, bf16[128,128]{1,0:T(8,128)(2,1)S(1)}, u32[]{:S(2)}, u32[]{:S(2)}) collective-permute-start(bf16[128,128]{1,0:T(8,128)(2,1)} %get-tuple-element.38.refs_1_), channel_id=1, source_target_pairs={{0,3},{1,2},{2,1},{3,0},{4,7},{5,6},{6,5},{7,4},{8,11},{9,10},{10,... | collective-permute-start | bytes 98312 | tf_op jit(solution)/shard_map/ppermute | solution.py:721
  14.6 1.9 %collective-permute-done.2.refs_4_ = bf16[128,128]{1,0:T(8,128)(2,1)S(1)} collective-permute-done((bf16[128,128]{1,0:T(8,128)(2,1)}, bf16[128,128]{1,0:T(8,128)(2,1)S(1)}, u32[]{:S(2)}, u32[]{:S(2)}) %collective-permute-start.2) | collective-permute-done | bytes 32800 | tf_op jit(solution)/shard_map/ppermute | solution.py:721
  16.5 0.0 collective-permute-done.refs_3_.refs_4_
  16.6 0.0 copy-start.6
  16.6 0.8 %copy-done.6 = bf16[128,128]{1,0:T(8,128)(2,1)S(1)} copy-done((bf16[128,128]{1,0:T(8,128)(2,1)S(1)}, bf16[128,128]{1,0:T(8,128)(2,1)}, u32[]{:S(2)}) %copy-start.6) | copy-done | bytes 32792
  17.3 1.6 %collective-permute-start.3 = (bf16[512,128]{1,0:T(8,128)(2,1)S(1)}, bf16[512,128]{1,0:T(8,128)(2,1)S(1)}, u32[]{:S(2)}, u32[]{:S(2)}) collective-permute-start(bf16[512,128]{1,0:T(8,128)(2,1)S(1)} %shard_map.131.refs_2_), channel_id=1, source_target_pairs={{0,16},{16,0},{1,17},{17,1},{2,18},{18,2},{3,19},{19,3},{4,20},{20... | collective-permute-start | bytes 393224 | tf_op jit(solution)/shard_map/ppermute | solution.py:737
  18.9 0.0 copy-start
  18.9 0.9 %copy-done = bf16[640,128]{1,0:T(8,128)(2,1)S(1)} copy-done((bf16[640,128]{1,0:T(8,128)(2,1)S(1)}, bf16[640,128]{1,0:T(8,128)(2,1)}, u32[]{:S(2)}) %copy-start) | copy-done | bytes 163864
  19.8 0.0 copy-start.2
  19.8 0.9 %copy-done.2 = bf16[64,768]{1,0:T(8,128)(2,1)S(1)} copy-done((bf16[64,768]{1,0:T(8,128)(2,1)S(1)}, bf16[64,768]{1,0:T(8,128)(2,1)}, u32[]{:S(2)}) %copy-start.2) | copy-done | bytes 98328
  20.7 2.4 %collective-permute-done.3.refs_4_ = bf16[512,128]{1,0:T(8,128)(2,1)S(1)} collective-permute-done((bf16[512,128]{1,0:T(8,128)(2,1)S(1)}, bf16[512,128]{1,0:T(8,128)(2,1)S(1)}, u32[]{:S(2)}, u32[]{:S(2)}) %collective-permute-start.3) | collective-permute-done | bytes 131104 | tf_op jit(solution)/shard_map/ppermute | solution.py:737
  23.1 0.0 collective-permute-done.5.refs_7_.refs_2_
  23.1 0.0 collective-permute-done.4.refs_6_.refs_1_
  23.1 0.0 collective-permute-start.6
  23.1 0.0 copy-start.7
  23.1 0.0 copy-start.8
  23.2 0.0 copy-start.9
  23.2 0.0 copy-start.11
  23.2 1.6 %collective-permute-start.9 = (bf16[512,128]{1,0:T(8,128)(2,1)S(1)}, bf16[512,128]{1,0:T(8,128)(2,1)S(1)}, u32[]{:S(2)}, u32[]{:S(2)}) collective-permute-start(bf16[512,128]{1,0:T(8,128)(2,1)S(1)} %shard_map.134.refs_3_), channel_id=1, source_target_pairs={{0,16},{16,0},{1,17},{17,1},{2,18},{18,2},{3,19},{19,3},{4,20},{20... | collective-permute-start | bytes 393224 | tf_op jit(solution)/shard_map/ppermute | solution.py:737
  24.7 0.0 collective-permute-done.6.refs_5_
  24.7 2.3 %shard_map.133 = (f32[16,8,256]{2,1,0:T(8,128)S(1)}, bf16[4,16,16,128]{3,2,1,0:T(8,128)(2,1)S(1)}) custom-call(s32[1]{0:T(128)} %bitcast.1.refs_0_, s32[1]{0:T(128)} %bitcast.refs_0_.refs_1_, bf16[640,128]{1,0:T(8,128)(2,1)S(1)} %get-tuple-element.43.refs_2_, bf16[768,128]{1,0:T(8,128)(2,1)S(1)} %collective-permute-done.1.refs_2_.refs_3_, ...), custom_call_target="tpu_custom_call" | custom-call | flops 3000000000 | bytes 3000000 | tf_op jit(solution)/shard_map/pallas_call | solution.py:62
  27.0 1.9 %collective-permute-start.8 = (bf16[4,16,16,128]{3,2,1,0:T(8,128)(2,1)S(1)}, bf16[4,16,16,128]{3,2,1,0:T(8,128)(2,1)S(1)}, u32[]{:S(2)}, u32[]{:S(2)}) collective-permute-start(bf16[4,16,16,128]{3,2,1,0:T(8,128)(2,1)S(1)} %get-tuple-element.48.refs_1_), channel_id=1, source_target_pairs={{0,2},{1,3},{2,0},{3,1},{4,6},{5,7},{6,4},{7,5},{8,10},{9,11},{10,... | collective-permute-start | bytes 786440 | tf_op jit(solution)/shard_map/ppermute | solution.py:721
  28.9 0.0 collective-permute-start.7
  28.9 1.1 %collective-permute-start.10 = (f32[16,8,256]{2,1,0:T(8,128)S(1)}, f32[16,8,256]{2,1,0:T(8,128)S(1)}, u32[]{:S(2)}, u32[]{:S(2)}) collective-permute-start(f32[16,8,256]{2,1,0:T(8,128)S(1)} %get-tuple-element.51.refs_2_), channel_id=1, source_target_pairs={{0,16},{16,0},{1,17},{17,1},{2,18},{18,2},{3,19},{19,3},{4,20},{20... | collective-permute-start | bytes 393224 | tf_op jit(solution)/shard_map/ppermute | solution.py:777
  30.1 0.0 collective-permute-done.9.refs_5_
  30.1 0.0 copy-done.7
  30.1 0.0 copy-done.8
  30.1 0.0 copy-done.9
  30.1 0.0 copy-done.11
  30.1 0.0 copy-start.3
  30.1 0.0 copy-start.4
  30.1 0.0 copy-start.10
  30.1 9.8 %shard_map.135 = (bf16[4096,128]{1,0:T(8,128)(2,1)}, f32[16,128,256]{2,1,0:T(8,128)S(1)}, f32[16,8,256]{2,1,0:T(8,128)S(1)}, f32[16,8,256]{2,1,0:T(8,128)S(1)}) custom-call(s32[1]{0:T(128)} %bitcast.refs_0_.refs_1_, s32[1]{0:T(128)} %bitcast.7.refs_1_, bf16[512,128]{1,0:T(8,128)(2,1)S(1)} %shard_map.131.refs_2_, bf16[512,128]{1,0:T(8,128)(2,1)S(1)} %shard_map.134.refs_3_, ...), custom_call_target="tpu_custom_call" | custom-call | flops 14000000000 | bytes 5000000 | tf_op jit(solution)/shard_map/pallas_call | solution.py:62
  40.0 0.0 collective-permute-done.10.refs_3_
  40.0 0.5 shard_map.136
  40.4 0.0 collective-permute-done.8.refs_3_
  40.4 0.0 collective-permute-done.7.refs_2_
  40.4 0.3 collective-permute-start.14
  40.7 0.3 collective-permute-start.11
  41.0 0.8 %collective-permute-start.12 = (f32[10,8,128]{2,1,0:T(8,128)S(1)}, f32[10,8,128]{2,1,0:T(8,128)S(1)}, u32[]{:S(2)}, u32[]{:S(2)}) collective-permute-start(f32[10,8,128]{2,1,0:T(8,128)S(1)} %get-tuple-element.55), channel_id=1, source_target_pairs={{0,2},{1,3},{2,0},{3,1},{4,6},{5,7},{6,4},{7,5},{8,10},{9,11},{10,... | collective-permute-start | bytes 122888 | tf_op jit(solution)/shard_map/ppermute | solution.py:829
  41.8 1.0 %collective-permute-start.13 = (f32[10,8,128]{2,1,0:T(8,128)S(1)}, f32[10,8,128]{2,1,0:T(8,128)S(1)}, u32[]{:S(2)}, u32[]{:S(2)}) collective-permute-start(f32[10,8,128]{2,1,0:T(8,128)S(1)} %get-tuple-element.56), channel_id=1, source_target_pairs={{0,3},{1,0},{2,1},{3,2},{4,7},{5,4},{6,5},{7,6},{8,11},{9,8},{10,9... | collective-permute-start | bytes 122888 | tf_op jit(solution)/shard_map/ppermute | solution.py:829
  42.9 0.0 collective-permute-done.14.refs_4_
  42.9 0.0 copy-done.3
  42.9 0.0 copy-done.4
  42.9 0.0 copy-done.10
  42.9 1.3 %shard_map.137 = (bf16[16,256,512]{2,1,0:T(8,128)(2,1)S(1)}, f32[512,256]{1,0:T(8,128)S(1)}) custom-call(s32[1]{0:T(128)} %bitcast.refs_0_.refs_1_, bf16[4,16,16,128]{3,2,1,0:T(8,128)(2,1)S(1)} %get-tuple-element.48.refs_1_, bf16[4,16,16,128]{3,2,1,0:T(8,128)(2,1)S(1)} %collective-permute-done.7.refs_2_, ...), custom_call_target="tpu_custom_call" | custom-call | flops 4000000000 | bytes 6000000 | tf_op jit(solution)/shard_map/pallas_call | solution.py:62
  44.2 0.0 collective-permute-done.11.refs_2_.refs_1_
  44.2 0.8 %collective-permute-done.12.refs_3_.refs_2_ = f32[10,8,128]{2,1,0:T(8,128)S(1)} collective-permute-done((f32[10,8,128]{2,1,0:T(8,128)S(1)}, f32[10,8,128]{2,1,0:T(8,128)S(1)}, u32[]{:S(2)}, u32[]{:S(2)}) %collective-permute-start.12) | collective-permute-done | bytes 40992 | tf_op jit(solution)/shard_map/ppermute | solution.py:829
  45.1 0.0 collective-permute-done.13.refs_4_.refs_3_
  45.1 0.0 copy-start.1
  45.1 0.0 copy-start.5
  45.1 2.6 %shard_map.139 = bf16[4096,128]{1,0:T(8,128)(2,1)} custom-call(f32[10,8,128]{2,1,0:T(8,128)S(1)} %get-tuple-element.53.refs_1_.refs_0_, f32[10,8,128]{2,1,0:T(8,128)S(1)} %collective-permute-done.11.refs_2_.refs_1_, f32[10,8,128]{2,1,0:T(8,128)S(1)} %collective-permute-done.12.refs_3_.refs_2_, f32[10,8,128]{2,1,0:T(8,128)S(1)} %collective-permute-done.13.refs_4_.refs_3_, ...), custom_call_target="tpu_custom_call" | custom-call | flops 4000000000 | bytes 3000000 | tf_op jit(solution)/shard_map/pallas_call | solution.py:62
  47.7 0.0 copy-done.1
  47.7 0.0 copy-done.5
  47.7 2.2 %shard_map.138 = bf16[512,64]{1,0:T(8,128)(2,1)} custom-call(s32[1]{0:T(128)} %bitcast.refs_0_.refs_1_, f32[10,8,128]{2,1,0:T(8,128)S(1)} %get-tuple-element.53.refs_1_.refs_0_, f32[10,8,128]{2,1,0:T(8,128)S(1)} %collective-permute-done.11.refs_2_.refs_1_, f32[10,8,128]{2,1,0:T(8,128)S(1)} %collective-permute-done.12.refs_3_.refs_2_, ...), custom_call_target="tpu_custom_call" | custom-call | flops 3000000000 | bytes 5000000 | tf_op jit(solution)/shard_map/pallas_call | solution.py:62
  (5 shorter events, 0.1 us)
Async XLA Ops:
  3.6 3.9 %collective-permute-start.1 = (bf16[768,128]{1,0:T(8,128)(2,1)}, bf16[768,128]{1,0:T(8,128)(2,1)S(1)}, u32[]{:S(2)}, u32[]{:S(2)}) collective-permute-start(bf16[768,128]{1,0:T(8,128)(2,1)} %get-tuple-element.39), channel_id=1, source_target_pairs={{0,1},{1,0},{2,3},{3,2},{4,5},{5,4},{6,7},{7,6},{8,9},{9,8},{10,11... | collective-permute-start | bytes 589832 | tf_op jit(solution)/shard_map/ppermute | solution.py:721
  4.0 12.5 %collective-permute-start = (bf16[640,128]{1,0:T(8,128)(2,1)}, bf16[640,128]{1,0:T(8,128)(2,1)S(1)}, u32[]{:S(2)}, u32[]{:S(2)}) collective-permute-start(bf16[640,128]{1,0:T(8,128)(2,1)} %get-tuple-element.37.refs_1_), channel_id=1, source_target_pairs={{0,2},{1,3},{2,0},{3,1},{4,6},{5,7},{6,4},{7,5},{8,10},{9,11},{10,... | collective-permute-start | bytes 491528 | tf_op jit(solution)/shard_map/ppermute | solution.py:721
  7.5 15.6 %collective-permute-start.5 = (bf16[768,128]{1,0:T(8,128)(2,1)S(1)}, bf16[768,128]{1,0:T(8,128)(2,1)S(1)}, u32[]{:S(2)}, u32[]{:S(2)}) collective-permute-start(bf16[768,128]{1,0:T(8,128)(2,1)S(1)} %pad_maximum_fusion), channel_id=1, source_target_pairs={{0,8},{1,12},{2,0},{3,4},{4,9},{5,13},{6,1},{7,5},{8,10},{9,14},{1... | collective-permute-start | bytes 589832 | tf_op jit(solution)/shard_map/ppermute | solution.py:727
  10.2 12.9 %collective-permute-start.4 = (bf16[768,128]{1,0:T(8,128)(2,1)S(1)}, bf16[768,128]{1,0:T(8,128)(2,1)S(1)}, u32[]{:S(2)}, u32[]{:S(2)}) collective-permute-start(bf16[768,128]{1,0:T(8,128)(2,1)S(1)} %pad_maximum_fusion), channel_id=1, source_target_pairs={{0,0},{1,4},{2,8},{3,12},{4,1},{5,5},{6,9},{7,13},{8,2},{9,6},{10,... | collective-permute-start | bytes 589832 | tf_op jit(solution)/shard_map/ppermute | solution.py:727
  10.8 5.7 %collective-permute-start.2 = (bf16[128,128]{1,0:T(8,128)(2,1)}, bf16[128,128]{1,0:T(8,128)(2,1)S(1)}, u32[]{:S(2)}, u32[]{:S(2)}) collective-permute-start(bf16[128,128]{1,0:T(8,128)(2,1)} %get-tuple-element.38.refs_1_), channel_id=1, source_target_pairs={{0,3},{1,2},{2,1},{3,0},{4,7},{5,6},{6,5},{7,4},{8,11},{9,10},{10,... | collective-permute-start | bytes 98312 | tf_op jit(solution)/shard_map/ppermute | solution.py:721
  16.6 0.8 %copy-start.6 = (bf16[128,128]{1,0:T(8,128)(2,1)S(1)}, bf16[128,128]{1,0:T(8,128)(2,1)}, u32[]{:S(2)}) copy-start(bf16[128,128]{1,0:T(8,128)(2,1)} %get-tuple-element.38.refs_1_) | copy-start | bytes 98308
  17.3 5.8 %collective-permute-start.3 = (bf16[512,128]{1,0:T(8,128)(2,1)S(1)}, bf16[512,128]{1,0:T(8,128)(2,1)S(1)}, u32[]{:S(2)}, u32[]{:S(2)}) collective-permute-start(bf16[512,128]{1,0:T(8,128)(2,1)S(1)} %shard_map.131.refs_2_), channel_id=1, source_target_pairs={{0,16},{16,0},{1,17},{17,1},{2,18},{18,2},{3,19},{19,3},{4,20},{20... | collective-permute-start | bytes 393224 | tf_op jit(solution)/shard_map/ppermute | solution.py:737
  18.9 0.9 %copy-start = (bf16[640,128]{1,0:T(8,128)(2,1)S(1)}, bf16[640,128]{1,0:T(8,128)(2,1)}, u32[]{:S(2)}) copy-start(bf16[640,128]{1,0:T(8,128)(2,1)} %get-tuple-element.37.refs_1_) | copy-start | bytes 491524
  19.8 0.9 %copy-start.2 = (bf16[64,768]{1,0:T(8,128)(2,1)S(1)}, bf16[64,768]{1,0:T(8,128)(2,1)}, u32[]{:S(2)}) copy-start(bf16[64,768]{1,0:T(8,128)(2,1)} %get-tuple-element.40.refs_0_) | copy-start | bytes 294916
  23.1 1.6 %collective-permute-start.6 = (bf16[640,128]{1,0:T(8,128)(2,1)S(1)}, bf16[640,128]{1,0:T(8,128)(2,1)S(1)}, u32[]{:S(2)}, u32[]{:S(2)}) collective-permute-start(bf16[640,128]{1,0:T(8,128)(2,1)S(1)} %collective-permute-done.refs_3_.refs_4_), channel_id=1, source_target_pairs={{0,1},{1,0},{2,3},{3,2},{4,5},{5,4},{6,7},{7,6},{8,9},{9,8},{10,11... | collective-permute-start | bytes 491528 | tf_op jit(solution)/shard_map/ppermute | solution.py:721
  23.1 6.9 %copy-start.7 = (s32[256]{0:T(256)S(1)}, s32[256]{0:T(256)}, u32[]{:S(2)}) copy-start(s32[256]{0:T(256)} %param.13) | copy-start | bytes 3076
  23.1 6.9 %copy-start.8 = (bf16[64,64,128]{2,1,0:T(8,128)(2,1)S(1)}, bf16[64,64,128]{2,1,0:T(8,128)(2,1)}, u32[]{:S(2)}) copy-start(bf16[64,64,128]{2,1,0:T(8,128)(2,1)} %param.12) | copy-start | bytes 3145732
  23.2 6.9 %copy-start.9 = (f32[1024,128]{1,0:T(8,128)S(1)}, f32[1024,128]{1,0:T(8,128)}, u32[]{:S(2)}) copy-start(f32[1024,128]{1,0:T(8,128)} %refs_7_.4) | copy-start | bytes 1572868
  23.2 6.9 %copy-start.11 = (f32[128,8]{0,1:T(8,128)S(1)}, f32[128,8]{0,1:T(8,128)}, u32[]{:S(2)}) copy-start(f32[128,8]{0,1:T(8,128)} %param.19) | copy-start | bytes 12292
  23.2 6.9 %collective-permute-start.9 = (bf16[512,128]{1,0:T(8,128)(2,1)S(1)}, bf16[512,128]{1,0:T(8,128)(2,1)S(1)}, u32[]{:S(2)}, u32[]{:S(2)}) collective-permute-start(bf16[512,128]{1,0:T(8,128)(2,1)S(1)} %shard_map.134.refs_3_), channel_id=1, source_target_pairs={{0,16},{16,0},{1,17},{17,1},{2,18},{18,2},{3,19},{19,3},{4,20},{20... | collective-permute-start | bytes 393224 | tf_op jit(solution)/shard_map/ppermute | solution.py:737
  27.0 13.4 %collective-permute-start.8 = (bf16[4,16,16,128]{3,2,1,0:T(8,128)(2,1)S(1)}, bf16[4,16,16,128]{3,2,1,0:T(8,128)(2,1)S(1)}, u32[]{:S(2)}, u32[]{:S(2)}) collective-permute-start(bf16[4,16,16,128]{3,2,1,0:T(8,128)(2,1)S(1)} %get-tuple-element.48.refs_1_), channel_id=1, source_target_pairs={{0,2},{1,3},{2,0},{3,1},{4,6},{5,7},{6,4},{7,5},{8,10},{9,11},{10,... | collective-permute-start | bytes 786440 | tf_op jit(solution)/shard_map/ppermute | solution.py:721
  28.9 11.5 %collective-permute-start.7 = (bf16[4,16,16,128]{3,2,1,0:T(8,128)(2,1)S(1)}, bf16[4,16,16,128]{3,2,1,0:T(8,128)(2,1)S(1)}, u32[]{:S(2)}, u32[]{:S(2)}) collective-permute-start(bf16[4,16,16,128]{3,2,1,0:T(8,128)(2,1)S(1)} %get-tuple-element.48.refs_1_), channel_id=1, source_target_pairs={{0,1},{1,0},{2,3},{3,2},{4,5},{5,4},{6,7},{7,6},{8,9},{9,8},{10,11... | collective-permute-start | bytes 786440 | tf_op jit(solution)/shard_map/ppermute | solution.py:721
  28.9 11.0 %collective-permute-start.10 = (f32[16,8,256]{2,1,0:T(8,128)S(1)}, f32[16,8,256]{2,1,0:T(8,128)S(1)}, u32[]{:S(2)}, u32[]{:S(2)}) collective-permute-start(f32[16,8,256]{2,1,0:T(8,128)S(1)} %get-tuple-element.51.refs_2_), channel_id=1, source_target_pairs={{0,16},{16,0},{1,17},{17,1},{2,18},{18,2},{3,19},{19,3},{4,20},{20... | collective-permute-start | bytes 393224 | tf_op jit(solution)/shard_map/ppermute | solution.py:777
  30.1 12.8 %copy-start.3 = (bf16[64,256]{1,0:T(8,128)(2,1)S(1)}, bf16[64,256]{1,0:T(8,128)(2,1)}, u32[]{:S(2)}) copy-start(bf16[64,256]{1,0:T(8,128)(2,1)} %refs_5_.1) | copy-start | bytes 98308
  30.1 12.8 %copy-start.4 = (bf16[64,256]{1,0:T(8,128)(2,1)S(1)}, bf16[64,256]{1,0:T(8,128)(2,1)}, u32[]{:S(2)}) copy-start(bf16[64,256]{1,0:T(8,128)(2,1)} %refs_7_.5) | copy-start | bytes 98308
  30.1 12.8 %copy-start.10 = (bf16[256,128]{1,0:T(8,128)(2,1)S(1)}, bf16[256,128]{1,0:T(8,128)(2,1)}, u32[]{:S(2)}) copy-start(bf16[256,128]{1,0:T(8,128)(2,1)} %get-tuple-element.59.refs_6_) | copy-start | bytes 196612
  40.4 2.4 %collective-permute-start.14 = (bf16[4,16,16,128]{3,2,1,0:T(8,128)(2,1)S(1)}, bf16[4,16,16,128]{3,2,1,0:T(8,128)(2,1)S(1)}, u32[]{:S(2)}, u32[]{:S(2)}) collective-permute-start(bf16[4,16,16,128]{3,2,1,0:T(8,128)(2,1)S(1)} %collective-permute-done.8.refs_3_), channel_id=1, source_target_pairs={{0,1},{1,0},{2,3},{3,2},{4,5},{5,4},{6,7},{7,6},{8,9},{9,8},{10,11... | collective-permute-start | bytes 786440 | tf_op jit(solution)/shard_map/ppermute | solution.py:721
  40.7 3.5 %collective-permute-start.11 = (f32[10,8,128]{2,1,0:T(8,128)S(1)}, f32[10,8,128]{2,1,0:T(8,128)S(1)}, u32[]{:S(2)}, u32[]{:S(2)}) collective-permute-start(f32[10,8,128]{2,1,0:T(8,128)S(1)} %get-tuple-element.54), channel_id=1, source_target_pairs={{0,1},{1,2},{2,3},{3,0},{4,5},{5,6},{6,7},{7,4},{8,9},{9,10},{10,1... | collective-permute-start | bytes 122888 | tf_op jit(solution)/shard_map/ppermute | solution.py:829
  41.0 4.0 %collective-permute-start.12 = (f32[10,8,128]{2,1,0:T(8,128)S(1)}, f32[10,8,128]{2,1,0:T(8,128)S(1)}, u32[]{:S(2)}, u32[]{:S(2)}) collective-permute-start(f32[10,8,128]{2,1,0:T(8,128)S(1)} %get-tuple-element.55), channel_id=1, source_target_pairs={{0,2},{1,3},{2,0},{3,1},{4,6},{5,7},{6,4},{7,5},{8,10},{9,11},{10,... | collective-permute-start | bytes 122888 | tf_op jit(solution)/shard_map/ppermute | solution.py:829
  41.8 3.2 %collective-permute-start.13 = (f32[10,8,128]{2,1,0:T(8,128)S(1)}, f32[10,8,128]{2,1,0:T(8,128)S(1)}, u32[]{:S(2)}, u32[]{:S(2)}) collective-permute-start(f32[10,8,128]{2,1,0:T(8,128)S(1)} %get-tuple-element.56), channel_id=1, source_target_pairs={{0,3},{1,0},{2,1},{3,2},{4,7},{5,4},{6,5},{7,6},{8,11},{9,8},{10,9... | collective-permute-start | bytes 122888 | tf_op jit(solution)/shard_map/ppermute | solution.py:829
  45.1 2.6 %copy-start.1 = (bf16[32,16,64]{2,1,0:T(8,128)(2,1)S(1)}, bf16[32,16,64]{2,1,0:T(8,128)(2,1)}, u32[]{:S(2)}) copy-start(bf16[32,16,64]{2,1,0:T(8,128)(2,1)} %refs_1_.1) | copy-start | bytes 196612
  45.1 2.6 %copy-start.5 = (bf16[256,64]{0,1:T(8,128)(2,1)S(1)}, bf16[256,64]{0,1:T(8,128)(2,1)}, u32[]{:S(2)}) copy-start(bf16[256,64]{0,1:T(8,128)(2,1)} %param.20) | copy-start | bytes 98308

commit v19 on v18

--- a/solution.py
+++ b/solution.py
@@ -105,6 +105,7 @@
     wf_ref,
     shard_ref,
     rows_ref,
+    mine_ref,
     left_ref,
     norm_ref,
     weights_ref,
@@ -159,6 +160,7 @@
     rows_ref[...] = shard_ref[: base + 2 * rows, :]
     left_ref[...] = shard_ref[:base, :]
     shard_ref[base + 2 * rows :, :] = right
+    mine_ref[...] = shard_ref[base + rows :, :]
 
 
 def join_left_kernel(ready, col_ref, rows0_ref, rows1_ref, rows2_ref, rows3_ref, out_ref):
@@ -266,22 +268,22 @@
                 rows.append(jnp.concatenate(pieces, axis=1))
         return jnp.concatenate(rows, axis=0)
 
-    def outer_of(n, carry):
+    def outer_of(n):
         block = jnp.concatenate([block_of(many * n + e) for e in range(many)], axis=1)
         for m in range(groups // chunk):
             out = nn_dot(lm_ref[m * chunk * fc : (m + 1) * chunk * fc, :], block)
             high, low = high_low(out)
             for e in range(many):
-                at = pl.ds(pl.multiple_of((many * n + e) * fc, fc), fc)
+                at = slice((many * n + e) * fc, (many * n + e + 1) * fc)
                 for g in range(chunk):
                     group = m * chunk + g
                     to = slice(group % wide * lanes, (group % wide + 1) * lanes)
                     cut = slice(g * fc, (g + 1) * fc), slice(e * lanes, (e + 1) * lanes)
                     oh_ref[group // wide, at, to] = high[cut]
                     ol_ref[group // wide, at, to] = low[cut]
-        return carry
-
-    lax.fori_loop(0, width_d // many, outer_of, 0, unroll=2)
+
+    for n in range(width_d // many):
+        outer_of(n)
 
     ready()
     some = z // fc
@@ -690,11 +692,12 @@
     l_rows = tokens // pack * fc
     r_rows = fd * tokens // 128 * seqs
     n_rows = half * tokens
-    shard, rows, own_left, normed, weights = call(
+    shard, rows, mine, own_left, normed, weights = call(
         prepare_kernel,
         (
             sds((l_rows + 2 * n_rows + r_rows, 128), bf16),
             sds((l_rows + 2 * n_rows, 128), bf16),
+            sds((n_rows + r_rows, 128), bf16),
             sds((l_rows, 128), bf16),
             sds((n_rows, 128), bf16),
             sds((width, 3 * chans), bf16),
@@ -722,7 +725,7 @@
 
     other = exchange(shard, 1)
     across = exchange(rows, 2)
-    pair = jnp.concatenate([x[l_rows + n_rows :] for x in (shard, other)], axis=0)
+    pair = jnp.concatenate([mine, other[l_rows + n_rows :]], axis=0)
     all_cols = [
         lax.ppermute(
             pair,

time: 50.7 us -> 50 us (0.986)
  Pallas kernels: 21.7 us -> 20.1 us
  starting transfers between devices: 18.7 us -> 19.6 us
  local copies, waits for them, and re-layouts: 3.52 us -> 2.62 us
  other arithmetic: 0.02 us -> 0.91 us
    pallas_call x10, Pallas kernels: 21.7 us -> 20.1 us  [run(): pl.pallas_call(body, out_shape=out_shape, in_specs=in_specs, out_specs=[p...]
    slice x2 -> x1, local copies, waits for them, and re-layouts: 0.91 us -> 0.01 us  [on_device(): pair = jnp.concatenate([mine, other[l_rows + n_rows:]], axis=0)]
    concatenate x1, other arithmetic: 0.02 us -> 0.91 us  [on_device(): pair = jnp.concatenate([mine, other[l_rows + n_rows:]], axis=0)]
    ppermute x7, starting transfers between devices: 9.07 us -> 9.89 us  [exchange(): return lax.ppermute(x, 'col', [(c, c ^ bit) for c in range(nk)])]
  transfers between devices with their start and end apart: 15 -> 15, of which waited for: 3 -> 3; matrix products, arithmetic and copies ran while one was open for 2% -> 2% of each run, Pallas kernels for 28% -> 25%
where the time goes in v19:
time: 50 us; the launch traced here: 49.2 us
  Pallas kernels  20.1 us (40%)
  starting transfers between devices  19.6 us (39%)
  waiting for transfers between devices  5.1 us (10%)
  local copies, waits for them, and re-layouts  2.62 us (5%)
  other arithmetic  0.91 us (2%)
  between operations  0.85 us (2%)
    pallas_call x10, Pallas kernels, run(): pl.pallas_call(body, out_shape=out_shape, in_specs=in_specs, out_specs=[p...  20.1 us
    ppermute x7, starting transfers between devices, exchange(): return lax.ppermute(x, 'col', [(c, c ^ bit) for c in range(nk)])  9.89 us
    ppermute x2, starting transfers between devices, on_device(): lax.ppermute(pair, ('row', 'col'), [(r * nk + c, (c ^ flip) * nk + r) for...  3.36 us
    ppermute x2, starting transfers between devices, over_seq(): return lax.ppermute(x, 'seq', [(0, 1), (1, 0)])  3.11 us
    unnamed x24, local copies, waits for them, and re-layouts  2.62 us
    ppermute x2, waiting for transfers between devices, over_seq(): return lax.ppermute(x, 'seq', [(0, 1), (1, 0)])  2.13 us
    ppermute x7, waiting for transfers between devices, exchange(): return lax.ppermute(x, 'col', [(c, c ^ bit) for c in range(nk)])  2.12 us
    ppermute x3, starting transfers between devices, on_device(): lax.ppermute(pay, 'col', [(c, (c + shift) % nk) for c in range(nk)])  2.11 us
  transfers between devices with their start and end apart: 15, of which 3 were waited for; matrix products, arithmetic and copies ran while one was open for 2% of the time, Pallas kernels for 25%

profile of v19, /device:TPU:0, one launch (start us, length us, event | category | flops | bytes accessed | tf_op | source)
XLA Modules:
  0.0 49.2 jit_solution(16837024600486844434)
XLA Ops:
  0.6 2.9 %shard_map.130 = (bf16[768,128]{1,0:T(8,128)(2,1)}, bf16[640,128]{1,0:T(8,128)(2,1)}, bf16[384,128]{1,0:T(8,128)(2,1)}, bf16[128,128]{1,0:T(8,128)(2,1)}, bf16[2...) custom-call(s32[1]{0:T(128)} %bitcast.2.refs_0_, bf16[32,16,64]{2,1,0:T(8,128)(2,1)} %refs_1_.1, bf16[32,16,64]{2,1,0:T(8,128)(2,1)} %refs_2_.1, ...), custom_call_target="tpu_custom_call" | custom-call | tf_op jit(solution)/shard_map/pallas_call | solution.py:62
  3.6 0.5 collective-permute-start.1
  4.0 2.6 %collective-permute-start = (bf16[640,128]{1,0:T(8,128)(2,1)}, bf16[640,128]{1,0:T(8,128)(2,1)S(1)}, u32[]{:S(2)}, u32[]{:S(2)}) collective-permute-start(bf16[640,128]{1,0:T(8,128)(2,1)} %get-tuple-element.38.refs_1_), channel_id=1, source_target_pairs={{0,2},{1,3},{2,0},{3,1},{4,6},{5,7},{6,4},{7,5},{8,10},{9,11},{10,... | collective-permute-start | bytes 491528 | tf_op jit(solution)/shard_map/ppermute | solution.py:724
  6.6 0.0 collective-permute-done.1.refs_2_.refs_3_
  6.6 0.9 %pad_maximum_fusion = bf16[768,128]{1,0:T(8,128)(2,1)S(1)} fusion(bf16[384,128]{1,0:T(8,128)(2,1)S(1)} %slice.4, bf16[384,128]{1,0:T(8,128)(2,1)} %get-tuple-element.44), kind=kLoop, calls=%fused_computation | loop fusion | flops 393216 | bytes 393216 | tf_op jit(solution)/shard_map/concatenate | solution.py:728
  7.5 2.7 %collective-permute-start.5 = (bf16[768,128]{1,0:T(8,128)(2,1)S(1)}, bf16[768,128]{1,0:T(8,128)(2,1)S(1)}, u32[]{:S(2)}, u32[]{:S(2)}) collective-permute-start(bf16[768,128]{1,0:T(8,128)(2,1)S(1)} %pad_maximum_fusion), channel_id=1, source_target_pairs={{0,8},{1,12},{2,0},{3,4},{4,9},{5,13},{6,1},{7,5},{8,10},{9,14},{1... | collective-permute-start | bytes 589832 | tf_op jit(solution)/shard_map/ppermute | solution.py:730
  10.2 0.7 %collective-permute-start.4 = (bf16[768,128]{1,0:T(8,128)(2,1)S(1)}, bf16[768,128]{1,0:T(8,128)(2,1)S(1)}, u32[]{:S(2)}, u32[]{:S(2)}) collective-permute-start(bf16[768,128]{1,0:T(8,128)(2,1)S(1)} %pad_maximum_fusion), channel_id=1, source_target_pairs={{0,0},{1,4},{2,8},{3,12},{4,1},{5,5},{6,9},{7,13},{8,2},{9,6},{10,... | collective-permute-start | bytes 589832 | tf_op jit(solution)/shard_map/ppermute | solution.py:730
  10.9 4.6 %collective-permute-start.2 = (bf16[128,128]{1,0:T(8,128)(2,1)}, bf16[128,128]{1,0:T(8,128)(2,1)S(1)}, u32[]{:S(2)}, u32[]{:S(2)}) collective-permute-start(bf16[128,128]{1,0:T(8,128)(2,1)} %get-tuple-element.39.refs_1_), channel_id=1, source_target_pairs={{0,3},{1,2},{2,1},{3,0},{4,7},{5,6},{6,5},{7,4},{8,11},{9,10},{10,... | collective-permute-start | bytes 98312 | tf_op jit(solution)/shard_map/ppermute | solution.py:724
  15.5 2.1 %collective-permute-done.2.refs_4_ = bf16[128,128]{1,0:T(8,128)(2,1)S(1)} collective-permute-done((bf16[128,128]{1,0:T(8,128)(2,1)}, bf16[128,128]{1,0:T(8,128)(2,1)S(1)}, u32[]{:S(2)}, u32[]{:S(2)}) %collective-permute-start.2) | collective-permute-done | bytes 32800 | tf_op jit(solution)/shard_map/ppermute | solution.py:724
  17.6 0.0 collective-permute-done.refs_3_.refs_4_
  17.6 0.0 copy-start.6
  17.6 0.8 %copy-done.6 = bf16[128,128]{1,0:T(8,128)(2,1)S(1)} copy-done((bf16[128,128]{1,0:T(8,128)(2,1)S(1)}, bf16[128,128]{1,0:T(8,128)(2,1)}, u32[]{:S(2)}) %copy-start.6) | copy-done | bytes 32792
  18.4 1.6 %collective-permute-start.3 = (bf16[512,128]{1,0:T(8,128)(2,1)S(1)}, bf16[512,128]{1,0:T(8,128)(2,1)S(1)}, u32[]{:S(2)}, u32[]{:S(2)}) collective-permute-start(bf16[512,128]{1,0:T(8,128)(2,1)S(1)} %shard_map.131.refs_2_), channel_id=1, source_target_pairs={{0,16},{16,0},{1,17},{17,1},{2,18},{18,2},{3,19},{19,3},{4,20},{20... | collective-permute-start | bytes 393224 | tf_op jit(solution)/shard_map/ppermute | solution.py:740
  20.0 0.0 copy-start
  20.0 0.9 %copy-done = bf16[640,128]{1,0:T(8,128)(2,1)S(1)} copy-done((bf16[640,128]{1,0:T(8,128)(2,1)S(1)}, bf16[640,128]{1,0:T(8,128)(2,1)}, u32[]{:S(2)}) %copy-start) | copy-done | bytes 163864
  20.9 0.0 copy-start.2
  20.9 0.9 %copy-done.2 = bf16[64,768]{1,0:T(8,128)(2,1)S(1)} copy-done((bf16[64,768]{1,0:T(8,128)(2,1)S(1)}, bf16[64,768]{1,0:T(8,128)(2,1)}, u32[]{:S(2)}) %copy-start.2) | copy-done | bytes 98328
  21.8 2.1 %collective-permute-done.3.refs_4_ = bf16[512,128]{1,0:T(8,128)(2,1)S(1)} collective-permute-done((bf16[512,128]{1,0:T(8,128)(2,1)S(1)}, bf16[512,128]{1,0:T(8,128)(2,1)S(1)}, u32[]{:S(2)}, u32[]{:S(2)}) %collective-permute-start.3) | collective-permute-done | bytes 131104 | tf_op jit(solution)/shard_map/ppermute | solution.py:740
  23.9 0.0 collective-permute-done.5.refs_7_.refs_2_
  23.9 0.0 collective-permute-done.4.refs_6_.refs_1_
  23.9 0.0 collective-permute-start.6
  24.0 0.0 copy-start.7
  24.0 0.0 copy-start.8
  24.0 0.0 copy-start.9
  24.0 0.0 copy-start.11
  24.0 1.6 %collective-permute-start.9 = (bf16[512,128]{1,0:T(8,128)(2,1)S(1)}, bf16[512,128]{1,0:T(8,128)(2,1)S(1)}, u32[]{:S(2)}, u32[]{:S(2)}) collective-permute-start(bf16[512,128]{1,0:T(8,128)(2,1)S(1)} %shard_map.134.refs_3_), channel_id=1, source_target_pairs={{0,16},{16,0},{1,17},{17,1},{2,18},{18,2},{3,19},{19,3},{4,20},{20... | collective-permute-start | bytes 393224 | tf_op jit(solution)/shard_map/ppermute | solution.py:740
  25.6 0.0 collective-permute-done.6.refs_5_
  25.6 2.3 %shard_map.133 = (f32[16,8,256]{2,1,0:T(8,128)S(1)}, bf16[4,16,16,128]{3,2,1,0:T(8,128)(2,1)S(1)}) custom-call(s32[1]{0:T(128)} %bitcast.1.refs_0_, s32[1]{0:T(128)} %bitcast.refs_0_.refs_1_, bf16[640,128]{1,0:T(8,128)(2,1)S(1)} %get-tuple-element.45.refs_2_, bf16[768,128]{1,0:T(8,128)(2,1)S(1)} %collective-permute-done.1.refs_2_.refs_3_, ...), custom_call_target="tpu_custom_call" | custom-call | flops 3000000000 | bytes 3000000 | tf_op jit(solution)/shard_map/pallas_call | solution.py:62
  27.9 1.9 %collective-permute-start.8 = (bf16[4,16,16,128]{3,2,1,0:T(8,128)(2,1)S(1)}, bf16[4,16,16,128]{3,2,1,0:T(8,128)(2,1)S(1)}, u32[]{:S(2)}, u32[]{:S(2)}) collective-permute-start(bf16[4,16,16,128]{3,2,1,0:T(8,128)(2,1)S(1)} %get-tuple-element.50.refs_1_), channel_id=1, source_target_pairs={{0,2},{1,3},{2,0},{3,1},{4,6},{5,7},{6,4},{7,5},{8,10},{9,11},{10,... | collective-permute-start | bytes 786440 | tf_op jit(solution)/shard_map/ppermute | solution.py:724
  29.8 0.0 collective-permute-start.7
  29.8 1.1 %collective-permute-start.10 = (f32[16,8,256]{2,1,0:T(8,128)S(1)}, f32[16,8,256]{2,1,0:T(8,128)S(1)}, u32[]{:S(2)}, u32[]{:S(2)}) collective-permute-start(f32[16,8,256]{2,1,0:T(8,128)S(1)} %get-tuple-element.53.refs_2_), channel_id=1, source_target_pairs={{0,16},{16,0},{1,17},{17,1},{2,18},{18,2},{3,19},{19,3},{4,20},{20... | collective-permute-start | bytes 393224 | tf_op jit(solution)/shard_map/ppermute | solution.py:780
  30.9 0.0 collective-permute-done.9.refs_5_
  30.9 0.0 copy-done.7
  30.9 0.0 copy-done.8
  30.9 0.0 copy-done.9
  30.9 0.0 copy-done.11
  30.9 0.0 copy-start.3
  30.9 0.0 copy-start.4
  31.0 0.0 copy-start.10
  31.0 8.3 %shard_map.135 = (bf16[4096,128]{1,0:T(8,128)(2,1)}, f32[16,128,256]{2,1,0:T(8,128)S(1)}, f32[16,8,256]{2,1,0:T(8,128)S(1)}, f32[16,8,256]{2,1,0:T(8,128)S(1)}) custom-call(s32[1]{0:T(128)} %bitcast.refs_0_.refs_1_, s32[1]{0:T(128)} %bitcast.7.refs_1_, bf16[512,128]{1,0:T(8,128)(2,1)S(1)} %shard_map.131.refs_2_, bf16[512,128]{1,0:T(8,128)(2,1)S(1)} %shard_map.134.refs_3_, ...), custom_call_target="tpu_custom_call" | custom-call | flops 14000000000 | bytes 5000000 | tf_op jit(solution)/shard_map/pallas_call | solution.py:62
  39.3 0.0 collective-permute-done.10.refs_3_
  39.3 0.5 shard_map.136
  39.8 0.0 collective-permute-done.8.refs_3_
  39.8 0.0 collective-permute-done.7.refs_2_
  39.8 0.3 collective-permute-start.14
  40.0 0.3 collective-permute-start.11
  40.3 0.8 %collective-permute-start.12 = (f32[10,8,128]{2,1,0:T(8,128)S(1)}, f32[10,8,128]{2,1,0:T(8,128)S(1)}, u32[]{:S(2)}, u32[]{:S(2)}) collective-permute-start(f32[10,8,128]{2,1,0:T(8,128)S(1)} %get-tuple-element.57), channel_id=1, source_target_pairs={{0,2},{1,3},{2,0},{3,1},{4,6},{5,7},{6,4},{7,5},{8,10},{9,11},{10,... | collective-permute-start | bytes 122888 | tf_op jit(solution)/shard_map/ppermute | solution.py:832
  41.1 1.0 %collective-permute-start.13 = (f32[10,8,128]{2,1,0:T(8,128)S(1)}, f32[10,8,128]{2,1,0:T(8,128)S(1)}, u32[]{:S(2)}, u32[]{:S(2)}) collective-permute-start(f32[10,8,128]{2,1,0:T(8,128)S(1)} %get-tuple-element.58), channel_id=1, source_target_pairs={{0,3},{1,0},{2,1},{3,2},{4,7},{5,4},{6,5},{7,6},{8,11},{9,8},{10,9... | collective-permute-start | bytes 122888 | tf_op jit(solution)/shard_map/ppermute | solution.py:832
  42.2 0.0 collective-permute-done.14.refs_4_
  42.2 0.0 copy-done.3
  42.2 0.0 copy-done.4
  42.2 0.0 copy-done.10
  42.2 1.3 %shard_map.137 = (bf16[16,256,512]{2,1,0:T(8,128)(2,1)S(1)}, f32[512,256]{1,0:T(8,128)S(1)}) custom-call(s32[1]{0:T(128)} %bitcast.refs_0_.refs_1_, bf16[4,16,16,128]{3,2,1,0:T(8,128)(2,1)S(1)} %get-tuple-element.50.refs_1_, bf16[4,16,16,128]{3,2,1,0:T(8,128)(2,1)S(1)} %collective-permute-done.7.refs_2_, ...), custom_call_target="tpu_custom_call" | custom-call | flops 4000000000 | bytes 6000000 | tf_op jit(solution)/shard_map/pallas_call | solution.py:62
  43.5 0.0 collective-permute-done.11.refs_2_.refs_1_
  43.5 0.8 %collective-permute-done.12.refs_3_.refs_2_ = f32[10,8,128]{2,1,0:T(8,128)S(1)} collective-permute-done((f32[10,8,128]{2,1,0:T(8,128)S(1)}, f32[10,8,128]{2,1,0:T(8,128)S(1)}, u32[]{:S(2)}, u32[]{:S(2)}) %collective-permute-start.12) | collective-permute-done | bytes 40992 | tf_op jit(solution)/shard_map/ppermute | solution.py:832
  44.4 0.0 collective-permute-done.13.refs_4_.refs_3_
  44.4 0.0 copy-start.1
  44.4 0.0 copy-start.5
  44.4 2.6 %shard_map.139 = bf16[4096,128]{1,0:T(8,128)(2,1)} custom-call(f32[10,8,128]{2,1,0:T(8,128)S(1)} %get-tuple-element.55.refs_1_.refs_0_, f32[10,8,128]{2,1,0:T(8,128)S(1)} %collective-permute-done.11.refs_2_.refs_1_, f32[10,8,128]{2,1,0:T(8,128)S(1)} %collective-permute-done.12.refs_3_.refs_2_, f32[10,8,128]{2,1,0:T(8,128)S(1)} %collective-permute-done.13.refs_4_.refs_3_, ...), custom_call_target="tpu_custom_call" | custom-call | flops 4000000000 | bytes 3000000 | tf_op jit(solution)/shard_map/pallas_call | solution.py:62
  47.0 0.0 copy-done.1
  47.0 0.0 copy-done.5
  47.0 2.2 %shard_map.138 = bf16[512,64]{1,0:T(8,128)(2,1)} custom-call(s32[1]{0:T(128)} %bitcast.refs_0_.refs_1_, f32[10,8,128]{2,1,0:T(8,128)S(1)} %get-tuple-element.55.refs_1_.refs_0_, f32[10,8,128]{2,1,0:T(8,128)S(1)} %collective-permute-done.11.refs_2_.refs_1_, f32[10,8,128]{2,1,0:T(8,128)S(1)} %collective-permute-done.12.refs_3_.refs_2_, ...), custom_call_target="tpu_custom_call" | custom-call | flops 3000000000 | bytes 5000000 | tf_op jit(solution)/shard_map/pallas_call | solution.py:62
  (4 shorter events, 0.1 us)
Async XLA Ops:
  3.6 3.0 %collective-permute-start.1 = (bf16[768,128]{1,0:T(8,128)(2,1)}, bf16[768,128]{1,0:T(8,128)(2,1)S(1)}, u32[]{:S(2)}, u32[]{:S(2)}) collective-permute-start(bf16[768,128]{1,0:T(8,128)(2,1)} %get-tuple-element.40), channel_id=1, source_target_pairs={{0,1},{1,0},{2,3},{3,2},{4,5},{5,4},{6,7},{7,6},{8,9},{9,8},{10,11... | collective-permute-start | bytes 589832 | tf_op jit(solution)/shard_map/ppermute | solution.py:724
  4.0 13.6 %collective-permute-start = (bf16[640,128]{1,0:T(8,128)(2,1)}, bf16[640,128]{1,0:T(8,128)(2,1)S(1)}, u32[]{:S(2)}, u32[]{:S(2)}) collective-permute-start(bf16[640,128]{1,0:T(8,128)(2,1)} %get-tuple-element.38.refs_1_), channel_id=1, source_target_pairs={{0,2},{1,3},{2,0},{3,1},{4,6},{5,7},{6,4},{7,5},{8,10},{9,11},{10,... | collective-permute-start | bytes 491528 | tf_op jit(solution)/shard_map/ppermute | solution.py:724
  7.5 16.4 %collective-permute-start.5 = (bf16[768,128]{1,0:T(8,128)(2,1)S(1)}, bf16[768,128]{1,0:T(8,128)(2,1)S(1)}, u32[]{:S(2)}, u32[]{:S(2)}) collective-permute-start(bf16[768,128]{1,0:T(8,128)(2,1)S(1)} %pad_maximum_fusion), channel_id=1, source_target_pairs={{0,8},{1,12},{2,0},{3,4},{4,9},{5,13},{6,1},{7,5},{8,10},{9,14},{1... | collective-permute-start | bytes 589832 | tf_op jit(solution)/shard_map/ppermute | solution.py:730
  10.2 13.7 %collective-permute-start.4 = (bf16[768,128]{1,0:T(8,128)(2,1)S(1)}, bf16[768,128]{1,0:T(8,128)(2,1)S(1)}, u32[]{:S(2)}, u32[]{:S(2)}) collective-permute-start(bf16[768,128]{1,0:T(8,128)(2,1)S(1)} %pad_maximum_fusion), channel_id=1, source_target_pairs={{0,0},{1,4},{2,8},{3,12},{4,1},{5,5},{6,9},{7,13},{8,2},{9,6},{10,... | collective-permute-start | bytes 589832 | tf_op jit(solution)/shard_map/ppermute | solution.py:730
  10.9 6.7 %collective-permute-start.2 = (bf16[128,128]{1,0:T(8,128)(2,1)}, bf16[128,128]{1,0:T(8,128)(2,1)S(1)}, u32[]{:S(2)}, u32[]{:S(2)}) collective-permute-start(bf16[128,128]{1,0:T(8,128)(2,1)} %get-tuple-element.39.refs_1_), channel_id=1, source_target_pairs={{0,3},{1,2},{2,1},{3,0},{4,7},{5,6},{6,5},{7,4},{8,11},{9,10},{10,... | collective-permute-start | bytes 98312 | tf_op jit(solution)/shard_map/ppermute | solution.py:724
  17.6 0.8 %copy-start.6 = (bf16[128,128]{1,0:T(8,128)(2,1)S(1)}, bf16[128,128]{1,0:T(8,128)(2,1)}, u32[]{:S(2)}) copy-start(bf16[128,128]{1,0:T(8,128)(2,1)} %get-tuple-element.39.refs_1_) | copy-start | bytes 98308
  18.4 5.5 %collective-permute-start.3 = (bf16[512,128]{1,0:T(8,128)(2,1)S(1)}, bf16[512,128]{1,0:T(8,128)(2,1)S(1)}, u32[]{:S(2)}, u32[]{:S(2)}) collective-permute-start(bf16[512,128]{1,0:T(8,128)(2,1)S(1)} %shard_map.131.refs_2_), channel_id=1, source_target_pairs={{0,16},{16,0},{1,17},{17,1},{2,18},{18,2},{3,19},{19,3},{4,20},{20... | collective-permute-start | bytes 393224 | tf_op jit(solution)/shard_map/ppermute | solution.py:740
  20.0 0.9 %copy-start = (bf16[640,128]{1,0:T(8,128)(2,1)S(1)}, bf16[640,128]{1,0:T(8,128)(2,1)}, u32[]{:S(2)}) copy-start(bf16[640,128]{1,0:T(8,128)(2,1)} %get-tuple-element.38.refs_1_) | copy-start | bytes 491524
  20.9 0.9 %copy-start.2 = (bf16[64,768]{1,0:T(8,128)(2,1)S(1)}, bf16[64,768]{1,0:T(8,128)(2,1)}, u32[]{:S(2)}) copy-start(bf16[64,768]{1,0:T(8,128)(2,1)} %get-tuple-element.41.refs_0_) | copy-start | bytes 294916
  23.9 1.6 %collective-permute-start.6 = (bf16[640,128]{1,0:T(8,128)(2,1)S(1)}, bf16[640,128]{1,0:T(8,128)(2,1)S(1)}, u32[]{:S(2)}, u32[]{:S(2)}) collective-permute-start(bf16[640,128]{1,0:T(8,128)(2,1)S(1)} %collective-permute-done.refs_3_.refs_4_), channel_id=1, source_target_pairs={{0,1},{1,0},{2,3},{3,2},{4,5},{5,4},{6,7},{7,6},{8,9},{9,8},{10,11... | collective-permute-start | bytes 491528 | tf_op jit(solution)/shard_map/ppermute | solution.py:724
  24.0 6.9 %copy-start.7 = (s32[256]{0:T(256)S(1)}, s32[256]{0:T(256)}, u32[]{:S(2)}) copy-start(s32[256]{0:T(256)} %param.13) | copy-start | bytes 3076
  24.0 6.9 %copy-start.8 = (bf16[64,64,128]{2,1,0:T(8,128)(2,1)S(1)}, bf16[64,64,128]{2,1,0:T(8,128)(2,1)}, u32[]{:S(2)}) copy-start(bf16[64,64,128]{2,1,0:T(8,128)(2,1)} %param.12) | copy-start | bytes 3145732
  24.0 6.9 %copy-start.9 = (f32[1024,128]{1,0:T(8,128)S(1)}, f32[1024,128]{1,0:T(8,128)}, u32[]{:S(2)}) copy-start(f32[1024,128]{1,0:T(8,128)} %refs_7_.4) | copy-start | bytes 1572868
  24.0 6.9 %copy-start.11 = (f32[128,8]{0,1:T(8,128)S(1)}, f32[128,8]{0,1:T(8,128)}, u32[]{:S(2)}) copy-start(f32[128,8]{0,1:T(8,128)} %param.19) | copy-start | bytes 12292
  24.0 6.9 %collective-permute-start.9 = (bf16[512,128]{1,0:T(8,128)(2,1)S(1)}, bf16[512,128]{1,0:T(8,128)(2,1)S(1)}, u32[]{:S(2)}, u32[]{:S(2)}) collective-permute-start(bf16[512,128]{1,0:T(8,128)(2,1)S(1)} %shard_map.134.refs_3_), channel_id=1, source_target_pairs={{0,16},{16,0},{1,17},{17,1},{2,18},{18,2},{3,19},{19,3},{4,20},{20... | collective-permute-start | bytes 393224 | tf_op jit(solution)/shard_map/ppermute | solution.py:740
  27.9 11.9 %collective-permute-start.8 = (bf16[4,16,16,128]{3,2,1,0:T(8,128)(2,1)S(1)}, bf16[4,16,16,128]{3,2,1,0:T(8,128)(2,1)S(1)}, u32[]{:S(2)}, u32[]{:S(2)}) collective-permute-start(bf16[4,16,16,128]{3,2,1,0:T(8,128)(2,1)S(1)} %get-tuple-element.50.refs_1_), channel_id=1, source_target_pairs={{0,2},{1,3},{2,0},{3,1},{4,6},{5,7},{6,4},{7,5},{8,10},{9,11},{10,... | collective-permute-start | bytes 786440 | tf_op jit(solution)/shard_map/ppermute | solution.py:724
  29.8 10.0 %collective-permute-start.7 = (bf16[4,16,16,128]{3,2,1,0:T(8,128)(2,1)S(1)}, bf16[4,16,16,128]{3,2,1,0:T(8,128)(2,1)S(1)}, u32[]{:S(2)}, u32[]{:S(2)}) collective-permute-start(bf16[4,16,16,128]{3,2,1,0:T(8,128)(2,1)S(1)} %get-tuple-element.50.refs_1_), channel_id=1, source_target_pairs={{0,1},{1,0},{2,3},{3,2},{4,5},{5,4},{6,7},{7,6},{8,9},{9,8},{10,11... | collective-permute-start | bytes 786440 | tf_op jit(solution)/shard_map/ppermute | solution.py:724
  29.8 9.5 %collective-permute-start.10 = (f32[16,8,256]{2,1,0:T(8,128)S(1)}, f32[16,8,256]{2,1,0:T(8,128)S(1)}, u32[]{:S(2)}, u32[]{:S(2)}) collective-permute-start(f32[16,8,256]{2,1,0:T(8,128)S(1)} %get-tuple-element.53.refs_2_), channel_id=1, source_target_pairs={{0,16},{16,0},{1,17},{17,1},{2,18},{18,2},{3,19},{19,3},{4,20},{20... | collective-permute-start | bytes 393224 | tf_op jit(solution)/shard_map/ppermute | solution.py:780
  30.9 11.2 %copy-start.3 = (bf16[64,256]{1,0:T(8,128)(2,1)S(1)}, bf16[64,256]{1,0:T(8,128)(2,1)}, u32[]{:S(2)}) copy-start(bf16[64,256]{1,0:T(8,128)(2,1)} %refs_5_.1) | copy-start | bytes 98308
  30.9 11.2 %copy-start.4 = (bf16[64,256]{1,0:T(8,128)(2,1)S(1)}, bf16[64,256]{1,0:T(8,128)(2,1)}, u32[]{:S(2)}) copy-start(bf16[64,256]{1,0:T(8,128)(2,1)} %refs_7_.5) | copy-start | bytes 98308
  31.0 11.2 %copy-start.10 = (bf16[256,128]{1,0:T(8,128)(2,1)S(1)}, bf16[256,128]{1,0:T(8,128)(2,1)}, u32[]{:S(2)}) copy-start(bf16[256,128]{1,0:T(8,128)(2,1)} %get-tuple-element.61.refs_6_) | copy-start | bytes 196612
  39.8 2.4 %collective-permute-start.14 = (bf16[4,16,16,128]{3,2,1,0:T(8,128)(2,1)S(1)}, bf16[4,16,16,128]{3,2,1,0:T(8,128)(2,1)S(1)}, u32[]{:S(2)}, u32[]{:S(2)}) collective-permute-start(bf16[4,16,16,128]{3,2,1,0:T(8,128)(2,1)S(1)} %collective-permute-done.8.refs_3_), channel_id=1, source_target_pairs={{0,1},{1,0},{2,3},{3,2},{4,5},{5,4},{6,7},{7,6},{8,9},{9,8},{10,11... | collective-permute-start | bytes 786440 | tf_op jit(solution)/shard_map/ppermute | solution.py:724
  40.0 3.5 %collective-permute-start.11 = (f32[10,8,128]{2,1,0:T(8,128)S(1)}, f32[10,8,128]{2,1,0:T(8,128)S(1)}, u32[]{:S(2)}, u32[]{:S(2)}) collective-permute-start(f32[10,8,128]{2,1,0:T(8,128)S(1)} %get-tuple-element.56), channel_id=1, source_target_pairs={{0,1},{1,2},{2,3},{3,0},{4,5},{5,6},{6,7},{7,4},{8,9},{9,10},{10,1... | collective-permute-start | bytes 122888 | tf_op jit(solution)/shard_map/ppermute | solution.py:832
  40.3 4.0 %collective-permute-start.12 = (f32[10,8,128]{2,1,0:T(8,128)S(1)}, f32[10,8,128]{2,1,0:T(8,128)S(1)}, u32[]{:S(2)}, u32[]{:S(2)}) collective-permute-start(f32[10,8,128]{2,1,0:T(8,128)S(1)} %get-tuple-element.57), channel_id=1, source_target_pairs={{0,2},{1,3},{2,0},{3,1},{4,6},{5,7},{6,4},{7,5},{8,10},{9,11},{10,... | collective-permute-start | bytes 122888 | tf_op jit(solution)/shard_map/ppermute | solution.py:832
  41.1 3.2 %collective-permute-start.13 = (f32[10,8,128]{2,1,0:T(8,128)S(1)}, f32[10,8,128]{2,1,0:T(8,128)S(1)}, u32[]{:S(2)}, u32[]{:S(2)}) collective-permute-start(f32[10,8,128]{2,1,0:T(8,128)S(1)} %get-tuple-element.58), channel_id=1, source_target_pairs={{0,3},{1,0},{2,1},{3,2},{4,7},{5,4},{6,5},{7,6},{8,11},{9,8},{10,9... | collective-permute-start | bytes 122888 | tf_op jit(solution)/shard_map/ppermute | solution.py:832
  44.4 2.6 %copy-start.1 = (bf16[32,16,64]{2,1,0:T(8,128)(2,1)S(1)}, bf16[32,16,64]{2,1,0:T(8,128)(2,1)}, u32[]{:S(2)}) copy-start(bf16[32,16,64]{2,1,0:T(8,128)(2,1)} %refs_1_.1) | copy-start | bytes 196612
  44.4 2.6 %copy-start.5 = (bf16[256,64]{0,1:T(8,128)(2,1)S(1)}, bf16[256,64]{0,1:T(8,128)(2,1)}, u32[]{:S(2)}) copy-start(bf16[256,64]{0,1:T(8,128)(2,1)} %param.20) | copy-start | bytes 98308

commit v20 on v19

--- a/solution.py
+++ b/solution.py
@@ -105,7 +105,6 @@
     wf_ref,
     shard_ref,
     rows_ref,
-    mine_ref,
     left_ref,
     norm_ref,
     weights_ref,
@@ -160,7 +159,6 @@
     rows_ref[...] = shard_ref[: base + 2 * rows, :]
     left_ref[...] = shard_ref[:base, :]
     shard_ref[base + 2 * rows :, :] = right
-    mine_ref[...] = shard_ref[base + rows :, :]
 
 
 def join_left_kernel(ready, col_ref, rows0_ref, rows1_ref, rows2_ref, rows3_ref, out_ref):
@@ -692,12 +690,11 @@
     l_rows = tokens // pack * fc
     r_rows = fd * tokens // 128 * seqs
     n_rows = half * tokens
-    shard, rows, mine, own_left, normed, weights = call(
+    shard, rows, own_left, normed, weights = call(
         prepare_kernel,
         (
             sds((l_rows + 2 * n_rows + r_rows, 128), bf16),
             sds((l_rows + 2 * n_rows, 128), bf16),
-            sds((n_rows + r_rows, 128), bf16),
             sds((l_rows, 128), bf16),
             sds((n_rows, 128), bf16),
             sds((width, 3 * chans), bf16),
@@ -725,7 +722,7 @@
 
     other = exchange(shard, 1)
     across = exchange(rows, 2)
-    pair = jnp.concatenate([mine, other[l_rows + n_rows :]], axis=0)
+    pair = jnp.concatenate([x[l_rows + n_rows :] for x in (shard, other)], axis=0)
     all_cols = [
         lax.ppermute(
             pair,

time: 50 us -> 49.2 us (0.984)
  starting transfers between devices: 19.6 us -> 18.7 us
  local copies, waits for them, and re-layouts: 2.62 us -> 3.52 us
  other arithmetic: 0.91 us -> 0.02 us
    slice x1 -> x2, local copies, waits for them, and re-layouts: 0.01 us -> 0.91 us  [on_device(): x[l_rows + n_rows:]]
    concatenate x1, other arithmetic: 0.91 us -> 0.02 us  [on_device(): jnp.concatenate([x[l_rows + n_rows:] for x in (shard, other)], axis=0)]
    ppermute x7, starting transfers between devices: 9.89 us -> 9.06 us  [exchange(): return lax.ppermute(x, 'col', [(c, c ^ bit) for c in range(nk)])]
  transfers between devices with their start and end apart: 15 -> 15, of which waited for: 3 -> 3; matrix products, arithmetic and copies ran while one was open for 2% -> 2% of each run, Pallas kernels for 25% -> 26%
where the time goes in v20:
time: 49.2 us; the launch traced here: 48.4 us
  Pallas kernels  20.1 us (41%)
  starting transfers between devices  18.7 us (38%)
  waiting for transfers between devices  5.14 us (10%)
  local copies, waits for them, and re-layouts  3.52 us (7%)
  between operations  0.86 us (2%)
    pallas_call x10, Pallas kernels, run(): pl.pallas_call(body, out_shape=out_shape, in_specs=in_specs, out_specs=[p...  20.1 us
    ppermute x7, starting transfers between devices, exchange(): return lax.ppermute(x, 'col', [(c, c ^ bit) for c in range(nk)])  9.06 us
    ppermute x2, starting transfers between devices, on_device(): lax.ppermute(pair, ('row', 'col'), [(r * nk + c, (c ^ flip) * nk + r) for...  3.3 us
    ppermute x2, starting transfers between devices, over_seq(): return lax.ppermute(x, 'seq', [(0, 1), (1, 0)])  3.11 us
    unnamed x24, local copies, waits for them, and re-layouts  2.62 us
    ppermute x2, waiting for transfers between devices, over_seq(): return lax.ppermute(x, 'seq', [(0, 1), (1, 0)])  2.37 us
    ppermute x3, starting transfers between devices, on_device(): lax.ppermute(pay, 'col', [(c, (c + shift) % nk) for c in range(nk)])  2.12 us
    ppermute x7, waiting for transfers between devices, exchange(): return lax.ppermute(x, 'col', [(c, c ^ bit) for c in range(nk)])  1.93 us
  transfers between devices with their start and end apart: 15, of which 3 were waited for; matrix products, arithmetic and copies ran while one was open for 2% of the time, Pallas kernels for 26%

profile of v20, /device:TPU:0, one launch (start us, length us, event | category | flops | bytes accessed | tf_op | source)
XLA Modules:
  0.0 48.4 jit_solution(10164278051745502300)
XLA Ops:
  0.6 2.9 %shard_map.130 = (bf16[768,128]{1,0:T(8,128)(2,1)}, bf16[640,128]{1,0:T(8,128)(2,1)}, bf16[128,128]{1,0:T(8,128)(2,1)}, bf16[256,128]{1,0:T(8,128)(2,1)}, bf16[64,768]{1,0:T(8,128)(2,1)}) custom-call(s32[1]{0:T(128)} %bitcast.2.refs_0_, bf16[32,16,64]{2,1,0:T(8,128)(2,1)} %refs_1_.1, bf16[32,16,64]{2,1,0:T(8,128)(2,1)} %refs_2_.1, bf16[32,64]{1,0:T(8,128)(2,1)} %bitcast.23, ...), custom_call_target="tpu_custom_call" | custom-call | tf_op jit(solution)/shard_map/pallas_call | solution.py:62
  3.6 0.5 collective-permute-start.1
  4.0 2.6 %collective-permute-start = (bf16[640,128]{1,0:T(8,128)(2,1)}, bf16[640,128]{1,0:T(8,128)(2,1)S(1)}, u32[]{:S(2)}, u32[]{:S(2)}) collective-permute-start(bf16[640,128]{1,0:T(8,128)(2,1)} %get-tuple-element.37.refs_1_), channel_id=1, source_target_pairs={{0,2},{1,3},{2,0},{3,1},{4,6},{5,7},{6,4},{7,5},{8,10},{9,11},{10,... | collective-permute-start | bytes 491528 | tf_op jit(solution)/shard_map/ppermute | solution.py:721
  6.6 0.9 %slice.6 = bf16[384,128]{1,0:T(8,128)(2,1)S(1)} slice(bf16[768,128]{1,0:T(8,128)(2,1)} %get-tuple-element.39), slice={[384:768], [0:128]} | slice | bytes 196608 | tf_op jit(solution)/shard_map/slice | solution.py:725
  7.5 0.0 collective-permute-done.1.refs_2_.refs_3_
  7.5 2.6 %collective-permute-start.5 = (bf16[768,128]{1,0:T(8,128)(2,1)S(1)}, bf16[768,128]{1,0:T(8,128)(2,1)S(1)}, u32[]{:S(2)}, u32[]{:S(2)}) collective-permute-start(bf16[768,128]{1,0:T(8,128)(2,1)S(1)} %pad_maximum_fusion), channel_id=1, source_target_pairs={{0,8},{1,12},{2,0},{3,4},{4,9},{5,13},{6,1},{7,5},{8,10},{9,14},{1... | collective-permute-start | bytes 589832 | tf_op jit(solution)/shard_map/ppermute | solution.py:727
  10.2 0.7 %collective-permute-start.4 = (bf16[768,128]{1,0:T(8,128)(2,1)S(1)}, bf16[768,128]{1,0:T(8,128)(2,1)S(1)}, u32[]{:S(2)}, u32[]{:S(2)}) collective-permute-start(bf16[768,128]{1,0:T(8,128)(2,1)S(1)} %pad_maximum_fusion), channel_id=1, source_target_pairs={{0,0},{1,4},{2,8},{3,12},{4,1},{5,5},{6,9},{7,13},{8,2},{9,6},{10,... | collective-permute-start | bytes 589832 | tf_op jit(solution)/shard_map/ppermute | solution.py:727
  10.8 3.8 %collective-permute-start.2 = (bf16[128,128]{1,0:T(8,128)(2,1)}, bf16[128,128]{1,0:T(8,128)(2,1)S(1)}, u32[]{:S(2)}, u32[]{:S(2)}) collective-permute-start(bf16[128,128]{1,0:T(8,128)(2,1)} %get-tuple-element.38.refs_1_), channel_id=1, source_target_pairs={{0,3},{1,2},{2,1},{3,0},{4,7},{5,6},{6,5},{7,4},{8,11},{9,10},{10,... | collective-permute-start | bytes 98312 | tf_op jit(solution)/shard_map/ppermute | solution.py:721
  14.6 1.9 %collective-permute-done.2.refs_4_ = bf16[128,128]{1,0:T(8,128)(2,1)S(1)} collective-permute-done((bf16[128,128]{1,0:T(8,128)(2,1)}, bf16[128,128]{1,0:T(8,128)(2,1)S(1)}, u32[]{:S(2)}, u32[]{:S(2)}) %collective-permute-start.2) | collective-permute-done | bytes 32800 | tf_op jit(solution)/shard_map/ppermute | solution.py:721
  16.5 0.0 collective-permute-done.refs_3_.refs_4_
  16.6 0.0 copy-start.6
  16.6 0.8 %copy-done.6 = bf16[128,128]{1,0:T(8,128)(2,1)S(1)} copy-done((bf16[128,128]{1,0:T(8,128)(2,1)S(1)}, bf16[128,128]{1,0:T(8,128)(2,1)}, u32[]{:S(2)}) %copy-start.6) | copy-done | bytes 32792
  17.3 1.6 %collective-permute-start.3 = (bf16[512,128]{1,0:T(8,128)(2,1)S(1)}, bf16[512,128]{1,0:T(8,128)(2,1)S(1)}, u32[]{:S(2)}, u32[]{:S(2)}) collective-permute-start(bf16[512,128]{1,0:T(8,128)(2,1)S(1)} %shard_map.131.refs_2_), channel_id=1, source_target_pairs={{0,16},{16,0},{1,17},{17,1},{2,18},{18,2},{3,19},{19,3},{4,20},{20... | collective-permute-start | bytes 393224 | tf_op jit(solution)/shard_map/ppermute | solution.py:737
  18.9 0.0 copy-start
  18.9 0.9 %copy-done = bf16[640,128]{1,0:T(8,128)(2,1)S(1)} copy-done((bf16[640,128]{1,0:T(8,128)(2,1)S(1)}, bf16[640,128]{1,0:T(8,128)(2,1)}, u32[]{:S(2)}) %copy-start) | copy-done | bytes 163864
  19.8 0.0 copy-start.2
  19.8 0.9 %copy-done.2 = bf16[64,768]{1,0:T(8,128)(2,1)S(1)} copy-done((bf16[64,768]{1,0:T(8,128)(2,1)S(1)}, bf16[64,768]{1,0:T(8,128)(2,1)}, u32[]{:S(2)}) %copy-start.2) | copy-done | bytes 98328
  20.7 2.4 %collective-permute-done.3.refs_4_ = bf16[512,128]{1,0:T(8,128)(2,1)S(1)} collective-permute-done((bf16[512,128]{1,0:T(8,128)(2,1)S(1)}, bf16[512,128]{1,0:T(8,128)(2,1)S(1)}, u32[]{:S(2)}, u32[]{:S(2)}) %collective-permute-start.3) | collective-permute-done | bytes 131104 | tf_op jit(solution)/shard_map/ppermute | solution.py:737
  23.1 0.0 collective-permute-done.5.refs_7_.refs_2_
  23.1 0.0 collective-permute-done.4.refs_6_.refs_1_
  23.1 0.0 collective-permute-start.6
  23.1 0.0 copy-start.7
  23.1 0.0 copy-start.8
  23.2 0.0 copy-start.9
  23.2 0.0 copy-start.11
  23.2 1.6 %collective-permute-start.9 = (bf16[512,128]{1,0:T(8,128)(2,1)S(1)}, bf16[512,128]{1,0:T(8,128)(2,1)S(1)}, u32[]{:S(2)}, u32[]{:S(2)}) collective-permute-start(bf16[512,128]{1,0:T(8,128)(2,1)S(1)} %shard_map.134.refs_3_), channel_id=1, source_target_pairs={{0,16},{16,0},{1,17},{17,1},{2,18},{18,2},{3,19},{19,3},{4,20},{20... | collective-permute-start | bytes 393224 | tf_op jit(solution)/shard_map/ppermute | solution.py:737
  24.7 0.0 collective-permute-done.6.refs_5_
  24.7 2.3 %shard_map.133 = (f32[16,8,256]{2,1,0:T(8,128)S(1)}, bf16[4,16,16,128]{3,2,1,0:T(8,128)(2,1)S(1)}) custom-call(s32[1]{0:T(128)} %bitcast.1.refs_0_, s32[1]{0:T(128)} %bitcast.refs_0_.refs_1_, bf16[640,128]{1,0:T(8,128)(2,1)S(1)} %get-tuple-element.43.refs_2_, bf16[768,128]{1,0:T(8,128)(2,1)S(1)} %collective-permute-done.1.refs_2_.refs_3_, ...), custom_call_target="tpu_custom_call" | custom-call | flops 3000000000 | bytes 3000000 | tf_op jit(solution)/shard_map/pallas_call | solution.py:62
  27.0 1.9 %collective-permute-start.8 = (bf16[4,16,16,128]{3,2,1,0:T(8,128)(2,1)S(1)}, bf16[4,16,16,128]{3,2,1,0:T(8,128)(2,1)S(1)}, u32[]{:S(2)}, u32[]{:S(2)}) collective-permute-start(bf16[4,16,16,128]{3,2,1,0:T(8,128)(2,1)S(1)} %get-tuple-element.48.refs_1_), channel_id=1, source_target_pairs={{0,2},{1,3},{2,0},{3,1},{4,6},{5,7},{6,4},{7,5},{8,10},{9,11},{10,... | collective-permute-start | bytes 786440 | tf_op jit(solution)/shard_map/ppermute | solution.py:721
  28.9 0.0 collective-permute-start.7
  28.9 1.1 %collective-permute-start.10 = (f32[16,8,256]{2,1,0:T(8,128)S(1)}, f32[16,8,256]{2,1,0:T(8,128)S(1)}, u32[]{:S(2)}, u32[]{:S(2)}) collective-permute-start(f32[16,8,256]{2,1,0:T(8,128)S(1)} %get-tuple-element.51.refs_2_), channel_id=1, source_target_pairs={{0,16},{16,0},{1,17},{17,1},{2,18},{18,2},{3,19},{19,3},{4,20},{20... | collective-permute-start | bytes 393224 | tf_op jit(solution)/shard_map/ppermute | solution.py:777
  30.1 0.0 collective-permute-done.9.refs_5_
  30.1 0.0 copy-done.7
  30.1 0.0 copy-done.8
  30.1 0.0 copy-done.9
  30.1 0.0 copy-done.11
  30.1 0.0 copy-start.3
  30.1 0.0 copy-start.4
  30.1 0.0 copy-start.10
  30.1 8.3 %shard_map.135 = (bf16[4096,128]{1,0:T(8,128)(2,1)}, f32[16,128,256]{2,1,0:T(8,128)S(1)}, f32[16,8,256]{2,1,0:T(8,128)S(1)}, f32[16,8,256]{2,1,0:T(8,128)S(1)}) custom-call(s32[1]{0:T(128)} %bitcast.refs_0_.refs_1_, s32[1]{0:T(128)} %bitcast.7.refs_1_, bf16[512,128]{1,0:T(8,128)(2,1)S(1)} %shard_map.131.refs_2_, bf16[512,128]{1,0:T(8,128)(2,1)S(1)} %shard_map.134.refs_3_, ...), custom_call_target="tpu_custom_call" | custom-call | flops 14000000000 | bytes 5000000 | tf_op jit(solution)/shard_map/pallas_call | solution.py:62
  38.4 0.0 collective-permute-done.10.refs_3_
  38.4 0.5 shard_map.136
  38.9 0.0 collective-permute-done.8.refs_3_
  38.9 0.0 collective-permute-done.7.refs_2_
  38.9 0.3 collective-permute-start.14
  39.2 0.3 collective-permute-start.11
  39.5 0.8 %collective-permute-start.12 = (f32[10,8,128]{2,1,0:T(8,128)S(1)}, f32[10,8,128]{2,1,0:T(8,128)S(1)}, u32[]{:S(2)}, u32[]{:S(2)}) collective-permute-start(f32[10,8,128]{2,1,0:T(8,128)S(1)} %get-tuple-element.55), channel_id=1, source_target_pairs={{0,2},{1,3},{2,0},{3,1},{4,6},{5,7},{6,4},{7,5},{8,10},{9,11},{10,... | collective-permute-start | bytes 122888 | tf_op jit(solution)/shard_map/ppermute | solution.py:829
  40.3 1.0 %collective-permute-start.13 = (f32[10,8,128]{2,1,0:T(8,128)S(1)}, f32[10,8,128]{2,1,0:T(8,128)S(1)}, u32[]{:S(2)}, u32[]{:S(2)}) collective-permute-start(f32[10,8,128]{2,1,0:T(8,128)S(1)} %get-tuple-element.56), channel_id=1, source_target_pairs={{0,3},{1,0},{2,1},{3,2},{4,7},{5,4},{6,5},{7,6},{8,11},{9,8},{10,9... | collective-permute-start | bytes 122888 | tf_op jit(solution)/shard_map/ppermute | solution.py:829
  41.3 0.0 collective-permute-done.14.refs_4_
  41.3 0.0 copy-done.3
  41.3 0.0 copy-done.4
  41.3 0.0 copy-done.10
  41.3 1.3 %shard_map.137 = (bf16[16,256,512]{2,1,0:T(8,128)(2,1)S(1)}, f32[512,256]{1,0:T(8,128)S(1)}) custom-call(s32[1]{0:T(128)} %bitcast.refs_0_.refs_1_, bf16[4,16,16,128]{3,2,1,0:T(8,128)(2,1)S(1)} %get-tuple-element.48.refs_1_, bf16[4,16,16,128]{3,2,1,0:T(8,128)(2,1)S(1)} %collective-permute-done.7.refs_2_, ...), custom_call_target="tpu_custom_call" | custom-call | flops 4000000000 | bytes 6000000 | tf_op jit(solution)/shard_map/pallas_call | solution.py:62
  42.7 0.0 collective-permute-done.11.refs_2_.refs_1_
  42.7 0.8 %collective-permute-done.12.refs_3_.refs_2_ = f32[10,8,128]{2,1,0:T(8,128)S(1)} collective-permute-done((f32[10,8,128]{2,1,0:T(8,128)S(1)}, f32[10,8,128]{2,1,0:T(8,128)S(1)}, u32[]{:S(2)}, u32[]{:S(2)}) %collective-permute-start.12) | collective-permute-done | bytes 40992 | tf_op jit(solution)/shard_map/ppermute | solution.py:829
  43.5 0.0 collective-permute-done.13.refs_4_.refs_3_
  43.5 0.0 copy-start.1
  43.5 0.0 copy-start.5
  43.5 2.6 %shard_map.139 = bf16[4096,128]{1,0:T(8,128)(2,1)} custom-call(f32[10,8,128]{2,1,0:T(8,128)S(1)} %get-tuple-element.53.refs_1_.refs_0_, f32[10,8,128]{2,1,0:T(8,128)S(1)} %collective-permute-done.11.refs_2_.refs_1_, f32[10,8,128]{2,1,0:T(8,128)S(1)} %collective-permute-done.12.refs_3_.refs_2_, f32[10,8,128]{2,1,0:T(8,128)S(1)} %collective-permute-done.13.refs_4_.refs_3_, ...), custom_call_target="tpu_custom_call" | custom-call | flops 4000000000 | bytes 3000000 | tf_op jit(solution)/shard_map/pallas_call | solution.py:62
  46.1 0.0 copy-done.1
  46.2 0.0 copy-done.5
  46.2 2.2 %shard_map.138 = bf16[512,64]{1,0:T(8,128)(2,1)} custom-call(s32[1]{0:T(128)} %bitcast.refs_0_.refs_1_, f32[10,8,128]{2,1,0:T(8,128)S(1)} %get-tuple-element.53.refs_1_.refs_0_, f32[10,8,128]{2,1,0:T(8,128)S(1)} %collective-permute-done.11.refs_2_.refs_1_, f32[10,8,128]{2,1,0:T(8,128)S(1)} %collective-permute-done.12.refs_3_.refs_2_, ...), custom_call_target="tpu_custom_call" | custom-call | flops 3000000000 | bytes 5000000 | tf_op jit(solution)/shard_map/pallas_call | solution.py:62
  (5 shorter events, 0.1 us)
Async XLA Ops:
  3.6 3.9 %collective-permute-start.1 = (bf16[768,128]{1,0:T(8,128)(2,1)}, bf16[768,128]{1,0:T(8,128)(2,1)S(1)}, u32[]{:S(2)}, u32[]{:S(2)}) collective-permute-start(bf16[768,128]{1,0:T(8,128)(2,1)} %get-tuple-element.39), channel_id=1, source_target_pairs={{0,1},{1,0},{2,3},{3,2},{4,5},{5,4},{6,7},{7,6},{8,9},{9,8},{10,11... | collective-permute-start | bytes 589832 | tf_op jit(solution)/shard_map/ppermute | solution.py:721
  4.0 12.5 %collective-permute-start = (bf16[640,128]{1,0:T(8,128)(2,1)}, bf16[640,128]{1,0:T(8,128)(2,1)S(1)}, u32[]{:S(2)}, u32[]{:S(2)}) collective-permute-start(bf16[640,128]{1,0:T(8,128)(2,1)} %get-tuple-element.37.refs_1_), channel_id=1, source_target_pairs={{0,2},{1,3},{2,0},{3,1},{4,6},{5,7},{6,4},{7,5},{8,10},{9,11},{10,... | collective-permute-start | bytes 491528 | tf_op jit(solution)/shard_map/ppermute | solution.py:721
  7.5 15.6 %collective-permute-start.5 = (bf16[768,128]{1,0:T(8,128)(2,1)S(1)}, bf16[768,128]{1,0:T(8,128)(2,1)S(1)}, u32[]{:S(2)}, u32[]{:S(2)}) collective-permute-start(bf16[768,128]{1,0:T(8,128)(2,1)S(1)} %pad_maximum_fusion), channel_id=1, source_target_pairs={{0,8},{1,12},{2,0},{3,4},{4,9},{5,13},{6,1},{7,5},{8,10},{9,14},{1... | collective-permute-start | bytes 589832 | tf_op jit(solution)/shard_map/ppermute | solution.py:727
  10.2 12.9 %collective-permute-start.4 = (bf16[768,128]{1,0:T(8,128)(2,1)S(1)}, bf16[768,128]{1,0:T(8,128)(2,1)S(1)}, u32[]{:S(2)}, u32[]{:S(2)}) collective-permute-start(bf16[768,128]{1,0:T(8,128)(2,1)S(1)} %pad_maximum_fusion), channel_id=1, source_target_pairs={{0,0},{1,4},{2,8},{3,12},{4,1},{5,5},{6,9},{7,13},{8,2},{9,6},{10,... | collective-permute-start | bytes 589832 | tf_op jit(solution)/shard_map/ppermute | solution.py:727
  10.8 5.7 %collective-permute-start.2 = (bf16[128,128]{1,0:T(8,128)(2,1)}, bf16[128,128]{1,0:T(8,128)(2,1)S(1)}, u32[]{:S(2)}, u32[]{:S(2)}) collective-permute-start(bf16[128,128]{1,0:T(8,128)(2,1)} %get-tuple-element.38.refs_1_), channel_id=1, source_target_pairs={{0,3},{1,2},{2,1},{3,0},{4,7},{5,6},{6,5},{7,4},{8,11},{9,10},{10,... | collective-permute-start | bytes 98312 | tf_op jit(solution)/shard_map/ppermute | solution.py:721
  16.6 0.8 %copy-start.6 = (bf16[128,128]{1,0:T(8,128)(2,1)S(1)}, bf16[128,128]{1,0:T(8,128)(2,1)}, u32[]{:S(2)}) copy-start(bf16[128,128]{1,0:T(8,128)(2,1)} %get-tuple-element.38.refs_1_) | copy-start | bytes 98308
  17.3 5.8 %collective-permute-start.3 = (bf16[512,128]{1,0:T(8,128)(2,1)S(1)}, bf16[512,128]{1,0:T(8,128)(2,1)S(1)}, u32[]{:S(2)}, u32[]{:S(2)}) collective-permute-start(bf16[512,128]{1,0:T(8,128)(2,1)S(1)} %shard_map.131.refs_2_), channel_id=1, source_target_pairs={{0,16},{16,0},{1,17},{17,1},{2,18},{18,2},{3,19},{19,3},{4,20},{20... | collective-permute-start | bytes 393224 | tf_op jit(solution)/shard_map/ppermute | solution.py:737
  18.9 0.9 %copy-start = (bf16[640,128]{1,0:T(8,128)(2,1)S(1)}, bf16[640,128]{1,0:T(8,128)(2,1)}, u32[]{:S(2)}) copy-start(bf16[640,128]{1,0:T(8,128)(2,1)} %get-tuple-element.37.refs_1_) | copy-start | bytes 491524
  19.8 0.9 %copy-start.2 = (bf16[64,768]{1,0:T(8,128)(2,1)S(1)}, bf16[64,768]{1,0:T(8,128)(2,1)}, u32[]{:S(2)}) copy-start(bf16[64,768]{1,0:T(8,128)(2,1)} %get-tuple-element.40.refs_0_) | copy-start | bytes 294916
  23.1 1.6 %collective-permute-start.6 = (bf16[640,128]{1,0:T(8,128)(2,1)S(1)}, bf16[640,128]{1,0:T(8,128)(2,1)S(1)}, u32[]{:S(2)}, u32[]{:S(2)}) collective-permute-start(bf16[640,128]{1,0:T(8,128)(2,1)S(1)} %collective-permute-done.refs_3_.refs_4_), channel_id=1, source_target_pairs={{0,1},{1,0},{2,3},{3,2},{4,5},{5,4},{6,7},{7,6},{8,9},{9,8},{10,11... | collective-permute-start | bytes 491528 | tf_op jit(solution)/shard_map/ppermute | solution.py:721
  23.1 6.9 %copy-start.7 = (s32[256]{0:T(256)S(1)}, s32[256]{0:T(256)}, u32[]{:S(2)}) copy-start(s32[256]{0:T(256)} %param.13) | copy-start | bytes 3076
  23.1 6.9 %copy-start.8 = (bf16[64,64,128]{2,1,0:T(8,128)(2,1)S(1)}, bf16[64,64,128]{2,1,0:T(8,128)(2,1)}, u32[]{:S(2)}) copy-start(bf16[64,64,128]{2,1,0:T(8,128)(2,1)} %param.12) | copy-start | bytes 3145732
  23.2 6.9 %copy-start.9 = (f32[1024,128]{1,0:T(8,128)S(1)}, f32[1024,128]{1,0:T(8,128)}, u32[]{:S(2)}) copy-start(f32[1024,128]{1,0:T(8,128)} %refs_7_.4) | copy-start | bytes 1572868
  23.2 6.9 %copy-start.11 = (f32[128,8]{0,1:T(8,128)S(1)}, f32[128,8]{0,1:T(8,128)}, u32[]{:S(2)}) copy-start(f32[128,8]{0,1:T(8,128)} %param.19) | copy-start | bytes 12292
  23.2 6.9 %collective-permute-start.9 = (bf16[512,128]{1,0:T(8,128)(2,1)S(1)}, bf16[512,128]{1,0:T(8,128)(2,1)S(1)}, u32[]{:S(2)}, u32[]{:S(2)}) collective-permute-start(bf16[512,128]{1,0:T(8,128)(2,1)S(1)} %shard_map.134.refs_3_), channel_id=1, source_target_pairs={{0,16},{16,0},{1,17},{17,1},{2,18},{18,2},{3,19},{19,3},{4,20},{20... | collective-permute-start | bytes 393224 | tf_op jit(solution)/shard_map/ppermute | solution.py:737
  27.0 11.9 %collective-permute-start.8 = (bf16[4,16,16,128]{3,2,1,0:T(8,128)(2,1)S(1)}, bf16[4,16,16,128]{3,2,1,0:T(8,128)(2,1)S(1)}, u32[]{:S(2)}, u32[]{:S(2)}) collective-permute-start(bf16[4,16,16,128]{3,2,1,0:T(8,128)(2,1)S(1)} %get-tuple-element.48.refs_1_), channel_id=1, source_target_pairs={{0,2},{1,3},{2,0},{3,1},{4,6},{5,7},{6,4},{7,5},{8,10},{9,11},{10,... | collective-permute-start | bytes 786440 | tf_op jit(solution)/shard_map/ppermute | solution.py:721
  28.9 10.0 %collective-permute-start.7 = (bf16[4,16,16,128]{3,2,1,0:T(8,128)(2,1)S(1)}, bf16[4,16,16,128]{3,2,1,0:T(8,128)(2,1)S(1)}, u32[]{:S(2)}, u32[]{:S(2)}) collective-permute-start(bf16[4,16,16,128]{3,2,1,0:T(8,128)(2,1)S(1)} %get-tuple-element.48.refs_1_), channel_id=1, source_target_pairs={{0,1},{1,0},{2,3},{3,2},{4,5},{5,4},{6,7},{7,6},{8,9},{9,8},{10,11... | collective-permute-start | bytes 786440 | tf_op jit(solution)/shard_map/ppermute | solution.py:721
  28.9 9.5 %collective-permute-start.10 = (f32[16,8,256]{2,1,0:T(8,128)S(1)}, f32[16,8,256]{2,1,0:T(8,128)S(1)}, u32[]{:S(2)}, u32[]{:S(2)}) collective-permute-start(f32[16,8,256]{2,1,0:T(8,128)S(1)} %get-tuple-element.51.refs_2_), channel_id=1, source_target_pairs={{0,16},{16,0},{1,17},{17,1},{2,18},{18,2},{3,19},{19,3},{4,20},{20... | collective-permute-start | bytes 393224 | tf_op jit(solution)/shard_map/ppermute | solution.py:777
  30.1 11.2 %copy-start.3 = (bf16[64,256]{1,0:T(8,128)(2,1)S(1)}, bf16[64,256]{1,0:T(8,128)(2,1)}, u32[]{:S(2)}) copy-start(bf16[64,256]{1,0:T(8,128)(2,1)} %refs_5_.1) | copy-start | bytes 98308
  30.1 11.2 %copy-start.4 = (bf16[64,256]{1,0:T(8,128)(2,1)S(1)}, bf16[64,256]{1,0:T(8,128)(2,1)}, u32[]{:S(2)}) copy-start(bf16[64,256]{1,0:T(8,128)(2,1)} %refs_7_.5) | copy-start | bytes 98308
  30.1 11.2 %copy-start.10 = (bf16[256,128]{1,0:T(8,128)(2,1)S(1)}, bf16[256,128]{1,0:T(8,128)(2,1)}, u32[]{:S(2)}) copy-start(bf16[256,128]{1,0:T(8,128)(2,1)} %get-tuple-element.59.refs_6_) | copy-start | bytes 196612
  38.9 2.4 %collective-permute-start.14 = (bf16[4,16,16,128]{3,2,1,0:T(8,128)(2,1)S(1)}, bf16[4,16,16,128]{3,2,1,0:T(8,128)(2,1)S(1)}, u32[]{:S(2)}, u32[]{:S(2)}) collective-permute-start(bf16[4,16,16,128]{3,2,1,0:T(8,128)(2,1)S(1)} %collective-permute-done.8.refs_3_), channel_id=1, source_target_pairs={{0,1},{1,0},{2,3},{3,2},{4,5},{5,4},{6,7},{7,6},{8,9},{9,8},{10,11... | collective-permute-start | bytes 786440 | tf_op jit(solution)/shard_map/ppermute | solution.py:721
  39.2 3.5 %collective-permute-start.11 = (f32[10,8,128]{2,1,0:T(8,128)S(1)}, f32[10,8,128]{2,1,0:T(8,128)S(1)}, u32[]{:S(2)}, u32[]{:S(2)}) collective-permute-start(f32[10,8,128]{2,1,0:T(8,128)S(1)} %get-tuple-element.54), channel_id=1, source_target_pairs={{0,1},{1,2},{2,3},{3,0},{4,5},{5,6},{6,7},{7,4},{8,9},{9,10},{10,1... | collective-permute-start | bytes 122888 | tf_op jit(solution)/shard_map/ppermute | solution.py:829
  39.5 4.0 %collective-permute-start.12 = (f32[10,8,128]{2,1,0:T(8,128)S(1)}, f32[10,8,128]{2,1,0:T(8,128)S(1)}, u32[]{:S(2)}, u32[]{:S(2)}) collective-permute-start(f32[10,8,128]{2,1,0:T(8,128)S(1)} %get-tuple-element.55), channel_id=1, source_target_pairs={{0,2},{1,3},{2,0},{3,1},{4,6},{5,7},{6,4},{7,5},{8,10},{9,11},{10,... | collective-permute-start | bytes 122888 | tf_op jit(solution)/shard_map/ppermute | solution.py:829
  40.3 3.2 %collective-permute-start.13 = (f32[10,8,128]{2,1,0:T(8,128)S(1)}, f32[10,8,128]{2,1,0:T(8,128)S(1)}, u32[]{:S(2)}, u32[]{:S(2)}) collective-permute-start(f32[10,8,128]{2,1,0:T(8,128)S(1)} %get-tuple-element.56), channel_id=1, source_target_pairs={{0,3},{1,0},{2,1},{3,2},{4,7},{5,4},{6,5},{7,6},{8,11},{9,8},{10,9... | collective-permute-start | bytes 122888 | tf_op jit(solution)/shard_map/ppermute | solution.py:829
  43.5 2.6 %copy-start.1 = (bf16[32,16,64]{2,1,0:T(8,128)(2,1)S(1)}, bf16[32,16,64]{2,1,0:T(8,128)(2,1)}, u32[]{:S(2)}) copy-start(bf16[32,16,64]{2,1,0:T(8,128)(2,1)} %refs_1_.1) | copy-start | bytes 196612
  43.5 2.6 %copy-start.5 = (bf16[256,64]{0,1:T(8,128)(2,1)S(1)}, bf16[256,64]{0,1:T(8,128)(2,1)}, u32[]{:S(2)}) copy-start(bf16[256,64]{0,1:T(8,128)(2,1)} %param.20) | copy-start | bytes 98308

commit v21 on v20

--- a/solution.py
+++ b/solution.py
@@ -250,7 +250,7 @@
                 at = (q * blocks + n) * seqs
                 rab_ref[n * size + e, q * seqs : (q + 1) * seqs, :] = res[at : at + seqs]
 
-    chunk = 8
+    chunk = 4
     many = 4
     wide = oh_ref.shape[2] // lanes
     empty = jnp.zeros((seqs, 2 * tile_j), bf16)

time: 49.2 us -> 49.2 us (level)
  no operation moved by 1% of the time
where the time goes in v21:
time: 49.2 us; the launch traced here: 48.4 us
  Pallas kernels  20.1 us (41%)
  starting transfers between devices  18.7 us (38%)
  waiting for transfers between devices  5.15 us (10%)
  local copies, waits for them, and re-layouts  3.52 us (7%)
  between operations  0.86 us (2%)
    pallas_call x10, Pallas kernels, run(): pl.pallas_call(body, out_shape=out_shape, in_specs=in_specs, out_specs=[p...  20.1 us
    ppermute x7, starting transfers between devices, exchange(): return lax.ppermute(x, 'col', [(c, c ^ bit) for c in range(nk)])  9.06 us
    ppermute x2, starting transfers between devices, on_device(): lax.ppermute(pair, ('row', 'col'), [(r * nk + c, (c ^ flip) * nk + r) for...  3.3 us
    ppermute x2, starting transfers between devices, over_seq(): return lax.ppermute(x, 'seq', [(0, 1), (1, 0)])  3.11 us
    unnamed x24, local copies, waits for them, and re-layouts  2.62 us
    ppermute x2, waiting for transfers between devices, over_seq(): return lax.ppermute(x, 'seq', [(0, 1), (1, 0)])  2.37 us
    ppermute x3, starting transfers between devices, on_device(): lax.ppermute(pay, 'col', [(c, (c + shift) % nk) for c in range(nk)])  2.12 us
    ppermute x7, waiting for transfers between devices, exchange(): return lax.ppermute(x, 'col', [(c, c ^ bit) for c in range(nk)])  1.93 us
  transfers between devices with their start and end apart: 15, of which 3 were waited for; matrix products, arithmetic and copies ran while one was open for 2% of the time, Pallas kernels for 26%

profile of v21, /device:TPU:0, one launch (start us, length us, event | category | flops | bytes accessed | tf_op | source)
XLA Modules:
  0.0 48.4 jit_solution(7869058334480044754)
XLA Ops:
  0.6 2.9 %shard_map.130 = (bf16[768,128]{1,0:T(8,128)(2,1)}, bf16[640,128]{1,0:T(8,128)(2,1)}, bf16[128,128]{1,0:T(8,128)(2,1)}, bf16[256,128]{1,0:T(8,128)(2,1)}, bf16[64,768]{1,0:T(8,128)(2,1)}) custom-call(s32[1]{0:T(128)} %bitcast.2.refs_0_, bf16[32,16,64]{2,1,0:T(8,128)(2,1)} %refs_1_.1, bf16[32,16,64]{2,1,0:T(8,128)(2,1)} %refs_2_.1, bf16[32,64]{1,0:T(8,128)(2,1)} %bitcast.23, ...), custom_call_target="tpu_custom_call" | custom-call | tf_op jit(solution)/shard_map/pallas_call | solution.py:62
  3.6 0.5 collective-permute-start.1
  4.0 2.6 %collective-permute-start = (bf16[640,128]{1,0:T(8,128)(2,1)}, bf16[640,128]{1,0:T(8,128)(2,1)S(1)}, u32[]{:S(2)}, u32[]{:S(2)}) collective-permute-start(bf16[640,128]{1,0:T(8,128)(2,1)} %get-tuple-element.37.refs_1_), channel_id=1, source_target_pairs={{0,2},{1,3},{2,0},{3,1},{4,6},{5,7},{6,4},{7,5},{8,10},{9,11},{10,... | collective-permute-start | bytes 491528 | tf_op jit(solution)/shard_map/ppermute | solution.py:721
  6.6 0.9 %slice.6 = bf16[384,128]{1,0:T(8,128)(2,1)S(1)} slice(bf16[768,128]{1,0:T(8,128)(2,1)} %get-tuple-element.39), slice={[384:768], [0:128]} | slice | bytes 196608 | tf_op jit(solution)/shard_map/slice | solution.py:725
  7.5 0.0 collective-permute-done.1.refs_2_.refs_3_
  7.5 2.6 %collective-permute-start.5 = (bf16[768,128]{1,0:T(8,128)(2,1)S(1)}, bf16[768,128]{1,0:T(8,128)(2,1)S(1)}, u32[]{:S(2)}, u32[]{:S(2)}) collective-permute-start(bf16[768,128]{1,0:T(8,128)(2,1)S(1)} %pad_maximum_fusion), channel_id=1, source_target_pairs={{0,8},{1,12},{2,0},{3,4},{4,9},{5,13},{6,1},{7,5},{8,10},{9,14},{1... | collective-permute-start | bytes 589832 | tf_op jit(solution)/shard_map/ppermute | solution.py:727
  10.2 0.7 %collective-permute-start.4 = (bf16[768,128]{1,0:T(8,128)(2,1)S(1)}, bf16[768,128]{1,0:T(8,128)(2,1)S(1)}, u32[]{:S(2)}, u32[]{:S(2)}) collective-permute-start(bf16[768,128]{1,0:T(8,128)(2,1)S(1)} %pad_maximum_fusion), channel_id=1, source_target_pairs={{0,0},{1,4},{2,8},{3,12},{4,1},{5,5},{6,9},{7,13},{8,2},{9,6},{10,... | collective-permute-start | bytes 589832 | tf_op jit(solution)/shard_map/ppermute | solution.py:727
  10.8 3.8 %collective-permute-start.2 = (bf16[128,128]{1,0:T(8,128)(2,1)}, bf16[128,128]{1,0:T(8,128)(2,1)S(1)}, u32[]{:S(2)}, u32[]{:S(2)}) collective-permute-start(bf16[128,128]{1,0:T(8,128)(2,1)} %get-tuple-element.38.refs_1_), channel_id=1, source_target_pairs={{0,3},{1,2},{2,1},{3,0},{4,7},{5,6},{6,5},{7,4},{8,11},{9,10},{10,... | collective-permute-start | bytes 98312 | tf_op jit(solution)/shard_map/ppermute | solution.py:721
  14.6 1.9 %collective-permute-done.2.refs_4_ = bf16[128,128]{1,0:T(8,128)(2,1)S(1)} collective-permute-done((bf16[128,128]{1,0:T(8,128)(2,1)}, bf16[128,128]{1,0:T(8,128)(2,1)S(1)}, u32[]{:S(2)}, u32[]{:S(2)}) %collective-permute-start.2) | collective-permute-done | bytes 32800 | tf_op jit(solution)/shard_map/ppermute | solution.py:721
  16.5 0.0 collective-permute-done.refs_3_.refs_4_
  16.6 0.0 copy-start.6
  16.6 0.8 %copy-done.6 = bf16[128,128]{1,0:T(8,128)(2,1)S(1)} copy-done((bf16[128,128]{1,0:T(8,128)(2,1)S(1)}, bf16[128,128]{1,0:T(8,128)(2,1)}, u32[]{:S(2)}) %copy-start.6) | copy-done | bytes 32792
  17.3 1.6 %collective-permute-start.3 = (bf16[512,128]{1,0:T(8,128)(2,1)S(1)}, bf16[512,128]{1,0:T(8,128)(2,1)S(1)}, u32[]{:S(2)}, u32[]{:S(2)}) collective-permute-start(bf16[512,128]{1,0:T(8,128)(2,1)S(1)} %shard_map.131.refs_2_), channel_id=1, source_target_pairs={{0,16},{16,0},{1,17},{17,1},{2,18},{18,2},{3,19},{19,3},{4,20},{20... | collective-permute-start | bytes 393224 | tf_op jit(solution)/shard_map/ppermute | solution.py:737
  18.9 0.0 copy-start
  18.9 0.9 %copy-done = bf16[640,128]{1,0:T(8,128)(2,1)S(1)} copy-done((bf16[640,128]{1,0:T(8,128)(2,1)S(1)}, bf16[640,128]{1,0:T(8,128)(2,1)}, u32[]{:S(2)}) %copy-start) | copy-done | bytes 163864
  19.8 0.0 copy-start.2
  19.8 0.9 %copy-done.2 = bf16[64,768]{1,0:T(8,128)(2,1)S(1)} copy-done((bf16[64,768]{1,0:T(8,128)(2,1)S(1)}, bf16[64,768]{1,0:T(8,128)(2,1)}, u32[]{:S(2)}) %copy-start.2) | copy-done | bytes 98328
  20.7 2.4 %collective-permute-done.3.refs_4_ = bf16[512,128]{1,0:T(8,128)(2,1)S(1)} collective-permute-done((bf16[512,128]{1,0:T(8,128)(2,1)S(1)}, bf16[512,128]{1,0:T(8,128)(2,1)S(1)}, u32[]{:S(2)}, u32[]{:S(2)}) %collective-permute-start.3) | collective-permute-done | bytes 131104 | tf_op jit(solution)/shard_map/ppermute | solution.py:737
  23.1 0.0 collective-permute-done.5.refs_7_.refs_2_
  23.1 0.0 collective-permute-done.4.refs_6_.refs_1_
  23.1 0.0 collective-permute-start.6
  23.1 0.0 copy-start.7
  23.1 0.0 copy-start.8
  23.2 0.0 copy-start.9
  23.2 0.0 copy-start.11
  23.2 1.6 %collective-permute-start.9 = (bf16[512,128]{1,0:T(8,128)(2,1)S(1)}, bf16[512,128]{1,0:T(8,128)(2,1)S(1)}, u32[]{:S(2)}, u32[]{:S(2)}) collective-permute-start(bf16[512,128]{1,0:T(8,128)(2,1)S(1)} %shard_map.134.refs_3_), channel_id=1, source_target_pairs={{0,16},{16,0},{1,17},{17,1},{2,18},{18,2},{3,19},{19,3},{4,20},{20... | collective-permute-start | bytes 393224 | tf_op jit(solution)/shard_map/ppermute | solution.py:737
  24.7 0.0 collective-permute-done.6.refs_5_
  24.7 2.3 %shard_map.133 = (f32[16,8,256]{2,1,0:T(8,128)S(1)}, bf16[4,16,16,128]{3,2,1,0:T(8,128)(2,1)S(1)}) custom-call(s32[1]{0:T(128)} %bitcast.1.refs_0_, s32[1]{0:T(128)} %bitcast.refs_0_.refs_1_, bf16[640,128]{1,0:T(8,128)(2,1)S(1)} %get-tuple-element.43.refs_2_, bf16[768,128]{1,0:T(8,128)(2,1)S(1)} %collective-permute-done.1.refs_2_.refs_3_, ...), custom_call_target="tpu_custom_call" | custom-call | flops 3000000000 | bytes 3000000 | tf_op jit(solution)/shard_map/pallas_call | solution.py:62
  27.0 1.9 %collective-permute-start.8 = (bf16[4,16,16,128]{3,2,1,0:T(8,128)(2,1)S(1)}, bf16[4,16,16,128]{3,2,1,0:T(8,128)(2,1)S(1)}, u32[]{:S(2)}, u32[]{:S(2)}) collective-permute-start(bf16[4,16,16,128]{3,2,1,0:T(8,128)(2,1)S(1)} %get-tuple-element.48.refs_1_), channel_id=1, source_target_pairs={{0,2},{1,3},{2,0},{3,1},{4,6},{5,7},{6,4},{7,5},{8,10},{9,11},{10,... | collective-permute-start | bytes 786440 | tf_op jit(solution)/shard_map/ppermute | solution.py:721
  28.9 0.0 collective-permute-start.7
  28.9 1.1 %collective-permute-start.10 = (f32[16,8,256]{2,1,0:T(8,128)S(1)}, f32[16,8,256]{2,1,0:T(8,128)S(1)}, u32[]{:S(2)}, u32[]{:S(2)}) collective-permute-start(f32[16,8,256]{2,1,0:T(8,128)S(1)} %get-tuple-element.51.refs_2_), channel_id=1, source_target_pairs={{0,16},{16,0},{1,17},{17,1},{2,18},{18,2},{3,19},{19,3},{4,20},{20... | collective-permute-start | bytes 393224 | tf_op jit(solution)/shard_map/ppermute | solution.py:777
  30.1 0.0 collective-permute-done.9.refs_5_
  30.1 0.0 copy-done.7
  30.1 0.0 copy-done.8
  30.1 0.0 copy-done.9
  30.1 0.0 copy-done.11
  30.1 0.0 copy-start.3
  30.1 0.0 copy-start.4
  30.1 0.0 copy-start.10
  30.1 8.3 %shard_map.135 = (bf16[4096,128]{1,0:T(8,128)(2,1)}, f32[16,128,256]{2,1,0:T(8,128)S(1)}, f32[16,8,256]{2,1,0:T(8,128)S(1)}, f32[16,8,256]{2,1,0:T(8,128)S(1)}) custom-call(s32[1]{0:T(128)} %bitcast.refs_0_.refs_1_, s32[1]{0:T(128)} %bitcast.7.refs_1_, bf16[512,128]{1,0:T(8,128)(2,1)S(1)} %shard_map.131.refs_2_, bf16[512,128]{1,0:T(8,128)(2,1)S(1)} %shard_map.134.refs_3_, ...), custom_call_target="tpu_custom_call" | custom-call | flops 14000000000 | bytes 5000000 | tf_op jit(solution)/shard_map/pallas_call | solution.py:62
  38.4 0.0 collective-permute-done.10.refs_3_
  38.4 0.5 shard_map.136
  38.9 0.0 collective-permute-done.8.refs_3_
  38.9 0.0 collective-permute-done.7.refs_2_
  38.9 0.3 collective-permute-start.14
  39.2 0.3 collective-permute-start.11
  39.5 0.8 %collective-permute-start.12 = (f32[10,8,128]{2,1,0:T(8,128)S(1)}, f32[10,8,128]{2,1,0:T(8,128)S(1)}, u32[]{:S(2)}, u32[]{:S(2)}) collective-permute-start(f32[10,8,128]{2,1,0:T(8,128)S(1)} %get-tuple-element.55), channel_id=1, source_target_pairs={{0,2},{1,3},{2,0},{3,1},{4,6},{5,7},{6,4},{7,5},{8,10},{9,11},{10,... | collective-permute-start | bytes 122888 | tf_op jit(solution)/shard_map/ppermute | solution.py:829
  40.3 1.0 %collective-permute-start.13 = (f32[10,8,128]{2,1,0:T(8,128)S(1)}, f32[10,8,128]{2,1,0:T(8,128)S(1)}, u32[]{:S(2)}, u32[]{:S(2)}) collective-permute-start(f32[10,8,128]{2,1,0:T(8,128)S(1)} %get-tuple-element.56), channel_id=1, source_target_pairs={{0,3},{1,0},{2,1},{3,2},{4,7},{5,4},{6,5},{7,6},{8,11},{9,8},{10,9... | collective-permute-start | bytes 122888 | tf_op jit(solution)/shard_map/ppermute | solution.py:829
  41.3 0.0 collective-permute-done.14.refs_4_
  41.3 0.0 copy-done.3
  41.3 0.0 copy-done.4
  41.3 0.0 copy-done.10
  41.3 1.3 %shard_map.137 = (bf16[16,256,512]{2,1,0:T(8,128)(2,1)S(1)}, f32[512,256]{1,0:T(8,128)S(1)}) custom-call(s32[1]{0:T(128)} %bitcast.refs_0_.refs_1_, bf16[4,16,16,128]{3,2,1,0:T(8,128)(2,1)S(1)} %get-tuple-element.48.refs_1_, bf16[4,16,16,128]{3,2,1,0:T(8,128)(2,1)S(1)} %collective-permute-done.7.refs_2_, ...), custom_call_target="tpu_custom_call" | custom-call | flops 4000000000 | bytes 6000000 | tf_op jit(solution)/shard_map/pallas_call | solution.py:62
  42.7 0.0 collective-permute-done.11.refs_2_.refs_1_
  42.7 0.8 %collective-permute-done.12.refs_3_.refs_2_ = f32[10,8,128]{2,1,0:T(8,128)S(1)} collective-permute-done((f32[10,8,128]{2,1,0:T(8,128)S(1)}, f32[10,8,128]{2,1,0:T(8,128)S(1)}, u32[]{:S(2)}, u32[]{:S(2)}) %collective-permute-start.12) | collective-permute-done | bytes 40992 | tf_op jit(solution)/shard_map/ppermute | solution.py:829
  43.5 0.0 collective-permute-done.13.refs_4_.refs_3_
  43.5 0.0 copy-start.1
  43.5 0.0 copy-start.5
  43.5 2.6 %shard_map.139 = bf16[4096,128]{1,0:T(8,128)(2,1)} custom-call(f32[10,8,128]{2,1,0:T(8,128)S(1)} %get-tuple-element.53.refs_1_.refs_0_, f32[10,8,128]{2,1,0:T(8,128)S(1)} %collective-permute-done.11.refs_2_.refs_1_, f32[10,8,128]{2,1,0:T(8,128)S(1)} %collective-permute-done.12.refs_3_.refs_2_, f32[10,8,128]{2,1,0:T(8,128)S(1)} %collective-permute-done.13.refs_4_.refs_3_, ...), custom_call_target="tpu_custom_call" | custom-call | flops 4000000000 | bytes 3000000 | tf_op jit(solution)/shard_map/pallas_call | solution.py:62
  46.1 0.0 copy-done.1
  46.1 0.0 copy-done.5
  46.2 2.2 %shard_map.138 = bf16[512,64]{1,0:T(8,128)(2,1)} custom-call(s32[1]{0:T(128)} %bitcast.refs_0_.refs_1_, f32[10,8,128]{2,1,0:T(8,128)S(1)} %get-tuple-element.53.refs_1_.refs_0_, f32[10,8,128]{2,1,0:T(8,128)S(1)} %collective-permute-done.11.refs_2_.refs_1_, f32[10,8,128]{2,1,0:T(8,128)S(1)} %collective-permute-done.12.refs_3_.refs_2_, ...), custom_call_target="tpu_custom_call" | custom-call | flops 3000000000 | bytes 5000000 | tf_op jit(solution)/shard_map/pallas_call | solution.py:62
  (5 shorter events, 0.1 us)
Async XLA Ops:
  3.6 3.9 %collective-permute-start.1 = (bf16[768,128]{1,0:T(8,128)(2,1)}, bf16[768,128]{1,0:T(8,128)(2,1)S(1)}, u32[]{:S(2)}, u32[]{:S(2)}) collective-permute-start(bf16[768,128]{1,0:T(8,128)(2,1)} %get-tuple-element.39), channel_id=1, source_target_pairs={{0,1},{1,0},{2,3},{3,2},{4,5},{5,4},{6,7},{7,6},{8,9},{9,8},{10,11... | collective-permute-start | bytes 589832 | tf_op jit(solution)/shard_map/ppermute | solution.py:721
  4.0 12.5 %collective-permute-start = (bf16[640,128]{1,0:T(8,128)(2,1)}, bf16[640,128]{1,0:T(8,128)(2,1)S(1)}, u32[]{:S(2)}, u32[]{:S(2)}) collective-permute-start(bf16[640,128]{1,0:T(8,128)(2,1)} %get-tuple-element.37.refs_1_), channel_id=1, source_target_pairs={{0,2},{1,3},{2,0},{3,1},{4,6},{5,7},{6,4},{7,5},{8,10},{9,11},{10,... | collective-permute-start | bytes 491528 | tf_op jit(solution)/shard_map/ppermute | solution.py:721
  7.5 15.6 %collective-permute-start.5 = (bf16[768,128]{1,0:T(8,128)(2,1)S(1)}, bf16[768,128]{1,0:T(8,128)(2,1)S(1)}, u32[]{:S(2)}, u32[]{:S(2)}) collective-permute-start(bf16[768,128]{1,0:T(8,128)(2,1)S(1)} %pad_maximum_fusion), channel_id=1, source_target_pairs={{0,8},{1,12},{2,0},{3,4},{4,9},{5,13},{6,1},{7,5},{8,10},{9,14},{1... | collective-permute-start | bytes 589832 | tf_op jit(solution)/shard_map/ppermute | solution.py:727
  10.2 12.9 %collective-permute-start.4 = (bf16[768,128]{1,0:T(8,128)(2,1)S(1)}, bf16[768,128]{1,0:T(8,128)(2,1)S(1)}, u32[]{:S(2)}, u32[]{:S(2)}) collective-permute-start(bf16[768,128]{1,0:T(8,128)(2,1)S(1)} %pad_maximum_fusion), channel_id=1, source_target_pairs={{0,0},{1,4},{2,8},{3,12},{4,1},{5,5},{6,9},{7,13},{8,2},{9,6},{10,... | collective-permute-start | bytes 589832 | tf_op jit(solution)/shard_map/ppermute | solution.py:727
  10.8 5.7 %collective-permute-start.2 = (bf16[128,128]{1,0:T(8,128)(2,1)}, bf16[128,128]{1,0:T(8,128)(2,1)S(1)}, u32[]{:S(2)}, u32[]{:S(2)}) collective-permute-start(bf16[128,128]{1,0:T(8,128)(2,1)} %get-tuple-element.38.refs_1_), channel_id=1, source_target_pairs={{0,3},{1,2},{2,1},{3,0},{4,7},{5,6},{6,5},{7,4},{8,11},{9,10},{10,... | collective-permute-start | bytes 98312 | tf_op jit(solution)/shard_map/ppermute | solution.py:721
  16.6 0.8 %copy-start.6 = (bf16[128,128]{1,0:T(8,128)(2,1)S(1)}, bf16[128,128]{1,0:T(8,128)(2,1)}, u32[]{:S(2)}) copy-start(bf16[128,128]{1,0:T(8,128)(2,1)} %get-tuple-element.38.refs_1_) | copy-start | bytes 98308
  17.3 5.8 %collective-permute-start.3 = (bf16[512,128]{1,0:T(8,128)(2,1)S(1)}, bf16[512,128]{1,0:T(8,128)(2,1)S(1)}, u32[]{:S(2)}, u32[]{:S(2)}) collective-permute-start(bf16[512,128]{1,0:T(8,128)(2,1)S(1)} %shard_map.131.refs_2_), channel_id=1, source_target_pairs={{0,16},{16,0},{1,17},{17,1},{2,18},{18,2},{3,19},{19,3},{4,20},{20... | collective-permute-start | bytes 393224 | tf_op jit(solution)/shard_map/ppermute | solution.py:737
  18.9 0.9 %copy-start = (bf16[640,128]{1,0:T(8,128)(2,1)S(1)}, bf16[640,128]{1,0:T(8,128)(2,1)}, u32[]{:S(2)}) copy-start(bf16[640,128]{1,0:T(8,128)(2,1)} %get-tuple-element.37.refs_1_) | copy-start | bytes 491524
  19.8 0.9 %copy-start.2 = (bf16[64,768]{1,0:T(8,128)(2,1)S(1)}, bf16[64,768]{1,0:T(8,128)(2,1)}, u32[]{:S(2)}) copy-start(bf16[64,768]{1,0:T(8,128)(2,1)} %get-tuple-element.40.refs_0_) | copy-start | bytes 294916
  23.1 1.6 %collective-permute-start.6 = (bf16[640,128]{1,0:T(8,128)(2,1)S(1)}, bf16[640,128]{1,0:T(8,128)(2,1)S(1)}, u32[]{:S(2)}, u32[]{:S(2)}) collective-permute-start(bf16[640,128]{1,0:T(8,128)(2,1)S(1)} %collective-permute-done.refs_3_.refs_4_), channel_id=1, source_target_pairs={{0,1},{1,0},{2,3},{3,2},{4,5},{5,4},{6,7},{7,6},{8,9},{9,8},{10,11... | collective-permute-start | bytes 491528 | tf_op jit(solution)/shard_map/ppermute | solution.py:721
  23.1 6.9 %copy-start.7 = (s32[256]{0:T(256)S(1)}, s32[256]{0:T(256)}, u32[]{:S(2)}) copy-start(s32[256]{0:T(256)} %param.13) | copy-start | bytes 3076
  23.1 6.9 %copy-start.8 = (bf16[64,64,128]{2,1,0:T(8,128)(2,1)S(1)}, bf16[64,64,128]{2,1,0:T(8,128)(2,1)}, u32[]{:S(2)}) copy-start(bf16[64,64,128]{2,1,0:T(8,128)(2,1)} %param.12) | copy-start | bytes 3145732
  23.2 6.9 %copy-start.9 = (f32[1024,128]{1,0:T(8,128)S(1)}, f32[1024,128]{1,0:T(8,128)}, u32[]{:S(2)}) copy-start(f32[1024,128]{1,0:T(8,128)} %refs_7_.4) | copy-start | bytes 1572868
  23.2 6.9 %copy-start.11 = (f32[128,8]{0,1:T(8,128)S(1)}, f32[128,8]{0,1:T(8,128)}, u32[]{:S(2)}) copy-start(f32[128,8]{0,1:T(8,128)} %param.19) | copy-start | bytes 12292
  23.2 6.9 %collective-permute-start.9 = (bf16[512,128]{1,0:T(8,128)(2,1)S(1)}, bf16[512,128]{1,0:T(8,128)(2,1)S(1)}, u32[]{:S(2)}, u32[]{:S(2)}) collective-permute-start(bf16[512,128]{1,0:T(8,128)(2,1)S(1)} %shard_map.134.refs_3_), channel_id=1, source_target_pairs={{0,16},{16,0},{1,17},{17,1},{2,18},{18,2},{3,19},{19,3},{4,20},{20... | collective-permute-start | bytes 393224 | tf_op jit(solution)/shard_map/ppermute | solution.py:737
  27.0 11.9 %collective-permute-start.8 = (bf16[4,16,16,128]{3,2,1,0:T(8,128)(2,1)S(1)}, bf16[4,16,16,128]{3,2,1,0:T(8,128)(2,1)S(1)}, u32[]{:S(2)}, u32[]{:S(2)}) collective-permute-start(bf16[4,16,16,128]{3,2,1,0:T(8,128)(2,1)S(1)} %get-tuple-element.48.refs_1_), channel_id=1, source_target_pairs={{0,2},{1,3},{2,0},{3,1},{4,6},{5,7},{6,4},{7,5},{8,10},{9,11},{10,... | collective-permute-start | bytes 786440 | tf_op jit(solution)/shard_map/ppermute | solution.py:721
  28.9 10.0 %collective-permute-start.7 = (bf16[4,16,16,128]{3,2,1,0:T(8,128)(2,1)S(1)}, bf16[4,16,16,128]{3,2,1,0:T(8,128)(2,1)S(1)}, u32[]{:S(2)}, u32[]{:S(2)}) collective-permute-start(bf16[4,16,16,128]{3,2,1,0:T(8,128)(2,1)S(1)} %get-tuple-element.48.refs_1_), channel_id=1, source_target_pairs={{0,1},{1,0},{2,3},{3,2},{4,5},{5,4},{6,7},{7,6},{8,9},{9,8},{10,11... | collective-permute-start | bytes 786440 | tf_op jit(solution)/shard_map/ppermute | solution.py:721
  28.9 9.5 %collective-permute-start.10 = (f32[16,8,256]{2,1,0:T(8,128)S(1)}, f32[16,8,256]{2,1,0:T(8,128)S(1)}, u32[]{:S(2)}, u32[]{:S(2)}) collective-permute-start(f32[16,8,256]{2,1,0:T(8,128)S(1)} %get-tuple-element.51.refs_2_), channel_id=1, source_target_pairs={{0,16},{16,0},{1,17},{17,1},{2,18},{18,2},{3,19},{19,3},{4,20},{20... | collective-permute-start | bytes 393224 | tf_op jit(solution)/shard_map/ppermute | solution.py:777
  30.1 11.2 %copy-start.3 = (bf16[64,256]{1,0:T(8,128)(2,1)S(1)}, bf16[64,256]{1,0:T(8,128)(2,1)}, u32[]{:S(2)}) copy-start(bf16[64,256]{1,0:T(8,128)(2,1)} %refs_5_.1) | copy-start | bytes 98308
  30.1 11.2 %copy-start.4 = (bf16[64,256]{1,0:T(8,128)(2,1)S(1)}, bf16[64,256]{1,0:T(8,128)(2,1)}, u32[]{:S(2)}) copy-start(bf16[64,256]{1,0:T(8,128)(2,1)} %refs_7_.5) | copy-start | bytes 98308
  30.1 11.2 %copy-start.10 = (bf16[256,128]{1,0:T(8,128)(2,1)S(1)}, bf16[256,128]{1,0:T(8,128)(2,1)}, u32[]{:S(2)}) copy-start(bf16[256,128]{1,0:T(8,128)(2,1)} %get-tuple-element.59.refs_6_) | copy-start | bytes 196612
  38.9 2.4 %collective-permute-start.14 = (bf16[4,16,16,128]{3,2,1,0:T(8,128)(2,1)S(1)}, bf16[4,16,16,128]{3,2,1,0:T(8,128)(2,1)S(1)}, u32[]{:S(2)}, u32[]{:S(2)}) collective-permute-start(bf16[4,16,16,128]{3,2,1,0:T(8,128)(2,1)S(1)} %collective-permute-done.8.refs_3_), channel_id=1, source_target_pairs={{0,1},{1,0},{2,3},{3,2},{4,5},{5,4},{6,7},{7,6},{8,9},{9,8},{10,11... | collective-permute-start | bytes 786440 | tf_op jit(solution)/shard_map/ppermute | solution.py:721
  39.2 3.5 %collective-permute-start.11 = (f32[10,8,128]{2,1,0:T(8,128)S(1)}, f32[10,8,128]{2,1,0:T(8,128)S(1)}, u32[]{:S(2)}, u32[]{:S(2)}) collective-permute-start(f32[10,8,128]{2,1,0:T(8,128)S(1)} %get-tuple-element.54), channel_id=1, source_target_pairs={{0,1},{1,2},{2,3},{3,0},{4,5},{5,6},{6,7},{7,4},{8,9},{9,10},{10,1... | collective-permute-start | bytes 122888 | tf_op jit(solution)/shard_map/ppermute | solution.py:829
  39.5 4.0 %collective-permute-start.12 = (f32[10,8,128]{2,1,0:T(8,128)S(1)}, f32[10,8,128]{2,1,0:T(8,128)S(1)}, u32[]{:S(2)}, u32[]{:S(2)}) collective-permute-start(f32[10,8,128]{2,1,0:T(8,128)S(1)} %get-tuple-element.55), channel_id=1, source_target_pairs={{0,2},{1,3},{2,0},{3,1},{4,6},{5,7},{6,4},{7,5},{8,10},{9,11},{10,... | collective-permute-start | bytes 122888 | tf_op jit(solution)/shard_map/ppermute | solution.py:829
  40.3 3.2 %collective-permute-start.13 = (f32[10,8,128]{2,1,0:T(8,128)S(1)}, f32[10,8,128]{2,1,0:T(8,128)S(1)}, u32[]{:S(2)}, u32[]{:S(2)}) collective-permute-start(f32[10,8,128]{2,1,0:T(8,128)S(1)} %get-tuple-element.56), channel_id=1, source_target_pairs={{0,3},{1,0},{2,1},{3,2},{4,7},{5,4},{6,5},{7,6},{8,11},{9,8},{10,9... | collective-permute-start | bytes 122888 | tf_op jit(solution)/shard_map/ppermute | solution.py:829
  43.5 2.6 %copy-start.1 = (bf16[32,16,64]{2,1,0:T(8,128)(2,1)S(1)}, bf16[32,16,64]{2,1,0:T(8,128)(2,1)}, u32[]{:S(2)}) copy-start(bf16[32,16,64]{2,1,0:T(8,128)(2,1)} %refs_1_.1) | copy-start | bytes 196612
  43.5 2.6 %copy-start.5 = (bf16[256,64]{0,1:T(8,128)(2,1)S(1)}, bf16[256,64]{0,1:T(8,128)(2,1)}, u32[]{:S(2)}) copy-start(bf16[256,64]{0,1:T(8,128)(2,1)} %param.20) | copy-start | bytes 98308
